TPU v7x, 32 devices: a whole 2x2x4 slice. The times are simulated.
32 devices in a mesh: dp: 8 (over z, core), fsdp: 4 (over y, x).
Axes of the slice: x: 2, y: 2, z: 4, core: 2. Of those that a mesh axis runs over, the one named last changes fastest.
Arguments:
- tokens: bfloat16 [16, 64, 16, 1152], P('dp', 'fsdp'), may hold values from -6 to 6
- conditioning: float32 [16, 1152], P('dp'), may hold values from -6 to 6
- frame_counts: int32 [16], P('dp'), may hold values from 8 to 16
- cotangent: bfloat16 [16, 64, 16, 1152], P('dp', 'fsdp'), may hold values from -6 to 6
- weights: float32 [18, 1152, 1152], P(None, 'dp', 'fsdp')
- biases: float32 [16128], P(('dp', 'fsdp')), may hold values from -1.2 to 1.2
- momentum: float32 [18, 1152, 1152], P(None, 'dp', 'fsdp'), may hold values from -0.17677669 to 0.17677669
- left_stats: float32 [18, 1152, 1152], P(None, 'dp', 'fsdp'), as said below
- right_stats: float32 [18, 1152, 1152], P(None, 'dp', 'fsdp'), as said below
- left_roots: float32 [18, 1152, 1152], P(None, 'dp', 'fsdp'), as said below
- right_roots: float32 [18, 1152, 1152], P(None, 'dp', 'fsdp'), as said below
- bias_moment: float32 [16128], P(('dp', 'fsdp')), may hold values from -3 to 3
- bias_second: float32 [16128], P(('dp', 'fsdp')), may hold values from 4096 to 16384
Outputs:
- block_out: bfloat16 [16, 64, 16, 1152], P('dp', 'fsdp')
- input_grad: bfloat16 [16, 64, 16, 1152], P('dp', 'fsdp')
- left_new: float32 [18, 1152, 1152], P(None, 'dp', 'fsdp')
- right_new: float32 [18, 1152, 1152], P(None, 'dp', 'fsdp')
- momentum_new: float32 [18, 1152, 1152], P(None, 'dp', 'fsdp')
- weights_new: float32 [18, 1152, 1152], P(None, 'dp', 'fsdp')
- weights_copy: bfloat16 [18, 1152, 1152], P(None, 'dp', 'fsdp')
- bias_moment_new: float32 [16128], P(('dp', 'fsdp'))
- bias_second_new: float32 [16128], P(('dp', 'fsdp'))
- biases_new: float32 [16128], P(('dp', 'fsdp'))
Inputs may be any that keep to these rules, and one draw needn't show every extreme that they name: `left_stats`: symmetric, with a dominant positive diagonal. `right_stats`: symmetric, with a dominant positive diagonal. `left_roots`: symmetric, with a dominant positive diagonal. `right_roots`: symmetric, with a dominant positive diagonal.
All inputs are finite; a program needn't handle non-finite values.
Results may differ from a plain program's by a relative error of at most 0.02.
Values may be sent and summed in bfloat16 or wider, within the bound.
No kernel may reach another device: no remote copies, remote signals or barrier semaphores. Data moves between devices by JAX's collectives and lax.ppermute only.
A program may use at most 320 MiB of HBM per device.

v0:
```python
import jax
import jax.numpy as jnp
from jax import lax
from jax.sharding import PartitionSpec as P

HEADS = 16


precise = lax.Precision.HIGHEST
norm_epsilon = 1e-06
masked_score = -1e30
stat_decay = 0.5
moment_decay = 0.9
weight_rate = 0.7
bias_rate = 0.1
diag_epsilon = 1e-08


def shortened(shard):

    def short(part):
        return part.astype(jnp.bfloat16) if part.dtype == jnp.float32 else part

    return jax.tree.map(short, shard)


def layer_norm(values):
    centered = values - jnp.mean(values, axis=-1, keepdims=True)
    variance = jnp.mean(centered * centered, axis=-1, keepdims=True)
    return centered * lax.rsqrt(variance + norm_epsilon)


def modulate(values, shift, scale):
    return layer_norm(values) * (1.0 + scale) + shift


def gelu_tanh(values_in):
    return jax.nn.gelu(values_in, approximate=True)


def attention_scores(query_rows, key_rows, key_keep):
    scale = query_rows.shape[-1] ** (-0.5)
    scores = jnp.einsum("sfhd,sghd->shfg", query_rows, key_rows, precision=precise) * scale
    return jnp.where(key_keep[:, None, None, :], scores, masked_score)


def attention_forward(query_rows, key_rows, value_rows, key_keep):
    scores = attention_scores(query_rows, key_rows, key_keep)
    highest = jnp.max(scores, axis=-1, keepdims=True)
    expons = jnp.exp(scores - highest)
    totals = jnp.sum(expons, axis=-1, keepdims=True)
    mixed = jnp.einsum("shfg,sghd->sfhd", expons / totals, value_rows, precision=precise)
    return (mixed, highest + jnp.log(totals))


def attention_backward(query_rows, key_rows, value_rows, key_keep, log_totals, grad_mixed):
    scale = query_rows.shape[-1] ** (-0.5)
    probs = jnp.exp(attention_scores(query_rows, key_rows, key_keep) - log_totals)
    grad_probs = jnp.einsum("sfhd,sghd->shfg", grad_mixed, value_rows, precision=precise)
    grad_values = jnp.einsum("shfg,sfhd->sghd", probs, grad_mixed, precision=precise)
    inner = jnp.sum(grad_probs * probs, axis=-1, keepdims=True)
    grad_scores = probs * (grad_probs - inner) * scale
    grad_query = jnp.einsum("shfg,sghd->sfhd", grad_scores, key_rows, precision=precise)
    grad_keys = jnp.einsum("shfg,sfhd->sghd", grad_scores, query_rows, precision=precise)
    return (grad_query, grad_keys, grad_values)


def owner_step(grad_shard, left_stats, right_stats, left_roots, right_roots):
    fsdp_count = lax.axis_size("fsdp")
    block_count, row_part, col_part = grad_shard.shape
    capacity = (block_count + fsdp_count - 1) // fsdp_count
    block_ids = jnp.arange(block_count, dtype=jnp.int32)
    holder = block_ids % fsdp_count
    slot_rank = block_ids // fsdp_count
    owner_match = holder[None, None, :] == jnp.arange(fsdp_count, dtype=jnp.int32)[:, None, None]
    slot_match = slot_rank[None, None, :] == jnp.arange(capacity, dtype=jnp.int32)[None, :, None]
    placement_table = (owner_match & slot_match).astype(jnp.float32)

    def outward(array):
        packed = jnp.einsum("pcb,brj->crpj", placement_table, array, precision=precise)
        return packed.reshape(capacity, row_part, fsdp_count * col_part)

    grad_slab, left_slab, right_slab, lroot_slab, rroot_slab = (
        lax.all_to_all(
            outward(grad_shard).astype(jnp.bfloat16),
            "fsdp",
            split_axis=2,
            concat_axis=2,
            tiled=True,
        ).astype(jnp.float32),
        lax.all_to_all(
            outward(left_stats).astype(jnp.bfloat16),
            "fsdp",
            split_axis=2,
            concat_axis=2,
            tiled=True,
        ).astype(jnp.float32),
        lax.all_to_all(
            outward(right_stats).astype(jnp.bfloat16),
            "fsdp",
            split_axis=2,
            concat_axis=2,
            tiled=True,
        ).astype(jnp.float32),
        lax.all_to_all(
            outward(left_roots).astype(jnp.bfloat16),
            "fsdp",
            split_axis=2,
            concat_axis=2,
            tiled=True,
        ).astype(jnp.float32),
        lax.all_to_all(
            outward(right_roots).astype(jnp.bfloat16),
            "fsdp",
            split_axis=2,
            concat_axis=2,
            tiled=True,
        ).astype(jnp.float32),
    )
    whole_grad = lax.all_gather(grad_slab.astype(jnp.bfloat16), "dp", axis=1, tiled=True).astype(
        grad_slab.dtype
    )
    row_start = lax.axis_index("dp") * row_part
    own_columns = lax.dynamic_slice_in_dim(whole_grad, row_start, row_part, 2)
    left_fresh = stat_decay * left_slab + (1.0 - stat_decay) * jnp.einsum(
        "crk,cjk->crj", grad_slab, whole_grad, precision=precise
    )
    right_fresh = stat_decay * right_slab + (1.0 - stat_decay) * jnp.einsum(
        "ckr,ckj->crj", own_columns, whole_grad, precision=precise
    )
    left_side = jnp.einsum("crk,ckj->crj", lroot_slab, whole_grad, precision=precise)
    empty = jnp.zeros(left_side.shape, jnp.float32)
    precond = empty + jnp.einsum(
        "crk,ckj->crj",
        left_side,
        lax.all_gather(rroot_slab.astype(jnp.bfloat16), "dp", axis=1, tiled=True).astype(
            jnp.float32
        ),
        precision=precise,
    )

    def inward(array):
        return array.reshape(capacity, row_part, fsdp_count, col_part)

    back_pre, back_left, back_right = (
        lax.all_to_all(shortened(inward(precond)), "fsdp", split_axis=2, concat_axis=2, tiled=True),
        lax.all_to_all(
            shortened(inward(left_fresh)), "fsdp", split_axis=2, concat_axis=2, tiled=True
        ),
        lax.all_to_all(
            shortened(inward(right_fresh)), "fsdp", split_axis=2, concat_axis=2, tiled=True
        ),
    )

    def unpack(array):
        return jnp.einsum("pcb,crpj->brj", placement_table, array, precision=precise)

    return (unpack(back_pre), unpack(back_left), unpack(back_right))


def per_device(
    tokens,
    conditioning,
    frame_counts,
    cotangent,
    weights,
    biases,
    momentum,
    left_stats,
    right_stats,
    left_roots,
    right_roots,
    bias_moment,
    bias_second,
):
    clip_count, pos_count, frame_count, width = tokens.shape
    row_count = pos_count * frame_count
    token_count = clip_count * row_count
    seq_count = clip_count * pos_count
    head_dim = width // HEADS
    stream = tokens.astype(jnp.float32).reshape(clip_count, row_count, width)
    frame_ids = lax.broadcasted_iota(jnp.int32, (clip_count, frame_count), 1)
    keep = frame_ids < frame_counts[:, None]
    keep_all = jnp.broadcast_to(keep[:, None, :], (clip_count, pos_count, frame_count))
    key_keep = keep_all.reshape(seq_count, frame_count)
    valid = keep_all.astype(jnp.float32).reshape(clip_count, row_count, 1)
    wide_part, bias_part = (
        lax.all_gather(weights.astype(jnp.bfloat16), "fsdp", axis=2, tiled=True),
        lax.all_gather(biases.astype(jnp.bfloat16), "fsdp", axis=0, tiled=True),
    )
    full_w, full_b = (
        lax.all_gather(wide_part, "dp", axis=1, tiled=True),
        lax.all_gather(bias_part, "dp", axis=0, tiled=True),
    )
    bias_all = full_b.astype(jnp.float32)
    cond_low = jax.nn.silu(conditioning).astype(jnp.bfloat16)
    mods = jnp.einsum(
        "cd,jde->cje", cond_low, full_w[0:6], preferred_element_type=jnp.float32
    ) + bias_all[0 : 6 * width].reshape(6, width)
    shift_one = mods[:, 0:1]
    scale_one = mods[:, 1:2]
    gate_one = mods[:, 2:3]
    shift_two = mods[:, 3:4]
    scale_two = mods[:, 4:5]
    gate_two = mods[:, 5:6]
    attn_in = (
        modulate(stream, shift_one, scale_one).astype(jnp.bfloat16).reshape(token_count, width)
    )
    qkv_bias = jnp.stack(
        [
            bias_all[6 * width : 7 * width],
            jnp.zeros((width,), jnp.float32),
            bias_all[7 * width : 8 * width],
        ]
    )
    qkv = (
        jnp.einsum("td,jde->tje", attn_in, full_w[6:9], preferred_element_type=jnp.float32)
        + qkv_bias
    )
    query_rows = qkv[:, 0].reshape(seq_count, frame_count, HEADS, head_dim)
    key_rows = qkv[:, 1].reshape(seq_count, frame_count, HEADS, head_dim)
    value_rows = qkv[:, 2].reshape(seq_count, frame_count, HEADS, head_dim)
    mixed, log_totals = attention_forward(query_rows, key_rows, value_rows, key_keep)
    mixed_low = mixed.reshape(token_count, width).astype(jnp.bfloat16)
    proj = (
        jnp.dot(mixed_low, full_w[9], preferred_element_type=jnp.float32)
        + bias_all[8 * width : 9 * width]
    )
    proj_rows = proj.reshape(clip_count, row_count, width)
    resid = stream + valid * gate_one * proj_rows
    mlp_in = modulate(resid, shift_two, scale_two).astype(jnp.bfloat16).reshape(token_count, width)
    pre = jnp.einsum(
        "td,jde->tje", mlp_in, full_w[10:14], preferred_element_type=jnp.float32
    ) + bias_all[9 * width : 13 * width].reshape(4, width)
    hidden = gelu_tanh(pre).astype(jnp.bfloat16)
    branch = (
        jnp.einsum("tjd,jde->te", hidden, full_w[14:18], preferred_element_type=jnp.float32)
        + bias_all[13 * width : 14 * width]
    )
    branch_rows = branch.reshape(clip_count, row_count, width)
    block_out = (resid + valid * gate_two * branch_rows).astype(jnp.bfloat16).reshape(tokens.shape)
    back_part = lax.all_gather(weights.astype(jnp.bfloat16), "fsdp", axis=2, tiled=True)
    back_w = lax.all_gather(back_part, "dp", axis=1, tiled=True)
    grad_out = cotangent.astype(jnp.float32).reshape(clip_count, row_count, width)
    d_branch = (grad_out * valid * gate_two).astype(jnp.bfloat16).reshape(token_count, width)
    d_gate_two = jnp.sum(grad_out * valid * branch_rows, axis=1, keepdims=True)
    grad_b_two = jnp.sum(d_branch.astype(jnp.float32), axis=0)
    d_hidden = jnp.einsum(
        "te,jde->tjd", d_branch, back_w[14:18], preferred_element_type=jnp.float32
    )
    gelu_value, gelu_pull = jax.vjp(gelu_tanh, pre)
    d_pre = gelu_pull(d_hidden)[0].astype(jnp.bfloat16)
    grad_b_one = jnp.sum(d_pre.astype(jnp.float32), axis=0).reshape(4 * width)
    d_mlp_in = jnp.einsum(
        "tje,jde->td", d_pre, back_w[10:14], preferred_element_type=jnp.float32
    ).reshape(clip_count, row_count, width)
    mod_value, mod_pull = jax.vjp(modulate, resid, shift_two, scale_two)
    d_resid_norm, d_shift_two, d_scale_two = mod_pull(d_mlp_in)
    d_resid = grad_out + d_resid_norm
    d_proj = (d_resid * valid * gate_one).astype(jnp.bfloat16).reshape(token_count, width)
    d_gate_one = jnp.sum(d_resid * valid * proj_rows, axis=1, keepdims=True)
    grad_b_out = jnp.sum(d_proj.astype(jnp.float32), axis=0)
    d_mixed = jnp.einsum(
        "te,de->td", d_proj, back_w[9], preferred_element_type=jnp.float32
    ).reshape(seq_count, frame_count, HEADS, head_dim)
    d_query, d_keys, d_values = attention_backward(
        query_rows, key_rows, value_rows, key_keep, log_totals, d_mixed
    )
    d_qkv = jnp.stack(
        [
            d_query.reshape(token_count, width),
            d_keys.reshape(token_count, width),
            d_values.reshape(token_count, width),
        ],
        axis=1,
    ).astype(jnp.bfloat16)
    qkv_sums = jnp.sum(d_qkv.astype(jnp.float32), axis=0)
    d_attn_in = jnp.einsum(
        "tje,jde->td", d_qkv, back_w[6:9], preferred_element_type=jnp.float32
    ).reshape(clip_count, row_count, width)
    first_value, first_pull = jax.vjp(modulate, stream, shift_one, scale_one)
    d_stream_norm, d_shift_one, d_scale_one = first_pull(d_attn_in)
    input_grad = (d_resid + d_stream_norm).astype(jnp.bfloat16).reshape(tokens.shape)
    d_mods = jnp.concatenate(
        [d_shift_one, d_scale_one, d_gate_one, d_shift_two, d_scale_two, d_gate_two], axis=1
    )
    grad_b_ada = jnp.sum(d_mods, axis=0).reshape(6 * width)
    grad_bias = jnp.concatenate(
        [grad_b_ada, qkv_sums[0], qkv_sums[2], grad_b_out, grad_b_one, grad_b_two]
    )
    dp_count = lax.axis_size("dp")
    row_part = width // dp_count
    block_count = weights.shape[0]
    per_index = block_count * row_part
    cond_wide = cond_low.astype(jnp.float32)

    def block_rows(index):
        row_first = index * row_part
        cond_part = lax.dynamic_slice_in_dim(cond_wide, row_first, row_part, 1)
        ada_rows = jnp.einsum("cr,cje->jre", cond_part, d_mods, precision=precise)
        attn_part = lax.dynamic_slice_in_dim(attn_in, row_first, row_part, 1)
        qkv_rows = jnp.einsum("tr,tje->jre", attn_part, d_qkv, preferred_element_type=jnp.float32)
        mixed_part = lax.dynamic_slice_in_dim(mixed_low, row_first, row_part, 1)
        out_rows = jnp.einsum("tr,te->re", mixed_part, d_proj, preferred_element_type=jnp.float32)[
            None
        ]
        mlp_part = lax.dynamic_slice_in_dim(mlp_in, row_first, row_part, 1)
        one_rows = jnp.einsum("tr,tje->jre", mlp_part, d_pre, preferred_element_type=jnp.float32)
        hidden_part = lax.dynamic_slice_in_dim(hidden, row_first, row_part, 2)
        two_rows = jnp.einsum(
            "tjr,te->jre", hidden_part, d_branch, preferred_element_type=jnp.float32
        )
        stacked = jnp.concatenate([ada_rows, qkv_rows, out_rows, one_rows, two_rows], axis=0)
        return stacked.reshape(per_index, width)

    indices = jnp.arange(lax.axis_size("dp") * per_index // per_index, dtype=jnp.int32)
    row_sums = lax.psum_scatter(
        lax.map(block_rows, indices)
        .reshape(lax.axis_size("dp") * per_index, width)
        .astype(jnp.bfloat16),
        "dp",
        scatter_dimension=0,
        tiled=True,
    ).astype(jnp.float32)
    grad_shard = lax.psum_scatter(
        row_sums.reshape(block_count, row_part, width).astype(jnp.bfloat16),
        "fsdp",
        scatter_dimension=2,
        tiled=True,
    ).astype(jnp.float32)
    bias_grad = lax.psum_scatter(grad_bias, ("dp", "fsdp"), scatter_dimension=0, tiled=True)
    precond, left_new, right_new = owner_step(
        grad_shard, left_stats, right_stats, left_roots, right_roots
    )
    momentum_new = moment_decay * momentum + precond
    weights_new = weights - weight_rate * momentum_new
    weights_copy = weights_new.astype(jnp.bfloat16)
    bias_second_new = stat_decay * bias_second + (1.0 - stat_decay) * bias_grad * bias_grad
    bias_moment_new = moment_decay * bias_moment + bias_grad * lax.rsqrt(
        bias_second_new + diag_epsilon
    )
    biases_new = biases - bias_rate * bias_moment_new
    return (
        block_out,
        input_grad,
        left_new,
        right_new,
        momentum_new,
        weights_new,
        weights_copy,
        bias_moment_new,
        bias_second_new,
        biases_new,
    )


def solution(mesh):
    placed = (
        P("dp", "fsdp", None, None),
        P("dp", None),
        P("dp"),
        P("dp", "fsdp", None, None),
        P(None, "dp", "fsdp"),
        P(("dp", "fsdp")),
        P(None, "dp", "fsdp"),
        P(None, "dp", "fsdp"),
        P(None, "dp", "fsdp"),
        P(None, "dp", "fsdp"),
        P(None, "dp", "fsdp"),
        P(("dp", "fsdp")),
        P(("dp", "fsdp")),
    )
    return jax.shard_map(
        per_device,
        mesh=mesh,
        in_specs=placed,
        out_specs=(
            P("dp", "fsdp", None, None),
            P("dp", "fsdp", None, None),
            P(None, "dp", "fsdp"),
            P(None, "dp", "fsdp"),
            P(None, "dp", "fsdp"),
            P(None, "dp", "fsdp"),
            P(None, "dp", "fsdp"),
            P(("dp", "fsdp")),
            P(("dp", "fsdp")),
            P(("dp", "fsdp")),
        ),
        check_vma=False,
    )
```

profile of v0, /device:TPU:0, one launch (start us, length us, event | category | flops | bytes accessed | tf_op | source)
XLA Modules:
  0.0 1997.3 jit_solution(13224123922564547091)
XLA Ops:
  14.3 138.4 %all-gather.5.cloned.1.call-done = bf16[18,144,1152]{1,0,2:T(8,128)(2,1)} async-done(((bf16[18,144,288]{1,0,2:T(8,128)(2,1)}), bf16[18,144,1152]{1,0,2:T(8,128)(2,1)}) %all-gather.5.cloned.1.call-update) | async-done | bytes 5971984 | tf_op jit(solution)/shard_map/all_gather | solution.py:188
  152.7 16.2 copy.189
  181.6 43.4 %all-reduce.1 = bf16[16128]{0:T(1024)(128)(2,1)S(1)} all-reduce(bf16[16128]{0:T(1024)(128)(2,1)S(1)} %dynamic-update-slice.1), channel_id=1, replica_groups=mesh['dp'=8,'fsdp'=4] {'dp'}, use_global_device_ids=true, to_apply=%add.1 | all-reduce | flops 16128 | bytes 64512
  230.5 345.5 %all-gather.7.cloned.1.call-done = bf16[18,1152,1152]{2,1,0:T(8,128)(2,1)} async-done(((bf16[18,144,1152]{2,1,0:T(8,128)(2,1)}), bf16[18,1152,1152]{2,1,0:T(8,128)(2,1)}) %all-gather.7.cloned.1.call-update) | async-done | bytes 47775760 | tf_op jit(solution)/shard_map/all_gather | solution.py:192
  609.2 13.3 fusion.186
  631.5 11.0 convert_bitcast_fusion.8
  661.2 13.9 multiply_convert_fusion
  675.1 15.7 convert_reduce_fusion
  690.8 10.8 fusion.29
  716.8 11.1 multiply_reduce_fusion
  727.9 10.9 convert_bitcast_fusion.7
  791.3 9.2 fusion.33
  812.5 16.3 multiply_reduce_fusion.1
  829.6 130.1 %while.10 = (s32[]{:T(128)}, bf16[8,2592,1152]{2,1,0:T(8,128)(2,1)}, s32[8]{0:T(128)S(1)}, f32[2,1152]{1,0:T(2,128)}, f32[2,6,1152]{2,0,1:T(2,128)}, /*index=5*/...) while((s32[]{:T(128)}, ...), condition=%wide.region_18.19_spmd, body=%wide.region_17.18_spmd.sunk | while | flops 2062319616 | bytes 78176616 | solution.py:318
  959.8 457.7 %reduce-scatter.5.cloned.1.call-done = bf16[2592,1152]{1,0:T(8,128)(2,1)} async-done(((bf16[20736,1152]{1,0:T(8,128)(2,1)}), bf16[2592,1152]{1,0:T(8,128)(2,1)}) %reduce-scatter.5.cloned.1.call-update) | async-done | bytes 5971984 | tf_op jit(solution)/shard_map/reduce_scatter | solution.py:317
  1417.5 18.5 copy.256
  1435.9 18.5 reshape.484
  1455.1 67.3 %reduce-scatter.7.cloned.1.call-done = bf16[288,2592]{1,0:T(8,128)(2,1)} async-done(((bf16[1152,2592]{1,0:T(8,128)(2,1)}), bf16[288,2592]{1,0:T(8,128)(2,1)}) %reduce-scatter.7.cloned.1.call-update) | async-done | bytes 1493008
  1556.3 25.5 %all_to_all.40 = bf16[4,2,103680]{2,1,0:T(2,128)(2,1)} all-to-all(bf16[4,2,103680]{2,1,0:T(2,128)(2,1)} %reshape.489), channel_id=1, replica_groups=mesh['dp'=8,'fsdp'=4] {'fsdp'}, dimensions={0} | all-to-all | bytes 3317760 | tf_op jit(solution)/shard_map/all_to_all | solution.py:84
  1596.4 9.1 convert_bitcast_fusion
  1605.5 9.3 copy.255
  1622.6 24.3 %all_to_all.41 = bf16[4,2,103680]{2,1,0:T(2,128)(2,1)} all-to-all(bf16[4,2,103680]{2,1,0:T(2,128)(2,1)} %reshape.497), channel_id=1, replica_groups=mesh['dp'=8,'fsdp'=4] {'fsdp'}, dimensions={0} | all-to-all | bytes 3317760 | tf_op jit(solution)/shard_map/all_to_all | solution.py:112
  1670.2 9.2 copy.249
  1691.8 9.2 convert_bitcast_fusion.2
  1701.0 9.2 copy.253
  1722.6 9.5 convert_bitcast_fusion.1
  1732.1 9.1 copy.254
  1815.3 11.0 fusion.73
  1836.7 11.0 fusion.74
  1864.8 10.9 fusion.82
  1875.8 14.2 convolution_convert_fusion
  1903.4 59.8 %all-reduce.2 = f32[16128]{0:T(1024)S(1)} all-reduce(f32[16128]{0:T(1024)S(1)} %constant_dynamic-update-slice_fusion.10), channel_id=4, replica_groups=mesh['dp'=8,'fsdp'=4] {'dp','fsdp'}, use_global_device_ids=true, to_apply=%region_26.27.clone | all-reduce | flops 16128 | bytes 129024
  (427 shorter events, 535.6 us)
Async XLA Ops:
  7.2 145.6 %all-gather.5.cloned.1.call-start = ((), (), s32[]{:S(2)}) async-start(), calls=%async_computation.10 | async-start | bytes 17694720 | tf_op jit(solution)/shard_map/all_gather | solution.py:188
  14.3 561.8 %all-gather.7.cloned.1.call-start = ((), (), s32[]{:S(2)}) async-start(), calls=%async_computation.11 | async-start | bytes 53747712 | tf_op jit(solution)/shard_map/all_gather | solution.py:192
  169.0 56.0 %copy-start.66 = (s32[2]{0:T(128)S(1)}, s32[2]{0:T(128)}, u32[]{:S(2)}) copy-start(s32[2]{0:T(128)} %param.17) | copy-start | bytes 28
  169.0 57.9 %copy-start = (bf16[2,16,16,1152]{3,2,1,0:T(8,128)(2,1)S(1)}, bf16[2,16,16,1152]{3,2,1,0:T(8,128)(2,1)}, u32[]{:S(2)}) copy-start(bf16[2,16,16,1152]{3,2,1,0:T(8,128)(2,1)} %param.15) | copy-start | bytes 3538948
  169.0 60.8 %copy-start.51 = (f32[2,1152]{1,0:T(2,128)S(1)}, f32[2,1152]{1,0:T(2,128)}, u32[]{:S(2)}) copy-start(f32[2,1152]{1,0:T(2,128)} %param.16) | copy-start | bytes 27652
  169.0 1248.4 %reduce-scatter.5.cloned.1.call-start = ((), (), s32[]{:S(2)}) async-start(), calls=%async_computation.12 | async-start | bytes 53747712 | tf_op jit(solution)/shard_map/reduce_scatter | solution.py:317
  225.6 476.0 %copy-start.50 = (f32[2,16]{1,0:T(2,128)}, f32[2,16]{1,0:T(2,128)S(1)}, u32[]{:S(2)}) copy-start(f32[2,16]{1,0:T(2,128)S(1)} %get-tuple-element.263) | copy-start | bytes 388
  227.2 356.6 %copy-start.27 = (f32[2,16,16]{2,1,0:T(8,128)}, f32[2,16,16]{2,1,0:T(8,128)S(1)}, u32[]{:S(2)}) copy-start(f32[2,16,16]{2,1,0:T(8,128)S(1)} %broadcast_multiply_fusion.1) | copy-start | bytes 6148
  227.2 357.1 %copy-start.59 = (f32[512]{0:T(512)}, f32[512]{0:T(512)S(1)}, u32[]{:S(2)}) copy-start(f32[512]{0:T(512)S(1)} %div.106) | copy-start | bytes 6148
  229.1 355.3 %copy-start.60 = (f32[512]{0:T(512)}, f32[512]{0:T(512)S(1)}, u32[]{:S(2)}) copy-start(f32[512]{0:T(512)S(1)} %rsqrt.42) | copy-start | bytes 6148
  661.2 13.9 copy-start.21
  661.2 13.9 copy-start.6
  690.8 10.8 copy-start.4
  690.8 12.2 copy-start.30
  690.8 12.2 copy-start.32
  708.7 48.5 %copy-start.55 = (f32[512]{0:T(512)}, f32[512]{0:T(512)S(1)}, u32[]{:S(2)}) copy-start(f32[512]{0:T(512)S(1)} %negate_multiply_fusion.1) | copy-start | bytes 6148
  716.8 11.1 copy-start.13
  727.9 10.9 copy-start.14
  791.3 10.7 copy-start.36
  959.7 562.6 %reduce-scatter.7.cloned.1.call-start = ((), (), s32[]{:S(2)}) async-start(), calls=%async_computation.15 | async-start | bytes 7741440
  1454.4 360.8 %all-gather.9.cloned.1.call-start = ((), (), s32[]{:S(2)}) async-start(), calls=%async_computation.13 | async-start | bytes 14929920 | tf_op jit(solution)/shard_map/all_gather | solution.py:120
  1595.9 279.9 %all-gather.11.cloned.1.call-start = ((), (), s32[]{:S(2)}) async-start(), calls=%async_computation.14 | async-start | bytes 14929920 | tf_op jit(solution)/shard_map/all_gather | solution.py:136
  1687.2 30.8 %all-to-all-start = ((bf16[4,2,103680]{2,1,0:T(2,128)(2,1)}), bf16[4,2,103680]{2,1,0:T(2,128)(2,1)}, u32[]{:S(2)}, u32[]{:S(2)}) async-start(bf16[4,2,103680]{2,1,0:T(2,128)(2,1)} %reshape.491), calls=%async_computation | async-start | bytes 3317760 | tf_op jit(solution)/shard_map/all_to_all | solution.py:91
  1718.0 31.1 %all-to-all-start.3 = ((bf16[4,2,103680]{2,1,0:T(2,128)(2,1)}), bf16[4,2,103680]{2,1,0:T(2,128)(2,1)}, u32[]{:S(2)}, u32[]{:S(2)}) async-start(bf16[4,2,103680]{2,1,0:T(2,128)(2,1)} %reshape.493), calls=%async_computation.4 | async-start | bytes 3317760 | tf_op jit(solution)/shard_map/all_to_all | solution.py:98
  1749.1 33.1 %all-to-all-start.5 = ((bf16[4,2,103680]{2,1,0:T(2,128)(2,1)}), bf16[4,2,103680]{2,1,0:T(2,128)(2,1)}, u32[]{:S(2)}, u32[]{:S(2)}) async-start(bf16[4,2,103680]{2,1,0:T(2,128)(2,1)} %reshape.495), calls=%async_computation.6 | async-start | bytes 3317760 | tf_op jit(solution)/shard_map/all_to_all | solution.py:105
  1832.5 27.7 %all-to-all-start.2 = ((bf16[5,144,4,288]{3,1,0,2:T(8,128)(2,1)}), bf16[5,144,4,288]{3,1,0,2:T(8,128)(2,1)S(1)}, u32[]{:S(2)}, u32[]{:S(2)}) async-start(bf16[5,144,4,288]{3,1,0,2:T(8,128)(2,1)} %copy.214), calls=%async_computation.3 | async-start | bytes 4423680 | tf_op jit(solution)/shard_map/all_to_all | solution.py:147
  1860.2 38.5 %all-to-all-start.4 = ((bf16[5,144,4,288]{3,1,0,2:T(8,128)(2,1)}), bf16[5,144,4,288]{3,1,0,2:T(8,128)(2,1)}, u32[]{:S(2)}, u32[]{:S(2)}) async-start(bf16[5,144,4,288]{3,1,0,2:T(8,128)(2,1)} %copy.221), calls=%async_computation.5 | async-start | bytes 4423680 | tf_op jit(solution)/shard_map/all_to_all | solution.py:150
  1898.7 64.5 %copy-start.63 = (f32[504]{0:T(512)S(1)}, f32[504]{0:T(512)}, u32[]{:S(2)}) copy-start(f32[504]{0:T(512)} %param.20) | copy-start | bytes 6052
  1898.7 64.5 %copy-start.64 = (f32[504]{0:T(512)S(1)}, f32[504]{0:T(512)}, u32[]{:S(2)}) copy-start(f32[504]{0:T(512)} %param.26) | copy-start | bytes 6052
  1898.7 64.5 %copy-start.65 = (f32[504]{0:T(512)S(1)}, f32[504]{0:T(512)}, u32[]{:S(2)}) copy-start(f32[504]{0:T(512)} %param.27) | copy-start | bytes 6052
  1898.7 65.2 %copy-start.52 = (pred[4,18]{1,0:T(4,128)(4,1)S(1)}, pred[4,18]{1,0:T(4,128)(4,1)}, u32[]{:S(2)}) copy-start(pred[4,18]{1,0:T(4,128)(4,1)} %iota_compare_fusion.1) | copy-start | bytes 220
  1898.7 75.7 %all-to-all-start.7 = ((bf16[5,144,4,288]{3,1,0,2:T(8,128)(2,1)}), bf16[5,144,4,288]{3,1,0,2:T(8,128)(2,1)}, u32[]{:S(2)}, u32[]{:S(2)}) async-start(bf16[5,144,4,288]{3,1,0,2:T(8,128)(2,1)} %copy.232), calls=%async_computation.8 | async-start | bytes 4423680 | tf_op jit(solution)/shard_map/all_to_all | solution.py:146
  (78 other events, 300.3 us)
Sparse Core Ops, SparseCore 0:
  14.4 138.2 all-gather.4
  169.2 406.8 all-gather.6
  959.9 457.5 reduce-scatter.4
  1454.5 67.7 reduce-scatter.6
  1596.0 121.6 all-gather.8
  1719.2 120.5 all-gather.10
where the time goes:
time: 2010 us; the launch traced here: 2000 us
  waiting for transfers between devices  1010 us (50%)
  local copies, waits for them, and re-layouts  387 us (19%)
  matrix products  348 us (17%)
  blocking collectives  162 us (8%)
  other arithmetic  36.5 us (2%)
  starting transfers between devices  28.3 us (1%)
    reduce_scatter x1, waiting for transfers between devices, per_device(): lax.psum_scatter(lax.map(block_rows, indices).reshape(lax.axis_size('dp')...  458 us
    all_gather x1, waiting for transfers between devices, per_device(): lax.all_gather(wide_part, 'dp', axis=1, tiled=True)  346 us
    unnamed x167, local copies, waits for them, and re-layouts  161 us
    all_gather x1, waiting for transfers between devices, per_device(): lax.all_gather(weights.astype(jnp.bfloat16), 'fsdp', axis=2, tiled=True)  138 us
    unnamed x3, blocking collectives  112 us
    unnamed x7, waiting for transfers between devices  67.4 us
    dot_general x5, matrix products, outward(): jnp.einsum('pcb,brj->crpj', placement_table, array, precision=precise)  41.3 us
  transfers between devices with their start and end apart: 12, of which 5 were waited for; matrix products, arithmetic and copies ran while one was open for 14% of the time, Pallas kernels for 0%

commit v1 on v0

v1 whole, which is shorter than its diff:
```python
import jax
import jax.numpy as jnp
from jax import lax
from jax.sharding import PartitionSpec as P

HEADS = 16


precise = lax.Precision.HIGHEST
norm_epsilon = 1e-06
masked_score = -1e30
stat_decay = 0.5
moment_decay = 0.9
weight_rate = 0.7
bias_rate = 0.1
diag_epsilon = 1e-08


def layer_norm(values):
    centered = values - jnp.mean(values, axis=-1, keepdims=True)
    variance = jnp.mean(centered * centered, axis=-1, keepdims=True)
    return centered * lax.rsqrt(variance + norm_epsilon)


def modulate(values, shift, scale):
    return layer_norm(values) * (1.0 + scale) + shift


def gelu_tanh(values_in):
    return jax.nn.gelu(values_in, approximate=True)


def attention_scores(query_rows, key_rows, key_keep):
    scale = query_rows.shape[-1] ** (-0.5)
    scores = jnp.einsum("sfhd,sghd->shfg", query_rows, key_rows, precision=precise) * scale
    return jnp.where(key_keep[:, None, None, :], scores, masked_score)


def attention_forward(query_rows, key_rows, value_rows, key_keep):
    scores = attention_scores(query_rows, key_rows, key_keep)
    highest = jnp.max(scores, axis=-1, keepdims=True)
    expons = jnp.exp(scores - highest)
    totals = jnp.sum(expons, axis=-1, keepdims=True)
    mixed = jnp.einsum("shfg,sghd->sfhd", expons / totals, value_rows, precision=precise)
    return (mixed, highest + jnp.log(totals))


def attention_backward(query_rows, key_rows, value_rows, key_keep, log_totals, grad_mixed):
    scale = query_rows.shape[-1] ** (-0.5)
    probs = jnp.exp(attention_scores(query_rows, key_rows, key_keep) - log_totals)
    grad_probs = jnp.einsum("sfhd,sghd->shfg", grad_mixed, value_rows, precision=precise)
    grad_values = jnp.einsum("shfg,sfhd->sghd", probs, grad_mixed, precision=precise)
    inner = jnp.sum(grad_probs * probs, axis=-1, keepdims=True)
    grad_scores = probs * (grad_probs - inner) * scale
    grad_query = jnp.einsum("shfg,sghd->sfhd", grad_scores, key_rows, precision=precise)
    grad_keys = jnp.einsum("shfg,sfhd->sghd", grad_scores, query_rows, precision=precise)
    return (grad_query, grad_keys, grad_values)


def narrow(array):
    return array.astype(jnp.bfloat16)


def wide(array):
    return array.astype(jnp.float32)


def packed(arrays, tile):
    flat = jnp.concatenate([array.reshape(-1) for array in arrays])
    return jnp.pad(flat, (0, -flat.shape[0] % (tile * 128))).reshape(-1, 128)


def own_rows(parts, group):
    ranks = lax.axis_size("fsdp")
    shares = ranks // group
    count, row_part, col_part = parts.shape
    chunk = row_part // shares
    split = parts.reshape(count // group, group, shares, chunk, col_part)
    split = split.transpose(1, 2, 0, 3, 4).reshape(ranks, count // group, chunk, col_part)
    moved = lax.all_to_all(split, "fsdp", 0, 0, tiled=True)
    return moved.transpose(1, 2, 0, 3).reshape(count // group, chunk, ranks * col_part)


def shard_rows(rows, group):
    ranks = lax.axis_size("fsdp")
    shares = ranks // group
    count, chunk, total = rows.shape
    col_part = total // ranks
    split = rows.reshape(count, chunk, ranks, col_part).transpose(2, 0, 1, 3)
    moved = lax.all_to_all(split, "fsdp", 0, 0, tiled=True)
    moved = moved.reshape(group, shares, count, chunk, col_part).transpose(2, 0, 1, 3, 4)
    return moved.reshape(count * group, shares * chunk, col_part)


def gather_blocks(rows, group):
    ranks, dp_count = lax.axis_size("fsdp"), lax.axis_size("dp")
    shares = ranks // group
    chunk, total = rows.shape
    all_rows = lax.all_gather(rows, ("fsdp", "dp"), axis=0, tiled=True)
    if shares > 1:
        all_rows = all_rows.reshape(group, shares, dp_count, chunk, total).transpose(0, 2, 1, 3, 4)
    return all_rows.reshape(group, total, total)


def gather_own(rows, group):
    ranks = lax.axis_size("fsdp")
    shares = ranks // group
    chunk, total = rows.shape
    if shares > 1:
        sets = [[share + shares * block for share in range(shares)] for block in range(group)]
        rows = lax.all_gather(rows, "fsdp", axis=0, tiled=True, axis_index_groups=sets)
    return lax.all_gather(rows, "dp", axis=0, tiled=True)


def scatter_blocks(blocks, group):
    ranks, dp_count = lax.axis_size("fsdp"), lax.axis_size("dp")
    shares = ranks // group
    count, total, last = blocks.shape
    if shares > 1:
        chunk = total // (dp_count * shares)
        blocks = blocks.reshape(group, dp_count, shares, chunk, last).transpose(0, 2, 1, 3, 4)
    return lax.psum_scatter(
        blocks.reshape(count * total, last), ("fsdp", "dp"), scatter_dimension=0, tiled=True
    )


def fast_dot(subscripts, left, right):
    return jnp.einsum(subscripts, left, right, preferred_element_type=jnp.float32)


def owned_step(grad_rows, left_root, right_root, group):
    chunk, total = grad_rows.shape
    whole = gather_own(grad_rows, group)
    shares = lax.axis_size("fsdp") // group
    first = lax.axis_index("dp") * (chunk * shares) + lax.axis_index("fsdp") % shares * chunk
    own_columns = lax.dynamic_slice_in_dim(whole, first, chunk, 1)
    outer = fast_dot("rk,jk->rj", grad_rows, whole)
    inner = fast_dot("kr,kj->rj", own_columns, whole)
    side = fast_dot("rk,kj->rj", left_root, whole)
    side_high = narrow(side)
    side_low = narrow(side - wide(side_high))
    precond = fast_dot("rk,kj->rj", side_high, right_root) + fast_dot(
        "rk,kj->rj", side_low, right_root
    )
    return narrow(jnp.stack([precond, outer, inner]))


def per_device(
    tokens,
    conditioning,
    frame_counts,
    cotangent,
    weights,
    biases,
    momentum,
    left_stats,
    right_stats,
    left_roots,
    right_roots,
    bias_moment,
    bias_second,
):
    group = 4
    mod_count = 6
    clip_count, pos_count, frame_count, width = tokens.shape
    row_count = pos_count * frame_count
    token_count = clip_count * row_count
    seq_count = clip_count * pos_count
    head_dim = width // HEADS
    block_count, row_part, col_part = weights.shape
    dp_count, ranks = lax.axis_size("dp"), lax.axis_size("fsdp")
    dp_at, rank_at = lax.axis_index("dp"), lax.axis_index("fsdp")
    all_clips = clip_count * dp_count
    bias_part = biases.shape[0]
    stream = tokens.astype(jnp.float32).reshape(clip_count, row_count, width)
    frame_ids = lax.broadcasted_iota(jnp.int32, (clip_count, frame_count), 1)
    keep = frame_ids < frame_counts[:, None]
    keep_all = jnp.broadcast_to(keep[:, None, :], (clip_count, pos_count, frame_count))
    key_keep = keep_all.reshape(seq_count, frame_count)
    valid = keep_all.astype(jnp.float32).reshape(clip_count, row_count, 1)

    weight_rows = own_rows(narrow(weights[mod_count:]), group)
    attn_w = gather_blocks(weight_rows[0], group)
    one_w = gather_blocks(weight_rows[1], group)
    two_w = gather_blocks(weight_rows[2], group)

    cond_low = jax.nn.silu(conditioning).astype(jnp.bfloat16)
    first_parts = lax.all_gather(
        packed([cond_low, narrow(biases)], 16), "dp", axis=0, tiled=True
    ).reshape(dp_count, -1)
    cond_all = first_parts[:, : clip_count * width].reshape(all_clips, width)
    bias_rows = wide(first_parts[:, clip_count * width : clip_count * width + bias_part])
    cond_rows = lax.dynamic_slice_in_dim(cond_all, dp_at * row_part, row_part, 1)
    cond_cols = wide(lax.dynamic_slice_in_dim(cond_all, rank_at * col_part, col_part, 1))
    mod_parts = fast_dot("cr,jre->cje", cond_rows, narrow(weights[:mod_count]))
    mod_parts = lax.all_to_all(mod_parts, "dp", 0, 0, tiled=True)
    mod_cols = jnp.sum(mod_parts.reshape(dp_count, clip_count, mod_count, col_part), axis=0)
    left_cond = jnp.einsum("jrk,ck->jrc", left_roots[:mod_count], cond_cols, precision=precise)
    mod_size, bias_size = mod_cols.size, dp_count * bias_part
    second_parts = lax.all_gather(
        packed([mod_cols, bias_rows, left_cond], 8), "fsdp", axis=0, tiled=True
    ).reshape(ranks, -1)
    mods = second_parts[:, :mod_size].reshape(ranks, clip_count, mod_count, col_part)
    mods = mods.transpose(1, 2, 0, 3).reshape(clip_count, mod_count, width)
    bias_all = second_parts[:, mod_size : mod_size + bias_size].reshape(ranks, dp_count, bias_part)
    bias_all = bias_all.transpose(1, 0, 2).reshape(-1)
    left_size = mod_size + bias_size + left_cond.size
    left_cond = jnp.sum(second_parts[:, mod_size + bias_size : left_size], axis=0)
    left_cond = left_cond.reshape(mod_count, row_part, all_clips)
    mods = mods + bias_all[0 : 6 * width].reshape(6, width)
    shift_one = mods[:, 0:1]
    scale_one = mods[:, 1:2]
    gate_one = mods[:, 2:3]
    shift_two = mods[:, 3:4]
    scale_two = mods[:, 4:5]
    gate_two = mods[:, 5:6]

    attn_in = (
        modulate(stream, shift_one, scale_one).astype(jnp.bfloat16).reshape(token_count, width)
    )
    qkv_bias = jnp.stack(
        [
            bias_all[6 * width : 7 * width],
            jnp.zeros((width,), jnp.float32),
            bias_all[7 * width : 8 * width],
        ]
    )
    qkv = fast_dot("td,jde->tje", attn_in, attn_w[0:3]) + qkv_bias
    query_rows = qkv[:, 0].reshape(seq_count, frame_count, HEADS, head_dim)
    key_rows = qkv[:, 1].reshape(seq_count, frame_count, HEADS, head_dim)
    value_rows = qkv[:, 2].reshape(seq_count, frame_count, HEADS, head_dim)
    mixed, log_totals = attention_forward(query_rows, key_rows, value_rows, key_keep)
    mixed_low = mixed.reshape(token_count, width).astype(jnp.bfloat16)
    proj = fast_dot("td,de->te", mixed_low, attn_w[3]) + bias_all[8 * width : 9 * width]
    proj_rows = proj.reshape(clip_count, row_count, width)
    resid = stream + valid * gate_one * proj_rows
    mlp_in = modulate(resid, shift_two, scale_two).astype(jnp.bfloat16).reshape(token_count, width)
    pre = fast_dot("td,jde->jte", mlp_in, one_w) + bias_all[9 * width : 13 * width].reshape(
        4, 1, width
    )
    hidden = gelu_tanh(pre).astype(jnp.bfloat16)
    grad_out = cotangent.astype(jnp.float32).reshape(clip_count, row_count, width)
    d_branch = (grad_out * valid * gate_two).astype(jnp.bfloat16).reshape(token_count, width)
    grad_two = narrow(fast_dot("jtd,te->jde", hidden, d_branch))
    rows_two = scatter_blocks(grad_two, group)
    branch = fast_dot("jtd,jde->te", hidden, two_w) + bias_all[13 * width : 14 * width]
    branch_rows = branch.reshape(clip_count, row_count, width)
    block_out = (resid + valid * gate_two * branch_rows).astype(jnp.bfloat16).reshape(tokens.shape)
    d_gate_two = jnp.sum(grad_out * valid * branch_rows, axis=1, keepdims=True)
    grad_b_two = jnp.sum(d_branch.astype(jnp.float32), axis=0)
    d_hidden = fast_dot("te,jde->jtd", d_branch, two_w)
    gelu_value, gelu_pull = jax.vjp(gelu_tanh, pre)
    d_pre = gelu_pull(d_hidden)[0].astype(jnp.bfloat16)
    grad_one = narrow(fast_dot("td,jte->jde", mlp_in, d_pre))
    rows_one = scatter_blocks(grad_one, group)
    grad_b_one = jnp.sum(d_pre.astype(jnp.float32), axis=1).reshape(4 * width)
    d_mlp_in = fast_dot("jte,jde->td", d_pre, one_w).reshape(clip_count, row_count, width)
    mod_value, mod_pull = jax.vjp(modulate, resid, shift_two, scale_two)
    d_resid_norm, d_shift_two, d_scale_two = mod_pull(d_mlp_in)
    d_resid = grad_out + d_resid_norm
    d_proj = (d_resid * valid * gate_one).astype(jnp.bfloat16).reshape(token_count, width)
    d_gate_one = jnp.sum(d_resid * valid * proj_rows, axis=1, keepdims=True)
    grad_b_out = jnp.sum(d_proj.astype(jnp.float32), axis=0)
    grad_out_w = narrow(fast_dot("td,te->de", mixed_low, d_proj))
    d_mixed = fast_dot("te,de->td", d_proj, attn_w[3]).reshape(
        seq_count, frame_count, HEADS, head_dim
    )
    d_query, d_keys, d_values = attention_backward(
        query_rows, key_rows, value_rows, key_keep, log_totals, d_mixed
    )
    d_qkv = jnp.stack(
        [
            d_query.reshape(token_count, width),
            d_keys.reshape(token_count, width),
            d_values.reshape(token_count, width),
        ],
        axis=0,
    ).astype(jnp.bfloat16)
    qkv_sums = jnp.sum(d_qkv.astype(jnp.float32), axis=1)
    grad_qkv = narrow(fast_dot("td,jte->jde", attn_in, d_qkv))
    rows_attn = scatter_blocks(jnp.concatenate([grad_qkv, grad_out_w[None]], axis=0), group)
    d_attn_in = fast_dot("jte,jde->td", d_qkv, attn_w[0:3]).reshape(clip_count, row_count, width)
    first_value, first_pull = jax.vjp(modulate, stream, shift_one, scale_one)
    d_stream_norm, d_shift_one, d_scale_one = first_pull(d_attn_in)
    input_grad = (d_resid + d_stream_norm).astype(jnp.bfloat16).reshape(tokens.shape)

    d_mods = jnp.concatenate(
        [d_shift_one, d_scale_one, d_gate_one, d_shift_two, d_scale_two, d_gate_two], axis=1
    )
    grad_b_ada = jnp.sum(d_mods, axis=0).reshape(6 * width)
    grad_bias = jnp.concatenate(
        [grad_b_ada, qkv_sums[0], qkv_sums[2], grad_b_out, grad_b_one, grad_b_two]
    )
    to_ranks = jnp.concatenate(
        [
            d_mods.reshape(clip_count, mod_count, ranks, col_part)
            .transpose(2, 0, 1, 3)
            .reshape(ranks, mod_size),
            grad_bias.reshape(dp_count, ranks, bias_part)
            .transpose(1, 0, 2)
            .reshape(ranks, bias_size),
        ],
        axis=1,
    )
    rank_sums = jnp.sum(lax.all_to_all(to_ranks, "fsdp", 0, 0, tiled=True), axis=0)
    to_rows = jnp.concatenate(
        [
            jnp.broadcast_to(rank_sums[None, :mod_size], (dp_count, mod_size)),
            rank_sums[mod_size:].reshape(dp_count, bias_part),
        ],
        axis=1,
    )
    from_rows = lax.all_to_all(to_rows, "dp", 0, 0, tiled=True)
    bias_grad = jnp.sum(from_rows[:, mod_size:], axis=0)
    mod_grad_cols = from_rows[:, :mod_size].reshape(all_clips, mod_count, col_part)
    mod_grad = lax.all_gather(mod_grad_cols, "fsdp", axis=2, tiled=True)

    mod_grad_rows = lax.dynamic_slice_in_dim(mod_grad, dp_at * row_part, row_part, 2)
    right_parts = jnp.einsum(
        "cjk,jke->cje", mod_grad_rows, right_roots[:mod_count], precision=precise
    )
    mod_right = jnp.sum(lax.all_gather(right_parts, "dp", axis=0), axis=0)
    ada_pre = jnp.einsum("jrc,cje->jre", left_cond, mod_right, precision=precise)
    cond_wide = wide(cond_all)
    cond_row_wide = wide(cond_rows)
    mod_gram = jnp.einsum("cjk,bjk->jcb", mod_grad, mod_grad, precision=precise)
    cond_gram = jnp.einsum("ck,bk->cb", cond_wide, cond_wide, precision=precise)
    mod_side = jnp.einsum("jcb,be->jce", mod_gram, cond_cols, precision=precise)
    ada_left = jnp.einsum("cr,jce->jre", cond_row_wide, mod_side, precision=precise)
    cond_side = jnp.einsum("cb,bje->jce", cond_gram, mod_grad_cols, precision=precise)
    ada_right = jnp.einsum("cjr,jce->jre", mod_grad_rows, cond_side, precision=precise)

    roots = own_rows(
        narrow(jnp.concatenate([left_roots[mod_count:], right_roots[mod_count:]])), group
    )
    right_wholes = [gather_own(roots[3 + piece], group) for piece in range(3)]
    back_two = shard_rows(owned_step(rows_two, roots[2], right_wholes[2], group), group)
    back_one = shard_rows(owned_step(rows_one, roots[1], right_wholes[1], group), group)
    back_attn = shard_rows(owned_step(rows_attn, roots[0], right_wholes[0], group), group)

    def joined(at, ada):
        span = slice(at * group, (at + 1) * group)
        return jnp.concatenate(
            [ada, wide(back_attn[span]), wide(back_one[span]), wide(back_two[span])]
        )

    precond = joined(0, ada_pre)
    left_new = stat_decay * left_stats + (1.0 - stat_decay) * joined(1, ada_left)
    right_new = stat_decay * right_stats + (1.0 - stat_decay) * joined(2, ada_right)
    momentum_new = moment_decay * momentum + precond
    weights_new = weights - weight_rate * momentum_new
    weights_copy = weights_new.astype(jnp.bfloat16)
    bias_second_new = stat_decay * bias_second + (1.0 - stat_decay) * bias_grad * bias_grad
    bias_moment_new = moment_decay * bias_moment + bias_grad * lax.rsqrt(
        bias_second_new + diag_epsilon
    )
    biases_new = biases - bias_rate * bias_moment_new
    return (
        block_out,
        input_grad,
        left_new,
        right_new,
        momentum_new,
        weights_new,
        weights_copy,
        bias_moment_new,
        bias_second_new,
        biases_new,
    )


def solution(mesh):
    placed = (
        P("dp", "fsdp", None, None),
        P("dp", None),
        P("dp"),
        P("dp", "fsdp", None, None),
        P(None, "dp", "fsdp"),
        P(("dp", "fsdp")),
        P(None, "dp", "fsdp"),
        P(None, "dp", "fsdp"),
        P(None, "dp", "fsdp"),
        P(None, "dp", "fsdp"),
        P(None, "dp", "fsdp"),
        P(("dp", "fsdp")),
        P(("dp", "fsdp")),
    )
    return jax.shard_map(
        per_device,
        mesh=mesh,
        in_specs=placed,
        out_specs=(
            P("dp", "fsdp", None, None),
            P("dp", "fsdp", None, None),
            P(None, "dp", "fsdp"),
            P(None, "dp", "fsdp"),
            P(None, "dp", "fsdp"),
            P(None, "dp", "fsdp"),
            P(None, "dp", "fsdp"),
            P(("dp", "fsdp")),
            P(("dp", "fsdp")),
            P(("dp", "fsdp")),
        ),
        check_vma=False,
    )
```

time: 2010 us -> 1050 us (0.52)
  waiting for transfers between devices: 1010 us -> 375 us
  local copies, waits for them, and re-layouts: 387 us -> 189 us
  matrix products: 348 us -> 210 us
  other arithmetic: 36.5 us -> 81.3 us
    all_gather x4 -> x9, waiting for transfers between devices: 484 us -> 109 us  [the longest x3 108 us: gather_blocks(): all_rows = lax.all_gather(rows, ('fsdp', 'dp'), axis=0, tiled=True)]
    reduce_scatter x1 -> x3, waiting for transfers between devices: 458 us -> 236 us  [scatter_blocks(): lax.psum_scatter(blocks.reshape(count * total, last), ('fsdp', 'dp'), sca...]
    dot_general x61 -> x37, matrix products: 287 us -> 150 us  [the longest x28 136 us: fast_dot(): jnp.einsum(subscripts, left, right, preferred_element_type=jnp.float32)]
    unnamed x167 -> x170, local copies, waits for them, and re-layouts: 161 us -> 32.2 us
    unnamed x3 -> x0, blocking collectives: 112 us -> none
    all_gather x0 -> x4, blocking collectives: none -> 87.5 us  [the longest x1 44.1 us: per_device(): mod_grad = lax.all_gather(mod_grad_cols, 'fsdp', axis=2, tiled=True)]
    convert_element_type x12 -> x0, local copies, waits for them, and re-layouts: 74 us -> none  [the longest x6 23.5 us: short(): return part.astype(jnp.bfloat16) if part.dtype == jnp.float32 else part]
    unnamed x7 -> x12, waiting for transfers between devices: 67.4 us -> 0.85 us
  transfers between devices with their start and end apart: 12 -> 18, of which waited for: 5 -> 10; matrix products, arithmetic and copies ran while one was open for 14% -> 43% of each run, Pallas kernels for 0% -> 0%
where the time goes in v1:
time: 1050 us; the launch traced here: 1040 us
  waiting for transfers between devices  375 us (36%)
  matrix products  210 us (20%)
  local copies, waits for them, and re-layouts  189 us (18%)
  blocking collectives  145 us (14%)
  other arithmetic  81.3 us (8%)
  starting transfers between devices  25.6 us (2%)
  between operations  15.7 us (1%)
    reduce_scatter x3, waiting for transfers between devices, scatter_blocks(): lax.psum_scatter(blocks.reshape(count * total, last), ('fsdp', 'dp'), sca...  236 us
    dot_general x28, matrix products, fast_dot(): jnp.einsum(subscripts, left, right, preferred_element_type=jnp.float32)  136 us
    all_gather x3, waiting for transfers between devices, gather_blocks(): all_rows = lax.all_gather(rows, ('fsdp', 'dp'), axis=0, tiled=True)  108 us
    all_to_all x2, blocking collectives, own_rows(): moved = lax.all_to_all(split, 'fsdp', 0, 0, tiled=True)  57.3 us
    all_gather x1, blocking collectives, per_device(): mod_grad = lax.all_gather(mod_grad_cols, 'fsdp', axis=2, tiled=True)  44.1 us
    unnamed x170, local copies, waits for them, and re-layouts  32.2 us
    all_gather x1, blocking collectives, per_device(): mod_right = jnp.sum(lax.all_gather(right_parts, 'dp', axis=0), axis=0)  21.2 us
  transfers between devices with their start and end apart: 18, of which 10 were waited for; matrix products, arithmetic and copies ran while one was open for 43% of the time, Pallas kernels for 0%

profile of v1, /device:TPU:0, one launch (start us, length us, event | category | flops | bytes accessed | tf_op | source)
XLA Modules:
  0.0 1041.2 jit_solution(12060837154520515516)
XLA Ops:
  9.9 22.4 %all_to_all.51 = bf16[4,3,144,288]{3,2,1,0:T(8,128)(2,1)S(1)} all-to-all(bf16[4,3,144,288]{3,2,1,0:T(8,128)(2,1)S(1)} %bitcast.447), channel_id=1, replica_groups=mesh['dp'=8,'fsdp'=4] {'fsdp'}, dimensions={0} | all-to-all | bytes 1990656 | tf_op jit(solution)/shard_map/all_to_all | solution.py:80
  41.9 14.2 %all_gather.42 = bf16[256,128]{1,0:T(8,128)(2,1)S(1)} all-gather(bf16[32,128]{1,0:T(8,128)(2,1)S(1)} %fusion.140), channel_id=1, replica_groups=mesh['dp'=8,'fsdp'=4] {'dp'}, dimensions={0}, use_global_device_ids=true | all-gather | bytes 73728 | tf_op jit(solution)/shard_map/all_gather | solution.py:188
  68.2 7.5 all-to-all-done
  75.9 7.9 all_gather.43
  87.4 35.9 %all-gather.11.cloned.1.call-done = bf16[4608,1152]{1,0:T(8,128)(2,1)} async-done(((bf16[144,1152]{1,0:T(8,128)(2,1)}), bf16[4608,1152]{1,0:T(8,128)(2,1)}) %all-gather.11.cloned.1.call-update) | async-done | bytes 10616848 | tf_op jit(solution)/shard_map/all_gather | solution.py:99
  123.3 7.0 slice.256
  130.2 7.8 convolution_add_fusion
  146.9 6.2 reshape_squeeze.11
  158.5 13.0 %fusion.170 = (f32[32,16,16]{2,1,0:T(8,128)S(1)}, f32[32,16,16,16]{2,3,1,0:T(8,128)S(1)}) fusion(f32[32,16,16,72]{3,2,1,0:T(8,128)} %reshape_squeeze.11, f32[32,16,16,72]{3,2,1,0:T(8,128)} %reshape_squeeze.10, pred[32,16]{1,0:T(8,128)(4,1)S(1)} %bitcast.465), kind=kOutput, calls=%fused_computation.300 | convolution fusion | flops 113631232 | bytes 5276160 | tf_op jit(solution)/shard_map/sfhd,sghd->shfg/dot_general | solution.py:35
  175.3 8.0 convert_bitcast_fusion.3
  202.1 10.7 %all-gather.13.cloned.1.call-done = bf16[4608,1152]{1,0:T(8,128)(2,1)} async-done(((bf16[144,1152]{1,0:T(8,128)(2,1)}), bf16[4608,1152]{1,0:T(8,128)(2,1)}) %all-gather.13.cloned.1.call-update) | async-done | bytes 10616848 | tf_op jit(solution)/shard_map/all_gather | solution.py:99
  212.8 9.7 fusion.91
  222.5 10.4 convolution_convert_fusion
  240.4 61.9 %all-gather.15.cloned.1.call-done = bf16[4608,1152]{1,0:T(8,128)(2,1)} async-done(((bf16[144,1152]{1,0:T(8,128)(2,1)}), bf16[4608,1152]{1,0:T(8,128)(2,1)}) %all-gather.15.cloned.1.call-update) | async-done | bytes 10616848 | tf_op jit(solution)/shard_map/all_gather | solution.py:99
  302.3 17.9 %fusion.14 = (bf16[512,1152,4]{1,0,2:T(8,128)(2,1)}, f32[512,4,1152]{2,0,1:T(8,128)}) fusion(f32[512,4,1152]{2,0,1:T(8,128)} %copy-done.3, f32[1152,4]{0,1:T(4,128)} %get-tuple-element.57, bf16[512,1152,1]{1,0,2:T(8,128)(2,1)} %bitcast.456, bf16[4,1152,1152]{2,1,0:T(8,128)(2,1)} %bitcast.440), kind=kOutput, calls=%fused_computation.22 | convolution fusion | flops 5485363200 | bytes 35407872 | tf_op jit(solution)/shard_map/te,jde->jtd/dot_general | solution.py:128
  320.2 13.1 %multiply_reduce_fusion.1 = (f32[2,1152]{1,0:T(2,128)}, f32[2,256]{1,0:T(2,128)S(1)}, f32[2,1152]{1,0:T(2,128)}, f32[2,256,1152]{2,1,0:T(8,128)S(1)}) fusion(f32[2,256]{1,0:T(2,128)S(1)} %copy-done.72, f32[2,256]{1,0:T(2,128)S(1)} %copy-done.71, f32[2,1152]{1,0:T(2,128)S(1)} %get-tuple-element.63, f32[2,256]{1,0:T(2,128)S(1)} %mul.485, ...), kind=kOutput, calls=%fused_computation.132 | convolution fusion | flops 5444660224 | bytes 23638016 | tf_op jit(solution)/shard_map/jte,jde->td/dot_general | solution.py:128
  338.9 16.6 %fusion.48 = (f32[2,1152]{1,0:T(2,128)}, f32[2,1152]{1,0:T(2,128)}, f32[1152]{0:T(1024)}, bf16[2,256,1152]{2,1,0:T(8,128)(2,1)S(1)}, f32[512,1152]{1,0:T(8,128)}) fusion(bf16[2,16,16,1152]{3,2,1,0:T(8,128)(2,1)} %param.16, f32[2,256]{1,0:T(2,128)S(1)} %mul.485, f32[512,1152]{1,0:T(8,128)S(1)} %convolution_add_fusion.1, f32[2,256,1152]{2,1,0:T(8,128)} %add_add_fusion.1, ...), kind=kOutput, calls=%fused_computation.100 | convolution fusion | flops 5467663360 | bytes 29550592 | tf_op jit(solution)/shard_map/jtd,jde->te/dot_general | solution.py:128
  363.3 9.9 multiply_reduce_fusion
  373.3 8.2 convert_bitcast_fusion.2
  388.2 11.3 %convert_bitcast_fusion.1 = bf16[32,16,16,72]{3,1,2,0:T(8,128)(2,1)S(1)} fusion(f32[32,16,16,72]{3,2,1,0:T(8,128)} %reshape_squeeze.10, f32[32,16,16,16]{2,3,1,0:T(8,128)} %copy-done.5, f32[32,16,16,16]{2,3,1,0:T(8,128)} %copy-done, f32[32,16,16]{2,1,0:T(8,128)} %copy-done.32, f32[32,16,16]{2,1,0:T(8,128)} %copy-done.16), kind=kOutput, calls=%fused_computation.140 | convolution fusion | flops 114360320 | bytes 4653056 | tf_op jit(solution)/shard_map/shfg,sfhd->sghd/dot_general | solution.py:56
  406.2 9.1 convert_bitcast_fusion
  437.3 11.6 %convert_reduce_fusion = (f32[4,1152]{1,0:T(4,128)}, bf16[4,512,1152]{2,1,0:T(8,128)(2,1)S(1)}) fusion(f32[512,4,1152]{2,0,1:T(8,128)} %copy-done.3, f32[4,1152]{1,0:T(4,128)} %get-tuple-element.58, f32[512,4,1152]{2,0,1:T(8,128)} %get-tuple-element.79), kind=kLoop, calls=%fused_computation.36 | loop fusion | flops 54259200 | bytes 23629824 | tf_op jit(solution)/shard_map/reduce_sum | solution.py:256
  448.9 8.4 convolution_convert_fusion.1
  463.0 34.9 %all_to_all.52 = bf16[4,6,144,288]{3,2,1,0:T(8,128)(2,1)S(1)} all-to-all(bf16[4,6,144,288]{3,2,1,0:T(8,128)(2,1)S(1)} %copy.181), channel_id=1, replica_groups=mesh['dp'=8,'fsdp'=4] {'fsdp'}, dimensions={0} | all-to-all | bytes 3981312 | tf_op jit(solution)/shard_map/all_to_all | solution.py:80
  502.4 93.0 %reduce-scatter.4.cloned.1.call-done = bf16[144,1152]{1,0:T(8,128)(2,1)} async-done(((bf16[4608,1152]{1,0:T(8,128)(2,1)}), bf16[144,1152]{1,0:T(8,128)(2,1)}) %reduce-scatter.4.cloned.1.call-update) | async-done | bytes 331792 | tf_op jit(solution)/shard_map/reduce_scatter | solution.py:122
  599.7 142.5 %reduce-scatter.6.cloned.1.call-done = bf16[144,1152]{1,0:T(8,128)(2,1)} async-done(((bf16[4608,1152]{1,0:T(8,128)(2,1)}), bf16[144,1152]{1,0:T(8,128)(2,1)}) %reduce-scatter.6.cloned.1.call-update) | async-done | bytes 331792 | tf_op jit(solution)/shard_map/reduce_scatter | solution.py:122
  767.3 8.4 fusion.67
  851.4 44.1 %all_gather.47 = f32[16,6,1152]{0,1,2:T(8,128)} all-gather(f32[16,6,288]{0,1,2:T(8,128)S(1)} %copy.178), channel_id=1, replica_groups=mesh['dp'=8,'fsdp'=4] {'fsdp'}, dimensions={2}, use_global_device_ids=true | all-gather | bytes 552960 | tf_op jit(solution)/shard_map/all_gather | solution.py:316
  904.7 21.2 %all-gather = f32[128,6,288]{2,0,1:T(8,128)S(1)} all-gather(f32[16,6,288]{2,0,1:T(8,128)S(1)} %fusion.93), channel_id=2, replica_groups=mesh['dp'=8,'fsdp'=4] {'dp'}, dimensions={0}, use_global_device_ids=true | all-gather | bytes 995328 | tf_op jit(solution)/shard_map/all_gather | solution.py:322
  989.3 8.5 all-to-all-done.5
  1007.9 10.0 all-to-all-done.6
  1020.8 7.3 fusion.164
  (414 shorter events, 326.9 us)
Async XLA Ops:
  7.2 116.1 %all-gather.11.cloned.1.call-start = ((), (), s32[]{:S(2)}) async-start(), calls=%async_computation.11 | async-start | bytes 10948608 | tf_op jit(solution)/shard_map/all_gather | solution.py:99
  34.4 178.3 %all-gather.13.cloned.1.call-start = ((), (), s32[]{:S(2)}) async-start(), calls=%async_computation.12 | async-start | bytes 10948608 | tf_op jit(solution)/shard_map/all_gather | solution.py:99
  35.4 26.6 %copy-start.2 = (bf16[2,16,16,1152]{3,2,1,0:T(8,128)(2,1)S(1)}, bf16[2,16,16,1152]{3,2,1,0:T(8,128)(2,1)}, u32[]{:S(2)}) copy-start(bf16[2,16,16,1152]{3,2,1,0:T(8,128)(2,1)} %param.13) | copy-start | bytes 3538948
  37.6 25.3 %copy-start.75 = (s32[2]{0:T(128)S(1)}, s32[2]{0:T(128)}, u32[]{:S(2)}) copy-start(s32[2]{0:T(128)} %param.15) | copy-start | bytes 28
  37.6 264.6 %all-gather.15.cloned.1.call-start = ((), (), s32[]{:S(2)}) async-start(), calls=%async_computation.13 | async-start | bytes 10948608 | tf_op jit(solution)/shard_map/all_gather | solution.py:99
  57.2 18.5 %all-to-all-start = ((f32[16,6,288]{2,1,0:T(8,128)}), f32[16,6,288]{2,1,0:T(8,128)S(1)}, u32[]{:S(2)}, u32[]{:S(2)}) async-start(f32[16,6,288]{2,1,0:T(8,128)} %copy.151), calls=%async_computation | async-start | bytes 393216 | tf_op jit(solution)/shard_map/all_to_all | solution.py:196
  61.9 395.4 %reduce-scatter.8.cloned.1.call-start = ((), (), s32[]{:S(2)}) async-start(), calls=%async_computation.20 | async-start | bytes 10948608 | tf_op jit(solution)/shard_map/reduce_scatter | solution.py:122
  62.3 24.6 %copy-start.57 = (f32[2,256]{1,0:T(2,128)}, f32[2,256]{1,0:T(2,128)S(1)}, u32[]{:S(2)}) copy-start(f32[2,256]{1,0:T(2,128)S(1)} %div.62) | copy-start | bytes 6148
  63.5 130.1 %copy-start.62 = (f32[2,16]{1,0:T(2,128)}, f32[2,16]{1,0:T(2,128)S(1)}, u32[]{:S(2)}) copy-start(f32[2,16]{1,0:T(2,128)S(1)} %get-tuple-element.74) | copy-start | bytes 388
  63.5 20.4 %copy-start.54 = (f32[2,16,16]{2,1,0:T(8,128)}, f32[2,16,16]{2,1,0:T(8,128)S(1)}, u32[]{:S(2)}) copy-start(f32[2,16,16]{2,1,0:T(8,128)S(1)} %broadcast_in_dim.72) | copy-start | bytes 6148
  65.4 19.3 %copy-start.65 = (f32[2,256]{1,0:T(2,128)}, f32[2,256]{1,0:T(2,128)S(1)}, u32[]{:S(2)}) copy-start(f32[2,256]{1,0:T(2,128)S(1)} %add.240) | copy-start | bytes 6148
  65.4 21.4 %copy-start.59 = (f32[2,256]{1,0:T(2,128)}, f32[2,256]{1,0:T(2,128)S(1)}, u32[]{:S(2)}) copy-start(f32[2,256]{1,0:T(2,128)S(1)} %rsqrt.37) | copy-start | bytes 6148
  84.0 46.3 %copy-start.37 = (f32[4,21504]{1,0:T(4,128)}, f32[4,21504]{1,0:T(4,128)S(1)}, u32[]{:S(2)}) copy-start(f32[4,21504]{1,0:T(4,128)S(1)} %reshape.579) | copy-start | bytes 1032196
  86.2 44.0 %copy-start.51 = (f32[2,1152]{1,0:T(2,128)}, f32[2,1152]{1,0:T(2,128)S(1)}, u32[]{:S(2)}) copy-start(f32[2,1152]{1,0:T(2,128)S(1)} %get-tuple-element.68) | copy-start | bytes 27652
  86.2 44.0 %copy-start.56 = (f32[2,1152]{1,0:T(2,128)}, f32[2,1152]{1,0:T(2,128)S(1)}, u32[]{:S(2)}) copy-start(f32[2,1152]{1,0:T(2,128)S(1)} %get-tuple-element.67) | copy-start | bytes 27652
  232.9 362.6 %reduce-scatter.4.cloned.1.call-start = ((), (), s32[]{:S(2)}) async-start(), calls=%async_computation.14 | async-start | bytes 10948608 | tf_op jit(solution)/shard_map/reduce_scatter | solution.py:122
  302.3 17.9 %copy-start.55 = (f32[2,1152]{1,0:T(2,128)S(1)}, f32[2,1152]{1,0:T(2,128)}, u32[]{:S(2)}) copy-start(f32[2,1152]{1,0:T(2,128)} %get-tuple-element.65) | copy-start | bytes 27652
  302.3 17.9 %copy-start.71 = (f32[2,256]{1,0:T(2,128)S(1)}, f32[2,256]{1,0:T(2,128)}, u32[]{:S(2)}) copy-start(f32[2,256]{1,0:T(2,128)} %div.69) | copy-start | bytes 6148
  302.3 17.9 %copy-start.72 = (f32[2,256]{1,0:T(2,128)S(1)}, f32[2,256]{1,0:T(2,128)}, u32[]{:S(2)}) copy-start(f32[2,256]{1,0:T(2,128)} %rsqrt.40) | copy-start | bytes 6148
  437.2 305.0 %reduce-scatter.6.cloned.1.call-start = ((), (), s32[]{:S(2)}) async-start(), calls=%async_computation.17 | async-start | bytes 10948608 | tf_op jit(solution)/shard_map/reduce_scatter | solution.py:122
  457.3 472.8 %all-gather.25.cloned.1.call-start = ((), (), s32[]{:S(2)}) async-start(), calls=%async_computation.21 | async-start | bytes 2985984 | tf_op jit(solution)/shard_map/all_gather | solution.py:112
  458.0 479.8 %all-gather.27.cloned.1.call-start = ((), (), s32[]{:S(2)}) async-start(), calls=%async_computation.22 | async-start | bytes 2985984 | tf_op jit(solution)/shard_map/all_gather | solution.py:112
  502.4 448.9 %all-gather.17.cloned.1.call-start = ((), (), s32[]{:S(2)}) async-start(), calls=%async_computation.15 | async-start | bytes 2985984 | tf_op jit(solution)/shard_map/all_gather | solution.py:112
  595.5 363.5 %all-gather.19.cloned.1.call-start = ((), (), s32[]{:S(2)}) async-start(), calls=%async_computation.16 | async-start | bytes 2985984 | tf_op jit(solution)/shard_map/all_gather | solution.py:112
  599.7 365.5 %all-gather.21.cloned.1.call-start = ((), (), s32[]{:S(2)}) async-start(), calls=%async_computation.18 | async-start | bytes 2985984 | tf_op jit(solution)/shard_map/all_gather | solution.py:112
  742.3 238.1 %all-gather.23.cloned.1.call-start = ((), (), s32[]{:S(2)}) async-start(), calls=%async_computation.19 | async-start | bytes 2985984 | tf_op jit(solution)/shard_map/all_gather | solution.py:112
  822.9 9.0 all-to-all-start.2
  839.1 10.7 %all-to-all-start.3 = ((f32[8,1,3960]{2,1,0:T(1,128)}), f32[8,1,3960]{2,1,0:T(1,128)}, u32[]{:S(2)}, u32[]{:S(2)}) async-start(f32[8,1,3960]{2,1,0:T(1,128)} %all_to_all.36), calls=%async_computation.3 | async-start | bytes 253952 | tf_op jit(solution)/shard_map/all_to_all | solution.py:313
  901.5 24.5 %copy-start.33 = (f32[6,144,16]{2,1,0:T(8,128)S(1)}, f32[6,144,16]{2,1,0:T(8,128)}, u32[]{:S(2)}) copy-start(f32[6,144,16]{2,1,0:T(8,128)} %reshape.616) | copy-start | bytes 165892
  946.8 29.2 %all-to-all-start.7 = ((bf16[4,3,144,288]{3,2,1,0:T(8,128)(2,1)}), bf16[4,3,144,288]{3,2,1,0:T(8,128)(2,1)}, u32[]{:S(2)}, u32[]{:S(2)}) async-start(bf16[4,3,144,288]{3,2,1,0:T(8,128)(2,1)} %copy.195), calls=%async_computation.10 | async-start | bytes 2654208 | tf_op jit(solution)/shard_map/all_to_all | solution.py:90
  976.0 21.8 %all-to-all-start.5 = ((bf16[4,3,144,288]{3,2,1,0:T(8,128)(2,1)}), bf16[4,3,144,288]{3,2,1,0:T(8,128)(2,1)}, u32[]{:S(2)}, u32[]{:S(2)}) async-start(bf16[4,3,144,288]{3,2,1,0:T(8,128)(2,1)} %copy.185), calls=%async_computation.6 | async-start | bytes 2654208 | tf_op jit(solution)/shard_map/all_to_all | solution.py:90
  997.8 20.1 %all-to-all-start.6 = ((bf16[4,3,144,288]{3,2,1,0:T(8,128)(2,1)}), bf16[4,3,144,288]{3,2,1,0:T(8,128)(2,1)S(1)}, u32[]{:S(2)}, u32[]{:S(2)}) async-start(bf16[4,3,144,288]{3,2,1,0:T(8,128)(2,1)} %copy.190), calls=%async_computation.8 | async-start | bytes 2654208 | tf_op jit(solution)/shard_map/all_to_all | solution.py:90
  (63 other events, 393.1 us)
Sparse Core Ops, SparseCore 0:
  34.5 88.6 all-gather.10
  126.8 85.8 all-gather.12
  216.4 85.8 all-gather.14
  308.2 140.3 reduce-scatter.7
  454.5 140.8 reduce-scatter.3
  601.4 140.7 reduce-scatter.5
  743.9 33.0 all-gather.24
  778.6 33.1 all-gather.26
  813.4 33.1 all-gather.16
  848.1 33.1 all-gather.18
  882.9 39.9 all-gather.20
  924.4 34.2 all-gather.22

commit v2 on v1

--- a/solution.py
+++ b/solution.py
@@ -70,15 +70,44 @@
     return jnp.pad(flat, (0, -flat.shape[0] % (tile * 128))).reshape(-1, 128)
 
 
+def core_swap(array):
+    count = lax.axis_size("dp")
+    return lax.ppermute(array, "dp", [(at, at ^ 1) for at in range(count)])
+
+
+def chip_shift(array, step):
+    count = lax.axis_size("dp")
+    return lax.ppermute(array, "dp", [(at, (at + 2 * step) % count) for at in range(count)])
+
+
+def rank_swap(array, bits):
+    count = lax.axis_size("fsdp")
+    return lax.ppermute(array, "fsdp", [(at, at ^ bits) for at in range(count)])
+
+
+def entry(array, at, axis=0):
+    return lax.dynamic_index_in_dim(array, at, axis, keepdims=False)
+
+
+def put(array, part, *at):
+    part = part.reshape((1,) * (array.ndim - part.ndim) + part.shape)
+    at = at + (0,) * (array.ndim - len(at))
+    return lax.dynamic_update_slice(array, part, at)
+
+
 def own_rows(parts, group):
-    ranks = lax.axis_size("fsdp")
+    ranks, at = lax.axis_size("fsdp"), lax.axis_index("fsdp")
     shares = ranks // group
-    count, row_part, col_part = parts.shape
+    row_part, col_part = parts.shape[1:]
     chunk = row_part // shares
-    split = parts.reshape(count // group, group, shares, chunk, col_part)
-    split = split.transpose(1, 2, 0, 3, 4).reshape(ranks, count // group, chunk, col_part)
-    moved = lax.all_to_all(split, "fsdp", 0, 0, tiled=True)
-    return moved.transpose(1, 2, 0, 3).reshape(count // group, chunk, ranks * col_part)
+    split = parts.reshape(ranks, chunk, col_part)
+    panels = [entry(split, at)]
+    panels += [rank_swap(entry(split, at ^ bits), bits) for bits in range(1, ranks)]
+    placed = [
+        lax.select_n(at, *[panels[panel ^ index] for index in range(ranks)])
+        for panel in range(ranks)
+    ]
+    return jnp.concatenate(placed, axis=1)
 
 
 def shard_rows(rows, group):
@@ -102,6 +131,29 @@
     return all_rows.reshape(group, total, total)
 
 
+def gather_pieces(rows, group):
+    ranks, at = lax.axis_size("fsdp"), lax.axis_index("fsdp")
+    if ranks != group:
+        return gather_blocks(rows, group)
+    chips = lax.axis_size("dp") // 2
+    core, chip = lax.axis_index("dp") % 2, lax.axis_index("dp") // 2
+    chunk, total = rows.shape
+    line = put(jnp.zeros((chips, chunk, total), rows.dtype), rows, chip)
+    for step in range(1, chips):
+        line = put(line, chip_shift(rows, step), (chip - step) % chips)
+    own = jnp.zeros((chips, 2, chunk, total), rows.dtype)
+    own = put(own, line[:, None], 0, core)
+    own = put(own, core_swap(line)[:, None], 0, 1 - core)
+    own = own.reshape(2, total // 2, total)
+    half = entry(own, core)
+    found = put(jnp.zeros((ranks, 2, total // 2, total), rows.dtype), own, at)
+    for bits in range(1, ranks):
+        mine = rank_swap(half, bits)
+        found = put(found, mine, at ^ bits, core)
+        found = put(found, core_swap(mine), at ^ bits, 1 - core)
+    return found.reshape(group, total, total)
+
+
 def gather_own(rows, group):
     ranks = lax.axis_size("fsdp")
     shares = ranks // group
@@ -112,27 +164,53 @@
     return lax.all_gather(rows, "dp", axis=0, tiled=True)
 
 
-def scatter_blocks(blocks, group):
+def scatter_blocks(product, left, group):
     ranks, dp_count = lax.axis_size("fsdp"), lax.axis_size("dp")
     shares = ranks // group
-    count, total, last = blocks.shape
+    total = left.shape[-1]
     if shares > 1:
+        blocks = narrow(product(left))
         chunk = total // (dp_count * shares)
-        blocks = blocks.reshape(group, dp_count, shares, chunk, last).transpose(0, 2, 1, 3, 4)
-    return lax.psum_scatter(
-        blocks.reshape(count * total, last), ("fsdp", "dp"), scatter_dimension=0, tiled=True
-    )
+        blocks = blocks.reshape(group, dp_count, shares, chunk, -1).transpose(0, 2, 1, 3, 4)
+        rows = lax.psum_scatter(
+            blocks.reshape(group * total, -1), ("fsdp", "dp"), scatter_dimension=0, tiled=True
+        )
+        return gather_own(rows, group)
+    chips, half = dp_count // 2, total // 2
+    chunk = half // chips
+    core, chip = lax.axis_index("dp") % 2, lax.axis_index("dp") // 2
+    low_bit, high_bit = lax.axis_index("fsdp") % 2, lax.axis_index("fsdp") // 2
+    away = narrow(product(lax.dynamic_slice_in_dim(left, (1 - core) * half, half, left.ndim - 1)))
+    here = product(lax.dynamic_slice_in_dim(left, core * half, half, left.ndim - 1))
+    here = narrow(here + wide(core_swap(away)))
+    here = here.reshape(2, 2, chips, chunk, -1)
+    cut = chips // 2
+    first, second = here[:, :, :cut], here[:, :, cut:]
+    first_in = rank_swap(entry(first, 1 - low_bit, 1), 1)
+    second_in = rank_swap(entry(second, 1 - high_bit, 0), 2)
+    first = narrow(wide(entry(first, low_bit, 1)) + wide(first_in))
+    second = narrow(wide(entry(second, high_bit, 0)) + wide(second_in))
+    first_in = rank_swap(entry(first, 1 - high_bit), 2)
+    second_in = rank_swap(entry(second, 1 - low_bit), 1)
+    first = narrow(wide(entry(first, high_bit)) + wide(first_in))
+    second = narrow(wide(entry(second, low_bit)) + wide(second_in))
+    line = jnp.concatenate([first, second])
+    rows = wide(entry(line, chip))
+    for step in range(1, chips):
+        rows = rows + wide(chip_shift(entry(line, (chip + step) % chips), step))
+    found = lax.all_gather(narrow(rows), "dp", axis=0, tiled=True)
+    return found.reshape(chips, 2, chunk, -1).transpose(1, 0, 2, 3).reshape(total, -1)
 
 
 def fast_dot(subscripts, left, right):
     return jnp.einsum(subscripts, left, right, preferred_element_type=jnp.float32)
 
 
-def owned_step(grad_rows, left_root, right_root, group):
-    chunk, total = grad_rows.shape
-    whole = gather_own(grad_rows, group)
+def owned_step(whole, left_root, right_root, group):
+    chunk = left_root.shape[0]
     shares = lax.axis_size("fsdp") // group
     first = lax.axis_index("dp") * (chunk * shares) + lax.axis_index("fsdp") % shares * chunk
+    grad_rows = lax.dynamic_slice_in_dim(whole, first, chunk, 0)
     own_columns = lax.dynamic_slice_in_dim(whole, first, chunk, 1)
     outer = fast_dot("rk,jk->rj", grad_rows, whole)
     inner = fast_dot("kr,kj->rj", own_columns, whole)
@@ -179,10 +257,12 @@
     key_keep = keep_all.reshape(seq_count, frame_count)
     valid = keep_all.astype(jnp.float32).reshape(clip_count, row_count, 1)
 
-    weight_rows = own_rows(narrow(weights[mod_count:]), group)
-    attn_w = gather_blocks(weight_rows[0], group)
-    one_w = gather_blocks(weight_rows[1], group)
-    two_w = gather_blocks(weight_rows[2], group)
+    pieces = [slice(mod_count + group * piece, mod_count + group * (piece + 1)) for piece in range(3)]
+    attn_w = gather_blocks(own_rows(narrow(weights[pieces[0]]), group), group)
+    one_w = gather_pieces(own_rows(narrow(weights[pieces[1]]), group), group)
+    two_w = gather_blocks(own_rows(narrow(weights[pieces[2]]), group), group)
+    left_rows = [own_rows(narrow(left_roots[piece]), group) for piece in pieces]
+    right_wholes = [gather_own(own_rows(narrow(right_roots[piece]), group), group) for piece in pieces]
 
     cond_low = jax.nn.silu(conditioning).astype(jnp.bfloat16)
     first_parts = lax.all_gather(
@@ -241,8 +321,7 @@
     hidden = gelu_tanh(pre).astype(jnp.bfloat16)
     grad_out = cotangent.astype(jnp.float32).reshape(clip_count, row_count, width)
     d_branch = (grad_out * valid * gate_two).astype(jnp.bfloat16).reshape(token_count, width)
-    grad_two = narrow(fast_dot("jtd,te->jde", hidden, d_branch))
-    rows_two = scatter_blocks(grad_two, group)
+    whole_two = scatter_blocks(lambda left: fast_dot("jtd,te->jde", left, d_branch), hidden, group)
     branch = fast_dot("jtd,jde->te", hidden, two_w) + bias_all[13 * width : 14 * width]
     branch_rows = branch.reshape(clip_count, row_count, width)
     block_out = (resid + valid * gate_two * branch_rows).astype(jnp.bfloat16).reshape(tokens.shape)
@@ -251,8 +330,7 @@
     d_hidden = fast_dot("te,jde->jtd", d_branch, two_w)
     gelu_value, gelu_pull = jax.vjp(gelu_tanh, pre)
     d_pre = gelu_pull(d_hidden)[0].astype(jnp.bfloat16)
-    grad_one = narrow(fast_dot("td,jte->jde", mlp_in, d_pre))
-    rows_one = scatter_blocks(grad_one, group)
+    whole_one = scatter_blocks(lambda left: fast_dot("td,jte->jde", left, d_pre), mlp_in, group)
     grad_b_one = jnp.sum(d_pre.astype(jnp.float32), axis=1).reshape(4 * width)
     d_mlp_in = fast_dot("jte,jde->td", d_pre, one_w).reshape(clip_count, row_count, width)
     mod_value, mod_pull = jax.vjp(modulate, resid, shift_two, scale_two)
@@ -261,7 +339,7 @@
     d_proj = (d_resid * valid * gate_one).astype(jnp.bfloat16).reshape(token_count, width)
     d_gate_one = jnp.sum(d_resid * valid * proj_rows, axis=1, keepdims=True)
     grad_b_out = jnp.sum(d_proj.astype(jnp.float32), axis=0)
-    grad_out_w = narrow(fast_dot("td,te->de", mixed_low, d_proj))
+    d_proj, right_wholes[2] = lax.optimization_barrier((d_proj, right_wholes[2]))
     d_mixed = fast_dot("te,de->td", d_proj, attn_w[3]).reshape(
         seq_count, frame_count, HEADS, head_dim
     )
@@ -276,9 +354,20 @@
         ],
         axis=0,
     ).astype(jnp.bfloat16)
+    d_qkv, right_wholes[1], right_wholes[0] = lax.optimization_barrier(
+        (d_qkv, right_wholes[1], right_wholes[0])
+    )
     qkv_sums = jnp.sum(d_qkv.astype(jnp.float32), axis=1)
-    grad_qkv = narrow(fast_dot("td,jte->jde", attn_in, d_qkv))
-    rows_attn = scatter_blocks(jnp.concatenate([grad_qkv, grad_out_w[None]], axis=0), group)
+    whole_attn = scatter_blocks(
+        lambda left: jnp.concatenate(
+            [
+                fast_dot("td,jte->jde", left[0], d_qkv),
+                fast_dot("td,te->de", left[1], d_proj)[None],
+            ]
+        ),
+        jnp.stack([attn_in, mixed_low]),
+        group,
+    )
     d_attn_in = fast_dot("jte,jde->td", d_qkv, attn_w[0:3]).reshape(clip_count, row_count, width)
     first_value, first_pull = jax.vjp(modulate, stream, shift_one, scale_one)
     d_stream_norm, d_shift_one, d_scale_one = first_pull(d_attn_in)
@@ -330,13 +419,9 @@
     cond_side = jnp.einsum("cb,bje->jce", cond_gram, mod_grad_cols, precision=precise)
     ada_right = jnp.einsum("cjr,jce->jre", mod_grad_rows, cond_side, precision=precise)
 
-    roots = own_rows(
-        narrow(jnp.concatenate([left_roots[mod_count:], right_roots[mod_count:]])), group
-    )
-    right_wholes = [gather_own(roots[3 + piece], group) for piece in range(3)]
-    back_two = shard_rows(owned_step(rows_two, roots[2], right_wholes[2], group), group)
-    back_one = shard_rows(owned_step(rows_one, roots[1], right_wholes[1], group), group)
-    back_attn = shard_rows(owned_step(rows_attn, roots[0], right_wholes[0], group), group)
+    back_two = shard_rows(owned_step(whole_two, left_rows[2], right_wholes[2], group), group)
+    back_one = shard_rows(owned_step(whole_one, left_rows[1], right_wholes[1], group), group)
+    back_attn = shard_rows(owned_step(whole_attn, left_rows[0], right_wholes[0], group), group)
 
     def joined(at, ada):
         span = slice(at * group, (at + 1) * group)

time: 1050 us -> 1060 us (level)
  waiting for transfers between devices: 375 us -> 208 us
  local copies, waits for them, and re-layouts: 189 us -> 267 us
  starting transfers between devices: 25.6 us -> 99.4 us
  other arithmetic: 81.3 us -> 121 us
  blocking collectives: 145 us -> 107 us
  matrix products: 210 us -> 226 us
    reduce_scatter x3 -> x0, waiting for transfers between devices: 236 us -> none  [scatter_blocks(): lax.psum_scatter(blocks.reshape(count * total, last), ('fsdp', 'dp'), sca...]
    ppermute x0 -> x61, waiting for transfers between devices: none -> 192 us  [the longest x42 144 us: rank_swap(): return lax.ppermute(array, 'fsdp', [(at, at ^ bits) for at in range(count)])]
    all_gather x3 -> x2, waiting for transfers between devices: 108 us -> 0.01 us  [gather_blocks(): all_rows = lax.all_gather(rows, ('fsdp', 'dp'), axis=0, tiled=True)]
    ppermute x0 -> x61, starting transfers between devices: none -> 72.1 us  [the longest x42 52 us: rank_swap(): return lax.ppermute(array, 'fsdp', [(at, at ^ bits) for at in range(count)])]
    all_to_all x2 -> x0, blocking collectives: 57.3 us -> none  [own_rows(): moved = lax.all_to_all(split, 'fsdp', 0, 0, tiled=True)]
    convert_element_type x1 -> x17, other arithmetic: 0.01 us -> 24.8 us  [narrow(): return array.astype(jnp.bfloat16)]
    dynamic_update_slice x0 -> x13, local copies, waits for them, and re-layouts: none -> 19.1 us  [put(): return lax.dynamic_update_slice(array, part, at)]
    slice x17 -> x7, local copies, waits for them, and re-layouts: 21.9 us -> 3.17 us  [the longest x3 1.25 us: scatter_blocks(): first, second = (here[:, :, :cut], here[:, :, cut:])]
  transfers between devices with their start and end apart: 18 -> 75, of which waited for: 10 -> 22; matrix products, arithmetic and copies ran while one was open for 43% -> 53% of each run, Pallas kernels for 0% -> 0%
where the time goes in v2:
time: 1060 us; the launch traced here: 1040 us
  local copies, waits for them, and re-layouts  267 us (25%)
  matrix products  226 us (21%)
  waiting for transfers between devices  208 us (20%)
  other arithmetic  121 us (11%)
  blocking collectives  107 us (10%)
  starting transfers between devices  99.4 us (9%)
  between operations  16.4 us (2%)
    dot_general x32, matrix products, fast_dot(): jnp.einsum(subscripts, left, right, preferred_element_type=jnp.float32)  149 us
    ppermute x42, waiting for transfers between devices, rank_swap(): return lax.ppermute(array, 'fsdp', [(at, at ^ bits) for at in range(count)])  144 us
    ppermute x42, starting transfers between devices, rank_swap(): return lax.ppermute(array, 'fsdp', [(at, at ^ bits) for at in range(count)])  52 us
    ppermute x12, waiting for transfers between devices, chip_shift(): lax.ppermute(array, 'dp', [(at, (at + 2 * step) % count) for at in range(...  48.1 us
    all_gather x1, blocking collectives, per_device(): mod_grad = lax.all_gather(mod_grad_cols, 'fsdp', axis=2, tiled=True)  44.2 us
    all_gather x1, blocking collectives, per_device(): mod_right = jnp.sum(lax.all_gather(right_parts, 'dp', axis=0), axis=0)  38.2 us
    unnamed x238, local copies, waits for them, and re-layouts  37.1 us
    convert_element_type x17, other arithmetic, narrow(): return array.astype(jnp.bfloat16)  24.8 us
  transfers between devices with their start and end apart: 75, of which 22 were waited for; matrix products, arithmetic and copies ran while one was open for 53% of the time, Pallas kernels for 0%

profile of v2, /device:TPU:0, one launch (start us, length us, event | category | flops | bytes accessed | tf_op | source)
XLA Modules:
  0.0 1044.1 jit_solution(7467135320082222953)
XLA Ops:
  58.8 14.5 %all_gather.39 = bf16[256,128]{1,0:T(8,128)(2,1)S(1)} all-gather(bf16[32,128]{1,0:T(8,128)(2,1)S(1)} %fusion.271), channel_id=1, replica_groups=mesh['dp'=8,'fsdp'=4] {'dp'}, dimensions={0}, use_global_device_ids=true | all-gather | bytes 73728 | tf_op jit(solution)/shard_map/all_gather | solution.py:268
  143.2 10.1 all_gather.40
  208.7 27.9 %collective-permute-done.10 = bf16[576,1152]{1,0:T(8,128)(2,1)S(1)} collective-permute-done((bf16[576,1152]{1,0:T(8,128)(2,1)}, bf16[576,1152]{1,0:T(8,128)(2,1)S(1)}, u32[]{:S(2)}, u32[]{:S(2)}) %collective-permute-start.10) | collective-permute-done | bytes 1327136 | tf_op jit(solution)/shard_map/ppermute | solution.py:85
  245.4 20.3 %collective-permute-done.14 = bf16[576,1152]{1,0:T(8,128)(2,1)S(1)} collective-permute-done((bf16[576,1152]{1,0:T(8,128)(2,1)}, bf16[576,1152]{1,0:T(8,128)(2,1)S(1)}, u32[]{:S(2)}, u32[]{:S(2)}) %collective-permute-start.14) | collective-permute-done | bytes 1327136 | tf_op jit(solution)/shard_map/ppermute | solution.py:85
  271.8 7.1 slice.280
  278.9 7.4 convolution_add_fusion
  306.7 13.4 %fusion.292 = (f32[32,16,16]{2,1,0:T(8,128)S(1)}, f32[32,16,16,16]{2,3,1,0:T(8,128)S(1)}) fusion(f32[32,16,16,72]{3,2,1,0:T(8,128)} %reshape_squeeze.11, f32[32,16,16,72]{3,2,1,0:T(8,128)} %reshape_squeeze.10, pred[32,16]{1,0:T(8,128)(4,1)S(1)} %bitcast.842), kind=kOutput, calls=%fused_computation.548 | convolution fusion | flops 113631232 | bytes 5276160 | tf_op jit(solution)/shard_map/sfhd,sghd->shfg/dot_general | solution.py:35
  324.0 7.8 convert_bitcast_fusion.3
  350.8 11.6 %fusion.293 = f32[4,1152,512]{2,1,0:T(8,128)} fusion(bf16[4,1152,1152]{2,1,0:T(8,128)(2,1)} %bitcast.811, bf16[512,1152,1]{1,0,2:T(8,128)(2,1)} %bitcast.832), kind=kOutput, calls=%fused_computation.549 | convolution fusion | flops 5435817984 | bytes 21233664 | tf_op jit(solution)/shard_map/te,jde->jtd/dot_general | solution.py:206
  364.4 22.1 %convert_reduce_fusion = (f32[4,1152]{1,0:T(4,128)}, bf16[4,512,1152]{1,2,0:T(8,128)(2,1)}, bf16[4,512,1152]{1,2,0:T(8,128)(2,1)}, f32[4,1152,512]{2,1,0:T(8,128)}) fusion(f32[4,1152]{1,0:T(4,128)S(1)} %copy-done.88, f32[4,1152,512]{2,1,0:T(8,128)} %fusion.293, bf16[4,1152,1152]{2,1,0:T(8,128)(2,1)} %bitcast.809, bf16[512,1152]{1,0:T(8,128)(2,1)S(1)} %get-tuple-element.163), kind=kOutput, calls=%fused_computation.36 | convolution fusion | flops 5494795776 | bytes 40144896 | tf_op jit(solution)/shard_map/td,jde->jte/dot_general | solution.py:206
  386.5 10.6 %fusion.15 = bf16[512,1152,4]{0,1,2:T(8,128)(2,1)S(1)} fusion(f32[4,1152,512]{2,1,0:T(8,128)} %fusion.293, f32[4,1152,512]{2,1,0:T(8,128)} %get-tuple-element.168, f32[1152,4]{0,1:T(4,128)S(1)} %copy-done.74), kind=kLoop, calls=%fused_computation.22 | loop fusion | flops 49545216 | bytes 23611392 | tf_op jit(solution)/shard_map/convert_element_type | solution.py:332
  397.2 13.4 %multiply_reduce_fusion.1 = (f32[2,1152]{1,0:T(2,128)}, f32[2,256]{1,0:T(2,128)S(1)}, f32[2,1152]{1,0:T(2,128)}, f32[2,256,1152]{2,1,0:T(8,128)}) fusion(f32[2,256]{1,0:T(2,128)} %rsqrt.40, f32[2,256]{1,0:T(2,128)} %div.92, f32[2,1152]{1,0:T(2,128)S(1)} %get-tuple-element.152, f32[2,256]{1,0:T(2,128)S(1)} %copy-done.82, ...), kind=kOutput, calls=%fused_computation.152 | convolution fusion | flops 5444660224 | bytes 23638016 | tf_op jit(solution)/shard_map/jte,jde->td/dot_general | solution.py:206
  418.3 14.4 %fusion.64 = (f32[2,1152]{1,0:T(2,128)}, f32[2,1152]{1,0:T(2,128)}, f32[1152]{0:T(1024)}, bf16[2,256,1152]{2,1,0:T(8,128)(2,1)}, f32[512,1152]{1,0:T(8,128)}) fusion(bf16[2,16,16,1152]{3,2,1,0:T(8,128)(2,1)} %param.16, f32[2,256]{1,0:T(2,128)} %mul.509, f32[512,1152]{1,0:T(8,128)S(1)} %convolution_add_fusion.1, f32[2,256,1152]{2,1,0:T(8,128)} %add_add_fusion.1, ...), kind=kOutput, calls=%fused_computation.118 | convolution fusion | flops 5444070400 | bytes 24813568 | tf_op jit(solution)/shard_map/jtd,jde->te/dot_general | solution.py:206
  445.4 9.4 convert_bitcast_fusion
  461.4 14.8 %multiply_reduce_fusion = (f32[32,16,16]{2,1,0:T(8,128)S(1)}, f32[32,16,16,16]{2,3,1,0:T(8,128)S(1)}) fusion(f32[32,16,16,16]{2,3,1,0:T(8,128)} %copy-done, f32[32,16,16]{2,1,0:T(8,128)} %copy-done.30, f32[32,16,16,72]{3,2,1,0:T(8,128)} %reshape_squeeze.9, f32[32,16,16,72]{3,2,1,0:T(8,128)} %reshape.756), kind=kOutput, calls=%fused_computation.49 | convolution fusion | flops 113631232 | bytes 5832704 | tf_op jit(solution)/shard_map/sfhd,sghd->shfg/dot_general | solution.py:51
  488.7 10.9 %convert_bitcast_fusion.2 = bf16[32,16,16,72]{3,1,2,0:T(8,128)(2,1)S(1)} fusion(f32[32,16,16,72]{3,2,1,0:T(8,128)} %reshape_squeeze.11, f32[32,16,16,16]{2,3,1,0:T(8,128)} %copy-done.5, f32[32,16,16,16]{2,3,1,0:T(8,128)} %copy-done, f32[32,16,16]{2,1,0:T(8,128)} %copy-done.45, f32[32,16,16]{2,1,0:T(8,128)} %copy-done.30), kind=kOutput, calls=%fused_computation.164 | convolution fusion | flops 114360320 | bytes 4653056 | tf_op jit(solution)/shard_map/shfg,sghd->sfhd/dot_general | solution.py:55
  513.1 8.3 fusion.80
  527.2 7.7 convolution_convert_fusion
  535.4 7.7 fusion.26
  641.9 7.1 fusion.1
  651.3 19.3 %collective-permute-done.54 = bf16[2,2,144,1152]{3,2,1,0:T(8,128)(2,1)} collective-permute-done((bf16[2,2,144,1152]{3,2,1,0:T(8,128)(2,1)S(1)}, bf16[2,2,144,1152]{3,2,1,0:T(8,128)(2,1)}, u32[]{:S(2)}, u32[]{:S(2)}) %collective-permute-start.54) | collective-permute-done | bytes 1327136 | tf_op jit(solution)/shard_map/ppermute | solution.py:85
  677.8 12.5 %collective-permute-done.55 = bf16[2,144,1152]{2,1,0:T(8,128)(2,1)S(1)} collective-permute-done((bf16[2,144,1152]{2,1,0:T(8,128)(2,1)S(1)}, bf16[2,144,1152]{2,1,0:T(8,128)(2,1)S(1)}, u32[]{:S(2)}, u32[]{:S(2)}) %collective-permute-start.55) | collective-permute-done | bytes 663584 | tf_op jit(solution)/shard_map/ppermute | solution.py:85
  690.5 22.3 %collective-permute-done.57 = bf16[2,144,1152]{2,1,0:T(8,128)(2,1)S(1)} collective-permute-done((bf16[2,144,1152]{2,1,0:T(8,128)(2,1)S(1)}, bf16[2,144,1152]{2,1,0:T(8,128)(2,1)S(1)}, u32[]{:S(2)}, u32[]{:S(2)}) %collective-permute-start.57) | collective-permute-done | bytes 663584 | tf_op jit(solution)/shard_map/ppermute | solution.py:85
  718.9 9.1 fusion
  728.0 18.1 %collective-permute-done.59 = bf16[144,1152]{1,0:T(8,128)(2,1)} collective-permute-done((bf16[144,1152]{1,0:T(8,128)(2,1)}, bf16[144,1152]{1,0:T(8,128)(2,1)}, u32[]{:S(2)}, u32[]{:S(2)}) %collective-permute-start.59) | collective-permute-done | bytes 331808 | tf_op jit(solution)/shard_map/ppermute | solution.py:80
  756.4 9.9 collective-permute-done.44
  780.2 7.5 collective-permute-done.49
  787.7 22.4 %collective-permute-done.48 = bf16[144,1152]{1,0:T(8,128)(2,1)S(1)} collective-permute-done((bf16[144,1152]{1,0:T(8,128)(2,1)S(1)}, bf16[144,1152]{1,0:T(8,128)(2,1)S(1)}, u32[]{:S(2)}, u32[]{:S(2)}) %collective-permute-start.48) | collective-permute-done | bytes 331808 | tf_op jit(solution)/shard_map/ppermute | solution.py:80
  816.6 44.2 %all_gather.46 = f32[16,6,1152]{0,1,2:T(8,128)} all-gather(f32[16,6,288]{0,1,2:T(8,128)S(1)} %copy.189), channel_id=1, replica_groups=mesh['dp'=8,'fsdp'=4] {'fsdp'}, dimensions={2}, use_global_device_ids=true | all-gather | bytes 552960 | tf_op jit(solution)/shard_map/all_gather | solution.py:405
  872.0 9.2 collective-permute-done.33
  887.7 38.2 %all-gather = f32[128,6,288]{2,0,1:T(8,128)S(1)} all-gather(f32[16,6,288]{2,0,1:T(8,128)S(1)} %fusion.131), channel_id=2, replica_groups=mesh['dp'=8,'fsdp'=4] {'dp'}, dimensions={0}, use_global_device_ids=true | all-gather | bytes 995328 | tf_op jit(solution)/shard_map/all_gather | solution.py:411
  1007.7 10.3 all-to-all-done.3
  (659 shorter events, 557.9 us)
Async XLA Ops:
  7.2 264.6 %all-gather.10.cloned.1.call-start = ((), (), s32[]{:S(2)}) async-start(), calls=%async_computation.6 | async-start | bytes 10948608 | tf_op jit(solution)/shard_map/all_gather | solution.py:128
  25.4 325.3 %all-gather.12.cloned.1.call-start = ((), (), s32[]{:S(2)}) async-start(), calls=%async_computation.7 | async-start | bytes 10948608 | tf_op jit(solution)/shard_map/all_gather | solution.py:128
  41.5 391.1 %all-gather.14.cloned.1.call-start = ((), (), s32[]{:S(2)}) async-start(), calls=%async_computation.8 | async-start | bytes 2985984 | tf_op jit(solution)/shard_map/all_gather | solution.py:164
  57.7 452.1 %all-gather.16.cloned.1.call-start = ((), (), s32[]{:S(2)}) async-start(), calls=%async_computation.9 | async-start | bytes 2985984 | tf_op jit(solution)/shard_map/all_gather | solution.py:164
  74.4 63.3 %all-to-all-start = ((f32[16,6,288]{2,1,0:T(8,128)}), f32[16,6,288]{2,1,0:T(8,128)}, u32[]{:S(2)}, u32[]{:S(2)}) async-start(f32[16,6,288]{2,1,0:T(8,128)} %copy.159), calls=%async_computation | async-start | bytes 393216 | tf_op jit(solution)/shard_map/all_to_all | solution.py:276
  79.6 430.1 %all-gather.18.cloned.1.call-start = ((), (), s32[]{:S(2)}) async-start(), calls=%async_computation.10 | async-start | bytes 2985984 | tf_op jit(solution)/shard_map/all_gather | solution.py:164
  124.2 50.2 %collective-permute-start.6 = (bf16[144,1152]{1,0:T(8,128)(2,1)}, bf16[144,1152]{1,0:T(8,128)(2,1)}, u32[]{:S(2)}, u32[]{:S(2)}) collective-permute-start(bf16[144,1152]{1,0:T(8,128)(2,1)} %concatenate.94), channel_id=1, source_target_pairs={{0,8},{4,12},{8,16},{12,20},{16,24},{20,28},{24,0},{28,4},{1,9},{5... | collective-permute-start | bytes 995336 | tf_op jit(solution)/shard_map/ppermute | solution.py:80
  125.7 50.3 %collective-permute-start.7 = (bf16[144,1152]{1,0:T(8,128)(2,1)}, bf16[144,1152]{1,0:T(8,128)(2,1)}, u32[]{:S(2)}, u32[]{:S(2)}) collective-permute-start(bf16[144,1152]{1,0:T(8,128)(2,1)} %concatenate.94), channel_id=1, source_target_pairs={{0,16},{4,20},{8,24},{12,28},{16,0},{20,4},{24,8},{28,12},{1,17},{... | collective-permute-start | bytes 995336 | tf_op jit(solution)/shard_map/ppermute | solution.py:80
  128.1 49.7 %collective-permute-start.8 = (bf16[144,1152]{1,0:T(8,128)(2,1)}, bf16[144,1152]{1,0:T(8,128)(2,1)}, u32[]{:S(2)}, u32[]{:S(2)}) collective-permute-start(bf16[144,1152]{1,0:T(8,128)(2,1)} %concatenate.94), channel_id=1, source_target_pairs={{0,24},{4,28},{8,0},{12,4},{16,8},{20,12},{24,16},{28,20},{1,25},{... | collective-permute-start | bytes 995336 | tf_op jit(solution)/shard_map/ppermute | solution.py:80
  201.9 34.7 %collective-permute-start.10 = (bf16[576,1152]{1,0:T(8,128)(2,1)}, bf16[576,1152]{1,0:T(8,128)(2,1)S(1)}, u32[]{:S(2)}, u32[]{:S(2)}) collective-permute-start(bf16[576,1152]{1,0:T(8,128)(2,1)} %dynamic-slice_bitcast_fusion.6), channel_id=1, source_target_pairs={{0,1},{1,0},{2,3},{3,2},{4,5},{5,4},{6,7},{7,6},{8,9},{9,8},{10,11... | collective-permute-start | bytes 3981320 | tf_op jit(solution)/shard_map/ppermute | solution.py:85
  205.7 38.1 %collective-permute-start.12 = (bf16[576,1152]{1,0:T(8,128)(2,1)}, bf16[576,1152]{1,0:T(8,128)(2,1)S(1)}, u32[]{:S(2)}, u32[]{:S(2)}) collective-permute-start(bf16[576,1152]{1,0:T(8,128)(2,1)} %dynamic-slice_bitcast_fusion.6), channel_id=1, source_target_pairs={{0,2},{1,3},{2,0},{3,1},{4,6},{5,7},{6,4},{7,5},{8,10},{9,11},{10,... | collective-permute-start | bytes 3981320 | tf_op jit(solution)/shard_map/ppermute | solution.py:85
  207.8 57.9 %collective-permute-start.14 = (bf16[576,1152]{1,0:T(8,128)(2,1)}, bf16[576,1152]{1,0:T(8,128)(2,1)S(1)}, u32[]{:S(2)}, u32[]{:S(2)}) collective-permute-start(bf16[576,1152]{1,0:T(8,128)(2,1)} %dynamic-slice_bitcast_fusion.6), channel_id=1, source_target_pairs={{0,3},{1,2},{2,1},{3,0},{4,7},{5,6},{6,5},{7,4},{8,11},{9,10},{10,... | collective-permute-start | bytes 3981320 | tf_op jit(solution)/shard_map/ppermute | solution.py:85
  236.6 29.2 %collective-permute-start.11 = (bf16[576,1152]{1,0:T(8,128)(2,1)S(1)}, bf16[576,1152]{1,0:T(8,128)(2,1)S(1)}, u32[]{:S(2)}, u32[]{:S(2)}) collective-permute-start(bf16[576,1152]{1,0:T(8,128)(2,1)S(1)} %collective-permute-done.10), channel_id=1, source_target_pairs={{0,4},{4,0},{8,12},{12,8},{16,20},{20,16},{24,28},{28,24},{1,5},{5... | collective-permute-start | bytes 3981320 | tf_op jit(solution)/shard_map/ppermute | solution.py:75
  534.9 96.2 %collective-permute-start.53 = (bf16[4,576,1152]{2,1,0:T(8,128)(2,1)}, bf16[4,576,1152]{2,1,0:T(8,128)(2,1)}, u32[]{:S(2)}, u32[]{:S(2)}) collective-permute-start(bf16[4,576,1152]{2,1,0:T(8,128)(2,1)} %convolution_convert_fusion), channel_id=1, source_target_pairs={{0,4},{4,0},{8,12},{12,8},{16,20},{20,16},{24,28},{28,24},{1,5},{5... | collective-permute-start | bytes 15925256 | tf_op jit(solution)/shard_map/ppermute | solution.py:75
  543.1 98.8 %collective-permute-start.42 = (bf16[4,576,1152]{2,1,0:T(8,128)(2,1)}, bf16[4,576,1152]{2,1,0:T(8,128)(2,1)}, u32[]{:S(2)}, u32[]{:S(2)}) collective-permute-start(bf16[4,576,1152]{2,1,0:T(8,128)(2,1)} %fusion.26), channel_id=1, source_target_pairs={{0,4},{4,0},{8,12},{12,8},{16,20},{20,16},{24,28},{28,24},{1,5},{5... | collective-permute-start | bytes 15925256 | tf_op jit(solution)/shard_map/ppermute | solution.py:75
  617.7 100.0 %collective-permute-start.31 = (bf16[4,576,1152]{2,1,0:T(8,128)(2,1)}, bf16[4,576,1152]{2,1,0:T(8,128)(2,1)}, u32[]{:S(2)}, u32[]{:S(2)}) collective-permute-start(bf16[4,576,1152]{2,1,0:T(8,128)(2,1)} %pad_maximum_fusion), channel_id=1, source_target_pairs={{0,4},{4,0},{8,12},{12,8},{16,20},{20,16},{24,28},{28,24},{1,5},{5... | collective-permute-start | bytes 15925256 | tf_op jit(solution)/shard_map/ppermute | solution.py:75
  626.1 188.4 %all-to-all-start.2 = ((f32[8,1,3960]{2,1,0:T(1,128)}), f32[8,1,3960]{2,1,0:T(1,128)}, u32[]{:S(2)}, u32[]{:S(2)}) async-start(f32[8,1,3960]{2,1,0:T(1,128)} %all_to_all.29), calls=%async_computation.2 | async-start | bytes 253952 | tf_op jit(solution)/shard_map/all_to_all | solution.py:402
  630.7 306.4 %all-gather.24.cloned.1.call-start = ((), (), s32[]{:S(2)}) async-start(), calls=%async_computation.13 | async-start | bytes 2985984 | tf_op jit(solution)/shard_map/all_gather | solution.py:201
  638.5 32.1 %collective-permute-start.54 = (bf16[2,2,144,1152]{3,2,1,0:T(8,128)(2,1)S(1)}, bf16[2,2,144,1152]{3,2,1,0:T(8,128)(2,1)}, u32[]{:S(2)}, u32[]{:S(2)}) collective-permute-start(bf16[2,2,144,1152]{3,2,1,0:T(8,128)(2,1)S(1)} %dynamic-slice_bitcast_fusion.1), channel_id=1, source_target_pairs={{0,1},{1,0},{2,3},{3,2},{4,5},{5,4},{6,7},{7,6},{8,9},{9,8},{10,11... | collective-permute-start | bytes 3981320 | tf_op jit(solution)/shard_map/ppermute | solution.py:85
  640.4 33.7 %collective-permute-start.56 = (bf16[2,2,144,1152]{3,2,1,0:T(8,128)(2,1)S(1)}, bf16[2,2,144,1152]{3,2,1,0:T(8,128)(2,1)S(1)}, u32[]{:S(2)}, u32[]{:S(2)}) collective-permute-start(bf16[2,2,144,1152]{3,2,1,0:T(8,128)(2,1)S(1)} %dynamic-slice_bitcast_fusion), channel_id=1, source_target_pairs={{0,2},{1,3},{2,0},{3,1},{4,6},{5,7},{6,4},{7,5},{8,10},{9,11},{10,... | collective-permute-start | bytes 3981320 | tf_op jit(solution)/shard_map/ppermute | solution.py:85
  650.7 97.9 %collective-permute-start.43 = (bf16[2,2,144,1152]{3,2,1,0:T(8,128)(2,1)}, bf16[2,2,144,1152]{3,2,1,0:T(8,128)(2,1)}, u32[]{:S(2)}, u32[]{:S(2)}) collective-permute-start(bf16[2,2,144,1152]{3,2,1,0:T(8,128)(2,1)} %dynamic-slice_bitcast_fusion.3), channel_id=1, source_target_pairs={{0,1},{1,0},{2,3},{3,2},{4,5},{5,4},{6,7},{7,6},{8,9},{9,8},{10,11... | collective-permute-start | bytes 3981320 | tf_op jit(solution)/shard_map/ppermute | solution.py:85
  674.5 38.2 %collective-permute-start.57 = (bf16[2,144,1152]{2,1,0:T(8,128)(2,1)S(1)}, bf16[2,144,1152]{2,1,0:T(8,128)(2,1)S(1)}, u32[]{:S(2)}, u32[]{:S(2)}) collective-permute-start(bf16[2,144,1152]{2,1,0:T(8,128)(2,1)S(1)} %dynamic-slice_bitcast_fusion.7), channel_id=1, source_target_pairs={{0,1},{1,0},{2,3},{3,2},{4,5},{5,4},{6,7},{7,6},{8,9},{9,8},{10,11... | collective-permute-start | bytes 1990664 | tf_op jit(solution)/shard_map/ppermute | solution.py:85
  677.2 75.5 %collective-permute-start.45 = (bf16[2,2,144,1152]{3,2,1,0:T(8,128)(2,1)}, bf16[2,2,144,1152]{3,2,1,0:T(8,128)(2,1)}, u32[]{:S(2)}, u32[]{:S(2)}) collective-permute-start(bf16[2,2,144,1152]{3,2,1,0:T(8,128)(2,1)} %dynamic-slice_bitcast_fusion.2), channel_id=1, source_target_pairs={{0,2},{1,3},{2,0},{3,1},{4,6},{5,7},{6,4},{7,5},{8,10},{9,11},{10,... | collective-permute-start | bytes 3981320 | tf_op jit(solution)/shard_map/ppermute | solution.py:85
  748.4 207.8 %all-gather.22.cloned.1.call-start = ((), (), s32[]{:S(2)}) async-start(), calls=%async_computation.12 | async-start | bytes 2985984 | tf_op jit(solution)/shard_map/all_gather | solution.py:201
  770.2 39.9 %collective-permute-start.48 = (bf16[144,1152]{1,0:T(8,128)(2,1)S(1)}, bf16[144,1152]{1,0:T(8,128)(2,1)S(1)}, u32[]{:S(2)}, u32[]{:S(2)}) collective-permute-start(bf16[144,1152]{1,0:T(8,128)(2,1)S(1)} %get-tuple-element.78), channel_id=1, source_target_pairs={{0,16},{4,20},{8,24},{12,28},{16,0},{20,4},{24,8},{28,12},{1,17},{... | collective-permute-start | bytes 995336 | tf_op jit(solution)/shard_map/ppermute | solution.py:80
  773.8 36.4 %collective-permute-start.47 = (bf16[144,1152]{1,0:T(8,128)(2,1)S(1)}, bf16[144,1152]{1,0:T(8,128)(2,1)S(1)}, u32[]{:S(2)}, u32[]{:S(2)}) collective-permute-start(bf16[144,1152]{1,0:T(8,128)(2,1)S(1)} %get-tuple-element.77), channel_id=1, source_target_pairs={{0,8},{4,12},{8,16},{12,20},{16,24},{20,28},{24,0},{28,4},{1,9},{5... | collective-permute-start | bytes 995336 | tf_op jit(solution)/shard_map/ppermute | solution.py:80
  776.9 87.1 %collective-permute-start.32 = (bf16[2,2,144,1152]{3,2,1,0:T(8,128)(2,1)}, bf16[2,2,144,1152]{3,2,1,0:T(8,128)(2,1)}, u32[]{:S(2)}, u32[]{:S(2)}) collective-permute-start(bf16[2,2,144,1152]{3,2,1,0:T(8,128)(2,1)} %dynamic-slice_bitcast_fusion.5), channel_id=1, source_target_pairs={{0,1},{1,0},{2,3},{3,2},{4,5},{5,4},{6,7},{7,6},{8,9},{9,8},{10,11... | collective-permute-start | bytes 3981320 | tf_op jit(solution)/shard_map/ppermute | solution.py:85
  779.8 86.6 %collective-permute-start.34 = (bf16[2,2,144,1152]{3,2,1,0:T(8,128)(2,1)}, bf16[2,2,144,1152]{3,2,1,0:T(8,128)(2,1)}, u32[]{:S(2)}, u32[]{:S(2)}) collective-permute-start(bf16[2,2,144,1152]{3,2,1,0:T(8,128)(2,1)} %dynamic-slice_bitcast_fusion.4), channel_id=1, source_target_pairs={{0,2},{1,3},{2,0},{3,1},{4,6},{5,7},{6,4},{7,5},{8,10},{9,11},{10,... | collective-permute-start | bytes 3981320 | tf_op jit(solution)/shard_map/ppermute | solution.py:85
  811.2 159.5 %all-gather.20.cloned.1.call-start = ((), (), s32[]{:S(2)}) async-start(), calls=%async_computation.11 | async-start | bytes 2985984 | tf_op jit(solution)/shard_map/all_gather | solution.py:201
  884.6 42.1 %collective-permute-start.38 = (bf16[144,1152]{1,0:T(8,128)(2,1)}, bf16[144,1152]{1,0:T(8,128)(2,1)}, u32[]{:S(2)}, u32[]{:S(2)}) collective-permute-start(bf16[144,1152]{1,0:T(8,128)(2,1)} %get-tuple-element.76), channel_id=1, source_target_pairs={{0,24},{4,28},{8,0},{12,4},{16,8},{20,12},{24,16},{28,20},{1,25},{... | collective-permute-start | bytes 995336 | tf_op jit(solution)/shard_map/ppermute | solution.py:80
  884.6 42.1 %collective-permute-start.37 = (bf16[144,1152]{1,0:T(8,128)(2,1)}, bf16[144,1152]{1,0:T(8,128)(2,1)}, u32[]{:S(2)}, u32[]{:S(2)}) collective-permute-start(bf16[144,1152]{1,0:T(8,128)(2,1)} %get-tuple-element.75), channel_id=1, source_target_pairs={{0,16},{4,20},{8,24},{12,28},{16,0},{20,4},{24,8},{28,12},{1,17},{... | collective-permute-start | bytes 995336 | tf_op jit(solution)/shard_map/ppermute | solution.py:80
  885.6 41.1 %collective-permute-start.36 = (bf16[144,1152]{1,0:T(8,128)(2,1)}, bf16[144,1152]{1,0:T(8,128)(2,1)}, u32[]{:S(2)}, u32[]{:S(2)}) collective-permute-start(bf16[144,1152]{1,0:T(8,128)(2,1)} %get-tuple-element.74), channel_id=1, source_target_pairs={{0,8},{4,12},{8,16},{12,20},{16,24},{20,28},{24,0},{28,4},{1,9},{5... | collective-permute-start | bytes 995336 | tf_op jit(solution)/shard_map/ppermute | solution.py:80
  (154 other events, 1559.8 us)
Sparse Core Ops, SparseCore 0:
  25.5 99.4 all-gather.9
  128.1 97.1 all-gather.11
  226.9 35.7 all-gather.13
  264.3 33.1 all-gather.15
  298.9 33.1 all-gather.17
  748.5 39.4 all-gather.23
  811.3 32.2 all-gather.21
  929.0 32.0 all-gather.19

commit v3 on v2

--- a/solution.py
+++ b/solution.py
@@ -131,10 +131,17 @@
     return all_rows.reshape(group, total, total)
 
 
+def tie(*values):
+    return lax.optimization_barrier(values)
+
+
 def gather_pieces(rows, group):
     ranks, at = lax.axis_size("fsdp"), lax.axis_index("fsdp")
     if ranks != group:
-        return gather_blocks(rows, group)
+        blocks = gather_blocks(rows, group)
+        (blocks,) = yield (blocks,)
+        yield blocks
+        return
     chips = lax.axis_size("dp") // 2
     core, chip = lax.axis_index("dp") % 2, lax.axis_index("dp") // 2
     chunk, total = rows.shape
@@ -146,12 +153,14 @@
     own = put(own, core_swap(line)[:, None], 0, 1 - core)
     own = own.reshape(2, total // 2, total)
     half = entry(own, core)
+    mine = [rank_swap(half, bits) for bits in range(1, ranks)]
+    own, *mine = yield (own, *mine)
+    others = [core_swap(part) for part in mine]
     found = put(jnp.zeros((ranks, 2, total // 2, total), rows.dtype), own, at)
     for bits in range(1, ranks):
-        mine = rank_swap(half, bits)
-        found = put(found, mine, at ^ bits, core)
-        found = put(found, core_swap(mine), at ^ bits, 1 - core)
-    return found.reshape(group, total, total)
+        found = put(found, mine[bits - 1], at ^ bits, core)
+        found = put(found, others[bits - 1], at ^ bits, 1 - core)
+    yield found.reshape(group, total, total)
 
 
 def gather_own(rows, group):
@@ -164,7 +173,7 @@
     return lax.all_gather(rows, "dp", axis=0, tiled=True)
 
 
-def scatter_blocks(product, left, group):
+def sum_blocks(product, left, group):
     ranks, dp_count = lax.axis_size("fsdp"), lax.axis_size("dp")
     shares = ranks // group
     total = left.shape[-1]
@@ -175,7 +184,10 @@
         rows = lax.psum_scatter(
             blocks.reshape(group * total, -1), ("fsdp", "dp"), scatter_dimension=0, tiled=True
         )
-        return gather_own(rows, group)
+        for _ in range(3):
+            (rows,) = yield (rows,)
+        yield gather_own(rows, group)
+        return
     chips, half = dp_count // 2, total // 2
     chunk = half // chips
     core, chip = lax.axis_index("dp") % 2, lax.axis_index("dp") // 2
@@ -188,18 +200,22 @@
     first, second = here[:, :, :cut], here[:, :, cut:]
     first_in = rank_swap(entry(first, 1 - low_bit, 1), 1)
     second_in = rank_swap(entry(second, 1 - high_bit, 0), 2)
+    here, first_in, second_in = yield (here, first_in, second_in)
+    first, second = here[:, :, :cut], here[:, :, cut:]
     first = narrow(wide(entry(first, low_bit, 1)) + wide(first_in))
     second = narrow(wide(entry(second, high_bit, 0)) + wide(second_in))
     first_in = rank_swap(entry(first, 1 - high_bit), 2)
     second_in = rank_swap(entry(second, 1 - low_bit), 1)
+    first, second, first_in, second_in = yield (first, second, first_in, second_in)
     first = narrow(wide(entry(first, high_bit)) + wide(first_in))
     second = narrow(wide(entry(second, low_bit)) + wide(second_in))
     line = jnp.concatenate([first, second])
-    rows = wide(entry(line, chip))
-    for step in range(1, chips):
-        rows = rows + wide(chip_shift(entry(line, (chip + step) % chips), step))
+    parts = [entry(line, chip)]
+    parts += [chip_shift(entry(line, (chip + step) % chips), step) for step in range(1, chips)]
+    parts = yield tuple(parts)
+    rows = sum(wide(part) for part in parts)
     found = lax.all_gather(narrow(rows), "dp", axis=0, tiled=True)
-    return found.reshape(chips, 2, chunk, -1).transpose(1, 0, 2, 3).reshape(total, -1)
+    yield found.reshape(chips, 2, chunk, -1).transpose(1, 0, 2, 3).reshape(total, -1)
 
 
 def fast_dot(subscripts, left, right):
@@ -259,8 +275,9 @@
 
     pieces = [slice(mod_count + group * piece, mod_count + group * (piece + 1)) for piece in range(3)]
     attn_w = gather_blocks(own_rows(narrow(weights[pieces[0]]), group), group)
-    one_w = gather_pieces(own_rows(narrow(weights[pieces[1]]), group), group)
     two_w = gather_blocks(own_rows(narrow(weights[pieces[2]]), group), group)
+    one_steps = gather_pieces(own_rows(narrow(weights[pieces[1]]), group), group)
+    one_parts = next(one_steps)
     left_rows = [own_rows(narrow(left_roots[piece]), group) for piece in pieces]
     right_wholes = [gather_own(own_rows(narrow(right_roots[piece]), group), group) for piece in pieces]
 
@@ -314,6 +331,8 @@
     proj = fast_dot("td,de->te", mixed_low, attn_w[3]) + bias_all[8 * width : 9 * width]
     proj_rows = proj.reshape(clip_count, row_count, width)
     resid = stream + valid * gate_one * proj_rows
+    resid, one_parts = tie(resid, one_parts)
+    one_w = one_steps.send(one_parts)
     mlp_in = modulate(resid, shift_two, scale_two).astype(jnp.bfloat16).reshape(token_count, width)
     pre = fast_dot("td,jde->jte", mlp_in, one_w) + bias_all[9 * width : 13 * width].reshape(
         4, 1, width
@@ -321,7 +340,8 @@
     hidden = gelu_tanh(pre).astype(jnp.bfloat16)
     grad_out = cotangent.astype(jnp.float32).reshape(clip_count, row_count, width)
     d_branch = (grad_out * valid * gate_two).astype(jnp.bfloat16).reshape(token_count, width)
-    whole_two = scatter_blocks(lambda left: fast_dot("jtd,te->jde", left, d_branch), hidden, group)
+    two_steps = sum_blocks(lambda left: fast_dot("jtd,te->jde", left, d_branch), hidden, group)
+    two_parts = next(two_steps)
     branch = fast_dot("jtd,jde->te", hidden, two_w) + bias_all[13 * width : 14 * width]
     branch_rows = branch.reshape(clip_count, row_count, width)
     block_out = (resid + valid * gate_two * branch_rows).astype(jnp.bfloat16).reshape(tokens.shape)
@@ -330,8 +350,13 @@
     d_hidden = fast_dot("te,jde->jtd", d_branch, two_w)
     gelu_value, gelu_pull = jax.vjp(gelu_tanh, pre)
     d_pre = gelu_pull(d_hidden)[0].astype(jnp.bfloat16)
-    whole_one = scatter_blocks(lambda left: fast_dot("td,jte->jde", left, d_pre), mlp_in, group)
+    d_pre, block_out, d_gate_two, two_parts = tie(d_pre, block_out, d_gate_two, two_parts)
+    two_parts = two_steps.send(two_parts)
+    one_steps = sum_blocks(lambda left: fast_dot("td,jte->jde", left, d_pre), mlp_in, group)
+    one_parts = list(next(one_steps))
     grad_b_one = jnp.sum(d_pre.astype(jnp.float32), axis=1).reshape(4 * width)
+    d_pre, one_parts[0], two_parts = tie(d_pre, one_parts[0], two_parts)
+    two_parts = two_steps.send(two_parts)
     d_mlp_in = fast_dot("jte,jde->td", d_pre, one_w).reshape(clip_count, row_count, width)
     mod_value, mod_pull = jax.vjp(modulate, resid, shift_two, scale_two)
     d_resid_norm, d_shift_two, d_scale_two = mod_pull(d_mlp_in)
@@ -339,10 +364,14 @@
     d_proj = (d_resid * valid * gate_one).astype(jnp.bfloat16).reshape(token_count, width)
     d_gate_one = jnp.sum(d_resid * valid * proj_rows, axis=1, keepdims=True)
     grad_b_out = jnp.sum(d_proj.astype(jnp.float32), axis=0)
-    d_proj, right_wholes[2] = lax.optimization_barrier((d_proj, right_wholes[2]))
     d_mixed = fast_dot("te,de->td", d_proj, attn_w[3]).reshape(
         seq_count, frame_count, HEADS, head_dim
     )
+    d_mixed, one_parts, two_parts, right_wholes[2] = tie(
+        d_mixed, one_parts, two_parts, right_wholes[2]
+    )
+    one_parts = one_steps.send(one_parts)
+    whole_two = two_steps.send(two_parts)
     d_query, d_keys, d_values = attention_backward(
         query_rows, key_rows, value_rows, key_keep, log_totals, d_mixed
     )
@@ -354,11 +383,12 @@
         ],
         axis=0,
     ).astype(jnp.bfloat16)
-    d_qkv, right_wholes[1], right_wholes[0] = lax.optimization_barrier(
-        (d_qkv, right_wholes[1], right_wholes[0])
-    )
+    d_qkv, one_parts, right_wholes[1], right_wholes[0] = tie(
+        d_qkv, one_parts, right_wholes[1], right_wholes[0]
+    )
+    one_parts = one_steps.send(one_parts)
     qkv_sums = jnp.sum(d_qkv.astype(jnp.float32), axis=1)
-    whole_attn = scatter_blocks(
+    attn_steps = sum_blocks(
         lambda left: jnp.concatenate(
             [
                 fast_dot("td,jte->jde", left[0], d_qkv),
@@ -368,10 +398,18 @@
         jnp.stack([attn_in, mixed_low]),
         group,
     )
+    attn_parts = list(next(attn_steps))
+    d_qkv, attn_parts[0] = tie(d_qkv, attn_parts[0])
     d_attn_in = fast_dot("jte,jde->td", d_qkv, attn_w[0:3]).reshape(clip_count, row_count, width)
     first_value, first_pull = jax.vjp(modulate, stream, shift_one, scale_one)
     d_stream_norm, d_shift_one, d_scale_one = first_pull(d_attn_in)
     input_grad = (d_resid + d_stream_norm).astype(jnp.bfloat16).reshape(tokens.shape)
+
+    d_shift_one, d_scale_one, input_grad, attn_parts, one_parts = tie(
+        d_shift_one, d_scale_one, input_grad, attn_parts, one_parts
+    )
+    attn_parts = attn_steps.send(attn_parts)
+    whole_one = one_steps.send(one_parts)
 
     d_mods = jnp.concatenate(
         [d_shift_one, d_scale_one, d_gate_one, d_shift_two, d_scale_two, d_gate_two], axis=1
@@ -400,6 +438,10 @@
         axis=1,
     )
     from_rows = lax.all_to_all(to_rows, "dp", 0, 0, tiled=True)
+    products_two = owned_step(whole_two, left_rows[2], right_wholes[2], group)
+    from_rows, products_two, attn_parts = tie(from_rows, products_two, attn_parts)
+    attn_parts = attn_steps.send(attn_parts)
+    back_two = shard_rows(products_two, group)
     bias_grad = jnp.sum(from_rows[:, mod_size:], axis=0)
     mod_grad_cols = from_rows[:, :mod_size].reshape(all_clips, mod_count, col_part)
     mod_grad = lax.all_gather(mod_grad_cols, "fsdp", axis=2, tiled=True)
@@ -408,8 +450,6 @@
     right_parts = jnp.einsum(
         "cjk,jke->cje", mod_grad_rows, right_roots[:mod_count], precision=precise
     )
-    mod_right = jnp.sum(lax.all_gather(right_parts, "dp", axis=0), axis=0)
-    ada_pre = jnp.einsum("jrc,cje->jre", left_cond, mod_right, precision=precise)
     cond_wide = wide(cond_all)
     cond_row_wide = wide(cond_rows)
     mod_gram = jnp.einsum("cjk,bjk->jcb", mod_grad, mod_grad, precision=precise)
@@ -419,8 +459,12 @@
     cond_side = jnp.einsum("cb,bje->jce", cond_gram, mod_grad_cols, precision=precise)
     ada_right = jnp.einsum("cjr,jce->jre", mod_grad_rows, cond_side, precision=precise)
 
-    back_two = shard_rows(owned_step(whole_two, left_rows[2], right_wholes[2], group), group)
-    back_one = shard_rows(owned_step(whole_one, left_rows[1], right_wholes[1], group), group)
+    products_one = owned_step(whole_one, left_rows[1], right_wholes[1], group)
+    products_one, right_parts, attn_parts = tie(products_one, right_parts, attn_parts)
+    whole_attn = attn_steps.send(attn_parts)
+    back_one = shard_rows(products_one, group)
+    mod_right = jnp.sum(lax.all_gather(right_parts, "dp", axis=0), axis=0)
+    ada_pre = jnp.einsum("jrc,cje->jre", left_cond, mod_right, precision=precise)
     back_attn = shard_rows(owned_step(whole_attn, left_rows[0], right_wholes[0], group), group)
 
     def joined(at, ada):

time: 1060 us -> 911 us (0.86)
  waiting for transfers between devices: 208 us -> 127 us
  local copies, waits for them, and re-layouts: 267 us -> 227 us
  starting transfers between devices: 99.4 us -> 122 us
  matrix products: 226 us -> 206 us
  other arithmetic: 121 us -> 103 us
    ppermute x42, waiting for transfers between devices: 144 us -> 62.7 us  [rank_swap(): return lax.ppermute(array, 'fsdp', [(at, at ^ bits) for at in range(count)])]
    ppermute x12, starting transfers between devices: 18.6 us -> 45.9 us  [chip_shift(): lax.ppermute(array, 'dp', [(at, (at + 2 * step) % count) for at in range(...]
    all_gather x1, blocking collectives: 38.2 us -> 17.7 us  [per_device(): mod_right = jnp.sum(lax.all_gather(right_parts, 'dp', axis=0), axis=0)]
    convert_element_type x3 -> x1, other arithmetic: 14.4 us -> 1.18 us  [per_device(): modulate(resid, shift_two, scale_two).astype(jnp.bfloat16)]
    optimization_barrier x0 -> x3, local copies, waits for them, and re-layouts: none -> 11.4 us  [tie(): return lax.optimization_barrier(values)]
    dot_general x32, matrix products: 149 us -> 138 us  [fast_dot(): jnp.einsum(subscripts, left, right, preferred_element_type=jnp.float32)]
    ppermute x12, waiting for transfers between devices: 48.1 us -> 37 us  [chip_shift(): lax.ppermute(array, 'dp', [(at, (at + 2 * step) % count) for at in range(...]
    unnamed x238 -> x300, local copies, waits for them, and re-layouts: 37.1 us -> 30 us
  transfers between devices with their start and end apart: 75 -> 75, of which waited for: 22 -> 27; matrix products, arithmetic and copies ran while one was open for 53% -> 53% of each run, Pallas kernels for 0% -> 0%
where the time goes in v3:
time: 911 us; the launch traced here: 898 us
  local copies, waits for them, and re-layouts  227 us (25%)
  matrix products  206 us (23%)
  waiting for transfers between devices  127 us (14%)
  starting transfers between devices  122 us (13%)
  other arithmetic  103 us (11%)
  blocking collectives  96.9 us (11%)
  between operations  16.7 us (2%)
    dot_general x32, matrix products, fast_dot(): jnp.einsum(subscripts, left, right, preferred_element_type=jnp.float32)  138 us
    ppermute x42, waiting for transfers between devices, rank_swap(): return lax.ppermute(array, 'fsdp', [(at, at ^ bits) for at in range(count)])  62.7 us
    all_gather x1, blocking collectives, per_device(): mod_grad = lax.all_gather(mod_grad_cols, 'fsdp', axis=2, tiled=True)  53 us
    ppermute x42, starting transfers between devices, rank_swap(): return lax.ppermute(array, 'fsdp', [(at, at ^ bits) for at in range(count)])  50.8 us
    ppermute x12, starting transfers between devices, chip_shift(): lax.ppermute(array, 'dp', [(at, (at + 2 * step) % count) for at in range(...  45.9 us
    ppermute x12, waiting for transfers between devices, chip_shift(): lax.ppermute(array, 'dp', [(at, (at + 2 * step) % count) for at in range(...  37 us
    unnamed x300, local copies, waits for them, and re-layouts  30 us
    convert_element_type x17, other arithmetic, narrow(): return array.astype(jnp.bfloat16)  27.1 us
  transfers between devices with their start and end apart: 75, of which 27 were waited for; matrix products, arithmetic and copies ran while one was open for 53% of the time, Pallas kernels for 0%

profile of v3, /device:TPU:0, one launch (start us, length us, event | category | flops | bytes accessed | tf_op | source)
XLA Modules:
  0.0 898.0 jit_solution(7541160575660110104)
XLA Ops:
  40.0 14.3 %all_gather.40 = bf16[256,128]{1,0:T(8,128)(2,1)S(1)} all-gather(bf16[32,128]{1,0:T(8,128)(2,1)S(1)} %fusion.224), channel_id=1, replica_groups=mesh['dp'=8,'fsdp'=4] {'dp'}, dimensions={0}, use_global_device_ids=true | all-gather | bytes 73728 | tf_op jit(solution)/shard_map/all_gather | solution.py:285
  92.1 11.9 %all_gather.41 = f32[672,128]{1,0:T(8,128)S(1)} all-gather(f32[168,128]{1,0:T(8,128)S(1)} %pad_bitcast_fusion), channel_id=1, replica_groups=mesh['dp'=8,'fsdp'=4] {'fsdp'}, dimensions={0}, use_global_device_ids=true | all-gather | bytes 430080 | tf_op jit(solution)/shard_map/all_gather | solution.py:297
  108.7 14.6 %collective-permute-done.10 = bf16[144,1152]{1,0:T(8,128)(2,1)} collective-permute-done((bf16[144,1152]{1,0:T(8,128)(2,1)S(1)}, bf16[144,1152]{1,0:T(8,128)(2,1)}, u32[]{:S(2)}, u32[]{:S(2)}) %collective-permute-start.10) | collective-permute-done | bytes 331808 | tf_op jit(solution)/shard_map/ppermute | solution.py:80
  138.5 6.0 all-gather.12.cloned.1.call-done
  144.5 7.0 slice.306
  151.5 7.8 convolution_add_fusion
  161.9 6.2 reshape_squeeze.11
  168.1 6.2 reshape_squeeze.10
  179.9 13.0 %fusion.246 = (f32[32,16,16]{2,1,0:T(8,128)S(1)}, f32[32,16,16,16]{2,3,1,0:T(8,128)S(1)}) fusion(f32[32,16,16,72]{3,2,1,0:T(8,128)} %reshape_squeeze.11, f32[32,16,16,72]{3,2,1,0:T(8,128)} %reshape_squeeze.10, pred[32,16]{1,0:T(8,128)(4,1)S(1)} %bitcast.769), kind=kOutput, calls=%fused_computation.500 | convolution fusion | flops 113631232 | bytes 5276160 | tf_op jit(solution)/shard_map/sfhd,sghd->shfg/dot_general | solution.py:35
  196.8 8.0 convert_bitcast_fusion.3
  241.5 14.2 %fusion.9 = (bf16[4,512,1152]{1,2,0:T(8,128)(2,1)S(1)}, f32[4,1152,512]{2,1,0:T(8,128)}) fusion(f32[4,1152]{1,0:T(4,128)S(1)} %copy-done.121, bf16[4,1152,1152]{2,1,0:T(8,128)(2,1)} %bitcast.729, bf16[512,1152,1]{1,0,2:T(8,128)(2,1)S(1)} %bitcast.750), kind=kOutput, calls=%fused_computation.16 | convolution fusion | flops 5459410944 | bytes 25970688 | tf_op jit(solution)/shard_map/td,jde->jte/dot_general | solution.py:222
  262.9 10.6 %fusion.36 = f32[512,1152]{1,0:T(8,128)S(1)} fusion(bf16[4,512,1152]{1,2,0:T(8,128)(2,1)} %copy-done.135, bf16[4,1152,1152]{2,1,0:T(8,128)(2,1)} %bitcast.770, f32[1152]{0:T(1024)} %get-tuple-element.249), kind=kOutput, calls=%fused_computation.66 | convolution fusion | flops 5436407808 | bytes 17699328 | tf_op jit(solution)/shard_map/jtd,jde->te/dot_general | solution.py:222
  276.1 6.5 add_convert_fusion
  286.5 17.0 %fusion.8 = bf16[4,512,1152]{1,2,0:T(8,128)(2,1)S(1)} fusion(bf16[4,1152,1152]{2,1,0:T(8,128)(2,1)} %bitcast.771, bf16[512,1152,1]{1,0,2:T(8,128)(2,1)S(1)} %bitcast.748, f32[4,1152,512]{2,1,0:T(8,128)} %get-tuple-element.267, f32[4,1152]{1,0:T(4,128)S(1)} %copy-done.122), kind=kOutput, calls=%fused_computation.13 | convolution fusion | flops 5485363200 | bytes 25970688 | tf_op jit(solution)/shard_map/te,jde->jtd/dot_general | solution.py:222
  303.5 12.9 %collective-permute-done.20 = bf16[2,2,144,1152]{3,2,1,0:T(8,128)(2,1)S(1)} collective-permute-done((bf16[2,2,144,1152]{3,2,1,0:T(8,128)(2,1)S(1)}, bf16[2,2,144,1152]{3,2,1,0:T(8,128)(2,1)S(1)}, u32[]{:S(2)}, u32[]{:S(2)}) %collective-permute-start.20) | collective-permute-done | bytes 1327136 | tf_op jit(solution)/shard_map/ppermute | solution.py:85
  377.4 7.1 fusion.1
  391.7 13.6 %multiply_reduce_fusion.1 = (f32[2,1152]{1,0:T(2,128)}, f32[2,256]{1,0:T(2,128)S(1)}, f32[2,1152]{1,0:T(2,128)}, f32[2,256,1152]{2,1,0:T(8,128)}) fusion(f32[2,256,1152]{2,1,0:T(8,128)S(1)} %bitcast_add_fusion.1, f32[2,256]{1,0:T(2,128)S(1)} %copy-done.124, f32[2,256]{1,0:T(2,128)S(1)} %copy-done.116, f32[2,1152]{1,0:T(2,128)S(1)} %copy-done.105, ...), kind=kOutput, calls=%fused_computation.113 | convolution fusion | flops 5440531456 | bytes 20087808 | tf_op jit(solution)/shard_map/jte,jde->td/dot_general | solution.py:222
  414.0 21.4 %collective-permute-start.27 = (bf16[144,1152]{1,0:T(8,128)(2,1)}, bf16[144,1152]{1,0:T(8,128)(2,1)}, u32[]{:S(2)}, u32[]{:S(2)}) collective-permute-start(bf16[144,1152]{1,0:T(8,128)(2,1)} %get-tuple-element.182), channel_id=1, source_target_pairs={{0,8},{4,12},{8,16},{12,20},{16,24},{20,28},{24,0},{28,4},{1,9},{5... | collective-permute-start | bytes 995336 | tf_op jit(solution)/shard_map/ppermute | solution.py:80
  448.7 11.2 %collective-permute-done.28 = bf16[144,1152]{1,0:T(8,128)(2,1)} collective-permute-done((bf16[144,1152]{1,0:T(8,128)(2,1)}, bf16[144,1152]{1,0:T(8,128)(2,1)}, u32[]{:S(2)}, u32[]{:S(2)}) %collective-permute-start.28) | collective-permute-done | bytes 331808 | tf_op jit(solution)/shard_map/ppermute | solution.py:80
  473.4 13.3 %multiply_reduce_fusion = (f32[32,16,16]{2,1,0:T(8,128)S(1)}, f32[32,16,16,16]{2,3,1,0:T(8,128)S(1)}) fusion(f32[32,16,16,16]{2,3,1,0:T(8,128)} %copy-done, f32[32,16,16]{2,1,0:T(8,128)S(1)} %copy-done.26, f32[32,16,16,72]{3,1,2,0:T(8,128)} %fusion.247, f32[32,16,16,72]{3,2,1,0:T(8,128)} %reshape_squeeze.9), kind=kOutput, calls=%fused_computation.34 | convolution fusion | flops 113631232 | bytes 5832704 | tf_op jit(solution)/shard_map/sfhd,sghd->shfg/dot_general | solution.py:51
  486.8 6.8 convert_bitcast_fusion.1
  493.5 9.0 %convert_bitcast_fusion.2 = bf16[32,16,16,72]{3,1,2,0:T(8,128)(2,1)} fusion(f32[32,16,16,72]{3,2,1,0:T(8,128)S(1)} %copy-done.3, f32[32,16,16,16]{2,3,1,0:T(8,128)S(1)} %get-tuple-element.270, f32[32,16,16,16]{2,3,1,0:T(8,128)S(1)} %copy-done.1, f32[32,16,16]{2,1,0:T(8,128)S(1)} %get-tuple-element.269, f32[32,16,16]{2,1,0:T(8,128)S(1)} %copy-done.26), kind=kOutput, calls=%fused_computation.139 | convolution fusion | flops 114360320 | bytes 4653056 | tf_op jit(solution)/shard_map/shfg,sghd->sfhd/dot_general | solution.py:55
  574.6 7.6 collective-permute-start.44
  586.1 5.5 convolution_bitcast_fusion
  599.6 9.0 fusion
  612.1 8.3 multiply_reduce_fusion.3
  626.6 24.0 %collective-permute-done.42 = bf16[2,2,144,1152]{3,2,1,0:T(8,128)(2,1)S(1)} collective-permute-done((bf16[2,2,144,1152]{3,2,1,0:T(8,128)(2,1)S(1)}, bf16[2,2,144,1152]{3,2,1,0:T(8,128)(2,1)S(1)}, u32[]{:S(2)}, u32[]{:S(2)}) %collective-permute-start.42) | collective-permute-done | bytes 1327136 | tf_op jit(solution)/shard_map/ppermute | solution.py:85
  693.8 7.3 all-to-all-done.2
  703.6 53.0 %all_gather.47 = f32[16,6,1152]{0,1,2:T(8,128)} all-gather(f32[16,6,288]{0,1,2:T(8,128)} %copy.171), channel_id=1, replica_groups=mesh['dp'=8,'fsdp'=4] {'fsdp'}, dimensions={2}, use_global_device_ids=true | all-gather | bytes 552960 | tf_op jit(solution)/shard_map/all_gather | solution.py:447
  777.4 10.9 %collective-permute-done.59 = bf16[144,1152]{1,0:T(8,128)(2,1)} collective-permute-done((bf16[144,1152]{1,0:T(8,128)(2,1)}, bf16[144,1152]{1,0:T(8,128)(2,1)}, u32[]{:S(2)}, u32[]{:S(2)}) %collective-permute-start.59) | collective-permute-done | bytes 331808 | tf_op jit(solution)/shard_map/ppermute | solution.py:80
  806.4 8.7 all-to-all-done.5
  849.8 17.7 %all-gather = f32[128,6,288]{2,0,1:T(8,128)S(1)} all-gather(f32[16,6,288]{2,0,1:T(8,128)S(1)} %copy-done.81), channel_id=2, replica_groups=mesh['dp'=8,'fsdp'=4] {'dp'}, dimensions={0}, use_global_device_ids=true | all-gather | bytes 995328 | tf_op jit(solution)/shard_map/all_gather | solution.py:466
  (728 shorter events, 490.8 us)
Async XLA Ops:
  7.2 137.3 %all-gather.12.cloned.1.call-start = ((), (), s32[]{:S(2)}) async-start(), calls=%async_computation.7 | async-start | bytes 10948608 | tf_op jit(solution)/shard_map/all_gather | solution.py:128
  30.5 232.4 %all-gather.10.cloned.1.call-start = ((), (), s32[]{:S(2)}) async-start(), calls=%async_computation.6 | async-start | bytes 10948608 | tf_op jit(solution)/shard_map/all_gather | solution.py:128
  55.4 35.6 %all-to-all-start = ((f32[16,6,288]{2,1,0:T(8,128)}), f32[16,6,288]{2,1,0:T(8,128)S(1)}, u32[]{:S(2)}, u32[]{:S(2)}) async-start(f32[16,6,288]{2,1,0:T(8,128)} %copy.132), calls=%async_computation | async-start | bytes 393216 | tf_op jit(solution)/shard_map/all_to_all | solution.py:293
  60.1 388.6 %all-gather.14.cloned.1.call-start = ((), (), s32[]{:S(2)}) async-start(), calls=%async_computation.8 | async-start | bytes 2985984 | tf_op jit(solution)/shard_map/all_gather | solution.py:173
  82.1 24.9 %collective-permute-start.9 = (bf16[144,1152]{1,0:T(8,128)(2,1)S(1)}, bf16[144,1152]{1,0:T(8,128)(2,1)}, u32[]{:S(2)}, u32[]{:S(2)}) collective-permute-start(bf16[144,1152]{1,0:T(8,128)(2,1)S(1)} %concatenate.91), channel_id=1, source_target_pairs={{0,8},{4,12},{8,16},{12,20},{16,24},{20,28},{24,0},{28,4},{1,9},{5... | collective-permute-start | bytes 995336 | tf_op jit(solution)/shard_map/ppermute | solution.py:80
  84.1 39.2 %collective-permute-start.10 = (bf16[144,1152]{1,0:T(8,128)(2,1)S(1)}, bf16[144,1152]{1,0:T(8,128)(2,1)}, u32[]{:S(2)}, u32[]{:S(2)}) collective-permute-start(bf16[144,1152]{1,0:T(8,128)(2,1)S(1)} %concatenate.91), channel_id=1, source_target_pairs={{0,16},{4,20},{8,24},{12,28},{16,0},{20,4},{24,8},{28,12},{1,17},{... | collective-permute-start | bytes 995336 | tf_op jit(solution)/shard_map/ppermute | solution.py:80
  86.5 38.9 %collective-permute-start.11 = (bf16[144,1152]{1,0:T(8,128)(2,1)S(1)}, bf16[144,1152]{1,0:T(8,128)(2,1)}, u32[]{:S(2)}, u32[]{:S(2)}) collective-permute-start(bf16[144,1152]{1,0:T(8,128)(2,1)S(1)} %concatenate.91), channel_id=1, source_target_pairs={{0,24},{4,28},{8,0},{12,4},{16,8},{20,12},{24,16},{28,20},{1,25},{... | collective-permute-start | bytes 995336 | tf_op jit(solution)/shard_map/ppermute | solution.py:80
  90.9 442.5 %all-gather.16.cloned.1.call-start = ((), (), s32[]{:S(2)}) async-start(), calls=%async_computation.9 | async-start | bytes 2985984 | tf_op jit(solution)/shard_map/all_gather | solution.py:173
  135.0 80.4 %collective-permute-start.13 = (bf16[576,1152]{1,0:T(8,128)(2,1)}, bf16[576,1152]{1,0:T(8,128)(2,1)}, u32[]{:S(2)}, u32[]{:S(2)}) collective-permute-start(bf16[576,1152]{1,0:T(8,128)(2,1)} %dynamic-slice_bitcast_fusion.6), channel_id=1, source_target_pairs={{0,1},{1,0},{2,3},{3,2},{4,5},{5,4},{6,7},{7,6},{8,9},{9,8},{10,11... | collective-permute-start | bytes 3981320 | tf_op jit(solution)/shard_map/ppermute | solution.py:85
  135.5 79.9 %collective-permute-start.14 = (bf16[576,1152]{1,0:T(8,128)(2,1)}, bf16[576,1152]{1,0:T(8,128)(2,1)}, u32[]{:S(2)}, u32[]{:S(2)}) collective-permute-start(bf16[576,1152]{1,0:T(8,128)(2,1)} %dynamic-slice_bitcast_fusion.6), channel_id=1, source_target_pairs={{0,2},{1,3},{2,0},{3,1},{4,6},{5,7},{6,4},{7,5},{8,10},{9,11},{10,... | collective-permute-start | bytes 3981320 | tf_op jit(solution)/shard_map/ppermute | solution.py:85
  136.9 78.5 %collective-permute-start.15 = (bf16[576,1152]{1,0:T(8,128)(2,1)}, bf16[576,1152]{1,0:T(8,128)(2,1)}, u32[]{:S(2)}, u32[]{:S(2)}) collective-permute-start(bf16[576,1152]{1,0:T(8,128)(2,1)} %dynamic-slice_bitcast_fusion.6), channel_id=1, source_target_pairs={{0,3},{1,2},{2,1},{3,0},{4,7},{5,6},{6,5},{7,4},{8,11},{9,10},{10,... | collective-permute-start | bytes 3981320 | tf_op jit(solution)/shard_map/ppermute | solution.py:85
  262.8 270.6 %all-gather.18.cloned.1.call-start = ((), (), s32[]{:S(2)}) async-start(), calls=%async_computation.10 | async-start | bytes 2985984 | tf_op jit(solution)/shard_map/all_gather | solution.py:173
  285.0 31.4 %collective-permute-start.20 = (bf16[2,2,144,1152]{3,2,1,0:T(8,128)(2,1)S(1)}, bf16[2,2,144,1152]{3,2,1,0:T(8,128)(2,1)S(1)}, u32[]{:S(2)}, u32[]{:S(2)}) collective-permute-start(bf16[2,2,144,1152]{3,2,1,0:T(8,128)(2,1)S(1)} %dynamic-slice_bitcast_fusion.5), channel_id=1, source_target_pairs={{0,1},{1,0},{2,3},{3,2},{4,5},{5,4},{6,7},{7,6},{8,9},{9,8},{10,11... | collective-permute-start | bytes 3981320 | tf_op jit(solution)/shard_map/ppermute | solution.py:85
  285.2 31.4 %collective-permute-start.21 = (bf16[2,2,144,1152]{3,2,1,0:T(8,128)(2,1)S(1)}, bf16[2,2,144,1152]{3,2,1,0:T(8,128)(2,1)S(1)}, u32[]{:S(2)}, u32[]{:S(2)}) collective-permute-start(bf16[2,2,144,1152]{3,2,1,0:T(8,128)(2,1)S(1)} %dynamic-slice_bitcast_fusion.4), channel_id=1, source_target_pairs={{0,2},{1,3},{2,0},{3,1},{4,6},{5,7},{6,4},{7,5},{8,10},{9,11},{10,... | collective-permute-start | bytes 3981320 | tf_op jit(solution)/shard_map/ppermute | solution.py:85
  321.7 55.7 %collective-permute-start.22 = (bf16[4,576,1152]{2,1,0:T(8,128)(2,1)}, bf16[4,576,1152]{2,1,0:T(8,128)(2,1)}, u32[]{:S(2)}, u32[]{:S(2)}) collective-permute-start(bf16[4,576,1152]{2,1,0:T(8,128)(2,1)} %fusion.16), channel_id=1, source_target_pairs={{0,4},{4,0},{8,12},{12,8},{16,20},{20,16},{24,28},{28,24},{1,5},{5... | collective-permute-start | bytes 15925256 | tf_op jit(solution)/shard_map/ppermute | solution.py:75
  342.8 248.9 %all-gather.20.cloned.1.call-start = ((), (), s32[]{:S(2)}) async-start(), calls=%async_computation.11 | async-start | bytes 2985984 | tf_op jit(solution)/shard_map/all_gather | solution.py:217
  406.4 53.5 %collective-permute-start.25 = (bf16[2,2,144,1152]{3,2,1,0:T(8,128)(2,1)}, bf16[2,2,144,1152]{3,2,1,0:T(8,128)(2,1)}, u32[]{:S(2)}, u32[]{:S(2)}) collective-permute-start(bf16[2,2,144,1152]{3,2,1,0:T(8,128)(2,1)} %dynamic-slice_bitcast_fusion.3), channel_id=1, source_target_pairs={{0,1},{1,0},{2,3},{3,2},{4,5},{5,4},{6,7},{7,6},{8,9},{9,8},{10,11... | collective-permute-start | bytes 3981320 | tf_op jit(solution)/shard_map/ppermute | solution.py:85
  409.3 50.6 %collective-permute-start.26 = (bf16[2,2,144,1152]{3,2,1,0:T(8,128)(2,1)}, bf16[2,2,144,1152]{3,2,1,0:T(8,128)(2,1)}, u32[]{:S(2)}, u32[]{:S(2)}) collective-permute-start(bf16[2,2,144,1152]{3,2,1,0:T(8,128)(2,1)} %dynamic-slice_bitcast_fusion.2), channel_id=1, source_target_pairs={{0,2},{1,3},{2,0},{3,1},{4,6},{5,7},{6,4},{7,5},{8,10},{9,11},{10,... | collective-permute-start | bytes 3981320 | tf_op jit(solution)/shard_map/ppermute | solution.py:85
  414.0 34.7 %collective-permute-start.27 = (bf16[144,1152]{1,0:T(8,128)(2,1)}, bf16[144,1152]{1,0:T(8,128)(2,1)}, u32[]{:S(2)}, u32[]{:S(2)}) collective-permute-start(bf16[144,1152]{1,0:T(8,128)(2,1)} %get-tuple-element.182), channel_id=1, source_target_pairs={{0,8},{4,12},{8,16},{12,20},{16,24},{20,28},{24,0},{28,4},{1,9},{5... | collective-permute-start | bytes 995336 | tf_op jit(solution)/shard_map/ppermute | solution.py:80
  466.7 66.7 %collective-permute-start.33 = (bf16[2,144,1152]{2,1,0:T(8,128)(2,1)}, bf16[2,144,1152]{2,1,0:T(8,128)(2,1)}, u32[]{:S(2)}, u32[]{:S(2)}) collective-permute-start(bf16[2,144,1152]{2,1,0:T(8,128)(2,1)} %dynamic-slice_bitcast_fusion.10), channel_id=1, source_target_pairs={{0,2},{1,3},{2,0},{3,1},{4,6},{5,7},{6,4},{7,5},{8,10},{9,11},{10,... | collective-permute-start | bytes 1990664 | tf_op jit(solution)/shard_map/ppermute | solution.py:85
  470.2 63.2 %collective-permute-start.34 = (bf16[2,144,1152]{2,1,0:T(8,128)(2,1)}, bf16[2,144,1152]{2,1,0:T(8,128)(2,1)}, u32[]{:S(2)}, u32[]{:S(2)}) collective-permute-start(bf16[2,144,1152]{2,1,0:T(8,128)(2,1)} %dynamic-slice_bitcast_fusion.9), channel_id=1, source_target_pairs={{0,1},{1,0},{2,3},{3,2},{4,5},{5,4},{6,7},{7,6},{8,9},{9,8},{10,11... | collective-permute-start | bytes 1990664 | tf_op jit(solution)/shard_map/ppermute | solution.py:85
  529.9 240.3 %all-gather.22.cloned.1.call-start = ((), (), s32[]{:S(2)}) async-start(), calls=%async_computation.12 | async-start | bytes 2985984 | tf_op jit(solution)/shard_map/all_gather | solution.py:217
  540.9 58.7 %collective-permute-start.41 = (bf16[4,576,1152]{2,1,0:T(8,128)(2,1)}, bf16[4,576,1152]{2,1,0:T(8,128)(2,1)}, u32[]{:S(2)}, u32[]{:S(2)}) collective-permute-start(bf16[4,576,1152]{2,1,0:T(8,128)(2,1)} %pad_maximum_fusion), channel_id=1, source_target_pairs={{0,4},{4,0},{8,12},{12,8},{16,20},{20,16},{24,28},{28,24},{1,5},{5... | collective-permute-start | bytes 15925256 | tf_op jit(solution)/shard_map/ppermute | solution.py:75
  574.6 51.9 %collective-permute-start.44 = (bf16[144,1152]{1,0:T(8,128)(2,1)}, bf16[144,1152]{1,0:T(8,128)(2,1)S(1)}, u32[]{:S(2)}, u32[]{:S(2)}) collective-permute-start(bf16[144,1152]{1,0:T(8,128)(2,1)} %get-tuple-element.178), channel_id=1, source_target_pairs={{0,8},{4,12},{8,16},{12,20},{16,24},{20,28},{24,0},{28,4},{1,9},{5... | collective-permute-start | bytes 995336 | tf_op jit(solution)/shard_map/ppermute | solution.py:80
  582.2 44.3 %collective-permute-start.45 = (bf16[144,1152]{1,0:T(8,128)(2,1)}, bf16[144,1152]{1,0:T(8,128)(2,1)S(1)}, u32[]{:S(2)}, u32[]{:S(2)}) collective-permute-start(bf16[144,1152]{1,0:T(8,128)(2,1)} %get-tuple-element.179), channel_id=1, source_target_pairs={{0,16},{4,20},{8,24},{12,28},{16,0},{20,4},{24,8},{28,12},{1,17},{... | collective-permute-start | bytes 995336 | tf_op jit(solution)/shard_map/ppermute | solution.py:80
  582.2 44.3 %collective-permute-start.46 = (bf16[144,1152]{1,0:T(8,128)(2,1)}, bf16[144,1152]{1,0:T(8,128)(2,1)S(1)}, u32[]{:S(2)}, u32[]{:S(2)}) collective-permute-start(bf16[144,1152]{1,0:T(8,128)(2,1)} %get-tuple-element.176), channel_id=1, source_target_pairs={{0,24},{4,28},{8,0},{12,4},{16,8},{20,12},{24,16},{28,20},{1,25},{... | collective-permute-start | bytes 995336 | tf_op jit(solution)/shard_map/ppermute | solution.py:80
  620.6 30.0 %collective-permute-start.42 = (bf16[2,2,144,1152]{3,2,1,0:T(8,128)(2,1)S(1)}, bf16[2,2,144,1152]{3,2,1,0:T(8,128)(2,1)S(1)}, u32[]{:S(2)}, u32[]{:S(2)}) collective-permute-start(bf16[2,2,144,1152]{3,2,1,0:T(8,128)(2,1)S(1)} %dynamic-slice_bitcast_fusion.1), channel_id=1, source_target_pairs={{0,1},{1,0},{2,3},{3,2},{4,5},{5,4},{6,7},{7,6},{8,9},{9,8},{10,11... | collective-permute-start | bytes 3981320 | tf_op jit(solution)/shard_map/ppermute | solution.py:85
  622.5 29.7 %collective-permute-start.43 = (bf16[2,2,144,1152]{3,2,1,0:T(8,128)(2,1)S(1)}, bf16[2,2,144,1152]{3,2,1,0:T(8,128)(2,1)S(1)}, u32[]{:S(2)}, u32[]{:S(2)}) collective-permute-start(bf16[2,2,144,1152]{3,2,1,0:T(8,128)(2,1)S(1)} %dynamic-slice_bitcast_fusion), channel_id=1, source_target_pairs={{0,2},{1,3},{2,0},{3,1},{4,6},{5,7},{6,4},{7,5},{8,10},{9,11},{10,... | collective-permute-start | bytes 3981320 | tf_op jit(solution)/shard_map/ppermute | solution.py:85
  691.7 136.5 %all-gather.24.cloned.1.call-start = ((), (), s32[]{:S(2)}) async-start(), calls=%async_computation.13 | async-start | bytes 2985984 | tf_op jit(solution)/shard_map/all_gather | solution.py:217
  763.5 24.9 %collective-permute-start.59 = (bf16[144,1152]{1,0:T(8,128)(2,1)}, bf16[144,1152]{1,0:T(8,128)(2,1)}, u32[]{:S(2)}, u32[]{:S(2)}) collective-permute-start(bf16[144,1152]{1,0:T(8,128)(2,1)} %get-tuple-element.175), channel_id=1, source_target_pairs={{0,16},{4,20},{8,24},{12,28},{16,0},{20,4},{24,8},{28,12},{1,17},{... | collective-permute-start | bytes 995336 | tf_op jit(solution)/shard_map/ppermute | solution.py:80
  819.1 27.0 %all-to-all-start.4 = ((bf16[4,3,144,288]{3,2,1,0:T(8,128)(2,1)}), bf16[4,3,144,288]{3,2,1,0:T(8,128)(2,1)}, u32[]{:S(2)}, u32[]{:S(2)}) async-start(bf16[4,3,144,288]{3,2,1,0:T(8,128)(2,1)} %copy.183), calls=%async_computation.4 | async-start | bytes 2654208 | tf_op jit(solution)/shard_map/all_to_all | solution.py:119
  846.1 27.4 %all-to-all-start.3 = ((bf16[4,3,144,288]{3,2,1,0:T(8,128)(2,1)}), bf16[4,3,144,288]{3,2,1,0:T(8,128)(2,1)S(1)}, u32[]{:S(2)}, u32[]{:S(2)}) async-start(bf16[4,3,144,288]{3,2,1,0:T(8,128)(2,1)} %copy.181), calls=%async_computation.3 | async-start | bytes 2654208 | tf_op jit(solution)/shard_map/all_to_all | solution.py:119
  (187 other events, 1888.8 us)
Sparse Core Ops, SparseCore 0:
  30.6 113.8 all-gather.11
  148.1 108.0 all-gather.9
  257.8 34.6 all-gather.13
  294.0 36.8 all-gather.15
  342.9 55.9 all-gather.17
  530.0 38.8 all-gather.19
  667.4 34.8 all-gather.21
  790.6 37.5 all-gather.23

commit v4 on v3

v4 whole, which is shorter than its diff:
```python
import functools
import math

import jax
import jax.numpy as jnp
from jax import lax
from jax.experimental import pallas as pl
from jax.experimental.pallas import tpu as pltpu
from jax.sharding import PartitionSpec as P

HEADS = 16


precise = lax.Precision.HIGHEST
norm_epsilon = 1e-06
masked_score = -1e30
stat_decay = 0.5
moment_decay = 0.9
weight_rate = 0.7
bias_rate = 0.1
diag_epsilon = 1e-08
vmem_bytes = 50 * 2**20


def narrow(array):
    return array.astype(jnp.bfloat16)


def wide(array):
    return array.astype(jnp.float32)


def spec(shape, index_map, **keywords):
    return pl.BlockSpec(shape, index_map, **keywords)


def held(shape):
    return pl.BlockSpec(shape, lambda step: (0,) * len(shape), pipeline_mode=pl.Buffered(1))


def column_cuts(total):
    cuts, at = [], 0
    while at < total:
        cuts.append((at, min(total, at + 256)))
        at += 256
    return cuts


def dot_nn(left, right):
    return lax.dot_general(left, right, (((1,), (0,)), ((), ())), preferred_element_type=jnp.float32)


def dot_nt(left, right):
    return lax.dot_general(left, right, (((1,), (1,)), ((), ())), preferred_element_type=jnp.float32)


def dot_tn(left, right):
    return lax.dot_general(left, right, (((0,), (0,)), ((), ())), preferred_element_type=jnp.float32)


def split_high(values):
    high = narrow(values)
    return high, narrow(values - wide(high))


def valid_rows(count, rows, frames):
    at = lax.broadcasted_iota(jnp.int32, (rows, 1), 0)
    return (lax.rem(at, frames) < count).astype(jnp.float32)


def score_offset(count, size, frames, key_axis):
    first = lax.broadcasted_iota(jnp.int32, (size, size), 0)
    second = lax.broadcasted_iota(jnp.int32, (size, size), 1)
    key = second if key_axis == 1 else first
    met = (lax.div(first, frames) == lax.div(second, frames)) & (lax.rem(key, frames) < count)
    return jnp.where(met, 0.0, masked_score)


def head_windows(width):
    size = width // HEADS
    windows = []
    for head in range(HEADS):
        low, high = head * size, (head + 1) * size
        start = low // 128 * 128
        stop = min(width, -(-high // 128) * 128)
        windows.append((low - start, high - start, start, stop))
    return windows


def lane_mask(low, high, count, dtype):
    lanes = lax.broadcasted_iota(jnp.int32, (1, count), 1)
    return ((lanes >= low) & (lanes < high)).astype(jnp.float32).astype(dtype)


def norm_parts(values):
    centered = values - jnp.mean(values, axis=-1, keepdims=True)
    variance = jnp.mean(centered * centered, axis=-1, keepdims=True)
    inverse = lax.rsqrt(variance + norm_epsilon)
    return centered * inverse, inverse


def norm_back(grad, normed, inverse):
    first = jnp.mean(grad, axis=-1, keepdims=True)
    second = jnp.mean(grad * normed, axis=-1, keepdims=True)
    return (grad - first - normed * second) * inverse


def column_sum(values):
    return jnp.sum(values, axis=0, keepdims=True)


def attention_kernel(
    frames,
    counts,
    tokens,
    cotangent,
    mods,
    bias,
    blocks,
    attn_in,
    parts,
    mixed_low,
    proj_out,
    resid_out,
    mlp_in,
    d_branch,
    d_branch_sum,
    mixed,
):
    rows, width = tokens.shape
    tile = min(rows, 128)
    count = counts[pl.program_id(0)]
    shift_one, scale_one, gate_one = (mods[0, at : at + 1, :] for at in range(3))
    shift_two, scale_two, gate_two = (mods[0, at : at + 1, :] for at in range(3, 6))
    for first in range(0, rows, tile):
        span = slice(first, first + tile)
        normed, _ = norm_parts(wide(tokens[span]))
        attn_in[span] = narrow(normed * (1.0 + scale_one) + shift_one)
        branch_back = narrow(wide(cotangent[span]) * valid_rows(count, tile, frames) * gate_two)
        d_branch[span] = branch_back
        part_sum = column_sum(wide(branch_back))
        d_branch_sum[0] = part_sum if first == 0 else d_branch_sum[0] + part_sum
    scale = (width // HEADS) ** -0.5
    source = attn_in[...]
    for low, high in column_cuts(width):
        span = slice(low, high)
        query = (dot_nn(source, blocks[0, :, span]) + bias[0:1, span]) * scale
        parts[0, :, span], parts[1, :, span] = split_high(query)
        parts[2, :, span], parts[3, :, span] = split_high(dot_nn(source, blocks[1, :, span]))
        parts[4, :, span] = narrow(dot_nn(source, blocks[2, :, span]) + bias[2:3, span])
    offset = score_offset(count, tile, frames, 1)
    mixed[...] = jnp.zeros_like(mixed)
    for first in range(0, rows, tile):
        span = slice(first, first + tile)
        for low, high, start, stop in head_windows(width):
            lanes = slice(start, stop)
            mask = lane_mask(low, high, stop - start, jnp.bfloat16)
            key_high = parts[2, span, lanes]
            query_high = parts[0, span, lanes] * mask
            scores = dot_nt(query_high, key_high)
            scores += dot_nt(parts[1, span, lanes] * mask, key_high)
            scores += dot_nt(query_high, parts[3, span, lanes]) + offset
            expons = jnp.exp(scores - jnp.max(scores, axis=-1, keepdims=True))
            probs = expons * (1.0 / jnp.sum(expons, axis=-1, keepdims=True))
            out = dot_nn(narrow(probs), parts[4, span, lanes] * mask)
            mixed[span, lanes] += out
    mixed_low[...] = narrow(mixed[...])
    source = mixed_low[...]
    for low, high in column_cuts(width):
        span = slice(low, high)
        proj_out[:, span] = dot_nn(source, blocks[3, :, span]) + bias[3:4, span]
    for first in range(0, rows, tile):
        span = slice(first, first + tile)
        resid = wide(tokens[span]) + valid_rows(count, tile, frames) * gate_one * proj_out[span]
        resid_out[span] = resid
        normed, _ = norm_parts(resid)
        mlp_in[span] = narrow(normed * (1.0 + scale_two) + shift_two)


def run_attention(frames, counts, tokens, cotangent, mods, bias, blocks):
    total, width = tokens.shape
    clips = mods.shape[0]
    rows = total // clips
    clip_rows = spec((rows, width), lambda clip: (clip, 0))
    low = jax.ShapeDtypeStruct((total, width), jnp.bfloat16)
    full = jax.ShapeDtypeStruct((total, width), jnp.float32)
    return pl.pallas_call(
        functools.partial(attention_kernel, frames),
        grid=(clips,),
        in_specs=[
            pl.BlockSpec(memory_space=pltpu.SMEM),
            clip_rows,
            clip_rows,
            spec((1,) + mods.shape[1:], lambda clip: (clip, 0, 0)),
            held(bias.shape),
            held(blocks.shape),
        ],
        out_specs=[
            clip_rows,
            spec((5, rows, width), lambda clip: (0, clip, 0)),
            clip_rows,
            clip_rows,
            clip_rows,
            clip_rows,
            clip_rows,
            spec((1, 1, width), lambda clip: (clip, 0, 0)),
        ],
        out_shape=[
            low,
            jax.ShapeDtypeStruct((5, total, width), jnp.bfloat16),
            low,
            full,
            full,
            low,
            low,
            jax.ShapeDtypeStruct((clips, 1, width), jnp.float32),
        ],
        scratch_shapes=[pltpu.VMEM((rows, width), jnp.float32)],
        compiler_params=pltpu.CompilerParams(vmem_limit_bytes=vmem_bytes),
        cost_estimate=pl.CostEstimate(
            flops=12 * total * width * width, bytes_accessed=40 * total * width, transcendentals=0
        ),
    )(counts, tokens, cotangent, mods, bias, blocks)


def hidden_kernel(mlp_in, block, bias, hidden, slope):
    root = (2.0 / math.pi) ** 0.5
    source = mlp_in[...]
    for low, high in column_cuts(block.shape[-1]):
        span = slice(low, high)
        pre = dot_nn(source, block[0, :, span]) + bias[0, :, span]
        square = pre * pre
        bent = jnp.tanh(root * pre * (1.0 + 0.044715 * square))
        half = 0.5 + 0.5 * bent
        hidden[0, :, span] = narrow(pre * half)
        steep = (0.5 * root) * pre * (1.0 + 3 * 0.044715 * square)
        slope[0, :, span] = narrow(half + steep * (1.0 - bent * bent))


def run_hidden(mlp_in, blocks, bias):
    total, width = mlp_in.shape
    count = blocks.shape[0]
    per_block = spec((1, total, width), lambda at: (at, 0, 0))
    out = jax.ShapeDtypeStruct((count, total, width), jnp.bfloat16)
    return pl.pallas_call(
        hidden_kernel,
        grid=(count,),
        in_specs=[
            held(mlp_in.shape),
            spec((1, width, width), lambda at: (at, 0, 0)),
            spec((1, 1, width), lambda at: (at, 0, 0)),
        ],
        out_specs=[per_block, per_block],
        out_shape=[out, out],
        compiler_params=pltpu.CompilerParams(vmem_limit_bytes=vmem_bytes),
        cost_estimate=pl.CostEstimate(
            flops=8 * total * width * width, bytes_accessed=30 * total * width, transcendentals=0
        ),
    )(mlp_in, blocks, bias)


def branch_kernel(
    frames,
    counts,
    hidden,
    slope,
    block,
    d_branch,
    bias,
    gates,
    resid,
    cotangent,
    d_pre,
    d_pre_sum,
    block_out,
    d_gate,
    branch,
):
    step, steps = pl.program_id(0), pl.num_programs(0)
    total, width = resid.shape
    clips = gates.shape[0]
    rows = total // clips
    source, back = hidden[0], d_branch[...]

    @pl.when(step == 0)
    def _():
        branch[...] = jnp.zeros_like(branch)

    for low, high in column_cuts(width):
        span = slice(low, high)
        d_hidden = dot_nt(back, block[0, span, :])
        low_back = narrow(d_hidden * wide(slope[0, :, span]))
        d_pre[0, :, span] = low_back
        d_pre_sum[0, :, span] = column_sum(wide(low_back))
        branch[:, span] += dot_nn(source, block[0, :, span])

    @pl.when(step == steps - 1)
    def _():
        for clip in range(clips):
            span = slice(clip * rows, (clip + 1) * rows)
            kept = valid_rows(counts[clip], rows, frames) * (branch[span] + bias[...])
            block_out[span] = narrow(resid[span] + gates[clip] * kept)
            d_gate[clip] = column_sum(wide(cotangent[span]) * kept)


def run_branch(frames, counts, hidden, slope, blocks, d_branch, bias, gates, resid, cotangent):
    count, total, width = hidden.shape
    clips = gates.shape[0]
    per_block = spec((1, total, width), lambda at: (at, 0, 0))
    low = jax.ShapeDtypeStruct((total, width), jnp.bfloat16)
    return pl.pallas_call(
        functools.partial(branch_kernel, frames),
        grid=(count,),
        in_specs=[
            pl.BlockSpec(memory_space=pltpu.SMEM),
            per_block,
            per_block,
            spec((1, width, width), lambda at: (at, 0, 0)),
            held((total, width)),
            held(bias.shape),
            held(gates.shape),
            held((total, width)),
            held((total, width)),
        ],
        out_specs=[
            per_block,
            spec((1, 1, width), lambda at: (at, 0, 0)),
            held((total, width)),
            held((clips, 1, width)),
        ],
        out_shape=[
            jax.ShapeDtypeStruct((count, total, width), jnp.bfloat16),
            jax.ShapeDtypeStruct((count, 1, width), jnp.float32),
            low,
            jax.ShapeDtypeStruct((clips, 1, width), jnp.float32),
        ],
        scratch_shapes=[pltpu.VMEM((total, width), jnp.float32)],
        compiler_params=pltpu.CompilerParams(vmem_limit_bytes=vmem_bytes),
        cost_estimate=pl.CostEstimate(
            flops=16 * total * width * width, bytes_accessed=40 * total * width, transcendentals=0
        ),
    )(counts, hidden, slope, blocks, d_branch, bias, gates, resid, cotangent)


def resid_kernel(
    frames,
    counts,
    d_pre,
    block,
    mods,
    resid,
    cotangent,
    proj,
    d_resid_out,
    d_proj,
    sums,
    total_grad,
):
    step, steps = pl.program_id(0), pl.num_programs(0)
    total, width = resid.shape
    clips = mods.shape[0]
    rows = total // clips
    tile = min(rows, 128)
    source = d_pre[0]

    @pl.when(step == 0)
    def _():
        total_grad[...] = jnp.zeros_like(total_grad)

    for low, high in column_cuts(width):
        span = slice(low, high)
        total_grad[:, span] += dot_nt(source, block[0, span, :])

    @pl.when(step == steps - 1)
    def _():
        for clip in range(clips):
            gate_one, scale_two = mods[clip, 2:3, :], mods[clip, 4:5, :]
            found = [0.0] * 4
            for first in range(clip * rows, (clip + 1) * rows, tile):
                span = slice(first, first + tile)
                grad = total_grad[span]
                normed, inverse = norm_parts(resid[span])
                back = norm_back(grad * (1.0 + scale_two), normed, inverse)
                d_resid = wide(cotangent[span]) + back
                d_resid_out[span] = d_resid
                kept = valid_rows(counts[clip], tile, frames) * d_resid
                low_back = narrow(kept * gate_one)
                d_proj[span] = low_back
                terms = (grad, grad * normed, kept * proj[span], wide(low_back))
                found = [old + column_sum(term) for old, term in zip(found, terms)]
            for at in range(4):
                sums[clip, at : at + 1, :] = found[at]


def run_resid(frames, counts, d_pre, blocks, mods, resid, cotangent, proj):
    count, total, width = d_pre.shape
    clips = mods.shape[0]
    return pl.pallas_call(
        functools.partial(resid_kernel, frames),
        grid=(count,),
        in_specs=[
            pl.BlockSpec(memory_space=pltpu.SMEM),
            spec((1, total, width), lambda at: (at, 0, 0)),
            spec((1, width, width), lambda at: (at, 0, 0)),
            held(mods.shape),
            held((total, width)),
            held((total, width)),
            held((total, width)),
        ],
        out_specs=[held((total, width)), held((total, width)), held((clips, 4, width))],
        out_shape=[
            jax.ShapeDtypeStruct((total, width), jnp.float32),
            jax.ShapeDtypeStruct((total, width), jnp.bfloat16),
            jax.ShapeDtypeStruct((clips, 4, width), jnp.float32),
        ],
        scratch_shapes=[pltpu.VMEM((total, width), jnp.float32)],
        compiler_params=pltpu.CompilerParams(vmem_limit_bytes=vmem_bytes),
        cost_estimate=pl.CostEstimate(
            flops=8 * total * width * width, bytes_accessed=40 * total * width, transcendentals=0
        ),
    )(counts, d_pre, blocks, mods, resid, cotangent, proj)


def attention_back_kernel(
    frames, counts, d_proj, parts, block, d_qkv, sums, d_mixed, d_query, d_key, d_value
):
    rows, width = d_proj.shape
    tile = min(rows, 128)
    count = counts[pl.program_id(0)]
    source = d_proj[...]
    for low, high in column_cuts(width):
        d_mixed[:, low:high] = narrow(dot_nt(source, block[0, low:high, :]))
    scale = (width // HEADS) ** -0.5
    offset = score_offset(count, tile, frames, 0)
    for ref in (d_query, d_key, d_value):
        ref[...] = jnp.zeros_like(ref)
    for first in range(0, rows, tile):
        span = slice(first, first + tile)
        for low, high, start, stop in head_windows(width):
            lanes = slice(start, stop)
            mask = lane_mask(low, high, stop - start, jnp.bfloat16)
            query_high = parts[0, span, lanes] * mask
            key_high = parts[2, span, lanes] * mask
            back = d_mixed[span, lanes] * mask
            scores = dot_nt(key_high, query_high)
            scores += dot_nt(key_high, parts[1, span, lanes])
            scores += dot_nt(parts[3, span, lanes], query_high) + offset
            expons = jnp.exp(scores - jnp.max(scores, axis=0, keepdims=True))
            probs = expons * (1.0 / jnp.sum(expons, axis=0, keepdims=True))
            d_probs = dot_nt(parts[4, span, lanes], back)
            inner = jnp.sum(d_probs * probs, axis=0, keepdims=True)
            d_scores = narrow(probs * (d_probs - inner))
            d_value[span, lanes] += dot_nn(narrow(probs), back)
            d_key[span, lanes] += dot_nn(d_scores, query_high)
            d_query[span, lanes] += dot_tn(d_scores, key_high)
    for at, ref in enumerate((d_query, d_key, d_value)):
        low_back = narrow(ref[...] * scale) if at == 0 else narrow(ref[...])
        d_qkv[at] = low_back
        sums[0, at : at + 1, :] = column_sum(wide(low_back))
    d_qkv[3] = source


def run_attention_back(frames, counts, d_proj, parts, block):
    total, width = d_proj.shape
    clips = counts.shape[0]
    rows = total // clips
    return pl.pallas_call(
        functools.partial(attention_back_kernel, frames),
        grid=(clips,),
        in_specs=[
            pl.BlockSpec(memory_space=pltpu.SMEM),
            spec((rows, width), lambda clip: (clip, 0)),
            spec((5, rows, width), lambda clip: (0, clip, 0)),
            spec((1, width, width), lambda clip: (3, 0, 0), pipeline_mode=pl.Buffered(1)),
        ],
        out_specs=[
            spec((4, rows, width), lambda clip: (0, clip, 0)),
            spec((1, 3, width), lambda clip: (clip, 0, 0)),
        ],
        out_shape=[
            jax.ShapeDtypeStruct((4, total, width), jnp.bfloat16),
            jax.ShapeDtypeStruct((clips, 3, width), jnp.float32),
        ],
        scratch_shapes=[pltpu.VMEM((rows, width), jnp.bfloat16)]
        + [pltpu.VMEM((rows, width), jnp.float32)] * 3,
        compiler_params=pltpu.CompilerParams(vmem_limit_bytes=vmem_bytes),
        cost_estimate=pl.CostEstimate(
            flops=12 * total * width * width, bytes_accessed=20 * total * width, transcendentals=0
        ),
    )(counts, d_proj, parts, block)


def input_kernel(d_qkv, block, mods, tokens, d_resid, input_grad, sums, total_grad):
    step, steps = pl.program_id(0), pl.num_programs(0)
    total, width = tokens.shape
    clips = mods.shape[0]
    rows = total // clips
    tile = min(rows, 128)
    source = d_qkv[0]

    @pl.when(step == 0)
    def _():
        total_grad[...] = jnp.zeros_like(total_grad)

    for low, high in column_cuts(width):
        span = slice(low, high)
        total_grad[:, span] += dot_nt(source, block[0, span, :])

    @pl.when(step == steps - 1)
    def _():
        for clip in range(clips):
            scale_one = mods[clip, 1:2, :]
            found = [0.0] * 2
            for first in range(clip * rows, (clip + 1) * rows, tile):
                span = slice(first, first + tile)
                grad = total_grad[span]
                normed, inverse = norm_parts(wide(tokens[span]))
                back = norm_back(grad * (1.0 + scale_one), normed, inverse)
                input_grad[span] = narrow(d_resid[span] + back)
                terms = (grad, grad * normed)
                found = [old + column_sum(term) for old, term in zip(found, terms)]
            for at in range(2):
                sums[clip, at : at + 1, :] = found[at]


def run_input(d_qkv, blocks, mods, tokens, d_resid):
    total, width = tokens.shape
    clips = mods.shape[0]
    return pl.pallas_call(
        input_kernel,
        grid=(3,),
        in_specs=[
            spec((1, total, width), lambda at: (at, 0, 0)),
            spec((1, width, width), lambda at: (at, 0, 0)),
            held(mods.shape),
            held((total, width)),
            held((total, width)),
        ],
        out_specs=[held((total, width)), held((clips, 2, width))],
        out_shape=[
            jax.ShapeDtypeStruct((total, width), jnp.bfloat16),
            jax.ShapeDtypeStruct((clips, 2, width), jnp.float32),
        ],
        scratch_shapes=[pltpu.VMEM((total, width), jnp.float32)],
        compiler_params=pltpu.CompilerParams(vmem_limit_bytes=vmem_bytes),
        cost_estimate=pl.CostEstimate(
            flops=6 * total * width * width, bytes_accessed=30 * total * width, transcendentals=0
        ),
    )(d_qkv, blocks, mods, tokens, d_resid)


def tie(*values):
    return lax.optimization_barrier(values)


def packed(arrays, tile):
    flat = jnp.concatenate([array.reshape(-1) for array in arrays])
    return jnp.pad(flat, (0, -flat.shape[0] % (tile * 128))).reshape(-1, 128)


def core_swap(array):
    count = lax.axis_size("dp")
    return lax.ppermute(array, "dp", [(at, at ^ 1) for at in range(count)])


def chip_shift(array, step):
    count = lax.axis_size("dp")
    return lax.ppermute(array, "dp", [(at, (at + 2 * step) % count) for at in range(count)])


def rank_swap(array, bits):
    count = lax.axis_size("fsdp")
    return lax.ppermute(array, "fsdp", [(at, at ^ bits) for at in range(count)])


def entry(array, at, axis=0):
    return lax.dynamic_index_in_dim(array, at, axis, keepdims=False)


def place_kernel(count, at, *refs):
    parts, whole, semaphores = refs[:count], refs[count], refs[count + 1]
    copies = []
    for index, part in enumerate(parts):
        rows = part.shape[0]
        first = pl.multiple_of(at[index] * 16, 16)
        copies.append(
            pltpu.make_async_copy(part, whole.at[pl.ds(first, rows)], semaphores.at[index])
        )
        copies[-1].start()
    for copy in copies:
        copy.wait()


def place(parts, starts, rows):
    width = parts[0].shape[-1]
    return pl.pallas_call(
        functools.partial(place_kernel, len(parts)),
        in_specs=[pl.BlockSpec(memory_space=pltpu.SMEM)]
        + [pl.BlockSpec(memory_space=pl.ANY)] * len(parts),
        out_specs=pl.BlockSpec(memory_space=pl.ANY),
        out_shape=jax.ShapeDtypeStruct((rows, width), parts[0].dtype),
        scratch_shapes=[pltpu.SemaphoreType.DMA((len(parts),))],
        cost_estimate=pl.CostEstimate(
            flops=0, bytes_accessed=4 * rows * width, transcendentals=0
        ),
    )(jnp.stack([jnp.asarray(start, jnp.int32) for start in starts]), *parts)


def own_rows(parts, group):
    ranks, at = lax.axis_size("fsdp"), lax.axis_index("fsdp")
    shares = ranks // group
    row_part, col_part = parts.shape[1:]
    chunk = row_part // shares
    split = parts.reshape(ranks, chunk, col_part)
    if shares > 1:
        moved = lax.all_to_all(split, "fsdp", 0, 0, tiled=True)
        return moved.transpose(1, 0, 2).reshape(chunk, ranks * col_part)
    panels = [entry(split, at)]
    panels += [rank_swap(entry(split, at ^ bits), bits) for bits in range(1, ranks)]
    placed = [
        lax.select_n(at, *[panels[panel ^ index] for index in range(ranks)])
        for panel in range(ranks)
    ]
    return jnp.concatenate(placed, axis=1)


def shard_rows(rows, group):
    ranks = lax.axis_size("fsdp")
    shares = ranks // group
    count, chunk, total = rows.shape
    col_part = total // ranks
    split = rows.reshape(count, chunk, ranks, col_part).transpose(2, 0, 1, 3)
    moved = lax.all_to_all(split, "fsdp", 0, 0, tiled=True)
    moved = moved.reshape(group, shares, count, chunk, col_part).transpose(2, 0, 1, 3, 4)
    return moved.reshape(count * group, shares * chunk, col_part)


def gather_blocks(rows, group):
    ranks, dp_count = lax.axis_size("fsdp"), lax.axis_size("dp")
    shares = ranks // group
    chunk, total = rows.shape
    all_rows = lax.all_gather(rows, ("fsdp", "dp"), axis=0, tiled=True)
    if shares > 1:
        all_rows = all_rows.reshape(group, shares, dp_count, chunk, total).transpose(0, 2, 1, 3, 4)
    return all_rows.reshape(group, total, total)


def gather_pieces(rows, group):
    ranks, at = lax.axis_size("fsdp"), lax.axis_index("fsdp")
    if ranks != group:
        blocks = gather_blocks(rows, group)
        (blocks,) = yield (blocks,)
        yield blocks
        return
    chips = lax.axis_size("dp") // 2
    core, chip = lax.axis_index("dp") % 2, lax.axis_index("dp") // 2
    chunk, total = rows.shape
    half = total // 2
    unit = chunk // 16
    found = [rows] + [chip_shift(rows, step) for step in range(1, chips)]
    line = place(found, [(chip - step) % chips * unit for step in range(chips)], half)
    other = core_swap(line)
    pairs = [part[step * chunk : (step + 1) * chunk] for part in (line, other) for step in range(chips)]
    starts = [(2 * step + side) * unit for side in (core, 1 - core) for step in range(chips)]
    own = place(pairs, starts, total)
    share = lax.dynamic_slice_in_dim(own, core * half, half, 0)
    mine = [rank_swap(share, bits) for bits in range(1, ranks)]
    own, *mine = yield (own, *mine)
    others = [core_swap(part) for part in mine]
    starts = [at * 2] + [
        (at ^ bits) * 2 + side for side in (core, 1 - core) for bits in range(1, ranks)
    ]
    starts = [start * (half // 16) for start in starts]
    yield place([own] + mine + others, starts, group * total).reshape(group, total, total)


def gather_own(rows, group):
    ranks = lax.axis_size("fsdp")
    shares = ranks // group
    chunk, total = rows.shape
    if shares > 1:
        sets = [[share + shares * block for share in range(shares)] for block in range(group)]
        rows = lax.all_gather(rows, "fsdp", axis=0, tiled=True, axis_index_groups=sets)
    return lax.all_gather(rows, "dp", axis=0, tiled=True)


def sum_blocks(product, cut, total, group):
    ranks, dp_count = lax.axis_size("fsdp"), lax.axis_size("dp")
    shares = ranks // group
    if shares > 1:
        blocks = narrow(product(cut(0, total)))
        chunk = total // (dp_count * shares)
        blocks = blocks.reshape(group, dp_count, shares, chunk, -1).transpose(0, 2, 1, 3, 4)
        rows = lax.psum_scatter(
            blocks.reshape(group * total, -1), ("fsdp", "dp"), scatter_dimension=0, tiled=True
        )
        for _ in range(3):
            (rows,) = yield (rows,)
        yield gather_own(rows, group)
        return
    chips, half = dp_count // 2, total // 2
    chunk = half // chips
    core, chip = lax.axis_index("dp") % 2, lax.axis_index("dp") // 2
    low_bit, high_bit = lax.axis_index("fsdp") % 2, lax.axis_index("fsdp") // 2
    away = narrow(product(cut((1 - core) * half, half)))
    here = product(cut(core * half, half))
    here = narrow(here + wide(core_swap(away)))
    here = here.reshape(2, 2, chips, chunk, -1)
    middle = chips // 2
    first, second = here[:, :, :middle], here[:, :, middle:]
    first_in = rank_swap(entry(first, 1 - low_bit, 1), 1)
    second_in = rank_swap(entry(second, 1 - high_bit, 0), 2)
    here, first_in, second_in = yield (here, first_in, second_in)
    first, second = here[:, :, :middle], here[:, :, middle:]
    first = narrow(wide(entry(first, low_bit, 1)) + wide(first_in))
    second = narrow(wide(entry(second, high_bit, 0)) + wide(second_in))
    first_in = rank_swap(entry(first, 1 - high_bit), 2)
    second_in = rank_swap(entry(second, 1 - low_bit), 1)
    first, second, first_in, second_in = yield (first, second, first_in, second_in)
    first = narrow(wide(entry(first, high_bit)) + wide(first_in))
    second = narrow(wide(entry(second, low_bit)) + wide(second_in))
    line = jnp.concatenate([first, second])
    parts = [entry(line, chip)]
    parts += [chip_shift(entry(line, (chip + step) % chips), step) for step in range(1, chips)]
    parts = yield tuple(parts)
    rows = sum(wide(part) for part in parts)
    found = lax.all_gather(narrow(rows), "dp", axis=0, tiled=True)
    yield found.reshape(chips, 2, chunk, -1).transpose(1, 0, 2, 3).reshape(total, -1)


def fast_dot(subscripts, left, right):
    return jnp.einsum(subscripts, left, right, preferred_element_type=jnp.float32)


def owned_step(whole, left_root, right_root, group):
    chunk = left_root.shape[0]
    shares = lax.axis_size("fsdp") // group
    first = lax.axis_index("dp") * (chunk * shares) + lax.axis_index("fsdp") % shares * chunk
    grad_rows = lax.dynamic_slice_in_dim(whole, first, chunk, 0)
    own_columns = lax.dynamic_slice_in_dim(whole, first, chunk, 1)
    outer = fast_dot("rk,jk->rj", grad_rows, whole)
    inner = fast_dot("kr,kj->rj", own_columns, whole)
    side = fast_dot("rk,kj->rj", left_root, whole)
    side_high = narrow(side)
    side_low = narrow(side - wide(side_high))
    precond = fast_dot("rk,kj->rj", side_high, right_root) + fast_dot(
        "rk,kj->rj", side_low, right_root
    )
    return narrow(jnp.stack([precond, outer, inner]))


def per_device(
    tokens,
    conditioning,
    frame_counts,
    cotangent,
    weights,
    biases,
    momentum,
    left_stats,
    right_stats,
    left_roots,
    right_roots,
    bias_moment,
    bias_second,
):
    group = 4
    mod_count = 6
    clip_count, pos_count, frames, width = tokens.shape
    token_count = clip_count * pos_count * frames
    block_count, row_part, col_part = weights.shape
    dp_count, ranks = lax.axis_size("dp"), lax.axis_size("fsdp")
    dp_at, rank_at = lax.axis_index("dp"), lax.axis_index("fsdp")
    all_clips = clip_count * dp_count
    bias_part = biases.shape[0]
    stream = tokens.reshape(token_count, width)
    grad_out = cotangent.reshape(token_count, width)
    pieces = [slice(mod_count + group * piece, mod_count + group * (piece + 1)) for piece in range(3)]

    attn_rows = own_rows(narrow(weights[pieces[0]]), group)
    cond_low = narrow(jax.nn.silu(conditioning))
    attn_rows, one_shard, two_shard, cond_low = tie(
        attn_rows, weights[pieces[1]], weights[pieces[2]], cond_low
    )
    attn_w = gather_blocks(attn_rows, group)
    two_w = gather_blocks(own_rows(narrow(two_shard), group), group)
    one_steps = gather_pieces(own_rows(narrow(one_shard), group), group)
    one_parts = next(one_steps)

    first_parts = lax.all_gather(
        packed([cond_low, narrow(biases)], 16), "dp", axis=0, tiled=True
    ).reshape(dp_count, -1)
    cond_all = first_parts[:, : clip_count * width].reshape(all_clips, width)
    bias_rows = wide(first_parts[:, clip_count * width : clip_count * width + bias_part])
    cond_rows = lax.dynamic_slice_in_dim(cond_all, dp_at * row_part, row_part, 1)
    cond_cols = wide(lax.dynamic_slice_in_dim(cond_all, rank_at * col_part, col_part, 1))
    mod_parts = fast_dot("cr,jre->cje", cond_rows, narrow(weights[:mod_count]))
    mod_parts = lax.all_to_all(mod_parts, "dp", 0, 0, tiled=True)
    mod_cols = jnp.sum(mod_parts.reshape(dp_count, clip_count, mod_count, col_part), axis=0)
    left_cond = jnp.einsum("jrk,ck->jrc", left_roots[:mod_count], cond_cols, precision=precise)
    mod_size, bias_size = mod_cols.size, dp_count * bias_part
    second_parts = lax.all_gather(
        packed([mod_cols, bias_rows, left_cond], 8), "fsdp", axis=0, tiled=True
    ).reshape(ranks, -1)
    mods = second_parts[:, :mod_size].reshape(ranks, clip_count, mod_count, col_part)
    mods = mods.transpose(1, 2, 0, 3).reshape(clip_count, mod_count, width)
    bias_all = second_parts[:, mod_size : mod_size + bias_size].reshape(ranks, dp_count, bias_part)
    bias_all = bias_all.transpose(1, 0, 2).reshape(-1, width)
    left_size = mod_size + bias_size + left_cond.size
    left_cond = jnp.sum(second_parts[:, mod_size + bias_size : left_size], axis=0)
    left_cond = left_cond.reshape(mod_count, row_part, all_clips)
    mods = mods + bias_all[:mod_count]
    bias_table = jnp.concatenate(
        [bias_all[6:7], jnp.zeros((1, width), jnp.float32), bias_all[7:14]]
    )

    attn_in, parts, mixed, proj, resid, mlp_in, d_branch, d_branch_sums = run_attention(
        frames, frame_counts, stream, grad_out, mods, bias_table, attn_w
    )
    left_rows = [own_rows(narrow(left_roots[piece]), group) for piece in pieces]
    right_wholes = [gather_own(own_rows(narrow(right_roots[piece]), group), group) for piece in pieces]
    mlp_in, one_parts = tie(mlp_in, one_parts)
    one_w = one_steps.send(one_parts)
    hidden, slope = run_hidden(mlp_in, one_w, bias_table[4:8, None])
    two_steps = sum_blocks(
        lambda left: fast_dot("jtd,te->jde", left, d_branch),
        lambda first, size: lax.dynamic_slice_in_dim(hidden, first, size, 2),
        width,
        group,
    )
    two_parts = list(next(two_steps))
    hidden, two_parts[0] = tie(hidden, two_parts[0])

    d_pre, d_pre_sums, block_out, d_gate_two = run_branch(
        frames,
        frame_counts,
        hidden,
        slope,
        two_w,
        d_branch,
        bias_table[8:9],
        mods[:, 5:6],
        resid,
        grad_out,
    )
    d_pre, two_parts = tie(d_pre, two_parts)
    two_parts = list(two_steps.send(two_parts))
    one_steps = sum_blocks(
        lambda left: fast_dot("td,jte->jde", left, d_pre),
        lambda first, size: lax.dynamic_slice_in_dim(mlp_in, first, size, 1),
        width,
        group,
    )
    one_parts = list(next(one_steps))
    d_pre, one_parts[0], two_parts = tie(d_pre, one_parts[0], two_parts)
    two_parts = two_steps.send(two_parts)
    d_resid, d_proj, resid_sums = run_resid(
        frames, frame_counts, d_pre, one_w, mods, resid, grad_out, proj
    )
    d_proj, one_parts = tie(d_proj, one_parts)
    one_parts = one_steps.send(one_parts)
    d_heads, head_sums = run_attention_back(frames, frame_counts, d_proj, parts, attn_w)
    d_heads, one_parts, two_parts, right_wholes[2] = tie(
        d_heads, one_parts, two_parts, right_wholes[2]
    )
    whole_two = two_steps.send(two_parts)
    attn_steps = sum_blocks(
        lambda left: fast_dot("jtd,jte->jde", left, d_heads),
        lambda first, size: jnp.stack(
            [lax.dynamic_slice_in_dim(left, first, size, 1) for left in (attn_in,) * 3 + (mixed,)]
        ),
        width,
        group,
    )
    attn_parts = list(next(attn_steps))
    d_heads, attn_parts[0], one_parts = tie(d_heads, attn_parts[0], one_parts)
    one_parts = one_steps.send(one_parts)
    input_grad, input_sums = run_input(d_heads, attn_w, mods, stream, d_resid)
    input_sums, attn_parts, one_parts = tie(input_sums, attn_parts, one_parts)
    attn_parts = attn_steps.send(attn_parts)
    whole_one = one_steps.send(one_parts)

    d_mods = jnp.stack(
        [
            input_sums[:, 0],
            input_sums[:, 1],
            resid_sums[:, 2],
            resid_sums[:, 0],
            resid_sums[:, 1],
            d_gate_two[:, 0],
        ],
        axis=1,
    )
    head_sums = jnp.sum(head_sums, axis=0)
    grad_bias = jnp.concatenate(
        [
            jnp.sum(d_mods, axis=0),
            head_sums[0:1],
            head_sums[2:3],
            jnp.sum(resid_sums[:, 3], axis=0)[None],
            d_pre_sums[:, 0],
            jnp.sum(d_branch_sums, axis=0),
        ]
    )
    to_ranks = jnp.concatenate(
        [
            d_mods.reshape(clip_count, mod_count, ranks, col_part)
            .transpose(2, 0, 1, 3)
            .reshape(ranks, mod_size),
            grad_bias.reshape(dp_count, ranks, bias_part)
            .transpose(1, 0, 2)
            .reshape(ranks, bias_size),
        ],
        axis=1,
    )
    rank_sums = jnp.sum(lax.all_to_all(to_ranks, "fsdp", 0, 0, tiled=True), axis=0)
    to_rows = jnp.concatenate(
        [
            jnp.broadcast_to(rank_sums[None, :mod_size], (dp_count, mod_size)),
            rank_sums[mod_size:].reshape(dp_count, bias_part),
        ],
        axis=1,
    )
    from_rows = lax.all_to_all(to_rows, "dp", 0, 0, tiled=True)
    products_two = owned_step(whole_two, left_rows[2], right_wholes[2], group)
    from_rows, products_two, attn_parts = tie(from_rows, products_two, attn_parts)
    attn_parts = attn_steps.send(attn_parts)
    back_two = shard_rows(products_two, group)
    bias_grad = jnp.sum(from_rows[:, mod_size:], axis=0)
    mod_grad_cols = from_rows[:, :mod_size].reshape(all_clips, mod_count, col_part)
    mod_grad = lax.all_gather(packed([mod_grad_cols], 8), "fsdp", axis=0, tiled=True)
    mod_grad = mod_grad.reshape(ranks, -1)[:, : mod_grad_cols.size]
    mod_grad = mod_grad.reshape(ranks, all_clips, mod_count, col_part).transpose(1, 2, 0, 3)
    mod_grad = mod_grad.reshape(all_clips, mod_count, width)

    mod_grad_rows = lax.dynamic_slice_in_dim(mod_grad, dp_at * row_part, row_part, 2)
    right_parts = jnp.einsum(
        "cjk,jke->cje", mod_grad_rows, right_roots[:mod_count], precision=precise
    )
    cond_wide = wide(cond_all)
    cond_row_wide = wide(cond_rows)
    mod_gram = jnp.einsum("cjk,bjk->jcb", mod_grad, mod_grad, precision=precise)
    cond_gram = jnp.einsum("ck,bk->cb", cond_wide, cond_wide, precision=precise)
    mod_side = jnp.einsum("jcb,be->jce", mod_gram, cond_cols, precision=precise)
    ada_left = jnp.einsum("cr,jce->jre", cond_row_wide, mod_side, precision=precise)
    cond_side = jnp.einsum("cb,bje->jce", cond_gram, mod_grad_cols, precision=precise)
    ada_right = jnp.einsum("cjr,jce->jre", mod_grad_rows, cond_side, precision=precise)

    products_one = owned_step(whole_one, left_rows[1], right_wholes[1], group)
    products_one, right_parts, attn_parts = tie(products_one, right_parts, attn_parts)
    whole_attn = attn_steps.send(attn_parts)
    back_one = shard_rows(products_one, group)
    right_parts = lax.all_gather(packed([right_parts], 8), "dp", axis=0, tiled=True)
    mod_right = jnp.sum(right_parts.reshape(dp_count, -1), axis=0)[: mod_grad_cols.size]
    mod_right = mod_right.reshape(all_clips, mod_count, col_part)
    ada_pre = jnp.einsum("jrc,cje->jre", left_cond, mod_right, precision=precise)
    back_attn = shard_rows(owned_step(whole_attn, left_rows[0], right_wholes[0], group), group)

    def joined(at, ada):
        span = slice(at * group, (at + 1) * group)
        return jnp.concatenate(
            [ada, wide(back_attn[span]), wide(back_one[span]), wide(back_two[span])]
        )

    precond = joined(0, ada_pre)
    left_new = stat_decay * left_stats + (1.0 - stat_decay) * joined(1, ada_left)
    right_new = stat_decay * right_stats + (1.0 - stat_decay) * joined(2, ada_right)
    momentum_new = moment_decay * momentum + precond
    weights_new = weights - weight_rate * momentum_new
    weights_copy = weights_new.astype(jnp.bfloat16)
    bias_second_new = stat_decay * bias_second + (1.0 - stat_decay) * bias_grad * bias_grad
    bias_moment_new = moment_decay * bias_moment + bias_grad * lax.rsqrt(
        bias_second_new + diag_epsilon
    )
    biases_new = biases - bias_rate * bias_moment_new
    return (
        block_out.reshape(tokens.shape),
        input_grad.reshape(tokens.shape),
        left_new,
        right_new,
        momentum_new,
        weights_new,
        weights_copy,
        bias_moment_new,
        bias_second_new,
        biases_new,
    )


def solution(mesh):
    placed = (
        P("dp", "fsdp", None, None),
        P("dp", None),
        P("dp"),
        P("dp", "fsdp", None, None),
        P(None, "dp", "fsdp"),
        P(("dp", "fsdp")),
        P(None, "dp", "fsdp"),
        P(None, "dp", "fsdp"),
        P(None, "dp", "fsdp"),
        P(None, "dp", "fsdp"),
        P(None, "dp", "fsdp"),
        P(("dp", "fsdp")),
        P(("dp", "fsdp")),
    )
    return jax.shard_map(
        per_device,
        mesh=mesh,
        in_specs=placed,
        out_specs=(
            P("dp", "fsdp", None, None),
            P("dp", "fsdp", None, None),
            P(None, "dp", "fsdp"),
            P(None, "dp", "fsdp"),
            P(None, "dp", "fsdp"),
            P(None, "dp", "fsdp"),
            P(None, "dp", "fsdp"),
            P(("dp", "fsdp")),
            P(("dp", "fsdp")),
            P(("dp", "fsdp")),
        ),
        check_vma=False,
    )
```

time: 911 us -> 1180 us (1.30)
  Pallas kernels: 0 us -> 574 us
  matrix products: 206 us -> 77.8 us
  local copies, waits for them, and re-layouts: 227 us -> 109 us
  other arithmetic: 103 us -> 52.9 us
  waiting for transfers between devices: 127 us -> 154 us
  starting transfers between devices: 122 us -> 104 us
  blocking collectives: 96.9 us -> 83.4 us
    pallas_call x0 -> x9, Pallas kernels: none -> 574 us  [the longest x3 448 us: place(): pl.pallas_call(functools.partial(place_kernel, len(parts)), in_specs=[pl....]
    dot_general x32 -> x22, matrix products: 138 us -> 64.7 us  [fast_dot(): jnp.einsum(subscripts, left, right, preferred_element_type=jnp.float32)]
    dot_general x6 -> x0, matrix products: 54.7 us -> none  [the longest x1 13.3 us: attention_backward(): jnp.einsum('sfhd,sghd->shfg', grad_mixed, value_rows, precision=precise)]
    all_gather x2, blocking collectives: 70.7 us -> 25.9 us  [the longest x1 16.2 us: per_device(): lax.all_gather(packed([right_parts], 8), 'dp', axis=0, tiled=True)]
    all_gather x3, waiting for transfers between devices: 0.01 us -> 32 us  [gather_own(): return lax.all_gather(rows, 'dp', axis=0, tiled=True)]
    all_gather x1, blocking collectives: 14.3 us -> 46 us  [per_device(): lax.all_gather(packed([cond_low, narrow(biases)], 16), 'dp', axis=0, tile...]
    another operation x9 -> x4, local copies, waits for them, and re-layouts: 31.9 us -> 2.78 us  [the longest x1 1.57 us: per_device(): mod_grad.reshape(ranks, all_clips, mod_count, col_part)]
    dynamic_update_slice x13 -> x0, local copies, waits for them, and re-layouts: 24.6 us -> none  [put(): return lax.dynamic_update_slice(array, part, at)]
  transfers between devices with their start and end apart: 75 -> 75, of which waited for: 27 -> 33; matrix products, arithmetic and copies ran while one was open for 53% -> 15% of each run, Pallas kernels for 0% -> 49%
where the time goes in v4:
time: 1180 us; the launch traced here: 1170 us
  Pallas kernels  574 us (49%)
  waiting for transfers between devices  154 us (13%)
  local copies, waits for them, and re-layouts  109 us (9%)
  starting transfers between devices  104 us (9%)
  blocking collectives  83.4 us (7%)
  matrix products  77.8 us (7%)
  other arithmetic  52.9 us (4%)
  between operations  18 us (2%)
    pallas_call x3, Pallas kernels, place(): pl.pallas_call(functools.partial(place_kernel, len(parts)), in_specs=[pl....  448 us
    dot_general x22, matrix products, fast_dot(): jnp.einsum(subscripts, left, right, preferred_element_type=jnp.float32)  64.7 us
    ppermute x42, waiting for transfers between devices, rank_swap(): return lax.ppermute(array, 'fsdp', [(at, at ^ bits) for at in range(count)])  56.6 us
    ppermute x42, starting transfers between devices, rank_swap(): return lax.ppermute(array, 'fsdp', [(at, at ^ bits) for at in range(count)])  50.5 us
    all_gather x1, blocking collectives, per_device(): lax.all_gather(packed([cond_low, narrow(biases)], 16), 'dp', axis=0, tile...  46 us
    pallas_call x1, Pallas kernels, run_attention(): pl.pallas_call(functools.partial(attention_kernel, frames), grid=(clips,)...  39.7 us
    all_gather x3, waiting for transfers between devices, gather_own(): return lax.all_gather(rows, 'dp', axis=0, tiled=True)  32 us
    pallas_call x1, Pallas kernels, run_attention_back(): pl.pallas_call(functools.partial(attention_back_kernel, frames), grid=(cl...  26 us
  transfers between devices with their start and end apart: 75, of which 33 were waited for; matrix products, arithmetic and copies ran while one was open for 15% of the time, Pallas kernels for 49%

profile of v4, /device:TPU:0, one launch (start us, length us, event | category | flops | bytes accessed | tf_op | source)
XLA Modules:
  0.0 1173.7 jit_solution(7112746492912276653)
XLA Ops:
  51.1 46.0 %all_gather.36 = bf16[256,128]{1,0:T(8,128)(2,1)S(1)} all-gather(bf16[32,128]{1,0:T(8,128)(2,1)S(1)} %fusion.177), channel_id=1, replica_groups=mesh['dp'=8,'fsdp'=4] {'dp'}, dimensions={0}, use_global_device_ids=true | all-gather | bytes 73728 | tf_op jit(solution)/shard_map/all_gather | solution.py:790
  98.8 42.0 %shard_map.205 = bf16[576,1152]{1,0:T(8,128)(2,1)} custom-call(s32[4]{0:T(128)} %pad_add_fusion.at, bf16[144,1152]{1,0:T(8,128)(2,1)} %copy-done.64, bf16[144,1152]{1,0:T(8,128)(2,1)} %copy-done.86, bf16[144,1152]{1,0:T(8,128)(2,1)} %copy-done.87, bf16[144,1152]{1,0:T(8,128)(2,1)} %copy-done.88), custom_call_target="tpu_custom_call" | custom-call | bytes 2654208 | tf_op jit(solution)/shard_map/pallas_call | solution.py:596
  149.3 8.9 all-to-all-done
  158.4 11.5 all_gather.37
  172.8 82.2 %shard_map.206.refs_0_ = bf16[1152,1152]{1,0:T(8,128)(2,1)} custom-call(s32[8]{0:T(128)} %stack.140.at, bf16[144,1152]{1,0:T(8,128)(2,1)} %get-tuple-element.222.refs_0_, bf16[144,1152]{1,0:T(8,128)(2,1)} %get-tuple-element.221.refs_1_, bf16[144,1152]{1,0:T(8,128)(2,1)} %get-tuple-element.220.refs_2_, bf16[144,1152]{1,0:T(8,128)(2,1)} %get-tuple-element.219.refs_3_, ...), custom_call_target="tpu_custom_call" | custom-call | bytes 5308416 | tf_op jit(solution)/shard_map/pallas_call | solution.py:596
  261.5 39.7 %shard_map.204 = (bf16[512,1152]{1,0:T(8,128)(2,1)S(1)}, bf16[5,512,1152]{2,1,0:T(8,128)(2,1)}, bf16[512,1152]{1,0:T(8,128)(2,1)S(1)}, f32[512,1152]{1,0:T(8,128...) custom-call(s32[2]{0:T(128)S(1)} %copy-done.11, ...), custom_call_target="tpu_custom_call" | custom-call | flops 8153726976 | bytes 23592960 | tf_op jit(solution)/shard_map/pallas_call | solution.py:187
  302.1 14.3 %collective-permute-done.11.refs_2_ = bf16[576,1152]{1,0:T(8,128)(2,1)} collective-permute-done((bf16[576,1152]{1,0:T(8,128)(2,1)}, bf16[576,1152]{1,0:T(8,128)(2,1)}, u32[]{:S(2)}, u32[]{:S(2)}) %collective-permute-start.11) | collective-permute-done | bytes 1327136 | tf_op jit(solution)/shard_map/ppermute | solution.py:573
  323.7 323.4 %shard_map.207 = bf16[4608,1152]{1,0:T(8,128)(2,1)} custom-call(s32[7]{0:T(128)} %stack.153.at, bf16[1152,1152]{1,0:T(8,128)(2,1)} %shard_map.206.refs_0_, bf16[576,1152]{1,0:T(8,128)(2,1)} %collective-permute-done.10.refs_1_, bf16[576,1152]{1,0:T(8,128)(2,1)} %collective-permute-done.11.refs_2_, bf16[576,1152]{1,0:T(8,128)(2,1)} %collective-permute-done.12.refs_3_, ...), custom_call_target="tpu_custom_call" | custom-call | bytes 21233664 | tf_op jit(solution)/shard_map/pallas_call | solution.py:596
  648.4 13.3 %shard_map.208 = (bf16[4,512,1152]{2,1,0:T(8,128)(2,1)}, bf16[4,512,1152]{2,1,0:T(8,128)(2,1)}) custom-call(bf16[512,1152]{1,0:T(8,128)(2,1)S(1)} %copy-done.13, bf16[4,1152,1152]{2,1,0:T(8,128)(2,1)} %bitcast.491, f32[4,1,1152]{2,1,0:T(1,128)S(1)} %copy.106.bias), custom_call_target="tpu_custom_call" | custom-call | flops 5435817984 | bytes 17694720 | tf_op jit(solution)/shard_map/pallas_call | solution.py:245
  661.7 7.9 convolution_convert_fusion.1
  670.0 8.8 collective-permute-done.16
  678.8 7.3 add_convert_fusion.1
  698.0 21.0 %shard_map.209 = (bf16[4,512,1152]{2,1,0:T(8,128)(2,1)}, f32[4,1,1152]{2,1,0:T(1,128)S(1)}, bf16[512,1152]{1,0:T(8,128)(2,1)}, f32[2,1,1152]{2,1,0:T(1,128)S(1)}) custom-call(s32[2]{0:T(128)S(1)} %copy-done.11, bf16[4,512,1152]{2,1,0:T(8,128)(2,1)} %get-tuple-element.103.hidden, bf16[4,512,1152]{2,1,0:T(8,128)(2,1)} %get-tuple-element.104.slope, ...), custom_call_target="tpu_custom_call" | custom-call | flops 10871635968 | bytes 23592960 | tf_op jit(solution)/shard_map/pallas_call | solution.py:311
  723.2 8.1 fusion.1
  770.5 5.5 fusion
  776.5 5.7 collective-permute-done.23
  794.5 15.5 %shard_map.210 = (f32[512,1152]{1,0:T(8,128)}, bf16[512,1152]{1,0:T(8,128)(2,1)S(1)}, f32[2,4,1152]{2,1,0:T(4,128)S(1)}) custom-call(s32[2]{0:T(128)S(1)} %copy-done.11, bf16[4,512,1152]{2,1,0:T(8,128)(2,1)} %get-tuple-element.114.d_pre, bf16[4,1152,1152]{2,1,0:T(8,128)(2,1)} %bitcast.492, f32[2,6,1152]{2,1,0:T(8,128)S(1)} %copy-done.4, ...), custom_call_target="tpu_custom_call" | custom-call | flops 5435817984 | bytes 23592960 | tf_op jit(solution)/shard_map/pallas_call | solution.py:398
  810.0 6.0 collective-permute-done.25
  823.1 26.0 %shard_map.211 = (bf16[4,512,1152]{2,1,0:T(8,128)(2,1)}, f32[2,3,1152]{2,1,0:T(4,128)S(1)}) custom-call(s32[2]{0:T(128)S(1)} %copy-done.11, bf16[512,1152]{1,0:T(8,128)(2,1)S(1)} %get-tuple-element.118.d_proj, bf16[5,512,1152]{2,1,0:T(8,128)(2,1)} %get-tuple-element.119.parts, bf16[4,1152,1152]{2,1,0:T(8,128)(2,1)} %bitcast.511), custom_call_target="tpu_custom_call" | custom-call | flops 8153726976 | bytes 11796480 | tf_op jit(solution)/shard_map/pallas_call | solution.py:467
  849.2 8.7 convolution_convert_fusion
  861.9 5.1 collective-permute-done.35
  867.0 7.4 add_convert_fusion
  886.2 11.1 shard_map.212
  898.5 13.2 %collective-permute-done.39 = bf16[144,1152]{1,0:T(8,128)(2,1)S(1)} collective-permute-done((bf16[144,1152]{1,0:T(8,128)(2,1)S(1)}, bf16[144,1152]{1,0:T(8,128)(2,1)S(1)}, u32[]{:S(2)}, u32[]{:S(2)}) %collective-permute-start.39) | collective-permute-done | bytes 331808 | tf_op jit(solution)/shard_map/ppermute | solution.py:568
  973.8 9.8 all-to-all-start.2
  991.2 9.6 all_gather.42
  1009.2 5.1 collective-permute-start.55
  1028.5 5.0 collective-permute-done.56
  1053.0 9.9 all-to-all-done.5
  1077.7 32.0 %all-gather.23.cloned.1.call-done = bf16[1152,1152]{1,0:T(8,128)(2,1)} async-done(((bf16[144,1152]{1,0:T(8,128)(2,1)}), bf16[1152,1152]{1,0:T(8,128)(2,1)}) %all-gather.23.cloned.1.call-update) | async-done | bytes 2654224 | tf_op jit(solution)/shard_map/all_gather | solution.py:684
  1126.8 16.2 %all_gather.47 = f32[1728,128]{1,0:T(8,128)S(1)} all-gather(f32[216,128]{1,0:T(8,128)S(1)} %copy-done.85), channel_id=1, replica_groups=mesh['dp'=8,'fsdp'=4] {'dp'}, dimensions={0}, use_global_device_ids=true | all-gather | bytes 995328 | tf_op jit(solution)/shard_map/all_gather | solution.py:953
  1160.3 5.4 fusion.186
  (568 shorter events, 324.0 us)
Async XLA Ops:
  8.0 253.4 %all-gather.9.cloned.1.call-start = ((), (), s32[]{:S(2)}) async-start(), calls=%async_computation.6 | async-start | bytes 10948608 | tf_op jit(solution)/shard_map/all_gather | solution.py:642
  26.2 669.2 %all-gather.11.cloned.1.call-start = ((), (), s32[]{:S(2)}) async-start(), calls=%async_computation.7 | async-start | bytes 10948608 | tf_op jit(solution)/shard_map/all_gather | solution.py:642
  43.5 53.7 %collective-permute-start.6 = (bf16[144,1152]{1,0:T(8,128)(2,1)S(1)}, bf16[144,1152]{1,0:T(8,128)(2,1)S(1)}, u32[]{:S(2)}, u32[]{:S(2)}) collective-permute-start(bf16[144,1152]{1,0:T(8,128)(2,1)S(1)} %concatenate.69.refs_0_), channel_id=1, source_target_pairs={{0,8},{4,12},{8,16},{12,20},{16,24},{20,28},{24,0},{28,4},{1,9},{5... | collective-permute-start | bytes 995336 | tf_op jit(solution)/shard_map/ppermute | solution.py:568
  45.7 51.5 %collective-permute-start.7 = (bf16[144,1152]{1,0:T(8,128)(2,1)S(1)}, bf16[144,1152]{1,0:T(8,128)(2,1)S(1)}, u32[]{:S(2)}, u32[]{:S(2)}) collective-permute-start(bf16[144,1152]{1,0:T(8,128)(2,1)S(1)} %concatenate.69.refs_0_), channel_id=1, source_target_pairs={{0,16},{4,20},{8,24},{12,28},{16,0},{20,4},{24,8},{28,12},{1,17},{... | collective-permute-start | bytes 995336 | tf_op jit(solution)/shard_map/ppermute | solution.py:568
  48.6 48.7 %collective-permute-start.8 = (bf16[144,1152]{1,0:T(8,128)(2,1)S(1)}, bf16[144,1152]{1,0:T(8,128)(2,1)S(1)}, u32[]{:S(2)}, u32[]{:S(2)}) collective-permute-start(bf16[144,1152]{1,0:T(8,128)(2,1)S(1)} %concatenate.69.refs_0_), channel_id=1, source_target_pairs={{0,24},{4,28},{8,0},{12,4},{16,8},{20,12},{24,16},{28,20},{1,25},{... | collective-permute-start | bytes 995336 | tf_op jit(solution)/shard_map/ppermute | solution.py:568
  140.8 30.9 %collective-permute-start.9 = (bf16[576,1152]{1,0:T(8,128)(2,1)}, bf16[576,1152]{1,0:T(8,128)(2,1)S(1)}, u32[]{:S(2)}, u32[]{:S(2)}) collective-permute-start(bf16[576,1152]{1,0:T(8,128)(2,1)} %shard_map.205), channel_id=1, source_target_pairs={{0,4},{4,0},{8,12},{12,8},{16,20},{20,16},{24,28},{28,24},{1,5},{5... | collective-permute-start | bytes 3981320 | tf_op jit(solution)/shard_map/ppermute | solution.py:563
  146.6 702.6 %all-gather.13.cloned.1.call-start = ((), (), s32[]{:S(2)}) async-start(), calls=%async_computation.8 | async-start | bytes 2985984 | tf_op jit(solution)/shard_map/all_gather | solution.py:684
  257.5 44.6 %collective-permute-start.10 = (bf16[576,1152]{1,0:T(8,128)(2,1)}, bf16[576,1152]{1,0:T(8,128)(2,1)}, u32[]{:S(2)}, u32[]{:S(2)}) collective-permute-start(bf16[576,1152]{1,0:T(8,128)(2,1)} %constant_dynamic-slice_fusion.4), channel_id=1, source_target_pairs={{0,1},{1,0},{2,3},{3,2},{4,5},{5,4},{6,7},{7,6},{8,9},{9,8},{10,11... | collective-permute-start | bytes 3981320 | tf_op jit(solution)/shard_map/ppermute | solution.py:573
  258.6 57.8 %collective-permute-start.11 = (bf16[576,1152]{1,0:T(8,128)(2,1)}, bf16[576,1152]{1,0:T(8,128)(2,1)}, u32[]{:S(2)}, u32[]{:S(2)}) collective-permute-start(bf16[576,1152]{1,0:T(8,128)(2,1)} %constant_dynamic-slice_fusion.4), channel_id=1, source_target_pairs={{0,2},{1,3},{2,0},{3,1},{4,6},{5,7},{6,4},{7,5},{8,10},{9,11},{10,... | collective-permute-start | bytes 3981320 | tf_op jit(solution)/shard_map/ppermute | solution.py:573
  259.5 56.9 %collective-permute-start.12 = (bf16[576,1152]{1,0:T(8,128)(2,1)}, bf16[576,1152]{1,0:T(8,128)(2,1)}, u32[]{:S(2)}, u32[]{:S(2)}) collective-permute-start(bf16[576,1152]{1,0:T(8,128)(2,1)} %constant_dynamic-slice_fusion.4), channel_id=1, source_target_pairs={{0,3},{1,2},{2,1},{3,0},{4,7},{5,6},{6,5},{7,4},{8,11},{9,10},{10,... | collective-permute-start | bytes 3981320 | tf_op jit(solution)/shard_map/ppermute | solution.py:573
  689.5 31.5 %collective-permute-start.20 = (bf16[2,2,144,1152]{3,2,1,0:T(8,128)(2,1)}, bf16[2,2,144,1152]{3,2,1,0:T(8,128)(2,1)}, u32[]{:S(2)}, u32[]{:S(2)}) collective-permute-start(bf16[2,2,144,1152]{3,2,1,0:T(8,128)(2,1)} %dynamic-slice_bitcast_fusion.5), channel_id=1, source_target_pairs={{0,1},{1,0},{2,3},{3,2},{4,5},{5,4},{6,7},{7,6},{8,9},{9,8},{10,11... | collective-permute-start | bytes 3981320 | tf_op jit(solution)/shard_map/ppermute | solution.py:573
  692.0 31.2 %collective-permute-start.21 = (bf16[2,2,144,1152]{3,2,1,0:T(8,128)(2,1)}, bf16[2,2,144,1152]{3,2,1,0:T(8,128)(2,1)}, u32[]{:S(2)}, u32[]{:S(2)}) collective-permute-start(bf16[2,2,144,1152]{3,2,1,0:T(8,128)(2,1)} %dynamic-slice_bitcast_fusion.4), channel_id=1, source_target_pairs={{0,2},{1,3},{2,0},{3,1},{4,6},{5,7},{6,4},{7,5},{8,10},{9,11},{10,... | collective-permute-start | bytes 3981320 | tf_op jit(solution)/shard_map/ppermute | solution.py:573
  731.3 39.2 %collective-permute-start.22 = (bf16[4,576,1152]{2,1,0:T(8,128)(2,1)}, bf16[4,576,1152]{2,1,0:T(8,128)(2,1)}, u32[]{:S(2)}, u32[]{:S(2)}) collective-permute-start(bf16[4,576,1152]{2,1,0:T(8,128)(2,1)} %fusion.1), channel_id=1, source_target_pairs={{0,4},{4,0},{8,12},{12,8},{16,20},{20,16},{24,28},{28,24},{1,5},{5... | collective-permute-start | bytes 15925256 | tf_op jit(solution)/shard_map/ppermute | solution.py:563
  752.4 192.4 %all-gather.15.cloned.1.call-start = ((), (), s32[]{:S(2)}) async-start(), calls=%async_computation.9 | async-start | bytes 2985984 | tf_op jit(solution)/shard_map/all_gather | solution.py:727
  786.5 29.5 %collective-permute-start.25 = (bf16[2,2,144,1152]{3,2,1,0:T(8,128)(2,1)}, bf16[2,2,144,1152]{3,2,1,0:T(8,128)(2,1)}, u32[]{:S(2)}, u32[]{:S(2)}) collective-permute-start(bf16[2,2,144,1152]{3,2,1,0:T(8,128)(2,1)} %dynamic-slice_bitcast_fusion.3), channel_id=1, source_target_pairs={{0,1},{1,0},{2,3},{3,2},{4,5},{5,4},{6,7},{7,6},{8,9},{9,8},{10,11... | collective-permute-start | bytes 3981320 | tf_op jit(solution)/shard_map/ppermute | solution.py:573
  787.2 28.8 %collective-permute-start.26 = (bf16[2,2,144,1152]{3,2,1,0:T(8,128)(2,1)S(1)}, bf16[2,2,144,1152]{3,2,1,0:T(8,128)(2,1)S(1)}, u32[]{:S(2)}, u32[]{:S(2)}) collective-permute-start(bf16[2,2,144,1152]{3,2,1,0:T(8,128)(2,1)S(1)} %dynamic-slice_bitcast_fusion.2), channel_id=1, source_target_pairs={{0,2},{1,3},{2,0},{3,1},{4,6},{5,7},{6,4},{7,5},{8,10},{9,11},{10,... | collective-permute-start | bytes 3981320 | tf_op jit(solution)/shard_map/ppermute | solution.py:573
  790.6 58.5 %collective-permute-start.29 = (bf16[144,1152]{1,0:T(8,128)(2,1)}, bf16[144,1152]{1,0:T(8,128)(2,1)}, u32[]{:S(2)}, u32[]{:S(2)}) collective-permute-start(bf16[144,1152]{1,0:T(8,128)(2,1)} %get-tuple-element.213), channel_id=1, source_target_pairs={{0,8},{4,12},{8,16},{12,20},{16,24},{20,28},{24,0},{28,4},{1,9},{5... | collective-permute-start | bytes 995336 | tf_op jit(solution)/shard_map/ppermute | solution.py:568
  790.6 58.5 %collective-permute-start.30 = (bf16[144,1152]{1,0:T(8,128)(2,1)}, bf16[144,1152]{1,0:T(8,128)(2,1)}, u32[]{:S(2)}, u32[]{:S(2)}) collective-permute-start(bf16[144,1152]{1,0:T(8,128)(2,1)} %get-tuple-element.214), channel_id=1, source_target_pairs={{0,16},{4,20},{8,24},{12,28},{16,0},{20,4},{24,8},{28,12},{1,17},{... | collective-permute-start | bytes 995336 | tf_op jit(solution)/shard_map/ppermute | solution.py:568
  790.6 58.5 %collective-permute-start.31 = (bf16[144,1152]{1,0:T(8,128)(2,1)}, bf16[144,1152]{1,0:T(8,128)(2,1)}, u32[]{:S(2)}, u32[]{:S(2)}) collective-permute-start(bf16[144,1152]{1,0:T(8,128)(2,1)} %get-tuple-element.211), channel_id=1, source_target_pairs={{0,24},{4,28},{8,0},{12,4},{16,8},{20,12},{24,16},{28,20},{1,25},{... | collective-permute-start | bytes 995336 | tf_op jit(solution)/shard_map/ppermute | solution.py:568
  819.7 29.5 %collective-permute-start.27 = (bf16[2,144,1152]{2,1,0:T(8,128)(2,1)S(1)}, bf16[2,144,1152]{2,1,0:T(8,128)(2,1)}, u32[]{:S(2)}, u32[]{:S(2)}) collective-permute-start(bf16[2,144,1152]{2,1,0:T(8,128)(2,1)S(1)} %dynamic-slice_bitcast_fusion.9), channel_id=1, source_target_pairs={{0,2},{1,3},{2,0},{3,1},{4,6},{5,7},{6,4},{7,5},{8,10},{9,11},{10,... | collective-permute-start | bytes 1990664 | tf_op jit(solution)/shard_map/ppermute | solution.py:573
  822.7 26.5 %collective-permute-start.28 = (bf16[2,144,1152]{2,1,0:T(8,128)(2,1)}, bf16[2,144,1152]{2,1,0:T(8,128)(2,1)}, u32[]{:S(2)}, u32[]{:S(2)}) collective-permute-start(bf16[2,144,1152]{2,1,0:T(8,128)(2,1)} %dynamic-slice_bitcast_fusion.8), channel_id=1, source_target_pairs={{0,1},{1,0},{2,3},{3,2},{4,5},{5,4},{6,7},{7,6},{8,9},{9,8},{10,11... | collective-permute-start | bytes 1990664 | tf_op jit(solution)/shard_map/ppermute | solution.py:573
  860.1 159.7 %all-gather.17.cloned.1.call-start = ((), (), s32[]{:S(2)}) async-start(), calls=%async_computation.10 | async-start | bytes 2985984 | tf_op jit(solution)/shard_map/all_gather | solution.py:727
  876.8 34.9 %collective-permute-start.36 = (bf16[2,2,144,1152]{3,2,1,0:T(8,128)(2,1)S(1)}, bf16[2,2,144,1152]{3,2,1,0:T(8,128)(2,1)S(1)}, u32[]{:S(2)}, u32[]{:S(2)}) collective-permute-start(bf16[2,2,144,1152]{3,2,1,0:T(8,128)(2,1)S(1)} %dynamic-slice_bitcast_fusion.1), channel_id=1, source_target_pairs={{0,1},{1,0},{2,3},{3,2},{4,5},{5,4},{6,7},{7,6},{8,9},{9,8},{10,11... | collective-permute-start | bytes 3981320 | tf_op jit(solution)/shard_map/ppermute | solution.py:573
  878.6 33.1 %collective-permute-start.37 = (bf16[2,2,144,1152]{3,2,1,0:T(8,128)(2,1)S(1)}, bf16[2,2,144,1152]{3,2,1,0:T(8,128)(2,1)S(1)}, u32[]{:S(2)}, u32[]{:S(2)}) collective-permute-start(bf16[2,2,144,1152]{3,2,1,0:T(8,128)(2,1)S(1)} %dynamic-slice_bitcast_fusion), channel_id=1, source_target_pairs={{0,2},{1,3},{2,0},{3,1},{4,6},{5,7},{6,4},{7,5},{8,10},{9,11},{10,... | collective-permute-start | bytes 3981320 | tf_op jit(solution)/shard_map/ppermute | solution.py:573
  882.4 29.3 %collective-permute-start.39 = (bf16[144,1152]{1,0:T(8,128)(2,1)S(1)}, bf16[144,1152]{1,0:T(8,128)(2,1)S(1)}, u32[]{:S(2)}, u32[]{:S(2)}) collective-permute-start(bf16[144,1152]{1,0:T(8,128)(2,1)S(1)} %get-tuple-element.210), channel_id=1, source_target_pairs={{0,16},{4,20},{8,24},{12,28},{16,0},{20,4},{24,8},{28,12},{1,17},{... | collective-permute-start | bytes 995336 | tf_op jit(solution)/shard_map/ppermute | solution.py:568
  882.7 28.9 %collective-permute-start.40 = (bf16[144,1152]{1,0:T(8,128)(2,1)S(1)}, bf16[144,1152]{1,0:T(8,128)(2,1)S(1)}, u32[]{:S(2)}, u32[]{:S(2)}) collective-permute-start(bf16[144,1152]{1,0:T(8,128)(2,1)S(1)} %get-tuple-element.207), channel_id=1, source_target_pairs={{0,24},{4,28},{8,0},{12,4},{16,8},{20,12},{24,16},{28,20},{1,25},{... | collective-permute-start | bytes 995336 | tf_op jit(solution)/shard_map/ppermute | solution.py:568
  914.1 109.9 %all-gather.19.cloned.1.call-start = ((), (), s32[]{:S(2)}) async-start(), calls=%async_computation.11 | async-start | bytes 2985984 | tf_op jit(solution)/shard_map/all_gather | solution.py:684
  967.9 22.4 %collective-permute-start.44 = (bf16[2,144,1152]{2,1,0:T(8,128)(2,1)}, bf16[2,144,1152]{2,1,0:T(8,128)(2,1)}, u32[]{:S(2)}, u32[]{:S(2)}) collective-permute-start(bf16[2,144,1152]{2,1,0:T(8,128)(2,1)} %dynamic-slice_bitcast_fusion.7), channel_id=1, source_target_pairs={{0,2},{1,3},{2,0},{3,1},{4,6},{5,7},{6,4},{7,5},{8,10},{9,11},{10,... | collective-permute-start | bytes 1990664 | tf_op jit(solution)/shard_map/ppermute | solution.py:573
  983.6 91.5 %all-gather.21.cloned.1.call-start = ((), (), s32[]{:S(2)}) async-start(), calls=%async_computation.12 | async-start | bytes 2985984 | tf_op jit(solution)/shard_map/all_gather | solution.py:727
  1035.6 74.2 %all-gather.23.cloned.1.call-start = ((), (), s32[]{:S(2)}) async-start(), calls=%async_computation.13 | async-start | bytes 2985984 | tf_op jit(solution)/shard_map/all_gather | solution.py:684
  1067.0 56.1 %all-to-all-start.4 = ((bf16[4,3,144,288]{3,2,1,0:T(8,128)(2,1)}), bf16[4,3,144,288]{3,2,1,0:T(8,128)(2,1)}, u32[]{:S(2)}, u32[]{:S(2)}) async-start(bf16[4,3,144,288]{3,2,1,0:T(8,128)(2,1)} %copy.132), calls=%async_computation.4 | async-start | bytes 2654208 | tf_op jit(solution)/shard_map/all_to_all | solution.py:633
  1123.1 25.4 %all-to-all-start.3 = ((bf16[4,3,144,288]{3,2,1,0:T(8,128)(2,1)}), bf16[4,3,144,288]{3,2,1,0:T(8,128)(2,1)S(1)}, u32[]{:S(2)}, u32[]{:S(2)}) async-start(bf16[4,3,144,288]{3,2,1,0:T(8,128)(2,1)} %copy.130), calls=%async_computation.3 | async-start | bytes 2654208 | tf_op jit(solution)/shard_map/all_to_all | solution.py:633
  (149 other events, 1519.3 us)
Sparse Core Ops, SparseCore 0:
  26.3 105.0 all-gather.8
  134.4 89.5 all-gather.10
Sparse Core Ops, SparseCore 1:
  752.4 31.1 all-gather.12
  860.2 48.0 all-gather.14
  914.2 39.7 all-gather.16
  955.6 33.0 all-gather.18
  1035.7 39.4 all-gather.20
  1076.7 33.0 all-gather.22

commit v5 on v4

--- a/solution.py
+++ b/solution.py
@@ -578,28 +578,41 @@
 
 
 def place_kernel(count, at, *refs):
-    parts, whole, semaphores = refs[:count], refs[count], refs[count + 1]
-    copies = []
+    parts, whole, held_rows, semaphores = refs[:count], refs[count], refs[count + 1], refs[count + 2]
+    spans, loads, stores = [], [], []
     for index, part in enumerate(parts):
-        rows = part.shape[0]
         first = pl.multiple_of(at[index] * 16, 16)
-        copies.append(
-            pltpu.make_async_copy(part, whole.at[pl.ds(first, rows)], semaphores.at[index])
+        spans.append(pl.ds(first, part.shape[0]))
+        loads.append(
+            pltpu.make_async_copy(part, held_rows.at[spans[index]], semaphores.at[0, index])
         )
-        copies[-1].start()
-    for copy in copies:
-        copy.wait()
+        loads[index].start()
+    for index in range(count):
+        loads[index].wait()
+        stores.append(
+            pltpu.make_async_copy(
+                held_rows.at[spans[index]], whole.at[spans[index]], semaphores.at[1, index]
+            )
+        )
+        stores[index].start()
+    for store in stores:
+        store.wait()
 
 
 def place(parts, starts, rows):
     width = parts[0].shape[-1]
+    dtype = parts[0].dtype
     return pl.pallas_call(
         functools.partial(place_kernel, len(parts)),
         in_specs=[pl.BlockSpec(memory_space=pltpu.SMEM)]
         + [pl.BlockSpec(memory_space=pl.ANY)] * len(parts),
         out_specs=pl.BlockSpec(memory_space=pl.ANY),
-        out_shape=jax.ShapeDtypeStruct((rows, width), parts[0].dtype),
-        scratch_shapes=[pltpu.SemaphoreType.DMA((len(parts),))],
+        out_shape=jax.ShapeDtypeStruct((rows, width), dtype),
+        scratch_shapes=[
+            pltpu.VMEM((rows, width), dtype),
+            pltpu.SemaphoreType.DMA((2, len(parts))),
+        ],
+        compiler_params=pltpu.CompilerParams(vmem_limit_bytes=vmem_bytes),
         cost_estimate=pl.CostEstimate(
             flops=0, bytes_accessed=4 * rows * width, transcendentals=0
         ),

time: 1180 us -> 760 us (0.64)
  Pallas kernels: 574 us -> 140 us
  waiting for transfers between devices: 154 us -> 176 us
    pallas_call x3, Pallas kernels: 448 us -> 13.3 us  [place(): pl.pallas_call(functools.partial(place_kernel, len(parts)), in_specs=[pl....]
    ppermute x42, waiting for transfers between devices: 56.6 us -> 75.2 us  [rank_swap(): return lax.ppermute(array, 'fsdp', [(at, at ^ bits) for at in range(count)])]
  transfers between devices with their start and end apart: 75 -> 75, of which waited for: 33 -> 33; matrix products, arithmetic and copies ran while one was open for 15% -> 23% of each run, Pallas kernels for 49% -> 19%
where the time goes in v5:
time: 760 us; the launch traced here: 753 us
  waiting for transfers between devices  176 us (23%)
  Pallas kernels  140 us (18%)
  starting transfers between devices  104 us (14%)
  local copies, waits for them, and re-layouts  103 us (14%)
  blocking collectives  83.7 us (11%)
  matrix products  78.6 us (10%)
  other arithmetic  50.2 us (7%)
  between operations  17.9 us (2%)
    ppermute x42, waiting for transfers between devices, rank_swap(): return lax.ppermute(array, 'fsdp', [(at, at ^ bits) for at in range(count)])  75.2 us
    dot_general x22, matrix products, fast_dot(): jnp.einsum(subscripts, left, right, preferred_element_type=jnp.float32)  65.5 us
    ppermute x42, starting transfers between devices, rank_swap(): return lax.ppermute(array, 'fsdp', [(at, at ^ bits) for at in range(count)])  51.1 us
    all_gather x1, blocking collectives, per_device(): lax.all_gather(packed([cond_low, narrow(biases)], 16), 'dp', axis=0, tile...  48.3 us
    pallas_call x1, Pallas kernels, run_attention(): pl.pallas_call(functools.partial(attention_kernel, frames), grid=(clips,)...  39.6 us
    all_gather x3, waiting for transfers between devices, gather_own(): return lax.all_gather(rows, 'dp', axis=0, tiled=True)  32 us
    pallas_call x1, Pallas kernels, run_attention_back(): pl.pallas_call(functools.partial(attention_back_kernel, frames), grid=(cl...  26.1 us
    ppermute x12, starting transfers between devices, chip_shift(): lax.ppermute(array, 'dp', [(at, (at + 2 * step) % count) for at in range(...  22 us
  transfers between devices with their start and end apart: 75, of which 33 were waited for; matrix products, arithmetic and copies ran while one was open for 23% of the time, Pallas kernels for 19%

profile of v5, /device:TPU:0, one launch (start us, length us, event | category | flops | bytes accessed | tf_op | source)
XLA Modules:
  0.0 753.2 jit_solution(10376053972004920527)
XLA Ops:
  46.3 48.3 %all_gather.36 = bf16[256,128]{1,0:T(8,128)(2,1)S(1)} all-gather(bf16[32,128]{1,0:T(8,128)(2,1)S(1)} %fusion.177), channel_id=1, replica_groups=mesh['dp'=8,'fsdp'=4] {'dp'}, dimensions={0}, use_global_device_ids=true | all-gather | bytes 73728 | tf_op jit(solution)/shard_map/all_gather | solution.py:803
  104.8 11.5 %all-to-all-done = f32[16,6,288]{2,1,0:T(8,128)S(1)} async-done(((f32[16,6,288]{2,1,0:T(8,128)}), f32[16,6,288]{2,1,0:T(8,128)S(1)}, u32[]{:S(2)}, u32[]{:S(2)}) %all-to-all-start) | async-done | bytes 110624 | tf_op jit(solution)/shard_map/all_to_all | solution.py:811
  116.5 9.5 %all_gather.37 = f32[672,128]{1,0:T(8,128)S(1)} all-gather(f32[168,128]{1,0:T(8,128)S(1)} %pad_bitcast_fusion), channel_id=1, replica_groups=mesh['dp'=8,'fsdp'=4] {'fsdp'}, dimensions={0}, use_global_device_ids=true | all-gather | bytes 430080 | tf_op jit(solution)/shard_map/all_gather | solution.py:815
  137.7 39.6 %shard_map.204 = (bf16[512,1152]{1,0:T(8,128)(2,1)S(1)}, bf16[5,512,1152]{2,1,0:T(8,128)(2,1)}, bf16[512,1152]{1,0:T(8,128)(2,1)S(1)}, f32[512,1152]{1,0:T(8,128...) custom-call(s32[2]{0:T(128)S(1)} %copy-done.11, ...), custom_call_target="tpu_custom_call" | custom-call | flops 8153726976 | bytes 23592960 | tf_op jit(solution)/shard_map/pallas_call | solution.py:187
  178.3 31.9 %collective-permute-done.12.refs_3_ = bf16[576,1152]{1,0:T(8,128)(2,1)} collective-permute-done((bf16[576,1152]{1,0:T(8,128)(2,1)}, bf16[576,1152]{1,0:T(8,128)(2,1)}, u32[]{:S(2)}, u32[]{:S(2)}) %collective-permute-start.12) | collective-permute-done | bytes 1327136 | tf_op jit(solution)/shard_map/ppermute | solution.py:573
  217.6 8.7 %shard_map.207 = bf16[4608,1152]{1,0:T(8,128)(2,1)} custom-call(s32[7]{0:T(128)S(1)} %stack.153.at, bf16[1152,1152]{1,0:T(8,128)(2,1)} %shard_map.206.refs_0_, bf16[576,1152]{1,0:T(8,128)(2,1)} %collective-permute-done.10.refs_1_, bf16[576,1152]{1,0:T(8,128)(2,1)} %collective-permute-done.11.refs_2_, bf16[576,1152]{1,0:T(8,128)(2,1)} %collective-permute-done.12.refs_3_, ...), custom_call_target="tpu_custom_call" | custom-call | bytes 21233664 | tf_op jit(solution)/shard_map/pallas_call | solution.py:605
  226.4 13.5 %shard_map.208 = (bf16[4,512,1152]{2,1,0:T(8,128)(2,1)}, bf16[4,512,1152]{2,1,0:T(8,128)(2,1)}) custom-call(bf16[512,1152]{1,0:T(8,128)(2,1)S(1)} %copy-done.13, bf16[4,1152,1152]{2,1,0:T(8,128)(2,1)} %bitcast.491, f32[4,1,1152]{2,1,0:T(1,128)S(1)} %copy.106.bias), custom_call_target="tpu_custom_call" | custom-call | flops 5435817984 | bytes 17694720 | tf_op jit(solution)/shard_map/pallas_call | solution.py:245
  239.9 7.8 %convolution_convert_fusion.1 = bf16[4,576,1152]{2,1,0:T(8,128)(2,1)} fusion(bf16[4,512,1152]{2,1,0:T(8,128)(2,1)} %get-tuple-element.103.hidden, s32[]{:T(128)S(6)} %select_n.805, bf16[512,1152]{1,0:T(8,128)(2,1)S(1)} %copy-done.16), kind=kOutput, calls=%fused_computation.5 | convolution fusion | flops 2720563200 | bytes 9109508 | tf_op jit(solution)/shard_map/jtd,te->jde/dot_general | solution.py:745
  248.0 8.8 %collective-permute-done.16 = bf16[4,576,1152]{2,1,0:T(8,128)(2,1)} collective-permute-done((bf16[4,576,1152]{2,1,0:T(8,128)(2,1)}, bf16[4,576,1152]{2,1,0:T(8,128)(2,1)}, u32[]{:S(2)}, u32[]{:S(2)}) %collective-permute-start.16) | collective-permute-done | bytes 5308448 | tf_op jit(solution)/shard_map/ppermute | solution.py:563
  256.8 7.3 add_convert_fusion.1
  278.2 21.0 %shard_map.209 = (bf16[4,512,1152]{2,1,0:T(8,128)(2,1)}, f32[4,1,1152]{2,1,0:T(1,128)S(1)}, bf16[512,1152]{1,0:T(8,128)(2,1)}, f32[2,1,1152]{2,1,0:T(1,128)S(1)}) custom-call(s32[2]{0:T(128)S(1)} %copy-done.11, bf16[4,512,1152]{2,1,0:T(8,128)(2,1)} %get-tuple-element.103.hidden, bf16[4,512,1152]{2,1,0:T(8,128)(2,1)} %get-tuple-element.104.slope, ...), custom_call_target="tpu_custom_call" | custom-call | flops 10871635968 | bytes 23592960 | tf_op jit(solution)/shard_map/pallas_call | solution.py:311
  302.0 8.0 %fusion.1 = bf16[4,576,1152]{2,1,0:T(8,128)(2,1)} fusion(bf16[4,512,1152]{2,1,0:T(8,128)(2,1)} %get-tuple-element.114.d_pre, bf16[512,1152]{1,0:T(8,128)(2,1)S(1)} %copy-done.14, s32[]{:T(128)S(6)} %select_n.805), kind=kOutput, calls=%fused_computation.7 | convolution fusion | flops 2720563200 | bytes 10682372 | tf_op jit(solution)/shard_map/td,jte->jde/dot_general | solution.py:745
  349.7 5.4 fusion
  355.5 7.1 collective-permute-done.23
  373.7 15.5 %shard_map.210 = (f32[512,1152]{1,0:T(8,128)}, bf16[512,1152]{1,0:T(8,128)(2,1)S(1)}, f32[2,4,1152]{2,1,0:T(4,128)S(1)}) custom-call(s32[2]{0:T(128)S(1)} %copy-done.11, bf16[4,512,1152]{2,1,0:T(8,128)(2,1)} %get-tuple-element.114.d_pre, bf16[4,1152,1152]{2,1,0:T(8,128)(2,1)} %bitcast.492, f32[2,6,1152]{2,1,0:T(8,128)S(1)} %copy-done.4, ...), custom_call_target="tpu_custom_call" | custom-call | flops 5435817984 | bytes 23592960 | tf_op jit(solution)/shard_map/pallas_call | solution.py:398
  389.3 5.4 collective-permute-done.25
  403.7 26.1 %shard_map.211 = (bf16[4,512,1152]{2,1,0:T(8,128)(2,1)}, f32[2,3,1152]{2,1,0:T(4,128)S(1)}) custom-call(s32[2]{0:T(128)S(1)} %copy-done.11, bf16[512,1152]{1,0:T(8,128)(2,1)S(1)} %get-tuple-element.118.d_proj, bf16[5,512,1152]{2,1,0:T(8,128)(2,1)} %get-tuple-element.119.parts, bf16[4,1152,1152]{2,1,0:T(8,128)(2,1)} %bitcast.511), custom_call_target="tpu_custom_call" | custom-call | flops 8153726976 | bytes 11796480 | tf_op jit(solution)/shard_map/pallas_call | solution.py:467
  429.9 8.7 %convolution_convert_fusion = bf16[4,576,1152]{2,1,0:T(8,128)(2,1)} fusion(bf16[4,512,1152]{2,1,0:T(8,128)(2,1)} %get-tuple-element.135.d_qkv, bf16[1,512,576]{1,2,0:T(8,128)(2,1)} %bitcast.525, bf16[1,512,576]{1,2,0:T(8,128)(2,1)} %bitcast.526), kind=kOutput, calls=%fused_computation.4 | convolution fusion | flops 2724102144 | bytes 11206656 | tf_op jit(solution)/shard_map/jtd,jte->jde/dot_general | solution.py:745
  442.6 5.1 collective-permute-done.35
  447.7 7.4 add_convert_fusion
  465.5 11.1 %shard_map.212 = (bf16[512,1152]{1,0:T(8,128)(2,1)}, f32[2,2,1152]{2,1,0:T(2,128)S(1)}) custom-call(bf16[4,512,1152]{2,1,0:T(8,128)(2,1)} %get-tuple-element.135.d_qkv, bf16[4,1152,1152]{2,1,0:T(8,128)(2,1)} %bitcast.512, f32[2,6,1152]{2,1,0:T(8,128)S(1)} %copy-done.4, bf16[512,1152]{1,0:T(8,128)(2,1)S(1)} %bitcast.485, f32[512,1152]{1,0:T(8,128)S(1)} %copy-done), custom_call_target="tpu_custom_call" | custom-call | flops 4076863488 | bytes 17694720 | tf_op jit(solution)/shard_map/pallas_call | solution.py:529
  478.0 13.2 %collective-permute-done.39 = bf16[144,1152]{1,0:T(8,128)(2,1)S(1)} collective-permute-done((bf16[144,1152]{1,0:T(8,128)(2,1)S(1)}, bf16[144,1152]{1,0:T(8,128)(2,1)S(1)}, u32[]{:S(2)}, u32[]{:S(2)}) %collective-permute-start.39) | collective-permute-done | bytes 331808 | tf_op jit(solution)/shard_map/ppermute | solution.py:568
  553.3 9.8 %all-to-all-start.2 = ((f32[8,1,3960]{2,1,0:T(1,128)}), f32[8,1,3960]{2,1,0:T(1,128)S(1)}, u32[]{:S(2)}, u32[]{:S(2)}) async-start(f32[8,1,3960]{2,1,0:T(1,128)} %all_to_all.29), calls=%async_computation.2 | async-start | bytes 253952 | tf_op jit(solution)/shard_map/all_to_all | solution.py:937
  565.2 4.6 all-to-all-done.2
  570.8 9.6 %all_gather.42 = f32[864,128]{1,0:T(8,128)} all-gather(f32[216,128]{1,0:T(8,128)S(1)} %reshape.282), channel_id=1, replica_groups=mesh['dp'=8,'fsdp'=4] {'fsdp'}, dimensions={0}, use_global_device_ids=true | all-gather | bytes 552960 | tf_op jit(solution)/shard_map/all_gather | solution.py:944
  588.8 5.2 collective-permute-start.55
  608.1 4.9 collective-permute-done.56
  632.5 9.9 %all-to-all-done.5 = bf16[4,3,144,288]{3,2,1,0:T(8,128)(2,1)S(1)} async-done(((bf16[4,3,144,288]{3,2,1,0:T(8,128)(2,1)}), bf16[4,3,144,288]{3,2,1,0:T(8,128)(2,1)S(1)}, u32[]{:S(2)}, u32[]{:S(2)}) %all-to-all-start.5) | async-done | bytes 995360 | tf_op jit(solution)/shard_map/all_to_all | solution.py:646
  646.5 4.6 all-to-all-start.4
  657.3 32.0 %all-gather.23.cloned.1.call-done = bf16[1152,1152]{1,0:T(8,128)(2,1)} async-done(((bf16[144,1152]{1,0:T(8,128)(2,1)}), bf16[1152,1152]{1,0:T(8,128)(2,1)}) %all-gather.23.cloned.1.call-update) | async-done | bytes 2654224 | tf_op jit(solution)/shard_map/all_gather | solution.py:697
  706.3 16.2 %all_gather.47 = f32[1728,128]{1,0:T(8,128)S(1)} all-gather(f32[216,128]{1,0:T(8,128)S(1)} %copy-done.83), channel_id=1, replica_groups=mesh['dp'=8,'fsdp'=4] {'dp'}, dimensions={0}, use_global_device_ids=true | all-gather | bytes 995328 | tf_op jit(solution)/shard_map/all_gather | solution.py:966
  739.9 5.4 fusion.186
  (554 shorter events, 312.0 us)
Async XLA Ops:
  8.0 129.7 %all-gather.9.cloned.1.call-start = ((), (), s32[]{:S(2)}) async-start(), calls=%async_computation.6 | async-start | bytes 10948608 | tf_op jit(solution)/shard_map/all_gather | solution.py:655
  23.9 251.7 %all-gather.11.cloned.1.call-start = ((), (), s32[]{:S(2)}) async-start(), calls=%async_computation.7 | async-start | bytes 10948608 | tf_op jit(solution)/shard_map/all_gather | solution.py:655
  39.6 55.0 %collective-permute-start.6 = (bf16[144,1152]{1,0:T(8,128)(2,1)S(1)}, bf16[144,1152]{1,0:T(8,128)(2,1)S(1)}, u32[]{:S(2)}, u32[]{:S(2)}) collective-permute-start(bf16[144,1152]{1,0:T(8,128)(2,1)S(1)} %concatenate.69.refs_0_), channel_id=1, source_target_pairs={{0,8},{4,12},{8,16},{12,20},{16,24},{20,28},{24,0},{28,4},{1,9},{5... | collective-permute-start | bytes 995336 | tf_op jit(solution)/shard_map/ppermute | solution.py:568
  41.9 52.8 %collective-permute-start.7 = (bf16[144,1152]{1,0:T(8,128)(2,1)S(1)}, bf16[144,1152]{1,0:T(8,128)(2,1)S(1)}, u32[]{:S(2)}, u32[]{:S(2)}) collective-permute-start(bf16[144,1152]{1,0:T(8,128)(2,1)S(1)} %concatenate.69.refs_0_), channel_id=1, source_target_pairs={{0,16},{4,20},{8,24},{12,28},{16,0},{20,4},{24,8},{28,12},{1,17},{... | collective-permute-start | bytes 995336 | tf_op jit(solution)/shard_map/ppermute | solution.py:568
  44.7 49.9 %collective-permute-start.8 = (bf16[144,1152]{1,0:T(8,128)(2,1)S(1)}, bf16[144,1152]{1,0:T(8,128)(2,1)S(1)}, u32[]{:S(2)}, u32[]{:S(2)}) collective-permute-start(bf16[144,1152]{1,0:T(8,128)(2,1)S(1)} %concatenate.69.refs_0_), channel_id=1, source_target_pairs={{0,24},{4,28},{8,0},{12,4},{16,8},{20,12},{24,16},{28,20},{1,25},{... | collective-permute-start | bytes 995336 | tf_op jit(solution)/shard_map/ppermute | solution.py:568
  96.2 30.6 %collective-permute-start.9 = (bf16[576,1152]{1,0:T(8,128)(2,1)S(1)}, bf16[576,1152]{1,0:T(8,128)(2,1)}, u32[]{:S(2)}, u32[]{:S(2)}) collective-permute-start(bf16[576,1152]{1,0:T(8,128)(2,1)S(1)} %shard_map.205), channel_id=1, source_target_pairs={{0,4},{4,0},{8,12},{12,8},{16,20},{20,16},{24,28},{28,24},{1,5},{5... | collective-permute-start | bytes 3981320 | tf_op jit(solution)/shard_map/ppermute | solution.py:563
  102.0 327.8 %all-gather.13.cloned.1.call-start = ((), (), s32[]{:S(2)}) async-start(), calls=%async_computation.8 | async-start | bytes 2985984 | tf_op jit(solution)/shard_map/all_gather | solution.py:697
  133.8 44.5 %collective-permute-start.10 = (bf16[576,1152]{1,0:T(8,128)(2,1)}, bf16[576,1152]{1,0:T(8,128)(2,1)}, u32[]{:S(2)}, u32[]{:S(2)}) collective-permute-start(bf16[576,1152]{1,0:T(8,128)(2,1)} %constant_dynamic-slice_fusion.4), channel_id=1, source_target_pairs={{0,1},{1,0},{2,3},{3,2},{4,5},{5,4},{6,7},{7,6},{8,9},{9,8},{10,11... | collective-permute-start | bytes 3981320 | tf_op jit(solution)/shard_map/ppermute | solution.py:573
  135.7 42.6 %collective-permute-start.11 = (bf16[576,1152]{1,0:T(8,128)(2,1)}, bf16[576,1152]{1,0:T(8,128)(2,1)}, u32[]{:S(2)}, u32[]{:S(2)}) collective-permute-start(bf16[576,1152]{1,0:T(8,128)(2,1)} %constant_dynamic-slice_fusion.4), channel_id=1, source_target_pairs={{0,2},{1,3},{2,0},{3,1},{4,6},{5,7},{6,4},{7,5},{8,10},{9,11},{10,... | collective-permute-start | bytes 3981320 | tf_op jit(solution)/shard_map/ppermute | solution.py:573
  135.9 74.3 %collective-permute-start.12 = (bf16[576,1152]{1,0:T(8,128)(2,1)}, bf16[576,1152]{1,0:T(8,128)(2,1)}, u32[]{:S(2)}, u32[]{:S(2)}) collective-permute-start(bf16[576,1152]{1,0:T(8,128)(2,1)} %constant_dynamic-slice_fusion.4), channel_id=1, source_target_pairs={{0,3},{1,2},{2,1},{3,0},{4,7},{5,6},{6,5},{7,4},{8,11},{9,10},{10,... | collective-permute-start | bytes 3981320 | tf_op jit(solution)/shard_map/ppermute | solution.py:573
  267.5 31.7 %collective-permute-start.20 = (bf16[2,2,144,1152]{3,2,1,0:T(8,128)(2,1)}, bf16[2,2,144,1152]{3,2,1,0:T(8,128)(2,1)}, u32[]{:S(2)}, u32[]{:S(2)}) collective-permute-start(bf16[2,2,144,1152]{3,2,1,0:T(8,128)(2,1)} %dynamic-slice_bitcast_fusion.5), channel_id=1, source_target_pairs={{0,1},{1,0},{2,3},{3,2},{4,5},{5,4},{6,7},{7,6},{8,9},{9,8},{10,11... | collective-permute-start | bytes 3981320 | tf_op jit(solution)/shard_map/ppermute | solution.py:573
  270.3 31.7 %collective-permute-start.21 = (bf16[2,2,144,1152]{3,2,1,0:T(8,128)(2,1)}, bf16[2,2,144,1152]{3,2,1,0:T(8,128)(2,1)}, u32[]{:S(2)}, u32[]{:S(2)}) collective-permute-start(bf16[2,2,144,1152]{3,2,1,0:T(8,128)(2,1)} %dynamic-slice_bitcast_fusion.4), channel_id=1, source_target_pairs={{0,2},{1,3},{2,0},{3,1},{4,6},{5,7},{6,4},{7,5},{8,10},{9,11},{10,... | collective-permute-start | bytes 3981320 | tf_op jit(solution)/shard_map/ppermute | solution.py:573
  310.1 39.6 %collective-permute-start.22 = (bf16[4,576,1152]{2,1,0:T(8,128)(2,1)}, bf16[4,576,1152]{2,1,0:T(8,128)(2,1)}, u32[]{:S(2)}, u32[]{:S(2)}) collective-permute-start(bf16[4,576,1152]{2,1,0:T(8,128)(2,1)} %fusion.1), channel_id=1, source_target_pairs={{0,4},{4,0},{8,12},{12,8},{16,20},{20,16},{24,28},{28,24},{1,5},{5... | collective-permute-start | bytes 15925256 | tf_op jit(solution)/shard_map/ppermute | solution.py:563
  331.8 192.5 %all-gather.15.cloned.1.call-start = ((), (), s32[]{:S(2)}) async-start(), calls=%async_computation.9 | async-start | bytes 2985984 | tf_op jit(solution)/shard_map/all_gather | solution.py:740
  365.7 29.0 %collective-permute-start.25 = (bf16[2,2,144,1152]{3,2,1,0:T(8,128)(2,1)}, bf16[2,2,144,1152]{3,2,1,0:T(8,128)(2,1)}, u32[]{:S(2)}, u32[]{:S(2)}) collective-permute-start(bf16[2,2,144,1152]{3,2,1,0:T(8,128)(2,1)} %dynamic-slice_bitcast_fusion.3), channel_id=1, source_target_pairs={{0,1},{1,0},{2,3},{3,2},{4,5},{5,4},{6,7},{7,6},{8,9},{9,8},{10,11... | collective-permute-start | bytes 3981320 | tf_op jit(solution)/shard_map/ppermute | solution.py:573
  366.4 28.8 %collective-permute-start.26 = (bf16[2,2,144,1152]{3,2,1,0:T(8,128)(2,1)S(1)}, bf16[2,2,144,1152]{3,2,1,0:T(8,128)(2,1)S(1)}, u32[]{:S(2)}, u32[]{:S(2)}) collective-permute-start(bf16[2,2,144,1152]{3,2,1,0:T(8,128)(2,1)S(1)} %dynamic-slice_bitcast_fusion.2), channel_id=1, source_target_pairs={{0,2},{1,3},{2,0},{3,1},{4,6},{5,7},{6,4},{7,5},{8,10},{9,11},{10,... | collective-permute-start | bytes 3981320 | tf_op jit(solution)/shard_map/ppermute | solution.py:573
  369.7 60.1 %collective-permute-start.29 = (bf16[144,1152]{1,0:T(8,128)(2,1)}, bf16[144,1152]{1,0:T(8,128)(2,1)}, u32[]{:S(2)}, u32[]{:S(2)}) collective-permute-start(bf16[144,1152]{1,0:T(8,128)(2,1)} %get-tuple-element.213), channel_id=1, source_target_pairs={{0,8},{4,12},{8,16},{12,20},{16,24},{20,28},{24,0},{28,4},{1,9},{5... | collective-permute-start | bytes 995336 | tf_op jit(solution)/shard_map/ppermute | solution.py:568
  369.7 60.1 %collective-permute-start.30 = (bf16[144,1152]{1,0:T(8,128)(2,1)}, bf16[144,1152]{1,0:T(8,128)(2,1)}, u32[]{:S(2)}, u32[]{:S(2)}) collective-permute-start(bf16[144,1152]{1,0:T(8,128)(2,1)} %get-tuple-element.214), channel_id=1, source_target_pairs={{0,16},{4,20},{8,24},{12,28},{16,0},{20,4},{24,8},{28,12},{1,17},{... | collective-permute-start | bytes 995336 | tf_op jit(solution)/shard_map/ppermute | solution.py:568
  369.7 60.1 %collective-permute-start.31 = (bf16[144,1152]{1,0:T(8,128)(2,1)}, bf16[144,1152]{1,0:T(8,128)(2,1)}, u32[]{:S(2)}, u32[]{:S(2)}) collective-permute-start(bf16[144,1152]{1,0:T(8,128)(2,1)} %get-tuple-element.211), channel_id=1, source_target_pairs={{0,24},{4,28},{8,0},{12,4},{16,8},{20,12},{24,16},{28,20},{1,25},{... | collective-permute-start | bytes 995336 | tf_op jit(solution)/shard_map/ppermute | solution.py:568
  398.9 31.0 %collective-permute-start.27 = (bf16[2,144,1152]{2,1,0:T(8,128)(2,1)S(1)}, bf16[2,144,1152]{2,1,0:T(8,128)(2,1)}, u32[]{:S(2)}, u32[]{:S(2)}) collective-permute-start(bf16[2,144,1152]{2,1,0:T(8,128)(2,1)S(1)} %dynamic-slice_bitcast_fusion.9), channel_id=1, source_target_pairs={{0,2},{1,3},{2,0},{3,1},{4,6},{5,7},{6,4},{7,5},{8,10},{9,11},{10,... | collective-permute-start | bytes 1990664 | tf_op jit(solution)/shard_map/ppermute | solution.py:573
  402.1 27.7 %collective-permute-start.28 = (bf16[2,144,1152]{2,1,0:T(8,128)(2,1)}, bf16[2,144,1152]{2,1,0:T(8,128)(2,1)}, u32[]{:S(2)}, u32[]{:S(2)}) collective-permute-start(bf16[2,144,1152]{2,1,0:T(8,128)(2,1)} %dynamic-slice_bitcast_fusion.8), channel_id=1, source_target_pairs={{0,1},{1,0},{2,3},{3,2},{4,5},{5,4},{6,7},{7,6},{8,9},{9,8},{10,11... | collective-permute-start | bytes 1990664 | tf_op jit(solution)/shard_map/ppermute | solution.py:573
  440.7 158.7 %all-gather.17.cloned.1.call-start = ((), (), s32[]{:S(2)}) async-start(), calls=%async_computation.10 | async-start | bytes 2985984 | tf_op jit(solution)/shard_map/all_gather | solution.py:740
  457.5 33.7 %collective-permute-start.36 = (bf16[2,2,144,1152]{3,2,1,0:T(8,128)(2,1)S(1)}, bf16[2,2,144,1152]{3,2,1,0:T(8,128)(2,1)S(1)}, u32[]{:S(2)}, u32[]{:S(2)}) collective-permute-start(bf16[2,2,144,1152]{3,2,1,0:T(8,128)(2,1)S(1)} %dynamic-slice_bitcast_fusion.1), channel_id=1, source_target_pairs={{0,1},{1,0},{2,3},{3,2},{4,5},{5,4},{6,7},{7,6},{8,9},{9,8},{10,11... | collective-permute-start | bytes 3981320 | tf_op jit(solution)/shard_map/ppermute | solution.py:573
  458.1 33.1 %collective-permute-start.37 = (bf16[2,2,144,1152]{3,2,1,0:T(8,128)(2,1)S(1)}, bf16[2,2,144,1152]{3,2,1,0:T(8,128)(2,1)S(1)}, u32[]{:S(2)}, u32[]{:S(2)}) collective-permute-start(bf16[2,2,144,1152]{3,2,1,0:T(8,128)(2,1)S(1)} %dynamic-slice_bitcast_fusion), channel_id=1, source_target_pairs={{0,2},{1,3},{2,0},{3,1},{4,6},{5,7},{6,4},{7,5},{8,10},{9,11},{10,... | collective-permute-start | bytes 3981320 | tf_op jit(solution)/shard_map/ppermute | solution.py:573
  461.7 29.4 %collective-permute-start.39 = (bf16[144,1152]{1,0:T(8,128)(2,1)S(1)}, bf16[144,1152]{1,0:T(8,128)(2,1)S(1)}, u32[]{:S(2)}, u32[]{:S(2)}) collective-permute-start(bf16[144,1152]{1,0:T(8,128)(2,1)S(1)} %get-tuple-element.210), channel_id=1, source_target_pairs={{0,16},{4,20},{8,24},{12,28},{16,0},{20,4},{24,8},{28,12},{1,17},{... | collective-permute-start | bytes 995336 | tf_op jit(solution)/shard_map/ppermute | solution.py:568
  462.0 29.2 %collective-permute-start.40 = (bf16[144,1152]{1,0:T(8,128)(2,1)S(1)}, bf16[144,1152]{1,0:T(8,128)(2,1)S(1)}, u32[]{:S(2)}, u32[]{:S(2)}) collective-permute-start(bf16[144,1152]{1,0:T(8,128)(2,1)S(1)} %get-tuple-element.207), channel_id=1, source_target_pairs={{0,24},{4,28},{8,0},{12,4},{16,8},{20,12},{24,16},{28,20},{1,25},{... | collective-permute-start | bytes 995336 | tf_op jit(solution)/shard_map/ppermute | solution.py:568
  493.6 110.0 %all-gather.19.cloned.1.call-start = ((), (), s32[]{:S(2)}) async-start(), calls=%async_computation.11 | async-start | bytes 2985984 | tf_op jit(solution)/shard_map/all_gather | solution.py:697
  547.5 22.4 %collective-permute-start.44 = (bf16[2,144,1152]{2,1,0:T(8,128)(2,1)}, bf16[2,144,1152]{2,1,0:T(8,128)(2,1)}, u32[]{:S(2)}, u32[]{:S(2)}) collective-permute-start(bf16[2,144,1152]{2,1,0:T(8,128)(2,1)} %dynamic-slice_bitcast_fusion.7), channel_id=1, source_target_pairs={{0,2},{1,3},{2,0},{3,1},{4,6},{5,7},{6,4},{7,5},{8,10},{9,11},{10,... | collective-permute-start | bytes 1990664 | tf_op jit(solution)/shard_map/ppermute | solution.py:573
  563.1 91.5 %all-gather.21.cloned.1.call-start = ((), (), s32[]{:S(2)}) async-start(), calls=%async_computation.12 | async-start | bytes 2985984 | tf_op jit(solution)/shard_map/all_gather | solution.py:740
  615.1 74.2 %all-gather.23.cloned.1.call-start = ((), (), s32[]{:S(2)}) async-start(), calls=%async_computation.13 | async-start | bytes 2985984 | tf_op jit(solution)/shard_map/all_gather | solution.py:697
  646.5 56.1 %all-to-all-start.4 = ((bf16[4,3,144,288]{3,2,1,0:T(8,128)(2,1)}), bf16[4,3,144,288]{3,2,1,0:T(8,128)(2,1)}, u32[]{:S(2)}, u32[]{:S(2)}) async-start(bf16[4,3,144,288]{3,2,1,0:T(8,128)(2,1)} %copy.132), calls=%async_computation.4 | async-start | bytes 2654208 | tf_op jit(solution)/shard_map/all_to_all | solution.py:646
  702.7 25.4 %all-to-all-start.3 = ((bf16[4,3,144,288]{3,2,1,0:T(8,128)(2,1)}), bf16[4,3,144,288]{3,2,1,0:T(8,128)(2,1)S(1)}, u32[]{:S(2)}, u32[]{:S(2)}) async-start(bf16[4,3,144,288]{3,2,1,0:T(8,128)(2,1)} %copy.130), calls=%async_computation.3 | async-start | bytes 2654208 | tf_op jit(solution)/shard_map/all_to_all | solution.py:646
  (142 other events, 1246.9 us)
Sparse Core Ops, SparseCore 0:
  24.0 107.1 all-gather.8
  134.8 99.8 all-gather.10
Sparse Core Ops, SparseCore 1:
  331.9 30.7 all-gather.12
  440.8 46.9 all-gather.14
  493.7 39.7 all-gather.16
  535.1 33.0 all-gather.18
  615.2 39.3 all-gather.20
  656.3 33.0 all-gather.22

commit v6 on v5

--- a/solution.py
+++ b/solution.py
@@ -577,40 +577,38 @@
     return lax.dynamic_index_in_dim(array, at, axis, keepdims=False)
 
 
-def place_kernel(count, at, *refs):
-    parts, whole, held_rows, semaphores = refs[:count], refs[count], refs[count + 1], refs[count + 2]
+def place_kernel(cuts, at, *refs):
+    parts, whole, held_rows, semaphores = refs[:-3], refs[-3], refs[-2], refs[-1]
     spans, loads, stores = [], [], []
-    for index, part in enumerate(parts):
-        first = pl.multiple_of(at[index] * 16, 16)
-        spans.append(pl.ds(first, part.shape[0]))
+    for index, (part, first, rows) in enumerate(cuts):
+        spans.append(pl.ds(pl.multiple_of(at[index] * 16, 16), rows))
+        source = parts[part].at[pl.ds(first, rows)]
         loads.append(
-            pltpu.make_async_copy(part, held_rows.at[spans[index]], semaphores.at[0, index])
+            pltpu.make_async_copy(source, held_rows.at[spans[index]], semaphores.at[0, index])
         )
         loads[index].start()
-    for index in range(count):
+    for index, span in enumerate(spans):
         loads[index].wait()
         stores.append(
-            pltpu.make_async_copy(
-                held_rows.at[spans[index]], whole.at[spans[index]], semaphores.at[1, index]
-            )
+            pltpu.make_async_copy(held_rows.at[span], whole.at[span], semaphores.at[1, index])
         )
         stores[index].start()
     for store in stores:
         store.wait()
 
 
-def place(parts, starts, rows):
+def place(parts, cuts, starts, rows):
     width = parts[0].shape[-1]
     dtype = parts[0].dtype
     return pl.pallas_call(
-        functools.partial(place_kernel, len(parts)),
+        functools.partial(place_kernel, cuts),
         in_specs=[pl.BlockSpec(memory_space=pltpu.SMEM)]
         + [pl.BlockSpec(memory_space=pl.ANY)] * len(parts),
         out_specs=pl.BlockSpec(memory_space=pl.ANY),
         out_shape=jax.ShapeDtypeStruct((rows, width), dtype),
         scratch_shapes=[
             pltpu.VMEM((rows, width), dtype),
-            pltpu.SemaphoreType.DMA((2, len(parts))),
+            pltpu.SemaphoreType.DMA((2, len(cuts))),
         ],
         compiler_params=pltpu.CompilerParams(vmem_limit_bytes=vmem_bytes),
         cost_estimate=pl.CostEstimate(
@@ -622,19 +620,23 @@
 def own_rows(parts, group):
     ranks, at = lax.axis_size("fsdp"), lax.axis_index("fsdp")
     shares = ranks // group
-    row_part, col_part = parts.shape[1:]
+    count, _, row_part, col_part = parts.shape
     chunk = row_part // shares
-    split = parts.reshape(ranks, chunk, col_part)
+    split = parts.reshape(count, group, shares, chunk, col_part).transpose(1, 2, 0, 3, 4)
+    split = split.reshape(ranks, count, chunk, col_part)
     if shares > 1:
         moved = lax.all_to_all(split, "fsdp", 0, 0, tiled=True)
-        return moved.transpose(1, 0, 2).reshape(chunk, ranks * col_part)
+        (moved,) = yield (moved,)
+        yield moved.transpose(1, 2, 0, 3).reshape(count, chunk, ranks * col_part)
+        return
     panels = [entry(split, at)]
     panels += [rank_swap(entry(split, at ^ bits), bits) for bits in range(1, ranks)]
+    panels = yield tuple(panels)
     placed = [
         lax.select_n(at, *[panels[panel ^ index] for index in range(ranks)])
         for panel in range(ranks)
     ]
-    return jnp.concatenate(placed, axis=1)
+    yield jnp.concatenate(placed, axis=2)
 
 
 def shard_rows(rows, group):
@@ -671,11 +673,11 @@
     half = total // 2
     unit = chunk // 16
     found = [rows] + [chip_shift(rows, step) for step in range(1, chips)]
-    line = place(found, [(chip - step) % chips * unit for step in range(chips)], half)
-    other = core_swap(line)
-    pairs = [part[step * chunk : (step + 1) * chunk] for part in (line, other) for step in range(chips)]
+    starts = [(chip - step) % chips * unit for step in range(chips)]
+    line = place(found, [(step, 0, chunk) for step in range(chips)], starts, half)
+    cuts = [(side, step * chunk, chunk) for side in range(2) for step in range(chips)]
     starts = [(2 * step + side) * unit for side in (core, 1 - core) for step in range(chips)]
-    own = place(pairs, starts, total)
+    own = place([line, core_swap(line)], cuts, starts, total)
     share = lax.dynamic_slice_in_dim(own, core * half, half, 0)
     mine = [rank_swap(share, bits) for bits in range(1, ranks)]
     own, *mine = yield (own, *mine)
@@ -684,17 +686,18 @@
         (at ^ bits) * 2 + side for side in (core, 1 - core) for bits in range(1, ranks)
     ]
     starts = [start * (half // 16) for start in starts]
-    yield place([own] + mine + others, starts, group * total).reshape(group, total, total)
+    cuts = [(0, 0, total)] + [(1 + index, 0, half) for index in range(2 * ranks - 2)]
+    found = place([own] + mine + others, cuts, starts, group * total)
+    yield found.reshape(group, total, total)
 
 
 def gather_own(rows, group):
     ranks = lax.axis_size("fsdp")
     shares = ranks // group
-    chunk, total = rows.shape
     if shares > 1:
         sets = [[share + shares * block for share in range(shares)] for block in range(group)]
-        rows = lax.all_gather(rows, "fsdp", axis=0, tiled=True, axis_index_groups=sets)
-    return lax.all_gather(rows, "dp", axis=0, tiled=True)
+        rows = lax.all_gather(rows, "fsdp", axis=1, tiled=True, axis_index_groups=sets)
+    return lax.all_gather(rows, "dp", axis=1, tiled=True)
 
 
 def sum_blocks(product, cut, total, group):
@@ -709,7 +712,7 @@
         )
         for _ in range(3):
             (rows,) = yield (rows,)
-        yield gather_own(rows, group)
+        yield gather_own(rows[None], group)[0]
         return
     chips, half = dp_count // 2, total // 2
     chunk = half // chips
@@ -788,26 +791,26 @@
     bias_part = biases.shape[0]
     stream = tokens.reshape(token_count, width)
     grad_out = cotangent.reshape(token_count, width)
-    pieces = [slice(mod_count + group * piece, mod_count + group * (piece + 1)) for piece in range(3)]
-
-    attn_rows = own_rows(narrow(weights[pieces[0]]), group)
-    cond_low = narrow(jax.nn.silu(conditioning))
-    attn_rows, one_shard, two_shard, cond_low = tie(
-        attn_rows, weights[pieces[1]], weights[pieces[2]], cond_low
-    )
-    attn_w = gather_blocks(attn_rows, group)
-    two_w = gather_blocks(own_rows(narrow(two_shard), group), group)
-    one_steps = gather_pieces(own_rows(narrow(one_shard), group), group)
+    low_weights = narrow(weights).reshape(block_count, row_part, col_part)
+    shards = low_weights[mod_count:].reshape(-1, group, row_part, col_part)
+
+    attn_rows, cond_low = own_rows(shards[:1], group), narrow(jax.nn.silu(conditioning))
+    attn_panels = next(attn_rows)
+    first_parts = lax.all_gather(packed([cond_low, narrow(biases)], 16), "dp", axis=0, tiled=True)
+    attn_panels, first_parts, other_shards = tie(attn_panels, first_parts, shards[1:])
+    attn_w = gather_blocks(attn_rows.send(attn_panels)[0], group)
+    other_rows = own_rows(other_shards, group)
+    other_rows = other_rows.send(next(other_rows))
+    one_steps = gather_pieces(other_rows[0], group)
     one_parts = next(one_steps)
-
-    first_parts = lax.all_gather(
-        packed([cond_low, narrow(biases)], 16), "dp", axis=0, tiled=True
-    ).reshape(dp_count, -1)
+    two_w = gather_blocks(other_rows[1], group)
+
+    first_parts = first_parts.reshape(dp_count, -1)
     cond_all = first_parts[:, : clip_count * width].reshape(all_clips, width)
     bias_rows = wide(first_parts[:, clip_count * width : clip_count * width + bias_part])
     cond_rows = lax.dynamic_slice_in_dim(cond_all, dp_at * row_part, row_part, 1)
     cond_cols = wide(lax.dynamic_slice_in_dim(cond_all, rank_at * col_part, col_part, 1))
-    mod_parts = fast_dot("cr,jre->cje", cond_rows, narrow(weights[:mod_count]))
+    mod_parts = fast_dot("cr,jre->cje", cond_rows, low_weights[:mod_count])
     mod_parts = lax.all_to_all(mod_parts, "dp", 0, 0, tiled=True)
     mod_cols = jnp.sum(mod_parts.reshape(dp_count, clip_count, mod_count, col_part), axis=0)
     left_cond = jnp.einsum("jrk,ck->jrc", left_roots[:mod_count], cond_cols, precision=precise)
@@ -830,9 +833,10 @@
     attn_in, parts, mixed, proj, resid, mlp_in, d_branch, d_branch_sums = run_attention(
         frames, frame_counts, stream, grad_out, mods, bias_table, attn_w
     )
-    left_rows = [own_rows(narrow(left_roots[piece]), group) for piece in pieces]
-    right_wholes = [gather_own(own_rows(narrow(right_roots[piece]), group), group) for piece in pieces]
-    mlp_in, one_parts = tie(mlp_in, one_parts)
+    roots = jnp.stack([narrow(left_roots[mod_count:]), narrow(right_roots[mod_count:])])
+    mlp_in, one_parts, roots = tie(mlp_in, one_parts, roots)
+    root_rows = own_rows(roots.reshape(-1, group, row_part, col_part), group)
+    root_panels = next(root_rows)
     one_w = one_steps.send(one_parts)
     hidden, slope = run_hidden(mlp_in, one_w, bias_table[4:8, None])
     two_steps = sum_blocks(
@@ -856,8 +860,10 @@
         resid,
         grad_out,
     )
-    d_pre, two_parts = tie(d_pre, two_parts)
+    d_pre, two_parts, root_panels = tie(d_pre, two_parts, root_panels)
     two_parts = list(two_steps.send(two_parts))
+    left_rows, right_rows = jnp.split(root_rows.send(root_panels), 2)
+    right_wholes = gather_own(right_rows, group)
     one_steps = sum_blocks(
         lambda left: fast_dot("td,jte->jde", left, d_pre),
         lambda first, size: lax.dynamic_slice_in_dim(mlp_in, first, size, 1),
@@ -873,9 +879,7 @@
     d_proj, one_parts = tie(d_proj, one_parts)
     one_parts = one_steps.send(one_parts)
     d_heads, head_sums = run_attention_back(frames, frame_counts, d_proj, parts, attn_w)
-    d_heads, one_parts, two_parts, right_wholes[2] = tie(
-        d_heads, one_parts, two_parts, right_wholes[2]
-    )
+    d_heads, one_parts, two_parts = tie(d_heads, one_parts, two_parts)
     whole_two = two_steps.send(two_parts)
     attn_steps = sum_blocks(
         lambda left: fast_dot("jtd,jte->jde", left, d_heads),
@@ -889,7 +893,9 @@
     d_heads, attn_parts[0], one_parts = tie(d_heads, attn_parts[0], one_parts)
     one_parts = one_steps.send(one_parts)
     input_grad, input_sums = run_input(d_heads, attn_w, mods, stream, d_resid)
-    input_sums, attn_parts, one_parts = tie(input_sums, attn_parts, one_parts)
+    input_sums, attn_parts, one_parts, right_wholes = tie(
+        input_sums, attn_parts, one_parts, right_wholes
+    )
     attn_parts = attn_steps.send(attn_parts)
     whole_one = one_steps.send(one_parts)
 
@@ -934,11 +940,10 @@
         ],
         axis=1,
     )
+    to_rows, attn_parts = tie(to_rows, attn_parts)
+    attn_parts = attn_steps.send(attn_parts)
     from_rows = lax.all_to_all(to_rows, "dp", 0, 0, tiled=True)
     products_two = owned_step(whole_two, left_rows[2], right_wholes[2], group)
-    from_rows, products_two, attn_parts = tie(from_rows, products_two, attn_parts)
-    attn_parts = attn_steps.send(attn_parts)
-    back_two = shard_rows(products_two, group)
     bias_grad = jnp.sum(from_rows[:, mod_size:], axis=0)
     mod_grad_cols = from_rows[:, :mod_size].reshape(all_clips, mod_count, col_part)
     mod_grad = lax.all_gather(packed([mod_grad_cols], 8), "fsdp", axis=0, tiled=True)
@@ -959,10 +964,10 @@
     cond_side = jnp.einsum("cb,bje->jce", cond_gram, mod_grad_cols, precision=precise)
     ada_right = jnp.einsum("cjr,jce->jre", mod_grad_rows, cond_side, precision=precise)
 
-    products_one = owned_step(whole_one, left_rows[1], right_wholes[1], group)
-    products_one, right_parts, attn_parts = tie(products_one, right_parts, attn_parts)
+    products_two, right_parts, attn_parts = tie(products_two, right_parts, attn_parts)
     whole_attn = attn_steps.send(attn_parts)
-    back_one = shard_rows(products_one, group)
+    back_two = shard_rows(products_two, group)
+    back_one = shard_rows(owned_step(whole_one, left_rows[1], right_wholes[1], group), group)
     right_parts = lax.all_gather(packed([right_parts], 8), "dp", axis=0, tiled=True)
     mod_right = jnp.sum(right_parts.reshape(dp_count, -1), axis=0)[: mod_grad_cols.size]
     mod_right = mod_right.reshape(all_clips, mod_count, col_part)

time: 760 us -> 798 us (1.050)
  waiting for transfers between devices: 176 us -> 245 us
  starting transfers between devices: 104 us -> 88 us
  blocking collectives: 83.7 us -> 67.8 us
  matrix products: 78.6 us -> 90.3 us
  local copies, waits for them, and re-layouts: 103 us -> 94 us
    ppermute x12, waiting for transfers between devices: 19.4 us -> 54.1 us  [chip_shift(): lax.ppermute(array, 'dp', [(at, (at + 2 * step) % count) for at in range(...]
    all_gather x1, blocking collectives: 48.3 us -> 14.7 us  [per_device(): lax.all_gather(packed([cond_low, narrow(biases)], 16), 'dp', axis=0, tile...]
    ppermute x42 -> x24, waiting for transfers between devices: 75.2 us -> 97.1 us  [rank_swap(): return lax.ppermute(array, 'fsdp', [(at, at ^ bits) for at in range(count)])]
    ppermute x42 -> x24, starting transfers between devices: 51.1 us -> 30 us  [rank_swap(): return lax.ppermute(array, 'fsdp', [(at, at ^ bits) for at in range(count)])]
    all_to_all x1, starting transfers between devices: 3.39 us -> 20.2 us  [per_device(): mod_parts = lax.all_to_all(mod_parts, 'dp', 0, 0, tiled=True)]
    all_gather x1, blocking collectives: 9.64 us -> 23.2 us  [per_device(): lax.all_gather(packed([mod_grad_cols], 8), 'fsdp', axis=0, tiled=True)]
    dot_general x22, matrix products: 65.5 us -> 78.9 us  [fast_dot(): jnp.einsum(subscripts, left, right, preferred_element_type=jnp.float32)]
    all_gather x3 -> x1, waiting for transfers between devices: 32 us -> 41.9 us  [gather_own(): return lax.all_gather(rows, 'dp', axis=1, tiled=True)]
  transfers between devices with their start and end apart: 75 -> 55, of which waited for: 33 -> 26; matrix products, arithmetic and copies ran while one was open for 23% -> 22% of each run, Pallas kernels for 19% -> 18%
where the time goes in v6:
time: 798 us; the launch traced here: 791 us
  waiting for transfers between devices  245 us (31%)
  Pallas kernels  140 us (18%)
  local copies, waits for them, and re-layouts  94 us (12%)
  matrix products  90.3 us (11%)
  starting transfers between devices  88 us (11%)
  blocking collectives  67.8 us (8%)
  other arithmetic  48.9 us (6%)
  between operations  16.1 us (2%)
    ppermute x24, waiting for transfers between devices, rank_swap(): return lax.ppermute(array, 'fsdp', [(at, at ^ bits) for at in range(count)])  97.1 us
    dot_general x22, matrix products, fast_dot(): jnp.einsum(subscripts, left, right, preferred_element_type=jnp.float32)  78.9 us
    ppermute x12, waiting for transfers between devices, chip_shift(): lax.ppermute(array, 'dp', [(at, (at + 2 * step) % count) for at in range(...  54.1 us
    all_gather x1, waiting for transfers between devices, gather_own(): return lax.all_gather(rows, 'dp', axis=1, tiled=True)  41.9 us
    pallas_call x1, Pallas kernels, run_attention(): pl.pallas_call(functools.partial(attention_kernel, frames), grid=(clips,)...  39.6 us
    ppermute x24, starting transfers between devices, rank_swap(): return lax.ppermute(array, 'fsdp', [(at, at ^ bits) for at in range(count)])  30 us
    pallas_call x1, Pallas kernels, run_attention_back(): pl.pallas_call(functools.partial(attention_back_kernel, frames), grid=(cl...  26.1 us
    all_gather x1, blocking collectives, per_device(): lax.all_gather(packed([mod_grad_cols], 8), 'fsdp', axis=0, tiled=True)  23.2 us
  transfers between devices with their start and end apart: 55, of which 26 were waited for; matrix products, arithmetic and copies ran while one was open for 22% of the time, Pallas kernels for 18%

profile of v6, /device:TPU:0, one launch (start us, length us, event | category | flops | bytes accessed | tf_op | source)
XLA Modules:
  0.0 790.9 jit_solution(12758769882737724126)
XLA Ops:
  14.5 14.7 %all_gather.30 = bf16[256,128]{1,0:T(8,128)(2,1)S(1)} all-gather(bf16[32,128]{1,0:T(8,128)(2,1)S(1)} %fusion.183), channel_id=1, replica_groups=mesh['dp'=8,'fsdp'=4] {'dp'}, dimensions={0}, use_global_device_ids=true | all-gather | bytes 73728 | tf_op jit(solution)/shard_map/all_gather | solution.py:799
  40.4 5.6 collective-permute-done.5
  55.3 9.7 %collective-permute-done.6.refs_1_ = bf16[144,1152]{1,0:T(8,128)(2,1)S(1)} collective-permute-done((bf16[144,1152]{1,0:T(8,128)(2,1)S(1)}, bf16[144,1152]{1,0:T(8,128)(2,1)S(1)}, u32[]{:S(2)}, u32[]{:S(2)}) %collective-permute-start.6) | collective-permute-done | bytes 331808 | tf_op jit(solution)/shard_map/ppermute | solution.py:568
  64.9 16.0 %collective-permute-done.7.refs_2_ = bf16[144,1152]{1,0:T(8,128)(2,1)S(1)} collective-permute-done((bf16[144,1152]{1,0:T(8,128)(2,1)S(1)}, bf16[144,1152]{1,0:T(8,128)(2,1)S(1)}, u32[]{:S(2)}, u32[]{:S(2)}) %collective-permute-start.7) | collective-permute-done | bytes 331808 | tf_op jit(solution)/shard_map/ppermute | solution.py:568
  89.6 20.2 %all-to-all-start = ((f32[16,6,288]{2,1,0:T(8,128)}), f32[16,6,288]{2,1,0:T(8,128)S(1)}, u32[]{:S(2)}, u32[]{:S(2)}) async-start(f32[16,6,288]{2,1,0:T(8,128)} %copy.118), calls=%async_computation | async-start | bytes 393216 | tf_op jit(solution)/shard_map/all_to_all | solution.py:814
  112.5 11.6 %all-to-all-done = f32[16,6,288]{2,1,0:T(8,128)S(1)} async-done(((f32[16,6,288]{2,1,0:T(8,128)}), f32[16,6,288]{2,1,0:T(8,128)S(1)}, u32[]{:S(2)}, u32[]{:S(2)}) %all-to-all-start) | async-done | bytes 110624 | tf_op jit(solution)/shard_map/all_to_all | solution.py:814
  124.3 9.9 %all_gather.31 = f32[672,128]{1,0:T(8,128)S(1)} all-gather(f32[168,128]{1,0:T(8,128)S(1)} %pad_bitcast_fusion), channel_id=1, replica_groups=mesh['dp'=8,'fsdp'=4] {'fsdp'}, dimensions={0}, use_global_device_ids=true | all-gather | bytes 430080 | tf_op jit(solution)/shard_map/all_gather | solution.py:818
  144.3 39.6 %shard_map.204 = (bf16[512,1152]{1,0:T(8,128)(2,1)S(1)}, bf16[5,512,1152]{2,1,0:T(8,128)(2,1)}, bf16[512,1152]{1,0:T(8,128)(2,1)S(1)}, f32[512,1152]{1,0:T(8,128...) custom-call(s32[2]{0:T(128)S(1)} %copy-done.14, ...), custom_call_target="tpu_custom_call" | custom-call | flops 8153726976 | bytes 23592960 | tf_op jit(solution)/shard_map/pallas_call | solution.py:187
  184.9 29.7 %collective-permute-done.12.refs_3_ = bf16[576,1152]{1,0:T(8,128)(2,1)} collective-permute-done((bf16[576,1152]{1,0:T(8,128)(2,1)}, bf16[576,1152]{1,0:T(8,128)(2,1)}, u32[]{:S(2)}, u32[]{:S(2)}) %collective-permute-start.12) | collective-permute-done | bytes 1327136 | tf_op jit(solution)/shard_map/ppermute | solution.py:573
  222.0 8.6 %shard_map.207 = bf16[4608,1152]{1,0:T(8,128)(2,1)} custom-call(s32[7]{0:T(128)S(1)} %stack.157.at, bf16[1152,1152]{1,0:T(8,128)(2,1)} %shard_map.206.refs_0_, bf16[576,1152]{1,0:T(8,128)(2,1)} %collective-permute-done.10.refs_1_, bf16[576,1152]{1,0:T(8,128)(2,1)} %collective-permute-done.11.refs_2_, bf16[576,1152]{1,0:T(8,128)(2,1)} %collective-permute-done.12.refs_3_, ...), custom_call_target="tpu_custom_call" | custom-call | bytes 21233664 | tf_op jit(solution)/shard_map/pallas_call | solution.py:603
  230.7 13.5 %shard_map.208 = (bf16[4,512,1152]{2,1,0:T(8,128)(2,1)}, bf16[4,512,1152]{2,1,0:T(8,128)(2,1)}) custom-call(bf16[512,1152]{1,0:T(8,128)(2,1)S(1)} %copy-done.16, bf16[4,1152,1152]{2,1,0:T(8,128)(2,1)} %bitcast.396, f32[4,1,1152]{2,1,0:T(1,128)S(1)} %copy.130.bias), custom_call_target="tpu_custom_call" | custom-call | flops 5435817984 | bytes 17694720 | tf_op jit(solution)/shard_map/pallas_call | solution.py:245
  244.1 7.9 %convolution_convert_fusion.1 = bf16[4,576,1152]{2,1,0:T(8,128)(2,1)} fusion(bf16[4,512,1152]{2,1,0:T(8,128)(2,1)} %get-tuple-element.112.hidden, s32[]{:T(128)S(6)} %select_n.438, bf16[512,1152]{1,0:T(8,128)(2,1)S(1)} %copy-done.19), kind=kOutput, calls=%fused_computation.5 | convolution fusion | flops 2720563200 | bytes 9109508 | tf_op jit(solution)/shard_map/jtd,te->jde/dot_general | solution.py:748
  252.3 8.9 %collective-permute-done.16 = bf16[4,576,1152]{2,1,0:T(8,128)(2,1)} collective-permute-done((bf16[4,576,1152]{2,1,0:T(8,128)(2,1)}, bf16[4,576,1152]{2,1,0:T(8,128)(2,1)}, u32[]{:S(2)}, u32[]{:S(2)}) %collective-permute-start.16) | collective-permute-done | bytes 5308448 | tf_op jit(solution)/shard_map/ppermute | solution.py:563
  261.2 7.7 add_convert_fusion.1
  286.9 20.8 %shard_map.209 = (bf16[4,512,1152]{2,1,0:T(8,128)(2,1)}, f32[4,1,1152]{2,1,0:T(1,128)S(1)}, bf16[512,1152]{1,0:T(8,128)(2,1)}, f32[2,1,1152]{2,1,0:T(1,128)S(1)}) custom-call(s32[2]{0:T(128)S(1)} %copy-done.14, bf16[4,512,1152]{2,1,0:T(8,128)(2,1)} %get-tuple-element.112.hidden, bf16[4,512,1152]{2,1,0:T(8,128)(2,1)} %get-tuple-element.113.slope, ...), custom_call_target="tpu_custom_call" | custom-call | flops 10871635968 | bytes 23592960 | tf_op jit(solution)/shard_map/pallas_call | solution.py:311
  307.7 11.2 %collective-permute-done.19 = bf16[6,144,288]{2,1,0:T(8,128)(2,1)} collective-permute-done((bf16[6,144,288]{2,1,0:T(8,128)(2,1)}, bf16[6,144,288]{2,1,0:T(8,128)(2,1)}, u32[]{:S(2)}, u32[]{:S(2)}) %collective-permute-start.19) | collective-permute-done | bytes 497696 | tf_op jit(solution)/shard_map/ppermute | solution.py:573
  318.9 16.8 %collective-permute-done.20 = bf16[6,144,288]{2,1,0:T(8,128)(2,1)} collective-permute-done((bf16[6,144,288]{2,1,0:T(8,128)(2,1)}, bf16[6,144,288]{2,1,0:T(8,128)(2,1)}, u32[]{:S(2)}, u32[]{:S(2)}) %collective-permute-start.20) | collective-permute-done | bytes 497696 | tf_op jit(solution)/shard_map/ppermute | solution.py:573
  335.7 7.8 fusion.1
  354.4 7.6 fusion
  378.7 15.9 %shard_map.210 = (f32[512,1152]{1,0:T(8,128)}, bf16[512,1152]{1,0:T(8,128)(2,1)S(1)}, f32[2,4,1152]{2,1,0:T(4,128)S(1)}) custom-call(s32[2]{0:T(128)S(1)} %copy-done.14, bf16[4,512,1152]{2,1,0:T(8,128)(2,1)} %get-tuple-element.123.d_pre, bf16[4,1152,1152]{2,1,0:T(8,128)(2,1)} %bitcast.397, f32[2,6,1152]{2,1,0:T(8,128)S(1)} %copy-done.4, ...), custom_call_target="tpu_custom_call" | custom-call | flops 5435817984 | bytes 23592960 | tf_op jit(solution)/shard_map/pallas_call | solution.py:398
  394.6 8.3 %collective-permute-done.25 = bf16[2,2,144,1152]{3,2,1,0:T(8,128)(2,1)} collective-permute-done((bf16[2,2,144,1152]{3,2,1,0:T(8,128)(2,1)}, bf16[2,2,144,1152]{3,2,1,0:T(8,128)(2,1)}, u32[]{:S(2)}, u32[]{:S(2)}) %collective-permute-start.25) | collective-permute-done | bytes 1327136 | tf_op jit(solution)/shard_map/ppermute | solution.py:573
  409.5 26.1 %shard_map.211 = (bf16[4,512,1152]{2,1,0:T(8,128)(2,1)}, f32[2,3,1152]{2,1,0:T(4,128)S(1)}) custom-call(s32[2]{0:T(128)S(1)} %copy-done.14, bf16[512,1152]{1,0:T(8,128)(2,1)S(1)} %get-tuple-element.127.d_proj, bf16[5,512,1152]{2,1,0:T(8,128)(2,1)} %get-tuple-element.128.parts, bf16[4,1152,1152]{2,1,0:T(8,128)(2,1)} %bitcast.412), custom_call_target="tpu_custom_call" | custom-call | flops 8153726976 | bytes 11796480 | tf_op jit(solution)/shard_map/pallas_call | solution.py:467
  442.8 5.5 concatenate.56
  455.9 7.4 convolution_convert_fusion
  463.9 8.6 %all-gather.11.cloned.1.call-done = bf16[1152,1152]{1,0:T(8,128)(2,1)} async-done(((bf16[144,1152]{1,0:T(8,128)(2,1)}), bf16[1152,1152]{1,0:T(8,128)(2,1)}) %all-gather.11.cloned.1.call-update) | async-done | bytes 2654224 | tf_op jit(solution)/shard_map/all_gather | solution.py:743
  479.6 6.2 add_convert_fusion
  495.9 11.4 %shard_map.212 = (bf16[512,1152]{1,0:T(8,128)(2,1)}, f32[2,2,1152]{2,1,0:T(2,128)S(1)}) custom-call(bf16[4,512,1152]{2,1,0:T(8,128)(2,1)} %get-tuple-element.144.d_qkv, bf16[4,1152,1152]{2,1,0:T(8,128)(2,1)} %bitcast.413, f32[2,6,1152]{2,1,0:T(8,128)S(1)} %copy-done.5, bf16[512,1152]{1,0:T(8,128)(2,1)S(1)} %bitcast.385, f32[512,1152]{1,0:T(8,128)S(1)} %copy-done), custom_call_target="tpu_custom_call" | custom-call | flops 4076863488 | bytes 17694720 | tf_op jit(solution)/shard_map/pallas_call | solution.py:529
  511.6 23.2 %collective-permute-done.36 = bf16[144,1152]{1,0:T(8,128)(2,1)S(1)} collective-permute-done((bf16[144,1152]{1,0:T(8,128)(2,1)S(1)}, bf16[144,1152]{1,0:T(8,128)(2,1)S(1)}, u32[]{:S(2)}, u32[]{:S(2)}) %collective-permute-start.36) | collective-permute-done | bytes 331808 | tf_op jit(solution)/shard_map/ppermute | solution.py:568
  536.9 41.9 %all-gather.9.cloned.1.call-done = bf16[3,1152,1152]{2,1,0:T(8,128)(2,1)} async-done(((bf16[3,144,1152]{2,1,0:T(8,128)(2,1)}), bf16[3,1152,1152]{2,1,0:T(8,128)(2,1)}) %all-gather.9.cloned.1.call-update) | async-done | bytes 7962640 | tf_op jit(solution)/shard_map/all_gather | solution.py:700
  634.4 23.2 %all_gather.35 = f32[864,128]{1,0:T(8,128)S(1)} all-gather(f32[216,128]{1,0:T(8,128)S(1)} %reshape.353), channel_id=1, replica_groups=mesh['dp'=8,'fsdp'=4] {'fsdp'}, dimensions={0}, use_global_device_ids=true | all-gather | bytes 552960 | tf_op jit(solution)/shard_map/all_gather | solution.py:949
  677.9 20.1 %all_gather.39 = f32[1728,128]{1,0:T(8,128)S(1)} all-gather(f32[216,128]{1,0:T(8,128)S(1)} %reshape.367), channel_id=1, replica_groups=mesh['dp'=8,'fsdp'=4] {'dp'}, dimensions={0}, use_global_device_ids=true | all-gather | bytes 995328 | tf_op jit(solution)/shard_map/all_gather | solution.py:971
  756.7 9.8 %all-to-all-done.3 = bf16[4,3,144,288]{3,2,1,0:T(8,128)(2,1)S(1)} async-done(((bf16[4,3,144,288]{3,2,1,0:T(8,128)(2,1)}), bf16[4,3,144,288]{3,2,1,0:T(8,128)(2,1)S(1)}, u32[]{:S(2)}, u32[]{:S(2)}) %all-to-all-start.3) | async-done | bytes 995360 | tf_op jit(solution)/shard_map/all_to_all | solution.py:648
  (453 shorter events, 299.5 us)
Async XLA Ops:
  7.2 137.1 %all-gather.17.cloned.1.call-start = ((), (), s32[]{:S(2)}) async-start(), calls=%async_computation.10 | async-start | bytes 10948608 | tf_op jit(solution)/shard_map/all_gather | solution.py:657
  31.9 252.3 %all-gather.19.cloned.1.call-start = ((), (), s32[]{:S(2)}) async-start(), calls=%async_computation.11 | async-start | bytes 10948608 | tf_op jit(solution)/shard_map/all_gather | solution.py:657
  52.6 28.3 %collective-permute-start.7 = (bf16[144,1152]{1,0:T(8,128)(2,1)S(1)}, bf16[144,1152]{1,0:T(8,128)(2,1)S(1)}, u32[]{:S(2)}, u32[]{:S(2)}) collective-permute-start(bf16[144,1152]{1,0:T(8,128)(2,1)S(1)} %get-tuple-element.239.refs_0_), channel_id=1, source_target_pairs={{0,16},{4,20},{8,24},{12,28},{16,0},{20,4},{24,8},{28,12},{1,17},{... | collective-permute-start | bytes 995336 | tf_op jit(solution)/shard_map/ppermute | solution.py:568
  82.5 52.3 %collective-permute-start.9 = (bf16[576,1152]{1,0:T(8,128)(2,1)S(1)}, bf16[576,1152]{1,0:T(8,128)(2,1)S(1)}, u32[]{:S(2)}, u32[]{:S(2)}) collective-permute-start(bf16[576,1152]{1,0:T(8,128)(2,1)S(1)} %shard_map.205.refs_0_), channel_id=1, source_target_pairs={{0,4},{4,0},{8,12},{12,8},{16,20},{20,16},{24,28},{28,24},{1,5},{5... | collective-permute-start | bytes 3981320 | tf_op jit(solution)/shard_map/ppermute | solution.py:563
  89.6 34.5 %all-to-all-start = ((f32[16,6,288]{2,1,0:T(8,128)}), f32[16,6,288]{2,1,0:T(8,128)S(1)}, u32[]{:S(2)}, u32[]{:S(2)}) async-start(f32[16,6,288]{2,1,0:T(8,128)} %copy.118), calls=%async_computation | async-start | bytes 393216 | tf_op jit(solution)/shard_map/all_to_all | solution.py:814
  109.8 362.8 %all-gather.11.cloned.1.call-start = ((), (), s32[]{:S(2)}) async-start(), calls=%async_computation.7 | async-start | bytes 2985984 | tf_op jit(solution)/shard_map/all_gather | solution.py:743
  140.4 44.5 %collective-permute-start.10 = (bf16[576,1152]{1,0:T(8,128)(2,1)}, bf16[576,1152]{1,0:T(8,128)(2,1)}, u32[]{:S(2)}, u32[]{:S(2)}) collective-permute-start(bf16[576,1152]{1,0:T(8,128)(2,1)} %constant_dynamic-slice_fusion.4), channel_id=1, source_target_pairs={{0,1},{1,0},{2,3},{3,2},{4,5},{5,4},{6,7},{7,6},{8,9},{9,8},{10,11... | collective-permute-start | bytes 3981320 | tf_op jit(solution)/shard_map/ppermute | solution.py:573
  141.3 43.6 %collective-permute-start.11 = (bf16[576,1152]{1,0:T(8,128)(2,1)}, bf16[576,1152]{1,0:T(8,128)(2,1)}, u32[]{:S(2)}, u32[]{:S(2)}) collective-permute-start(bf16[576,1152]{1,0:T(8,128)(2,1)} %constant_dynamic-slice_fusion.4), channel_id=1, source_target_pairs={{0,2},{1,3},{2,0},{3,1},{4,6},{5,7},{6,4},{7,5},{8,10},{9,11},{10,... | collective-permute-start | bytes 3981320 | tf_op jit(solution)/shard_map/ppermute | solution.py:573
  142.5 72.1 %collective-permute-start.12 = (bf16[576,1152]{1,0:T(8,128)(2,1)}, bf16[576,1152]{1,0:T(8,128)(2,1)}, u32[]{:S(2)}, u32[]{:S(2)}) collective-permute-start(bf16[576,1152]{1,0:T(8,128)(2,1)} %constant_dynamic-slice_fusion.4), channel_id=1, source_target_pairs={{0,3},{1,2},{2,1},{3,0},{4,7},{5,6},{6,5},{7,4},{8,11},{9,10},{10,... | collective-permute-start | bytes 3981320 | tf_op jit(solution)/shard_map/ppermute | solution.py:573
  272.4 63.3 %collective-permute-start.17 = (bf16[2,2,144,1152]{3,2,1,0:T(8,128)(2,1)}, bf16[2,2,144,1152]{3,2,1,0:T(8,128)(2,1)}, u32[]{:S(2)}, u32[]{:S(2)}) collective-permute-start(bf16[2,2,144,1152]{3,2,1,0:T(8,128)(2,1)} %dynamic-slice_bitcast_fusion.5), channel_id=1, source_target_pairs={{0,1},{1,0},{2,3},{3,2},{4,5},{5,4},{6,7},{7,6},{8,9},{9,8},{10,11... | collective-permute-start | bytes 3981320 | tf_op jit(solution)/shard_map/ppermute | solution.py:573
  273.9 61.8 %collective-permute-start.18 = (bf16[2,2,144,1152]{3,2,1,0:T(8,128)(2,1)}, bf16[2,2,144,1152]{3,2,1,0:T(8,128)(2,1)}, u32[]{:S(2)}, u32[]{:S(2)}) collective-permute-start(bf16[2,2,144,1152]{3,2,1,0:T(8,128)(2,1)} %dynamic-slice_bitcast_fusion.4), channel_id=1, source_target_pairs={{0,2},{1,3},{2,0},{3,1},{4,6},{5,7},{6,4},{7,5},{8,10},{9,11},{10,... | collective-permute-start | bytes 3981320 | tf_op jit(solution)/shard_map/ppermute | solution.py:573
  280.7 38.2 %collective-permute-start.19 = (bf16[6,144,288]{2,1,0:T(8,128)(2,1)}, bf16[6,144,288]{2,1,0:T(8,128)(2,1)}, u32[]{:S(2)}, u32[]{:S(2)}) collective-permute-start(bf16[6,144,288]{2,1,0:T(8,128)(2,1)} %get-tuple-element.204), channel_id=1, source_target_pairs={{0,1},{1,0},{2,3},{3,2},{4,5},{5,4},{6,7},{7,6},{8,9},{9,8},{10,11... | collective-permute-start | bytes 1493000 | tf_op jit(solution)/shard_map/ppermute | solution.py:573
  280.7 55.0 %collective-permute-start.20 = (bf16[6,144,288]{2,1,0:T(8,128)(2,1)}, bf16[6,144,288]{2,1,0:T(8,128)(2,1)}, u32[]{:S(2)}, u32[]{:S(2)}) collective-permute-start(bf16[6,144,288]{2,1,0:T(8,128)(2,1)} %get-tuple-element.203), channel_id=1, source_target_pairs={{0,2},{1,3},{2,0},{3,1},{4,6},{5,7},{6,4},{7,5},{8,10},{9,11},{10,... | collective-permute-start | bytes 1493000 | tf_op jit(solution)/shard_map/ppermute | solution.py:573
  280.7 55.0 %collective-permute-start.21 = (bf16[6,144,288]{2,1,0:T(8,128)(2,1)}, bf16[6,144,288]{2,1,0:T(8,128)(2,1)}, u32[]{:S(2)}, u32[]{:S(2)}) collective-permute-start(bf16[6,144,288]{2,1,0:T(8,128)(2,1)} %get-tuple-element.202), channel_id=1, source_target_pairs={{0,3},{1,2},{2,1},{3,0},{4,7},{5,6},{6,5},{7,4},{8,11},{9,10},{10,... | collective-permute-start | bytes 1493000 | tf_op jit(solution)/shard_map/ppermute | solution.py:573
  372.2 30.7 %collective-permute-start.25 = (bf16[2,2,144,1152]{3,2,1,0:T(8,128)(2,1)}, bf16[2,2,144,1152]{3,2,1,0:T(8,128)(2,1)}, u32[]{:S(2)}, u32[]{:S(2)}) collective-permute-start(bf16[2,2,144,1152]{3,2,1,0:T(8,128)(2,1)} %dynamic-slice_bitcast_fusion.3), channel_id=1, source_target_pairs={{0,1},{1,0},{2,3},{3,2},{4,5},{5,4},{6,7},{7,6},{8,9},{9,8},{10,11... | collective-permute-start | bytes 3981320 | tf_op jit(solution)/shard_map/ppermute | solution.py:573
  372.6 30.3 %collective-permute-start.26 = (bf16[2,2,144,1152]{3,2,1,0:T(8,128)(2,1)S(1)}, bf16[2,2,144,1152]{3,2,1,0:T(8,128)(2,1)}, u32[]{:S(2)}, u32[]{:S(2)}) collective-permute-start(bf16[2,2,144,1152]{3,2,1,0:T(8,128)(2,1)S(1)} %dynamic-slice_bitcast_fusion.2), channel_id=1, source_target_pairs={{0,2},{1,3},{2,0},{3,1},{4,6},{5,7},{6,4},{7,5},{8,10},{9,11},{10,... | collective-permute-start | bytes 3981320 | tf_op jit(solution)/shard_map/ppermute | solution.py:573
  374.8 60.8 %collective-permute-start.29 = (bf16[144,1152]{1,0:T(8,128)(2,1)}, bf16[144,1152]{1,0:T(8,128)(2,1)}, u32[]{:S(2)}, u32[]{:S(2)}) collective-permute-start(bf16[144,1152]{1,0:T(8,128)(2,1)} %get-tuple-element.229), channel_id=1, source_target_pairs={{0,8},{4,12},{8,16},{12,20},{16,24},{20,28},{24,0},{28,4},{1,9},{5... | collective-permute-start | bytes 995336 | tf_op jit(solution)/shard_map/ppermute | solution.py:568
  374.8 60.8 %collective-permute-start.30 = (bf16[144,1152]{1,0:T(8,128)(2,1)}, bf16[144,1152]{1,0:T(8,128)(2,1)}, u32[]{:S(2)}, u32[]{:S(2)}) collective-permute-start(bf16[144,1152]{1,0:T(8,128)(2,1)} %get-tuple-element.230), channel_id=1, source_target_pairs={{0,16},{4,20},{8,24},{12,28},{16,0},{20,4},{24,8},{28,12},{1,17},{... | collective-permute-start | bytes 995336 | tf_op jit(solution)/shard_map/ppermute | solution.py:568
  374.8 60.8 %collective-permute-start.31 = (bf16[144,1152]{1,0:T(8,128)(2,1)}, bf16[144,1152]{1,0:T(8,128)(2,1)}, u32[]{:S(2)}, u32[]{:S(2)}) collective-permute-start(bf16[144,1152]{1,0:T(8,128)(2,1)} %get-tuple-element.227), channel_id=1, source_target_pairs={{0,24},{4,28},{8,0},{12,4},{16,8},{20,12},{24,16},{28,20},{1,25},{... | collective-permute-start | bytes 995336 | tf_op jit(solution)/shard_map/ppermute | solution.py:568
  405.5 30.2 %collective-permute-start.27 = (bf16[2,144,1152]{2,1,0:T(8,128)(2,1)S(1)}, bf16[2,144,1152]{2,1,0:T(8,128)(2,1)S(1)}, u32[]{:S(2)}, u32[]{:S(2)}) collective-permute-start(bf16[2,144,1152]{2,1,0:T(8,128)(2,1)S(1)} %dynamic-slice_bitcast_fusion.9), channel_id=1, source_target_pairs={{0,2},{1,3},{2,0},{3,1},{4,6},{5,7},{6,4},{7,5},{8,10},{9,11},{10,... | collective-permute-start | bytes 1990664 | tf_op jit(solution)/shard_map/ppermute | solution.py:573
  407.8 27.9 %collective-permute-start.28 = (bf16[2,144,1152]{2,1,0:T(8,128)(2,1)S(1)}, bf16[2,144,1152]{2,1,0:T(8,128)(2,1)S(1)}, u32[]{:S(2)}, u32[]{:S(2)}) collective-permute-start(bf16[2,144,1152]{2,1,0:T(8,128)(2,1)S(1)} %dynamic-slice_bitcast_fusion.8), channel_id=1, source_target_pairs={{0,1},{1,0},{2,3},{3,2},{4,5},{5,4},{6,7},{7,6},{8,9},{9,8},{10,11... | collective-permute-start | bytes 1990664 | tf_op jit(solution)/shard_map/ppermute | solution.py:573
  439.5 139.3 %all-gather.9.cloned.1.call-start = ((), (), s32[]{:S(2)}) async-start(), calls=%async_computation.6 | async-start | bytes 8957952 | tf_op jit(solution)/shard_map/all_gather | solution.py:700
  488.3 47.4 %collective-permute-start.33 = (bf16[2,2,144,1152]{3,2,1,0:T(8,128)(2,1)S(1)}, bf16[2,2,144,1152]{3,2,1,0:T(8,128)(2,1)S(1)}, u32[]{:S(2)}, u32[]{:S(2)}) collective-permute-start(bf16[2,2,144,1152]{3,2,1,0:T(8,128)(2,1)S(1)} %dynamic-slice_bitcast_fusion.1), channel_id=1, source_target_pairs={{0,1},{1,0},{2,3},{3,2},{4,5},{5,4},{6,7},{7,6},{8,9},{9,8},{10,11... | collective-permute-start | bytes 3981320 | tf_op jit(solution)/shard_map/ppermute | solution.py:573
  488.8 48.1 %collective-permute-start.34 = (bf16[2,2,144,1152]{3,2,1,0:T(8,128)(2,1)S(1)}, bf16[2,2,144,1152]{3,2,1,0:T(8,128)(2,1)}, u32[]{:S(2)}, u32[]{:S(2)}) collective-permute-start(bf16[2,2,144,1152]{3,2,1,0:T(8,128)(2,1)S(1)} %dynamic-slice_bitcast_fusion), channel_id=1, source_target_pairs={{0,2},{1,3},{2,0},{3,1},{4,6},{5,7},{6,4},{7,5},{8,10},{9,11},{10,... | collective-permute-start | bytes 3981320 | tf_op jit(solution)/shard_map/ppermute | solution.py:573
  492.4 42.4 %collective-permute-start.36 = (bf16[144,1152]{1,0:T(8,128)(2,1)S(1)}, bf16[144,1152]{1,0:T(8,128)(2,1)S(1)}, u32[]{:S(2)}, u32[]{:S(2)}) collective-permute-start(bf16[144,1152]{1,0:T(8,128)(2,1)S(1)} %get-tuple-element.226), channel_id=1, source_target_pairs={{0,16},{4,20},{8,24},{12,28},{16,0},{20,4},{24,8},{28,12},{1,17},{... | collective-permute-start | bytes 995336 | tf_op jit(solution)/shard_map/ppermute | solution.py:568
  493.5 42.3 %collective-permute-start.37 = (bf16[144,1152]{1,0:T(8,128)(2,1)S(1)}, bf16[144,1152]{1,0:T(8,128)(2,1)S(1)}, u32[]{:S(2)}, u32[]{:S(2)}) collective-permute-start(bf16[144,1152]{1,0:T(8,128)(2,1)S(1)} %get-tuple-element.223), channel_id=1, source_target_pairs={{0,24},{4,28},{8,0},{12,4},{16,8},{20,12},{24,16},{28,20},{1,25},{... | collective-permute-start | bytes 995336 | tf_op jit(solution)/shard_map/ppermute | solution.py:568
  592.6 106.6 %all-gather.15.cloned.1.call-start = ((), (), s32[]{:S(2)}) async-start(), calls=%async_computation.9 | async-start | bytes 2985984 | tf_op jit(solution)/shard_map/all_gather | solution.py:743
  623.3 93.8 %all-gather.13.cloned.1.call-start = ((), (), s32[]{:S(2)}) async-start(), calls=%async_computation.8 | async-start | bytes 2985984 | tf_op jit(solution)/shard_map/all_gather | solution.py:743
  627.2 33.9 %collective-permute-start.40 = (bf16[144,1152]{1,0:T(8,128)(2,1)}, bf16[144,1152]{1,0:T(8,128)(2,1)S(1)}, u32[]{:S(2)}, u32[]{:S(2)}) collective-permute-start(bf16[144,1152]{1,0:T(8,128)(2,1)} %get-tuple-element.221), channel_id=1, source_target_pairs={{0,8},{4,12},{8,16},{12,20},{16,24},{20,28},{24,0},{28,4},{1,9},{5... | collective-permute-start | bytes 995336 | tf_op jit(solution)/shard_map/ppermute | solution.py:568
  629.0 32.0 %collective-permute-start.41 = (bf16[144,1152]{1,0:T(8,128)(2,1)S(1)}, bf16[144,1152]{1,0:T(8,128)(2,1)}, u32[]{:S(2)}, u32[]{:S(2)}) collective-permute-start(bf16[144,1152]{1,0:T(8,128)(2,1)S(1)} %get-tuple-element.222), channel_id=1, source_target_pairs={{0,16},{4,20},{8,24},{12,28},{16,0},{20,4},{24,8},{28,12},{1,17},{... | collective-permute-start | bytes 995336 | tf_op jit(solution)/shard_map/ppermute | solution.py:568
  631.5 29.6 %collective-permute-start.42 = (bf16[144,1152]{1,0:T(8,128)(2,1)S(1)}, bf16[144,1152]{1,0:T(8,128)(2,1)}, u32[]{:S(2)}, u32[]{:S(2)}) collective-permute-start(bf16[144,1152]{1,0:T(8,128)(2,1)S(1)} %get-tuple-element.219), channel_id=1, source_target_pairs={{0,24},{4,28},{8,0},{12,4},{16,8},{20,12},{24,16},{28,20},{1,25},{... | collective-permute-start | bytes 995336 | tf_op jit(solution)/shard_map/ppermute | solution.py:568
  673.4 50.5 %all-to-all-start.5 = ((bf16[4,3,144,288]{3,2,1,0:T(8,128)(2,1)}), bf16[4,3,144,288]{3,2,1,0:T(8,128)(2,1)}, u32[]{:S(2)}, u32[]{:S(2)}) async-start(bf16[4,3,144,288]{3,2,1,0:T(8,128)(2,1)} %copy.162), calls=%async_computation.5 | async-start | bytes 2654208 | tf_op jit(solution)/shard_map/all_to_all | solution.py:648
  (100 other events, 1208.9 us)
Sparse Core Ops, SparseCore 0:
  32.0 107.0 all-gather.16
  142.7 97.9 all-gather.18
  439.6 32.9 all-gather.10
  474.6 104.0 all-gather.8
  600.1 48.9 all-gather.14
  663.2 40.7 all-gather.12

commit v7 on v6

--- a/solution.py
+++ b/solution.py
@@ -639,15 +639,12 @@
     yield jnp.concatenate(placed, axis=2)
 
 
-def shard_rows(rows, group):
-    ranks = lax.axis_size("fsdp")
+def shard_rows(split, group):
+    ranks, count, chunk, col_part = split.shape
     shares = ranks // group
-    count, chunk, total = rows.shape
-    col_part = total // ranks
-    split = rows.reshape(count, chunk, ranks, col_part).transpose(2, 0, 1, 3)
     moved = lax.all_to_all(split, "fsdp", 0, 0, tiled=True)
     moved = moved.reshape(group, shares, count, chunk, col_part).transpose(2, 0, 1, 3, 4)
-    return moved.reshape(count * group, shares * chunk, col_part)
+    return moved.reshape(count, group, shares * chunk, col_part)
 
 
 def gather_blocks(rows, group):
@@ -664,6 +661,7 @@
     ranks, at = lax.axis_size("fsdp"), lax.axis_index("fsdp")
     if ranks != group:
         blocks = gather_blocks(rows, group)
+        (blocks,) = yield (blocks,)
         (blocks,) = yield (blocks,)
         yield blocks
         return
@@ -678,6 +676,7 @@
     cuts = [(side, step * chunk, chunk) for side in range(2) for step in range(chips)]
     starts = [(2 * step + side) * unit for side in (core, 1 - core) for step in range(chips)]
     own = place([line, core_swap(line)], cuts, starts, total)
+    (own,) = yield (own,)
     share = lax.dynamic_slice_in_dim(own, core * half, half, 0)
     mine = [rank_swap(share, bits) for bits in range(1, ranks)]
     own, *mine = yield (own, *mine)
@@ -726,43 +725,94 @@
     first, second = here[:, :, :middle], here[:, :, middle:]
     first_in = rank_swap(entry(first, 1 - low_bit, 1), 1)
     second_in = rank_swap(entry(second, 1 - high_bit, 0), 2)
-    here, first_in, second_in = yield (here, first_in, second_in)
-    first, second = here[:, :, :middle], here[:, :, middle:]
+    first_in, second_in = yield (first_in, second_in)
     first = narrow(wide(entry(first, low_bit, 1)) + wide(first_in))
     second = narrow(wide(entry(second, high_bit, 0)) + wide(second_in))
     first_in = rank_swap(entry(first, 1 - high_bit), 2)
     second_in = rank_swap(entry(second, 1 - low_bit), 1)
-    first, second, first_in, second_in = yield (first, second, first_in, second_in)
+    first_in, second_in = yield (first_in, second_in)
     first = narrow(wide(entry(first, high_bit)) + wide(first_in))
     second = narrow(wide(entry(second, low_bit)) + wide(second_in))
     line = jnp.concatenate([first, second])
-    parts = [entry(line, chip)]
-    parts += [chip_shift(entry(line, (chip + step) % chips), step) for step in range(1, chips)]
+    parts = [chip_shift(entry(line, (chip + step) % chips), step) for step in range(1, chips)]
     parts = yield tuple(parts)
-    rows = sum(wide(part) for part in parts)
-    found = lax.all_gather(narrow(rows), "dp", axis=0, tiled=True)
-    yield found.reshape(chips, 2, chunk, -1).transpose(1, 0, 2, 3).reshape(total, -1)
+    rows = sum([wide(part) for part in parts], wide(entry(line, chip)))
+    yield lax.all_gather(narrow(rows), "dp", axis=0, tiled=True)
 
 
 def fast_dot(subscripts, left, right):
     return jnp.einsum(subscripts, left, right, preferred_element_type=jnp.float32)
 
 
+def products_kernel(chips, at, gathered, left_root, right_root, out, whole, semaphores):
+    chunk, width = left_root.shape
+    ranks = out.shape[0]
+    copies = []
+    for index in range(2 * chips):
+        first = (index % 2 * chips + index // 2) * chunk
+        copies.append(
+            pltpu.make_async_copy(
+                gathered.at[pl.ds(index * chunk, chunk)],
+                whole.at[pl.ds(first, chunk)],
+                semaphores.at[index],
+            )
+        )
+        copies[-1].start()
+    for copy in copies:
+        copy.wait()
+    first = at[0] * 16
+    grad = whole[...]
+    picked = lax.broadcasted_iota(jnp.int32, (width, chunk), 0) - first
+    picked = picked == lax.broadcasted_iota(jnp.int32, (width, chunk), 1)
+    own_columns = narrow(dot_nn(grad, narrow(picked.astype(jnp.float32))))
+    side_high, side_low = split_high(dot_nn(left_root[...], grad))
+    right = right_root[...]
+    precond = dot_nn(side_high, right) + dot_nn(side_low, right)
+    outer = dot_nt(whole[pl.ds(pl.multiple_of(first, 16), chunk), :], grad)
+    inner = dot_tn(own_columns, grad)
+    for at_out, product in enumerate((precond, outer, inner)):
+        low = narrow(product)
+        for rank in range(ranks):
+            span = slice(rank * (width // ranks), (rank + 1) * (width // ranks))
+            out[rank, at_out] = low[:, span]
+
+
 def owned_step(whole, left_root, right_root, group):
-    chunk = left_root.shape[0]
-    shares = lax.axis_size("fsdp") // group
+    ranks, dp_count = lax.axis_size("fsdp"), lax.axis_size("dp")
+    shares = ranks // group
+    chunk, total = left_root.shape
+    col_part = total // ranks
     first = lax.axis_index("dp") * (chunk * shares) + lax.axis_index("fsdp") % shares * chunk
+    if shares == 1:
+        return pl.pallas_call(
+            functools.partial(products_kernel, dp_count // 2),
+            in_specs=[
+                pl.BlockSpec(memory_space=pltpu.SMEM),
+                pl.BlockSpec(memory_space=pl.ANY),
+                pl.BlockSpec(memory_space=pltpu.VMEM),
+                pl.BlockSpec(memory_space=pltpu.VMEM),
+            ],
+            out_specs=pl.BlockSpec(memory_space=pltpu.VMEM),
+            out_shape=jax.ShapeDtypeStruct((ranks, 3, chunk, col_part), jnp.bfloat16),
+            scratch_shapes=[
+                pltpu.VMEM((total, total), jnp.bfloat16),
+                pltpu.SemaphoreType.DMA((dp_count,)),
+            ],
+            compiler_params=pltpu.CompilerParams(vmem_limit_bytes=vmem_bytes),
+            cost_estimate=pl.CostEstimate(
+                flops=12 * chunk * total * total, bytes_accessed=6 * total * total, transcendentals=0
+            ),
+        )((first // 16)[None], whole, left_root, right_root)
     grad_rows = lax.dynamic_slice_in_dim(whole, first, chunk, 0)
     own_columns = lax.dynamic_slice_in_dim(whole, first, chunk, 1)
     outer = fast_dot("rk,jk->rj", grad_rows, whole)
     inner = fast_dot("kr,kj->rj", own_columns, whole)
-    side = fast_dot("rk,kj->rj", left_root, whole)
-    side_high = narrow(side)
-    side_low = narrow(side - wide(side_high))
+    side_high, side_low = split_high(fast_dot("rk,kj->rj", left_root, whole))
     precond = fast_dot("rk,kj->rj", side_high, right_root) + fast_dot(
         "rk,kj->rj", side_low, right_root
     )
-    return narrow(jnp.stack([precond, outer, inner]))
+    products = narrow(jnp.stack([precond, outer, inner]))
+    return products.reshape(3, chunk, ranks, col_part).transpose(2, 0, 1, 3)
 
 
 def per_device(
@@ -802,8 +852,13 @@
     other_rows = own_rows(other_shards, group)
     other_rows = other_rows.send(next(other_rows))
     one_steps = gather_pieces(other_rows[0], group)
-    one_parts = next(one_steps)
+    one_parts, first_parts = tie(next(one_steps), first_parts)
+    one_parts = one_steps.send(one_parts)
     two_w = gather_blocks(other_rows[1], group)
+    roots = jnp.stack([narrow(left_roots[mod_count:]), narrow(right_roots[mod_count:])])
+    roots, first_parts = tie(roots, first_parts)
+    root_rows = own_rows(roots.reshape(-1, group, row_part, col_part), group)
+    root_panels = next(root_rows)
 
     first_parts = first_parts.reshape(dp_count, -1)
     cond_all = first_parts[:, : clip_count * width].reshape(all_clips, width)
@@ -833,10 +888,7 @@
     attn_in, parts, mixed, proj, resid, mlp_in, d_branch, d_branch_sums = run_attention(
         frames, frame_counts, stream, grad_out, mods, bias_table, attn_w
     )
-    roots = jnp.stack([narrow(left_roots[mod_count:]), narrow(right_roots[mod_count:])])
-    mlp_in, one_parts, roots = tie(mlp_in, one_parts, roots)
-    root_rows = own_rows(roots.reshape(-1, group, row_part, col_part), group)
-    root_panels = next(root_rows)
+    mlp_in, one_parts, root_panels = tie(mlp_in, one_parts, root_panels)
     one_w = one_steps.send(one_parts)
     hidden, slope = run_hidden(mlp_in, one_w, bias_table[4:8, None])
     two_steps = sum_blocks(
@@ -846,7 +898,10 @@
         group,
     )
     two_parts = list(next(two_steps))
-    hidden, two_parts[0] = tie(hidden, two_parts[0])
+    root_rows = root_rows.send(root_panels)
+    hidden, two_parts[0], root_rows = tie(hidden, two_parts[0], root_rows)
+    left_rows, right_rows = jnp.split(root_rows, 2)
+    right_wholes = [gather_own(rows[None], group)[0] for rows in right_rows]
 
     d_pre, d_pre_sums, block_out, d_gate_two = run_branch(
         frames,
@@ -860,10 +915,8 @@
         resid,
         grad_out,
     )
-    d_pre, two_parts, root_panels = tie(d_pre, two_parts, root_panels)
+    d_pre, two_parts = tie(d_pre, two_parts)
     two_parts = list(two_steps.send(two_parts))
-    left_rows, right_rows = jnp.split(root_rows.send(root_panels), 2)
-    right_wholes = gather_own(right_rows, group)
     one_steps = sum_blocks(
         lambda left: fast_dot("td,jte->jde", left, d_pre),
         lambda first, size: lax.dynamic_slice_in_dim(mlp_in, first, size, 1),
@@ -893,8 +946,9 @@
     d_heads, attn_parts[0], one_parts = tie(d_heads, attn_parts[0], one_parts)
     one_parts = one_steps.send(one_parts)
     input_grad, input_sums = run_input(d_heads, attn_w, mods, stream, d_resid)
-    input_sums, attn_parts, one_parts, right_wholes = tie(
-        input_sums, attn_parts, one_parts, right_wholes
+    products_two = owned_step(whole_two, left_rows[2], right_wholes[2], group)
+    input_sums, attn_parts, one_parts, products_two = tie(
+        input_sums, attn_parts, one_parts, products_two
     )
     attn_parts = attn_steps.send(attn_parts)
     whole_one = one_steps.send(one_parts)
@@ -943,7 +997,7 @@
     to_rows, attn_parts = tie(to_rows, attn_parts)
     attn_parts = attn_steps.send(attn_parts)
     from_rows = lax.all_to_all(to_rows, "dp", 0, 0, tiled=True)
-    products_two = owned_step(whole_two, left_rows[2], right_wholes[2], group)
+    back_two = shard_rows(products_two, group)
     bias_grad = jnp.sum(from_rows[:, mod_size:], axis=0)
     mod_grad_cols = from_rows[:, :mod_size].reshape(all_clips, mod_count, col_part)
     mod_grad = lax.all_gather(packed([mod_grad_cols], 8), "fsdp", axis=0, tiled=True)
@@ -964,21 +1018,23 @@
     cond_side = jnp.einsum("cb,bje->jce", cond_gram, mod_grad_cols, precision=precise)
     ada_right = jnp.einsum("cjr,jce->jre", mod_grad_rows, cond_side, precision=precise)
 
-    products_two, right_parts, attn_parts = tie(products_two, right_parts, attn_parts)
+    products_one = owned_step(whole_one, left_rows[1], right_wholes[1], group)
+    back_two, products_one, right_parts, attn_parts = tie(
+        back_two, products_one, right_parts, attn_parts
+    )
     whole_attn = attn_steps.send(attn_parts)
-    back_two = shard_rows(products_two, group)
-    back_one = shard_rows(owned_step(whole_one, left_rows[1], right_wholes[1], group), group)
+    back_one = shard_rows(products_one, group)
     right_parts = lax.all_gather(packed([right_parts], 8), "dp", axis=0, tiled=True)
     mod_right = jnp.sum(right_parts.reshape(dp_count, -1), axis=0)[: mod_grad_cols.size]
     mod_right = mod_right.reshape(all_clips, mod_count, col_part)
     ada_pre = jnp.einsum("jrc,cje->jre", left_cond, mod_right, precision=precise)
+    whole_attn, back_one, ada_pre, ada_left, ada_right = tie(
+        whole_attn, back_one, ada_pre, ada_left, ada_right
+    )
     back_attn = shard_rows(owned_step(whole_attn, left_rows[0], right_wholes[0], group), group)
 
     def joined(at, ada):
-        span = slice(at * group, (at + 1) * group)
-        return jnp.concatenate(
-            [ada, wide(back_attn[span]), wide(back_one[span]), wide(back_two[span])]
-        )
+        return jnp.concatenate([ada, wide(back_attn[at]), wide(back_one[at]), wide(back_two[at])])
 
     precond = joined(0, ada_pre)
     left_new = stat_decay * left_stats + (1.0 - stat_decay) * joined(1, ada_left)

time: 798 us -> 809 us (1.014)
  blocking collectives: 67.8 us -> 112 us
  waiting for transfers between devices: 245 us -> 203 us
  matrix products: 90.3 us -> 61.2 us
  Pallas kernels: 140 us -> 167 us
  starting transfers between devices: 88 us -> 112 us
  local copies, waits for them, and re-layouts: 94 us -> 75.7 us
    all_gather x1, blocking collectives: 9.85 us -> 60.2 us  [per_device(): lax.all_gather(packed([mod_cols, bias_rows, left_cond], 8), 'fsdp', axis=...]
    dot_general x22 -> x7, matrix products: 78.9 us -> 47.2 us  [fast_dot(): jnp.einsum(subscripts, left, right, preferred_element_type=jnp.float32)]
    pallas_call x0 -> x3, Pallas kernels: none -> 25.1 us  [owned_step(): pl.pallas_call(functools.partial(products_kernel, dp_count // 2), in_spec...]
    ppermute x24, waiting for transfers between devices: 97.1 us -> 76 us  [rank_swap(): return lax.ppermute(array, 'fsdp', [(at, at ^ bits) for at in range(count)])]
    ppermute x12, waiting for transfers between devices: 54.1 us -> 38.1 us  [chip_shift(): lax.ppermute(array, 'dp', [(at, (at + 2 * step) % count) for at in range(...]
    ppermute x12, starting transfers between devices: 17.4 us -> 31.7 us  [chip_shift(): lax.ppermute(array, 'dp', [(at, (at + 2 * step) % count) for at in range(...]
    transpose x6 -> x0, local copies, waits for them, and re-layouts: 9.65 us -> none  [the longest x3 6.03 us: sum_blocks(): found.reshape(chips, 2, chunk, -1).transpose(1, 0, 2, 3).reshape(total, -1)]
    all_to_all x1, waiting for transfers between devices: 11.6 us -> 1.95 us  [per_device(): mod_parts = lax.all_to_all(mod_parts, 'dp', 0, 0, tiled=True)]
  transfers between devices with their start and end apart: 55 -> 57, of which waited for: 26 -> 22; matrix products, arithmetic and copies ran while one was open for 22% -> 18% of each run, Pallas kernels for 18% -> 20%
where the time goes in v7:
time: 809 us; the launch traced here: 800 us
  waiting for transfers between devices  203 us (25%)
  Pallas kernels  167 us (21%)
  starting transfers between devices  112 us (14%)
  blocking collectives  112 us (14%)
  local copies, waits for them, and re-layouts  75.7 us (9%)
  matrix products  61.2 us (8%)
  other arithmetic  54.2 us (7%)
  between operations  16 us (2%)
    ppermute x24, waiting for transfers between devices, rank_swap(): return lax.ppermute(array, 'fsdp', [(at, at ^ bits) for at in range(count)])  76 us
    all_gather x1, blocking collectives, per_device(): lax.all_gather(packed([mod_cols, bias_rows, left_cond], 8), 'fsdp', axis=...  60.2 us
    dot_general x7, matrix products, fast_dot(): jnp.einsum(subscripts, left, right, preferred_element_type=jnp.float32)  47.2 us
    pallas_call x1, Pallas kernels, run_attention(): pl.pallas_call(functools.partial(attention_kernel, frames), grid=(clips,)...  40 us
    ppermute x12, waiting for transfers between devices, chip_shift(): lax.ppermute(array, 'dp', [(at, (at + 2 * step) % count) for at in range(...  38.1 us
    all_gather x3, waiting for transfers between devices, gather_own(): return lax.all_gather(rows, 'dp', axis=1, tiled=True)  33.8 us
    ppermute x12, starting transfers between devices, chip_shift(): lax.ppermute(array, 'dp', [(at, (at + 2 * step) % count) for at in range(...  31.7 us
    ppermute x24, starting transfers between devices, rank_swap(): return lax.ppermute(array, 'fsdp', [(at, at ^ bits) for at in range(count)])  30.3 us
  transfers between devices with their start and end apart: 57, of which 22 were waited for; matrix products, arithmetic and copies ran while one was open for 18% of the time, Pallas kernels for 20%

profile of v7, /device:TPU:0, one launch (start us, length us, event | category | flops | bytes accessed | tf_op | source)
XLA Modules:
  0.0 800.4 jit_solution(13333439285837258001)
XLA Ops:
  14.5 14.7 %all_gather.36 = bf16[256,128]{1,0:T(8,128)(2,1)S(1)} all-gather(bf16[32,128]{1,0:T(8,128)(2,1)S(1)} %fusion.116), channel_id=1, replica_groups=mesh['dp'=8,'fsdp'=4] {'dp'}, dimensions={0}, use_global_device_ids=true | all-gather | bytes 73728 | tf_op jit(solution)/shard_map/all_gather | solution.py:849
  52.5 11.3 %collective-permute-done.6.refs_1_ = bf16[144,1152]{1,0:T(8,128)(2,1)S(1)} collective-permute-done((bf16[144,1152]{1,0:T(8,128)(2,1)S(1)}, bf16[144,1152]{1,0:T(8,128)(2,1)S(1)}, u32[]{:S(2)}, u32[]{:S(2)}) %collective-permute-start.6) | collective-permute-done | bytes 331808 | tf_op jit(solution)/shard_map/ppermute | solution.py:568
  63.8 13.0 %collective-permute-done.7.refs_2_ = bf16[144,1152]{1,0:T(8,128)(2,1)S(1)} collective-permute-done((bf16[144,1152]{1,0:T(8,128)(2,1)S(1)}, bf16[144,1152]{1,0:T(8,128)(2,1)S(1)}, u32[]{:S(2)}, u32[]{:S(2)}) %collective-permute-start.7) | collective-permute-done | bytes 331808 | tf_op jit(solution)/shard_map/ppermute | solution.py:568
  94.7 23.2 %all-to-all-start = ((f32[16,6,288]{2,1,0:T(8,128)}), f32[16,6,288]{2,1,0:T(8,128)S(1)}, u32[]{:S(2)}, u32[]{:S(2)}) async-start(f32[16,6,288]{2,1,0:T(8,128)} %copy.98), calls=%async_computation | async-start | bytes 393216 | tf_op jit(solution)/shard_map/all_to_all | solution.py:869
  127.5 60.2 %all_gather.37 = f32[672,128]{1,0:T(8,128)S(1)} all-gather(f32[168,128]{1,0:T(8,128)S(1)} %pad_bitcast_fusion), channel_id=1, replica_groups=mesh['dp'=8,'fsdp'=4] {'fsdp'}, dimensions={0}, use_global_device_ids=true | all-gather | bytes 430080 | tf_op jit(solution)/shard_map/all_gather | solution.py:873
  190.1 40.0 %shard_map.206 = (bf16[512,1152]{1,0:T(8,128)(2,1)S(1)}, bf16[5,512,1152]{2,1,0:T(8,128)(2,1)}, bf16[512,1152]{1,0:T(8,128)(2,1)S(1)}, f32[512,1152]{1,0:T(8,128...) custom-call(s32[2]{0:T(128)S(1)} %copy-done.11, ...), custom_call_target="tpu_custom_call" | custom-call | flops 8153726976 | bytes 23592960 | tf_op jit(solution)/shard_map/pallas_call | solution.py:187
  238.4 9.1 %shard_map.207 = bf16[4608,1152]{1,0:T(8,128)(2,1)} custom-call(s32[7]{0:T(128)S(1)} %stack.125.at, bf16[1152,1152]{1,0:T(8,128)(2,1)} %shard_map.205.refs_0_, bf16[576,1152]{1,0:T(8,128)(2,1)} %collective-permute-done.10.refs_1_, bf16[576,1152]{1,0:T(8,128)(2,1)} %collective-permute-done.11.refs_2_, bf16[576,1152]{1,0:T(8,128)(2,1)} %collective-permute-done.12.refs_3_, ...), custom_call_target="tpu_custom_call" | custom-call | bytes 21233664 | tf_op jit(solution)/shard_map/pallas_call | solution.py:603
  247.5 13.5 %shard_map.208 = (bf16[4,512,1152]{2,1,0:T(8,128)(2,1)}, bf16[4,512,1152]{2,1,0:T(8,128)(2,1)}) custom-call(bf16[512,1152]{1,0:T(8,128)(2,1)S(1)} %copy-done.13, bf16[4,1152,1152]{2,1,0:T(8,128)(2,1)} %bitcast.301, f32[4,1,1152]{2,1,0:T(1,128)S(1)} %copy.110.bias), custom_call_target="tpu_custom_call" | custom-call | flops 5435817984 | bytes 17694720 | tf_op jit(solution)/shard_map/pallas_call | solution.py:245
  261.1 7.8 convolution_convert_fusion.1
  269.2 9.1 %collective-permute-done.19 = bf16[4,576,1152]{2,1,0:T(8,128)(2,1)} collective-permute-done((bf16[4,576,1152]{2,1,0:T(8,128)(2,1)}, bf16[4,576,1152]{2,1,0:T(8,128)(2,1)}, u32[]{:S(2)}, u32[]{:S(2)}) %collective-permute-start.19) | collective-permute-done | bytes 5308448 | tf_op jit(solution)/shard_map/ppermute | solution.py:563
  278.3 7.7 add_convert_fusion.1
  304.7 17.2 %collective-permute-done.20 = bf16[2,2,144,1152]{3,2,1,0:T(8,128)(2,1)} collective-permute-done((bf16[2,2,144,1152]{3,2,1,0:T(8,128)(2,1)}, bf16[2,2,144,1152]{3,2,1,0:T(8,128)(2,1)}, u32[]{:S(2)}, u32[]{:S(2)}) %collective-permute-start.20) | collective-permute-done | bytes 1327136 | tf_op jit(solution)/shard_map/ppermute | solution.py:573
  324.6 21.0 %shard_map.209 = (bf16[4,512,1152]{2,1,0:T(8,128)(2,1)}, f32[4,1,1152]{2,1,0:T(1,128)S(1)}, bf16[512,1152]{1,0:T(8,128)(2,1)}, f32[2,1,1152]{2,1,0:T(1,128)S(1)}) custom-call(s32[2]{0:T(128)S(1)} %copy-done.11, bf16[4,512,1152]{2,1,0:T(8,128)(2,1)} %get-tuple-element.116.hidden, bf16[4,512,1152]{2,1,0:T(8,128)(2,1)} %get-tuple-element.117.slope, ...), custom_call_target="tpu_custom_call" | custom-call | flops 10871635968 | bytes 23592960 | tf_op jit(solution)/shard_map/pallas_call | solution.py:311
  345.6 7.8 fusion.1
  383.6 13.4 %collective-permute-done.24 = bf16[2,144,1152]{2,1,0:T(8,128)(2,1)} collective-permute-done((bf16[2,144,1152]{2,1,0:T(8,128)(2,1)}, bf16[2,144,1152]{2,1,0:T(8,128)(2,1)}, u32[]{:S(2)}, u32[]{:S(2)}) %collective-permute-start.24) | collective-permute-done | bytes 663584 | tf_op jit(solution)/shard_map/ppermute | solution.py:573
  397.0 10.9 %collective-permute-done.23 = bf16[2,2,144,1152]{3,2,1,0:T(8,128)(2,1)} collective-permute-done((bf16[2,2,144,1152]{3,2,1,0:T(8,128)(2,1)}, bf16[2,2,144,1152]{3,2,1,0:T(8,128)(2,1)}, u32[]{:S(2)}, u32[]{:S(2)}) %collective-permute-start.23) | collective-permute-done | bytes 1327136 | tf_op jit(solution)/shard_map/ppermute | solution.py:573
  411.4 16.1 %collective-permute-start.29 = (bf16[144,1152]{1,0:T(8,128)(2,1)S(1)}, bf16[144,1152]{1,0:T(8,128)(2,1)S(1)}, u32[]{:S(2)}, u32[]{:S(2)}) collective-permute-start(bf16[144,1152]{1,0:T(8,128)(2,1)S(1)} %get-tuple-element.224), channel_id=1, source_target_pairs={{0,8},{4,12},{8,16},{12,20},{16,24},{20,28},{24,0},{28,4},{1,9},{5... | collective-permute-start | bytes 995336 | tf_op jit(solution)/shard_map/ppermute | solution.py:568
  431.3 15.9 %shard_map.210 = (f32[512,1152]{1,0:T(8,128)}, bf16[512,1152]{1,0:T(8,128)(2,1)S(1)}, f32[2,4,1152]{2,1,0:T(4,128)S(1)}) custom-call(s32[2]{0:T(128)S(1)} %copy-done.11, bf16[4,512,1152]{2,1,0:T(8,128)(2,1)} %get-tuple-element.125.d_pre, bf16[4,1152,1152]{2,1,0:T(8,128)(2,1)} %bitcast.302, f32[2,6,1152]{2,1,0:T(8,128)S(1)} %copy-done.4, ...), custom_call_target="tpu_custom_call" | custom-call | flops 5435817984 | bytes 23592960 | tf_op jit(solution)/shard_map/pallas_call | solution.py:398
  452.7 25.9 %shard_map.211 = (bf16[4,512,1152]{2,1,0:T(8,128)(2,1)}, f32[2,3,1152]{2,1,0:T(4,128)S(1)}) custom-call(s32[2]{0:T(128)S(1)} %copy-done.11, bf16[512,1152]{1,0:T(8,128)(2,1)S(1)} %get-tuple-element.129.d_proj, bf16[5,512,1152]{2,1,0:T(8,128)(2,1)} %get-tuple-element.130.parts, bf16[4,1152,1152]{2,1,0:T(8,128)(2,1)} %bitcast.305), custom_call_target="tpu_custom_call" | custom-call | flops 8153726976 | bytes 11796480 | tf_op jit(solution)/shard_map/pallas_call | solution.py:467
  478.8 8.1 %convolution_convert_fusion = bf16[4,576,1152]{2,1,0:T(8,128)(2,1)} fusion(bf16[4,512,1152]{2,1,0:T(8,128)(2,1)} %get-tuple-element.141.d_qkv, bf16[1,512,576]{1,2,0:T(8,128)(2,1)S(1)} %bitcast.316, bf16[1,512,576]{1,2,0:T(8,128)(2,1)S(1)} %bitcast.315), kind=kOutput, calls=%fused_computation.4 | convolution fusion | flops 2724102144 | bytes 11206656 | tf_op jit(solution)/shard_map/jtd,jte->jde/dot_general | solution.py:744
  510.3 10.6 %all-gather.11.cloned.1.call-done.gathered = bf16[1152,1152]{1,0:T(8,128)(2,1)} async-done(((bf16[144,1152]{1,0:T(8,128)(2,1)}), bf16[1152,1152]{1,0:T(8,128)(2,1)}) %all-gather.11.cloned.1.call-update) | async-done | bytes 2654224 | tf_op jit(solution)/shard_map/all_gather | solution.py:740
  520.9 8.5 %shard_map.213 = bf16[4,3,144,288]{3,2,1,0:T(8,128)(2,1)} custom-call(s32[1]{0:T(128)} %bitcast.85.at, bf16[1152,1152]{1,0:T(8,128)(2,1)} %all-gather.11.cloned.1.call-done.gathered, bf16[144,1152]{1,0:T(8,128)(2,1)S(1)} %get-tuple-element.203.left_root, bf16[1152,1152]{1,0:T(8,128)(2,1)} %bitcast.329), custom_call_target="tpu_custom_call" | custom-call | flops 2293235712 | bytes 7962624 | tf_op jit(solution)/shard_map/pallas_call | solution.py:787
  542.5 11.6 %shard_map.212 = (bf16[512,1152]{1,0:T(8,128)(2,1)}, f32[2,2,1152]{2,1,0:T(2,128)S(1)}) custom-call(bf16[4,512,1152]{2,1,0:T(8,128)(2,1)} %get-tuple-element.141.d_qkv, bf16[4,1152,1152]{2,1,0:T(8,128)(2,1)} %bitcast.306, f32[2,6,1152]{2,1,0:T(8,128)S(1)} %copy-done.4, bf16[512,1152]{1,0:T(8,128)(2,1)S(1)} %bitcast.300, f32[512,1152]{1,0:T(8,128)S(1)} %copy-done), custom_call_target="tpu_custom_call" | custom-call | flops 4076863488 | bytes 17694720 | tf_op jit(solution)/shard_map/pallas_call | solution.py:529
  561.9 13.8 %collective-permute-done.36 = bf16[144,1152]{1,0:T(8,128)(2,1)S(1)} collective-permute-done((bf16[144,1152]{1,0:T(8,128)(2,1)S(1)}, bf16[144,1152]{1,0:T(8,128)(2,1)S(1)}, u32[]{:S(2)}, u32[]{:S(2)}) %collective-permute-start.36) | collective-permute-done | bytes 331808 | tf_op jit(solution)/shard_map/ppermute | solution.py:568
  598.3 9.9 %collective-permute-done.38 = bf16[2,144,1152]{2,1,0:T(8,128)(2,1)S(1)} collective-permute-done((bf16[2,144,1152]{2,1,0:T(8,128)(2,1)S(1)}, bf16[2,144,1152]{2,1,0:T(8,128)(2,1)S(1)}, u32[]{:S(2)}, u32[]{:S(2)}) %collective-permute-start.38) | collective-permute-done | bytes 663584 | tf_op jit(solution)/shard_map/ppermute | solution.py:573
  609.0 9.5 %all-to-all-start.3 = ((f32[8,1,3960]{2,1,0:T(1,128)}), f32[8,1,3960]{2,1,0:T(1,128)S(1)}, u32[]{:S(2)}, u32[]{:S(2)}) async-start(f32[8,1,3960]{2,1,0:T(1,128)} %all_to_all.30), calls=%async_computation.3 | async-start | bytes 253952 | tf_op jit(solution)/shard_map/all_to_all | solution.py:999
  635.5 16.4 %all_gather.44 = f32[864,128]{1,0:T(8,128)} all-gather(f32[216,128]{1,0:T(8,128)} %reshape.299), channel_id=1, replica_groups=mesh['dp'=8,'fsdp'=4] {'fsdp'}, dimensions={0}, use_global_device_ids=true | all-gather | bytes 552960 | tf_op jit(solution)/shard_map/all_gather | solution.py:1003
  661.6 8.3 %shard_map.214 = bf16[4,3,144,288]{3,2,1,0:T(8,128)(2,1)} custom-call(s32[1]{0:T(128)} %bitcast.85.at, bf16[1152,1152]{1,0:T(8,128)(2,1)} %all-gather.15.cloned.1.call-done.gathered, bf16[144,1152]{1,0:T(8,128)(2,1)S(1)} %get-tuple-element.201.left_root, bf16[1152,1152]{1,0:T(8,128)(2,1)} %bitcast.328), custom_call_target="tpu_custom_call" | custom-call | flops 2293235712 | bytes 7962624 | tf_op jit(solution)/shard_map/pallas_call | solution.py:787
  687.7 20.8 %all_gather.46 = f32[1728,128]{1,0:T(8,128)} all-gather(f32[216,128]{1,0:T(8,128)S(1)} %reshape.304), channel_id=1, replica_groups=mesh['dp'=8,'fsdp'=4] {'dp'}, dimensions={0}, use_global_device_ids=true | all-gather | bytes 995328 | tf_op jit(solution)/shard_map/all_gather | solution.py:1027
  713.0 33.8 %all-gather.21.cloned.1.call-done = bf16[1,1152,1152]{2,1,0:T(8,128)(2,1)} async-done(((bf16[1,144,1152]{2,1,0:T(8,128)(2,1)}), bf16[1,1152,1152]{2,1,0:T(8,128)(2,1)}) %all-gather.21.cloned.1.call-update) | async-done | bytes 2654224 | tf_op jit(solution)/shard_map/all_gather | solution.py:699
  746.8 8.3 %shard_map.215 = bf16[4,3,144,288]{3,2,1,0:T(8,128)(2,1)} custom-call(s32[1]{0:T(128)} %bitcast.85.at, bf16[1152,1152]{1,0:T(8,128)(2,1)} %all-gather.19.cloned.1.call-done.gathered, bf16[144,1152]{1,0:T(8,128)(2,1)S(1)} %get-tuple-element.199.left_root, bf16[1152,1152]{1,0:T(8,128)(2,1)} %bitcast.330), custom_call_target="tpu_custom_call" | custom-call | flops 2293235712 | bytes 7962624 | tf_op jit(solution)/shard_map/pallas_call | solution.py:787
  766.0 11.0 %all-to-all-done.5 = bf16[4,3,144,288]{3,2,1,0:T(8,128)(2,1)} async-done(((bf16[4,3,144,288]{3,2,1,0:T(8,128)(2,1)}), bf16[4,3,144,288]{3,2,1,0:T(8,128)(2,1)}, u32[]{:S(2)}, u32[]{:S(2)}) %all-to-all-start.5) | async-done | bytes 995360 | tf_op jit(solution)/shard_map/all_to_all | solution.py:645
  (426 shorter events, 276.0 us)
Async XLA Ops:
  7.2 183.0 %all-gather.23.cloned.1.call-start = ((), (), s32[]{:S(2)}) async-start(), calls=%async_computation.12 | async-start | bytes 10948608 | tf_op jit(solution)/shard_map/all_gather | solution.py:654
  31.9 290.0 %all-gather.25.cloned.1.call-start = ((), (), s32[]{:S(2)}) async-start(), calls=%async_computation.13 | async-start | bytes 10948608 | tf_op jit(solution)/shard_map/all_gather | solution.py:654
  89.1 142.1 %collective-permute-start.10 = (bf16[576,1152]{1,0:T(8,128)(2,1)}, bf16[576,1152]{1,0:T(8,128)(2,1)}, u32[]{:S(2)}, u32[]{:S(2)}) collective-permute-start(bf16[576,1152]{1,0:T(8,128)(2,1)} %constant_dynamic-slice_fusion.4), channel_id=1, source_target_pairs={{0,1},{1,0},{2,3},{3,2},{4,5},{5,4},{6,7},{7,6},{8,9},{9,8},{10,11... | collective-permute-start | bytes 3981320 | tf_op jit(solution)/shard_map/ppermute | solution.py:573
  90.2 141.0 %collective-permute-start.11 = (bf16[576,1152]{1,0:T(8,128)(2,1)}, bf16[576,1152]{1,0:T(8,128)(2,1)}, u32[]{:S(2)}, u32[]{:S(2)}) collective-permute-start(bf16[576,1152]{1,0:T(8,128)(2,1)} %constant_dynamic-slice_fusion.4), channel_id=1, source_target_pairs={{0,2},{1,3},{2,0},{3,1},{4,6},{5,7},{6,4},{7,5},{8,10},{9,11},{10,... | collective-permute-start | bytes 3981320 | tf_op jit(solution)/shard_map/ppermute | solution.py:573
  91.0 140.1 %collective-permute-start.12 = (bf16[576,1152]{1,0:T(8,128)(2,1)}, bf16[576,1152]{1,0:T(8,128)(2,1)}, u32[]{:S(2)}, u32[]{:S(2)}) collective-permute-start(bf16[576,1152]{1,0:T(8,128)(2,1)} %constant_dynamic-slice_fusion.4), channel_id=1, source_target_pairs={{0,3},{1,2},{2,1},{3,0},{4,7},{5,6},{6,5},{7,4},{8,11},{9,10},{10,... | collective-permute-start | bytes 3981320 | tf_op jit(solution)/shard_map/ppermute | solution.py:573
  94.7 31.7 %all-to-all-start = ((f32[16,6,288]{2,1,0:T(8,128)}), f32[16,6,288]{2,1,0:T(8,128)S(1)}, u32[]{:S(2)}, u32[]{:S(2)}) async-start(f32[16,6,288]{2,1,0:T(8,128)} %copy.98), calls=%async_computation | async-start | bytes 393216 | tf_op jit(solution)/shard_map/all_to_all | solution.py:869
  117.9 392.4 %all-gather.13.cloned.1.call-start = ((), (), s32[]{:S(2)}) async-start(), calls=%async_computation.7 | async-start | bytes 2985984 | tf_op jit(solution)/shard_map/all_gather | solution.py:699
  123.2 65.5 %collective-permute-start.13 = (bf16[6,144,288]{2,1,0:T(8,128)(2,1)}, bf16[6,144,288]{2,1,0:T(8,128)(2,1)S(1)}, u32[]{:S(2)}, u32[]{:S(2)}) collective-permute-start(bf16[6,144,288]{2,1,0:T(8,128)(2,1)} %get-tuple-element.196), channel_id=1, source_target_pairs={{0,1},{1,0},{2,3},{3,2},{4,5},{5,4},{6,7},{7,6},{8,9},{9,8},{10,11... | collective-permute-start | bytes 1493000 | tf_op jit(solution)/shard_map/ppermute | solution.py:573
  123.8 107.4 %collective-permute-start.14 = (bf16[6,144,288]{2,1,0:T(8,128)(2,1)}, bf16[6,144,288]{2,1,0:T(8,128)(2,1)}, u32[]{:S(2)}, u32[]{:S(2)}) collective-permute-start(bf16[6,144,288]{2,1,0:T(8,128)(2,1)} %get-tuple-element.195), channel_id=1, source_target_pairs={{0,2},{1,3},{2,0},{3,1},{4,6},{5,7},{6,4},{7,5},{8,10},{9,11},{10,... | collective-permute-start | bytes 1493000 | tf_op jit(solution)/shard_map/ppermute | solution.py:573
  188.7 42.4 %collective-permute-start.15 = (bf16[6,144,288]{2,1,0:T(8,128)(2,1)}, bf16[6,144,288]{2,1,0:T(8,128)(2,1)}, u32[]{:S(2)}, u32[]{:S(2)}) collective-permute-start(bf16[6,144,288]{2,1,0:T(8,128)(2,1)} %get-tuple-element.194), channel_id=1, source_target_pairs={{0,3},{1,2},{2,1},{3,0},{4,7},{5,6},{6,5},{7,4},{8,11},{9,10},{10,... | collective-permute-start | bytes 1493000 | tf_op jit(solution)/shard_map/ppermute | solution.py:573
  290.6 31.3 %collective-permute-start.20 = (bf16[2,2,144,1152]{3,2,1,0:T(8,128)(2,1)}, bf16[2,2,144,1152]{3,2,1,0:T(8,128)(2,1)}, u32[]{:S(2)}, u32[]{:S(2)}) collective-permute-start(bf16[2,2,144,1152]{3,2,1,0:T(8,128)(2,1)} %dynamic-slice_bitcast_fusion.5), channel_id=1, source_target_pairs={{0,1},{1,0},{2,3},{3,2},{4,5},{5,4},{6,7},{7,6},{8,9},{9,8},{10,11... | collective-permute-start | bytes 3981320 | tf_op jit(solution)/shard_map/ppermute | solution.py:573
  295.7 50.0 %collective-permute-start.21 = (bf16[2,2,144,1152]{3,2,1,0:T(8,128)(2,1)}, bf16[2,2,144,1152]{3,2,1,0:T(8,128)(2,1)}, u32[]{:S(2)}, u32[]{:S(2)}) collective-permute-start(bf16[2,2,144,1152]{3,2,1,0:T(8,128)(2,1)} %dynamic-slice_bitcast_fusion.4), channel_id=1, source_target_pairs={{0,2},{1,3},{2,0},{3,1},{4,6},{5,7},{6,4},{7,5},{8,10},{9,11},{10,... | collective-permute-start | bytes 3981320 | tf_op jit(solution)/shard_map/ppermute | solution.py:573
  374.3 33.6 %collective-permute-start.23 = (bf16[2,2,144,1152]{3,2,1,0:T(8,128)(2,1)}, bf16[2,2,144,1152]{3,2,1,0:T(8,128)(2,1)}, u32[]{:S(2)}, u32[]{:S(2)}) collective-permute-start(bf16[2,2,144,1152]{3,2,1,0:T(8,128)(2,1)} %dynamic-slice_bitcast_fusion.3), channel_id=1, source_target_pairs={{0,1},{1,0},{2,3},{3,2},{4,5},{5,4},{6,7},{7,6},{8,9},{9,8},{10,11... | collective-permute-start | bytes 3981320 | tf_op jit(solution)/shard_map/ppermute | solution.py:573
  380.9 140.0 %all-gather.11.cloned.1.call-start = ((), (), s32[]{:S(2)}) async-start(), calls=%async_computation.6 | async-start | bytes 2985984 | tf_op jit(solution)/shard_map/all_gather | solution.py:740
  382.5 64.7 %collective-permute-start.26 = (bf16[2,2,144,1152]{3,2,1,0:T(8,128)(2,1)S(1)}, bf16[2,2,144,1152]{3,2,1,0:T(8,128)(2,1)S(1)}, u32[]{:S(2)}, u32[]{:S(2)}) collective-permute-start(bf16[2,2,144,1152]{3,2,1,0:T(8,128)(2,1)S(1)} %dynamic-slice_bitcast_fusion.2), channel_id=1, source_target_pairs={{0,2},{1,3},{2,0},{3,1},{4,6},{5,7},{6,4},{7,5},{8,10},{9,11},{10,... | collective-permute-start | bytes 3981320 | tf_op jit(solution)/shard_map/ppermute | solution.py:573
  411.4 67.3 %collective-permute-start.29 = (bf16[144,1152]{1,0:T(8,128)(2,1)S(1)}, bf16[144,1152]{1,0:T(8,128)(2,1)S(1)}, u32[]{:S(2)}, u32[]{:S(2)}) collective-permute-start(bf16[144,1152]{1,0:T(8,128)(2,1)S(1)} %get-tuple-element.224), channel_id=1, source_target_pairs={{0,8},{4,12},{8,16},{12,20},{16,24},{20,28},{24,0},{28,4},{1,9},{5... | collective-permute-start | bytes 995336 | tf_op jit(solution)/shard_map/ppermute | solution.py:568
  427.5 51.2 %collective-permute-start.30 = (bf16[144,1152]{1,0:T(8,128)(2,1)S(1)}, bf16[144,1152]{1,0:T(8,128)(2,1)S(1)}, u32[]{:S(2)}, u32[]{:S(2)}) collective-permute-start(bf16[144,1152]{1,0:T(8,128)(2,1)S(1)} %get-tuple-element.225), channel_id=1, source_target_pairs={{0,16},{4,20},{8,24},{12,28},{16,0},{20,4},{24,8},{28,12},{1,17},{... | collective-permute-start | bytes 995336 | tf_op jit(solution)/shard_map/ppermute | solution.py:568
  429.8 48.9 %collective-permute-start.31 = (bf16[144,1152]{1,0:T(8,128)(2,1)S(1)}, bf16[144,1152]{1,0:T(8,128)(2,1)S(1)}, u32[]{:S(2)}, u32[]{:S(2)}) collective-permute-start(bf16[144,1152]{1,0:T(8,128)(2,1)S(1)} %get-tuple-element.223), channel_id=1, source_target_pairs={{0,24},{4,28},{8,0},{12,4},{16,8},{20,12},{24,16},{28,20},{1,25},{... | collective-permute-start | bytes 995336 | tf_op jit(solution)/shard_map/ppermute | solution.py:568
  447.7 31.1 %collective-permute-start.28 = (bf16[2,144,1152]{2,1,0:T(8,128)(2,1)S(1)}, bf16[2,144,1152]{2,1,0:T(8,128)(2,1)S(1)}, u32[]{:S(2)}, u32[]{:S(2)}) collective-permute-start(bf16[2,144,1152]{2,1,0:T(8,128)(2,1)S(1)} %dynamic-slice_bitcast_fusion.8), channel_id=1, source_target_pairs={{0,1},{1,0},{2,3},{3,2},{4,5},{5,4},{6,7},{7,6},{8,9},{9,8},{10,11... | collective-permute-start | bytes 1990664 | tf_op jit(solution)/shard_map/ppermute | solution.py:573
  489.3 172.3 %all-gather.17.cloned.1.call-start = ((), (), s32[]{:S(2)}) async-start(), calls=%async_computation.9 | async-start | bytes 2985984 | tf_op jit(solution)/shard_map/all_gather | solution.py:699
  490.9 170.7 %all-gather.15.cloned.1.call-start = ((), (), s32[]{:S(2)}) async-start(), calls=%async_computation.8 | async-start | bytes 2985984 | tf_op jit(solution)/shard_map/all_gather | solution.py:740
  506.4 31.4 %collective-permute-start.33 = (bf16[2,2,144,1152]{3,2,1,0:T(8,128)(2,1)S(1)}, bf16[2,2,144,1152]{3,2,1,0:T(8,128)(2,1)}, u32[]{:S(2)}, u32[]{:S(2)}) collective-permute-start(bf16[2,2,144,1152]{3,2,1,0:T(8,128)(2,1)S(1)} %dynamic-slice_bitcast_fusion.1), channel_id=1, source_target_pairs={{0,1},{1,0},{2,3},{3,2},{4,5},{5,4},{6,7},{7,6},{8,9},{9,8},{10,11... | collective-permute-start | bytes 3981320 | tf_op jit(solution)/shard_map/ppermute | solution.py:573
  529.5 31.3 %collective-permute-start.34 = (bf16[2,2,144,1152]{3,2,1,0:T(8,128)(2,1)S(1)}, bf16[2,2,144,1152]{3,2,1,0:T(8,128)(2,1)S(1)}, u32[]{:S(2)}, u32[]{:S(2)}) collective-permute-start(bf16[2,2,144,1152]{3,2,1,0:T(8,128)(2,1)S(1)} %dynamic-slice_bitcast_fusion), channel_id=1, source_target_pairs={{0,2},{1,3},{2,0},{3,1},{4,6},{5,7},{6,4},{7,5},{8,10},{9,11},{10,... | collective-permute-start | bytes 3981320 | tf_op jit(solution)/shard_map/ppermute | solution.py:573
  539.2 36.5 %collective-permute-start.36 = (bf16[144,1152]{1,0:T(8,128)(2,1)S(1)}, bf16[144,1152]{1,0:T(8,128)(2,1)S(1)}, u32[]{:S(2)}, u32[]{:S(2)}) collective-permute-start(bf16[144,1152]{1,0:T(8,128)(2,1)S(1)} %get-tuple-element.222), channel_id=1, source_target_pairs={{0,16},{4,20},{8,24},{12,28},{16,0},{20,4},{24,8},{28,12},{1,17},{... | collective-permute-start | bytes 995336 | tf_op jit(solution)/shard_map/ppermute | solution.py:568
  540.1 35.6 %collective-permute-start.37 = (bf16[144,1152]{1,0:T(8,128)(2,1)S(1)}, bf16[144,1152]{1,0:T(8,128)(2,1)S(1)}, u32[]{:S(2)}, u32[]{:S(2)}) collective-permute-start(bf16[144,1152]{1,0:T(8,128)(2,1)S(1)} %get-tuple-element.220), channel_id=1, source_target_pairs={{0,24},{4,28},{8,0},{12,4},{16,8},{20,12},{24,16},{28,20},{1,25},{... | collective-permute-start | bytes 995336 | tf_op jit(solution)/shard_map/ppermute | solution.py:568
  625.2 44.7 %all-to-all-start.2 = ((bf16[4,3,144,288]{3,2,1,0:T(8,128)(2,1)}), bf16[4,3,144,288]{3,2,1,0:T(8,128)(2,1)S(1)}, u32[]{:S(2)}, u32[]{:S(2)}) async-start(bf16[4,3,144,288]{3,2,1,0:T(8,128)(2,1)} %shard_map.213), calls=%async_computation.2 | async-start | bytes 2654208 | tf_op jit(solution)/shard_map/all_to_all | solution.py:645
  629.1 84.0 %all-gather.19.cloned.1.call-start = ((), (), s32[]{:S(2)}) async-start(), calls=%async_computation.10 | async-start | bytes 2985984 | tf_op jit(solution)/shard_map/all_gather | solution.py:740
  630.3 39.6 %collective-permute-start.40 = (bf16[144,1152]{1,0:T(8,128)(2,1)}, bf16[144,1152]{1,0:T(8,128)(2,1)}, u32[]{:S(2)}, u32[]{:S(2)}) collective-permute-start(bf16[144,1152]{1,0:T(8,128)(2,1)} %get-tuple-element.218), channel_id=1, source_target_pairs={{0,8},{4,12},{8,16},{12,20},{16,24},{20,28},{24,0},{28,4},{1,9},{5... | collective-permute-start | bytes 995336 | tf_op jit(solution)/shard_map/ppermute | solution.py:568
  631.2 38.8 %collective-permute-start.41 = (bf16[144,1152]{1,0:T(8,128)(2,1)}, bf16[144,1152]{1,0:T(8,128)(2,1)}, u32[]{:S(2)}, u32[]{:S(2)}) collective-permute-start(bf16[144,1152]{1,0:T(8,128)(2,1)} %get-tuple-element.219), channel_id=1, source_target_pairs={{0,16},{4,20},{8,24},{12,28},{16,0},{20,4},{24,8},{28,12},{1,17},{... | collective-permute-start | bytes 995336 | tf_op jit(solution)/shard_map/ppermute | solution.py:568
  632.3 37.7 %collective-permute-start.42 = (bf16[144,1152]{1,0:T(8,128)(2,1)}, bf16[144,1152]{1,0:T(8,128)(2,1)}, u32[]{:S(2)}, u32[]{:S(2)}) collective-permute-start(bf16[144,1152]{1,0:T(8,128)(2,1)} %get-tuple-element.217), channel_id=1, source_target_pairs={{0,24},{4,28},{8,0},{12,4},{16,8},{20,12},{24,16},{28,20},{1,25},{... | collective-permute-start | bytes 995336 | tf_op jit(solution)/shard_map/ppermute | solution.py:568
  672.6 74.2 %all-gather.21.cloned.1.call-start = ((), (), s32[]{:S(2)}) async-start(), calls=%async_computation.11 | async-start | bytes 2985984 | tf_op jit(solution)/shard_map/all_gather | solution.py:699
  682.5 30.5 %all-to-all-start.4 = ((bf16[4,3,144,288]{3,2,1,0:T(8,128)(2,1)}), bf16[4,3,144,288]{3,2,1,0:T(8,128)(2,1)}, u32[]{:S(2)}, u32[]{:S(2)}) async-start(bf16[4,3,144,288]{3,2,1,0:T(8,128)(2,1)} %shard_map.214), calls=%async_computation.4 | async-start | bytes 2654208 | tf_op jit(solution)/shard_map/all_to_all | solution.py:645
  (105 other events, 1255.8 us)
Sparse Core Ops, SparseCore 0:
  32.0 148.6 all-gather.22
  183.7 97.2 all-gather.24
  381.0 48.5 all-gather.12
  489.4 31.4 all-gather.10
  522.4 53.5 all-gather.16
  577.5 39.1 all-gather.14
  672.8 39.1 all-gather.18
  713.6 33.1 all-gather.20

commit v8 on v7

--- a/solution.py
+++ b/solution.py
@@ -109,25 +109,40 @@
     return jnp.sum(values, axis=0, keepdims=True)
 
 
+def start_loads(cuts, at, parts, whole, semaphores, first_index=0):
+    loads = []
+    for index, (part, first, rows) in enumerate(cuts, first_index):
+        span = pl.ds(pl.multiple_of(at[index] * 16, 16), rows)
+        source = parts[part].at[pl.ds(first, rows)]
+        loads.append(pltpu.make_async_copy(source, whole.at[span], semaphores.at[index]))
+        loads[-1].start()
+    return loads
+
+
 def attention_kernel(
     frames,
+    cuts,
     counts,
+    starts,
     tokens,
     cotangent,
     mods,
     bias,
-    blocks,
-    attn_in,
-    parts,
-    mixed_low,
-    proj_out,
-    resid_out,
-    mlp_in,
-    d_branch,
-    d_branch_sum,
-    mixed,
+    *refs,
 ):
+    whole_out, attn_in, parts, mixed_low, proj_out, resid_out, mlp_in, d_branch, d_branch_sum = refs[
+        -13:-4
+    ]
+    mixed, whole, semaphores, store_semaphore = refs[-4:]
+    pieces = refs[:-13]
     rows, width = tokens.shape
+    clip, clips = pl.program_id(0), pl.num_programs(0)
+    blocks = [whole.at[pl.ds(index * width, width)] for index in range(4)]
+    store = pltpu.make_async_copy(whole, whole_out, store_semaphore)
+
+    @pl.when(clip == 0)
+    def _():
+        start_loads(cuts, starts, pieces, whole, semaphores)
     tile = min(rows, 128)
     count = counts[pl.program_id(0)]
     shift_one, scale_one, gate_one = (mods[0, at : at + 1, :] for at in range(3))
@@ -140,14 +155,23 @@
         d_branch[span] = branch_back
         part_sum = column_sum(wide(branch_back))
         d_branch_sum[0] = part_sum if first == 0 else d_branch_sum[0] + part_sum
+
+    @pl.when(clip == 0)
+    def _():
+        for index, (part, first, size) in enumerate(cuts):
+            span = pl.ds(pl.multiple_of(starts[index] * 16, 16), size)
+            source = pieces[part].at[pl.ds(first, size)]
+            pltpu.make_async_copy(source, whole.at[span], semaphores.at[index]).wait()
+        store.start()
+
     scale = (width // HEADS) ** -0.5
     source = attn_in[...]
     for low, high in column_cuts(width):
         span = slice(low, high)
-        query = (dot_nn(source, blocks[0, :, span]) + bias[0:1, span]) * scale
+        query = (dot_nn(source, blocks[0][:, span]) + bias[0:1, span]) * scale
         parts[0, :, span], parts[1, :, span] = split_high(query)
-        parts[2, :, span], parts[3, :, span] = split_high(dot_nn(source, blocks[1, :, span]))
-        parts[4, :, span] = narrow(dot_nn(source, blocks[2, :, span]) + bias[2:3, span])
+        parts[2, :, span], parts[3, :, span] = split_high(dot_nn(source, blocks[1][:, span]))
+        parts[4, :, span] = narrow(dot_nn(source, blocks[2][:, span]) + bias[2:3, span])
     offset = score_offset(count, tile, frames, 1)
     mixed[...] = jnp.zeros_like(mixed)
     for first in range(0, rows, tile):
@@ -168,7 +192,7 @@
     source = mixed_low[...]
     for low, high in column_cuts(width):
         span = slice(low, high)
-        proj_out[:, span] = dot_nn(source, blocks[3, :, span]) + bias[3:4, span]
+        proj_out[:, span] = dot_nn(source, blocks[3][:, span]) + bias[3:4, span]
     for first in range(0, rows, tile):
         span = slice(first, first + tile)
         resid = wide(tokens[span]) + valid_rows(count, tile, frames) * gate_one * proj_out[span]
@@ -176,8 +200,13 @@
         normed, _ = norm_parts(resid)
         mlp_in[span] = narrow(normed * (1.0 + scale_two) + shift_two)
 
-
-def run_attention(frames, counts, tokens, cotangent, mods, bias, blocks):
+    @pl.when(clip == clips - 1)
+    def _():
+        store.wait()
+
+
+def run_attention(frames, counts, tokens, cotangent, mods, bias, gathered):
+    pieces, cuts, starts = gathered
     total, width = tokens.shape
     clips = mods.shape[0]
     rows = total // clips
@@ -185,17 +214,19 @@
     low = jax.ShapeDtypeStruct((total, width), jnp.bfloat16)
     full = jax.ShapeDtypeStruct((total, width), jnp.float32)
     return pl.pallas_call(
-        functools.partial(attention_kernel, frames),
+        functools.partial(attention_kernel, frames, cuts),
         grid=(clips,),
         in_specs=[
+            pl.BlockSpec(memory_space=pltpu.SMEM),
             pl.BlockSpec(memory_space=pltpu.SMEM),
             clip_rows,
             clip_rows,
             spec((1,) + mods.shape[1:], lambda clip: (clip, 0, 0)),
             held(bias.shape),
-            held(blocks.shape),
-        ],
+        ]
+        + [pl.BlockSpec(memory_space=pl.ANY)] * len(pieces),
         out_specs=[
+            pl.BlockSpec(memory_space=pl.ANY),
             clip_rows,
             spec((5, rows, width), lambda clip: (0, clip, 0)),
             clip_rows,
@@ -206,6 +237,7 @@
             spec((1, 1, width), lambda clip: (clip, 0, 0)),
         ],
         out_shape=[
+            jax.ShapeDtypeStruct((4 * width, width), jnp.bfloat16),
             low,
             jax.ShapeDtypeStruct((5, total, width), jnp.bfloat16),
             low,
@@ -215,48 +247,102 @@
             low,
             jax.ShapeDtypeStruct((clips, 1, width), jnp.float32),
         ],
-        scratch_shapes=[pltpu.VMEM((rows, width), jnp.float32)],
+        scratch_shapes=[
+            pltpu.VMEM((rows, width), jnp.float32),
+            pltpu.VMEM((4 * width, width), jnp.bfloat16),
+            pltpu.SemaphoreType.DMA((len(cuts),)),
+            pltpu.SemaphoreType.DMA,
+        ],
         compiler_params=pltpu.CompilerParams(vmem_limit_bytes=vmem_bytes),
         cost_estimate=pl.CostEstimate(
-            flops=12 * total * width * width, bytes_accessed=40 * total * width, transcendentals=0
+            flops=16 * total * width * width, bytes_accessed=100 * total * width, transcendentals=0
         ),
-    )(counts, tokens, cotangent, mods, bias, blocks)
-
-
-def hidden_kernel(mlp_in, block, bias, hidden, slope):
+    )(counts, stacked(starts), tokens, cotangent, mods, bias, *pieces)
+
+
+def stacked(numbers):
+    return jnp.stack([jnp.asarray(number, jnp.int32) for number in numbers])
+
+
+def hidden_kernel(cuts, order, starts, mlp_in, bias, *refs):
+    whole_out, hidden, slope, whole, semaphores, store_semaphores = refs[-6:]
+    pieces = refs[:-6]
+    step, steps = pl.program_id(0), pl.num_programs(0)
+    width = mlp_in.shape[-1]
+    flat = [cut for group in cuts for cut in group]
+    span = pl.ds(pl.multiple_of(order[step] * width, width), width)
+
+    @pl.when(step == 0)
+    def _():
+        start_loads(flat, starts, pieces, whole, semaphores)
+
+    index = 0
+    for at, group in enumerate(cuts):
+        first_index = index
+        index += len(group)
+
+        @pl.when(step == at)
+        def _(group=group, first_index=first_index):
+            for offset, (part, first, size) in enumerate(group):
+                target = pl.ds(pl.multiple_of(starts[first_index + offset] * 16, 16), size)
+                pltpu.make_async_copy(
+                    pieces[part].at[pl.ds(first, size)],
+                    whole.at[target],
+                    semaphores.at[first_index + offset],
+                ).wait()
+
+    pltpu.make_async_copy(whole.at[span], whole_out.at[span], store_semaphores.at[step]).start()
     root = (2.0 / math.pi) ** 0.5
     source = mlp_in[...]
-    for low, high in column_cuts(block.shape[-1]):
-        span = slice(low, high)
-        pre = dot_nn(source, block[0, :, span]) + bias[0, :, span]
+    block = whole.at[span]
+    for low, high in column_cuts(width):
+        lanes = slice(low, high)
+        pre = dot_nn(source, block[:, lanes]) + bias[0, :, lanes]
         square = pre * pre
         bent = jnp.tanh(root * pre * (1.0 + 0.044715 * square))
         half = 0.5 + 0.5 * bent
-        hidden[0, :, span] = narrow(pre * half)
+        hidden[0, :, lanes] = narrow(pre * half)
         steep = (0.5 * root) * pre * (1.0 + 3 * 0.044715 * square)
-        slope[0, :, span] = narrow(half + steep * (1.0 - bent * bent))
-
-
-def run_hidden(mlp_in, blocks, bias):
+        slope[0, :, lanes] = narrow(half + steep * (1.0 - bent * bent))
+
+    @pl.when(step == steps - 1)
+    def _():
+        for at in range(len(cuts)):
+            rows = pl.ds(pl.multiple_of(order[at] * width, width), width)
+            pltpu.make_async_copy(
+                whole.at[rows], whole_out.at[rows], store_semaphores.at[at]
+            ).wait()
+
+
+def run_hidden(mlp_in, gathered, bias):
+    pieces, cuts, starts, order = gathered
     total, width = mlp_in.shape
-    count = blocks.shape[0]
-    per_block = spec((1, total, width), lambda at: (at, 0, 0))
+    count = len(cuts)
+    per_block = pl.BlockSpec((1, total, width), lambda at, order, starts: (order[at], 0, 0))
     out = jax.ShapeDtypeStruct((count, total, width), jnp.bfloat16)
     return pl.pallas_call(
-        hidden_kernel,
-        grid=(count,),
-        in_specs=[
-            held(mlp_in.shape),
-            spec((1, width, width), lambda at: (at, 0, 0)),
-            spec((1, 1, width), lambda at: (at, 0, 0)),
-        ],
-        out_specs=[per_block, per_block],
-        out_shape=[out, out],
+        functools.partial(hidden_kernel, cuts),
+        grid_spec=pltpu.PrefetchScalarGridSpec(
+            num_scalar_prefetch=2,
+            grid=(count,),
+            in_specs=[
+                pl.BlockSpec((total, width), lambda at, order, starts: (0, 0)),
+                pl.BlockSpec((1, 1, width), lambda at, order, starts: (order[at], 0, 0)),
+            ]
+            + [pl.BlockSpec(memory_space=pl.ANY)] * len(pieces),
+            out_specs=[pl.BlockSpec(memory_space=pl.ANY), per_block, per_block],
+            scratch_shapes=[
+                pltpu.VMEM((count * width, width), jnp.bfloat16),
+                pltpu.SemaphoreType.DMA((len(starts),)),
+                pltpu.SemaphoreType.DMA((count,)),
+            ],
+        ),
+        out_shape=[jax.ShapeDtypeStruct((count * width, width), jnp.bfloat16), out, out],
         compiler_params=pltpu.CompilerParams(vmem_limit_bytes=vmem_bytes),
         cost_estimate=pl.CostEstimate(
-            flops=8 * total * width * width, bytes_accessed=30 * total * width, transcendentals=0
+            flops=8 * total * width * width, bytes_accessed=50 * total * width, transcendentals=0
         ),
-    )(mlp_in, blocks, bias)
+    )(stacked(order), stacked(starts), mlp_in, bias, *pieces)
 
 
 def branch_kernel(
@@ -614,7 +700,7 @@
         cost_estimate=pl.CostEstimate(
             flops=0, bytes_accessed=4 * rows * width, transcendentals=0
         ),
-    )(jnp.stack([jnp.asarray(start, jnp.int32) for start in starts]), *parts)
+    )(stacked(starts), *parts)
 
 
 def own_rows(parts, group):
@@ -657,37 +743,72 @@
     return all_rows.reshape(group, total, total)
 
 
-def gather_pieces(rows, group):
+def join_line(rows):
+    chips, chip = lax.axis_size("dp") // 2, lax.axis_index("dp") // 2
+    chunk = rows.shape[0]
+    found = [rows] + [chip_shift(rows, step) for step in range(1, chips)]
+    starts = [(chip - step) % chips * (chunk // 16) for step in range(chips)]
+    return place(found, [(step, 0, chunk) for step in range(chips)], starts, chips * chunk)
+
+
+def gather_first(rows, group):
     ranks, at = lax.axis_size("fsdp"), lax.axis_index("fsdp")
+    total = rows.shape[-1]
     if ranks != group:
-        blocks = gather_blocks(rows, group)
-        (blocks,) = yield (blocks,)
-        (blocks,) = yield (blocks,)
-        yield blocks
+        blocks = gather_blocks(rows, group).reshape(group * total, total)
+        for _ in range(3):
+            (blocks,) = yield (blocks,)
+        yield [blocks], [(0, 0, group * total)], [0]
         return
     chips = lax.axis_size("dp") // 2
-    core, chip = lax.axis_index("dp") % 2, lax.axis_index("dp") // 2
-    chunk, total = rows.shape
-    half = total // 2
-    unit = chunk // 16
-    found = [rows] + [chip_shift(rows, step) for step in range(1, chips)]
-    starts = [(chip - step) % chips * unit for step in range(chips)]
-    line = place(found, [(step, 0, chunk) for step in range(chips)], starts, half)
+    core = lax.axis_index("dp") % 2
+    chunk = rows.shape[0]
+    (line,) = yield (join_line(rows),)
+    low_in, high_in = yield (rank_swap(line, 1), rank_swap(line, 2))
+    half = total // 4
+    parts = [line, low_in, high_in]
+    parts += [rank_swap(high_in[:half], 1), rank_swap(low_in[half:], 2)]
+    others = [core_swap(part) for part in parts[:3]]
+    parts[3:] = yield tuple(parts[3:])
+    others += [core_swap(part) for part in parts[3:]]
+    cuts, starts = [], []
+    for side, found in ((core, parts), (1 - core, others)):
+        for index, part in enumerate(found):
+            bits, first_chip = ((0, 0), (1, 0), (2, 0), (3, 0), (3, chips // 2))[index]
+            for step in range(part.shape[0] // chunk):
+                cuts.append((len(parts) * (found is others) + index, step * chunk, chunk))
+                row = (at ^ bits) * (2 * chips) + 2 * (first_chip + step) + side
+                starts.append(row * (chunk // 16))
+    yield parts + others, cuts, starts
+
+
+def gather_second(rows, group):
+    ranks, at = lax.axis_size("fsdp"), lax.axis_index("fsdp")
+    total = rows.shape[-1]
+    if ranks != group:
+        blocks = gather_blocks(rows, group).reshape(group * total, total)
+        for _ in range(2):
+            (blocks,) = yield (blocks,)
+        cuts = [[(0, index * total, total)] for index in range(group)]
+        yield [blocks], cuts, [index * (total // 16) for index in range(group)], range(group)
+        return
+    chips = lax.axis_size("dp") // 2
+    core = lax.axis_index("dp") % 2
+    chunk, half = rows.shape[0], total // 2
+    line = join_line(rows)
     cuts = [(side, step * chunk, chunk) for side in range(2) for step in range(chips)]
-    starts = [(2 * step + side) * unit for side in (core, 1 - core) for step in range(chips)]
-    own = place([line, core_swap(line)], cuts, starts, total)
-    (own,) = yield (own,)
+    starts = [
+        (2 * step + side) * (chunk // 16) for side in (core, 1 - core) for step in range(chips)
+    ]
+    (own,) = yield (place([line, core_swap(line)], cuts, starts, total),)
     share = lax.dynamic_slice_in_dim(own, core * half, half, 0)
-    mine = [rank_swap(share, bits) for bits in range(1, ranks)]
-    own, *mine = yield (own, *mine)
-    others = [core_swap(part) for part in mine]
-    starts = [at * 2] + [
-        (at ^ bits) * 2 + side for side in (core, 1 - core) for bits in range(1, ranks)
-    ]
-    starts = [start * (half // 16) for start in starts]
-    cuts = [(0, 0, total)] + [(1 + index, 0, half) for index in range(2 * ranks - 2)]
-    found = place([own] + mine + others, cuts, starts, group * total)
-    yield found.reshape(group, total, total)
+    mine = yield tuple(rank_swap(share, bits) for bits in range(1, ranks))
+    parts, cuts, starts = [own], [[(0, 0, total)]], [at * (total // 16)]
+    for bits in range(1, ranks):
+        parts += [mine[bits - 1], core_swap(mine[bits - 1])]
+        cuts.append([(2 * bits - 1, 0, half), (2 * bits, 0, half)])
+        starts += [((at ^ bits) * 2 + side) * (half // 16) for side in (core, 1 - core)]
+    yield parts, cuts, starts, [at ^ bits for bits in range(ranks)]
 
 
 def gather_own(rows, group):
@@ -709,7 +830,7 @@
         rows = lax.psum_scatter(
             blocks.reshape(group * total, -1), ("fsdp", "dp"), scatter_dimension=0, tiled=True
         )
-        for _ in range(3):
+        for _ in range(6):
             (rows,) = yield (rows,)
         yield gather_own(rows[None], group)[0]
         return
@@ -717,15 +838,15 @@
     chunk = half // chips
     core, chip = lax.axis_index("dp") % 2, lax.axis_index("dp") // 2
     low_bit, high_bit = lax.axis_index("fsdp") % 2, lax.axis_index("fsdp") // 2
-    away = narrow(product(cut((1 - core) * half, half)))
+    (away,) = yield (narrow(product(cut((1 - core) * half, half))),)
+    (away_in,) = yield (core_swap(away),)
     here = product(cut(core * half, half))
-    here = narrow(here + wide(core_swap(away)))
+    here = narrow(here + wide(away_in))
     here = here.reshape(2, 2, chips, chunk, -1)
     middle = chips // 2
     first, second = here[:, :, :middle], here[:, :, middle:]
-    first_in = rank_swap(entry(first, 1 - low_bit, 1), 1)
-    second_in = rank_swap(entry(second, 1 - high_bit, 0), 2)
-    first_in, second_in = yield (first_in, second_in)
+    first_out, second_out = yield (entry(first, 1 - low_bit, 1), entry(second, 1 - high_bit, 0))
+    first_in, second_in = yield (rank_swap(first_out, 1), rank_swap(second_out, 2))
     first = narrow(wide(entry(first, low_bit, 1)) + wide(first_in))
     second = narrow(wide(entry(second, high_bit, 0)) + wide(second_in))
     first_in = rank_swap(entry(first, 1 - high_bit), 2)
@@ -848,17 +969,12 @@
     attn_panels = next(attn_rows)
     first_parts = lax.all_gather(packed([cond_low, narrow(biases)], 16), "dp", axis=0, tiled=True)
     attn_panels, first_parts, other_shards = tie(attn_panels, first_parts, shards[1:])
-    attn_w = gather_blocks(attn_rows.send(attn_panels)[0], group)
+    attn_rows = attn_rows.send(attn_panels)[0]
     other_rows = own_rows(other_shards, group)
-    other_rows = other_rows.send(next(other_rows))
-    one_steps = gather_pieces(other_rows[0], group)
-    one_parts, first_parts = tie(next(one_steps), first_parts)
-    one_parts = one_steps.send(one_parts)
-    two_w = gather_blocks(other_rows[1], group)
-    roots = jnp.stack([narrow(left_roots[mod_count:]), narrow(right_roots[mod_count:])])
-    roots, first_parts = tie(roots, first_parts)
-    root_rows = own_rows(roots.reshape(-1, group, row_part, col_part), group)
-    root_panels = next(root_rows)
+    other_panels = next(other_rows)
+    attn_steps = gather_first(attn_rows, group)
+    attn_parts = next(attn_steps)
+    one_rows, two_rows = other_rows.send(other_panels)
 
     first_parts = first_parts.reshape(dp_count, -1)
     cond_all = first_parts[:, : clip_count * width].reshape(all_clips, width)
@@ -866,13 +982,24 @@
     cond_rows = lax.dynamic_slice_in_dim(cond_all, dp_at * row_part, row_part, 1)
     cond_cols = wide(lax.dynamic_slice_in_dim(cond_all, rank_at * col_part, col_part, 1))
     mod_parts = fast_dot("cr,jre->cje", cond_rows, low_weights[:mod_count])
+    mod_parts, attn_parts = tie(mod_parts, attn_parts)
+    attn_parts = attn_steps.send(attn_parts)
     mod_parts = lax.all_to_all(mod_parts, "dp", 0, 0, tiled=True)
+    mod_parts, one_rows = tie(mod_parts, one_rows)
+    one_steps = gather_second(one_rows, group)
+    one_parts = next(one_steps)
     mod_cols = jnp.sum(mod_parts.reshape(dp_count, clip_count, mod_count, col_part), axis=0)
     left_cond = jnp.einsum("jrk,ck->jrc", left_roots[:mod_count], cond_cols, precision=precise)
     mod_size, bias_size = mod_cols.size, dp_count * bias_part
-    second_parts = lax.all_gather(
-        packed([mod_cols, bias_rows, left_cond], 8), "fsdp", axis=0, tiled=True
-    ).reshape(ranks, -1)
+    second_parts, attn_parts = tie(packed([mod_cols, bias_rows, left_cond], 8), attn_parts)
+    attn_parts = attn_steps.send(attn_parts)
+    second_parts = lax.all_gather(second_parts, "fsdp", axis=0, tiled=True)
+    second_parts, one_parts, attn_parts = tie(second_parts, one_parts, attn_parts)
+    one_parts = one_steps.send(one_parts)
+    gathered = attn_steps.send(attn_parts)
+    attn_parts, two_rows = tie(attn_parts, two_rows)
+    two_w = gather_blocks(two_rows, group)
+    second_parts = second_parts.reshape(ranks, -1)
     mods = second_parts[:, :mod_size].reshape(ranks, clip_count, mod_count, col_part)
     mods = mods.transpose(1, 2, 0, 3).reshape(clip_count, mod_count, width)
     bias_all = second_parts[:, mod_size : mod_size + bias_size].reshape(ranks, dp_count, bias_part)
@@ -885,24 +1012,26 @@
         [bias_all[6:7], jnp.zeros((1, width), jnp.float32), bias_all[7:14]]
     )
 
-    attn_in, parts, mixed, proj, resid, mlp_in, d_branch, d_branch_sums = run_attention(
-        frames, frame_counts, stream, grad_out, mods, bias_table, attn_w
-    )
-    mlp_in, one_parts, root_panels = tie(mlp_in, one_parts, root_panels)
-    one_w = one_steps.send(one_parts)
-    hidden, slope = run_hidden(mlp_in, one_w, bias_table[4:8, None])
+    attn_w, attn_in, parts, mixed, proj, resid, mlp_in, d_branch, d_branch_sums = run_attention(
+        frames, frame_counts, stream, grad_out, mods, bias_table, gathered
+    )
+    attn_w = attn_w.reshape(group, width, width)
+    roots = jnp.stack([narrow(left_roots[mod_count:]), narrow(right_roots[mod_count:])])
+    mlp_in, one_parts, roots = tie(mlp_in, one_parts, roots)
+    root_rows = own_rows(roots.reshape(-1, group, row_part, col_part), group)
+    root_panels = next(root_rows)
+    one_w, hidden, slope = run_hidden(mlp_in, one_steps.send(one_parts), bias_table[4:8, None])
+    one_w = one_w.reshape(group, width, width)
+
     two_steps = sum_blocks(
         lambda left: fast_dot("jtd,te->jde", left, d_branch),
         lambda first, size: lax.dynamic_slice_in_dim(hidden, first, size, 2),
         width,
         group,
     )
-    two_parts = list(next(two_steps))
-    root_rows = root_rows.send(root_panels)
-    hidden, two_parts[0], root_rows = tie(hidden, two_parts[0], root_rows)
-    left_rows, right_rows = jnp.split(root_rows, 2)
-    right_wholes = [gather_own(rows[None], group)[0] for rows in right_rows]
-
+    two_parts = next(two_steps)
+    hidden, two_parts = tie(hidden, two_parts)
+    two_parts = two_steps.send(two_parts)
     d_pre, d_pre_sums, block_out, d_gate_two = run_branch(
         frames,
         frame_counts,
@@ -915,25 +1044,32 @@
         resid,
         grad_out,
     )
+    d_pre, two_parts, root_panels = tie(d_pre, two_parts, root_panels)
+    two_parts = two_steps.send(two_parts)
     d_pre, two_parts = tie(d_pre, two_parts)
-    two_parts = list(two_steps.send(two_parts))
+    two_parts = two_steps.send(two_parts)
+    left_rows, right_rows = jnp.split(root_rows.send(root_panels), 2)
+    right_wholes = [gather_own(rows[None], group)[0] for rows in right_rows]
     one_steps = sum_blocks(
         lambda left: fast_dot("td,jte->jde", left, d_pre),
         lambda first, size: lax.dynamic_slice_in_dim(mlp_in, first, size, 1),
         width,
         group,
     )
-    one_parts = list(next(one_steps))
-    d_pre, one_parts[0], two_parts = tie(d_pre, one_parts[0], two_parts)
-    two_parts = two_steps.send(two_parts)
+    one_parts = next(one_steps)
+    d_pre, one_parts = tie(d_pre, one_parts)
+    one_parts = one_steps.send(one_parts)
     d_resid, d_proj, resid_sums = run_resid(
         frames, frame_counts, d_pre, one_w, mods, resid, grad_out, proj
     )
+    d_proj, one_parts, two_parts = tie(d_proj, one_parts, two_parts)
+    two_parts = two_steps.send(two_parts)
+    one_parts = one_steps.send(one_parts)
     d_proj, one_parts = tie(d_proj, one_parts)
     one_parts = one_steps.send(one_parts)
     d_heads, head_sums = run_attention_back(frames, frame_counts, d_proj, parts, attn_w)
-    d_heads, one_parts, two_parts = tie(d_heads, one_parts, two_parts)
-    whole_two = two_steps.send(two_parts)
+    d_heads, two_parts = tie(d_heads, two_parts)
+    two_parts = two_steps.send(two_parts)
     attn_steps = sum_blocks(
         lambda left: fast_dot("jtd,jte->jde", left, d_heads),
         lambda first, size: jnp.stack(
@@ -942,16 +1078,20 @@
         width,
         group,
     )
-    attn_parts = list(next(attn_steps))
-    d_heads, attn_parts[0], one_parts = tie(d_heads, attn_parts[0], one_parts)
+    attn_parts = next(attn_steps)
+    d_heads, attn_parts = tie(d_heads, attn_parts)
+    attn_parts = attn_steps.send(attn_parts)
+    d_heads, attn_parts, one_parts = tie(d_heads, attn_parts, one_parts)
     one_parts = one_steps.send(one_parts)
+    attn_parts = attn_steps.send(attn_parts)
+    d_heads, attn_parts = tie(d_heads, attn_parts)
+    attn_parts = attn_steps.send(attn_parts)
     input_grad, input_sums = run_input(d_heads, attn_w, mods, stream, d_resid)
-    products_two = owned_step(whole_two, left_rows[2], right_wholes[2], group)
-    input_sums, attn_parts, one_parts, products_two = tie(
-        input_sums, attn_parts, one_parts, products_two
-    )
+    input_sums, one_parts, two_parts = tie(input_sums, one_parts, two_parts)
+    whole_two = two_steps.send(two_parts)
+    one_parts = one_steps.send(one_parts)
+    input_sums, attn_parts = tie(input_sums, attn_parts)
     attn_parts = attn_steps.send(attn_parts)
-    whole_one = one_steps.send(one_parts)
 
     d_mods = jnp.stack(
         [
@@ -987,6 +1127,8 @@
         axis=1,
     )
     rank_sums = jnp.sum(lax.all_to_all(to_ranks, "fsdp", 0, 0, tiled=True), axis=0)
+    rank_sums, attn_parts = tie(rank_sums, attn_parts)
+    attn_parts = attn_steps.send(attn_parts)
     to_rows = jnp.concatenate(
         [
             jnp.broadcast_to(rank_sums[None, :mod_size], (dp_count, mod_size)),
@@ -994,10 +1136,9 @@
         ],
         axis=1,
     )
-    to_rows, attn_parts = tie(to_rows, attn_parts)
-    attn_parts = attn_steps.send(attn_parts)
     from_rows = lax.all_to_all(to_rows, "dp", 0, 0, tiled=True)
-    back_two = shard_rows(products_two, group)
+    from_rows, one_parts = tie(from_rows, one_parts)
+    whole_one = one_steps.send(one_parts)
     bias_grad = jnp.sum(from_rows[:, mod_size:], axis=0)
     mod_grad_cols = from_rows[:, :mod_size].reshape(all_clips, mod_count, col_part)
     mod_grad = lax.all_gather(packed([mod_grad_cols], 8), "fsdp", axis=0, tiled=True)
@@ -1018,18 +1159,18 @@
     cond_side = jnp.einsum("cb,bje->jce", cond_gram, mod_grad_cols, precision=precise)
     ada_right = jnp.einsum("cjr,jce->jre", mod_grad_rows, cond_side, precision=precise)
 
+    products_two = owned_step(whole_two, left_rows[2], right_wholes[2], group)
+    products_two, right_parts, attn_parts = tie(products_two, right_parts, attn_parts)
+    whole_attn = attn_steps.send(attn_parts)
+    back_two = shard_rows(products_two, group)
     products_one = owned_step(whole_one, left_rows[1], right_wholes[1], group)
-    back_two, products_one, right_parts, attn_parts = tie(
-        back_two, products_one, right_parts, attn_parts
-    )
-    whole_attn = attn_steps.send(attn_parts)
     back_one = shard_rows(products_one, group)
     right_parts = lax.all_gather(packed([right_parts], 8), "dp", axis=0, tiled=True)
     mod_right = jnp.sum(right_parts.reshape(dp_count, -1), axis=0)[: mod_grad_cols.size]
     mod_right = mod_right.reshape(all_clips, mod_count, col_part)
     ada_pre = jnp.einsum("jrc,cje->jre", left_cond, mod_right, precision=precise)
-    whole_attn, back_one, ada_pre, ada_left, ada_right = tie(
-        whole_attn, back_one, ada_pre, ada_left, ada_right
+    whole_attn, back_one, back_two, ada_pre, ada_left, ada_right = tie(
+        whole_attn, back_one, back_two, ada_pre, ada_left, ada_right
     )
     back_attn = shard_rows(owned_step(whole_attn, left_rows[0], right_wholes[0], group), group)
 

time: 809 us -> 778 us (0.962)
  starting transfers between devices: 112 us -> 96.8 us
  waiting for transfers between devices: 203 us -> 189 us
  blocking collectives: 112 us -> 121 us
    all_to_all x0 -> x1, blocking collectives: none -> 44.9 us  [per_device(): from_rows = lax.all_to_all(to_rows, 'dp', 0, 0, tiled=True)]
    all_gather x1, blocking collectives: 60.2 us -> 21.1 us  [per_device(): second_parts = lax.all_gather(second_parts, 'fsdp', axis=0, tiled=True)]
    ppermute x24 -> x28, waiting for transfers between devices: 76 us -> 97.4 us  [rank_swap(): return lax.ppermute(array, 'fsdp', [(at, at ^ bits) for at in range(count)])]
    all_to_all x1, starting transfers between devices: 23.2 us -> 8.85 us  [per_device(): mod_parts = lax.all_to_all(mod_parts, 'dp', 0, 0, tiled=True)]
    ppermute x7 -> x12, waiting for transfers between devices: 20.7 us -> 6.66 us  [core_swap(): return lax.ppermute(array, 'dp', [(at, at ^ 1) for at in range(count)])]
    all_gather x3, waiting for transfers between devices: 33.8 us -> 20.8 us  [gather_own(): return lax.all_gather(rows, 'dp', axis=1, tiled=True)]
    all_gather x3, waiting for transfers between devices: 10.6 us -> 0.04 us  [sum_blocks(): yield lax.all_gather(narrow(rows), 'dp', axis=0, tiled=True)]
    all_gather x1, blocking collectives: 20.8 us -> 31 us  [per_device(): lax.all_gather(packed([right_parts], 8), 'dp', axis=0, tiled=True)]
  transfers between devices with their start and end apart: 57 -> 67, of which waited for: 22 -> 19; matrix products, arithmetic and copies ran while one was open for 18% -> 17% of each run, Pallas kernels for 20% -> 20%
where the time goes in v8:
time: 778 us; the launch traced here: 769 us
  waiting for transfers between devices  189 us (24%)
  Pallas kernels  160 us (21%)
  blocking collectives  121 us (16%)
  starting transfers between devices  96.8 us (12%)
  local copies, waits for them, and re-layouts  70.8 us (9%)
  other arithmetic  59.6 us (8%)
  matrix products  54.6 us (7%)
  between operations  16.4 us (2%)
    ppermute x28, waiting for transfers between devices, rank_swap(): return lax.ppermute(array, 'fsdp', [(at, at ^ bits) for at in range(count)])  97.4 us
    all_to_all x1, blocking collectives, per_device(): from_rows = lax.all_to_all(to_rows, 'dp', 0, 0, tiled=True)  44.9 us
    dot_general x7, matrix products, fast_dot(): jnp.einsum(subscripts, left, right, preferred_element_type=jnp.float32)  42.7 us
    ppermute x15, waiting for transfers between devices, chip_shift(): lax.ppermute(array, 'dp', [(at, (at + 2 * step) % count) for at in range(...  40.9 us
    pallas_call x1, Pallas kernels, run_attention(): pl.pallas_call(functools.partial(attention_kernel, frames, cuts), grid=(c...  40.7 us
    ppermute x15, starting transfers between devices, chip_shift(): lax.ppermute(array, 'dp', [(at, (at + 2 * step) % count) for at in range(...  34.5 us
    ppermute x28, starting transfers between devices, rank_swap(): return lax.ppermute(array, 'fsdp', [(at, at ^ bits) for at in range(count)])  33.8 us
    all_gather x1, blocking collectives, per_device(): lax.all_gather(packed([right_parts], 8), 'dp', axis=0, tiled=True)  31 us
  transfers between devices with their start and end apart: 67, of which 19 were waited for; matrix products, arithmetic and copies ran while one was open for 17% of the time, Pallas kernels for 20%

profile of v8, /device:TPU:0, one launch (start us, length us, event | category | flops | bytes accessed | tf_op | source)
XLA Modules:
  0.0 768.9 jit_solution(14184480557869638196)
XLA Ops:
  14.5 14.7 %all_gather.33 = bf16[256,128]{1,0:T(8,128)(2,1)S(1)} all-gather(bf16[32,128]{1,0:T(8,128)(2,1)S(1)} %fusion.116), channel_id=1, replica_groups=mesh['dp'=8,'fsdp'=4] {'dp'}, dimensions={0}, use_global_device_ids=true | all-gather | bytes 73728 | tf_op jit(solution)/shard_map/all_gather | solution.py:970
  42.0 6.9 collective-permute-done.7
  63.4 8.9 %all-to-all-start = ((f32[16,6,288]{2,1,0:T(8,128)}), f32[16,6,288]{2,1,0:T(8,128)S(1)}, u32[]{:S(2)}, u32[]{:S(2)}) async-start(f32[16,6,288]{2,1,0:T(8,128)} %copy.94), calls=%async_computation | async-start | bytes 393216 | tf_op jit(solution)/shard_map/all_to_all | solution.py:987
  84.4 8.8 %collective-permute-done.11.refs_1_ = bf16[144,1152]{1,0:T(8,128)(2,1)S(1)} collective-permute-done((bf16[144,1152]{1,0:T(8,128)(2,1)S(1)}, bf16[144,1152]{1,0:T(8,128)(2,1)S(1)}, u32[]{:S(2)}, u32[]{:S(2)}) %collective-permute-start.11) | collective-permute-done | bytes 331808 | tf_op jit(solution)/shard_map/ppermute | solution.py:654
  93.2 11.9 %collective-permute-done.12.refs_2_ = bf16[144,1152]{1,0:T(8,128)(2,1)S(1)} collective-permute-done((bf16[144,1152]{1,0:T(8,128)(2,1)S(1)}, bf16[144,1152]{1,0:T(8,128)(2,1)S(1)}, u32[]{:S(2)}, u32[]{:S(2)}) %collective-permute-start.12) | collective-permute-done | bytes 331808 | tf_op jit(solution)/shard_map/ppermute | solution.py:654
  116.3 21.1 %all_gather.34 = f32[672,128]{1,0:T(8,128)} all-gather(f32[168,128]{1,0:T(8,128)S(1)} %pad_bitcast_fusion), channel_id=1, replica_groups=mesh['dp'=8,'fsdp'=4] {'fsdp'}, dimensions={0}, use_global_device_ids=true | all-gather | bytes 430080 | tf_op jit(solution)/shard_map/all_gather | solution.py:996
  156.4 40.7 %shard_map.207 = (bf16[4608,1152]{1,0:T(8,128)(2,1)}, bf16[512,1152]{1,0:T(8,128)(2,1)S(1)}, bf16[5,512,1152]{2,1,0:T(8,128)(2,1)}, bf16[512,1152]{1,0:T(8,128)(...) custom-call(s32[2]{0:T(128)S(1)} %copy-done.4, ...), custom_call_target="tpu_custom_call" | custom-call | flops 10871635968 | bytes 58982400 | tf_op jit(solution)/shard_map/pallas_call | solution.py:216
  197.1 37.5 %collective-permute-done.24.refs_5_ = bf16[576,1152]{1,0:T(8,128)(2,1)} collective-permute-done((bf16[576,1152]{1,0:T(8,128)(2,1)S(1)}, bf16[576,1152]{1,0:T(8,128)(2,1)}, u32[]{:S(2)}, u32[]{:S(2)}) %collective-permute-start.24) | collective-permute-done | bytes 1327136 | tf_op jit(solution)/shard_map/ppermute | solution.py:659
  243.2 14.1 %shard_map.208 = (bf16[4608,1152]{1,0:T(8,128)(2,1)}, bf16[4,512,1152]{2,1,0:T(8,128)(2,1)}, bf16[4,512,1152]{2,1,0:T(8,128)(2,1)}) custom-call(s32[4]{0:T(128)S(1)} %pad_add_fusion.order, s32[7]{0:T(128)S(1)} %stack.232.starts, bf16[512,1152]{1,0:T(8,128)(2,1)S(1)} %copy-done.7, f32[4,1,1152]{2,1,0:T(1,128)S(1)} %copy.106.bias, ...), custom_call_target="tpu_custom_call" | custom-call | flops 5435817984 | bytes 29491200 | tf_op jit(solution)/shard_map/pallas_call | solution.py:323
  257.3 8.0 %convolution_convert_fusion.1 = bf16[4,576,1152]{2,1,0:T(8,128)(2,1)} fusion(bf16[4,512,1152]{2,1,0:T(8,128)(2,1)} %get-tuple-element.139.hidden, s32[]{:T(128)S(6)} %select_n.448, bf16[512,1152]{1,0:T(8,128)(2,1)S(1)} %copy-done.10), kind=kOutput, calls=%fused_computation.5 | convolution fusion | flops 2720563200 | bytes 9109508 | tf_op jit(solution)/shard_map/jtd,te->jde/dot_general | solution.py:865
  273.7 20.7 %shard_map.209 = (bf16[4,512,1152]{2,1,0:T(8,128)(2,1)}, f32[4,1,1152]{2,1,0:T(1,128)S(1)}, bf16[512,1152]{1,0:T(8,128)(2,1)}, f32[2,1,1152]{2,1,0:T(1,128)S(1)}) custom-call(s32[2]{0:T(128)S(1)} %copy-done.4, bf16[4,512,1152]{2,1,0:T(8,128)(2,1)} %get-tuple-element.139.hidden, bf16[4,512,1152]{2,1,0:T(8,128)(2,1)} %get-tuple-element.140.slope, ...), custom_call_target="tpu_custom_call" | custom-call | flops 10871635968 | bytes 23592960 | tf_op jit(solution)/shard_map/pallas_call | solution.py:397
  294.4 7.2 collective-permute-done.30
  301.6 7.3 add_convert_fusion.1
  330.0 15.9 %shard_map.210 = (f32[512,1152]{1,0:T(8,128)}, bf16[512,1152]{1,0:T(8,128)(2,1)S(1)}, f32[2,4,1152]{2,1,0:T(4,128)S(1)}) custom-call(s32[2]{0:T(128)S(1)} %copy-done.4, bf16[4,512,1152]{2,1,0:T(8,128)(2,1)} %get-tuple-element.150.d_pre, bf16[4,1152,1152]{2,1,0:T(8,128)(2,1)} %bitcast.349, f32[2,6,1152]{2,1,0:T(8,128)S(1)} %broadcast_add_fusion.mods, ...), custom_call_target="tpu_custom_call" | custom-call | flops 5435817984 | bytes 23592960 | tf_op jit(solution)/shard_map/pallas_call | solution.py:484
  361.3 7.6 fusion
  372.5 26.3 %shard_map.211 = (bf16[4,512,1152]{2,1,0:T(8,128)(2,1)}, f32[2,3,1152]{2,1,0:T(4,128)S(1)}) custom-call(s32[2]{0:T(128)S(1)} %copy-done.4, bf16[512,1152]{1,0:T(8,128)(2,1)S(1)} %get-tuple-element.159.d_proj, bf16[5,512,1152]{2,1,0:T(8,128)(2,1)} %get-tuple-element.160.parts, bf16[4,1152,1152]{2,1,0:T(8,128)(2,1)} %bitcast.347), custom_call_target="tpu_custom_call" | custom-call | flops 8153726976 | bytes 11796480 | tf_op jit(solution)/shard_map/pallas_call | solution.py:553
  398.8 7.4 convolution_convert_fusion
  423.9 9.3 %collective-permute-start.42 = (bf16[144,1152]{1,0:T(8,128)(2,1)}, bf16[144,1152]{1,0:T(8,128)(2,1)}, u32[]{:S(2)}, u32[]{:S(2)}) collective-permute-start(bf16[144,1152]{1,0:T(8,128)(2,1)} %get-tuple-element.266), channel_id=1, source_target_pairs={{0,8},{4,12},{8,16},{12,20},{16,24},{20,28},{24,0},{28,4},{1,9},{5... | collective-permute-start | bytes 995336 | tf_op jit(solution)/shard_map/ppermute | solution.py:654
  433.4 13.7 %collective-permute-done.38 = bf16[2,2,144,1152]{3,2,1,0:T(8,128)(2,1)} collective-permute-done((bf16[2,2,144,1152]{3,2,1,0:T(8,128)(2,1)}, bf16[2,2,144,1152]{3,2,1,0:T(8,128)(2,1)}, u32[]{:S(2)}, u32[]{:S(2)}) %collective-permute-start.38) | collective-permute-done | bytes 1327136 | tf_op jit(solution)/shard_map/ppermute | solution.py:659
  447.1 8.5 %collective-permute-start.44 = (bf16[144,1152]{1,0:T(8,128)(2,1)}, bf16[144,1152]{1,0:T(8,128)(2,1)}, u32[]{:S(2)}, u32[]{:S(2)}) collective-permute-start(bf16[144,1152]{1,0:T(8,128)(2,1)} %get-tuple-element.265), channel_id=1, source_target_pairs={{0,24},{4,28},{8,0},{12,4},{16,8},{20,12},{24,16},{28,20},{1,25},{... | collective-permute-start | bytes 995336 | tf_op jit(solution)/shard_map/ppermute | solution.py:654
  473.8 11.2 %shard_map.212 = (bf16[512,1152]{1,0:T(8,128)(2,1)}, f32[2,2,1152]{2,1,0:T(2,128)S(1)}) custom-call(bf16[4,512,1152]{2,1,0:T(8,128)(2,1)} %get-tuple-element.174.d_qkv, bf16[4,1152,1152]{2,1,0:T(8,128)(2,1)} %bitcast.348, f32[2,6,1152]{2,1,0:T(8,128)S(1)} %broadcast_add_fusion.mods, bf16[512,1152]{1,0:T(8,128)(2,1)S(1)} %bitcast.345, f32[512,1152]{1,0:T(8,128)S(1)} %copy-done), custom_call_target="tpu_custom_call" | custom-call | flops 4076863488 | bytes 17694720 | tf_op jit(solution)/shard_map/pallas_call | solution.py:615
  493.2 25.2 %collective-permute-done.45 = bf16[2,2,144,1152]{3,2,1,0:T(8,128)(2,1)S(1)} collective-permute-done((bf16[2,2,144,1152]{3,2,1,0:T(8,128)(2,1)}, bf16[2,2,144,1152]{3,2,1,0:T(8,128)(2,1)S(1)}, u32[]{:S(2)}, u32[]{:S(2)}) %collective-permute-start.45) | collective-permute-done | bytes 1327136 | tf_op jit(solution)/shard_map/ppermute | solution.py:659
  538.4 44.9 %all_to_all.41 = f32[8,1,3960]{2,1,0:T(1,128)S(1)} all-to-all(f32[8,1,3960]{2,1,0:T(1,128)S(1)} %all_to_all.29), channel_id=1, replica_groups=mesh['dp'=8,'fsdp'=4] {'dp'}, dimensions={0} | all-to-all | bytes 253440 | tf_op jit(solution)/shard_map/all_to_all | solution.py:1139
  594.4 9.9 %all_gather.38 = f32[864,128]{1,0:T(8,128)S(1)} all-gather(f32[216,128]{1,0:T(8,128)S(1)} %reshape.297), channel_id=1, replica_groups=mesh['dp'=8,'fsdp'=4] {'fsdp'}, dimensions={0}, use_global_device_ids=true | all-gather | bytes 552960 | tf_op jit(solution)/shard_map/all_gather | solution.py:1144
  610.3 8.3 %shard_map.213 = bf16[4,3,144,288]{3,2,1,0:T(8,128)(2,1)} custom-call(s32[1]{0:T(128)} %bitcast.127.at, bf16[1152,1152]{1,0:T(8,128)(2,1)} %all-gather.10.cloned.1.call-done.gathered, bf16[144,1152]{1,0:T(8,128)(2,1)S(1)} %get-tuple-element.245.left_root, bf16[1152,1152]{1,0:T(8,128)(2,1)} %bitcast.370), custom_call_target="tpu_custom_call" | custom-call | flops 2293235712 | bytes 7962624 | tf_op jit(solution)/shard_map/pallas_call | solution.py:908
  618.6 13.4 %collective-permute-done.53 = bf16[144,1152]{1,0:T(8,128)(2,1)} collective-permute-done((bf16[144,1152]{1,0:T(8,128)(2,1)}, bf16[144,1152]{1,0:T(8,128)(2,1)}, u32[]{:S(2)}, u32[]{:S(2)}) %collective-permute-start.53) | collective-permute-done | bytes 331808 | tf_op jit(solution)/shard_map/ppermute | solution.py:654
  645.0 8.3 %shard_map.214 = bf16[4,3,144,288]{3,2,1,0:T(8,128)(2,1)} custom-call(s32[1]{0:T(128)} %bitcast.127.at, bf16[1152,1152]{1,0:T(8,128)(2,1)} %all-gather.16.cloned.1.call-done.gathered, bf16[144,1152]{1,0:T(8,128)(2,1)S(1)} %get-tuple-element.243.left_root, bf16[1152,1152]{1,0:T(8,128)(2,1)} %bitcast.371), custom_call_target="tpu_custom_call" | custom-call | flops 2293235712 | bytes 7962624 | tf_op jit(solution)/shard_map/pallas_call | solution.py:908
  658.7 31.0 %all_gather.42 = f32[1728,128]{1,0:T(8,128)} all-gather(f32[216,128]{1,0:T(8,128)S(1)} %reshape.304), channel_id=1, replica_groups=mesh['dp'=8,'fsdp'=4] {'dp'}, dimensions={0}, use_global_device_ids=true | all-gather | bytes 995328 | tf_op jit(solution)/shard_map/all_gather | solution.py:1168
  694.1 20.8 %all-gather.20.cloned.1.call-done = bf16[1,1152,1152]{2,1,0:T(8,128)(2,1)} async-done(((bf16[1,144,1152]{2,1,0:T(8,128)(2,1)}), bf16[1,1152,1152]{2,1,0:T(8,128)(2,1)}) %all-gather.20.cloned.1.call-update) | async-done | bytes 2654224 | tf_op jit(solution)/shard_map/all_gather | solution.py:820
  714.9 8.3 %shard_map.215 = bf16[4,3,144,288]{3,2,1,0:T(8,128)(2,1)} custom-call(s32[1]{0:T(128)} %bitcast.127.at, bf16[1152,1152]{1,0:T(8,128)(2,1)} %all-gather.14.cloned.1.call-done.gathered, bf16[144,1152]{1,0:T(8,128)(2,1)S(1)} %get-tuple-element.241.left_root, bf16[1152,1152]{1,0:T(8,128)(2,1)} %bitcast.372), custom_call_target="tpu_custom_call" | custom-call | flops 2293235712 | bytes 7962624 | tf_op jit(solution)/shard_map/pallas_call | solution.py:908
  734.2 11.0 %all-to-all-done.5 = bf16[4,3,144,288]{3,2,1,0:T(8,128)(2,1)} async-done(((bf16[4,3,144,288]{3,2,1,0:T(8,128)(2,1)}), bf16[4,3,144,288]{3,2,1,0:T(8,128)(2,1)}, u32[]{:S(2)}, u32[]{:S(2)}) %all-to-all-start.5) | async-done | bytes 995360 | tf_op jit(solution)/shard_map/all_to_all | solution.py:731
  747.7 7.2 fusion.125
  (413 shorter events, 256.9 us)
Async XLA Ops:
  60.5 49.7 %collective-permute-start.10 = (bf16[576,1152]{1,0:T(8,128)(2,1)S(1)}, bf16[576,1152]{1,0:T(8,128)(2,1)}, u32[]{:S(2)}, u32[]{:S(2)}) collective-permute-start(bf16[576,1152]{1,0:T(8,128)(2,1)S(1)} %shard_map.204.refs_0_), channel_id=1, source_target_pairs={{0,2},{1,3},{2,0},{3,1},{4,6},{5,7},{6,4},{7,5},{8,10},{9,11},{10,... | collective-permute-start | bytes 3981320 | tf_op jit(solution)/shard_map/ppermute | solution.py:659
  62.1 48.1 %collective-permute-start.9 = (bf16[576,1152]{1,0:T(8,128)(2,1)S(1)}, bf16[576,1152]{1,0:T(8,128)(2,1)}, u32[]{:S(2)}, u32[]{:S(2)}) collective-permute-start(bf16[576,1152]{1,0:T(8,128)(2,1)S(1)} %shard_map.204.refs_0_), channel_id=1, source_target_pairs={{0,1},{1,0},{2,3},{3,2},{4,5},{5,4},{6,7},{7,6},{8,9},{9,8},{10,11... | collective-permute-start | bytes 3981320 | tf_op jit(solution)/shard_map/ppermute | solution.py:659
  72.2 200.2 %all-gather.8.cloned.1.call-start = ((), (), s32[]{:S(2)}) async-start(), calls=%async_computation.6 | async-start | bytes 10948608 | tf_op jit(solution)/shard_map/all_gather | solution.py:740
  106.6 30.8 %collective-permute-start.14 = (bf16[576,1152]{1,0:T(8,128)(2,1)S(1)}, bf16[576,1152]{1,0:T(8,128)(2,1)}, u32[]{:S(2)}, u32[]{:S(2)}) collective-permute-start(bf16[576,1152]{1,0:T(8,128)(2,1)S(1)} %shard_map.205.refs_0_), channel_id=1, source_target_pairs={{0,4},{4,0},{8,12},{12,8},{16,20},{20,16},{24,28},{28,24},{1,5},{5... | collective-permute-start | bytes 3981320 | tf_op jit(solution)/shard_map/ppermute | solution.py:649
  141.1 469.2 %all-gather.12.cloned.1.call-start = ((), (), s32[]{:S(2)}) async-start(), calls=%async_computation.8 | async-start | bytes 2985984 | tf_op jit(solution)/shard_map/all_gather | solution.py:820
  150.3 46.8 %collective-permute-start.22 = (bf16[576,1152]{1,0:T(8,128)(2,1)S(1)}, bf16[576,1152]{1,0:T(8,128)(2,1)}, u32[]{:S(2)}, u32[]{:S(2)}) collective-permute-start(bf16[576,1152]{1,0:T(8,128)(2,1)S(1)} %constant_dynamic-slice_fusion.4), channel_id=1, source_target_pairs={{0,1},{1,0},{2,3},{3,2},{4,5},{5,4},{6,7},{7,6},{8,9},{9,8},{10,11... | collective-permute-start | bytes 3981320 | tf_op jit(solution)/shard_map/ppermute | solution.py:659
  152.7 44.5 %collective-permute-start.23 = (bf16[576,1152]{1,0:T(8,128)(2,1)S(1)}, bf16[576,1152]{1,0:T(8,128)(2,1)}, u32[]{:S(2)}, u32[]{:S(2)}) collective-permute-start(bf16[576,1152]{1,0:T(8,128)(2,1)S(1)} %constant_dynamic-slice_fusion.4), channel_id=1, source_target_pairs={{0,2},{1,3},{2,0},{3,1},{4,6},{5,7},{6,4},{7,5},{8,10},{9,11},{10,... | collective-permute-start | bytes 3981320 | tf_op jit(solution)/shard_map/ppermute | solution.py:659
  153.6 81.0 %collective-permute-start.24 = (bf16[576,1152]{1,0:T(8,128)(2,1)S(1)}, bf16[576,1152]{1,0:T(8,128)(2,1)}, u32[]{:S(2)}, u32[]{:S(2)}) collective-permute-start(bf16[576,1152]{1,0:T(8,128)(2,1)S(1)} %constant_dynamic-slice_fusion.4), channel_id=1, source_target_pairs={{0,3},{1,2},{2,1},{3,0},{4,7},{5,6},{6,5},{7,4},{8,11},{9,10},{10,... | collective-permute-start | bytes 3981320 | tf_op jit(solution)/shard_map/ppermute | solution.py:659
  265.3 36.3 %collective-permute-start.28 = (bf16[4,576,1152]{2,1,0:T(8,128)(2,1)}, bf16[4,576,1152]{2,1,0:T(8,128)(2,1)}, u32[]{:S(2)}, u32[]{:S(2)}) collective-permute-start(bf16[4,576,1152]{2,1,0:T(8,128)(2,1)} %convolution_convert_fusion.1), channel_id=1, source_target_pairs={{0,4},{4,0},{8,12},{12,8},{16,20},{20,16},{24,28},{28,24},{1,5},{5... | collective-permute-start | bytes 15925256 | tf_op jit(solution)/shard_map/ppermute | solution.py:649
  269.6 32.0 %collective-permute-start.30 = (bf16[6,144,288]{2,1,0:T(8,128)(2,1)}, bf16[6,144,288]{2,1,0:T(8,128)(2,1)}, u32[]{:S(2)}, u32[]{:S(2)}) collective-permute-start(bf16[6,144,288]{2,1,0:T(8,128)(2,1)} %get-tuple-element.237), channel_id=1, source_target_pairs={{0,2},{1,3},{2,0},{3,1},{4,6},{5,7},{6,4},{7,5},{8,10},{9,11},{10,... | collective-permute-start | bytes 1493000 | tf_op jit(solution)/shard_map/ppermute | solution.py:659
  319.5 33.0 %collective-permute-start.32 = (bf16[4,576,1152]{2,1,0:T(8,128)(2,1)}, bf16[4,576,1152]{2,1,0:T(8,128)(2,1)}, u32[]{:S(2)}, u32[]{:S(2)}) collective-permute-start(bf16[4,576,1152]{2,1,0:T(8,128)(2,1)} %fusion.1), channel_id=1, source_target_pairs={{0,4},{4,0},{8,12},{12,8},{16,20},{20,16},{24,28},{28,24},{1,5},{5... | collective-permute-start | bytes 15925256 | tf_op jit(solution)/shard_map/ppermute | solution.py:649
  319.5 31.9 %collective-permute-start.33 = (bf16[2,2,144,1152]{3,2,1,0:T(8,128)(2,1)}, bf16[2,2,144,1152]{3,2,1,0:T(8,128)(2,1)}, u32[]{:S(2)}, u32[]{:S(2)}) collective-permute-start(bf16[2,2,144,1152]{3,2,1,0:T(8,128)(2,1)} %dynamic-slice_bitcast_fusion.5), channel_id=1, source_target_pairs={{0,1},{1,0},{2,3},{3,2},{4,5},{5,4},{6,7},{7,6},{8,9},{9,8},{10,11... | collective-permute-start | bytes 3981320 | tf_op jit(solution)/shard_map/ppermute | solution.py:659
  321.0 31.6 %collective-permute-start.34 = (bf16[2,2,144,1152]{3,2,1,0:T(8,128)(2,1)}, bf16[2,2,144,1152]{3,2,1,0:T(8,128)(2,1)}, u32[]{:S(2)}, u32[]{:S(2)}) collective-permute-start(bf16[2,2,144,1152]{3,2,1,0:T(8,128)(2,1)} %dynamic-slice_bitcast_fusion.4), channel_id=1, source_target_pairs={{0,2},{1,3},{2,0},{3,1},{4,6},{5,7},{6,4},{7,5},{8,10},{9,11},{10,... | collective-permute-start | bytes 3981320 | tf_op jit(solution)/shard_map/ppermute | solution.py:659
  356.3 42.4 %collective-permute-start.36 = (bf16[2,144,1152]{2,1,0:T(8,128)(2,1)}, bf16[2,144,1152]{2,1,0:T(8,128)(2,1)}, u32[]{:S(2)}, u32[]{:S(2)}) collective-permute-start(bf16[2,144,1152]{2,1,0:T(8,128)(2,1)} %dynamic-slice_bitcast_fusion.10), channel_id=1, source_target_pairs={{0,1},{1,0},{2,3},{3,2},{4,5},{5,4},{6,7},{7,6},{8,9},{9,8},{10,11... | collective-permute-start | bytes 1990664 | tf_op jit(solution)/shard_map/ppermute | solution.py:659
  359.5 39.2 %collective-permute-start.35 = (bf16[2,144,1152]{2,1,0:T(8,128)(2,1)}, bf16[2,144,1152]{2,1,0:T(8,128)(2,1)}, u32[]{:S(2)}, u32[]{:S(2)}) collective-permute-start(bf16[2,144,1152]{2,1,0:T(8,128)(2,1)} %dynamic-slice_bitcast_fusion.11), channel_id=1, source_target_pairs={{0,2},{1,3},{2,0},{3,1},{4,6},{5,7},{6,4},{7,5},{8,10},{9,11},{10,... | collective-permute-start | bytes 1990664 | tf_op jit(solution)/shard_map/ppermute | solution.py:659
  406.1 49.5 %collective-permute-start.37 = (bf16[4,576,1152]{2,1,0:T(8,128)(2,1)}, bf16[4,576,1152]{2,1,0:T(8,128)(2,1)}, u32[]{:S(2)}, u32[]{:S(2)}) collective-permute-start(bf16[4,576,1152]{2,1,0:T(8,128)(2,1)} %convolution_convert_fusion), channel_id=1, source_target_pairs={{0,4},{4,0},{8,12},{12,8},{16,20},{20,16},{24,28},{28,24},{1,5},{5... | collective-permute-start | bytes 15925256 | tf_op jit(solution)/shard_map/ppermute | solution.py:649
  415.2 31.9 %collective-permute-start.38 = (bf16[2,2,144,1152]{3,2,1,0:T(8,128)(2,1)}, bf16[2,2,144,1152]{3,2,1,0:T(8,128)(2,1)}, u32[]{:S(2)}, u32[]{:S(2)}) collective-permute-start(bf16[2,2,144,1152]{3,2,1,0:T(8,128)(2,1)} %dynamic-slice_bitcast_fusion.3), channel_id=1, source_target_pairs={{0,1},{1,0},{2,3},{3,2},{4,5},{5,4},{6,7},{7,6},{8,9},{9,8},{10,11... | collective-permute-start | bytes 3981320 | tf_op jit(solution)/shard_map/ppermute | solution.py:659
  415.6 40.0 %collective-permute-start.39 = (bf16[2,2,144,1152]{3,2,1,0:T(8,128)(2,1)}, bf16[2,2,144,1152]{3,2,1,0:T(8,128)(2,1)}, u32[]{:S(2)}, u32[]{:S(2)}) collective-permute-start(bf16[2,2,144,1152]{3,2,1,0:T(8,128)(2,1)} %dynamic-slice_bitcast_fusion.2), channel_id=1, source_target_pairs={{0,2},{1,3},{2,0},{3,1},{4,6},{5,7},{6,4},{7,5},{8,10},{9,11},{10,... | collective-permute-start | bytes 3981320 | tf_op jit(solution)/shard_map/ppermute | solution.py:659
  419.5 190.8 %all-gather.10.cloned.1.call-start = ((), (), s32[]{:S(2)}) async-start(), calls=%async_computation.7 | async-start | bytes 2985984 | tf_op jit(solution)/shard_map/all_gather | solution.py:861
  423.9 61.2 %collective-permute-start.42 = (bf16[144,1152]{1,0:T(8,128)(2,1)}, bf16[144,1152]{1,0:T(8,128)(2,1)}, u32[]{:S(2)}, u32[]{:S(2)}) collective-permute-start(bf16[144,1152]{1,0:T(8,128)(2,1)} %get-tuple-element.266), channel_id=1, source_target_pairs={{0,8},{4,12},{8,16},{12,20},{16,24},{20,28},{24,0},{28,4},{1,9},{5... | collective-permute-start | bytes 995336 | tf_op jit(solution)/shard_map/ppermute | solution.py:654
  433.2 51.9 %collective-permute-start.43 = (bf16[144,1152]{1,0:T(8,128)(2,1)}, bf16[144,1152]{1,0:T(8,128)(2,1)}, u32[]{:S(2)}, u32[]{:S(2)}) collective-permute-start(bf16[144,1152]{1,0:T(8,128)(2,1)} %get-tuple-element.267), channel_id=1, source_target_pairs={{0,16},{4,20},{8,24},{12,28},{16,0},{20,4},{24,8},{28,12},{1,17},{... | collective-permute-start | bytes 995336 | tf_op jit(solution)/shard_map/ppermute | solution.py:654
  447.1 38.0 %collective-permute-start.44 = (bf16[144,1152]{1,0:T(8,128)(2,1)}, bf16[144,1152]{1,0:T(8,128)(2,1)}, u32[]{:S(2)}, u32[]{:S(2)}) collective-permute-start(bf16[144,1152]{1,0:T(8,128)(2,1)} %get-tuple-element.265), channel_id=1, source_target_pairs={{0,24},{4,28},{8,0},{12,4},{16,8},{20,12},{24,16},{28,20},{1,25},{... | collective-permute-start | bytes 995336 | tf_op jit(solution)/shard_map/ppermute | solution.py:654
  487.3 157.7 %all-gather.18.cloned.1.call-start = ((), (), s32[]{:S(2)}) async-start(), calls=%async_computation.11 | async-start | bytes 2985984 | tf_op jit(solution)/shard_map/all_gather | solution.py:820
  527.5 117.5 %all-gather.16.cloned.1.call-start = ((), (), s32[]{:S(2)}) async-start(), calls=%async_computation.10 | async-start | bytes 2985984 | tf_op jit(solution)/shard_map/all_gather | solution.py:861
  528.8 54.4 %collective-permute-start.49 = (bf16[144,1152]{1,0:T(8,128)(2,1)}, bf16[144,1152]{1,0:T(8,128)(2,1)}, u32[]{:S(2)}, u32[]{:S(2)}) collective-permute-start(bf16[144,1152]{1,0:T(8,128)(2,1)} %get-tuple-element.263), channel_id=1, source_target_pairs={{0,8},{4,12},{8,16},{12,20},{16,24},{20,28},{24,0},{28,4},{1,9},{5... | collective-permute-start | bytes 995336 | tf_op jit(solution)/shard_map/ppermute | solution.py:654
  530.4 52.9 %collective-permute-start.50 = (bf16[144,1152]{1,0:T(8,128)(2,1)}, bf16[144,1152]{1,0:T(8,128)(2,1)}, u32[]{:S(2)}, u32[]{:S(2)}) collective-permute-start(bf16[144,1152]{1,0:T(8,128)(2,1)} %get-tuple-element.264), channel_id=1, source_target_pairs={{0,16},{4,20},{8,24},{12,28},{16,0},{20,4},{24,8},{28,12},{1,17},{... | collective-permute-start | bytes 995336 | tf_op jit(solution)/shard_map/ppermute | solution.py:654
  531.1 52.2 %collective-permute-start.51 = (bf16[144,1152]{1,0:T(8,128)(2,1)S(1)}, bf16[144,1152]{1,0:T(8,128)(2,1)}, u32[]{:S(2)}, u32[]{:S(2)}) collective-permute-start(bf16[144,1152]{1,0:T(8,128)(2,1)S(1)} %get-tuple-element.262), channel_id=1, source_target_pairs={{0,24},{4,28},{8,0},{12,4},{16,8},{20,12},{24,16},{28,20},{1,25},{... | collective-permute-start | bytes 995336 | tf_op jit(solution)/shard_map/ppermute | solution.py:654
  585.5 108.6 %all-gather.14.cloned.1.call-start = ((), (), s32[]{:S(2)}) async-start(), calls=%async_computation.9 | async-start | bytes 2985984 | tf_op jit(solution)/shard_map/all_gather | solution.py:861
  590.0 42.1 %collective-permute-start.53 = (bf16[144,1152]{1,0:T(8,128)(2,1)}, bf16[144,1152]{1,0:T(8,128)(2,1)}, u32[]{:S(2)}, u32[]{:S(2)}) collective-permute-start(bf16[144,1152]{1,0:T(8,128)(2,1)} %get-tuple-element.261), channel_id=1, source_target_pairs={{0,16},{4,20},{8,24},{12,28},{16,0},{20,4},{24,8},{28,12},{1,17},{... | collective-permute-start | bytes 995336 | tf_op jit(solution)/shard_map/ppermute | solution.py:654
  592.0 40.1 %collective-permute-start.54 = (bf16[144,1152]{1,0:T(8,128)(2,1)}, bf16[144,1152]{1,0:T(8,128)(2,1)}, u32[]{:S(2)}, u32[]{:S(2)}) collective-permute-start(bf16[144,1152]{1,0:T(8,128)(2,1)} %get-tuple-element.259), channel_id=1, source_target_pairs={{0,24},{4,28},{8,0},{12,4},{16,8},{20,12},{24,16},{28,20},{1,25},{... | collective-permute-start | bytes 995336 | tf_op jit(solution)/shard_map/ppermute | solution.py:654
  634.3 80.6 %all-gather.20.cloned.1.call-start = ((), (), s32[]{:S(2)}) async-start(), calls=%async_computation.12 | async-start | bytes 2985984 | tf_op jit(solution)/shard_map/all_gather | solution.py:820
  653.3 40.8 %all-to-all-start.3 = ((bf16[4,3,144,288]{3,2,1,0:T(8,128)(2,1)}), bf16[4,3,144,288]{3,2,1,0:T(8,128)(2,1)}, u32[]{:S(2)}, u32[]{:S(2)}) async-start(bf16[4,3,144,288]{3,2,1,0:T(8,128)(2,1)} %shard_map.214), calls=%async_computation.3 | async-start | bytes 2654208 | tf_op jit(solution)/shard_map/all_to_all | solution.py:731
  (97 other events, 1248.4 us)
Sparse Core Ops, SparseCore 0:
  141.2 119.6 all-gather.7
  419.6 62.0 all-gather.11
  487.4 32.8 all-gather.9
  521.8 58.0 all-gather.17
  585.6 56.7 all-gather.15
  644.5 33.8 all-gather.13
  680.0 34.8 all-gather.19

commit v9 on v8

--- a/solution.py
+++ b/solution.py
@@ -121,30 +121,37 @@
 
 def attention_kernel(
     frames,
-    cuts,
     counts,
-    starts,
     tokens,
     cotangent,
     mods,
     bias,
-    *refs,
+    blocks,
+    attn_in,
+    parts,
+    mixed_low,
+    proj_out,
+    resid_out,
+    mlp_in,
+    d_branch,
+    d_branch_sum,
+    mixed,
+    whole,
+    semaphores,
 ):
-    whole_out, attn_in, parts, mixed_low, proj_out, resid_out, mlp_in, d_branch, d_branch_sum = refs[
-        -13:-4
+    rows, width = tokens.shape
+    clip = pl.program_id(0)
+    loads = [
+        pltpu.make_async_copy(blocks.at[at], whole.at[at], semaphores.at[at]) for at in range(4)
     ]
-    mixed, whole, semaphores, store_semaphore = refs[-4:]
-    pieces = refs[:-13]
-    rows, width = tokens.shape
-    clip, clips = pl.program_id(0), pl.num_programs(0)
-    blocks = [whole.at[pl.ds(index * width, width)] for index in range(4)]
-    store = pltpu.make_async_copy(whole, whole_out, store_semaphore)
 
     @pl.when(clip == 0)
     def _():
-        start_loads(cuts, starts, pieces, whole, semaphores)
+        for load in loads:
+            load.start()
+
     tile = min(rows, 128)
-    count = counts[pl.program_id(0)]
+    count = counts[clip]
     shift_one, scale_one, gate_one = (mods[0, at : at + 1, :] for at in range(3))
     shift_two, scale_two, gate_two = (mods[0, at : at + 1, :] for at in range(3, 6))
     for first in range(0, rows, tile):
@@ -158,20 +165,17 @@
 
     @pl.when(clip == 0)
     def _():
-        for index, (part, first, size) in enumerate(cuts):
-            span = pl.ds(pl.multiple_of(starts[index] * 16, 16), size)
-            source = pieces[part].at[pl.ds(first, size)]
-            pltpu.make_async_copy(source, whole.at[span], semaphores.at[index]).wait()
-        store.start()
+        for load in loads:
+            load.wait()
 
     scale = (width // HEADS) ** -0.5
     source = attn_in[...]
     for low, high in column_cuts(width):
         span = slice(low, high)
-        query = (dot_nn(source, blocks[0][:, span]) + bias[0:1, span]) * scale
+        query = (dot_nn(source, whole[0, :, span]) + bias[0:1, span]) * scale
         parts[0, :, span], parts[1, :, span] = split_high(query)
-        parts[2, :, span], parts[3, :, span] = split_high(dot_nn(source, blocks[1][:, span]))
-        parts[4, :, span] = narrow(dot_nn(source, blocks[2][:, span]) + bias[2:3, span])
+        parts[2, :, span], parts[3, :, span] = split_high(dot_nn(source, whole[1, :, span]))
+        parts[4, :, span] = narrow(dot_nn(source, whole[2, :, span]) + bias[2:3, span])
     offset = score_offset(count, tile, frames, 1)
     mixed[...] = jnp.zeros_like(mixed)
     for first in range(0, rows, tile):
@@ -192,7 +196,7 @@
     source = mixed_low[...]
     for low, high in column_cuts(width):
         span = slice(low, high)
-        proj_out[:, span] = dot_nn(source, blocks[3][:, span]) + bias[3:4, span]
+        proj_out[:, span] = dot_nn(source, whole[3, :, span]) + bias[3:4, span]
     for first in range(0, rows, tile):
         span = slice(first, first + tile)
         resid = wide(tokens[span]) + valid_rows(count, tile, frames) * gate_one * proj_out[span]
@@ -200,13 +204,8 @@
         normed, _ = norm_parts(resid)
         mlp_in[span] = narrow(normed * (1.0 + scale_two) + shift_two)
 
-    @pl.when(clip == clips - 1)
-    def _():
-        store.wait()
-
-
-def run_attention(frames, counts, tokens, cotangent, mods, bias, gathered):
-    pieces, cuts, starts = gathered
+
+def run_attention(frames, counts, tokens, cotangent, mods, bias, blocks):
     total, width = tokens.shape
     clips = mods.shape[0]
     rows = total // clips
@@ -214,19 +213,17 @@
     low = jax.ShapeDtypeStruct((total, width), jnp.bfloat16)
     full = jax.ShapeDtypeStruct((total, width), jnp.float32)
     return pl.pallas_call(
-        functools.partial(attention_kernel, frames, cuts),
+        functools.partial(attention_kernel, frames),
         grid=(clips,),
         in_specs=[
-            pl.BlockSpec(memory_space=pltpu.SMEM),
             pl.BlockSpec(memory_space=pltpu.SMEM),
             clip_rows,
             clip_rows,
             spec((1,) + mods.shape[1:], lambda clip: (clip, 0, 0)),
             held(bias.shape),
-        ]
-        + [pl.BlockSpec(memory_space=pl.ANY)] * len(pieces),
+            pl.BlockSpec(memory_space=pl.ANY),
+        ],
         out_specs=[
-            pl.BlockSpec(memory_space=pl.ANY),
             clip_rows,
             spec((5, rows, width), lambda clip: (0, clip, 0)),
             clip_rows,
@@ -237,7 +234,6 @@
             spec((1, 1, width), lambda clip: (clip, 0, 0)),
         ],
         out_shape=[
-            jax.ShapeDtypeStruct((4 * width, width), jnp.bfloat16),
             low,
             jax.ShapeDtypeStruct((5, total, width), jnp.bfloat16),
             low,
@@ -249,15 +245,14 @@
         ],
         scratch_shapes=[
             pltpu.VMEM((rows, width), jnp.float32),
-            pltpu.VMEM((4 * width, width), jnp.bfloat16),
-            pltpu.SemaphoreType.DMA((len(cuts),)),
-            pltpu.SemaphoreType.DMA,
+            pltpu.VMEM(blocks.shape, jnp.bfloat16),
+            pltpu.SemaphoreType.DMA((4,)),
         ],
         compiler_params=pltpu.CompilerParams(vmem_limit_bytes=vmem_bytes),
         cost_estimate=pl.CostEstimate(
             flops=16 * total * width * width, bytes_accessed=100 * total * width, transcendentals=0
         ),
-    )(counts, stacked(starts), tokens, cotangent, mods, bias, *pieces)
+    )(counts, tokens, cotangent, mods, bias, blocks)
 
 
 def stacked(numbers):
@@ -654,6 +649,11 @@
     return lax.ppermute(array, "dp", [(at, (at + 2 * step) % count) for at in range(count)])
 
 
+def chip_swap(array, bits):
+    count = lax.axis_size("dp")
+    return lax.ppermute(array, "dp", [(at, at ^ (2 * bits)) for at in range(count)])
+
+
 def rank_swap(array, bits):
     count = lax.axis_size("fsdp")
     return lax.ppermute(array, "fsdp", [(at, at ^ bits) for at in range(count)])
@@ -749,37 +749,6 @@
     found = [rows] + [chip_shift(rows, step) for step in range(1, chips)]
     starts = [(chip - step) % chips * (chunk // 16) for step in range(chips)]
     return place(found, [(step, 0, chunk) for step in range(chips)], starts, chips * chunk)
-
-
-def gather_first(rows, group):
-    ranks, at = lax.axis_size("fsdp"), lax.axis_index("fsdp")
-    total = rows.shape[-1]
-    if ranks != group:
-        blocks = gather_blocks(rows, group).reshape(group * total, total)
-        for _ in range(3):
-            (blocks,) = yield (blocks,)
-        yield [blocks], [(0, 0, group * total)], [0]
-        return
-    chips = lax.axis_size("dp") // 2
-    core = lax.axis_index("dp") % 2
-    chunk = rows.shape[0]
-    (line,) = yield (join_line(rows),)
-    low_in, high_in = yield (rank_swap(line, 1), rank_swap(line, 2))
-    half = total // 4
-    parts = [line, low_in, high_in]
-    parts += [rank_swap(high_in[:half], 1), rank_swap(low_in[half:], 2)]
-    others = [core_swap(part) for part in parts[:3]]
-    parts[3:] = yield tuple(parts[3:])
-    others += [core_swap(part) for part in parts[3:]]
-    cuts, starts = [], []
-    for side, found in ((core, parts), (1 - core, others)):
-        for index, part in enumerate(found):
-            bits, first_chip = ((0, 0), (1, 0), (2, 0), (3, 0), (3, chips // 2))[index]
-            for step in range(part.shape[0] // chunk):
-                cuts.append((len(parts) * (found is others) + index, step * chunk, chunk))
-                row = (at ^ bits) * (2 * chips) + 2 * (first_chip + step) + side
-                starts.append(row * (chunk // 16))
-    yield parts + others, cuts, starts
 
 
 def gather_second(rows, group):
@@ -830,7 +799,7 @@
         rows = lax.psum_scatter(
             blocks.reshape(group * total, -1), ("fsdp", "dp"), scatter_dimension=0, tiled=True
         )
-        for _ in range(6):
+        for _ in range(7):
             (rows,) = yield (rows,)
         yield gather_own(rows[None], group)[0]
         return
@@ -855,10 +824,14 @@
     first = narrow(wide(entry(first, high_bit)) + wide(first_in))
     second = narrow(wide(entry(second, low_bit)) + wide(second_in))
     line = jnp.concatenate([first, second])
-    parts = [chip_shift(entry(line, (chip + step) % chips), step) for step in range(1, chips)]
-    parts = yield tuple(parts)
-    rows = sum([wide(part) for part in parts], wide(entry(line, chip)))
-    yield lax.all_gather(narrow(rows), "dp", axis=0, tiled=True)
+    step = 1
+    while step < chips:
+        bit = chip // step % 2
+        line = line.reshape(-1, 2, *line.shape[1:])
+        (line_in,) = yield (chip_swap(entry(line, 1 - bit, 1), step),)
+        line = narrow(wide(entry(line, bit, 1)) + wide(line_in))
+        step *= 2
+    yield lax.all_gather(line[0], "dp", axis=0, tiled=True)
 
 
 def fast_dot(subscripts, left, right):
@@ -972,9 +945,9 @@
     attn_rows = attn_rows.send(attn_panels)[0]
     other_rows = own_rows(other_shards, group)
     other_panels = next(other_rows)
-    attn_steps = gather_first(attn_rows, group)
-    attn_parts = next(attn_steps)
+    attn_w = gather_blocks(attn_rows, group)
     one_rows, two_rows = other_rows.send(other_panels)
+    two_w = gather_blocks(two_rows, group)
 
     first_parts = first_parts.reshape(dp_count, -1)
     cond_all = first_parts[:, : clip_count * width].reshape(all_clips, width)
@@ -982,8 +955,6 @@
     cond_rows = lax.dynamic_slice_in_dim(cond_all, dp_at * row_part, row_part, 1)
     cond_cols = wide(lax.dynamic_slice_in_dim(cond_all, rank_at * col_part, col_part, 1))
     mod_parts = fast_dot("cr,jre->cje", cond_rows, low_weights[:mod_count])
-    mod_parts, attn_parts = tie(mod_parts, attn_parts)
-    attn_parts = attn_steps.send(attn_parts)
     mod_parts = lax.all_to_all(mod_parts, "dp", 0, 0, tiled=True)
     mod_parts, one_rows = tie(mod_parts, one_rows)
     one_steps = gather_second(one_rows, group)
@@ -991,14 +962,11 @@
     mod_cols = jnp.sum(mod_parts.reshape(dp_count, clip_count, mod_count, col_part), axis=0)
     left_cond = jnp.einsum("jrk,ck->jrc", left_roots[:mod_count], cond_cols, precision=precise)
     mod_size, bias_size = mod_cols.size, dp_count * bias_part
-    second_parts, attn_parts = tie(packed([mod_cols, bias_rows, left_cond], 8), attn_parts)
-    attn_parts = attn_steps.send(attn_parts)
-    second_parts = lax.all_gather(second_parts, "fsdp", axis=0, tiled=True)
-    second_parts, one_parts, attn_parts = tie(second_parts, one_parts, attn_parts)
+    second_parts = lax.all_gather(
+        packed([mod_cols, bias_rows, left_cond], 8), "fsdp", axis=0, tiled=True
+    )
+    second_parts, one_parts = tie(second_parts, one_parts)
     one_parts = one_steps.send(one_parts)
-    gathered = attn_steps.send(attn_parts)
-    attn_parts, two_rows = tie(attn_parts, two_rows)
-    two_w = gather_blocks(two_rows, group)
     second_parts = second_parts.reshape(ranks, -1)
     mods = second_parts[:, :mod_size].reshape(ranks, clip_count, mod_count, col_part)
     mods = mods.transpose(1, 2, 0, 3).reshape(clip_count, mod_count, width)
@@ -1012,14 +980,14 @@
         [bias_all[6:7], jnp.zeros((1, width), jnp.float32), bias_all[7:14]]
     )
 
-    attn_w, attn_in, parts, mixed, proj, resid, mlp_in, d_branch, d_branch_sums = run_attention(
-        frames, frame_counts, stream, grad_out, mods, bias_table, gathered
-    )
-    attn_w = attn_w.reshape(group, width, width)
     roots = jnp.stack([narrow(left_roots[mod_count:]), narrow(right_roots[mod_count:])])
-    mlp_in, one_parts, roots = tie(mlp_in, one_parts, roots)
+    mods, roots = tie(mods, roots)
     root_rows = own_rows(roots.reshape(-1, group, row_part, col_part), group)
     root_panels = next(root_rows)
+    attn_in, parts, mixed, proj, resid, mlp_in, d_branch, d_branch_sums = run_attention(
+        frames, frame_counts, stream, grad_out, mods, bias_table, attn_w
+    )
+    mlp_in, one_parts = tie(mlp_in, one_parts)
     one_w, hidden, slope = run_hidden(mlp_in, one_steps.send(one_parts), bias_table[4:8, None])
     one_w = one_w.reshape(group, width, width)
 
@@ -1030,8 +998,12 @@
         group,
     )
     two_parts = next(two_steps)
-    hidden, two_parts = tie(hidden, two_parts)
+    hidden, two_parts, root_panels = tie(hidden, two_parts, root_panels)
     two_parts = two_steps.send(two_parts)
+    root_rows = root_rows.send(root_panels)
+    hidden, root_rows = tie(hidden, root_rows)
+    left_rows, right_rows = jnp.split(root_rows, 2)
+    right_wholes = [gather_own(rows[None], group)[0] for rows in right_rows]
     d_pre, d_pre_sums, block_out, d_gate_two = run_branch(
         frames,
         frame_counts,
@@ -1044,12 +1016,10 @@
         resid,
         grad_out,
     )
-    d_pre, two_parts, root_panels = tie(d_pre, two_parts, root_panels)
+    d_pre, two_parts = tie(d_pre, two_parts)
     two_parts = two_steps.send(two_parts)
     d_pre, two_parts = tie(d_pre, two_parts)
     two_parts = two_steps.send(two_parts)
-    left_rows, right_rows = jnp.split(root_rows.send(root_panels), 2)
-    right_wholes = [gather_own(rows[None], group)[0] for rows in right_rows]
     one_steps = sum_blocks(
         lambda left: fast_dot("td,jte->jde", left, d_pre),
         lambda first, size: lax.dynamic_slice_in_dim(mlp_in, first, size, 1),
@@ -1081,7 +1051,8 @@
     attn_parts = next(attn_steps)
     d_heads, attn_parts = tie(d_heads, attn_parts)
     attn_parts = attn_steps.send(attn_parts)
-    d_heads, attn_parts, one_parts = tie(d_heads, attn_parts, one_parts)
+    d_heads, attn_parts, one_parts, two_parts = tie(d_heads, attn_parts, one_parts, two_parts)
+    two_parts = two_steps.send(two_parts)
     one_parts = one_steps.send(one_parts)
     attn_parts = attn_steps.send(attn_parts)
     d_heads, attn_parts = tie(d_heads, attn_parts)
@@ -1090,8 +1061,9 @@
     input_sums, one_parts, two_parts = tie(input_sums, one_parts, two_parts)
     whole_two = two_steps.send(two_parts)
     one_parts = one_steps.send(one_parts)
-    input_sums, attn_parts = tie(input_sums, attn_parts)
+    input_sums, attn_parts, one_parts = tie(input_sums, attn_parts, one_parts)
     attn_parts = attn_steps.send(attn_parts)
+    one_parts = one_steps.send(one_parts)
 
     d_mods = jnp.stack(
         [
@@ -1127,8 +1099,9 @@
         axis=1,
     )
     rank_sums = jnp.sum(lax.all_to_all(to_ranks, "fsdp", 0, 0, tiled=True), axis=0)
-    rank_sums, attn_parts = tie(rank_sums, attn_parts)
+    rank_sums, attn_parts, one_parts = tie(rank_sums, attn_parts, one_parts)
     attn_parts = attn_steps.send(attn_parts)
+    whole_one = one_steps.send(one_parts)
     to_rows = jnp.concatenate(
         [
             jnp.broadcast_to(rank_sums[None, :mod_size], (dp_count, mod_size)),
@@ -1137,8 +1110,8 @@
         axis=1,
     )
     from_rows = lax.all_to_all(to_rows, "dp", 0, 0, tiled=True)
-    from_rows, one_parts = tie(from_rows, one_parts)
-    whole_one = one_steps.send(one_parts)
+    from_rows, attn_parts = tie(from_rows, attn_parts)
+    attn_parts = attn_steps.send(attn_parts)
     bias_grad = jnp.sum(from_rows[:, mod_size:], axis=0)
     mod_grad_cols = from_rows[:, :mod_size].reshape(all_clips, mod_count, col_part)
     mod_grad = lax.all_gather(packed([mod_grad_cols], 8), "fsdp", axis=0, tiled=True)

time: 778 us -> 761 us (0.978)
  waiting for transfers between devices: 189 us -> 238 us
  blocking collectives: 121 us -> 75.3 us
  starting transfers between devices: 96.8 us -> 72 us
  other arithmetic: 59.6 us -> 67.7 us
    ppermute x0 -> x6, waiting for transfers between devices: none -> 37 us  [chip_swap(): lax.ppermute(array, 'dp', [(at, at ^ 2 * bits) for at in range(count)])]
    ppermute x15 -> x3, starting transfers between devices: 34.5 us -> 4.02 us  [chip_shift(): lax.ppermute(array, 'dp', [(at, (at + 2 * step) % count) for at in range(...]
    all_to_all x1 -> x2, blocking collectives: 44.9 us -> 20.4 us  [the longest x1 13 us: per_device(): mod_parts = lax.all_to_all(mod_parts, 'dp', 0, 0, tiled=True)]
    ppermute x0 -> x6, starting transfers between devices: none -> 20.6 us  [chip_swap(): lax.ppermute(array, 'dp', [(at, at ^ 2 * bits) for at in range(count)])]
    all_gather x1, blocking collectives: 31 us -> 16.9 us  [per_device(): lax.all_gather(packed([right_parts], 8), 'dp', axis=0, tiled=True)]
    ppermute x28 -> x24, waiting for transfers between devices: 97.4 us -> 108 us  [rank_swap(): return lax.ppermute(array, 'fsdp', [(at, at ^ bits) for at in range(count)])]
    convert_element_type x18 -> x22, other arithmetic: 26 us -> 36.5 us  [narrow(): return array.astype(jnp.bfloat16)]
    ppermute x15 -> x3, waiting for transfers between devices: 40.9 us -> 31.3 us  [chip_shift(): lax.ppermute(array, 'dp', [(at, (at + 2 * step) % count) for at in range(...]
  transfers between devices with their start and end apart: 67 -> 52, of which waited for: 19 -> 26; matrix products, arithmetic and copies ran while one was open for 17% -> 16% of each run, Pallas kernels for 20% -> 20%
where the time goes in v9:
time: 761 us; the launch traced here: 754 us
  waiting for transfers between devices  238 us (31%)
  Pallas kernels  158 us (21%)
  blocking collectives  75.3 us (10%)
  starting transfers between devices  72 us (9%)
  local copies, waits for them, and re-layouts  70.2 us (9%)
  other arithmetic  67.7 us (9%)
  matrix products  56.5 us (7%)
  between operations  16 us (2%)
    ppermute x24, waiting for transfers between devices, rank_swap(): return lax.ppermute(array, 'fsdp', [(at, at ^ bits) for at in range(count)])  108 us
    dot_general x7, matrix products, fast_dot(): jnp.einsum(subscripts, left, right, preferred_element_type=jnp.float32)  44.6 us
    pallas_call x1, Pallas kernels, run_attention(): pl.pallas_call(functools.partial(attention_kernel, frames), grid=(clips,)...  40.6 us
    ppermute x6, waiting for transfers between devices, chip_swap(): lax.ppermute(array, 'dp', [(at, at ^ 2 * bits) for at in range(count)])  37 us
    convert_element_type x22, other arithmetic, narrow(): return array.astype(jnp.bfloat16)  36.5 us
    ppermute x3, waiting for transfers between devices, chip_shift(): lax.ppermute(array, 'dp', [(at, (at + 2 * step) % count) for at in range(...  31.3 us
    ppermute x24, starting transfers between devices, rank_swap(): return lax.ppermute(array, 'fsdp', [(at, at ^ bits) for at in range(count)])  27 us
    pallas_call x1, Pallas kernels, run_attention_back(): pl.pallas_call(functools.partial(attention_back_kernel, frames), grid=(cl...  26.2 us
  transfers between devices with their start and end apart: 52, of which 26 were waited for; matrix products, arithmetic and copies ran while one was open for 16% of the time, Pallas kernels for 20%

profile of v9, /device:TPU:0, one launch (start us, length us, event | category | flops | bytes accessed | tf_op | source)
XLA Modules:
  0.0 753.8 jit_solution(15523347014568772182)
XLA Ops:
  14.5 14.7 %all_gather.36 = bf16[256,128]{1,0:T(8,128)(2,1)S(1)} all-gather(bf16[32,128]{1,0:T(8,128)(2,1)S(1)} %fusion.88), channel_id=1, replica_groups=mesh['dp'=8,'fsdp'=4] {'dp'}, dimensions={0}, use_global_device_ids=true | all-gather | bytes 73728 | tf_op jit(solution)/shard_map/all_gather | solution.py:943
  53.1 13.0 %all_to_all.41 = f32[16,6,288]{2,1,0:T(8,128)S(1)} all-to-all(f32[16,6,288]{2,1,0:T(8,128)S(1)} %copy.103), channel_id=1, replica_groups=mesh['dp'=8,'fsdp'=4] {'dp'}, dimensions={0} | all-to-all | bytes 221184 | tf_op jit(solution)/shard_map/all_to_all | solution.py:958
  70.2 15.4 %collective-permute-done.6.refs_1_ = bf16[144,1152]{1,0:T(8,128)(2,1)S(1)} collective-permute-done((bf16[144,1152]{1,0:T(8,128)(2,1)S(1)}, bf16[144,1152]{1,0:T(8,128)(2,1)S(1)}, u32[]{:S(2)}, u32[]{:S(2)}) %collective-permute-start.6) | collective-permute-done | bytes 331808 | tf_op jit(solution)/shard_map/ppermute | solution.py:649
  85.7 15.8 %collective-permute-done.7.refs_2_ = bf16[144,1152]{1,0:T(8,128)(2,1)S(1)} collective-permute-done((bf16[144,1152]{1,0:T(8,128)(2,1)S(1)}, bf16[144,1152]{1,0:T(8,128)(2,1)S(1)}, u32[]{:S(2)}, u32[]{:S(2)}) %collective-permute-start.7) | collective-permute-done | bytes 331808 | tf_op jit(solution)/shard_map/ppermute | solution.py:649
  111.8 13.5 %all_gather.37 = f32[672,128]{1,0:T(8,128)S(1)} all-gather(f32[168,128]{1,0:T(8,128)S(1)} %pad_bitcast_fusion), channel_id=1, replica_groups=mesh['dp'=8,'fsdp'=4] {'fsdp'}, dimensions={0}, use_global_device_ids=true | all-gather | bytes 430080 | tf_op jit(solution)/shard_map/all_gather | solution.py:965
  139.5 40.6 %shard_map.206 = (bf16[512,1152]{1,0:T(8,128)(2,1)S(1)}, bf16[5,512,1152]{2,1,0:T(8,128)(2,1)}, bf16[512,1152]{1,0:T(8,128)(2,1)S(1)}, f32[512,1152]{1,0:T(8,128...) custom-call(s32[2]{0:T(128)S(1)} %copy-done.11, ...), custom_call_target="tpu_custom_call" | custom-call | flops 10871635968 | bytes 58982400 | tf_op jit(solution)/shard_map/pallas_call | solution.py:215
  181.3 22.1 %collective-permute-done.12.refs_5_ = bf16[576,1152]{1,0:T(8,128)(2,1)} collective-permute-done((bf16[576,1152]{1,0:T(8,128)(2,1)}, bf16[576,1152]{1,0:T(8,128)(2,1)}, u32[]{:S(2)}, u32[]{:S(2)}) %collective-permute-start.12) | collective-permute-done | bytes 1327136 | tf_op jit(solution)/shard_map/ppermute | solution.py:659
  213.9 14.2 %shard_map.207 = (bf16[4608,1152]{1,0:T(8,128)(2,1)}, bf16[4,512,1152]{2,1,0:T(8,128)(2,1)}, bf16[4,512,1152]{2,1,0:T(8,128)(2,1)}) custom-call(s32[4]{0:T(128)S(1)} %pad_add_fusion.order, s32[7]{0:T(128)S(1)} %stack.128.starts, bf16[512,1152]{1,0:T(8,128)(2,1)S(1)} %copy-done.15, f32[4,1,1152]{2,1,0:T(1,128)S(1)} %copy.115.bias, ...), custom_call_target="tpu_custom_call" | custom-call | flops 5435817984 | bytes 29491200 | tf_op jit(solution)/shard_map/pallas_call | solution.py:318
  228.2 7.9 %convolution_convert_fusion.1 = bf16[4,576,1152]{2,1,0:T(8,128)(2,1)} fusion(bf16[4,512,1152]{2,1,0:T(8,128)(2,1)} %get-tuple-element.130.hidden, s32[]{:T(128)S(6)} %select_n.438, bf16[512,1152]{1,0:T(8,128)(2,1)S(1)} %copy-done.12), kind=kOutput, calls=%fused_computation.5 | convolution fusion | flops 2720563200 | bytes 9109508 | tf_op jit(solution)/shard_map/jtd,te->jde/dot_general | solution.py:838
  239.8 16.3 %collective-permute-done.18 = bf16[6,144,288]{2,1,0:T(8,128)(2,1)} collective-permute-done((bf16[6,144,288]{2,1,0:T(8,128)(2,1)S(1)}, bf16[6,144,288]{2,1,0:T(8,128)(2,1)}, u32[]{:S(2)}, u32[]{:S(2)}) %collective-permute-start.18) | collective-permute-done | bytes 497696 | tf_op jit(solution)/shard_map/ppermute | solution.py:659
  265.8 10.1 %fusion.10 = f32[4,576,1152]{2,1,0:T(8,128)} fusion(bf16[4,512,1152]{2,1,0:T(8,128)(2,1)} %get-tuple-element.130.hidden, s32[]{:T(128)S(6)} %select_n.437, bf16[512,1152]{1,0:T(8,128)(2,1)} %get-tuple-element.123.d_branch), kind=kOutput, calls=%fused_computation.29 | convolution fusion | flops 2717908992 | bytes 14417924 | tf_op jit(solution)/shard_map/jtd,te->jde/dot_general | solution.py:838
  278.5 20.7 %shard_map.208 = (bf16[4,512,1152]{2,1,0:T(8,128)(2,1)}, f32[4,1,1152]{2,1,0:T(1,128)S(1)}, bf16[512,1152]{1,0:T(8,128)(2,1)}, f32[2,1,1152]{2,1,0:T(1,128)S(1)}) custom-call(s32[2]{0:T(128)S(1)} %copy-done.11, bf16[4,512,1152]{2,1,0:T(8,128)(2,1)} %get-tuple-element.130.hidden, bf16[4,512,1152]{2,1,0:T(8,128)(2,1)} %get-tuple-element.131.slope, ...), custom_call_target="tpu_custom_call" | custom-call | flops 10871635968 | bytes 23592960 | tf_op jit(solution)/shard_map/pallas_call | solution.py:392
  300.4 8.9 %add_convert_fusion.1 = bf16[4,576,1152]{2,1,0:T(8,128)(2,1)} fusion(f32[4,576,1152]{2,1,0:T(8,128)} %fusion.10, bf16[4,576,1152]{2,1,0:T(8,128)(2,1)} %collective-permute-done.19), kind=kLoop, calls=%fused_computation.3 | loop fusion | flops 7962624 | bytes 21233664 | tf_op jit(solution)/shard_map/convert_element_type | solution.py:26
  328.6 15.8 %shard_map.209 = (f32[512,1152]{1,0:T(8,128)}, bf16[512,1152]{1,0:T(8,128)(2,1)S(1)}, f32[2,4,1152]{2,1,0:T(4,128)S(1)}) custom-call(s32[2]{0:T(128)S(1)} %copy-done.11, bf16[4,512,1152]{2,1,0:T(8,128)(2,1)} %get-tuple-element.139.d_pre, bf16[4,1152,1152]{2,1,0:T(8,128)(2,1)} %bitcast.306, f32[2,6,1152]{2,1,0:T(8,128)S(1)} %copy-done.4, ...), custom_call_target="tpu_custom_call" | custom-call | flops 5435817984 | bytes 23592960 | tf_op jit(solution)/shard_map/pallas_call | solution.py:479
  344.4 8.1 %collective-permute-done.21 = bf16[2,2,144,1152]{3,2,1,0:T(8,128)(2,1)} collective-permute-done((bf16[2,2,144,1152]{3,2,1,0:T(8,128)(2,1)}, bf16[2,2,144,1152]{3,2,1,0:T(8,128)(2,1)}, u32[]{:S(2)}, u32[]{:S(2)}) %collective-permute-start.21) | collective-permute-done | bytes 1327136 | tf_op jit(solution)/shard_map/ppermute | solution.py:659
  352.8 7.6 %fusion = bf16[4,576,1152]{2,1,0:T(8,128)(2,1)S(1)} fusion(bf16[4,576,1152]{2,1,0:T(8,128)(2,1)} %collective-permute-done.20, bf16[4,512,1152]{2,1,0:T(8,128)(2,1)} %get-tuple-element.139.d_pre, bf16[512,1152]{1,0:T(8,128)(2,1)S(1)} %copy-done.17, s32[]{:T(128)S(6)} %select_n.437), kind=kOutput, calls=%fused_computation.1 | convolution fusion | flops 2725871616 | bytes 15990788 | tf_op jit(solution)/shard_map/td,jte->jde/dot_general | solution.py:838
  370.3 26.2 %shard_map.210 = (bf16[4,512,1152]{2,1,0:T(8,128)(2,1)}, f32[2,3,1152]{2,1,0:T(4,128)S(1)}) custom-call(s32[2]{0:T(128)S(1)} %copy-done.11, bf16[512,1152]{1,0:T(8,128)(2,1)S(1)} %get-tuple-element.148.d_proj, bf16[5,512,1152]{2,1,0:T(8,128)(2,1)} %get-tuple-element.149.parts, bf16[4,1152,1152]{2,1,0:T(8,128)(2,1)} %bitcast.304), custom_call_target="tpu_custom_call" | custom-call | flops 8153726976 | bytes 11796480 | tf_op jit(solution)/shard_map/pallas_call | solution.py:548
  396.6 7.5 convolution_convert_fusion
  417.5 18.5 %collective-permute-done.26 = bf16[2,2,144,1152]{3,2,1,0:T(8,128)(2,1)} collective-permute-done((bf16[2,2,144,1152]{3,2,1,0:T(8,128)(2,1)}, bf16[2,2,144,1152]{3,2,1,0:T(8,128)(2,1)}, u32[]{:S(2)}, u32[]{:S(2)}) %collective-permute-start.26) | collective-permute-done | bytes 1327136 | tf_op jit(solution)/shard_map/ppermute | solution.py:659
  458.5 11.1 %shard_map.211 = (bf16[512,1152]{1,0:T(8,128)(2,1)}, f32[2,2,1152]{2,1,0:T(2,128)S(1)}) custom-call(bf16[4,512,1152]{2,1,0:T(8,128)(2,1)} %get-tuple-element.164.d_qkv, bf16[4,1152,1152]{2,1,0:T(8,128)(2,1)} %bitcast.305, f32[2,6,1152]{2,1,0:T(8,128)S(1)} %copy-done.4, bf16[512,1152]{1,0:T(8,128)(2,1)S(1)} %bitcast.300, f32[512,1152]{1,0:T(8,128)S(1)} %copy-done), custom_call_target="tpu_custom_call" | custom-call | flops 4076863488 | bytes 17694720 | tf_op jit(solution)/shard_map/pallas_call | solution.py:610
  479.4 24.8 %collective-permute-done.32 = bf16[2,2,144,1152]{3,2,1,0:T(8,128)(2,1)} collective-permute-done((bf16[2,2,144,1152]{3,2,1,0:T(8,128)(2,1)}, bf16[2,2,144,1152]{3,2,1,0:T(8,128)(2,1)}, u32[]{:S(2)}, u32[]{:S(2)}) %collective-permute-start.32) | collective-permute-done | bytes 1327136 | tf_op jit(solution)/shard_map/ppermute | solution.py:659
  504.3 11.0 %collective-permute-done.34 = bf16[2,144,1152]{2,1,0:T(8,128)(2,1)} collective-permute-done((bf16[2,144,1152]{2,1,0:T(8,128)(2,1)S(1)}, bf16[2,144,1152]{2,1,0:T(8,128)(2,1)}, u32[]{:S(2)}, u32[]{:S(2)}) %collective-permute-start.34) | collective-permute-done | bytes 663584 | tf_op jit(solution)/shard_map/ppermute | solution.py:654
  536.9 22.5 %collective-permute-done.37 = bf16[1,144,1152]{2,1,0:T(8,128)(2,1)S(1)} collective-permute-done((bf16[1,144,1152]{2,1,0:T(8,128)(2,1)}, bf16[1,144,1152]{2,1,0:T(8,128)(2,1)S(1)}, u32[]{:S(2)}, u32[]{:S(2)}) %collective-permute-start.37) | collective-permute-done | bytes 331808 | tf_op jit(solution)/shard_map/ppermute | solution.py:654
  570.8 18.9 %all-to-all-done.2 = f32[8,1,3960]{2,1,0:T(1,128)S(1)} async-done(((f32[8,1,3960]{2,1,0:T(1,128)}), f32[8,1,3960]{2,1,0:T(1,128)S(1)}, u32[]{:S(2)}, u32[]{:S(2)}) %all-to-all-start.2) | async-done | bytes 126752 | tf_op jit(solution)/shard_map/all_to_all | solution.py:1112
  590.3 9.8 %all_gather.42 = f32[864,128]{1,0:T(8,128)} all-gather(f32[216,128]{1,0:T(8,128)S(1)} %reshape.330), channel_id=1, replica_groups=mesh['dp'=8,'fsdp'=4] {'fsdp'}, dimensions={0}, use_global_device_ids=true | all-gather | bytes 552960 | tf_op jit(solution)/shard_map/all_gather | solution.py:1117
  605.5 12.2 %collective-permute-start.39 = (bf16[1,144,1152]{2,1,0:T(8,128)(2,1)S(1)}, bf16[1,144,1152]{2,1,0:T(8,128)(2,1)S(1)}, u32[]{:S(2)}, u32[]{:S(2)}) collective-permute-start(bf16[1,144,1152]{2,1,0:T(8,128)(2,1)S(1)} %constant_dynamic-slice_fusion), channel_id=1, source_target_pairs={{0,16},{4,20},{8,24},{12,28},{16,0},{20,4},{24,8},{28,12},{1,17},{... | collective-permute-start | bytes 995336 | tf_op jit(solution)/shard_map/ppermute | solution.py:654
  620.6 8.4 %shard_map.212 = bf16[4,3,144,288]{3,2,1,0:T(8,128)(2,1)} custom-call(s32[1]{0:T(128)} %bitcast.100.at, bf16[1152,1152]{1,0:T(8,128)(2,1)} %bitcast.334, bf16[144,1152]{1,0:T(8,128)(2,1)S(1)} %get-tuple-element.227.left_root, bf16[1152,1152]{1,0:T(8,128)(2,1)} %bitcast.332), custom_call_target="tpu_custom_call" | custom-call | flops 2293235712 | bytes 7962624 | tf_op jit(solution)/shard_map/pallas_call | solution.py:881
  641.3 8.4 %shard_map.213 = bf16[4,3,144,288]{3,2,1,0:T(8,128)(2,1)} custom-call(s32[1]{0:T(128)} %bitcast.100.at, bf16[1152,1152]{1,0:T(8,128)(2,1)} %bitcast.335, bf16[144,1152]{1,0:T(8,128)(2,1)S(1)} %get-tuple-element.225.left_root, bf16[1152,1152]{1,0:T(8,128)(2,1)} %bitcast.333), custom_call_target="tpu_custom_call" | custom-call | flops 2293235712 | bytes 7962624 | tf_op jit(solution)/shard_map/pallas_call | solution.py:881
  659.9 16.9 %all_gather.46 = f32[1728,128]{1,0:T(8,128)} all-gather(f32[216,128]{1,0:T(8,128)S(1)} %reshape.337), channel_id=1, replica_groups=mesh['dp'=8,'fsdp'=4] {'dp'}, dimensions={0}, use_global_device_ids=true | all-gather | bytes 995328 | tf_op jit(solution)/shard_map/all_gather | solution.py:1141
  681.2 17.2 %all-gather.18.cloned.1.call-done = bf16[1,1152,1152]{2,1,0:T(8,128)(2,1)} async-done(((bf16[1,144,1152]{2,1,0:T(8,128)(2,1)}), bf16[1,1152,1152]{2,1,0:T(8,128)(2,1)}) %all-gather.18.cloned.1.call-update) | async-done | bytes 2654224 | tf_op jit(solution)/shard_map/all_gather | solution.py:789
  698.4 8.3 %shard_map.214 = bf16[4,3,144,288]{3,2,1,0:T(8,128)(2,1)} custom-call(s32[1]{0:T(128)} %bitcast.100.at, bf16[1152,1152]{1,0:T(8,128)(2,1)} %bitcast.336, bf16[144,1152]{1,0:T(8,128)(2,1)S(1)} %get-tuple-element.223.left_root, bf16[1152,1152]{1,0:T(8,128)(2,1)} %bitcast.337), custom_call_target="tpu_custom_call" | custom-call | flops 2293235712 | bytes 7962624 | tf_op jit(solution)/shard_map/pallas_call | solution.py:881
  717.5 11.1 %all-to-all-done.5 = bf16[4,3,144,288]{3,2,1,0:T(8,128)(2,1)} async-done(((bf16[4,3,144,288]{3,2,1,0:T(8,128)(2,1)}), bf16[4,3,144,288]{3,2,1,0:T(8,128)(2,1)}, u32[]{:S(2)}, u32[]{:S(2)}) %all-to-all-start.5) | async-done | bytes 995360 | tf_op jit(solution)/shard_map/all_to_all | solution.py:731
  (398 shorter events, 260.3 us)
Async XLA Ops:
  7.2 132.3 %all-gather.20.cloned.1.call-start = ((), (), s32[]{:S(2)}) async-start(), calls=%async_computation.9 | async-start | bytes 10948608 | tf_op jit(solution)/shard_map/all_gather | solution.py:740
  31.9 244.0 %all-gather.22.cloned.1.call-start = ((), (), s32[]{:S(2)}) async-start(), calls=%async_computation.10 | async-start | bytes 10948608 | tf_op jit(solution)/shard_map/all_gather | solution.py:740
  52.6 568.0 %all-gather.14.cloned.1.call-start = ((), (), s32[]{:S(2)}) async-start(), calls=%async_computation.6 | async-start | bytes 2985984 | tf_op jit(solution)/shard_map/all_gather | solution.py:789
  66.3 35.2 %collective-permute-start.7 = (bf16[144,1152]{1,0:T(8,128)(2,1)S(1)}, bf16[144,1152]{1,0:T(8,128)(2,1)S(1)}, u32[]{:S(2)}, u32[]{:S(2)}) collective-permute-start(bf16[144,1152]{1,0:T(8,128)(2,1)S(1)} %get-tuple-element.109.refs_0_), channel_id=1, source_target_pairs={{0,16},{4,20},{8,24},{12,28},{16,0},{20,4},{24,8},{28,12},{1,17},{... | collective-permute-start | bytes 995336 | tf_op jit(solution)/shard_map/ppermute | solution.py:649
  70.1 31.4 %collective-permute-start.8 = (bf16[144,1152]{1,0:T(8,128)(2,1)S(1)}, bf16[144,1152]{1,0:T(8,128)(2,1)S(1)}, u32[]{:S(2)}, u32[]{:S(2)}) collective-permute-start(bf16[144,1152]{1,0:T(8,128)(2,1)S(1)} %get-tuple-element.109.refs_0_), channel_id=1, source_target_pairs={{0,24},{4,28},{8,0},{12,4},{16,8},{20,12},{24,16},{28,20},{1,25},{... | collective-permute-start | bytes 995336 | tf_op jit(solution)/shard_map/ppermute | solution.py:649
  131.5 49.8 %collective-permute-start.10 = (bf16[576,1152]{1,0:T(8,128)(2,1)}, bf16[576,1152]{1,0:T(8,128)(2,1)}, u32[]{:S(2)}, u32[]{:S(2)}) collective-permute-start(bf16[576,1152]{1,0:T(8,128)(2,1)} %constant_dynamic-slice_fusion.7), channel_id=1, source_target_pairs={{0,1},{1,0},{2,3},{3,2},{4,5},{5,4},{6,7},{7,6},{8,9},{9,8},{10,11... | collective-permute-start | bytes 3981320 | tf_op jit(solution)/shard_map/ppermute | solution.py:659
  132.8 48.5 %collective-permute-start.11 = (bf16[576,1152]{1,0:T(8,128)(2,1)}, bf16[576,1152]{1,0:T(8,128)(2,1)}, u32[]{:S(2)}, u32[]{:S(2)}) collective-permute-start(bf16[576,1152]{1,0:T(8,128)(2,1)} %constant_dynamic-slice_fusion.7), channel_id=1, source_target_pairs={{0,2},{1,3},{2,0},{3,1},{4,6},{5,7},{6,4},{7,5},{8,10},{9,11},{10,... | collective-permute-start | bytes 3981320 | tf_op jit(solution)/shard_map/ppermute | solution.py:659
  133.5 69.9 %collective-permute-start.12 = (bf16[576,1152]{1,0:T(8,128)(2,1)}, bf16[576,1152]{1,0:T(8,128)(2,1)}, u32[]{:S(2)}, u32[]{:S(2)}) collective-permute-start(bf16[576,1152]{1,0:T(8,128)(2,1)} %constant_dynamic-slice_fusion.7), channel_id=1, source_target_pairs={{0,3},{1,2},{2,1},{3,0},{4,7},{5,6},{6,5},{7,4},{8,11},{9,10},{10,... | collective-permute-start | bytes 3981320 | tf_op jit(solution)/shard_map/ppermute | solution.py:659
  206.5 32.1 %collective-permute-start.16 = (bf16[6,144,288]{2,1,0:T(8,128)(2,1)S(1)}, bf16[6,144,288]{2,1,0:T(8,128)(2,1)}, u32[]{:S(2)}, u32[]{:S(2)}) collective-permute-start(bf16[6,144,288]{2,1,0:T(8,128)(2,1)S(1)} %get-tuple-element.220), channel_id=1, source_target_pairs={{0,1},{1,0},{2,3},{3,2},{4,5},{5,4},{6,7},{7,6},{8,9},{9,8},{10,11... | collective-permute-start | bytes 1493000 | tf_op jit(solution)/shard_map/ppermute | solution.py:659
  206.6 33.2 %collective-permute-start.17 = (bf16[6,144,288]{2,1,0:T(8,128)(2,1)S(1)}, bf16[6,144,288]{2,1,0:T(8,128)(2,1)}, u32[]{:S(2)}, u32[]{:S(2)}) collective-permute-start(bf16[6,144,288]{2,1,0:T(8,128)(2,1)S(1)} %get-tuple-element.219), channel_id=1, source_target_pairs={{0,2},{1,3},{2,0},{3,1},{4,6},{5,7},{6,4},{7,5},{8,10},{9,11},{10,... | collective-permute-start | bytes 1493000 | tf_op jit(solution)/shard_map/ppermute | solution.py:659
  208.3 47.8 %collective-permute-start.18 = (bf16[6,144,288]{2,1,0:T(8,128)(2,1)S(1)}, bf16[6,144,288]{2,1,0:T(8,128)(2,1)}, u32[]{:S(2)}, u32[]{:S(2)}) collective-permute-start(bf16[6,144,288]{2,1,0:T(8,128)(2,1)S(1)} %get-tuple-element.218), channel_id=1, source_target_pairs={{0,3},{1,2},{2,1},{3,0},{4,7},{5,6},{6,5},{7,4},{8,11},{9,10},{10,... | collective-permute-start | bytes 1493000 | tf_op jit(solution)/shard_map/ppermute | solution.py:659
  256.1 44.3 %collective-permute-start.19 = (bf16[4,576,1152]{2,1,0:T(8,128)(2,1)}, bf16[4,576,1152]{2,1,0:T(8,128)(2,1)}, u32[]{:S(2)}, u32[]{:S(2)}) collective-permute-start(bf16[4,576,1152]{2,1,0:T(8,128)(2,1)} %convolution_convert_fusion.1), channel_id=1, source_target_pairs={{0,4},{4,0},{8,12},{12,8},{16,20},{20,16},{24,28},{28,24},{1,5},{5... | collective-permute-start | bytes 15925256 | tf_op jit(solution)/shard_map/ppermute | solution.py:644
  320.7 32.2 %collective-permute-start.20 = (bf16[4,576,1152]{2,1,0:T(8,128)(2,1)}, bf16[4,576,1152]{2,1,0:T(8,128)(2,1)}, u32[]{:S(2)}, u32[]{:S(2)}) collective-permute-start(bf16[4,576,1152]{2,1,0:T(8,128)(2,1)} %fusion.1), channel_id=1, source_target_pairs={{0,4},{4,0},{8,12},{12,8},{16,20},{20,16},{24,28},{28,24},{1,5},{5... | collective-permute-start | bytes 15925256 | tf_op jit(solution)/shard_map/ppermute | solution.py:644
  321.0 31.5 %collective-permute-start.21 = (bf16[2,2,144,1152]{3,2,1,0:T(8,128)(2,1)}, bf16[2,2,144,1152]{3,2,1,0:T(8,128)(2,1)}, u32[]{:S(2)}, u32[]{:S(2)}) collective-permute-start(bf16[2,2,144,1152]{3,2,1,0:T(8,128)(2,1)} %dynamic-slice_bitcast_fusion.5), channel_id=1, source_target_pairs={{0,1},{1,0},{2,3},{3,2},{4,5},{5,4},{6,7},{7,6},{8,9},{9,8},{10,11... | collective-permute-start | bytes 3981320 | tf_op jit(solution)/shard_map/ppermute | solution.py:659
  321.6 31.2 %collective-permute-start.22 = (bf16[2,2,144,1152]{3,2,1,0:T(8,128)(2,1)}, bf16[2,2,144,1152]{3,2,1,0:T(8,128)(2,1)}, u32[]{:S(2)}, u32[]{:S(2)}) collective-permute-start(bf16[2,2,144,1152]{3,2,1,0:T(8,128)(2,1)} %dynamic-slice_bitcast_fusion.4), channel_id=1, source_target_pairs={{0,2},{1,3},{2,0},{3,1},{4,6},{5,7},{6,4},{7,5},{8,10},{9,11},{10,... | collective-permute-start | bytes 3981320 | tf_op jit(solution)/shard_map/ppermute | solution.py:659
  366.5 30.1 %collective-permute-start.23 = (bf16[2,144,1152]{2,1,0:T(8,128)(2,1)S(1)}, bf16[2,144,1152]{2,1,0:T(8,128)(2,1)S(1)}, u32[]{:S(2)}, u32[]{:S(2)}) collective-permute-start(bf16[2,144,1152]{2,1,0:T(8,128)(2,1)S(1)} %dynamic-slice_bitcast_fusion.14), channel_id=1, source_target_pairs={{0,2},{1,3},{2,0},{3,1},{4,6},{5,7},{6,4},{7,5},{8,10},{9,11},{10,... | collective-permute-start | bytes 1990664 | tf_op jit(solution)/shard_map/ppermute | solution.py:659
  404.1 32.5 %collective-permute-start.25 = (bf16[4,576,1152]{2,1,0:T(8,128)(2,1)}, bf16[4,576,1152]{2,1,0:T(8,128)(2,1)}, u32[]{:S(2)}, u32[]{:S(2)}) collective-permute-start(bf16[4,576,1152]{2,1,0:T(8,128)(2,1)} %convolution_convert_fusion), channel_id=1, source_target_pairs={{0,4},{4,0},{8,12},{12,8},{16,20},{20,16},{24,28},{28,24},{1,5},{5... | collective-permute-start | bytes 15925256 | tf_op jit(solution)/shard_map/ppermute | solution.py:644
  404.1 31.9 %collective-permute-start.26 = (bf16[2,2,144,1152]{3,2,1,0:T(8,128)(2,1)}, bf16[2,2,144,1152]{3,2,1,0:T(8,128)(2,1)}, u32[]{:S(2)}, u32[]{:S(2)}) collective-permute-start(bf16[2,2,144,1152]{3,2,1,0:T(8,128)(2,1)} %dynamic-slice_bitcast_fusion.3), channel_id=1, source_target_pairs={{0,1},{1,0},{2,3},{3,2},{4,5},{5,4},{6,7},{7,6},{8,9},{9,8},{10,11... | collective-permute-start | bytes 3981320 | tf_op jit(solution)/shard_map/ppermute | solution.py:659
  405.0 31.6 %collective-permute-start.27 = (bf16[2,2,144,1152]{3,2,1,0:T(8,128)(2,1)}, bf16[2,2,144,1152]{3,2,1,0:T(8,128)(2,1)}, u32[]{:S(2)}, u32[]{:S(2)}) collective-permute-start(bf16[2,2,144,1152]{3,2,1,0:T(8,128)(2,1)} %dynamic-slice_bitcast_fusion.2), channel_id=1, source_target_pairs={{0,2},{1,3},{2,0},{3,1},{4,6},{5,7},{6,4},{7,5},{8,10},{9,11},{10,... | collective-permute-start | bytes 3981320 | tf_op jit(solution)/shard_map/ppermute | solution.py:659
  417.4 203.1 %all-gather.24.cloned.1.call-start = ((), (), s32[]{:S(2)}) async-start(), calls=%async_computation.11 | async-start | bytes 2985984 | tf_op jit(solution)/shard_map/all_gather | solution.py:834
  438.8 34.2 %collective-permute-start.29 = (bf16[2,144,1152]{2,1,0:T(8,128)(2,1)S(1)}, bf16[2,144,1152]{2,1,0:T(8,128)(2,1)}, u32[]{:S(2)}, u32[]{:S(2)}) collective-permute-start(bf16[2,144,1152]{2,1,0:T(8,128)(2,1)S(1)} %dynamic-slice_bitcast_fusion.11), channel_id=1, source_target_pairs={{0,2},{1,3},{2,0},{3,1},{4,6},{5,7},{6,4},{7,5},{8,10},{9,11},{10,... | collective-permute-start | bytes 1990664 | tf_op jit(solution)/shard_map/ppermute | solution.py:659
  443.1 29.9 %collective-permute-start.30 = (bf16[2,144,1152]{2,1,0:T(8,128)(2,1)}, bf16[2,144,1152]{2,1,0:T(8,128)(2,1)}, u32[]{:S(2)}, u32[]{:S(2)}) collective-permute-start(bf16[2,144,1152]{2,1,0:T(8,128)(2,1)} %dynamic-slice_bitcast_fusion.10), channel_id=1, source_target_pairs={{0,1},{1,0},{2,3},{3,2},{4,5},{5,4},{6,7},{7,6},{8,9},{9,8},{10,11... | collective-permute-start | bytes 1990664 | tf_op jit(solution)/shard_map/ppermute | solution.py:659
  473.9 167.5 %all-gather.16.cloned.1.call-start = ((), (), s32[]{:S(2)}) async-start(), calls=%async_computation.7 | async-start | bytes 2985984 | tf_op jit(solution)/shard_map/all_gather | solution.py:789
  474.4 166.9 %all-gather.28.cloned.1.call-start = ((), (), s32[]{:S(2)}) async-start(), calls=%async_computation.13 | async-start | bytes 2985984 | tf_op jit(solution)/shard_map/all_gather | solution.py:834
  474.5 29.7 %collective-permute-start.32 = (bf16[2,2,144,1152]{3,2,1,0:T(8,128)(2,1)}, bf16[2,2,144,1152]{3,2,1,0:T(8,128)(2,1)}, u32[]{:S(2)}, u32[]{:S(2)}) collective-permute-start(bf16[2,2,144,1152]{3,2,1,0:T(8,128)(2,1)} %dynamic-slice_bitcast_fusion.1), channel_id=1, source_target_pairs={{0,1},{1,0},{2,3},{3,2},{4,5},{5,4},{6,7},{7,6},{8,9},{9,8},{10,11... | collective-permute-start | bytes 3981320 | tf_op jit(solution)/shard_map/ppermute | solution.py:659
  475.2 29.0 %collective-permute-start.33 = (bf16[2,2,144,1152]{3,2,1,0:T(8,128)(2,1)}, bf16[2,2,144,1152]{3,2,1,0:T(8,128)(2,1)}, u32[]{:S(2)}, u32[]{:S(2)}) collective-permute-start(bf16[2,2,144,1152]{3,2,1,0:T(8,128)(2,1)} %dynamic-slice_bitcast_fusion), channel_id=1, source_target_pairs={{0,2},{1,3},{2,0},{3,1},{4,6},{5,7},{6,4},{7,5},{8,10},{9,11},{10,... | collective-permute-start | bytes 3981320 | tf_op jit(solution)/shard_map/ppermute | solution.py:659
  478.9 36.3 %collective-permute-start.34 = (bf16[2,144,1152]{2,1,0:T(8,128)(2,1)S(1)}, bf16[2,144,1152]{2,1,0:T(8,128)(2,1)}, u32[]{:S(2)}, u32[]{:S(2)}) collective-permute-start(bf16[2,144,1152]{2,1,0:T(8,128)(2,1)S(1)} %dynamic-slice_bitcast_fusion.9), channel_id=1, source_target_pairs={{0,8},{4,12},{8,0},{12,4},{16,24},{20,28},{24,16},{28,20},{1,9},{5... | collective-permute-start | bytes 1990664 | tf_op jit(solution)/shard_map/ppermute | solution.py:654
  519.2 40.2 %collective-permute-start.35 = (bf16[2,144,1152]{2,1,0:T(8,128)(2,1)}, bf16[2,144,1152]{2,1,0:T(8,128)(2,1)}, u32[]{:S(2)}, u32[]{:S(2)}) collective-permute-start(bf16[2,144,1152]{2,1,0:T(8,128)(2,1)} %dynamic-slice_bitcast_fusion.8), channel_id=1, source_target_pairs={{0,2},{1,3},{2,0},{3,1},{4,6},{5,7},{6,4},{7,5},{8,10},{9,11},{10,... | collective-permute-start | bytes 1990664 | tf_op jit(solution)/shard_map/ppermute | solution.py:659
  523.3 36.1 %collective-permute-start.36 = (bf16[2,144,1152]{2,1,0:T(8,128)(2,1)}, bf16[2,144,1152]{2,1,0:T(8,128)(2,1)}, u32[]{:S(2)}, u32[]{:S(2)}) collective-permute-start(bf16[2,144,1152]{2,1,0:T(8,128)(2,1)} %dynamic-slice_bitcast_fusion.7), channel_id=1, source_target_pairs={{0,1},{1,0},{2,3},{3,2},{4,5},{5,4},{6,7},{7,6},{8,9},{9,8},{10,11... | collective-permute-start | bytes 1990664 | tf_op jit(solution)/shard_map/ppermute | solution.py:659
  526.7 32.7 %collective-permute-start.37 = (bf16[1,144,1152]{2,1,0:T(8,128)(2,1)}, bf16[1,144,1152]{2,1,0:T(8,128)(2,1)S(1)}, u32[]{:S(2)}, u32[]{:S(2)}) collective-permute-start(bf16[1,144,1152]{2,1,0:T(8,128)(2,1)} %constant_dynamic-slice_fusion.1), channel_id=1, source_target_pairs={{0,16},{4,20},{8,24},{12,28},{16,0},{20,4},{24,8},{28,12},{1,17},{... | collective-permute-start | bytes 995336 | tf_op jit(solution)/shard_map/ppermute | solution.py:654
  570.7 110.5 %all-gather.26.cloned.1.call-start = ((), (), s32[]{:S(2)}) async-start(), calls=%async_computation.12 | async-start | bytes 2985984 | tf_op jit(solution)/shard_map/all_gather | solution.py:834
  629.9 68.5 %all-gather.18.cloned.1.call-start = ((), (), s32[]{:S(2)}) async-start(), calls=%async_computation.8 | async-start | bytes 2985984 | tf_op jit(solution)/shard_map/all_gather | solution.py:789
  (85 other events, 1042.5 us)
Sparse Core Ops, SparseCore 0:
  32.0 107.4 all-gather.19
  142.5 112.3 all-gather.21
  417.5 33.3 all-gather.13
  474.0 42.5 all-gather.23
  518.1 47.3 all-gather.15
  567.6 35.4 all-gather.27
  630.0 33.6 all-gather.25
  665.4 33.0 all-gather.17

commit v10 on v9

--- a/solution.py
+++ b/solution.py
@@ -20,6 +20,7 @@
 bias_rate = 0.1
 diag_epsilon = 1e-08
 vmem_bytes = 50 * 2**20
+little_cost = pl.CostEstimate(flops=1024, bytes_accessed=1024, transcendentals=0)
 
 
 def narrow(array):
@@ -249,14 +250,34 @@
             pltpu.SemaphoreType.DMA((4,)),
         ],
         compiler_params=pltpu.CompilerParams(vmem_limit_bytes=vmem_bytes),
-        cost_estimate=pl.CostEstimate(
-            flops=16 * total * width * width, bytes_accessed=100 * total * width, transcendentals=0
-        ),
+        cost_estimate=little_cost,
     )(counts, tokens, cotangent, mods, bias, blocks)
 
 
 def stacked(numbers):
     return jnp.stack([jnp.asarray(number, jnp.int32) for number in numbers])
+
+
+def start_loads(cuts, at, parts, whole, semaphores):
+    for index, (part, first, rows) in enumerate(cuts):
+        span = pl.ds(pl.multiple_of(at[index] * 16, 16), rows)
+        source = parts[part].at[pl.ds(first, rows)]
+        pltpu.make_async_copy(source, whole.at[span], semaphores.at[index]).start()
+
+
+def wait_loads(groups, at, parts, whole, semaphores):
+    index = 0
+    for step, cuts in enumerate(groups):
+        base = index
+        index += len(cuts)
+
+        @pl.when(pl.program_id(0) == step)
+        def _(cuts=cuts, base=base):
+            for offset, (part, first, rows) in enumerate(cuts):
+                span = pl.ds(pl.multiple_of(at[base + offset] * 16, 16), rows)
+                source = parts[part].at[pl.ds(first, rows)]
+                semaphore = semaphores.at[base + offset]
+                pltpu.make_async_copy(source, whole.at[span], semaphore).wait()
 
 
 def hidden_kernel(cuts, order, starts, mlp_in, bias, *refs):
@@ -264,28 +285,13 @@
     pieces = refs[:-6]
     step, steps = pl.program_id(0), pl.num_programs(0)
     width = mlp_in.shape[-1]
-    flat = [cut for group in cuts for cut in group]
     span = pl.ds(pl.multiple_of(order[step] * width, width), width)
 
     @pl.when(step == 0)
     def _():
-        start_loads(flat, starts, pieces, whole, semaphores)
-
-    index = 0
-    for at, group in enumerate(cuts):
-        first_index = index
-        index += len(group)
-
-        @pl.when(step == at)
-        def _(group=group, first_index=first_index):
-            for offset, (part, first, size) in enumerate(group):
-                target = pl.ds(pl.multiple_of(starts[first_index + offset] * 16, 16), size)
-                pltpu.make_async_copy(
-                    pieces[part].at[pl.ds(first, size)],
-                    whole.at[target],
-                    semaphores.at[first_index + offset],
-                ).wait()
-
+        start_loads([cut for group in cuts for cut in group], starts, pieces, whole, semaphores)
+
+    wait_loads(cuts, starts, pieces, whole, semaphores)
     pltpu.make_async_copy(whole.at[span], whole_out.at[span], store_semaphores.at[step]).start()
     root = (2.0 / math.pi) ** 0.5
     source = mlp_in[...]
@@ -334,29 +340,27 @@
         ),
         out_shape=[jax.ShapeDtypeStruct((count * width, width), jnp.bfloat16), out, out],
         compiler_params=pltpu.CompilerParams(vmem_limit_bytes=vmem_bytes),
-        cost_estimate=pl.CostEstimate(
-            flops=8 * total * width * width, bytes_accessed=50 * total * width, transcendentals=0
-        ),
+        cost_estimate=little_cost,
     )(stacked(order), stacked(starts), mlp_in, bias, *pieces)
 
 
 def branch_kernel(
     frames,
+    cuts,
+    order,
+    starts,
     counts,
     hidden,
     slope,
-    block,
     d_branch,
     bias,
     gates,
     resid,
     cotangent,
-    d_pre,
-    d_pre_sum,
-    block_out,
-    d_gate,
-    branch,
+    *refs,
 ):
+    d_pre, d_pre_sum, block_out, d_gate, branch, whole, semaphores = refs[-7:]
+    pieces = refs[:-7]
     step, steps = pl.program_id(0), pl.num_programs(0)
     total, width = resid.shape
     clips = gates.shape[0]
@@ -365,15 +369,18 @@
 
     @pl.when(step == 0)
     def _():
+        start_loads([cut for group in cuts for cut in group], starts, pieces, whole, semaphores)
         branch[...] = jnp.zeros_like(branch)
 
+    wait_loads(cuts, starts, pieces, whole, semaphores)
+    block = whole.at[pl.ds(pl.multiple_of(order[step] * width, width), width)]
     for low, high in column_cuts(width):
         span = slice(low, high)
-        d_hidden = dot_nt(back, block[0, span, :])
+        d_hidden = dot_nt(back, block[span, :])
         low_back = narrow(d_hidden * wide(slope[0, :, span]))
         d_pre[0, :, span] = low_back
         d_pre_sum[0, :, span] = column_sum(wide(low_back))
-        branch[:, span] += dot_nn(source, block[0, :, span])
+        branch[:, span] += dot_nn(source, block[:, span])
 
     @pl.when(step == steps - 1)
     def _():
@@ -384,43 +391,53 @@
             d_gate[clip] = column_sum(wide(cotangent[span]) * kept)
 
 
-def run_branch(frames, counts, hidden, slope, blocks, d_branch, bias, gates, resid, cotangent):
+def run_branch(frames, counts, hidden, slope, gathered, d_branch, bias, gates, resid, cotangent):
+    pieces, cuts, starts, order = gathered
     count, total, width = hidden.shape
     clips = gates.shape[0]
-    per_block = spec((1, total, width), lambda at: (at, 0, 0))
+
+    def all_of(*shape):
+        return pl.BlockSpec(shape, lambda at, order, starts: (0,) * len(shape))
+
+    per_block = pl.BlockSpec((1, total, width), lambda at, order, starts: (order[at], 0, 0))
     low = jax.ShapeDtypeStruct((total, width), jnp.bfloat16)
     return pl.pallas_call(
-        functools.partial(branch_kernel, frames),
-        grid=(count,),
-        in_specs=[
-            pl.BlockSpec(memory_space=pltpu.SMEM),
-            per_block,
-            per_block,
-            spec((1, width, width), lambda at: (at, 0, 0)),
-            held((total, width)),
-            held(bias.shape),
-            held(gates.shape),
-            held((total, width)),
-            held((total, width)),
-        ],
-        out_specs=[
-            per_block,
-            spec((1, 1, width), lambda at: (at, 0, 0)),
-            held((total, width)),
-            held((clips, 1, width)),
-        ],
+        functools.partial(branch_kernel, frames, cuts),
+        grid_spec=pltpu.PrefetchScalarGridSpec(
+            num_scalar_prefetch=2,
+            grid=(count,),
+            in_specs=[
+                pl.BlockSpec(memory_space=pltpu.SMEM),
+                per_block,
+                per_block,
+                all_of(total, width),
+                all_of(*bias.shape),
+                all_of(*gates.shape),
+                all_of(total, width),
+                all_of(total, width),
+            ]
+            + [pl.BlockSpec(memory_space=pl.ANY)] * len(pieces),
+            out_specs=[
+                per_block,
+                pl.BlockSpec((1, 1, width), lambda at, order, starts: (order[at], 0, 0)),
+                all_of(total, width),
+                all_of(clips, 1, width),
+            ],
+            scratch_shapes=[
+                pltpu.VMEM((total, width), jnp.float32),
+                pltpu.VMEM((count * width, width), jnp.bfloat16),
+                pltpu.SemaphoreType.DMA((len(starts),)),
+            ],
+        ),
         out_shape=[
             jax.ShapeDtypeStruct((count, total, width), jnp.bfloat16),
             jax.ShapeDtypeStruct((count, 1, width), jnp.float32),
             low,
             jax.ShapeDtypeStruct((clips, 1, width), jnp.float32),
         ],
-        scratch_shapes=[pltpu.VMEM((total, width), jnp.float32)],
         compiler_params=pltpu.CompilerParams(vmem_limit_bytes=vmem_bytes),
-        cost_estimate=pl.CostEstimate(
-            flops=16 * total * width * width, bytes_accessed=40 * total * width, transcendentals=0
-        ),
-    )(counts, hidden, slope, blocks, d_branch, bias, gates, resid, cotangent)
+        cost_estimate=little_cost,
+    )(stacked(order), stacked(starts), counts, hidden, slope, d_branch, bias, gates, resid, cotangent, *pieces)
 
 
 def resid_kernel(
@@ -496,9 +513,7 @@
         ],
         scratch_shapes=[pltpu.VMEM((total, width), jnp.float32)],
         compiler_params=pltpu.CompilerParams(vmem_limit_bytes=vmem_bytes),
-        cost_estimate=pl.CostEstimate(
-            flops=8 * total * width * width, bytes_accessed=40 * total * width, transcendentals=0
-        ),
+        cost_estimate=little_cost,
     )(counts, d_pre, blocks, mods, resid, cotangent, proj)
 
 
@@ -565,9 +580,7 @@
         scratch_shapes=[pltpu.VMEM((rows, width), jnp.bfloat16)]
         + [pltpu.VMEM((rows, width), jnp.float32)] * 3,
         compiler_params=pltpu.CompilerParams(vmem_limit_bytes=vmem_bytes),
-        cost_estimate=pl.CostEstimate(
-            flops=12 * total * width * width, bytes_accessed=20 * total * width, transcendentals=0
-        ),
+        cost_estimate=little_cost,
     )(counts, d_proj, parts, block)
 
 
@@ -624,9 +637,7 @@
         ],
         scratch_shapes=[pltpu.VMEM((total, width), jnp.float32)],
         compiler_params=pltpu.CompilerParams(vmem_limit_bytes=vmem_bytes),
-        cost_estimate=pl.CostEstimate(
-            flops=6 * total * width * width, bytes_accessed=30 * total * width, transcendentals=0
-        ),
+        cost_estimate=little_cost,
     )(d_qkv, blocks, mods, tokens, d_resid)
 
 
@@ -697,9 +708,7 @@
             pltpu.SemaphoreType.DMA((2, len(cuts))),
         ],
         compiler_params=pltpu.CompilerParams(vmem_limit_bytes=vmem_bytes),
-        cost_estimate=pl.CostEstimate(
-            flops=0, bytes_accessed=4 * rows * width, transcendentals=0
-        ),
+        cost_estimate=little_cost,
     )(stacked(starts), *parts)
 
 
@@ -743,10 +752,9 @@
     return all_rows.reshape(group, total, total)
 
 
-def join_line(rows):
+def join_line(found):
     chips, chip = lax.axis_size("dp") // 2, lax.axis_index("dp") // 2
-    chunk = rows.shape[0]
-    found = [rows] + [chip_shift(rows, step) for step in range(1, chips)]
+    chunk = found[0].shape[0]
     starts = [(chip - step) % chips * (chunk // 16) for step in range(chips)]
     return place(found, [(step, 0, chunk) for step in range(chips)], starts, chips * chunk)
 
@@ -756,7 +764,7 @@
     total = rows.shape[-1]
     if ranks != group:
         blocks = gather_blocks(rows, group).reshape(group * total, total)
-        for _ in range(2):
+        for _ in range(3):
             (blocks,) = yield (blocks,)
         cuts = [[(0, index * total, total)] for index in range(group)]
         yield [blocks], cuts, [index * (total // 16) for index in range(group)], range(group)
@@ -764,7 +772,8 @@
     chips = lax.axis_size("dp") // 2
     core = lax.axis_index("dp") % 2
     chunk, half = rows.shape[0], total // 2
-    line = join_line(rows)
+    others = yield tuple(chip_shift(rows, step) for step in range(1, chips))
+    line = join_line([rows, *others])
     cuts = [(side, step * chunk, chunk) for side in range(2) for step in range(chips)]
     starts = [
         (2 * step + side) * (chunk // 16) for side in (core, 1 - core) for step in range(chips)
@@ -893,9 +902,7 @@
                 pltpu.SemaphoreType.DMA((dp_count,)),
             ],
             compiler_params=pltpu.CompilerParams(vmem_limit_bytes=vmem_bytes),
-            cost_estimate=pl.CostEstimate(
-                flops=12 * chunk * total * total, bytes_accessed=6 * total * total, transcendentals=0
-            ),
+            cost_estimate=little_cost,
         )((first // 16)[None], whole, left_root, right_root)
     grad_rows = lax.dynamic_slice_in_dim(whole, first, chunk, 0)
     own_columns = lax.dynamic_slice_in_dim(whole, first, chunk, 1)
@@ -938,16 +945,13 @@
     low_weights = narrow(weights).reshape(block_count, row_part, col_part)
     shards = low_weights[mod_count:].reshape(-1, group, row_part, col_part)
 
-    attn_rows, cond_low = own_rows(shards[:1], group), narrow(jax.nn.silu(conditioning))
-    attn_panels = next(attn_rows)
+    weight_rows = own_rows(shards, group)
+    weight_panels = next(weight_rows)
+    cond_low = narrow(jax.nn.silu(conditioning))
     first_parts = lax.all_gather(packed([cond_low, narrow(biases)], 16), "dp", axis=0, tiled=True)
-    attn_panels, first_parts, other_shards = tie(attn_panels, first_parts, shards[1:])
-    attn_rows = attn_rows.send(attn_panels)[0]
-    other_rows = own_rows(other_shards, group)
-    other_panels = next(other_rows)
+    weight_panels, first_parts = tie(weight_panels, first_parts)
+    attn_rows, one_rows, two_rows = weight_rows.send(weight_panels)
     attn_w = gather_blocks(attn_rows, group)
-    one_rows, two_rows = other_rows.send(other_panels)
-    two_w = gather_blocks(two_rows, group)
 
     first_parts = first_parts.reshape(dp_count, -1)
     cond_all = first_parts[:, : clip_count * width].reshape(all_clips, width)
@@ -965,8 +969,11 @@
     second_parts = lax.all_gather(
         packed([mod_cols, bias_rows, left_cond], 8), "fsdp", axis=0, tiled=True
     )
-    second_parts, one_parts = tie(second_parts, one_parts)
-    one_parts = one_steps.send(one_parts)
+    second_parts, one_parts, two_rows = tie(second_parts, one_parts, two_rows)
+    two_steps = gather_second(two_rows, group)
+    two_parts = next(two_steps)
+    one_parts = one_steps.send(one_steps.send(one_parts))
+    two_parts = two_steps.send(two_parts)
     second_parts = second_parts.reshape(ranks, -1)
     mods = second_parts[:, :mod_size].reshape(ranks, clip_count, mod_count, col_part)
     mods = mods.transpose(1, 2, 0, 3).reshape(clip_count, mod_count, width)
@@ -981,7 +988,8 @@
     )
 
     roots = jnp.stack([narrow(left_roots[mod_count:]), narrow(right_roots[mod_count:])])
-    mods, roots = tie(mods, roots)
+    mods, roots, two_parts = tie(mods, roots, two_parts)
+    two_parts = two_steps.send(two_parts)
     root_rows = own_rows(roots.reshape(-1, group, row_part, col_part), group)
     root_panels = next(root_rows)
     attn_in, parts, mixed, proj, resid, mlp_in, d_branch, d_branch_sums = run_attention(
@@ -991,6 +999,7 @@
     one_w, hidden, slope = run_hidden(mlp_in, one_steps.send(one_parts), bias_table[4:8, None])
     one_w = one_w.reshape(group, width, width)
 
+    weight_steps, two_w_parts = two_steps, two_parts
     two_steps = sum_blocks(
         lambda left: fast_dot("jtd,te->jde", left, d_branch),
         lambda first, size: lax.dynamic_slice_in_dim(hidden, first, size, 2),
@@ -1001,6 +1010,7 @@
     hidden, two_parts, root_panels = tie(hidden, two_parts, root_panels)
     two_parts = two_steps.send(two_parts)
     root_rows = root_rows.send(root_panels)
+    gathered = weight_steps.send(two_w_parts)
     hidden, root_rows = tie(hidden, root_rows)
     left_rows, right_rows = jnp.split(root_rows, 2)
     right_wholes = [gather_own(rows[None], group)[0] for rows in right_rows]
@@ -1009,7 +1019,7 @@
         frame_counts,
         hidden,
         slope,
-        two_w,
+        gathered,
         d_branch,
         bias_table[8:9],
         mods[:, 5:6],
@@ -1032,13 +1042,15 @@
     d_resid, d_proj, resid_sums = run_resid(
         frames, frame_counts, d_pre, one_w, mods, resid, grad_out, proj
     )
-    d_proj, one_parts, two_parts = tie(d_proj, one_parts, two_parts)
+    d_proj, one_parts, two_parts, right_wholes[2] = tie(
+        d_proj, one_parts, two_parts, right_wholes[2]
+    )
     two_parts = two_steps.send(two_parts)
     one_parts = one_steps.send(one_parts)
     d_proj, one_parts = tie(d_proj, one_parts)
     one_parts = one_steps.send(one_parts)
     d_heads, head_sums = run_attention_back(frames, frame_counts, d_proj, parts, attn_w)
-    d_heads, two_parts = tie(d_heads, two_parts)
+    d_heads, two_parts, right_wholes[1] = tie(d_heads, two_parts, right_wholes[1])
     two_parts = two_steps.send(two_parts)
     attn_steps = sum_blocks(
         lambda left: fast_dot("jtd,jte->jde", left, d_heads),
@@ -1058,7 +1070,9 @@
     d_heads, attn_parts = tie(d_heads, attn_parts)
     attn_parts = attn_steps.send(attn_parts)
     input_grad, input_sums = run_input(d_heads, attn_w, mods, stream, d_resid)
-    input_sums, one_parts, two_parts = tie(input_sums, one_parts, two_parts)
+    input_sums, one_parts, two_parts, right_wholes[0] = tie(
+        input_sums, one_parts, two_parts, right_wholes[0]
+    )
     whole_two = two_steps.send(two_parts)
     one_parts = one_steps.send(one_parts)
     input_sums, attn_parts, one_parts = tie(input_sums, attn_parts, one_parts)

time: 761 us -> 788 us (1.035)
  starting transfers between devices: 72 us -> 96.2 us
  blocking collectives: 75.3 us -> 61.7 us
    ppermute x3 -> x6, starting transfers between devices: 4.02 us -> 27.2 us  [chip_shift(): lax.ppermute(array, 'dp', [(at, (at + 2 * step) % count) for at in range(...]
    all_gather x3, waiting for transfers between devices: 17.2 us -> 0.01 us  [gather_own(): return lax.all_gather(rows, 'dp', axis=1, tiled=True)]
    ppermute x3 -> x6, waiting for transfers between devices: 31.3 us -> 47.7 us  [chip_shift(): lax.ppermute(array, 'dp', [(at, (at + 2 * step) % count) for at in range(...]
    ppermute x24, waiting for transfers between devices: 108 us -> 94.8 us  [rank_swap(): return lax.ppermute(array, 'fsdp', [(at, at ^ bits) for at in range(count)])]
    all_to_all x1 -> x0, blocking collectives: 13 us -> none  [per_device(): mod_parts = lax.all_to_all(mod_parts, 'dp', 0, 0, tiled=True)]
    all_to_all x0 -> x1, waiting for transfers between devices: none -> 10.3 us  [per_device(): mod_parts = lax.all_to_all(mod_parts, 'dp', 0, 0, tiled=True)]
    all_to_all x1, waiting for transfers between devices: 18.9 us -> 28.7 us  [per_device(): from_rows = lax.all_to_all(to_rows, 'dp', 0, 0, tiled=True)]
    ppermute x6, waiting for transfers between devices: 37 us -> 46.1 us  [chip_swap(): lax.ppermute(array, 'dp', [(at, at ^ 2 * bits) for at in range(count)])]
  transfers between devices with their start and end apart: 52 -> 59, of which waited for: 26 -> 21; matrix products, arithmetic and copies ran while one was open for 16% -> 20% of each run, Pallas kernels for 20% -> 20%
where the time goes in v10:
time: 788 us; the launch traced here: 782 us
  waiting for transfers between devices  242 us (31%)
  Pallas kernels  165 us (21%)
  starting transfers between devices  96.2 us (12%)
  local copies, waits for them, and re-layouts  72.6 us (9%)
  other arithmetic  68.4 us (9%)
  blocking collectives  61.7 us (8%)
  matrix products  60.6 us (8%)
  between operations  16.1 us (2%)
    ppermute x24, waiting for transfers between devices, rank_swap(): return lax.ppermute(array, 'fsdp', [(at, at ^ bits) for at in range(count)])  94.8 us
    ppermute x6, waiting for transfers between devices, chip_shift(): lax.ppermute(array, 'dp', [(at, (at + 2 * step) % count) for at in range(...  47.7 us
    dot_general x7, matrix products, fast_dot(): jnp.einsum(subscripts, left, right, preferred_element_type=jnp.float32)  47.1 us
    ppermute x6, waiting for transfers between devices, chip_swap(): lax.ppermute(array, 'dp', [(at, at ^ 2 * bits) for at in range(count)])  46.1 us
    pallas_call x1, Pallas kernels, run_attention(): pl.pallas_call(functools.partial(attention_kernel, frames), grid=(clips,)...  41 us
    convert_element_type x22, other arithmetic, narrow(): return array.astype(jnp.bfloat16)  37 us
    all_to_all x1, waiting for transfers between devices, per_device(): from_rows = lax.all_to_all(to_rows, 'dp', 0, 0, tiled=True)  28.7 us
    ppermute x24, starting transfers between devices, rank_swap(): return lax.ppermute(array, 'fsdp', [(at, at ^ bits) for at in range(count)])  27.5 us
  transfers between devices with their start and end apart: 59, of which 21 were waited for; matrix products, arithmetic and copies ran while one was open for 20% of the time, Pallas kernels for 20%

profile of v10, /device:TPU:0, one launch (start us, length us, event | category | flops | bytes accessed | tf_op | source)
XLA Modules:
  0.0 782.0 jit_solution(17042676946635648023)
XLA Ops:
  15.8 14.7 %all_gather.33 = bf16[256,128]{1,0:T(8,128)(2,1)S(1)} all-gather(bf16[32,128]{1,0:T(8,128)(2,1)S(1)} %fusion.84), channel_id=1, replica_groups=mesh['dp'=8,'fsdp'=4] {'dp'}, dimensions={0}, use_global_device_ids=true | all-gather | bytes 73728 | tf_op jit(solution)/shard_map/all_gather | solution.py:951
  41.6 10.3 %all-to-all-done = f32[16,6,288]{2,1,0:T(8,128)S(1)} async-done(((f32[16,6,288]{2,1,0:T(8,128)}), f32[16,6,288]{2,1,0:T(8,128)S(1)}, u32[]{:S(2)}, u32[]{:S(2)}) %all-to-all-start) | async-done | bytes 110624 | tf_op jit(solution)/shard_map/all_to_all | solution.py:962
  58.4 10.5 %all_gather.34 = f32[672,128]{1,0:T(8,128)} all-gather(f32[168,128]{1,0:T(8,128)S(1)} %pad_bitcast_fusion), channel_id=1, replica_groups=mesh['dp'=8,'fsdp'=4] {'fsdp'}, dimensions={0}, use_global_device_ids=true | all-gather | bytes 430080 | tf_op jit(solution)/shard_map/all_gather | solution.py:969
  68.9 10.1 %collective-permute-done.4.refs_2_ = bf16[144,1152]{1,0:T(8,128)(2,1)S(1)} collective-permute-done((bf16[144,1152]{1,0:T(8,128)(2,1)S(1)}, bf16[144,1152]{1,0:T(8,128)(2,1)S(1)}, u32[]{:S(2)}, u32[]{:S(2)}) %collective-permute-start.4) | collective-permute-done | bytes 331808 | tf_op jit(solution)/shard_map/ppermute | solution.py:660
  80.6 20.7 %collective-permute-start.6 = (bf16[144,1152]{1,0:T(8,128)(2,1)S(1)}, bf16[144,1152]{1,0:T(8,128)(2,1)S(1)}, u32[]{:S(2)}, u32[]{:S(2)}) collective-permute-start(bf16[144,1152]{1,0:T(8,128)(2,1)S(1)} %get-tuple-element.120.refs_0_), channel_id=1, source_target_pairs={{0,8},{4,12},{8,16},{12,20},{16,24},{20,28},{24,0},{28,4},{1,9},{5... | collective-permute-start | bytes 995336 | tf_op jit(solution)/shard_map/ppermute | solution.py:660
  104.1 10.4 %collective-permute-done.6.refs_1_ = bf16[144,1152]{1,0:T(8,128)(2,1)S(1)} collective-permute-done((bf16[144,1152]{1,0:T(8,128)(2,1)S(1)}, bf16[144,1152]{1,0:T(8,128)(2,1)S(1)}, u32[]{:S(2)}, u32[]{:S(2)}) %collective-permute-start.6) | collective-permute-done | bytes 331808 | tf_op jit(solution)/shard_map/ppermute | solution.py:660
  114.5 25.9 %collective-permute-done.7.refs_2_ = bf16[144,1152]{1,0:T(8,128)(2,1)S(1)} collective-permute-done((bf16[144,1152]{1,0:T(8,128)(2,1)S(1)}, bf16[144,1152]{1,0:T(8,128)(2,1)S(1)}, u32[]{:S(2)}, u32[]{:S(2)}) %collective-permute-start.7) | collective-permute-done | bytes 331808 | tf_op jit(solution)/shard_map/ppermute | solution.py:660
  166.0 41.0 %shard_map.206 = (bf16[512,1152]{1,0:T(8,128)(2,1)S(1)}, bf16[5,512,1152]{2,1,0:T(8,128)(2,1)}, bf16[512,1152]{1,0:T(8,128)(2,1)S(1)}, f32[512,1152]{1,0:T(8,128...) custom-call(s32[2]{0:T(128)S(1)} %copy-done.25, ...), custom_call_target="tpu_custom_call" | custom-call | flops 1024 | bytes 1024 | tf_op jit(solution)/shard_map/pallas_call | solution.py:216
  221.3 13.7 %shard_map.209 = (bf16[4608,1152]{1,0:T(8,128)(2,1)}, bf16[4,512,1152]{2,1,0:T(8,128)(2,1)}, bf16[4,512,1152]{2,1,0:T(8,128)(2,1)}) custom-call(s32[4]{0:T(128)S(1)} %pad_add_fusion.order, s32[7]{0:T(128)S(1)} %stack.155.starts, bf16[512,1152]{1,0:T(8,128)(2,1)S(1)} %copy-done.9, f32[4,1,1152]{2,1,0:T(1,128)S(1)} %copy.115.bias, ...), custom_call_target="tpu_custom_call" | custom-call | flops 1024 | bytes 1024 | tf_op jit(solution)/shard_map/pallas_call | solution.py:324
  235.0 8.0 %convolution_convert_fusion.1 = bf16[4,576,1152]{2,1,0:T(8,128)(2,1)} fusion(bf16[4,512,1152]{2,1,0:T(8,128)(2,1)} %get-tuple-element.138.hidden, s32[]{:T(128)S(6)} %select_n.364, bf16[512,1152]{1,0:T(8,128)(2,1)S(1)} %copy-done.12), kind=kOutput, calls=%fused_computation.5 | convolution fusion | flops 2720563200 | bytes 9109508 | tf_op jit(solution)/shard_map/jtd,te->jde/dot_general | solution.py:847
  254.3 28.5 %collective-permute-done.20.refs_1_ = bf16[576,1152]{1,0:T(8,128)(2,1)} collective-permute-done((bf16[576,1152]{1,0:T(8,128)(2,1)S(1)}, bf16[576,1152]{1,0:T(8,128)(2,1)}, u32[]{:S(2)}, u32[]{:S(2)}) %collective-permute-start.20) | collective-permute-done | bytes 1327136 | tf_op jit(solution)/shard_map/ppermute | solution.py:670
  283.4 28.5 %collective-permute-done.24.refs_5_ = bf16[576,1152]{1,0:T(8,128)(2,1)} collective-permute-done((bf16[576,1152]{1,0:T(8,128)(2,1)S(1)}, bf16[576,1152]{1,0:T(8,128)(2,1)}, u32[]{:S(2)}, u32[]{:S(2)}) %collective-permute-start.24) | collective-permute-done | bytes 1327136 | tf_op jit(solution)/shard_map/ppermute | solution.py:670
  327.2 21.9 %shard_map.210 = (bf16[4,512,1152]{2,1,0:T(8,128)(2,1)}, f32[4,1,1152]{2,1,0:T(1,128)S(1)}, bf16[512,1152]{1,0:T(8,128)(2,1)}, f32[2,1,1152]{2,1,0:T(1,128)S(1)}) custom-call(s32[4]{0:T(128)S(1)} %copy-done.27, s32[7]{0:T(128)S(1)} %copy-done.29, s32[2]{0:T(128)S(1)} %copy-done.25, bf16[4,512,1152]{2,1,0:T(8,128)(2,1)} %get-tuple-element.138.hidden, ...), custom_call_target="tpu_custom_call" | custom-call | flops 1024 | bytes 1024 | tf_op jit(solution)/shard_map/pallas_call | solution.py:404
  349.0 9.7 %fusion.10 = f32[4,576,1152]{2,1,0:T(8,128)} fusion(bf16[4,512,1152]{2,1,0:T(8,128)(2,1)} %get-tuple-element.138.hidden, s32[]{:T(128)S(6)} %select_n.363, bf16[512,1152]{1,0:T(8,128)(2,1)S(1)} %copy-done.13), kind=kOutput, calls=%fused_computation.29 | convolution fusion | flops 2717908992 | bytes 14417924 | tf_op jit(solution)/shard_map/jtd,te->jde/dot_general | solution.py:847
  358.7 9.1 %add_convert_fusion.1 = bf16[4,576,1152]{2,1,0:T(8,128)(2,1)} fusion(f32[4,576,1152]{2,1,0:T(8,128)} %fusion.10, bf16[4,576,1152]{2,1,0:T(8,128)(2,1)} %collective-permute-done.26), kind=kLoop, calls=%fused_computation.3 | loop fusion | flops 7962624 | bytes 21233664 | tf_op jit(solution)/shard_map/convert_element_type | solution.py:27
  388.6 15.5 %shard_map.211 = (f32[512,1152]{1,0:T(8,128)}, bf16[512,1152]{1,0:T(8,128)(2,1)S(1)}, f32[2,4,1152]{2,1,0:T(4,128)S(1)}) custom-call(s32[2]{0:T(128)S(1)} %copy-done.25, bf16[4,512,1152]{2,1,0:T(8,128)(2,1)} %get-tuple-element.148.d_pre, bf16[4,1152,1152]{2,1,0:T(8,128)(2,1)} %bitcast.304, f32[2,6,1152]{2,1,0:T(8,128)S(1)} %copy-done.7, ...), custom_call_target="tpu_custom_call" | custom-call | flops 1024 | bytes 1024 | tf_op jit(solution)/shard_map/pallas_call | solution.py:496
  418.9 7.7 fusion
  430.2 26.2 %shard_map.212 = (bf16[4,512,1152]{2,1,0:T(8,128)(2,1)}, f32[2,3,1152]{2,1,0:T(4,128)S(1)}) custom-call(s32[2]{0:T(128)S(1)} %copy-done.25, bf16[512,1152]{1,0:T(8,128)(2,1)S(1)} %get-tuple-element.158.d_proj, bf16[5,512,1152]{2,1,0:T(8,128)(2,1)} %get-tuple-element.159.parts, bf16[4,1152,1152]{2,1,0:T(8,128)(2,1)} %bitcast.300), custom_call_target="tpu_custom_call" | custom-call | flops 1024 | bytes 1024 | tf_op jit(solution)/shard_map/pallas_call | solution.py:563
  456.4 8.7 %convolution_convert_fusion = bf16[4,576,1152]{2,1,0:T(8,128)(2,1)} fusion(bf16[4,512,1152]{2,1,0:T(8,128)(2,1)} %get-tuple-element.174.d_qkv, bf16[1,512,576]{1,2,0:T(8,128)(2,1)} %bitcast.323, bf16[1,512,576]{1,2,0:T(8,128)(2,1)} %bitcast.324), kind=kOutput, calls=%fused_computation.4 | convolution fusion | flops 2724102144 | bytes 11206656 | tf_op jit(solution)/shard_map/jtd,jte->jde/dot_general | solution.py:847
  471.4 18.5 %collective-permute-start.35 = (bf16[2,144,1152]{2,1,0:T(8,128)(2,1)}, bf16[2,144,1152]{2,1,0:T(8,128)(2,1)}, u32[]{:S(2)}, u32[]{:S(2)}) collective-permute-start(bf16[2,144,1152]{2,1,0:T(8,128)(2,1)} %dynamic-slice_bitcast_fusion.12), channel_id=1, source_target_pairs={{0,8},{4,12},{8,0},{12,4},{16,24},{20,28},{24,16},{28,20},{1,9},{5... | collective-permute-start | bytes 1990664 | tf_op jit(solution)/shard_map/ppermute | solution.py:665
  498.5 21.3 %collective-permute-done.35 = bf16[2,144,1152]{2,1,0:T(8,128)(2,1)} collective-permute-done((bf16[2,144,1152]{2,1,0:T(8,128)(2,1)}, bf16[2,144,1152]{2,1,0:T(8,128)(2,1)}, u32[]{:S(2)}, u32[]{:S(2)}) %collective-permute-start.35) | collective-permute-done | bytes 663584 | tf_op jit(solution)/shard_map/ppermute | solution.py:665
  540.7 11.2 %shard_map.213 = (bf16[512,1152]{1,0:T(8,128)(2,1)}, f32[2,2,1152]{2,1,0:T(2,128)S(1)}) custom-call(bf16[4,512,1152]{2,1,0:T(8,128)(2,1)} %get-tuple-element.174.d_qkv, bf16[4,1152,1152]{2,1,0:T(8,128)(2,1)} %bitcast.301, f32[2,6,1152]{2,1,0:T(8,128)S(1)} %copy-done.7, bf16[512,1152]{1,0:T(8,128)(2,1)S(1)} %bitcast.298, f32[512,1152]{1,0:T(8,128)S(1)} %copy-done.2), custom_call_target="tpu_custom_call" | custom-call | flops 1024 | bytes 1024 | tf_op jit(solution)/shard_map/pallas_call | solution.py:623
  556.0 11.5 %collective-permute-done.39 = bf16[2,2,144,1152]{3,2,1,0:T(8,128)(2,1)} collective-permute-done((bf16[2,2,144,1152]{3,2,1,0:T(8,128)(2,1)}, bf16[2,2,144,1152]{3,2,1,0:T(8,128)(2,1)}, u32[]{:S(2)}, u32[]{:S(2)}) %collective-permute-start.39) | collective-permute-done | bytes 1327136 | tf_op jit(solution)/shard_map/ppermute | solution.py:670
  567.5 23.2 %collective-permute-done.41 = bf16[2,144,1152]{2,1,0:T(8,128)(2,1)S(1)} collective-permute-done((bf16[2,144,1152]{2,1,0:T(8,128)(2,1)S(1)}, bf16[2,144,1152]{2,1,0:T(8,128)(2,1)S(1)}, u32[]{:S(2)}, u32[]{:S(2)}) %collective-permute-start.41) | collective-permute-done | bytes 663584 | tf_op jit(solution)/shard_map/ppermute | solution.py:665
  600.5 9.6 %all_to_all.41 = f32[4,1,7488]{2,1,0:T(1,128)S(1)} all-to-all(f32[4,1,7488]{2,1,0:T(1,128)S(1)} %copy.132), channel_id=1, replica_groups=mesh['dp'=8,'fsdp'=4] {'fsdp'}, dimensions={0} | all-to-all | bytes 239616 | tf_op jit(solution)/shard_map/all_to_all | solution.py:1115
  620.8 28.7 %all-to-all-done.2 = f32[8,1,3960]{2,1,0:T(1,128)S(1)} async-done(((f32[8,1,3960]{2,1,0:T(1,128)}), f32[8,1,3960]{2,1,0:T(1,128)S(1)}, u32[]{:S(2)}, u32[]{:S(2)}) %all-to-all-start.2) | async-done | bytes 126752 | tf_op jit(solution)/shard_map/all_to_all | solution.py:1126
  650.5 9.5 %all_gather.40 = f32[864,128]{1,0:T(8,128)S(1)} all-gather(f32[216,128]{1,0:T(8,128)S(1)} %reshape.305), channel_id=1, replica_groups=mesh['dp'=8,'fsdp'=4] {'fsdp'}, dimensions={0}, use_global_device_ids=true | all-gather | bytes 552960 | tf_op jit(solution)/shard_map/all_gather | solution.py:1131
  664.1 8.3 %shard_map.214 = bf16[4,3,144,288]{3,2,1,0:T(8,128)(2,1)} custom-call(s32[1]{0:T(128)} %bitcast.103.at, bf16[1152,1152]{1,0:T(8,128)(2,1)} %bitcast.319, bf16[144,1152]{1,0:T(8,128)(2,1)S(1)} %copy-done.5, bf16[1152,1152]{1,0:T(8,128)(2,1)} %bitcast.316), custom_call_target="tpu_custom_call" | custom-call | flops 1024 | bytes 1024 | tf_op jit(solution)/shard_map/pallas_call | solution.py:890
  685.6 8.4 %shard_map.215 = bf16[4,3,144,288]{3,2,1,0:T(8,128)(2,1)} custom-call(s32[1]{0:T(128)} %bitcast.103.at, bf16[1152,1152]{1,0:T(8,128)(2,1)} %bitcast.320, bf16[144,1152]{1,0:T(8,128)(2,1)S(1)} %copy-done.4, bf16[1152,1152]{1,0:T(8,128)(2,1)} %bitcast.317), custom_call_target="tpu_custom_call" | custom-call | flops 1024 | bytes 1024 | tf_op jit(solution)/shard_map/pallas_call | solution.py:890
  702.2 17.4 %all_gather.43 = f32[1728,128]{1,0:T(8,128)} all-gather(f32[216,128]{1,0:T(8,128)S(1)} %reshape.312), channel_id=1, replica_groups=mesh['dp'=8,'fsdp'=4] {'dp'}, dimensions={0}, use_global_device_ids=true | all-gather | bytes 995328 | tf_op jit(solution)/shard_map/all_gather | solution.py:1155
  726.2 8.3 %shard_map.216 = bf16[4,3,144,288]{3,2,1,0:T(8,128)(2,1)} custom-call(s32[1]{0:T(128)} %bitcast.103.at, bf16[1152,1152]{1,0:T(8,128)(2,1)} %bitcast.321, bf16[144,1152]{1,0:T(8,128)(2,1)S(1)} %copy-done.3, bf16[1152,1152]{1,0:T(8,128)(2,1)} %bitcast.318), custom_call_target="tpu_custom_call" | custom-call | flops 1024 | bytes 1024 | tf_op jit(solution)/shard_map/pallas_call | solution.py:890
  745.3 11.6 %all-to-all-done.5 = bf16[4,3,144,288]{3,2,1,0:T(8,128)(2,1)} async-done(((bf16[4,3,144,288]{3,2,1,0:T(8,128)(2,1)}), bf16[4,3,144,288]{3,2,1,0:T(8,128)(2,1)}, u32[]{:S(2)}, u32[]{:S(2)}) %all-to-all-start.5) | async-done | bytes 995360 | tf_op jit(solution)/shard_map/all_to_all | solution.py:740
  (443 shorter events, 257.4 us)
Async XLA Ops:
  7.2 158.9 %all-gather.18.cloned.1.call-start = ((), (), s32[]{:S(2)}) async-start(), calls=%async_computation.9 | async-start | bytes 10948608 | tf_op jit(solution)/shard_map/all_gather | solution.py:749
  41.4 362.7 %all-gather.12.cloned.1.call-start = ((), (), s32[]{:S(2)}) async-start(), calls=%async_computation.6 | async-start | bytes 2985984 | tf_op jit(solution)/shard_map/all_gather | solution.py:798
  80.5 66.2 %collective-permute-start.10 = (bf16[576,1152]{1,0:T(8,128)(2,1)S(1)}, bf16[576,1152]{1,0:T(8,128)(2,1)}, u32[]{:S(2)}, u32[]{:S(2)}) collective-permute-start(bf16[576,1152]{1,0:T(8,128)(2,1)S(1)} %shard_map.207.refs_0_), channel_id=1, source_target_pairs={{0,4},{4,0},{8,12},{12,8},{16,20},{20,16},{24,28},{28,24},{1,5},{5... | collective-permute-start | bytes 3981320 | tf_op jit(solution)/shard_map/ppermute | solution.py:655
  80.6 33.9 %collective-permute-start.6 = (bf16[144,1152]{1,0:T(8,128)(2,1)S(1)}, bf16[144,1152]{1,0:T(8,128)(2,1)S(1)}, u32[]{:S(2)}, u32[]{:S(2)}) collective-permute-start(bf16[144,1152]{1,0:T(8,128)(2,1)S(1)} %get-tuple-element.120.refs_0_), channel_id=1, source_target_pairs={{0,8},{4,12},{8,16},{12,20},{16,24},{20,28},{24,0},{28,4},{1,9},{5... | collective-permute-start | bytes 995336 | tf_op jit(solution)/shard_map/ppermute | solution.py:660
  101.3 39.1 %collective-permute-start.7 = (bf16[144,1152]{1,0:T(8,128)(2,1)S(1)}, bf16[144,1152]{1,0:T(8,128)(2,1)S(1)}, u32[]{:S(2)}, u32[]{:S(2)}) collective-permute-start(bf16[144,1152]{1,0:T(8,128)(2,1)S(1)} %get-tuple-element.120.refs_0_), channel_id=1, source_target_pairs={{0,16},{4,20},{8,24},{12,28},{16,0},{20,4},{24,8},{28,12},{1,17},{... | collective-permute-start | bytes 995336 | tf_op jit(solution)/shard_map/ppermute | solution.py:660
  102.8 39.7 %collective-permute-start.8 = (bf16[144,1152]{1,0:T(8,128)(2,1)S(1)}, bf16[144,1152]{1,0:T(8,128)(2,1)S(1)}, u32[]{:S(2)}, u32[]{:S(2)}) collective-permute-start(bf16[144,1152]{1,0:T(8,128)(2,1)S(1)} %get-tuple-element.120.refs_0_), channel_id=1, source_target_pairs={{0,24},{4,28},{8,0},{12,4},{16,8},{20,12},{24,16},{28,20},{1,25},{... | collective-permute-start | bytes 995336 | tf_op jit(solution)/shard_map/ppermute | solution.py:660
  152.9 55.8 %collective-permute-start.11 = (bf16[576,1152]{1,0:T(8,128)(2,1)}, bf16[576,1152]{1,0:T(8,128)(2,1)}, u32[]{:S(2)}, u32[]{:S(2)}) collective-permute-start(bf16[576,1152]{1,0:T(8,128)(2,1)} %constant_dynamic-slice_fusion.8), channel_id=1, source_target_pairs={{0,1},{1,0},{2,3},{3,2},{4,5},{5,4},{6,7},{7,6},{8,9},{9,8},{10,11... | collective-permute-start | bytes 3981320 | tf_op jit(solution)/shard_map/ppermute | solution.py:670
  152.9 55.8 %collective-permute-start.12 = (bf16[576,1152]{1,0:T(8,128)(2,1)}, bf16[576,1152]{1,0:T(8,128)(2,1)}, u32[]{:S(2)}, u32[]{:S(2)}) collective-permute-start(bf16[576,1152]{1,0:T(8,128)(2,1)} %constant_dynamic-slice_fusion.8), channel_id=1, source_target_pairs={{0,2},{1,3},{2,0},{3,1},{4,6},{5,7},{6,4},{7,5},{8,10},{9,11},{10,... | collective-permute-start | bytes 3981320 | tf_op jit(solution)/shard_map/ppermute | solution.py:670
  154.4 59.7 %collective-permute-start.13 = (bf16[576,1152]{1,0:T(8,128)(2,1)}, bf16[576,1152]{1,0:T(8,128)(2,1)}, u32[]{:S(2)}, u32[]{:S(2)}) collective-permute-start(bf16[576,1152]{1,0:T(8,128)(2,1)} %constant_dynamic-slice_fusion.8), channel_id=1, source_target_pairs={{0,3},{1,2},{2,1},{3,0},{4,7},{5,6},{6,5},{7,4},{8,11},{9,10},{10,... | collective-permute-start | bytes 3981320 | tf_op jit(solution)/shard_map/ppermute | solution.py:670
  250.7 108.1 %collective-permute-start.26 = (bf16[4,576,1152]{2,1,0:T(8,128)(2,1)}, bf16[4,576,1152]{2,1,0:T(8,128)(2,1)}, u32[]{:S(2)}, u32[]{:S(2)}) collective-permute-start(bf16[4,576,1152]{2,1,0:T(8,128)(2,1)} %convolution_convert_fusion.1), channel_id=1, source_target_pairs={{0,4},{4,0},{8,12},{12,8},{16,20},{20,16},{24,28},{28,24},{1,5},{5... | collective-permute-start | bytes 15925256 | tf_op jit(solution)/shard_map/ppermute | solution.py:655
  250.8 32.1 %collective-permute-start.20 = (bf16[576,1152]{1,0:T(8,128)(2,1)S(1)}, bf16[576,1152]{1,0:T(8,128)(2,1)}, u32[]{:S(2)}, u32[]{:S(2)}) collective-permute-start(bf16[576,1152]{1,0:T(8,128)(2,1)S(1)} %constant_dynamic-slice_fusion.7), channel_id=1, source_target_pairs={{0,1},{1,0},{2,3},{3,2},{4,5},{5,4},{6,7},{7,6},{8,9},{9,8},{10,11... | collective-permute-start | bytes 3981320 | tf_op jit(solution)/shard_map/ppermute | solution.py:670
  251.5 31.4 %collective-permute-start.22 = (bf16[576,1152]{1,0:T(8,128)(2,1)S(1)}, bf16[576,1152]{1,0:T(8,128)(2,1)}, u32[]{:S(2)}, u32[]{:S(2)}) collective-permute-start(bf16[576,1152]{1,0:T(8,128)(2,1)S(1)} %constant_dynamic-slice_fusion.7), channel_id=1, source_target_pairs={{0,2},{1,3},{2,0},{3,1},{4,6},{5,7},{6,4},{7,5},{8,10},{9,11},{10,... | collective-permute-start | bytes 3981320 | tf_op jit(solution)/shard_map/ppermute | solution.py:670
  252.4 59.4 %collective-permute-start.24 = (bf16[576,1152]{1,0:T(8,128)(2,1)S(1)}, bf16[576,1152]{1,0:T(8,128)(2,1)}, u32[]{:S(2)}, u32[]{:S(2)}) collective-permute-start(bf16[576,1152]{1,0:T(8,128)(2,1)S(1)} %constant_dynamic-slice_fusion.7), channel_id=1, source_target_pairs={{0,3},{1,2},{2,1},{3,0},{4,7},{5,6},{6,5},{7,4},{8,11},{9,10},{10,... | collective-permute-start | bytes 3981320 | tf_op jit(solution)/shard_map/ppermute | solution.py:670
  282.9 41.0 %collective-permute-start.21 = (bf16[576,1152]{1,0:T(8,128)(2,1)}, bf16[576,1152]{1,0:T(8,128)(2,1)}, u32[]{:S(2)}, u32[]{:S(2)}) collective-permute-start(bf16[576,1152]{1,0:T(8,128)(2,1)} %collective-permute-done.20.refs_1_), channel_id=1, source_target_pairs={{0,4},{4,0},{8,12},{12,8},{16,20},{20,16},{24,28},{28,24},{1,5},{5... | collective-permute-start | bytes 3981320 | tf_op jit(solution)/shard_map/ppermute | solution.py:655
  282.9 41.0 %collective-permute-start.23 = (bf16[576,1152]{1,0:T(8,128)(2,1)}, bf16[576,1152]{1,0:T(8,128)(2,1)}, u32[]{:S(2)}, u32[]{:S(2)}) collective-permute-start(bf16[576,1152]{1,0:T(8,128)(2,1)} %collective-permute-done.22.refs_3_), channel_id=1, source_target_pairs={{0,4},{4,0},{8,12},{12,8},{16,20},{20,16},{24,28},{28,24},{1,5},{5... | collective-permute-start | bytes 3981320 | tf_op jit(solution)/shard_map/ppermute | solution.py:655
  323.8 132.6 %all-gather.14.cloned.1.call-start = ((), (), s32[]{:S(2)}) async-start(), calls=%async_computation.7 | async-start | bytes 2985984 | tf_op jit(solution)/shard_map/all_gather | solution.py:798
  379.1 33.0 %collective-permute-start.27 = (bf16[4,576,1152]{2,1,0:T(8,128)(2,1)}, bf16[4,576,1152]{2,1,0:T(8,128)(2,1)}, u32[]{:S(2)}, u32[]{:S(2)}) collective-permute-start(bf16[4,576,1152]{2,1,0:T(8,128)(2,1)} %fusion.1), channel_id=1, source_target_pairs={{0,4},{4,0},{8,12},{12,8},{16,20},{20,16},{24,28},{28,24},{1,5},{5... | collective-permute-start | bytes 15925256 | tf_op jit(solution)/shard_map/ppermute | solution.py:655
  379.5 31.5 %collective-permute-start.28 = (bf16[2,2,144,1152]{3,2,1,0:T(8,128)(2,1)}, bf16[2,2,144,1152]{3,2,1,0:T(8,128)(2,1)}, u32[]{:S(2)}, u32[]{:S(2)}) collective-permute-start(bf16[2,2,144,1152]{3,2,1,0:T(8,128)(2,1)} %dynamic-slice_bitcast_fusion.5), channel_id=1, source_target_pairs={{0,1},{1,0},{2,3},{3,2},{4,5},{5,4},{6,7},{7,6},{8,9},{9,8},{10,11... | collective-permute-start | bytes 3981320 | tf_op jit(solution)/shard_map/ppermute | solution.py:670
  380.6 31.6 %collective-permute-start.29 = (bf16[2,2,144,1152]{3,2,1,0:T(8,128)(2,1)}, bf16[2,2,144,1152]{3,2,1,0:T(8,128)(2,1)}, u32[]{:S(2)}, u32[]{:S(2)}) collective-permute-start(bf16[2,2,144,1152]{3,2,1,0:T(8,128)(2,1)} %dynamic-slice_bitcast_fusion.4), channel_id=1, source_target_pairs={{0,2},{1,3},{2,0},{3,1},{4,6},{5,7},{6,4},{7,5},{8,10},{9,11},{10,... | collective-permute-start | bytes 3981320 | tf_op jit(solution)/shard_map/ppermute | solution.py:670
  382.0 170.0 %all-gather.16.cloned.1.call-start = ((), (), s32[]{:S(2)}) async-start(), calls=%async_computation.8 | async-start | bytes 2985984 | tf_op jit(solution)/shard_map/all_gather | solution.py:798
  414.5 41.9 %collective-permute-start.30 = (bf16[2,144,1152]{2,1,0:T(8,128)(2,1)S(1)}, bf16[2,144,1152]{2,1,0:T(8,128)(2,1)}, u32[]{:S(2)}, u32[]{:S(2)}) collective-permute-start(bf16[2,144,1152]{2,1,0:T(8,128)(2,1)S(1)} %dynamic-slice_bitcast_fusion.14), channel_id=1, source_target_pairs={{0,2},{1,3},{2,0},{3,1},{4,6},{5,7},{6,4},{7,5},{8,10},{9,11},{10,... | collective-permute-start | bytes 1990664 | tf_op jit(solution)/shard_map/ppermute | solution.py:670
  418.7 37.7 %collective-permute-start.31 = (bf16[2,144,1152]{2,1,0:T(8,128)(2,1)S(1)}, bf16[2,144,1152]{2,1,0:T(8,128)(2,1)}, u32[]{:S(2)}, u32[]{:S(2)}) collective-permute-start(bf16[2,144,1152]{2,1,0:T(8,128)(2,1)S(1)} %dynamic-slice_bitcast_fusion.13), channel_id=1, source_target_pairs={{0,1},{1,0},{2,3},{3,2},{4,5},{5,4},{6,7},{7,6},{8,9},{9,8},{10,11... | collective-permute-start | bytes 1990664 | tf_op jit(solution)/shard_map/ppermute | solution.py:670
  465.1 54.7 %collective-permute-start.32 = (bf16[4,576,1152]{2,1,0:T(8,128)(2,1)}, bf16[4,576,1152]{2,1,0:T(8,128)(2,1)}, u32[]{:S(2)}, u32[]{:S(2)}) collective-permute-start(bf16[4,576,1152]{2,1,0:T(8,128)(2,1)} %convolution_convert_fusion), channel_id=1, source_target_pairs={{0,4},{4,0},{8,12},{12,8},{16,20},{20,16},{24,28},{28,24},{1,5},{5... | collective-permute-start | bytes 15925256 | tf_op jit(solution)/shard_map/ppermute | solution.py:655
  465.1 31.9 %collective-permute-start.33 = (bf16[2,2,144,1152]{3,2,1,0:T(8,128)(2,1)}, bf16[2,2,144,1152]{3,2,1,0:T(8,128)(2,1)}, u32[]{:S(2)}, u32[]{:S(2)}) collective-permute-start(bf16[2,2,144,1152]{3,2,1,0:T(8,128)(2,1)} %dynamic-slice_bitcast_fusion.3), channel_id=1, source_target_pairs={{0,1},{1,0},{2,3},{3,2},{4,5},{5,4},{6,7},{7,6},{8,9},{9,8},{10,11... | collective-permute-start | bytes 3981320 | tf_op jit(solution)/shard_map/ppermute | solution.py:670
  466.9 31.6 %collective-permute-start.34 = (bf16[2,2,144,1152]{3,2,1,0:T(8,128)(2,1)}, bf16[2,2,144,1152]{3,2,1,0:T(8,128)(2,1)}, u32[]{:S(2)}, u32[]{:S(2)}) collective-permute-start(bf16[2,2,144,1152]{3,2,1,0:T(8,128)(2,1)} %dynamic-slice_bitcast_fusion.2), channel_id=1, source_target_pairs={{0,2},{1,3},{2,0},{3,1},{4,6},{5,7},{6,4},{7,5},{8,10},{9,11},{10,... | collective-permute-start | bytes 3981320 | tf_op jit(solution)/shard_map/ppermute | solution.py:670
  471.4 48.4 %collective-permute-start.35 = (bf16[2,144,1152]{2,1,0:T(8,128)(2,1)}, bf16[2,144,1152]{2,1,0:T(8,128)(2,1)}, u32[]{:S(2)}, u32[]{:S(2)}) collective-permute-start(bf16[2,144,1152]{2,1,0:T(8,128)(2,1)} %dynamic-slice_bitcast_fusion.12), channel_id=1, source_target_pairs={{0,8},{4,12},{8,0},{12,4},{16,24},{20,28},{24,16},{28,20},{1,9},{5... | collective-permute-start | bytes 1990664 | tf_op jit(solution)/shard_map/ppermute | solution.py:665
  492.1 172.0 %all-gather.20.cloned.1.call-start = ((), (), s32[]{:S(2)}) async-start(), calls=%async_computation.10 | async-start | bytes 2985984 | tf_op jit(solution)/shard_map/all_gather | solution.py:843
  552.8 132.8 %all-gather.24.cloned.1.call-start = ((), (), s32[]{:S(2)}) async-start(), calls=%async_computation.12 | async-start | bytes 2985984 | tf_op jit(solution)/shard_map/all_gather | solution.py:843
  555.8 34.9 %collective-permute-start.41 = (bf16[2,144,1152]{2,1,0:T(8,128)(2,1)S(1)}, bf16[2,144,1152]{2,1,0:T(8,128)(2,1)S(1)}, u32[]{:S(2)}, u32[]{:S(2)}) collective-permute-start(bf16[2,144,1152]{2,1,0:T(8,128)(2,1)S(1)} %dynamic-slice_bitcast_fusion.9), channel_id=1, source_target_pairs={{0,8},{4,12},{8,0},{12,4},{16,24},{20,28},{24,16},{28,20},{1,9},{5... | collective-permute-start | bytes 1990664 | tf_op jit(solution)/shard_map/ppermute | solution.py:665
  616.5 33.0 %collective-permute-start.45 = (bf16[2,144,1152]{2,1,0:T(8,128)(2,1)S(1)}, bf16[2,144,1152]{2,1,0:T(8,128)(2,1)S(1)}, u32[]{:S(2)}, u32[]{:S(2)}) collective-permute-start(bf16[2,144,1152]{2,1,0:T(8,128)(2,1)S(1)} %dynamic-slice_bitcast_fusion.6), channel_id=1, source_target_pairs={{0,8},{4,12},{8,0},{12,4},{16,24},{20,28},{24,16},{28,20},{1,9},{5... | collective-permute-start | bytes 1990664 | tf_op jit(solution)/shard_map/ppermute | solution.py:665
  617.3 32.1 %all-to-all-start.2 = ((f32[8,1,3960]{2,1,0:T(1,128)}), f32[8,1,3960]{2,1,0:T(1,128)S(1)}, u32[]{:S(2)}, u32[]{:S(2)}) async-start(f32[8,1,3960]{2,1,0:T(1,128)} %all_to_all.29), calls=%async_computation.2 | async-start | bytes 253952 | tf_op jit(solution)/shard_map/all_to_all | solution.py:1126
  620.7 105.4 %all-gather.22.cloned.1.call-start = ((), (), s32[]{:S(2)}) async-start(), calls=%async_computation.11 | async-start | bytes 2985984 | tf_op jit(solution)/shard_map/all_gather | solution.py:843
  (109 other events, 1277.6 us)
Sparse Core Ops, SparseCore 0:
  34.3 128.3 all-gather.17
  324.0 49.9 all-gather.11
  382.1 48.9 all-gather.13
  492.2 35.7 all-gather.15
  552.9 38.7 all-gather.19
  613.8 38.4 all-gather.23
  674.4 33.7 all-gather.21

commit v11 on v10

--- a/solution.py
+++ b/solution.py
@@ -122,34 +122,25 @@
 
 def attention_kernel(
     frames,
+    cuts,
     counts,
+    starts,
     tokens,
     cotangent,
     mods,
     bias,
-    blocks,
-    attn_in,
-    parts,
-    mixed_low,
-    proj_out,
-    resid_out,
-    mlp_in,
-    d_branch,
-    d_branch_sum,
-    mixed,
-    whole,
-    semaphores,
+    *refs,
 ):
+    whole_out, attn_in, parts, mixed_low, proj_out, resid_out, mlp_in = refs[-13:-6]
+    d_branch, d_branch_sum, mixed, whole, semaphores, store_semaphore = refs[-6:]
+    pieces = refs[:-13]
     rows, width = tokens.shape
-    clip = pl.program_id(0)
-    loads = [
-        pltpu.make_async_copy(blocks.at[at], whole.at[at], semaphores.at[at]) for at in range(4)
-    ]
+    clip, clips = pl.program_id(0), pl.num_programs(0)
+    store = pltpu.make_async_copy(whole, whole_out, store_semaphore)
 
     @pl.when(clip == 0)
     def _():
-        for load in loads:
-            load.start()
+        start_loads(cuts, starts, pieces, whole, semaphores)
 
     tile = min(rows, 128)
     count = counts[clip]
@@ -164,19 +155,20 @@
         part_sum = column_sum(wide(branch_back))
         d_branch_sum[0] = part_sum if first == 0 else d_branch_sum[0] + part_sum
 
+    wait_loads([cuts], starts, pieces, whole, semaphores)
+
     @pl.when(clip == 0)
     def _():
-        for load in loads:
-            load.wait()
+        store.start()
 
     scale = (width // HEADS) ** -0.5
     source = attn_in[...]
     for low, high in column_cuts(width):
         span = slice(low, high)
-        query = (dot_nn(source, whole[0, :, span]) + bias[0:1, span]) * scale
+        query = (dot_nn(source, whole[0 * width : 1 * width, span]) + bias[0:1, span]) * scale
         parts[0, :, span], parts[1, :, span] = split_high(query)
-        parts[2, :, span], parts[3, :, span] = split_high(dot_nn(source, whole[1, :, span]))
-        parts[4, :, span] = narrow(dot_nn(source, whole[2, :, span]) + bias[2:3, span])
+        parts[2, :, span], parts[3, :, span] = split_high(dot_nn(source, whole[1 * width : 2 * width, span]))
+        parts[4, :, span] = narrow(dot_nn(source, whole[2 * width : 3 * width, span]) + bias[2:3, span])
     offset = score_offset(count, tile, frames, 1)
     mixed[...] = jnp.zeros_like(mixed)
     for first in range(0, rows, tile):
@@ -197,7 +189,7 @@
     source = mixed_low[...]
     for low, high in column_cuts(width):
         span = slice(low, high)
-        proj_out[:, span] = dot_nn(source, whole[3, :, span]) + bias[3:4, span]
+        proj_out[:, span] = dot_nn(source, whole[3 * width : 4 * width, span]) + bias[3:4, span]
     for first in range(0, rows, tile):
         span = slice(first, first + tile)
         resid = wide(tokens[span]) + valid_rows(count, tile, frames) * gate_one * proj_out[span]
@@ -205,8 +197,13 @@
         normed, _ = norm_parts(resid)
         mlp_in[span] = narrow(normed * (1.0 + scale_two) + shift_two)
 
-
-def run_attention(frames, counts, tokens, cotangent, mods, bias, blocks):
+    @pl.when(clip == clips - 1)
+    def _():
+        store.wait()
+
+
+def run_attention(frames, counts, tokens, cotangent, mods, bias, gathered):
+    pieces, cuts, starts = gathered
     total, width = tokens.shape
     clips = mods.shape[0]
     rows = total // clips
@@ -214,17 +211,19 @@
     low = jax.ShapeDtypeStruct((total, width), jnp.bfloat16)
     full = jax.ShapeDtypeStruct((total, width), jnp.float32)
     return pl.pallas_call(
-        functools.partial(attention_kernel, frames),
+        functools.partial(attention_kernel, frames, cuts),
         grid=(clips,),
         in_specs=[
+            pl.BlockSpec(memory_space=pltpu.SMEM),
             pl.BlockSpec(memory_space=pltpu.SMEM),
             clip_rows,
             clip_rows,
             spec((1,) + mods.shape[1:], lambda clip: (clip, 0, 0)),
             held(bias.shape),
+        ]
+        + [pl.BlockSpec(memory_space=pl.ANY)] * len(pieces),
+        out_specs=[
             pl.BlockSpec(memory_space=pl.ANY),
-        ],
-        out_specs=[
             clip_rows,
             spec((5, rows, width), lambda clip: (0, clip, 0)),
             clip_rows,
@@ -235,6 +234,7 @@
             spec((1, 1, width), lambda clip: (clip, 0, 0)),
         ],
         out_shape=[
+            jax.ShapeDtypeStruct((4 * width, width), jnp.bfloat16),
             low,
             jax.ShapeDtypeStruct((5, total, width), jnp.bfloat16),
             low,
@@ -246,12 +246,13 @@
         ],
         scratch_shapes=[
             pltpu.VMEM((rows, width), jnp.float32),
-            pltpu.VMEM(blocks.shape, jnp.bfloat16),
-            pltpu.SemaphoreType.DMA((4,)),
+            pltpu.VMEM((4 * width, width), jnp.bfloat16),
+            pltpu.SemaphoreType.DMA((len(cuts),)),
+            pltpu.SemaphoreType.DMA,
         ],
         compiler_params=pltpu.CompilerParams(vmem_limit_bytes=vmem_bytes),
         cost_estimate=little_cost,
-    )(counts, tokens, cotangent, mods, bias, blocks)
+    )(counts, stacked(starts), tokens, cotangent, mods, bias, *pieces)
 
 
 def stacked(numbers):
@@ -757,6 +758,37 @@
     chunk = found[0].shape[0]
     starts = [(chip - step) % chips * (chunk // 16) for step in range(chips)]
     return place(found, [(step, 0, chunk) for step in range(chips)], starts, chips * chunk)
+
+
+def gather_first(rows, group):
+    ranks, at = lax.axis_size("fsdp"), lax.axis_index("fsdp")
+    total = rows.shape[-1]
+    if ranks != group:
+        blocks = gather_blocks(rows, group).reshape(group * total, total)
+        for _ in range(3):
+            (blocks,) = yield (blocks,)
+        yield [blocks], [(0, 0, group * total)], [0]
+        return
+    chips = lax.axis_size("dp") // 2
+    core = lax.axis_index("dp") % 2
+    chunk = rows.shape[0]
+    found = yield tuple(chip_shift(rows, step) for step in range(1, chips))
+    line = join_line([rows, *found])
+    low_in, high_in = yield (rank_swap(line, 1), rank_swap(line, 2))
+    half = total // 4
+    parts = [line, low_in, high_in]
+    others = [core_swap(part) for part in parts]
+    parts += yield (rank_swap(high_in[:half], 1), rank_swap(low_in[half:], 2))
+    others += [core_swap(part) for part in parts[3:]]
+    cuts, starts = [], []
+    for side, family in ((core, 0), (1 - core, len(parts))):
+        for index, part in enumerate(parts):
+            bits, first_chip = ((0, 0), (1, 0), (2, 0), (3, 0), (3, chips // 2))[index]
+            for step in range(part.shape[0] // chunk):
+                cuts.append((family + index, step * chunk, chunk))
+                row = (at ^ bits) * (2 * chips) + 2 * (first_chip + step) + side
+                starts.append(row * (chunk // 16))
+    yield parts + others, cuts, starts
 
 
 def gather_second(rows, group):
@@ -951,7 +983,6 @@
     first_parts = lax.all_gather(packed([cond_low, narrow(biases)], 16), "dp", axis=0, tiled=True)
     weight_panels, first_parts = tie(weight_panels, first_parts)
     attn_rows, one_rows, two_rows = weight_rows.send(weight_panels)
-    attn_w = gather_blocks(attn_rows, group)
 
     first_parts = first_parts.reshape(dp_count, -1)
     cond_all = first_parts[:, : clip_count * width].reshape(all_clips, width)
@@ -960,20 +991,33 @@
     cond_cols = wide(lax.dynamic_slice_in_dim(cond_all, rank_at * col_part, col_part, 1))
     mod_parts = fast_dot("cr,jre->cje", cond_rows, low_weights[:mod_count])
     mod_parts = lax.all_to_all(mod_parts, "dp", 0, 0, tiled=True)
-    mod_parts, one_rows = tie(mod_parts, one_rows)
-    one_steps = gather_second(one_rows, group)
-    one_parts = next(one_steps)
+    roots = jnp.stack([narrow(left_roots[mod_count:]), narrow(right_roots[mod_count:])])
+    mod_parts, attn_rows, roots = tie(mod_parts, attn_rows, roots)
+    attn_steps = gather_first(attn_rows, group)
+    attn_parts = next(attn_steps)
+    root_rows = own_rows(roots.reshape(-1, group, row_part, col_part), group)
+    root_panels = next(root_rows)
     mod_cols = jnp.sum(mod_parts.reshape(dp_count, clip_count, mod_count, col_part), axis=0)
     left_cond = jnp.einsum("jrk,ck->jrc", left_roots[:mod_count], cond_cols, precision=precise)
     mod_size, bias_size = mod_cols.size, dp_count * bias_part
     second_parts = lax.all_gather(
         packed([mod_cols, bias_rows, left_cond], 8), "fsdp", axis=0, tiled=True
     )
-    second_parts, one_parts, two_rows = tie(second_parts, one_parts, two_rows)
-    two_steps = gather_second(two_rows, group)
-    two_parts = next(two_steps)
-    one_parts = one_steps.send(one_steps.send(one_parts))
-    two_parts = two_steps.send(two_parts)
+    second_parts, attn_parts, one_rows = tie(second_parts, attn_parts, one_rows)
+    attn_parts = attn_steps.send(attn_parts)
+    one_steps = gather_second(one_rows, group)
+    one_parts = next(one_steps)
+    root_rows = root_rows.send(root_panels)
+    attn_parts, root_rows = tie(attn_parts, root_rows)
+    attn_parts = attn_steps.send(attn_parts)
+    one_parts = one_steps.send(one_parts)
+    attn_parts, one_parts, two_rows = tie(attn_parts, one_parts, two_rows)
+    one_parts = one_steps.send(one_parts)
+    weight_steps = gather_second(two_rows, group)
+    two_w_parts = next(weight_steps)
+    gathered = attn_steps.send(attn_parts)
+    left_rows, right_rows = jnp.split(root_rows, 2)
+    right_wholes = [gather_own(rows[None], group)[0] for rows in right_rows]
     second_parts = second_parts.reshape(ranks, -1)
     mods = second_parts[:, :mod_size].reshape(ranks, clip_count, mod_count, col_part)
     mods = mods.transpose(1, 2, 0, 3).reshape(clip_count, mod_count, width)
@@ -987,19 +1031,17 @@
         [bias_all[6:7], jnp.zeros((1, width), jnp.float32), bias_all[7:14]]
     )
 
-    roots = jnp.stack([narrow(left_roots[mod_count:]), narrow(right_roots[mod_count:])])
-    mods, roots, two_parts = tie(mods, roots, two_parts)
-    two_parts = two_steps.send(two_parts)
-    root_rows = own_rows(roots.reshape(-1, group, row_part, col_part), group)
-    root_panels = next(root_rows)
-    attn_in, parts, mixed, proj, resid, mlp_in, d_branch, d_branch_sums = run_attention(
-        frames, frame_counts, stream, grad_out, mods, bias_table, attn_w
-    )
-    mlp_in, one_parts = tie(mlp_in, one_parts)
+    attn_w, attn_in, parts, mixed, proj, resid, mlp_in, d_branch, d_branch_sums = run_attention(
+        frames, frame_counts, stream, grad_out, mods, bias_table, gathered
+    )
+    attn_w = attn_w.reshape(group, width, width)
+    mlp_in, two_w_parts = tie(mlp_in, two_w_parts)
+    two_w_parts = weight_steps.send(two_w_parts)
+    mlp_in, two_w_parts = tie(mlp_in, two_w_parts)
+    two_w_parts = weight_steps.send(two_w_parts)
     one_w, hidden, slope = run_hidden(mlp_in, one_steps.send(one_parts), bias_table[4:8, None])
     one_w = one_w.reshape(group, width, width)
 
-    weight_steps, two_w_parts = two_steps, two_parts
     two_steps = sum_blocks(
         lambda left: fast_dot("jtd,te->jde", left, d_branch),
         lambda first, size: lax.dynamic_slice_in_dim(hidden, first, size, 2),
@@ -1007,13 +1049,9 @@
         group,
     )
     two_parts = next(two_steps)
-    hidden, two_parts, root_panels = tie(hidden, two_parts, root_panels)
+    hidden, two_parts, right_wholes[2] = tie(hidden, two_parts, right_wholes[2])
     two_parts = two_steps.send(two_parts)
-    root_rows = root_rows.send(root_panels)
     gathered = weight_steps.send(two_w_parts)
-    hidden, root_rows = tie(hidden, root_rows)
-    left_rows, right_rows = jnp.split(root_rows, 2)
-    right_wholes = [gather_own(rows[None], group)[0] for rows in right_rows]
     d_pre, d_pre_sums, block_out, d_gate_two = run_branch(
         frames,
         frame_counts,
@@ -1026,7 +1064,7 @@
         resid,
         grad_out,
     )
-    d_pre, two_parts = tie(d_pre, two_parts)
+    d_pre, two_parts, right_wholes[1] = tie(d_pre, two_parts, right_wholes[1])
     two_parts = two_steps.send(two_parts)
     d_pre, two_parts = tie(d_pre, two_parts)
     two_parts = two_steps.send(two_parts)
@@ -1042,16 +1080,17 @@
     d_resid, d_proj, resid_sums = run_resid(
         frames, frame_counts, d_pre, one_w, mods, resid, grad_out, proj
     )
-    d_proj, one_parts, two_parts, right_wholes[2] = tie(
-        d_proj, one_parts, two_parts, right_wholes[2]
+    d_proj, one_parts, two_parts, right_wholes[0] = tie(
+        d_proj, one_parts, two_parts, right_wholes[0]
     )
     two_parts = two_steps.send(two_parts)
     one_parts = one_steps.send(one_parts)
     d_proj, one_parts = tie(d_proj, one_parts)
     one_parts = one_steps.send(one_parts)
     d_heads, head_sums = run_attention_back(frames, frame_counts, d_proj, parts, attn_w)
-    d_heads, two_parts, right_wholes[1] = tie(d_heads, two_parts, right_wholes[1])
+    d_heads, two_parts, one_parts = tie(d_heads, two_parts, one_parts)
     two_parts = two_steps.send(two_parts)
+    one_parts = one_steps.send(one_parts)
     attn_steps = sum_blocks(
         lambda left: fast_dot("jtd,jte->jde", left, d_heads),
         lambda first, size: jnp.stack(
@@ -1063,16 +1102,13 @@
     attn_parts = next(attn_steps)
     d_heads, attn_parts = tie(d_heads, attn_parts)
     attn_parts = attn_steps.send(attn_parts)
-    d_heads, attn_parts, one_parts, two_parts = tie(d_heads, attn_parts, one_parts, two_parts)
+    d_heads, attn_parts, two_parts = tie(d_heads, attn_parts, two_parts)
     two_parts = two_steps.send(two_parts)
-    one_parts = one_steps.send(one_parts)
     attn_parts = attn_steps.send(attn_parts)
     d_heads, attn_parts = tie(d_heads, attn_parts)
     attn_parts = attn_steps.send(attn_parts)
     input_grad, input_sums = run_input(d_heads, attn_w, mods, stream, d_resid)
-    input_sums, one_parts, two_parts, right_wholes[0] = tie(
-        input_sums, one_parts, two_parts, right_wholes[0]
-    )
+    input_sums, one_parts, two_parts = tie(input_sums, one_parts, two_parts)
     whole_two = two_steps.send(two_parts)
     one_parts = one_steps.send(one_parts)
     input_sums, attn_parts, one_parts = tie(input_sums, attn_parts, one_parts)

time: 788 us -> 792 us (level)
  waiting for transfers between devices: 242 us -> 263 us
  starting transfers between devices: 96.2 us -> 81.9 us
  other arithmetic: 68.4 us -> 58.9 us
    ppermute x24 -> x28, waiting for transfers between devices: 94.8 us -> 112 us  [rank_swap(): return lax.ppermute(array, 'fsdp', [(at, at ^ bits) for at in range(count)])]
    all_gather x3, waiting for transfers between devices: 0.01 us -> 15.3 us  [gather_own(): return lax.all_gather(rows, 'dp', axis=1, tiled=True)]
    ppermute x6, starting transfers between devices: 18.6 us -> 5.33 us  [chip_swap(): lax.ppermute(array, 'dp', [(at, at ^ 2 * bits) for at in range(count)])]
    ppermute x6 -> x9, waiting for transfers between devices: 47.7 us -> 38.7 us  [chip_shift(): lax.ppermute(array, 'dp', [(at, (at + 2 * step) % count) for at in range(...]
    convert_element_type x22 -> x21, other arithmetic: 37 us -> 28.6 us  [narrow(): return array.astype(jnp.bfloat16)]
    ppermute x6 -> x9, starting transfers between devices: 27.2 us -> 22.6 us  [chip_shift(): lax.ppermute(array, 'dp', [(at, (at + 2 * step) % count) for at in range(...]
    unnamed x166 -> x128, local copies, waits for them, and re-layouts: 16.4 us -> 13.7 us
    ppermute x24 -> x28, starting transfers between devices: 27.5 us -> 29.9 us  [rank_swap(): return lax.ppermute(array, 'fsdp', [(at, at ^ bits) for at in range(count)])]
  transfers between devices with their start and end apart: 59 -> 70, of which waited for: 21 -> 23; matrix products, arithmetic and copies ran while one was open for 20% -> 16% of each run, Pallas kernels for 20% -> 20%
where the time goes in v11:
time: 792 us; the launch traced here: 782 us
  waiting for transfers between devices  263 us (33%)
  Pallas kernels  167 us (21%)
  starting transfers between devices  81.9 us (10%)
  local copies, waits for them, and re-layouts  79.1 us (10%)
  blocking collectives  61.9 us (8%)
  other arithmetic  58.9 us (7%)
  matrix products  53.5 us (7%)
  between operations  16.2 us (2%)
    ppermute x28, waiting for transfers between devices, rank_swap(): return lax.ppermute(array, 'fsdp', [(at, at ^ bits) for at in range(count)])  112 us
    dot_general x7, matrix products, fast_dot(): jnp.einsum(subscripts, left, right, preferred_element_type=jnp.float32)  42.1 us
    pallas_call x1, Pallas kernels, run_attention(): pl.pallas_call(functools.partial(attention_kernel, frames, cuts), grid=(c...  40.6 us
    ppermute x6, waiting for transfers between devices, chip_swap(): lax.ppermute(array, 'dp', [(at, at ^ 2 * bits) for at in range(count)])  39.3 us
    ppermute x9, waiting for transfers between devices, chip_shift(): lax.ppermute(array, 'dp', [(at, (at + 2 * step) % count) for at in range(...  38.7 us
    all_to_all x1, waiting for transfers between devices, per_device(): from_rows = lax.all_to_all(to_rows, 'dp', 0, 0, tiled=True)  31.5 us
    ppermute x28, starting transfers between devices, rank_swap(): return lax.ppermute(array, 'fsdp', [(at, at ^ bits) for at in range(count)])  29.9 us
    convert_element_type x21, other arithmetic, narrow(): return array.astype(jnp.bfloat16)  28.6 us
  transfers between devices with their start and end apart: 70, of which 23 were waited for; matrix products, arithmetic and copies ran while one was open for 16% of the time, Pallas kernels for 20%

profile of v11, /device:TPU:0, one launch (start us, length us, event | category | flops | bytes accessed | tf_op | source)
XLA Modules:
  0.0 782.4 jit_solution(16643239642405565804)
XLA Ops:
  21.3 14.6 %all_gather.30 = bf16[256,128]{1,0:T(8,128)(2,1)S(1)} all-gather(bf16[32,128]{1,0:T(8,128)(2,1)S(1)} %fusion.87), channel_id=1, replica_groups=mesh['dp'=8,'fsdp'=4] {'dp'}, dimensions={0}, use_global_device_ids=true | all-gather | bytes 73728 | tf_op jit(solution)/shard_map/all_gather | solution.py:983
  65.1 10.5 %all_gather.31 = f32[672,128]{1,0:T(8,128)} all-gather(f32[168,128]{1,0:T(8,128)S(1)} %pad_bitcast_fusion), channel_id=1, replica_groups=mesh['dp'=8,'fsdp'=4] {'fsdp'}, dimensions={0}, use_global_device_ids=true | all-gather | bytes 430080 | tf_op jit(solution)/shard_map/all_gather | solution.py:1003
  75.6 9.8 %collective-permute-done.4.refs_2_ = bf16[144,1152]{1,0:T(8,128)(2,1)S(1)} collective-permute-done((bf16[144,1152]{1,0:T(8,128)(2,1)S(1)}, bf16[144,1152]{1,0:T(8,128)(2,1)S(1)}, u32[]{:S(2)}, u32[]{:S(2)}) %collective-permute-start.4) | collective-permute-done | bytes 331808 | tf_op jit(solution)/shard_map/ppermute | solution.py:661
  106.5 11.4 %collective-permute-done.14.refs_2_ = bf16[144,1152]{1,0:T(8,128)(2,1)S(1)} collective-permute-done((bf16[144,1152]{1,0:T(8,128)(2,1)S(1)}, bf16[144,1152]{1,0:T(8,128)(2,1)S(1)}, u32[]{:S(2)}, u32[]{:S(2)}) %collective-permute-start.14) | collective-permute-done | bytes 331808 | tf_op jit(solution)/shard_map/ppermute | solution.py:661
  120.5 13.7 %collective-permute-done.10 = bf16[6,144,288]{2,1,0:T(8,128)(2,1)S(1)} collective-permute-done((bf16[6,144,288]{2,1,0:T(8,128)(2,1)S(1)}, bf16[6,144,288]{2,1,0:T(8,128)(2,1)S(1)}, u32[]{:S(2)}, u32[]{:S(2)}) %collective-permute-start.10) | collective-permute-done | bytes 497696 | tf_op jit(solution)/shard_map/ppermute | solution.py:671
  134.2 12.2 %collective-permute-done.8 = bf16[6,144,288]{2,1,0:T(8,128)(2,1)S(1)} collective-permute-done((bf16[6,144,288]{2,1,0:T(8,128)(2,1)S(1)}, bf16[6,144,288]{2,1,0:T(8,128)(2,1)S(1)}, u32[]{:S(2)}, u32[]{:S(2)}) %collective-permute-start.8) | collective-permute-done | bytes 497696 | tf_op jit(solution)/shard_map/ppermute | solution.py:671
  166.5 9.3 %collective-permute-done.11.refs_3_ = bf16[288,1152]{1,0:T(8,128)(2,1)} collective-permute-done((bf16[288,1152]{1,0:T(8,128)(2,1)}, bf16[288,1152]{1,0:T(8,128)(2,1)}, u32[]{:S(2)}, u32[]{:S(2)}) %collective-permute-start.11) | collective-permute-done | bytes 663584 | tf_op jit(solution)/shard_map/ppermute | solution.py:671
  179.9 7.7 collective-permute-start.22
  190.1 11.6 %collective-permute-done.22.refs_1_ = bf16[144,1152]{1,0:T(8,128)(2,1)S(1)} collective-permute-done((bf16[144,1152]{1,0:T(8,128)(2,1)}, bf16[144,1152]{1,0:T(8,128)(2,1)S(1)}, u32[]{:S(2)}, u32[]{:S(2)}) %collective-permute-start.22) | collective-permute-done | bytes 331808 | tf_op jit(solution)/shard_map/ppermute | solution.py:661
  208.7 40.6 %shard_map.207 = (bf16[4608,1152]{1,0:T(8,128)(2,1)}, bf16[512,1152]{1,0:T(8,128)(2,1)S(1)}, bf16[5,512,1152]{2,1,0:T(8,128)(2,1)}, bf16[512,1152]{1,0:T(8,128)(...) custom-call(s32[2]{0:T(128)S(1)} %copy-done.14, ...), custom_call_target="tpu_custom_call" | custom-call | flops 1024 | bytes 1024 | tf_op jit(solution)/shard_map/pallas_call | solution.py:213
  252.1 9.4 %collective-permute-done.30.refs_5_ = bf16[576,1152]{1,0:T(8,128)(2,1)} collective-permute-done((bf16[576,1152]{1,0:T(8,128)(2,1)}, bf16[576,1152]{1,0:T(8,128)(2,1)}, u32[]{:S(2)}, u32[]{:S(2)}) %collective-permute-start.30) | collective-permute-done | bytes 1327136 | tf_op jit(solution)/shard_map/ppermute | solution.py:671
  265.5 14.1 %shard_map.210 = (bf16[4608,1152]{1,0:T(8,128)(2,1)}, bf16[4,512,1152]{2,1,0:T(8,128)(2,1)}, bf16[4,512,1152]{2,1,0:T(8,128)(2,1)}) custom-call(s32[4]{0:T(128)S(1)} %pad_add_fusion.order, s32[7]{0:T(128)S(1)} %stack.259.starts, bf16[512,1152]{1,0:T(8,128)(2,1)S(1)} %copy-done.5, f32[4,1,1152]{2,1,0:T(1,128)S(1)} %copy.119.bias, ...), custom_call_target="tpu_custom_call" | custom-call | flops 1024 | bytes 1024 | tf_op jit(solution)/shard_map/pallas_call | solution.py:325
  279.6 7.9 %convolution_convert_fusion.1 = bf16[4,576,1152]{2,1,0:T(8,128)(2,1)} fusion(bf16[4,512,1152]{2,1,0:T(8,128)(2,1)} %get-tuple-element.142.hidden, s32[]{:T(128)S(6)} %select_n.390, bf16[512,1152]{1,0:T(8,128)(2,1)S(1)} %copy-done.10), kind=kOutput, calls=%fused_computation.5 | convolution fusion | flops 2720563200 | bytes 9109508 | tf_op jit(solution)/shard_map/jtd,te->jde/dot_general | solution.py:879
  293.5 28.5 %collective-permute-done.32.refs_1_ = bf16[576,1152]{1,0:T(8,128)(2,1)} collective-permute-done((bf16[576,1152]{1,0:T(8,128)(2,1)S(1)}, bf16[576,1152]{1,0:T(8,128)(2,1)}, u32[]{:S(2)}, u32[]{:S(2)}) %collective-permute-start.32) | collective-permute-done | bytes 1327136 | tf_op jit(solution)/shard_map/ppermute | solution.py:671
  322.0 29.6 %collective-permute-done.34.refs_3_ = bf16[576,1152]{1,0:T(8,128)(2,1)} collective-permute-done((bf16[576,1152]{1,0:T(8,128)(2,1)S(1)}, bf16[576,1152]{1,0:T(8,128)(2,1)}, u32[]{:S(2)}, u32[]{:S(2)}) %collective-permute-start.34) | collective-permute-done | bytes 1327136 | tf_op jit(solution)/shard_map/ppermute | solution.py:671
  358.1 22.1 %shard_map.211 = (bf16[4,512,1152]{2,1,0:T(8,128)(2,1)}, f32[4,1,1152]{2,1,0:T(1,128)S(1)}, bf16[512,1152]{1,0:T(8,128)(2,1)}, f32[2,1,1152]{2,1,0:T(1,128)S(1)}) custom-call(s32[4]{0:T(128)S(1)} %pad_add_fusion.order, s32[7]{0:T(128)S(1)} %stack.259.starts, s32[2]{0:T(128)S(1)} %copy-done.14, bf16[4,512,1152]{2,1,0:T(8,128)(2,1)} %get-tuple-element.142.hidden, ...), custom_call_target="tpu_custom_call" | custom-call | flops 1024 | bytes 1024 | tf_op jit(solution)/shard_map/pallas_call | solution.py:405
  380.2 7.7 add_convert_fusion.1
  399.8 15.7 %shard_map.212 = (f32[512,1152]{1,0:T(8,128)}, bf16[512,1152]{1,0:T(8,128)(2,1)S(1)}, f32[2,4,1152]{2,1,0:T(4,128)S(1)}) custom-call(s32[2]{0:T(128)S(1)} %copy-done.14, bf16[4,512,1152]{2,1,0:T(8,128)(2,1)} %get-tuple-element.152.d_pre, bf16[4,1152,1152]{2,1,0:T(8,128)(2,1)} %bitcast.348, f32[2,6,1152]{2,1,0:T(8,128)S(1)} %broadcast_add_fusion.mods, ...), custom_call_target="tpu_custom_call" | custom-call | flops 1024 | bytes 1024 | tf_op jit(solution)/shard_map/pallas_call | solution.py:497
  416.5 15.3 %all-gather.14.cloned.1.call-done = bf16[1,1152,1152]{2,1,0:T(8,128)(2,1)} async-done(((bf16[1,144,1152]{2,1,0:T(8,128)(2,1)}), bf16[1,1152,1152]{2,1,0:T(8,128)(2,1)}) %all-gather.14.cloned.1.call-update) | async-done | bytes 2654224 | tf_op jit(solution)/shard_map/all_gather | solution.py:830
  436.8 7.7 fusion
  462.6 26.3 %shard_map.213 = (bf16[4,512,1152]{2,1,0:T(8,128)(2,1)}, f32[2,3,1152]{2,1,0:T(4,128)S(1)}) custom-call(s32[2]{0:T(128)S(1)} %copy-done.14, bf16[512,1152]{1,0:T(8,128)(2,1)S(1)} %copy-done.9, bf16[5,512,1152]{2,1,0:T(8,128)(2,1)} %get-tuple-element.162.parts, bf16[4,1152,1152]{2,1,0:T(8,128)(2,1)} %bitcast.344), custom_call_target="tpu_custom_call" | custom-call | flops 1024 | bytes 1024 | tf_op jit(solution)/shard_map/pallas_call | solution.py:564
  515.1 9.3 %collective-permute-done.47 = bf16[2,144,1152]{2,1,0:T(8,128)(2,1)S(1)} collective-permute-done((bf16[2,144,1152]{2,1,0:T(8,128)(2,1)S(1)}, bf16[2,144,1152]{2,1,0:T(8,128)(2,1)S(1)}, u32[]{:S(2)}, u32[]{:S(2)}) %collective-permute-start.47) | collective-permute-done | bytes 663584 | tf_op jit(solution)/shard_map/ppermute | solution.py:666
  539.5 11.3 %shard_map.214 = (bf16[512,1152]{1,0:T(8,128)(2,1)}, f32[2,2,1152]{2,1,0:T(2,128)S(1)}) custom-call(bf16[4,512,1152]{2,1,0:T(8,128)(2,1)} %get-tuple-element.178.d_qkv, bf16[4,1152,1152]{2,1,0:T(8,128)(2,1)} %bitcast.345, f32[2,6,1152]{2,1,0:T(8,128)S(1)} %broadcast_add_fusion.mods, bf16[512,1152]{1,0:T(8,128)(2,1)S(1)} %bitcast.343, f32[512,1152]{1,0:T(8,128)S(1)} %copy-done.3), custom_call_target="tpu_custom_call" | custom-call | flops 1024 | bytes 1024 | tf_op jit(solution)/shard_map/pallas_call | solution.py:624
  556.3 30.0 %collective-permute-done.53 = bf16[2,144,1152]{2,1,0:T(8,128)(2,1)S(1)} collective-permute-done((bf16[2,144,1152]{2,1,0:T(8,128)(2,1)S(1)}, bf16[2,144,1152]{2,1,0:T(8,128)(2,1)S(1)}, u32[]{:S(2)}, u32[]{:S(2)}) %collective-permute-start.53) | collective-permute-done | bytes 663584 | tf_op jit(solution)/shard_map/ppermute | solution.py:666
  597.0 9.3 %all_to_all.41 = f32[4,1,7488]{2,1,0:T(1,128)S(1)} all-to-all(f32[4,1,7488]{2,1,0:T(1,128)S(1)} %copy.132), channel_id=1, replica_groups=mesh['dp'=8,'fsdp'=4] {'fsdp'}, dimensions={0} | all-to-all | bytes 239616 | tf_op jit(solution)/shard_map/all_to_all | solution.py:1151
  617.9 31.5 %all-to-all-done.2 = f32[8,1,3960]{2,1,0:T(1,128)S(1)} async-done(((f32[8,1,3960]{2,1,0:T(1,128)}), f32[8,1,3960]{2,1,0:T(1,128)S(1)}, u32[]{:S(2)}, u32[]{:S(2)}) %all-to-all-start.2) | async-done | bytes 126752 | tf_op jit(solution)/shard_map/all_to_all | solution.py:1162
  652.4 8.9 %all_gather.36 = f32[864,128]{1,0:T(8,128)S(1)} all-gather(f32[216,128]{1,0:T(8,128)S(1)} %reshape.305), channel_id=1, replica_groups=mesh['dp'=8,'fsdp'=4] {'fsdp'}, dimensions={0}, use_global_device_ids=true | all-gather | bytes 552960 | tf_op jit(solution)/shard_map/all_gather | solution.py:1167
  666.6 8.4 %shard_map.215 = bf16[4,3,144,288]{3,2,1,0:T(8,128)(2,1)} custom-call(s32[1]{0:T(128)} %bitcast.136.at, bf16[1152,1152]{1,0:T(8,128)(2,1)} %bitcast.366, bf16[144,1152]{1,0:T(8,128)(2,1)S(1)} %copy-done.4, bf16[1152,1152]{1,0:T(8,128)(2,1)} %bitcast.363), custom_call_target="tpu_custom_call" | custom-call | flops 1024 | bytes 1024 | tf_op jit(solution)/shard_map/pallas_call | solution.py:922
  686.7 8.3 %shard_map.216 = bf16[4,3,144,288]{3,2,1,0:T(8,128)(2,1)} custom-call(s32[1]{0:T(128)} %bitcast.136.at, bf16[1152,1152]{1,0:T(8,128)(2,1)} %bitcast.367, bf16[144,1152]{1,0:T(8,128)(2,1)S(1)} %get-tuple-element.238.left_root, bf16[1152,1152]{1,0:T(8,128)(2,1)} %bitcast.364), custom_call_target="tpu_custom_call" | custom-call | flops 1024 | bytes 1024 | tf_op jit(solution)/shard_map/pallas_call | solution.py:922
  703.6 18.5 %all_gather.39 = f32[1728,128]{1,0:T(8,128)} all-gather(f32[216,128]{1,0:T(8,128)S(1)} %reshape.312), channel_id=1, replica_groups=mesh['dp'=8,'fsdp'=4] {'dp'}, dimensions={0}, use_global_device_ids=true | all-gather | bytes 995328 | tf_op jit(solution)/shard_map/all_gather | solution.py:1191
  728.1 8.3 %shard_map.217 = bf16[4,3,144,288]{3,2,1,0:T(8,128)(2,1)} custom-call(s32[1]{0:T(128)} %bitcast.136.at, bf16[1152,1152]{1,0:T(8,128)(2,1)} %bitcast.368, bf16[144,1152]{1,0:T(8,128)(2,1)S(1)} %get-tuple-element.237.left_root, bf16[1152,1152]{1,0:T(8,128)(2,1)} %bitcast.365), custom_call_target="tpu_custom_call" | custom-call | flops 1024 | bytes 1024 | tf_op jit(solution)/shard_map/pallas_call | solution.py:922
  746.3 12.4 %all-to-all-done.5 = bf16[4,3,144,288]{3,2,1,0:T(8,128)(2,1)} async-done(((bf16[4,3,144,288]{3,2,1,0:T(8,128)(2,1)}), bf16[4,3,144,288]{3,2,1,0:T(8,128)(2,1)}, u32[]{:S(2)}, u32[]{:S(2)}) %all-to-all-start.5) | async-done | bytes 995360 | tf_op jit(solution)/shard_map/all_to_all | solution.py:741
  (430 shorter events, 284.2 us)
Async XLA Ops:
  52.6 234.9 %all-gather.10.cloned.1.call-start = ((), (), s32[]{:S(2)}) async-start(), calls=%async_computation.6 | async-start | bytes 2985984 | tf_op jit(solution)/shard_map/all_gather | solution.py:830
  86.9 67.2 %collective-permute-start.6 = (bf16[576,1152]{1,0:T(8,128)(2,1)S(1)}, bf16[576,1152]{1,0:T(8,128)(2,1)}, u32[]{:S(2)}, u32[]{:S(2)}) collective-permute-start(bf16[576,1152]{1,0:T(8,128)(2,1)S(1)} %shard_map.204.refs_0_), channel_id=1, source_target_pairs={{0,1},{1,0},{2,3},{3,2},{4,5},{5,4},{6,7},{7,6},{8,9},{9,8},{10,11... | collective-permute-start | bytes 3981320 | tf_op jit(solution)/shard_map/ppermute | solution.py:671
  88.5 65.6 %collective-permute-start.7 = (bf16[576,1152]{1,0:T(8,128)(2,1)S(1)}, bf16[576,1152]{1,0:T(8,128)(2,1)}, u32[]{:S(2)}, u32[]{:S(2)}) collective-permute-start(bf16[576,1152]{1,0:T(8,128)(2,1)S(1)} %shard_map.204.refs_0_), channel_id=1, source_target_pairs={{0,2},{1,3},{2,0},{3,1},{4,6},{5,7},{6,4},{7,5},{8,10},{9,11},{10,... | collective-permute-start | bytes 3981320 | tf_op jit(solution)/shard_map/ppermute | solution.py:671
  134.2 45.7 %collective-permute-start.17 = (bf16[576,1152]{1,0:T(8,128)(2,1)S(1)}, bf16[576,1152]{1,0:T(8,128)(2,1)}, u32[]{:S(2)}, u32[]{:S(2)}) collective-permute-start(bf16[576,1152]{1,0:T(8,128)(2,1)S(1)} %shard_map.204.refs_0_), channel_id=1, source_target_pairs={{0,4},{4,0},{8,12},{12,8},{16,20},{20,16},{24,28},{28,24},{1,5},{5... | collective-permute-start | bytes 3981320 | tf_op jit(solution)/shard_map/ppermute | solution.py:656
  156.7 223.5 %all-gather.12.cloned.1.call-start = ((), (), s32[]{:S(2)}) async-start(), calls=%async_computation.7 | async-start | bytes 2985984 | tf_op jit(solution)/shard_map/all_gather | solution.py:830
  201.7 49.8 %collective-permute-start.26 = (bf16[576,1152]{1,0:T(8,128)(2,1)}, bf16[576,1152]{1,0:T(8,128)(2,1)}, u32[]{:S(2)}, u32[]{:S(2)}) collective-permute-start(bf16[576,1152]{1,0:T(8,128)(2,1)} %constant_dynamic-slice_fusion.8), channel_id=1, source_target_pairs={{0,1},{1,0},{2,3},{3,2},{4,5},{5,4},{6,7},{7,6},{8,9},{9,8},{10,11... | collective-permute-start | bytes 3981320 | tf_op jit(solution)/shard_map/ppermute | solution.py:671
  202.5 49.5 %collective-permute-start.28 = (bf16[576,1152]{1,0:T(8,128)(2,1)}, bf16[576,1152]{1,0:T(8,128)(2,1)}, u32[]{:S(2)}, u32[]{:S(2)}) collective-permute-start(bf16[576,1152]{1,0:T(8,128)(2,1)} %constant_dynamic-slice_fusion.8), channel_id=1, source_target_pairs={{0,2},{1,3},{2,0},{3,1},{4,6},{5,7},{6,4},{7,5},{8,10},{9,11},{10,... | collective-permute-start | bytes 3981320 | tf_op jit(solution)/shard_map/ppermute | solution.py:671
  203.4 58.1 %collective-permute-start.30 = (bf16[576,1152]{1,0:T(8,128)(2,1)}, bf16[576,1152]{1,0:T(8,128)(2,1)}, u32[]{:S(2)}, u32[]{:S(2)}) collective-permute-start(bf16[576,1152]{1,0:T(8,128)(2,1)} %constant_dynamic-slice_fusion.8), channel_id=1, source_target_pairs={{0,3},{1,2},{2,1},{3,0},{4,7},{5,6},{6,5},{7,4},{8,11},{9,10},{10,... | collective-permute-start | bytes 3981320 | tf_op jit(solution)/shard_map/ppermute | solution.py:671
  207.4 42.0 %collective-permute-start.23 = (bf16[144,1152]{1,0:T(8,128)(2,1)}, bf16[144,1152]{1,0:T(8,128)(2,1)S(1)}, u32[]{:S(2)}, u32[]{:S(2)}) collective-permute-start(bf16[144,1152]{1,0:T(8,128)(2,1)} %get-tuple-element.132.refs_0_), channel_id=1, source_target_pairs={{0,16},{4,20},{8,24},{12,28},{16,0},{20,4},{24,8},{28,12},{1,17},{... | collective-permute-start | bytes 995336 | tf_op jit(solution)/shard_map/ppermute | solution.py:661
  207.5 41.9 %collective-permute-start.24 = (bf16[144,1152]{1,0:T(8,128)(2,1)}, bf16[144,1152]{1,0:T(8,128)(2,1)S(1)}, u32[]{:S(2)}, u32[]{:S(2)}) collective-permute-start(bf16[144,1152]{1,0:T(8,128)(2,1)} %get-tuple-element.132.refs_0_), channel_id=1, source_target_pairs={{0,24},{4,28},{8,0},{12,4},{16,8},{20,12},{24,16},{28,20},{1,25},{... | collective-permute-start | bytes 995336 | tf_op jit(solution)/shard_map/ppermute | solution.py:661
  287.5 92.7 %collective-permute-start.38 = (bf16[4,576,1152]{2,1,0:T(8,128)(2,1)}, bf16[4,576,1152]{2,1,0:T(8,128)(2,1)}, u32[]{:S(2)}, u32[]{:S(2)}) collective-permute-start(bf16[4,576,1152]{2,1,0:T(8,128)(2,1)} %convolution_convert_fusion.1), channel_id=1, source_target_pairs={{0,4},{4,0},{8,12},{12,8},{16,20},{20,16},{24,28},{28,24},{1,5},{5... | collective-permute-start | bytes 15925256 | tf_op jit(solution)/shard_map/ppermute | solution.py:656
  288.2 143.7 %all-gather.14.cloned.1.call-start = ((), (), s32[]{:S(2)}) async-start(), calls=%async_computation.8 | async-start | bytes 2985984 | tf_op jit(solution)/shard_map/all_gather | solution.py:830
  289.7 32.3 %collective-permute-start.32 = (bf16[576,1152]{1,0:T(8,128)(2,1)S(1)}, bf16[576,1152]{1,0:T(8,128)(2,1)}, u32[]{:S(2)}, u32[]{:S(2)}) collective-permute-start(bf16[576,1152]{1,0:T(8,128)(2,1)S(1)} %constant_dynamic-slice_fusion.7), channel_id=1, source_target_pairs={{0,1},{1,0},{2,3},{3,2},{4,5},{5,4},{6,7},{7,6},{8,9},{9,8},{10,11... | collective-permute-start | bytes 3981320 | tf_op jit(solution)/shard_map/ppermute | solution.py:671
  291.9 59.6 %collective-permute-start.34 = (bf16[576,1152]{1,0:T(8,128)(2,1)S(1)}, bf16[576,1152]{1,0:T(8,128)(2,1)}, u32[]{:S(2)}, u32[]{:S(2)}) collective-permute-start(bf16[576,1152]{1,0:T(8,128)(2,1)S(1)} %constant_dynamic-slice_fusion.7), channel_id=1, source_target_pairs={{0,2},{1,3},{2,0},{3,1},{4,6},{5,7},{6,4},{7,5},{8,10},{9,11},{10,... | collective-permute-start | bytes 3981320 | tf_op jit(solution)/shard_map/ppermute | solution.py:671
  293.1 58.4 %collective-permute-start.36 = (bf16[576,1152]{1,0:T(8,128)(2,1)S(1)}, bf16[576,1152]{1,0:T(8,128)(2,1)}, u32[]{:S(2)}, u32[]{:S(2)}) collective-permute-start(bf16[576,1152]{1,0:T(8,128)(2,1)S(1)} %constant_dynamic-slice_fusion.7), channel_id=1, source_target_pairs={{0,3},{1,2},{2,1},{3,0},{4,7},{5,6},{6,5},{7,4},{8,11},{9,10},{10,... | collective-permute-start | bytes 3981320 | tf_op jit(solution)/shard_map/ppermute | solution.py:671
  398.5 33.4 %collective-permute-start.39 = (bf16[4,576,1152]{2,1,0:T(8,128)(2,1)}, bf16[4,576,1152]{2,1,0:T(8,128)(2,1)}, u32[]{:S(2)}, u32[]{:S(2)}) collective-permute-start(bf16[4,576,1152]{2,1,0:T(8,128)(2,1)} %fusion.1), channel_id=1, source_target_pairs={{0,4},{4,0},{8,12},{12,8},{16,20},{20,16},{24,28},{28,24},{1,5},{5... | collective-permute-start | bytes 15925256 | tf_op jit(solution)/shard_map/ppermute | solution.py:656
  398.5 268.1 %all-gather.16.cloned.1.call-start = ((), (), s32[]{:S(2)}) async-start(), calls=%async_computation.9 | async-start | bytes 2985984 | tf_op jit(solution)/shard_map/all_gather | solution.py:875
  398.6 33.3 %collective-permute-start.40 = (bf16[2,2,144,1152]{3,2,1,0:T(8,128)(2,1)}, bf16[2,2,144,1152]{3,2,1,0:T(8,128)(2,1)}, u32[]{:S(2)}, u32[]{:S(2)}) collective-permute-start(bf16[2,2,144,1152]{3,2,1,0:T(8,128)(2,1)} %dynamic-slice_bitcast_fusion.5), channel_id=1, source_target_pairs={{0,1},{1,0},{2,3},{3,2},{4,5},{5,4},{6,7},{7,6},{8,9},{9,8},{10,11... | collective-permute-start | bytes 3981320 | tf_op jit(solution)/shard_map/ppermute | solution.py:671
  398.6 33.2 %collective-permute-start.41 = (bf16[2,2,144,1152]{3,2,1,0:T(8,128)(2,1)}, bf16[2,2,144,1152]{3,2,1,0:T(8,128)(2,1)}, u32[]{:S(2)}, u32[]{:S(2)}) collective-permute-start(bf16[2,2,144,1152]{3,2,1,0:T(8,128)(2,1)} %dynamic-slice_bitcast_fusion.4), channel_id=1, source_target_pairs={{0,2},{1,3},{2,0},{3,1},{4,6},{5,7},{6,4},{7,5},{8,10},{9,11},{10,... | collective-permute-start | bytes 3981320 | tf_op jit(solution)/shard_map/ppermute | solution.py:671
  435.3 53.6 %collective-permute-start.43 = (bf16[2,144,1152]{2,1,0:T(8,128)(2,1)}, bf16[2,144,1152]{2,1,0:T(8,128)(2,1)}, u32[]{:S(2)}, u32[]{:S(2)}) collective-permute-start(bf16[2,144,1152]{2,1,0:T(8,128)(2,1)} %dynamic-slice_bitcast_fusion.13), channel_id=1, source_target_pairs={{0,1},{1,0},{2,3},{3,2},{4,5},{5,4},{6,7},{7,6},{8,9},{9,8},{10,11... | collective-permute-start | bytes 1990664 | tf_op jit(solution)/shard_map/ppermute | solution.py:671
  448.5 45.8 %collective-permute-start.44 = (bf16[2,2,144,1152]{3,2,1,0:T(8,128)(2,1)}, bf16[2,2,144,1152]{3,2,1,0:T(8,128)(2,1)}, u32[]{:S(2)}, u32[]{:S(2)}) collective-permute-start(bf16[2,2,144,1152]{3,2,1,0:T(8,128)(2,1)} %dynamic-slice_bitcast_fusion.3), channel_id=1, source_target_pairs={{0,1},{1,0},{2,3},{3,2},{4,5},{5,4},{6,7},{7,6},{8,9},{9,8},{10,11... | collective-permute-start | bytes 3981320 | tf_op jit(solution)/shard_map/ppermute | solution.py:671
  449.0 45.2 %collective-permute-start.45 = (bf16[2,2,144,1152]{3,2,1,0:T(8,128)(2,1)}, bf16[2,2,144,1152]{3,2,1,0:T(8,128)(2,1)}, u32[]{:S(2)}, u32[]{:S(2)}) collective-permute-start(bf16[2,2,144,1152]{3,2,1,0:T(8,128)(2,1)} %dynamic-slice_bitcast_fusion.2), channel_id=1, source_target_pairs={{0,2},{1,3},{2,0},{3,1},{4,6},{5,7},{6,4},{7,5},{8,10},{9,11},{10,... | collective-permute-start | bytes 3981320 | tf_op jit(solution)/shard_map/ppermute | solution.py:671
  453.2 41.1 %collective-permute-start.42 = (bf16[2,144,1152]{2,1,0:T(8,128)(2,1)}, bf16[2,144,1152]{2,1,0:T(8,128)(2,1)}, u32[]{:S(2)}, u32[]{:S(2)}) collective-permute-start(bf16[2,144,1152]{2,1,0:T(8,128)(2,1)} %dynamic-slice_bitcast_fusion.14), channel_id=1, source_target_pairs={{0,2},{1,3},{2,0},{3,1},{4,6},{5,7},{6,4},{7,5},{8,10},{9,11},{10,... | collective-permute-start | bytes 1990664 | tf_op jit(solution)/shard_map/ppermute | solution.py:671
  510.2 40.6 %collective-permute-start.49 = (bf16[2,144,1152]{2,1,0:T(8,128)(2,1)S(1)}, bf16[2,144,1152]{2,1,0:T(8,128)(2,1)}, u32[]{:S(2)}, u32[]{:S(2)}) collective-permute-start(bf16[2,144,1152]{2,1,0:T(8,128)(2,1)S(1)} %dynamic-slice_bitcast_fusion.10), channel_id=1, source_target_pairs={{0,1},{1,0},{2,3},{3,2},{4,5},{5,4},{6,7},{7,6},{8,9},{9,8},{10,11... | collective-permute-start | bytes 1990664 | tf_op jit(solution)/shard_map/ppermute | solution.py:671
  513.5 37.3 %collective-permute-start.48 = (bf16[2,144,1152]{2,1,0:T(8,128)(2,1)S(1)}, bf16[2,144,1152]{2,1,0:T(8,128)(2,1)}, u32[]{:S(2)}, u32[]{:S(2)}) collective-permute-start(bf16[2,144,1152]{2,1,0:T(8,128)(2,1)S(1)} %dynamic-slice_bitcast_fusion.11), channel_id=1, source_target_pairs={{0,2},{1,3},{2,0},{3,1},{4,6},{5,7},{6,4},{7,5},{8,10},{9,11},{10,... | collective-permute-start | bytes 1990664 | tf_op jit(solution)/shard_map/ppermute | solution.py:671
  536.6 49.7 %collective-permute-start.51 = (bf16[2,2,144,1152]{3,2,1,0:T(8,128)(2,1)}, bf16[2,2,144,1152]{3,2,1,0:T(8,128)(2,1)}, u32[]{:S(2)}, u32[]{:S(2)}) collective-permute-start(bf16[2,2,144,1152]{3,2,1,0:T(8,128)(2,1)} %dynamic-slice_bitcast_fusion.1), channel_id=1, source_target_pairs={{0,1},{1,0},{2,3},{3,2},{4,5},{5,4},{6,7},{7,6},{8,9},{9,8},{10,11... | collective-permute-start | bytes 3981320 | tf_op jit(solution)/shard_map/ppermute | solution.py:671
  538.1 48.2 %collective-permute-start.52 = (bf16[2,2,144,1152]{3,2,1,0:T(8,128)(2,1)}, bf16[2,2,144,1152]{3,2,1,0:T(8,128)(2,1)}, u32[]{:S(2)}, u32[]{:S(2)}) collective-permute-start(bf16[2,2,144,1152]{3,2,1,0:T(8,128)(2,1)} %dynamic-slice_bitcast_fusion), channel_id=1, source_target_pairs={{0,2},{1,3},{2,0},{3,1},{4,6},{5,7},{6,4},{7,5},{8,10},{9,11},{10,... | collective-permute-start | bytes 3981320 | tf_op jit(solution)/shard_map/ppermute | solution.py:671
  554.7 31.6 %collective-permute-start.53 = (bf16[2,144,1152]{2,1,0:T(8,128)(2,1)S(1)}, bf16[2,144,1152]{2,1,0:T(8,128)(2,1)S(1)}, u32[]{:S(2)}, u32[]{:S(2)}) collective-permute-start(bf16[2,144,1152]{2,1,0:T(8,128)(2,1)S(1)} %dynamic-slice_bitcast_fusion.9), channel_id=1, source_target_pairs={{0,8},{4,12},{8,0},{12,4},{16,24},{20,28},{24,16},{28,20},{1,9},{5... | collective-permute-start | bytes 1990664 | tf_op jit(solution)/shard_map/ppermute | solution.py:666
  556.2 130.6 %all-gather.20.cloned.1.call-start = ((), (), s32[]{:S(2)}) async-start(), calls=%async_computation.11 | async-start | bytes 2985984 | tf_op jit(solution)/shard_map/all_gather | solution.py:875
  611.3 38.2 %collective-permute-start.57 = (bf16[2,144,1152]{2,1,0:T(8,128)(2,1)S(1)}, bf16[2,144,1152]{2,1,0:T(8,128)(2,1)S(1)}, u32[]{:S(2)}, u32[]{:S(2)}) collective-permute-start(bf16[2,144,1152]{2,1,0:T(8,128)(2,1)S(1)} %dynamic-slice_bitcast_fusion.6), channel_id=1, source_target_pairs={{0,8},{4,12},{8,0},{12,4},{16,24},{20,28},{24,16},{28,20},{1,9},{5... | collective-permute-start | bytes 1990664 | tf_op jit(solution)/shard_map/ppermute | solution.py:666
  614.5 34.9 %all-to-all-start.2 = ((f32[8,1,3960]{2,1,0:T(1,128)}), f32[8,1,3960]{2,1,0:T(1,128)S(1)}, u32[]{:S(2)}, u32[]{:S(2)}) async-start(f32[8,1,3960]{2,1,0:T(1,128)} %all_to_all.29), calls=%async_computation.2 | async-start | bytes 253952 | tf_op jit(solution)/shard_map/all_to_all | solution.py:1162
  617.9 110.2 %all-gather.18.cloned.1.call-start = ((), (), s32[]{:S(2)}) async-start(), calls=%async_computation.10 | async-start | bytes 2985984 | tf_op jit(solution)/shard_map/all_gather | solution.py:875
  (101 other events, 1378.1 us)
Sparse Core Ops, SparseCore 0:
  156.8 45.1 all-gather.9
  288.3 33.8 all-gather.11
  398.6 33.1 all-gather.13
  556.3 45.8 all-gather.15
  608.5 41.9 all-gather.19
  677.0 34.2 all-gather.17

commit v12 on v10

--- a/solution.py
+++ b/solution.py
@@ -952,6 +952,13 @@
     weight_panels, first_parts = tie(weight_panels, first_parts)
     attn_rows, one_rows, two_rows = weight_rows.send(weight_panels)
     attn_w = gather_blocks(attn_rows, group)
+    two_w = gather_blocks(two_rows, group).reshape(group * width, width)
+    two_gathered = (
+        [two_w],
+        [[(0, index * width, width)] for index in range(group)],
+        [index * (width // 16) for index in range(group)],
+        range(group),
+    )
 
     first_parts = first_parts.reshape(dp_count, -1)
     cond_all = first_parts[:, : clip_count * width].reshape(all_clips, width)
@@ -969,11 +976,8 @@
     second_parts = lax.all_gather(
         packed([mod_cols, bias_rows, left_cond], 8), "fsdp", axis=0, tiled=True
     )
-    second_parts, one_parts, two_rows = tie(second_parts, one_parts, two_rows)
-    two_steps = gather_second(two_rows, group)
-    two_parts = next(two_steps)
+    second_parts, one_parts = tie(second_parts, one_parts)
     one_parts = one_steps.send(one_steps.send(one_parts))
-    two_parts = two_steps.send(two_parts)
     second_parts = second_parts.reshape(ranks, -1)
     mods = second_parts[:, :mod_size].reshape(ranks, clip_count, mod_count, col_part)
     mods = mods.transpose(1, 2, 0, 3).reshape(clip_count, mod_count, width)
@@ -988,8 +992,7 @@
     )
 
     roots = jnp.stack([narrow(left_roots[mod_count:]), narrow(right_roots[mod_count:])])
-    mods, roots, two_parts = tie(mods, roots, two_parts)
-    two_parts = two_steps.send(two_parts)
+    mods, roots = tie(mods, roots)
     root_rows = own_rows(roots.reshape(-1, group, row_part, col_part), group)
     root_panels = next(root_rows)
     attn_in, parts, mixed, proj, resid, mlp_in, d_branch, d_branch_sums = run_attention(
@@ -999,7 +1002,6 @@
     one_w, hidden, slope = run_hidden(mlp_in, one_steps.send(one_parts), bias_table[4:8, None])
     one_w = one_w.reshape(group, width, width)
 
-    weight_steps, two_w_parts = two_steps, two_parts
     two_steps = sum_blocks(
         lambda left: fast_dot("jtd,te->jde", left, d_branch),
         lambda first, size: lax.dynamic_slice_in_dim(hidden, first, size, 2),
@@ -1010,7 +1012,6 @@
     hidden, two_parts, root_panels = tie(hidden, two_parts, root_panels)
     two_parts = two_steps.send(two_parts)
     root_rows = root_rows.send(root_panels)
-    gathered = weight_steps.send(two_w_parts)
     hidden, root_rows = tie(hidden, root_rows)
     left_rows, right_rows = jnp.split(root_rows, 2)
     right_wholes = [gather_own(rows[None], group)[0] for rows in right_rows]
@@ -1019,14 +1020,14 @@
         frame_counts,
         hidden,
         slope,
-        gathered,
+        two_gathered,
         d_branch,
         bias_table[8:9],
         mods[:, 5:6],
         resid,
         grad_out,
     )
-    d_pre, two_parts = tie(d_pre, two_parts)
+    d_pre, two_parts, right_wholes[2] = tie(d_pre, two_parts, right_wholes[2])
     two_parts = two_steps.send(two_parts)
     d_pre, two_parts = tie(d_pre, two_parts)
     two_parts = two_steps.send(two_parts)
@@ -1042,16 +1043,19 @@
     d_resid, d_proj, resid_sums = run_resid(
         frames, frame_counts, d_pre, one_w, mods, resid, grad_out, proj
     )
-    d_proj, one_parts, two_parts, right_wholes[2] = tie(
-        d_proj, one_parts, two_parts, right_wholes[2]
+    d_proj, one_parts, two_parts, right_wholes[1] = tie(
+        d_proj, one_parts, two_parts, right_wholes[1]
     )
     two_parts = two_steps.send(two_parts)
     one_parts = one_steps.send(one_parts)
     d_proj, one_parts = tie(d_proj, one_parts)
     one_parts = one_steps.send(one_parts)
     d_heads, head_sums = run_attention_back(frames, frame_counts, d_proj, parts, attn_w)
-    d_heads, two_parts, right_wholes[1] = tie(d_heads, two_parts, right_wholes[1])
+    d_heads, two_parts, one_parts, right_wholes[0] = tie(
+        d_heads, two_parts, one_parts, right_wholes[0]
+    )
     two_parts = two_steps.send(two_parts)
+    one_parts = one_steps.send(one_parts)
     attn_steps = sum_blocks(
         lambda left: fast_dot("jtd,jte->jde", left, d_heads),
         lambda first, size: jnp.stack(
@@ -1063,16 +1067,13 @@
     attn_parts = next(attn_steps)
     d_heads, attn_parts = tie(d_heads, attn_parts)
     attn_parts = attn_steps.send(attn_parts)
-    d_heads, attn_parts, one_parts, two_parts = tie(d_heads, attn_parts, one_parts, two_parts)
+    d_heads, attn_parts, two_parts = tie(d_heads, attn_parts, two_parts)
     two_parts = two_steps.send(two_parts)
-    one_parts = one_steps.send(one_parts)
     attn_parts = attn_steps.send(attn_parts)
     d_heads, attn_parts = tie(d_heads, attn_parts)
     attn_parts = attn_steps.send(attn_parts)
     input_grad, input_sums = run_input(d_heads, attn_w, mods, stream, d_resid)
-    input_sums, one_parts, two_parts, right_wholes[0] = tie(
-        input_sums, one_parts, two_parts, right_wholes[0]
-    )
+    input_sums, one_parts, two_parts = tie(input_sums, one_parts, two_parts)
     whole_two = two_steps.send(two_parts)
     one_parts = one_steps.send(one_parts)
     input_sums, attn_parts, one_parts = tie(input_sums, attn_parts, one_parts)

time: 788 us -> 753 us (0.956)
  starting transfers between devices: 96.2 us -> 64.5 us
    all_gather x1 -> x2, waiting for transfers between devices: 0.02 us -> 84.3 us  [gather_blocks(): all_rows = lax.all_gather(rows, ('fsdp', 'dp'), axis=0, tiled=True)]
    ppermute x24 -> x21, waiting for transfers between devices: 94.8 us -> 23.4 us  [rank_swap(): return lax.ppermute(array, 'fsdp', [(at, at ^ bits) for at in range(count)])]
    ppermute x6 -> x3, waiting for transfers between devices: 47.7 us -> 9.62 us  [chip_shift(): lax.ppermute(array, 'dp', [(at, (at + 2 * step) % count) for at in range(...]
    ppermute x6 -> x3, starting transfers between devices: 27.2 us -> 3.83 us  [chip_shift(): lax.ppermute(array, 'dp', [(at, (at + 2 * step) % count) for at in range(...]
    ppermute x6, starting transfers between devices: 18.6 us -> 3.04 us  [chip_swap(): lax.ppermute(array, 'dp', [(at, at ^ 2 * bits) for at in range(count)])]
    all_gather x3, waiting for transfers between devices: 0.01 us -> 11.5 us  [gather_own(): return lax.all_gather(rows, 'dp', axis=1, tiled=True)]
    ppermute x24 -> x21, starting transfers between devices: 27.5 us -> 35.1 us  [rank_swap(): return lax.ppermute(array, 'fsdp', [(at, at ^ bits) for at in range(count)])]
    unnamed x166 -> x156, local copies, waits for them, and re-layouts: 16.4 us -> 17 us
  transfers between devices with their start and end apart: 59 -> 50, of which waited for: 21 -> 15; matrix products, arithmetic and copies ran while one was open for 20% -> 18% of each run, Pallas kernels for 20% -> 20%
where the time goes in v12:
time: 753 us; the launch traced here: 747 us
  waiting for transfers between devices  241 us (32%)
  Pallas kernels  160 us (21%)
  local copies, waits for them, and re-layouts  74.7 us (10%)
  other arithmetic  64.9 us (9%)
  blocking collectives  64.9 us (9%)
  starting transfers between devices  64.5 us (9%)
  matrix products  60.4 us (8%)
  between operations  16 us (2%)
    all_gather x2, waiting for transfers between devices, gather_blocks(): all_rows = lax.all_gather(rows, ('fsdp', 'dp'), axis=0, tiled=True)  84.3 us
    ppermute x6, waiting for transfers between devices, chip_swap(): lax.ppermute(array, 'dp', [(at, at ^ 2 * bits) for at in range(count)])  48.2 us
    dot_general x7, matrix products, fast_dot(): jnp.einsum(subscripts, left, right, preferred_element_type=jnp.float32)  46.9 us
    pallas_call x1, Pallas kernels, run_attention(): pl.pallas_call(functools.partial(attention_kernel, frames), grid=(clips,)...  40.9 us
    all_to_all x1, waiting for transfers between devices, per_device(): from_rows = lax.all_to_all(to_rows, 'dp', 0, 0, tiled=True)  35.8 us
    convert_element_type x22, other arithmetic, narrow(): return array.astype(jnp.bfloat16)  35.8 us
    ppermute x21, starting transfers between devices, rank_swap(): return lax.ppermute(array, 'fsdp', [(at, at ^ bits) for at in range(count)])  35.1 us
    pallas_call x1, Pallas kernels, run_attention_back(): pl.pallas_call(functools.partial(attention_back_kernel, frames), grid=(cl...  26.5 us
  transfers between devices with their start and end apart: 50, of which 15 were waited for; matrix products, arithmetic and copies ran while one was open for 18% of the time, Pallas kernels for 20%

profile of v12, /device:TPU:0, one launch (start us, length us, event | category | flops | bytes accessed | tf_op | source)
XLA Modules:
  0.0 746.7 jit_solution(16534231503845299783)
XLA Ops:
  15.8 14.7 %all_gather.36 = bf16[256,128]{1,0:T(8,128)(2,1)S(1)} all-gather(bf16[32,128]{1,0:T(8,128)(2,1)S(1)} %fusion.84), channel_id=1, replica_groups=mesh['dp'=8,'fsdp'=4] {'dp'}, dimensions={0}, use_global_device_ids=true | all-gather | bytes 73728 | tf_op jit(solution)/shard_map/all_gather | solution.py:951
  40.7 11.3 %all-to-all-done = f32[16,6,288]{2,1,0:T(8,128)S(1)} async-done(((f32[16,6,288]{2,1,0:T(8,128)}), f32[16,6,288]{2,1,0:T(8,128)S(1)}, u32[]{:S(2)}, u32[]{:S(2)}) %all-to-all-start) | async-done | bytes 110624 | tf_op jit(solution)/shard_map/all_to_all | solution.py:969
  58.7 9.7 %all_gather.37 = f32[672,128]{1,0:T(8,128)S(1)} all-gather(f32[168,128]{1,0:T(8,128)S(1)} %pad_bitcast_fusion), channel_id=1, replica_groups=mesh['dp'=8,'fsdp'=4] {'fsdp'}, dimensions={0}, use_global_device_ids=true | all-gather | bytes 430080 | tf_op jit(solution)/shard_map/all_gather | solution.py:976
  68.3 9.6 %collective-permute-done.4.refs_2_ = bf16[144,1152]{1,0:T(8,128)(2,1)S(1)} collective-permute-done((bf16[144,1152]{1,0:T(8,128)(2,1)S(1)}, bf16[144,1152]{1,0:T(8,128)(2,1)S(1)}, u32[]{:S(2)}, u32[]{:S(2)}) %collective-permute-start.4) | collective-permute-done | bytes 331808 | tf_op jit(solution)/shard_map/ppermute | solution.py:660
  97.6 69.3 %all-gather.20.cloned.1.call-done = bf16[1,4608,1152]{2,1,0:T(8,128)(2,1)} async-done(((bf16[1,144,1152]{2,1,0:T(8,128)(2,1)}), bf16[1,4608,1152]{2,1,0:T(8,128)(2,1)}) %all-gather.20.cloned.1.call-update) | async-done | bytes 10616848 | tf_op jit(solution)/shard_map/all_gather | solution.py:749
  166.9 40.9 %shard_map.204 = (bf16[512,1152]{1,0:T(8,128)(2,1)S(1)}, bf16[5,512,1152]{2,1,0:T(8,128)(2,1)}, bf16[512,1152]{1,0:T(8,128)(2,1)S(1)}, f32[512,1152]{1,0:T(8,128...) custom-call(s32[2]{0:T(128)S(1)} %copy-done.25, ...), custom_call_target="tpu_custom_call" | custom-call | flops 1024 | bytes 1024 | tf_op jit(solution)/shard_map/pallas_call | solution.py:216
  213.8 12.6 %collective-permute-start.14 = (bf16[6,144,288]{2,1,0:T(8,128)(2,1)S(1)}, bf16[6,144,288]{2,1,0:T(8,128)(2,1)S(1)}, u32[]{:S(2)}, u32[]{:S(2)}) collective-permute-start(bf16[6,144,288]{2,1,0:T(8,128)(2,1)S(1)} %get-tuple-element.227), channel_id=1, source_target_pairs={{0,2},{1,3},{2,0},{3,1},{4,6},{5,7},{6,4},{7,5},{8,10},{9,11},{10,... | collective-permute-start | bytes 1493000 | tf_op jit(solution)/shard_map/ppermute | solution.py:670
  227.1 13.8 %shard_map.207 = (bf16[4608,1152]{1,0:T(8,128)(2,1)}, bf16[4,512,1152]{2,1,0:T(8,128)(2,1)}, bf16[4,512,1152]{2,1,0:T(8,128)(2,1)}) custom-call(s32[4]{0:T(128)S(1)} %pad_add_fusion.order, s32[7]{0:T(128)S(1)} %stack.128.starts, bf16[512,1152]{1,0:T(8,128)(2,1)S(1)} %copy-done.10, f32[4,1,1152]{2,1,0:T(1,128)S(1)} %copy.115.bias, ...), custom_call_target="tpu_custom_call" | custom-call | flops 1024 | bytes 1024 | tf_op jit(solution)/shard_map/pallas_call | solution.py:324
  240.9 7.9 %convolution_convert_fusion.1 = bf16[4,576,1152]{2,1,0:T(8,128)(2,1)} fusion(bf16[4,512,1152]{2,1,0:T(8,128)(2,1)} %get-tuple-element.135.hidden, s32[]{:T(128)S(6)} %select_n.352, bf16[512,1152]{1,0:T(8,128)(2,1)S(1)} %copy-done.14), kind=kOutput, calls=%fused_computation.5 | convolution fusion | flops 2720563200 | bytes 9109508 | tf_op jit(solution)/shard_map/jtd,te->jde/dot_general | solution.py:847
  248.8 12.5 %collective-permute-done.14 = bf16[6,144,288]{2,1,0:T(8,128)(2,1)S(1)} collective-permute-done((bf16[6,144,288]{2,1,0:T(8,128)(2,1)S(1)}, bf16[6,144,288]{2,1,0:T(8,128)(2,1)S(1)}, u32[]{:S(2)}, u32[]{:S(2)}) %collective-permute-start.14) | collective-permute-done | bytes 497696 | tf_op jit(solution)/shard_map/ppermute | solution.py:670
  278.1 15.0 %all-gather.22.cloned.1.call-done = bf16[1,4608,1152]{2,1,0:T(8,128)(2,1)} async-done(((bf16[1,144,1152]{2,1,0:T(8,128)(2,1)}), bf16[1,4608,1152]{2,1,0:T(8,128)(2,1)}) %all-gather.22.cloned.1.call-update) | async-done | bytes 10616848 | tf_op jit(solution)/shard_map/all_gather | solution.py:749
  295.7 22.1 %shard_map.208 = (bf16[4,512,1152]{2,1,0:T(8,128)(2,1)}, f32[4,1,1152]{2,1,0:T(1,128)S(1)}, bf16[512,1152]{1,0:T(8,128)(2,1)}, f32[2,1,1152]{2,1,0:T(1,128)S(1)}) custom-call(s32[4]{0:T(128)S(1)} %iota.6.order, s32[4]{0:T(128)S(1)} %copy-done.26, s32[2]{0:T(128)S(1)} %copy-done.25, bf16[4,512,1152]{2,1,0:T(8,128)(2,1)} %get-tuple-element.135.hidden, ...), custom_call_target="tpu_custom_call" | custom-call | flops 1024 | bytes 1024 | tf_op jit(solution)/shard_map/pallas_call | solution.py:404
  319.1 9.6 %fusion.10 = f32[4,576,1152]{2,1,0:T(8,128)} fusion(bf16[4,512,1152]{2,1,0:T(8,128)(2,1)} %get-tuple-element.135.hidden, s32[]{:T(128)S(6)} %select_n.351, bf16[512,1152]{1,0:T(8,128)(2,1)S(1)} %copy-done.15), kind=kOutput, calls=%fused_computation.29 | convolution fusion | flops 2717908992 | bytes 14417924 | tf_op jit(solution)/shard_map/jtd,te->jde/dot_general | solution.py:847
  328.7 8.9 %add_convert_fusion.1 = bf16[4,576,1152]{2,1,0:T(8,128)(2,1)} fusion(f32[4,576,1152]{2,1,0:T(8,128)} %fusion.10, bf16[4,576,1152]{2,1,0:T(8,128)(2,1)} %collective-permute-done.16), kind=kLoop, calls=%fused_computation.3 | loop fusion | flops 7962624 | bytes 21233664 | tf_op jit(solution)/shard_map/convert_element_type | solution.py:27
  352.6 16.2 %shard_map.209 = (f32[512,1152]{1,0:T(8,128)}, bf16[512,1152]{1,0:T(8,128)(2,1)S(1)}, f32[2,4,1152]{2,1,0:T(4,128)S(1)}) custom-call(s32[2]{0:T(128)S(1)} %copy-done.25, bf16[4,512,1152]{2,1,0:T(8,128)(2,1)} %get-tuple-element.145.d_pre, bf16[4,1152,1152]{2,1,0:T(8,128)(2,1)} %bitcast.303, f32[2,6,1152]{2,1,0:T(8,128)S(1)} %copy-done.7, ...), custom_call_target="tpu_custom_call" | custom-call | flops 1024 | bytes 1024 | tf_op jit(solution)/shard_map/pallas_call | solution.py:496
  370.5 11.5 %all-gather.16.cloned.1.call-done = bf16[1,1152,1152]{2,1,0:T(8,128)(2,1)} async-done(((bf16[1,144,1152]{2,1,0:T(8,128)(2,1)}), bf16[1,1152,1152]{2,1,0:T(8,128)(2,1)}) %all-gather.16.cloned.1.call-update) | async-done | bytes 2654224 | tf_op jit(solution)/shard_map/all_gather | solution.py:798
  382.0 7.8 %fusion = bf16[4,576,1152]{2,1,0:T(8,128)(2,1)S(1)} fusion(bf16[4,576,1152]{2,1,0:T(8,128)(2,1)} %collective-permute-done.17, bf16[4,512,1152]{2,1,0:T(8,128)(2,1)} %get-tuple-element.145.d_pre, bf16[512,1152]{1,0:T(8,128)(2,1)} %copy-done.9, s32[]{:T(128)S(6)} %select_n.351), kind=kOutput, calls=%fused_computation.1 | convolution fusion | flops 2725871616 | bytes 15990788 | tf_op jit(solution)/shard_map/td,jte->jde/dot_general | solution.py:847
  411.0 26.5 %shard_map.210 = (bf16[4,512,1152]{2,1,0:T(8,128)(2,1)}, f32[2,3,1152]{2,1,0:T(4,128)S(1)}) custom-call(s32[2]{0:T(128)S(1)} %copy-done.25, bf16[512,1152]{1,0:T(8,128)(2,1)S(1)} %copy-done.13, bf16[5,512,1152]{2,1,0:T(8,128)(2,1)} %get-tuple-element.155.parts, bf16[4,1152,1152]{2,1,0:T(8,128)(2,1)} %bitcast.299), custom_call_target="tpu_custom_call" | custom-call | flops 1024 | bytes 1024 | tf_op jit(solution)/shard_map/pallas_call | solution.py:563
  437.5 6.3 collective-permute-done.21
  443.8 8.5 %convolution_convert_fusion = bf16[4,576,1152]{2,1,0:T(8,128)(2,1)} fusion(bf16[4,512,1152]{2,1,0:T(8,128)(2,1)} %get-tuple-element.170.d_qkv, bf16[1,512,576]{1,2,0:T(8,128)(2,1)S(1)} %bitcast.325, bf16[1,512,576]{1,2,0:T(8,128)(2,1)} %bitcast.326), kind=kOutput, calls=%fused_computation.4 | convolution fusion | flops 2724102144 | bytes 11206656 | tf_op jit(solution)/shard_map/jtd,jte->jde/dot_general | solution.py:847
  465.8 10.1 %collective-permute-done.25 = bf16[2,144,1152]{2,1,0:T(8,128)(2,1)S(1)} collective-permute-done((bf16[2,144,1152]{2,1,0:T(8,128)(2,1)S(1)}, bf16[2,144,1152]{2,1,0:T(8,128)(2,1)S(1)}, u32[]{:S(2)}, u32[]{:S(2)}) %collective-permute-start.25) | collective-permute-done | bytes 663584 | tf_op jit(solution)/shard_map/ppermute | solution.py:665
  475.9 6.6 add_convert_fusion
  489.0 11.1 %shard_map.211 = (bf16[512,1152]{1,0:T(8,128)(2,1)}, f32[2,2,1152]{2,1,0:T(2,128)S(1)}) custom-call(bf16[4,512,1152]{2,1,0:T(8,128)(2,1)} %get-tuple-element.170.d_qkv, bf16[4,1152,1152]{2,1,0:T(8,128)(2,1)} %bitcast.300, f32[2,6,1152]{2,1,0:T(8,128)S(1)} %copy-done.8, bf16[512,1152]{1,0:T(8,128)(2,1)S(1)} %bitcast.297, f32[512,1152]{1,0:T(8,128)S(1)} %copy-done.2), custom_call_target="tpu_custom_call" | custom-call | flops 1024 | bytes 1024 | tf_op jit(solution)/shard_map/pallas_call | solution.py:623
  506.3 36.8 %collective-permute-done.31 = bf16[2,144,1152]{2,1,0:T(8,128)(2,1)} collective-permute-done((bf16[2,144,1152]{2,1,0:T(8,128)(2,1)S(1)}, bf16[2,144,1152]{2,1,0:T(8,128)(2,1)}, u32[]{:S(2)}, u32[]{:S(2)}) %collective-permute-start.31) | collective-permute-done | bytes 663584 | tf_op jit(solution)/shard_map/ppermute | solution.py:665
  554.8 12.6 %all_to_all.41 = f32[4,1,7488]{2,1,0:T(1,128)S(1)} all-to-all(f32[4,1,7488]{2,1,0:T(1,128)S(1)} %copy.132), channel_id=1, replica_groups=mesh['dp'=8,'fsdp'=4] {'fsdp'}, dimensions={0} | all-to-all | bytes 239616 | tf_op jit(solution)/shard_map/all_to_all | solution.py:1116
  577.7 35.8 %all-to-all-done.2 = f32[8,1,3960]{2,1,0:T(1,128)S(1)} async-done(((f32[8,1,3960]{2,1,0:T(1,128)}), f32[8,1,3960]{2,1,0:T(1,128)S(1)}, u32[]{:S(2)}, u32[]{:S(2)}) %all-to-all-start.2) | async-done | bytes 126752 | tf_op jit(solution)/shard_map/all_to_all | solution.py:1127
  614.6 10.3 %all_gather.44 = f32[864,128]{1,0:T(8,128)S(1)} all-gather(f32[216,128]{1,0:T(8,128)S(1)} %reshape.305), channel_id=1, replica_groups=mesh['dp'=8,'fsdp'=4] {'fsdp'}, dimensions={0}, use_global_device_ids=true | all-gather | bytes 552960 | tf_op jit(solution)/shard_map/all_gather | solution.py:1132
  629.0 8.3 %shard_map.212 = bf16[4,3,144,288]{3,2,1,0:T(8,128)(2,1)} custom-call(s32[1]{0:T(128)} %bitcast.103.at, bf16[1152,1152]{1,0:T(8,128)(2,1)} %bitcast.319, bf16[144,1152]{1,0:T(8,128)(2,1)S(1)} %copy-done.5, bf16[1152,1152]{1,0:T(8,128)(2,1)} %bitcast.316), custom_call_target="tpu_custom_call" | custom-call | flops 1024 | bytes 1024 | tf_op jit(solution)/shard_map/pallas_call | solution.py:890
  650.7 8.3 %shard_map.213 = bf16[4,3,144,288]{3,2,1,0:T(8,128)(2,1)} custom-call(s32[1]{0:T(128)} %bitcast.103.at, bf16[1152,1152]{1,0:T(8,128)(2,1)} %bitcast.320, bf16[144,1152]{1,0:T(8,128)(2,1)S(1)} %copy-done.4, bf16[1152,1152]{1,0:T(8,128)(2,1)} %bitcast.318), custom_call_target="tpu_custom_call" | custom-call | flops 1024 | bytes 1024 | tf_op jit(solution)/shard_map/pallas_call | solution.py:890
  666.6 17.7 %all_gather.47 = f32[1728,128]{1,0:T(8,128)} all-gather(f32[216,128]{1,0:T(8,128)S(1)} %reshape.312), channel_id=1, replica_groups=mesh['dp'=8,'fsdp'=4] {'dp'}, dimensions={0}, use_global_device_ids=true | all-gather | bytes 995328 | tf_op jit(solution)/shard_map/all_gather | solution.py:1156
  690.9 8.3 %shard_map.214 = bf16[4,3,144,288]{3,2,1,0:T(8,128)(2,1)} custom-call(s32[1]{0:T(128)} %bitcast.103.at, bf16[1152,1152]{1,0:T(8,128)(2,1)} %bitcast.321, bf16[144,1152]{1,0:T(8,128)(2,1)S(1)} %copy-done.3, bf16[1152,1152]{1,0:T(8,128)(2,1)} %bitcast.317), custom_call_target="tpu_custom_call" | custom-call | flops 1024 | bytes 1024 | tf_op jit(solution)/shard_map/pallas_call | solution.py:890
  710.2 11.6 %all-to-all-done.5 = bf16[4,3,144,288]{3,2,1,0:T(8,128)(2,1)} async-done(((bf16[4,3,144,288]{3,2,1,0:T(8,128)(2,1)}), bf16[4,3,144,288]{3,2,1,0:T(8,128)(2,1)}, u32[]{:S(2)}, u32[]{:S(2)}) %all-to-all-start.5) | async-done | bytes 995360 | tf_op jit(solution)/shard_map/all_to_all | solution.py:740
  (415 shorter events, 218.2 us)
Async XLA Ops:
  7.2 159.7 %all-gather.20.cloned.1.call-start = ((), (), s32[]{:S(2)}) async-start(), calls=%async_computation.9 | async-start | bytes 10948608 | tf_op jit(solution)/shard_map/all_gather | solution.py:749
  32.6 260.5 %all-gather.22.cloned.1.call-start = ((), (), s32[]{:S(2)}) async-start(), calls=%async_computation.10 | async-start | bytes 10948608 | tf_op jit(solution)/shard_map/all_gather | solution.py:749
  40.6 288.1 %all-gather.14.cloned.1.call-start = ((), (), s32[]{:S(2)}) async-start(), calls=%async_computation.6 | async-start | bytes 2985984 | tf_op jit(solution)/shard_map/all_gather | solution.py:798
  52.1 25.9 %collective-permute-start.4 = (bf16[144,1152]{1,0:T(8,128)(2,1)S(1)}, bf16[144,1152]{1,0:T(8,128)(2,1)S(1)}, u32[]{:S(2)}, u32[]{:S(2)}) collective-permute-start(bf16[144,1152]{1,0:T(8,128)(2,1)S(1)} %get-tuple-element.116.refs_0_), channel_id=1, source_target_pairs={{0,16},{4,20},{8,24},{12,28},{16,0},{20,4},{24,8},{28,12},{1,17},{... | collective-permute-start | bytes 995336 | tf_op jit(solution)/shard_map/ppermute | solution.py:660
  54.1 23.9 %collective-permute-start.5 = (bf16[144,1152]{1,0:T(8,128)(2,1)S(1)}, bf16[144,1152]{1,0:T(8,128)(2,1)S(1)}, u32[]{:S(2)}, u32[]{:S(2)}) collective-permute-start(bf16[144,1152]{1,0:T(8,128)(2,1)S(1)} %get-tuple-element.116.refs_0_), channel_id=1, source_target_pairs={{0,24},{4,28},{8,0},{12,4},{16,8},{20,12},{24,16},{28,20},{1,25},{... | collective-permute-start | bytes 995336 | tf_op jit(solution)/shard_map/ppermute | solution.py:660
  88.2 121.4 %collective-permute-start.7 = (bf16[576,1152]{1,0:T(8,128)(2,1)}, bf16[576,1152]{1,0:T(8,128)(2,1)}, u32[]{:S(2)}, u32[]{:S(2)}) collective-permute-start(bf16[576,1152]{1,0:T(8,128)(2,1)} %constant_dynamic-slice_fusion.7), channel_id=1, source_target_pairs={{0,1},{1,0},{2,3},{3,2},{4,5},{5,4},{6,7},{7,6},{8,9},{9,8},{10,11... | collective-permute-start | bytes 3981320 | tf_op jit(solution)/shard_map/ppermute | solution.py:670
  89.3 120.2 %collective-permute-start.8 = (bf16[576,1152]{1,0:T(8,128)(2,1)}, bf16[576,1152]{1,0:T(8,128)(2,1)}, u32[]{:S(2)}, u32[]{:S(2)}) collective-permute-start(bf16[576,1152]{1,0:T(8,128)(2,1)} %constant_dynamic-slice_fusion.7), channel_id=1, source_target_pairs={{0,2},{1,3},{2,0},{3,1},{4,6},{5,7},{6,4},{7,5},{8,10},{9,11},{10,... | collective-permute-start | bytes 3981320 | tf_op jit(solution)/shard_map/ppermute | solution.py:670
  90.8 118.8 %collective-permute-start.9 = (bf16[576,1152]{1,0:T(8,128)(2,1)}, bf16[576,1152]{1,0:T(8,128)(2,1)}, u32[]{:S(2)}, u32[]{:S(2)}) collective-permute-start(bf16[576,1152]{1,0:T(8,128)(2,1)} %constant_dynamic-slice_fusion.7), channel_id=1, source_target_pairs={{0,3},{1,2},{2,1},{3,0},{4,7},{5,6},{6,5},{7,4},{8,11},{9,10},{10,... | collective-permute-start | bytes 3981320 | tf_op jit(solution)/shard_map/ppermute | solution.py:670
  212.5 36.3 %collective-permute-start.13 = (bf16[6,144,288]{2,1,0:T(8,128)(2,1)S(1)}, bf16[6,144,288]{2,1,0:T(8,128)(2,1)S(1)}, u32[]{:S(2)}, u32[]{:S(2)}) collective-permute-start(bf16[6,144,288]{2,1,0:T(8,128)(2,1)S(1)} %get-tuple-element.228), channel_id=1, source_target_pairs={{0,1},{1,0},{2,3},{3,2},{4,5},{5,4},{6,7},{7,6},{8,9},{9,8},{10,11... | collective-permute-start | bytes 1493000 | tf_op jit(solution)/shard_map/ppermute | solution.py:670
  213.8 47.5 %collective-permute-start.14 = (bf16[6,144,288]{2,1,0:T(8,128)(2,1)S(1)}, bf16[6,144,288]{2,1,0:T(8,128)(2,1)S(1)}, u32[]{:S(2)}, u32[]{:S(2)}) collective-permute-start(bf16[6,144,288]{2,1,0:T(8,128)(2,1)S(1)} %get-tuple-element.227), channel_id=1, source_target_pairs={{0,2},{1,3},{2,0},{3,1},{4,6},{5,7},{6,4},{7,5},{8,10},{9,11},{10,... | collective-permute-start | bytes 1493000 | tf_op jit(solution)/shard_map/ppermute | solution.py:670
  226.4 39.4 %collective-permute-start.15 = (bf16[6,144,288]{2,1,0:T(8,128)(2,1)S(1)}, bf16[6,144,288]{2,1,0:T(8,128)(2,1)S(1)}, u32[]{:S(2)}, u32[]{:S(2)}) collective-permute-start(bf16[6,144,288]{2,1,0:T(8,128)(2,1)S(1)} %get-tuple-element.226), channel_id=1, source_target_pairs={{0,3},{1,2},{2,1},{3,0},{4,7},{5,6},{6,5},{7,4},{8,11},{9,10},{10,... | collective-permute-start | bytes 1493000 | tf_op jit(solution)/shard_map/ppermute | solution.py:670
  265.8 62.8 %collective-permute-start.16 = (bf16[4,576,1152]{2,1,0:T(8,128)(2,1)}, bf16[4,576,1152]{2,1,0:T(8,128)(2,1)}, u32[]{:S(2)}, u32[]{:S(2)}) collective-permute-start(bf16[4,576,1152]{2,1,0:T(8,128)(2,1)} %convolution_convert_fusion.1), channel_id=1, source_target_pairs={{0,4},{4,0},{8,12},{12,8},{16,20},{20,16},{24,28},{28,24},{1,5},{5... | collective-permute-start | bytes 15925256 | tf_op jit(solution)/shard_map/ppermute | solution.py:655
  275.3 106.7 %all-gather.16.cloned.1.call-start = ((), (), s32[]{:S(2)}) async-start(), calls=%async_computation.7 | async-start | bytes 2985984 | tf_op jit(solution)/shard_map/all_gather | solution.py:798
  348.9 33.0 %collective-permute-start.17 = (bf16[4,576,1152]{2,1,0:T(8,128)(2,1)}, bf16[4,576,1152]{2,1,0:T(8,128)(2,1)}, u32[]{:S(2)}, u32[]{:S(2)}) collective-permute-start(bf16[4,576,1152]{2,1,0:T(8,128)(2,1)} %fusion.1), channel_id=1, source_target_pairs={{0,4},{4,0},{8,12},{12,8},{16,20},{20,16},{24,28},{28,24},{1,5},{5... | collective-permute-start | bytes 15925256 | tf_op jit(solution)/shard_map/ppermute | solution.py:655
  349.1 88.4 %all-gather.18.cloned.1.call-start = ((), (), s32[]{:S(2)}) async-start(), calls=%async_computation.8 | async-start | bytes 2985984 | tf_op jit(solution)/shard_map/all_gather | solution.py:798
  349.2 32.8 %collective-permute-start.18 = (bf16[2,2,144,1152]{3,2,1,0:T(8,128)(2,1)}, bf16[2,2,144,1152]{3,2,1,0:T(8,128)(2,1)}, u32[]{:S(2)}, u32[]{:S(2)}) collective-permute-start(bf16[2,2,144,1152]{3,2,1,0:T(8,128)(2,1)} %dynamic-slice_bitcast_fusion.5), channel_id=1, source_target_pairs={{0,1},{1,0},{2,3},{3,2},{4,5},{5,4},{6,7},{7,6},{8,9},{9,8},{10,11... | collective-permute-start | bytes 3981320 | tf_op jit(solution)/shard_map/ppermute | solution.py:670
  350.2 31.8 %collective-permute-start.19 = (bf16[2,2,144,1152]{3,2,1,0:T(8,128)(2,1)}, bf16[2,2,144,1152]{3,2,1,0:T(8,128)(2,1)}, u32[]{:S(2)}, u32[]{:S(2)}) collective-permute-start(bf16[2,2,144,1152]{3,2,1,0:T(8,128)(2,1)} %dynamic-slice_bitcast_fusion.4), channel_id=1, source_target_pairs={{0,2},{1,3},{2,0},{3,1},{4,6},{5,7},{6,4},{7,5},{8,10},{9,11},{10,... | collective-permute-start | bytes 3981320 | tf_op jit(solution)/shard_map/ppermute | solution.py:670
  351.7 277.3 %all-gather.24.cloned.1.call-start = ((), (), s32[]{:S(2)}) async-start(), calls=%async_computation.11 | async-start | bytes 2985984 | tf_op jit(solution)/shard_map/all_gather | solution.py:843
  396.8 40.7 %collective-permute-start.20 = (bf16[2,144,1152]{2,1,0:T(8,128)(2,1)}, bf16[2,144,1152]{2,1,0:T(8,128)(2,1)}, u32[]{:S(2)}, u32[]{:S(2)}) collective-permute-start(bf16[2,144,1152]{2,1,0:T(8,128)(2,1)} %dynamic-slice_bitcast_fusion.14), channel_id=1, source_target_pairs={{0,2},{1,3},{2,0},{3,1},{4,6},{5,7},{6,4},{7,5},{8,10},{9,11},{10,... | collective-permute-start | bytes 1990664 | tf_op jit(solution)/shard_map/ppermute | solution.py:670
  398.4 45.5 %collective-permute-start.22 = (bf16[2,2,144,1152]{3,2,1,0:T(8,128)(2,1)}, bf16[2,2,144,1152]{3,2,1,0:T(8,128)(2,1)}, u32[]{:S(2)}, u32[]{:S(2)}) collective-permute-start(bf16[2,2,144,1152]{3,2,1,0:T(8,128)(2,1)} %dynamic-slice_bitcast_fusion.3), channel_id=1, source_target_pairs={{0,1},{1,0},{2,3},{3,2},{4,5},{5,4},{6,7},{7,6},{8,9},{9,8},{10,11... | collective-permute-start | bytes 3981320 | tf_op jit(solution)/shard_map/ppermute | solution.py:670
  399.8 44.0 %collective-permute-start.23 = (bf16[2,2,144,1152]{3,2,1,0:T(8,128)(2,1)}, bf16[2,2,144,1152]{3,2,1,0:T(8,128)(2,1)}, u32[]{:S(2)}, u32[]{:S(2)}) collective-permute-start(bf16[2,2,144,1152]{3,2,1,0:T(8,128)(2,1)} %dynamic-slice_bitcast_fusion.2), channel_id=1, source_target_pairs={{0,2},{1,3},{2,0},{3,1},{4,6},{5,7},{6,4},{7,5},{8,10},{9,11},{10,... | collective-permute-start | bytes 3981320 | tf_op jit(solution)/shard_map/ppermute | solution.py:670
  403.0 40.8 %collective-permute-start.21 = (bf16[2,144,1152]{2,1,0:T(8,128)(2,1)}, bf16[2,144,1152]{2,1,0:T(8,128)(2,1)}, u32[]{:S(2)}, u32[]{:S(2)}) collective-permute-start(bf16[2,144,1152]{2,1,0:T(8,128)(2,1)} %dynamic-slice_bitcast_fusion.13), channel_id=1, source_target_pairs={{0,1},{1,0},{2,3},{3,2},{4,5},{5,4},{6,7},{7,6},{8,9},{9,8},{10,11... | collective-permute-start | bytes 1990664 | tf_op jit(solution)/shard_map/ppermute | solution.py:670
  461.9 38.3 %collective-permute-start.26 = (bf16[2,144,1152]{2,1,0:T(8,128)(2,1)S(1)}, bf16[2,144,1152]{2,1,0:T(8,128)(2,1)}, u32[]{:S(2)}, u32[]{:S(2)}) collective-permute-start(bf16[2,144,1152]{2,1,0:T(8,128)(2,1)S(1)} %dynamic-slice_bitcast_fusion.11), channel_id=1, source_target_pairs={{0,2},{1,3},{2,0},{3,1},{4,6},{5,7},{6,4},{7,5},{8,10},{9,11},{10,... | collective-permute-start | bytes 1990664 | tf_op jit(solution)/shard_map/ppermute | solution.py:670
  464.3 35.8 %collective-permute-start.27 = (bf16[2,144,1152]{2,1,0:T(8,128)(2,1)S(1)}, bf16[2,144,1152]{2,1,0:T(8,128)(2,1)S(1)}, u32[]{:S(2)}, u32[]{:S(2)}) collective-permute-start(bf16[2,144,1152]{2,1,0:T(8,128)(2,1)S(1)} %dynamic-slice_bitcast_fusion.10), channel_id=1, source_target_pairs={{0,1},{1,0},{2,3},{3,2},{4,5},{5,4},{6,7},{7,6},{8,9},{9,8},{10,11... | collective-permute-start | bytes 1990664 | tf_op jit(solution)/shard_map/ppermute | solution.py:670
  487.0 56.1 %collective-permute-start.29 = (bf16[2,2,144,1152]{3,2,1,0:T(8,128)(2,1)}, bf16[2,2,144,1152]{3,2,1,0:T(8,128)(2,1)}, u32[]{:S(2)}, u32[]{:S(2)}) collective-permute-start(bf16[2,2,144,1152]{3,2,1,0:T(8,128)(2,1)} %dynamic-slice_bitcast_fusion.1), channel_id=1, source_target_pairs={{0,1},{1,0},{2,3},{3,2},{4,5},{5,4},{6,7},{7,6},{8,9},{9,8},{10,11... | collective-permute-start | bytes 3981320 | tf_op jit(solution)/shard_map/ppermute | solution.py:670
  488.5 54.6 %collective-permute-start.30 = (bf16[2,2,144,1152]{3,2,1,0:T(8,128)(2,1)}, bf16[2,2,144,1152]{3,2,1,0:T(8,128)(2,1)}, u32[]{:S(2)}, u32[]{:S(2)}) collective-permute-start(bf16[2,2,144,1152]{3,2,1,0:T(8,128)(2,1)} %dynamic-slice_bitcast_fusion), channel_id=1, source_target_pairs={{0,2},{1,3},{2,0},{3,1},{4,6},{5,7},{6,4},{7,5},{8,10},{9,11},{10,... | collective-permute-start | bytes 3981320 | tf_op jit(solution)/shard_map/ppermute | solution.py:670
  501.9 148.9 %all-gather.28.cloned.1.call-start = ((), (), s32[]{:S(2)}) async-start(), calls=%async_computation.13 | async-start | bytes 2985984 | tf_op jit(solution)/shard_map/all_gather | solution.py:843
  505.3 37.9 %collective-permute-start.31 = (bf16[2,144,1152]{2,1,0:T(8,128)(2,1)S(1)}, bf16[2,144,1152]{2,1,0:T(8,128)(2,1)}, u32[]{:S(2)}, u32[]{:S(2)}) collective-permute-start(bf16[2,144,1152]{2,1,0:T(8,128)(2,1)S(1)} %dynamic-slice_bitcast_fusion.9), channel_id=1, source_target_pairs={{0,8},{4,12},{8,0},{12,4},{16,24},{20,28},{24,16},{28,20},{1,9},{5... | collective-permute-start | bytes 1990664 | tf_op jit(solution)/shard_map/ppermute | solution.py:665
  573.4 40.1 %collective-permute-start.35 = (bf16[2,144,1152]{2,1,0:T(8,128)(2,1)S(1)}, bf16[2,144,1152]{2,1,0:T(8,128)(2,1)S(1)}, u32[]{:S(2)}, u32[]{:S(2)}) collective-permute-start(bf16[2,144,1152]{2,1,0:T(8,128)(2,1)S(1)} %dynamic-slice_bitcast_fusion.6), channel_id=1, source_target_pairs={{0,8},{4,12},{8,0},{12,4},{16,24},{20,28},{24,16},{28,20},{1,9},{5... | collective-permute-start | bytes 1990664 | tf_op jit(solution)/shard_map/ppermute | solution.py:665
  574.2 39.3 %all-to-all-start.2 = ((f32[8,1,3960]{2,1,0:T(1,128)}), f32[8,1,3960]{2,1,0:T(1,128)S(1)}, u32[]{:S(2)}, u32[]{:S(2)}) async-start(f32[8,1,3960]{2,1,0:T(1,128)} %all_to_all.29), calls=%async_computation.2 | async-start | bytes 253952 | tf_op jit(solution)/shard_map/all_to_all | solution.py:1127
  577.6 113.3 %all-gather.26.cloned.1.call-start = ((), (), s32[]{:S(2)}) async-start(), calls=%async_computation.12 | async-start | bytes 2985984 | tf_op jit(solution)/shard_map/all_gather | solution.py:843
  660.6 30.3 %all-to-all-start.3 = ((bf16[4,3,144,288]{3,2,1,0:T(8,128)(2,1)}), bf16[4,3,144,288]{3,2,1,0:T(8,128)(2,1)}, u32[]{:S(2)}, u32[]{:S(2)}) async-start(bf16[4,3,144,288]{3,2,1,0:T(8,128)(2,1)} %shard_map.213), calls=%async_computation.3 | async-start | bytes 2654208 | tf_op jit(solution)/shard_map/all_to_all | solution.py:740
  (95 other events, 1174.1 us)
Sparse Core Ops, SparseCore 0:
  32.7 134.1 all-gather.19
  169.9 123.0 all-gather.21
  295.3 32.7 all-gather.13
  349.2 32.6 all-gather.15
  383.5 33.1 all-gather.17
  502.0 41.7 all-gather.23
  570.7 42.7 all-gather.27
  639.3 33.7 all-gather.25

commit v13 on v12

--- a/solution.py
+++ b/solution.py
@@ -977,7 +977,8 @@
         packed([mod_cols, bias_rows, left_cond], 8), "fsdp", axis=0, tiled=True
     )
     second_parts, one_parts = tie(second_parts, one_parts)
-    one_parts = one_steps.send(one_steps.send(one_parts))
+    one_parts, attn_w = tie(one_steps.send(one_parts), attn_w)
+    one_parts = one_steps.send(one_parts)
     second_parts = second_parts.reshape(ranks, -1)
     mods = second_parts[:, :mod_size].reshape(ranks, clip_count, mod_count, col_part)
     mods = mods.transpose(1, 2, 0, 3).reshape(clip_count, mod_count, width)
@@ -991,10 +992,6 @@
         [bias_all[6:7], jnp.zeros((1, width), jnp.float32), bias_all[7:14]]
     )
 
-    roots = jnp.stack([narrow(left_roots[mod_count:]), narrow(right_roots[mod_count:])])
-    mods, roots = tie(mods, roots)
-    root_rows = own_rows(roots.reshape(-1, group, row_part, col_part), group)
-    root_panels = next(root_rows)
     attn_in, parts, mixed, proj, resid, mlp_in, d_branch, d_branch_sums = run_attention(
         frames, frame_counts, stream, grad_out, mods, bias_table, attn_w
     )
@@ -1009,12 +1006,11 @@
         group,
     )
     two_parts = next(two_steps)
-    hidden, two_parts, root_panels = tie(hidden, two_parts, root_panels)
+    roots = jnp.stack([narrow(left_roots[mod_count:]), narrow(right_roots[mod_count:])])
+    hidden, two_parts, roots = tie(hidden, two_parts, roots)
     two_parts = two_steps.send(two_parts)
-    root_rows = root_rows.send(root_panels)
-    hidden, root_rows = tie(hidden, root_rows)
-    left_rows, right_rows = jnp.split(root_rows, 2)
-    right_wholes = [gather_own(rows[None], group)[0] for rows in right_rows]
+    root_rows = own_rows(roots.reshape(-1, group, row_part, col_part), group)
+    root_panels = next(root_rows)
     d_pre, d_pre_sums, block_out, d_gate_two = run_branch(
         frames,
         frame_counts,
@@ -1027,10 +1023,13 @@
         resid,
         grad_out,
     )
-    d_pre, two_parts, right_wholes[2] = tie(d_pre, two_parts, right_wholes[2])
+    d_pre, two_parts, root_panels = tie(d_pre, two_parts, root_panels)
     two_parts = two_steps.send(two_parts)
-    d_pre, two_parts = tie(d_pre, two_parts)
+    root_rows = root_rows.send(root_panels)
+    d_pre, two_parts, root_rows = tie(d_pre, two_parts, root_rows)
     two_parts = two_steps.send(two_parts)
+    left_rows, right_rows = jnp.split(root_rows, 2)
+    right_wholes = [gather_own(rows[None], group)[0] for rows in right_rows]
     one_steps = sum_blocks(
         lambda left: fast_dot("td,jte->jde", left, d_pre),
         lambda first, size: lax.dynamic_slice_in_dim(mlp_in, first, size, 1),
@@ -1043,16 +1042,14 @@
     d_resid, d_proj, resid_sums = run_resid(
         frames, frame_counts, d_pre, one_w, mods, resid, grad_out, proj
     )
-    d_proj, one_parts, two_parts, right_wholes[1] = tie(
-        d_proj, one_parts, two_parts, right_wholes[1]
-    )
+    d_proj, one_parts, two_parts = tie(d_proj, one_parts, two_parts)
     two_parts = two_steps.send(two_parts)
     one_parts = one_steps.send(one_parts)
-    d_proj, one_parts = tie(d_proj, one_parts)
+    d_proj, one_parts, right_wholes[2] = tie(d_proj, one_parts, right_wholes[2])
     one_parts = one_steps.send(one_parts)
     d_heads, head_sums = run_attention_back(frames, frame_counts, d_proj, parts, attn_w)
-    d_heads, two_parts, one_parts, right_wholes[0] = tie(
-        d_heads, two_parts, one_parts, right_wholes[0]
+    d_heads, two_parts, one_parts, right_wholes[1] = tie(
+        d_heads, two_parts, one_parts, right_wholes[1]
     )
     two_parts = two_steps.send(two_parts)
     one_parts = one_steps.send(one_parts)
@@ -1073,11 +1070,10 @@
     d_heads, attn_parts = tie(d_heads, attn_parts)
     attn_parts = attn_steps.send(attn_parts)
     input_grad, input_sums = run_input(d_heads, attn_w, mods, stream, d_resid)
-    input_sums, one_parts, two_parts = tie(input_sums, one_parts, two_parts)
+    input_sums, one_parts, two_parts, right_wholes[0] = tie(
+        input_sums, one_parts, two_parts, right_wholes[0]
+    )
     whole_two = two_steps.send(two_parts)
-    one_parts = one_steps.send(one_parts)
-    input_sums, attn_parts, one_parts = tie(input_sums, attn_parts, one_parts)
-    attn_parts = attn_steps.send(attn_parts)
     one_parts = one_steps.send(one_parts)
 
     d_mods = jnp.stack(
@@ -1113,10 +1109,11 @@
         ],
         axis=1,
     )
-    rank_sums = jnp.sum(lax.all_to_all(to_ranks, "fsdp", 0, 0, tiled=True), axis=0)
+    rank_sums = lax.all_to_all(to_ranks, "fsdp", 0, 0, tiled=True)
     rank_sums, attn_parts, one_parts = tie(rank_sums, attn_parts, one_parts)
     attn_parts = attn_steps.send(attn_parts)
-    whole_one = one_steps.send(one_parts)
+    one_parts = one_steps.send(one_parts)
+    rank_sums = jnp.sum(rank_sums, axis=0)
     to_rows = jnp.concatenate(
         [
             jnp.broadcast_to(rank_sums[None, :mod_size], (dp_count, mod_size)),
@@ -1125,11 +1122,14 @@
         axis=1,
     )
     from_rows = lax.all_to_all(to_rows, "dp", 0, 0, tiled=True)
-    from_rows, attn_parts = tie(from_rows, attn_parts)
+    from_rows, attn_parts, one_parts = tie(from_rows, attn_parts, one_parts)
     attn_parts = attn_steps.send(attn_parts)
+    whole_one = one_steps.send(one_parts)
     bias_grad = jnp.sum(from_rows[:, mod_size:], axis=0)
     mod_grad_cols = from_rows[:, :mod_size].reshape(all_clips, mod_count, col_part)
     mod_grad = lax.all_gather(packed([mod_grad_cols], 8), "fsdp", axis=0, tiled=True)
+    mod_grad, attn_parts = tie(mod_grad, attn_parts)
+    attn_parts = attn_steps.send(attn_parts)
     mod_grad = mod_grad.reshape(ranks, -1)[:, : mod_grad_cols.size]
     mod_grad = mod_grad.reshape(ranks, all_clips, mod_count, col_part).transpose(1, 2, 0, 3)
     mod_grad = mod_grad.reshape(all_clips, mod_count, width)

time: 753 us -> 728 us (0.967)
  waiting for transfers between devices: 241 us -> 206 us
  blocking collectives: 64.9 us -> 86 us
  starting transfers between devices: 64.5 us -> 52.1 us
    all_to_all x1 -> x0, waiting for transfers between devices: 35.8 us -> none  [per_device(): from_rows = lax.all_to_all(to_rows, 'dp', 0, 0, tiled=True)]
    all_gather x2, waiting for transfers between devices: 84.3 us -> 53.8 us  [gather_blocks(): all_rows = lax.all_gather(rows, ('fsdp', 'dp'), axis=0, tiled=True)]
    ppermute x21, waiting for transfers between devices: 23.4 us -> 52.2 us  [rank_swap(): return lax.ppermute(array, 'fsdp', [(at, at ^ bits) for at in range(count)])]
    all_to_all x1 -> x2, blocking collectives: 12.6 us -> 35 us  [the longest x1 26.5 us: per_device(): from_rows = lax.all_to_all(to_rows, 'dp', 0, 0, tiled=True)]
    all_gather x3, waiting for transfers between devices: 11.5 us -> 0.01 us  [gather_own(): return lax.all_gather(rows, 'dp', axis=1, tiled=True)]
    ppermute x21, starting transfers between devices: 35.1 us -> 24.1 us  [rank_swap(): return lax.ppermute(array, 'fsdp', [(at, at ^ bits) for at in range(count)])]
    ppermute x6, waiting for transfers between devices: 48.2 us -> 58.1 us  [chip_swap(): lax.ppermute(array, 'dp', [(at, at ^ 2 * bits) for at in range(count)])]
    unnamed x156 -> x157, local copies, waits for them, and re-layouts: 17 us -> 15.2 us
  transfers between devices with their start and end apart: 50 -> 49, of which waited for: 15 -> 15; matrix products, arithmetic and copies ran while one was open for 18% -> 18% of each run, Pallas kernels for 20% -> 21%
where the time goes in v13:
time: 728 us; the launch traced here: 722 us
  waiting for transfers between devices  206 us (28%)
  Pallas kernels  161 us (22%)
  blocking collectives  86 us (12%)
  local copies, waits for them, and re-layouts  73.4 us (10%)
  other arithmetic  65 us (9%)
  matrix products  62.3 us (9%)
  starting transfers between devices  52.1 us (7%)
  between operations  16.3 us (2%)
    ppermute x6, waiting for transfers between devices, chip_swap(): lax.ppermute(array, 'dp', [(at, at ^ 2 * bits) for at in range(count)])  58.1 us
    all_gather x2, waiting for transfers between devices, gather_blocks(): all_rows = lax.all_gather(rows, ('fsdp', 'dp'), axis=0, tiled=True)  53.8 us
    ppermute x21, waiting for transfers between devices, rank_swap(): return lax.ppermute(array, 'fsdp', [(at, at ^ bits) for at in range(count)])  52.2 us
    dot_general x7, matrix products, fast_dot(): jnp.einsum(subscripts, left, right, preferred_element_type=jnp.float32)  48.1 us
    pallas_call x1, Pallas kernels, run_attention(): pl.pallas_call(functools.partial(attention_kernel, frames), grid=(clips,)...  41.1 us
    convert_element_type x22, other arithmetic, narrow(): return array.astype(jnp.bfloat16)  37.7 us
    all_to_all x1, blocking collectives, per_device(): from_rows = lax.all_to_all(to_rows, 'dp', 0, 0, tiled=True)  26.5 us
    pallas_call x1, Pallas kernels, run_attention_back(): pl.pallas_call(functools.partial(attention_back_kernel, frames), grid=(cl...  26.3 us
  transfers between devices with their start and end apart: 49, of which 15 were waited for; matrix products, arithmetic and copies ran while one was open for 18% of the time, Pallas kernels for 21%

profile of v13, /device:TPU:0, one launch (start us, length us, event | category | flops | bytes accessed | tf_op | source)
XLA Modules:
  0.0 722.4 jit_solution(1702583396319428296)
XLA Ops:
  15.8 14.7 %all_gather.36 = bf16[256,128]{1,0:T(8,128)(2,1)S(1)} all-gather(bf16[32,128]{1,0:T(8,128)(2,1)S(1)} %fusion.84), channel_id=1, replica_groups=mesh['dp'=8,'fsdp'=4] {'dp'}, dimensions={0}, use_global_device_ids=true | all-gather | bytes 73728 | tf_op jit(solution)/shard_map/all_gather | solution.py:951
  43.3 8.8 %all-to-all-done = f32[16,6,288]{2,1,0:T(8,128)S(1)} async-done(((f32[16,6,288]{2,1,0:T(8,128)}), f32[16,6,288]{2,1,0:T(8,128)S(1)}, u32[]{:S(2)}, u32[]{:S(2)}) %all-to-all-start) | async-done | bytes 110624 | tf_op jit(solution)/shard_map/all_to_all | solution.py:969
  56.2 9.5 %all_gather.37 = f32[672,128]{1,0:T(8,128)S(1)} all-gather(f32[168,128]{1,0:T(8,128)S(1)} %pad_bitcast_fusion), channel_id=1, replica_groups=mesh['dp'=8,'fsdp'=4] {'fsdp'}, dimensions={0}, use_global_device_ids=true | all-gather | bytes 430080 | tf_op jit(solution)/shard_map/all_gather | solution.py:976
  65.7 12.2 %collective-permute-done.4.refs_2_ = bf16[144,1152]{1,0:T(8,128)(2,1)S(1)} collective-permute-done((bf16[144,1152]{1,0:T(8,128)(2,1)S(1)}, bf16[144,1152]{1,0:T(8,128)(2,1)S(1)}, u32[]{:S(2)}, u32[]{:S(2)}) %collective-permute-start.4) | collective-permute-done | bytes 331808 | tf_op jit(solution)/shard_map/ppermute | solution.py:660
  85.9 53.8 %all-gather.20.cloned.1.call-done = bf16[1,4608,1152]{2,1,0:T(8,128)(2,1)} async-done(((bf16[1,144,1152]{2,1,0:T(8,128)(2,1)}), bf16[1,4608,1152]{2,1,0:T(8,128)(2,1)}) %all-gather.20.cloned.1.call-update) | async-done | bytes 10616848 | tf_op jit(solution)/shard_map/all_gather | solution.py:749
  146.8 41.1 %shard_map.206 = (bf16[512,1152]{1,0:T(8,128)(2,1)S(1)}, bf16[5,512,1152]{2,1,0:T(8,128)(2,1)}, bf16[512,1152]{1,0:T(8,128)(2,1)S(1)}, f32[512,1152]{1,0:T(8,128...) custom-call(s32[2]{0:T(128)S(1)} %copy-done.25, ...), custom_call_target="tpu_custom_call" | custom-call | flops 1024 | bytes 1024 | tf_op jit(solution)/shard_map/pallas_call | solution.py:216
  189.5 32.8 %collective-permute-done.9.refs_5_ = bf16[576,1152]{1,0:T(8,128)(2,1)} collective-permute-done((bf16[576,1152]{1,0:T(8,128)(2,1)}, bf16[576,1152]{1,0:T(8,128)(2,1)}, u32[]{:S(2)}, u32[]{:S(2)}) %collective-permute-start.9) | collective-permute-done | bytes 1327136 | tf_op jit(solution)/shard_map/ppermute | solution.py:670
  229.7 14.2 %shard_map.207 = (bf16[4608,1152]{1,0:T(8,128)(2,1)}, bf16[4,512,1152]{2,1,0:T(8,128)(2,1)}, bf16[4,512,1152]{2,1,0:T(8,128)(2,1)}) custom-call(s32[4]{0:T(128)S(1)} %pad_add_fusion.order, s32[7]{0:T(128)S(1)} %stack.128.starts, bf16[512,1152]{1,0:T(8,128)(2,1)S(1)} %copy-done.10, f32[4,1,1152]{2,1,0:T(1,128)S(1)} %copy.115.bias, ...), custom_call_target="tpu_custom_call" | custom-call | flops 1024 | bytes 1024 | tf_op jit(solution)/shard_map/pallas_call | solution.py:324
  244.0 7.9 %convolution_convert_fusion.1 = bf16[4,576,1152]{2,1,0:T(8,128)(2,1)} fusion(bf16[4,512,1152]{2,1,0:T(8,128)(2,1)} %get-tuple-element.130.hidden, s32[]{:T(128)S(6)} %select_n.352, bf16[512,1152]{1,0:T(8,128)(2,1)S(1)} %copy-done.14), kind=kOutput, calls=%fused_computation.5 | convolution fusion | flops 2720563200 | bytes 9109508 | tf_op jit(solution)/shard_map/jtd,te->jde/dot_general | solution.py:847
  262.8 21.8 %shard_map.208 = (bf16[4,512,1152]{2,1,0:T(8,128)(2,1)}, f32[4,1,1152]{2,1,0:T(1,128)S(1)}, bf16[512,1152]{1,0:T(8,128)(2,1)}, f32[2,1,1152]{2,1,0:T(1,128)S(1)}) custom-call(s32[4]{0:T(128)S(1)} %iota.6.order, s32[4]{0:T(128)S(1)} %copy-done.26, s32[2]{0:T(128)S(1)} %copy-done.25, bf16[4,512,1152]{2,1,0:T(8,128)(2,1)} %get-tuple-element.130.hidden, ...), custom_call_target="tpu_custom_call" | custom-call | flops 1024 | bytes 1024 | tf_op jit(solution)/shard_map/pallas_call | solution.py:404
  284.6 9.6 %fusion.10 = f32[4,576,1152]{2,1,0:T(8,128)} fusion(bf16[4,512,1152]{2,1,0:T(8,128)(2,1)} %get-tuple-element.130.hidden, s32[]{:T(128)S(6)} %select_n.351, bf16[512,1152]{1,0:T(8,128)(2,1)S(1)} %copy-done.15), kind=kOutput, calls=%fused_computation.29 | convolution fusion | flops 2717908992 | bytes 14417924 | tf_op jit(solution)/shard_map/jtd,te->jde/dot_general | solution.py:847
  294.3 8.9 %add_convert_fusion.1 = bf16[4,576,1152]{2,1,0:T(8,128)(2,1)} fusion(f32[4,576,1152]{2,1,0:T(8,128)} %fusion.10, bf16[4,576,1152]{2,1,0:T(8,128)(2,1)} %collective-permute-done.13), kind=kLoop, calls=%fused_computation.3 | loop fusion | flops 7962624 | bytes 21233664 | tf_op jit(solution)/shard_map/convert_element_type | solution.py:27
  317.8 8.2 %fusion.1 = bf16[4,576,1152]{2,1,0:T(8,128)(2,1)} fusion(bf16[4,512,1152]{2,1,0:T(8,128)(2,1)} %get-tuple-element.144.d_pre, bf16[512,1152]{1,0:T(8,128)(2,1)} %copy-done.9, s32[]{:T(128)S(6)} %select_n.352), kind=kOutput, calls=%fused_computation.7 | convolution fusion | flops 2720563200 | bytes 10682372 | tf_op jit(solution)/shard_map/td,jte->jde/dot_general | solution.py:847
  331.6 16.4 %shard_map.209 = (f32[512,1152]{1,0:T(8,128)}, bf16[512,1152]{1,0:T(8,128)(2,1)S(1)}, f32[2,4,1152]{2,1,0:T(4,128)S(1)}) custom-call(s32[2]{0:T(128)S(1)} %copy-done.25, bf16[4,512,1152]{2,1,0:T(8,128)(2,1)} %get-tuple-element.144.d_pre, bf16[4,1152,1152]{2,1,0:T(8,128)(2,1)} %bitcast.306, f32[2,6,1152]{2,1,0:T(8,128)S(1)} %copy-done.7, ...), custom_call_target="tpu_custom_call" | custom-call | flops 1024 | bytes 1024 | tf_op jit(solution)/shard_map/pallas_call | solution.py:496
  348.0 11.4 %collective-permute-done.18 = bf16[2,2,144,1152]{3,2,1,0:T(8,128)(2,1)} collective-permute-done((bf16[2,2,144,1152]{3,2,1,0:T(8,128)(2,1)}, bf16[2,2,144,1152]{3,2,1,0:T(8,128)(2,1)}, u32[]{:S(2)}, u32[]{:S(2)}) %collective-permute-start.18) | collective-permute-done | bytes 1327136 | tf_op jit(solution)/shard_map/ppermute | solution.py:670
  364.2 7.7 %fusion = bf16[4,576,1152]{2,1,0:T(8,128)(2,1)S(1)} fusion(bf16[4,576,1152]{2,1,0:T(8,128)(2,1)} %collective-permute-done.17, bf16[4,512,1152]{2,1,0:T(8,128)(2,1)} %get-tuple-element.144.d_pre, bf16[512,1152]{1,0:T(8,128)(2,1)S(1)} %copy-done.11, s32[]{:T(128)S(6)} %select_n.351), kind=kOutput, calls=%fused_computation.1 | convolution fusion | flops 2725871616 | bytes 15990788 | tf_op jit(solution)/shard_map/td,jte->jde/dot_general | solution.py:847
  389.0 26.3 %shard_map.210 = (bf16[4,512,1152]{2,1,0:T(8,128)(2,1)}, f32[2,3,1152]{2,1,0:T(4,128)S(1)}) custom-call(s32[2]{0:T(128)S(1)} %copy-done.25, bf16[512,1152]{1,0:T(8,128)(2,1)S(1)} %copy-done.13, bf16[5,512,1152]{2,1,0:T(8,128)(2,1)} %get-tuple-element.155.parts, bf16[4,1152,1152]{2,1,0:T(8,128)(2,1)} %bitcast.302), custom_call_target="tpu_custom_call" | custom-call | flops 1024 | bytes 1024 | tf_op jit(solution)/shard_map/pallas_call | solution.py:563
  415.4 6.9 collective-permute-done.20
  422.3 7.3 %convolution_convert_fusion = bf16[4,576,1152]{2,1,0:T(8,128)(2,1)} fusion(bf16[4,512,1152]{2,1,0:T(8,128)(2,1)} %get-tuple-element.170.d_qkv, bf16[1,512,576]{1,2,0:T(8,128)(2,1)S(1)} %bitcast.331, bf16[1,512,576]{1,2,0:T(8,128)(2,1)S(1)} %bitcast.330), kind=kOutput, calls=%fused_computation.4 | convolution fusion | flops 2724102144 | bytes 11206656 | tf_op jit(solution)/shard_map/jtd,jte->jde/dot_general | solution.py:847
  446.9 28.9 %collective-permute-done.25 = bf16[2,144,1152]{2,1,0:T(8,128)(2,1)S(1)} collective-permute-done((bf16[2,144,1152]{2,1,0:T(8,128)(2,1)S(1)}, bf16[2,144,1152]{2,1,0:T(8,128)(2,1)S(1)}, u32[]{:S(2)}, u32[]{:S(2)}) %collective-permute-start.25) | collective-permute-done | bytes 663584 | tf_op jit(solution)/shard_map/ppermute | solution.py:665
  476.8 6.2 add_convert_fusion
  488.2 11.1 %shard_map.211 = (bf16[512,1152]{1,0:T(8,128)(2,1)}, f32[2,2,1152]{2,1,0:T(2,128)S(1)}) custom-call(bf16[4,512,1152]{2,1,0:T(8,128)(2,1)} %get-tuple-element.170.d_qkv, bf16[4,1152,1152]{2,1,0:T(8,128)(2,1)} %bitcast.303, f32[2,6,1152]{2,1,0:T(8,128)S(1)} %copy-done.8, bf16[512,1152]{1,0:T(8,128)(2,1)S(1)} %bitcast.300, f32[512,1152]{1,0:T(8,128)S(1)} %copy-done.2), custom_call_target="tpu_custom_call" | custom-call | flops 1024 | bytes 1024 | tf_op jit(solution)/shard_map/pallas_call | solution.py:623
  510.2 8.5 %all_to_all.44 = f32[4,1,7488]{2,1,0:T(1,128)S(1)} all-to-all(f32[4,1,7488]{2,1,0:T(1,128)S(1)} %copy.132), channel_id=1, replica_groups=mesh['dp'=8,'fsdp'=4] {'fsdp'}, dimensions={0} | all-to-all | bytes 239616 | tf_op jit(solution)/shard_map/all_to_all | solution.py:1112
  532.3 26.5 %all_to_all.45 = f32[8,1,3960]{2,1,0:T(1,128)S(1)} all-to-all(f32[8,1,3960]{2,1,0:T(1,128)S(1)} %all_to_all.32), channel_id=1, replica_groups=mesh['dp'=8,'fsdp'=4] {'dp'}, dimensions={0} | all-to-all | bytes 253440 | tf_op jit(solution)/shard_map/all_to_all | solution.py:1124
  563.6 10.0 %all_gather.43 = f32[864,128]{1,0:T(8,128)S(1)} all-gather(f32[216,128]{1,0:T(8,128)S(1)} %reshape.305), channel_id=1, replica_groups=mesh['dp'=8,'fsdp'=4] {'fsdp'}, dimensions={0}, use_global_device_ids=true | all-gather | bytes 552960 | tf_op jit(solution)/shard_map/all_gather | solution.py:1130
  573.5 27.0 %collective-permute-done.35 = bf16[2,144,1152]{2,1,0:T(8,128)(2,1)S(1)} collective-permute-done((bf16[2,144,1152]{2,1,0:T(8,128)(2,1)S(1)}, bf16[2,144,1152]{2,1,0:T(8,128)(2,1)S(1)}, u32[]{:S(2)}, u32[]{:S(2)}) %collective-permute-start.35) | collective-permute-done | bytes 663584 | tf_op jit(solution)/shard_map/ppermute | solution.py:665
  605.5 8.3 %shard_map.212 = bf16[4,3,144,288]{3,2,1,0:T(8,128)(2,1)} custom-call(s32[1]{0:T(128)} %bitcast.103.at, bf16[1152,1152]{1,0:T(8,128)(2,1)} %bitcast.324, bf16[144,1152]{1,0:T(8,128)(2,1)S(1)} %copy-done.5, bf16[1152,1152]{1,0:T(8,128)(2,1)} %bitcast.322), custom_call_target="tpu_custom_call" | custom-call | flops 1024 | bytes 1024 | tf_op jit(solution)/shard_map/pallas_call | solution.py:890
  628.0 8.4 %shard_map.213 = bf16[4,3,144,288]{3,2,1,0:T(8,128)(2,1)} custom-call(s32[1]{0:T(128)} %bitcast.103.at, bf16[1152,1152]{1,0:T(8,128)(2,1)} %bitcast.325, bf16[144,1152]{1,0:T(8,128)(2,1)S(1)} %copy-done.4, bf16[1152,1152]{1,0:T(8,128)(2,1)} %bitcast.321), custom_call_target="tpu_custom_call" | custom-call | flops 1024 | bytes 1024 | tf_op jit(solution)/shard_map/pallas_call | solution.py:890
  647.2 16.9 %all_gather.47 = f32[1728,128]{1,0:T(8,128)} all-gather(f32[216,128]{1,0:T(8,128)S(1)} %reshape.312), channel_id=1, replica_groups=mesh['dp'=8,'fsdp'=4] {'dp'}, dimensions={0}, use_global_device_ids=true | all-gather | bytes 995328 | tf_op jit(solution)/shard_map/all_gather | solution.py:1156
  668.6 8.3 %shard_map.214 = bf16[4,3,144,288]{3,2,1,0:T(8,128)(2,1)} custom-call(s32[1]{0:T(128)} %bitcast.103.at, bf16[1152,1152]{1,0:T(8,128)(2,1)} %bitcast.326, bf16[144,1152]{1,0:T(8,128)(2,1)S(1)} %copy-done.3, bf16[1152,1152]{1,0:T(8,128)(2,1)} %bitcast.323), custom_call_target="tpu_custom_call" | custom-call | flops 1024 | bytes 1024 | tf_op jit(solution)/shard_map/pallas_call | solution.py:890
  686.5 12.5 %all-to-all-done.5 = bf16[4,3,144,288]{3,2,1,0:T(8,128)(2,1)} async-done(((bf16[4,3,144,288]{3,2,1,0:T(8,128)(2,1)}), bf16[4,3,144,288]{3,2,1,0:T(8,128)(2,1)}, u32[]{:S(2)}, u32[]{:S(2)}) %all-to-all-start.5) | async-done | bytes 995360 | tf_op jit(solution)/shard_map/all_to_all | solution.py:740
  701.5 6.7 fusion.92
  (416 shorter events, 207.3 us)
Async XLA Ops:
  7.2 132.5 %all-gather.20.cloned.1.call-start = ((), (), s32[]{:S(2)}) async-start(), calls=%async_computation.9 | async-start | bytes 10948608 | tf_op jit(solution)/shard_map/all_gather | solution.py:749
  32.6 227.6 %all-gather.22.cloned.1.call-start = ((), (), s32[]{:S(2)}) async-start(), calls=%async_computation.10 | async-start | bytes 10948608 | tf_op jit(solution)/shard_map/all_gather | solution.py:749
  40.6 335.7 %all-gather.14.cloned.1.call-start = ((), (), s32[]{:S(2)}) async-start(), calls=%async_computation.6 | async-start | bytes 2985984 | tf_op jit(solution)/shard_map/all_gather | solution.py:798
  142.2 47.4 %collective-permute-start.7 = (bf16[576,1152]{1,0:T(8,128)(2,1)}, bf16[576,1152]{1,0:T(8,128)(2,1)}, u32[]{:S(2)}, u32[]{:S(2)}) collective-permute-start(bf16[576,1152]{1,0:T(8,128)(2,1)} %constant_dynamic-slice_fusion.7), channel_id=1, source_target_pairs={{0,1},{1,0},{2,3},{3,2},{4,5},{5,4},{6,7},{7,6},{8,9},{9,8},{10,11... | collective-permute-start | bytes 3981320 | tf_op jit(solution)/shard_map/ppermute | solution.py:670
  143.6 45.9 %collective-permute-start.8 = (bf16[576,1152]{1,0:T(8,128)(2,1)}, bf16[576,1152]{1,0:T(8,128)(2,1)}, u32[]{:S(2)}, u32[]{:S(2)}) collective-permute-start(bf16[576,1152]{1,0:T(8,128)(2,1)} %constant_dynamic-slice_fusion.7), channel_id=1, source_target_pairs={{0,2},{1,3},{2,0},{3,1},{4,6},{5,7},{6,4},{7,5},{8,10},{9,11},{10,... | collective-permute-start | bytes 3981320 | tf_op jit(solution)/shard_map/ppermute | solution.py:670
  144.2 78.2 %collective-permute-start.9 = (bf16[576,1152]{1,0:T(8,128)(2,1)}, bf16[576,1152]{1,0:T(8,128)(2,1)}, u32[]{:S(2)}, u32[]{:S(2)}) collective-permute-start(bf16[576,1152]{1,0:T(8,128)(2,1)} %constant_dynamic-slice_fusion.7), channel_id=1, source_target_pairs={{0,3},{1,2},{2,1},{3,0},{4,7},{5,6},{6,5},{7,4},{8,11},{9,10},{10,... | collective-permute-start | bytes 3981320 | tf_op jit(solution)/shard_map/ppermute | solution.py:670
  251.8 42.5 %collective-permute-start.13 = (bf16[4,576,1152]{2,1,0:T(8,128)(2,1)}, bf16[4,576,1152]{2,1,0:T(8,128)(2,1)}, u32[]{:S(2)}, u32[]{:S(2)}) collective-permute-start(bf16[4,576,1152]{2,1,0:T(8,128)(2,1)} %convolution_convert_fusion.1), channel_id=1, source_target_pairs={{0,4},{4,0},{8,12},{12,8},{16,20},{20,16},{24,28},{28,24},{1,5},{5... | collective-permute-start | bytes 15925256 | tf_op jit(solution)/shard_map/ppermute | solution.py:655
  256.7 37.6 %collective-permute-start.14 = (bf16[6,144,288]{2,1,0:T(8,128)(2,1)}, bf16[6,144,288]{2,1,0:T(8,128)(2,1)}, u32[]{:S(2)}, u32[]{:S(2)}) collective-permute-start(bf16[6,144,288]{2,1,0:T(8,128)(2,1)} %get-tuple-element.228), channel_id=1, source_target_pairs={{0,1},{1,0},{2,3},{3,2},{4,5},{5,4},{6,7},{7,6},{8,9},{9,8},{10,11... | collective-permute-start | bytes 1493000 | tf_op jit(solution)/shard_map/ppermute | solution.py:670
  257.2 37.1 %collective-permute-start.15 = (bf16[6,144,288]{2,1,0:T(8,128)(2,1)}, bf16[6,144,288]{2,1,0:T(8,128)(2,1)}, u32[]{:S(2)}, u32[]{:S(2)}) collective-permute-start(bf16[6,144,288]{2,1,0:T(8,128)(2,1)} %get-tuple-element.227), channel_id=1, source_target_pairs={{0,2},{1,3},{2,0},{3,1},{4,6},{5,7},{6,4},{7,5},{8,10},{9,11},{10,... | collective-permute-start | bytes 1493000 | tf_op jit(solution)/shard_map/ppermute | solution.py:670
  259.7 34.6 %collective-permute-start.16 = (bf16[6,144,288]{2,1,0:T(8,128)(2,1)}, bf16[6,144,288]{2,1,0:T(8,128)(2,1)}, u32[]{:S(2)}, u32[]{:S(2)}) collective-permute-start(bf16[6,144,288]{2,1,0:T(8,128)(2,1)} %get-tuple-element.226), channel_id=1, source_target_pairs={{0,3},{1,2},{2,1},{3,0},{4,7},{5,6},{6,5},{7,4},{8,11},{9,10},{10,... | collective-permute-start | bytes 1493000 | tf_op jit(solution)/shard_map/ppermute | solution.py:670
  326.0 34.4 %collective-permute-start.17 = (bf16[4,576,1152]{2,1,0:T(8,128)(2,1)}, bf16[4,576,1152]{2,1,0:T(8,128)(2,1)}, u32[]{:S(2)}, u32[]{:S(2)}) collective-permute-start(bf16[4,576,1152]{2,1,0:T(8,128)(2,1)} %fusion.1), channel_id=1, source_target_pairs={{0,4},{4,0},{8,12},{12,8},{16,20},{20,16},{24,28},{28,24},{1,5},{5... | collective-permute-start | bytes 15925256 | tf_op jit(solution)/shard_map/ppermute | solution.py:655
  327.5 87.9 %all-gather.16.cloned.1.call-start = ((), (), s32[]{:S(2)}) async-start(), calls=%async_computation.7 | async-start | bytes 2985984 | tf_op jit(solution)/shard_map/all_gather | solution.py:798
  327.5 31.9 %collective-permute-start.18 = (bf16[2,2,144,1152]{3,2,1,0:T(8,128)(2,1)}, bf16[2,2,144,1152]{3,2,1,0:T(8,128)(2,1)}, u32[]{:S(2)}, u32[]{:S(2)}) collective-permute-start(bf16[2,2,144,1152]{3,2,1,0:T(8,128)(2,1)} %dynamic-slice_bitcast_fusion.5), channel_id=1, source_target_pairs={{0,1},{1,0},{2,3},{3,2},{4,5},{5,4},{6,7},{7,6},{8,9},{9,8},{10,11... | collective-permute-start | bytes 3981320 | tf_op jit(solution)/shard_map/ppermute | solution.py:670
  328.6 31.9 %collective-permute-start.19 = (bf16[2,2,144,1152]{3,2,1,0:T(8,128)(2,1)}, bf16[2,2,144,1152]{3,2,1,0:T(8,128)(2,1)}, u32[]{:S(2)}, u32[]{:S(2)}) collective-permute-start(bf16[2,2,144,1152]{3,2,1,0:T(8,128)(2,1)} %dynamic-slice_bitcast_fusion.4), channel_id=1, source_target_pairs={{0,2},{1,3},{2,0},{3,1},{4,6},{5,7},{6,4},{7,5},{8,10},{9,11},{10,... | collective-permute-start | bytes 3981320 | tf_op jit(solution)/shard_map/ppermute | solution.py:670
  330.6 168.7 %all-gather.18.cloned.1.call-start = ((), (), s32[]{:S(2)}) async-start(), calls=%async_computation.8 | async-start | bytes 2985984 | tf_op jit(solution)/shard_map/all_gather | solution.py:798
  363.5 51.9 %collective-permute-start.21 = (bf16[2,144,1152]{2,1,0:T(8,128)(2,1)}, bf16[2,144,1152]{2,1,0:T(8,128)(2,1)}, u32[]{:S(2)}, u32[]{:S(2)}) collective-permute-start(bf16[2,144,1152]{2,1,0:T(8,128)(2,1)} %dynamic-slice_bitcast_fusion.13), channel_id=1, source_target_pairs={{0,1},{1,0},{2,3},{3,2},{4,5},{5,4},{6,7},{7,6},{8,9},{9,8},{10,11... | collective-permute-start | bytes 1990664 | tf_op jit(solution)/shard_map/ppermute | solution.py:670
  376.3 45.9 %collective-permute-start.22 = (bf16[2,2,144,1152]{3,2,1,0:T(8,128)(2,1)}, bf16[2,2,144,1152]{3,2,1,0:T(8,128)(2,1)}, u32[]{:S(2)}, u32[]{:S(2)}) collective-permute-start(bf16[2,2,144,1152]{3,2,1,0:T(8,128)(2,1)} %dynamic-slice_bitcast_fusion.3), channel_id=1, source_target_pairs={{0,1},{1,0},{2,3},{3,2},{4,5},{5,4},{6,7},{7,6},{8,9},{9,8},{10,11... | collective-permute-start | bytes 3981320 | tf_op jit(solution)/shard_map/ppermute | solution.py:670
  377.6 44.7 %collective-permute-start.23 = (bf16[2,2,144,1152]{3,2,1,0:T(8,128)(2,1)}, bf16[2,2,144,1152]{3,2,1,0:T(8,128)(2,1)}, u32[]{:S(2)}, u32[]{:S(2)}) collective-permute-start(bf16[2,2,144,1152]{3,2,1,0:T(8,128)(2,1)} %dynamic-slice_bitcast_fusion.2), channel_id=1, source_target_pairs={{0,2},{1,3},{2,0},{3,1},{4,6},{5,7},{6,4},{7,5},{8,10},{9,11},{10,... | collective-permute-start | bytes 3981320 | tf_op jit(solution)/shard_map/ppermute | solution.py:670
  383.4 38.9 %collective-permute-start.20 = (bf16[2,144,1152]{2,1,0:T(8,128)(2,1)}, bf16[2,144,1152]{2,1,0:T(8,128)(2,1)}, u32[]{:S(2)}, u32[]{:S(2)}) collective-permute-start(bf16[2,144,1152]{2,1,0:T(8,128)(2,1)} %dynamic-slice_bitcast_fusion.14), channel_id=1, source_target_pairs={{0,2},{1,3},{2,0},{3,1},{4,6},{5,7},{6,4},{7,5},{8,10},{9,11},{10,... | collective-permute-start | bytes 1990664 | tf_op jit(solution)/shard_map/ppermute | solution.py:670
  429.5 46.3 %collective-permute-start.24 = (bf16[4,576,1152]{2,1,0:T(8,128)(2,1)}, bf16[4,576,1152]{2,1,0:T(8,128)(2,1)}, u32[]{:S(2)}, u32[]{:S(2)}) collective-permute-start(bf16[4,576,1152]{2,1,0:T(8,128)(2,1)} %convolution_convert_fusion), channel_id=1, source_target_pairs={{0,4},{4,0},{8,12},{12,8},{16,20},{20,16},{24,28},{28,24},{1,5},{5... | collective-permute-start | bytes 15925256 | tf_op jit(solution)/shard_map/ppermute | solution.py:655
  433.1 172.4 %all-gather.24.cloned.1.call-start = ((), (), s32[]{:S(2)}) async-start(), calls=%async_computation.11 | async-start | bytes 2985984 | tf_op jit(solution)/shard_map/all_gather | solution.py:843
  437.3 38.6 %collective-permute-start.25 = (bf16[2,144,1152]{2,1,0:T(8,128)(2,1)S(1)}, bf16[2,144,1152]{2,1,0:T(8,128)(2,1)S(1)}, u32[]{:S(2)}, u32[]{:S(2)}) collective-permute-start(bf16[2,144,1152]{2,1,0:T(8,128)(2,1)S(1)} %dynamic-slice_bitcast_fusion.12), channel_id=1, source_target_pairs={{0,8},{4,12},{8,0},{12,4},{16,24},{20,28},{24,16},{28,20},{1,9},{5... | collective-permute-start | bytes 1990664 | tf_op jit(solution)/shard_map/ppermute | solution.py:665
  441.5 57.8 %collective-permute-start.27 = (bf16[2,144,1152]{2,1,0:T(8,128)(2,1)}, bf16[2,144,1152]{2,1,0:T(8,128)(2,1)}, u32[]{:S(2)}, u32[]{:S(2)}) collective-permute-start(bf16[2,144,1152]{2,1,0:T(8,128)(2,1)} %dynamic-slice_bitcast_fusion.10), channel_id=1, source_target_pairs={{0,1},{1,0},{2,3},{3,2},{4,5},{5,4},{6,7},{7,6},{8,9},{9,8},{10,11... | collective-permute-start | bytes 1990664 | tf_op jit(solution)/shard_map/ppermute | solution.py:670
  445.3 54.0 %collective-permute-start.26 = (bf16[2,144,1152]{2,1,0:T(8,128)(2,1)}, bf16[2,144,1152]{2,1,0:T(8,128)(2,1)}, u32[]{:S(2)}, u32[]{:S(2)}) collective-permute-start(bf16[2,144,1152]{2,1,0:T(8,128)(2,1)} %dynamic-slice_bitcast_fusion.11), channel_id=1, source_target_pairs={{0,2},{1,3},{2,0},{3,1},{4,6},{5,7},{6,4},{7,5},{8,10},{9,11},{10,... | collective-permute-start | bytes 1990664 | tf_op jit(solution)/shard_map/ppermute | solution.py:670
  486.1 33.5 %collective-permute-start.29 = (bf16[2,2,144,1152]{3,2,1,0:T(8,128)(2,1)}, bf16[2,2,144,1152]{3,2,1,0:T(8,128)(2,1)}, u32[]{:S(2)}, u32[]{:S(2)}) collective-permute-start(bf16[2,2,144,1152]{3,2,1,0:T(8,128)(2,1)} %dynamic-slice_bitcast_fusion.1), channel_id=1, source_target_pairs={{0,1},{1,0},{2,3},{3,2},{4,5},{5,4},{6,7},{7,6},{8,9},{9,8},{10,11... | collective-permute-start | bytes 3981320 | tf_op jit(solution)/shard_map/ppermute | solution.py:670
  486.5 33.1 %collective-permute-start.30 = (bf16[2,2,144,1152]{3,2,1,0:T(8,128)(2,1)}, bf16[2,2,144,1152]{3,2,1,0:T(8,128)(2,1)}, u32[]{:S(2)}, u32[]{:S(2)}) collective-permute-start(bf16[2,2,144,1152]{3,2,1,0:T(8,128)(2,1)} %dynamic-slice_bitcast_fusion), channel_id=1, source_target_pairs={{0,2},{1,3},{2,0},{3,1},{4,6},{5,7},{6,4},{7,5},{8,10},{9,11},{10,... | collective-permute-start | bytes 3981320 | tf_op jit(solution)/shard_map/ppermute | solution.py:670
  509.1 118.8 %all-gather.28.cloned.1.call-start = ((), (), s32[]{:S(2)}) async-start(), calls=%async_computation.13 | async-start | bytes 2985984 | tf_op jit(solution)/shard_map/all_gather | solution.py:843
  522.1 36.7 %collective-permute-start.34 = (bf16[1,144,1152]{2,1,0:T(8,128)(2,1)}, bf16[1,144,1152]{2,1,0:T(8,128)(2,1)}, u32[]{:S(2)}, u32[]{:S(2)}) collective-permute-start(bf16[1,144,1152]{2,1,0:T(8,128)(2,1)} %constant_dynamic-slice_fusion.1), channel_id=1, source_target_pairs={{0,16},{4,20},{8,24},{12,28},{16,0},{20,4},{24,8},{28,12},{1,17},{... | collective-permute-start | bytes 995336 | tf_op jit(solution)/shard_map/ppermute | solution.py:665
  527.9 30.9 %collective-permute-start.33 = (bf16[2,144,1152]{2,1,0:T(8,128)(2,1)}, bf16[2,144,1152]{2,1,0:T(8,128)(2,1)}, u32[]{:S(2)}, u32[]{:S(2)}) collective-permute-start(bf16[2,144,1152]{2,1,0:T(8,128)(2,1)} %dynamic-slice_bitcast_fusion.7), channel_id=1, source_target_pairs={{0,1},{1,0},{2,3},{3,2},{4,5},{5,4},{6,7},{7,6},{8,9},{9,8},{10,11... | collective-permute-start | bytes 1990664 | tf_op jit(solution)/shard_map/ppermute | solution.py:670
  560.6 107.9 %all-gather.26.cloned.1.call-start = ((), (), s32[]{:S(2)}) async-start(), calls=%async_computation.12 | async-start | bytes 2985984 | tf_op jit(solution)/shard_map/all_gather | solution.py:843
  563.4 37.1 %collective-permute-start.35 = (bf16[2,144,1152]{2,1,0:T(8,128)(2,1)S(1)}, bf16[2,144,1152]{2,1,0:T(8,128)(2,1)S(1)}, u32[]{:S(2)}, u32[]{:S(2)}) collective-permute-start(bf16[2,144,1152]{2,1,0:T(8,128)(2,1)S(1)} %dynamic-slice_bitcast_fusion.6), channel_id=1, source_target_pairs={{0,8},{4,12},{8,0},{12,4},{16,24},{20,28},{24,16},{28,20},{1,9},{5... | collective-permute-start | bytes 1990664 | tf_op jit(solution)/shard_map/ppermute | solution.py:665
  639.6 28.9 %all-to-all-start.3 = ((bf16[4,3,144,288]{3,2,1,0:T(8,128)(2,1)}), bf16[4,3,144,288]{3,2,1,0:T(8,128)(2,1)}, u32[]{:S(2)}, u32[]{:S(2)}) async-start(bf16[4,3,144,288]{3,2,1,0:T(8,128)(2,1)} %shard_map.213), calls=%async_computation.3 | async-start | bytes 2654208 | tf_op jit(solution)/shard_map/all_to_all | solution.py:740
  (95 other events, 957.8 us)
Sparse Core Ops, SparseCore 0:
  32.7 106.8 all-gather.19
  143.3 105.3 all-gather.21
  327.6 32.8 all-gather.13
  362.0 33.1 all-gather.15
  433.3 41.9 all-gather.17
  509.3 50.8 all-gather.23
  562.4 40.7 all-gather.27
  617.2 33.1 all-gather.25

commit v14 on v13

--- a/solution.py
+++ b/solution.py
@@ -641,6 +641,108 @@
     )(d_qkv, blocks, mods, tokens, d_resid)
 
 
+def halves_kernel(left_of, adds, steps, order, side, *refs):
+    lefts = refs[: max(left_of) + 1]
+    right = refs[len(lefts)]
+    turned, total_low = refs[-2:]
+    if adds:
+        incoming, first_keep, first_out, second_keep, second_out = refs[len(lefts) + 1 : -2]
+    else:
+        out = refs[-3]
+    step = pl.program_id(0)
+    block = order[step]
+    width = lefts[0].shape[-1]
+    half = width // 2
+
+    def pick(left, at):
+        lanes = slice(at * half, (at + 1) * half)
+        turned[...] = (left[:, lanes] if left.ndim == 2 else left[0, :, lanes]).T
+
+    fresh = (step == 0) | (lefts[0].ndim == 3) | (len(lefts) > 1)
+    for at in range(2):
+        for index, left in enumerate(lefts):
+            of_left = [block == number for number, source in enumerate(left_of) if source == index]
+
+            @pl.when(fresh & (side[0] == at) & functools.reduce(jnp.logical_or, of_left))
+            def _(left=left, at=at):
+                pick(left, at)
+
+    found = dot_nn(turned[...], right[0] if right.ndim == 3 else right[...])
+    if not adds:
+        out[0] = narrow(found)
+        return
+    total_low[...] = narrow(found + wide(incoming[0]))
+    for state, target, rows in (
+        (steps[0][0], first_keep, slice(0, half // 2)),
+        (steps[0][1], first_out, slice(0, half // 2)),
+        (steps[1][0], second_keep, slice(half // 2, half)),
+        (steps[1][1], second_out, slice(half // 2, half)),
+    ):
+
+        @pl.when(functools.reduce(jnp.logical_or, [step == at_step for at_step in state]))
+        def _(target=target, rows=rows):
+            target[0] = total_low[rows]
+
+
+def run_halves(lefts, left_of, right, side, at, incoming=None):
+    total, width = lefts[0].shape[-2:]
+    half = width // 2
+    low_bit, high_bit = at % 2, at // 2
+    order = stacked([at ^ 3, at ^ 1, at, at ^ 2])
+    places = {
+        "first_keep": [high_bit, high_bit, high_bit, 1 - high_bit],
+        "first_out": [1 - high_bit, high_bit, high_bit, high_bit],
+        "second_keep": [1 - low_bit, 1 - low_bit, low_bit, low_bit],
+        "second_out": [1 - low_bit, low_bit, low_bit, low_bit],
+    }
+    steps = (((2, 3), (0, 1)), ((1, 2), (0, 3)))
+    adds = incoming is not None
+    table = stacked([place for row in places.values() for place in row])
+
+    def block_of(array, *rest):
+        if array.ndim == 2:
+            return pl.BlockSpec(array.shape, lambda step, order, side, table: (0, 0))
+        return pl.BlockSpec((1,) + array.shape[1:], lambda step, order, side, table: (order[step], 0, 0))
+
+    per_block = pl.BlockSpec((1, half, width), lambda step, order, side, table: (order[step], 0, 0))
+    operands = list(lefts) + [right]
+    in_specs = [block_of(array) for array in operands]
+    if adds:
+        operands.append(incoming)
+        in_specs.append(per_block)
+        out_specs = [
+            pl.BlockSpec(
+                (1, half // 2, width),
+                functools.partial(lambda row, step, order, side, table: (table[row * 4 + step], 0, 0), row),
+            )
+            for row in range(4)
+        ]
+        out_shape = [jax.ShapeDtypeStruct((2, half // 2, width), jnp.bfloat16)] * 4
+    else:
+        out_specs = per_block
+        out_shape = jax.ShapeDtypeStruct((4, half, width), jnp.bfloat16)
+
+    def body(order, side, table, *refs):
+        halves_kernel(left_of, adds, steps, order, side, *refs)
+
+    return pl.pallas_call(
+        body,
+        grid_spec=pltpu.PrefetchScalarGridSpec(
+            num_scalar_prefetch=3,
+            grid=(4,),
+            in_specs=in_specs,
+            out_specs=out_specs,
+            scratch_shapes=[
+                pltpu.VMEM((half, total), jnp.bfloat16),
+                pltpu.VMEM((half, width), jnp.bfloat16),
+            ],
+        ),
+        out_shape=out_shape,
+        compiler_params=pltpu.CompilerParams(vmem_limit_bytes=vmem_bytes),
+        cost_estimate=little_cost,
+    )(order, stacked([side]), table, *operands)
+
+
 def tie(*values):
     return lax.optimization_barrier(values)
 
@@ -798,11 +900,23 @@
     return lax.all_gather(rows, "dp", axis=1, tiled=True)
 
 
-def sum_blocks(product, cut, total, group):
+def sum_blocks(lefts, left_of, right, group):
     ranks, dp_count = lax.axis_size("fsdp"), lax.axis_size("dp")
     shares = ranks // group
+    total = lefts[0].shape[-1]
     if shares > 1:
-        blocks = narrow(product(cut(0, total)))
+        blocks = jnp.stack(
+            [
+                narrow(
+                    fast_dot(
+                        "tr,te->re",
+                        lefts[index] if lefts[index].ndim == 2 else lefts[index][block],
+                        right if right.ndim == 2 else right[block],
+                    )
+                )
+                for block, index in enumerate(left_of)
+            ]
+        )
         chunk = total // (dp_count * shares)
         blocks = blocks.reshape(group, dp_count, shares, chunk, -1).transpose(0, 2, 1, 3, 4)
         rows = lax.psum_scatter(
@@ -814,19 +928,16 @@
         return
     chips, half = dp_count // 2, total // 2
     chunk = half // chips
+    at = lax.axis_index("fsdp")
     core, chip = lax.axis_index("dp") % 2, lax.axis_index("dp") // 2
-    low_bit, high_bit = lax.axis_index("fsdp") % 2, lax.axis_index("fsdp") // 2
-    (away,) = yield (narrow(product(cut((1 - core) * half, half))),)
+    low_bit, high_bit = at % 2, at // 2
+    (away,) = yield (run_halves(lefts, left_of, right, 1 - core, at),)
     (away_in,) = yield (core_swap(away),)
-    here = product(cut(core * half, half))
-    here = narrow(here + wide(away_in))
-    here = here.reshape(2, 2, chips, chunk, -1)
-    middle = chips // 2
-    first, second = here[:, :, :middle], here[:, :, middle:]
-    first_out, second_out = yield (entry(first, 1 - low_bit, 1), entry(second, 1 - high_bit, 0))
+    first, first_out, second, second_out = run_halves(lefts, left_of, right, core, at, away_in)
+    first_out, second_out = yield (first_out, second_out)
     first_in, second_in = yield (rank_swap(first_out, 1), rank_swap(second_out, 2))
-    first = narrow(wide(entry(first, low_bit, 1)) + wide(first_in))
-    second = narrow(wide(entry(second, high_bit, 0)) + wide(second_in))
+    first = narrow(wide(first) + wide(first_in)).reshape(2, chips // 2, chunk, -1)
+    second = narrow(wide(second) + wide(second_in)).reshape(2, chips // 2, chunk, -1)
     first_in = rank_swap(entry(first, 1 - high_bit), 2)
     second_in = rank_swap(entry(second, 1 - low_bit), 1)
     first_in, second_in = yield (first_in, second_in)
@@ -999,12 +1110,7 @@
     one_w, hidden, slope = run_hidden(mlp_in, one_steps.send(one_parts), bias_table[4:8, None])
     one_w = one_w.reshape(group, width, width)
 
-    two_steps = sum_blocks(
-        lambda left: fast_dot("jtd,te->jde", left, d_branch),
-        lambda first, size: lax.dynamic_slice_in_dim(hidden, first, size, 2),
-        width,
-        group,
-    )
+    two_steps = sum_blocks([hidden], [0] * group, d_branch, group)
     two_parts = next(two_steps)
     roots = jnp.stack([narrow(left_roots[mod_count:]), narrow(right_roots[mod_count:])])
     hidden, two_parts, roots = tie(hidden, two_parts, roots)
@@ -1023,19 +1129,15 @@
         resid,
         grad_out,
     )
-    d_pre, two_parts, root_panels = tie(d_pre, two_parts, root_panels)
-    two_parts = two_steps.send(two_parts)
+    d_pre, root_panels = tie(d_pre, root_panels)
     root_rows = root_rows.send(root_panels)
     d_pre, two_parts, root_rows = tie(d_pre, two_parts, root_rows)
     two_parts = two_steps.send(two_parts)
+    d_pre, two_parts = tie(d_pre, two_parts)
+    two_parts = two_steps.send(two_parts)
     left_rows, right_rows = jnp.split(root_rows, 2)
     right_wholes = [gather_own(rows[None], group)[0] for rows in right_rows]
-    one_steps = sum_blocks(
-        lambda left: fast_dot("td,jte->jde", left, d_pre),
-        lambda first, size: lax.dynamic_slice_in_dim(mlp_in, first, size, 1),
-        width,
-        group,
-    )
+    one_steps = sum_blocks([mlp_in], [0] * group, d_pre, group)
     one_parts = next(one_steps)
     d_pre, one_parts = tie(d_pre, one_parts)
     one_parts = one_steps.send(one_parts)
@@ -1053,14 +1155,7 @@
     )
     two_parts = two_steps.send(two_parts)
     one_parts = one_steps.send(one_parts)
-    attn_steps = sum_blocks(
-        lambda left: fast_dot("jtd,jte->jde", left, d_heads),
-        lambda first, size: jnp.stack(
-            [lax.dynamic_slice_in_dim(left, first, size, 1) for left in (attn_in,) * 3 + (mixed,)]
-        ),
-        width,
-        group,
-    )
+    attn_steps = sum_blocks([attn_in, mixed], [0, 0, 0, 1], d_heads, group)
     attn_parts = next(attn_steps)
     d_heads, attn_parts = tie(d_heads, attn_parts)
     attn_parts = attn_steps.send(attn_parts)
@@ -1121,15 +1216,19 @@
         ],
         axis=1,
     )
-    from_rows = lax.all_to_all(to_rows, "dp", 0, 0, tiled=True)
-    from_rows, attn_parts, one_parts = tie(from_rows, attn_parts, one_parts)
+    to_rows, attn_parts, one_parts = tie(to_rows, attn_parts, one_parts)
     attn_parts = attn_steps.send(attn_parts)
     whole_one = one_steps.send(one_parts)
+    products_two = owned_step(whole_two, left_rows[2], right_wholes[2], group)
+    products_two, attn_parts = tie(products_two, attn_parts)
+    attn_parts = attn_steps.send(attn_parts)
+    back_two = shard_rows(products_two, group)
+    to_rows, back_two, attn_parts = tie(to_rows, back_two, attn_parts)
+    whole_attn = attn_steps.send(attn_parts)
+    from_rows = lax.all_to_all(to_rows, "dp", 0, 0, tiled=True)
     bias_grad = jnp.sum(from_rows[:, mod_size:], axis=0)
     mod_grad_cols = from_rows[:, :mod_size].reshape(all_clips, mod_count, col_part)
     mod_grad = lax.all_gather(packed([mod_grad_cols], 8), "fsdp", axis=0, tiled=True)
-    mod_grad, attn_parts = tie(mod_grad, attn_parts)
-    attn_parts = attn_steps.send(attn_parts)
     mod_grad = mod_grad.reshape(ranks, -1)[:, : mod_grad_cols.size]
     mod_grad = mod_grad.reshape(ranks, all_clips, mod_count, col_part).transpose(1, 2, 0, 3)
     mod_grad = mod_grad.reshape(all_clips, mod_count, width)
@@ -1147,19 +1246,13 @@
     cond_side = jnp.einsum("cb,bje->jce", cond_gram, mod_grad_cols, precision=precise)
     ada_right = jnp.einsum("cjr,jce->jre", mod_grad_rows, cond_side, precision=precise)
 
-    products_two = owned_step(whole_two, left_rows[2], right_wholes[2], group)
-    products_two, right_parts, attn_parts = tie(products_two, right_parts, attn_parts)
-    whole_attn = attn_steps.send(attn_parts)
-    back_two = shard_rows(products_two, group)
     products_one = owned_step(whole_one, left_rows[1], right_wholes[1], group)
     back_one = shard_rows(products_one, group)
     right_parts = lax.all_gather(packed([right_parts], 8), "dp", axis=0, tiled=True)
     mod_right = jnp.sum(right_parts.reshape(dp_count, -1), axis=0)[: mod_grad_cols.size]
     mod_right = mod_right.reshape(all_clips, mod_count, col_part)
     ada_pre = jnp.einsum("jrc,cje->jre", left_cond, mod_right, precision=precise)
-    whole_attn, back_one, back_two, ada_pre, ada_left, ada_right = tie(
-        whole_attn, back_one, back_two, ada_pre, ada_left, ada_right
-    )
+    whole_attn, right_parts = tie(whole_attn, right_parts)
     back_attn = shard_rows(owned_step(whole_attn, left_rows[0], right_wholes[0], group), group)
 
     def joined(at, ada):

time: 728 us -> 734 us (level)
  waiting for transfers between devices: 206 us -> 268 us
  Pallas kernels: 161 us -> 214 us
  matrix products: 62.3 us -> 11.8 us
  local copies, waits for them, and re-layouts: 73.4 us -> 49.5 us
  blocking collectives: 86 us -> 64 us
  other arithmetic: 65 us -> 54.5 us
    pallas_call x0 -> x6, Pallas kernels: none -> 54.5 us  [run_halves(): pl.pallas_call(body, grid_spec=pltpu.PrefetchScalarGridSpec(num_scalar_pr...]
    dot_general x7 -> x1, matrix products: 48.1 us -> 1.37 us  [fast_dot(): jnp.einsum(subscripts, left, right, preferred_element_type=jnp.float32)]
    ppermute x6, waiting for transfers between devices: 58.1 us -> 97.3 us  [chip_swap(): lax.ppermute(array, 'dp', [(at, at ^ 2 * bits) for at in range(count)])]
    all_to_all x1 -> x0, blocking collectives: 26.5 us -> none  [per_device(): from_rows = lax.all_to_all(to_rows, 'dp', 0, 0, tiled=True)]
    ppermute x21, waiting for transfers between devices: 52.2 us -> 63.8 us  [rank_swap(): return lax.ppermute(array, 'fsdp', [(at, at ^ bits) for at in range(count)])]
    squeeze x20 -> x14, local copies, waits for them, and re-layouts: 19 us -> 8.22 us  [entry(): return lax.dynamic_index_in_dim(array, at, axis, keepdims=False)]
    convert_element_type x22 -> x21, other arithmetic: 37.7 us -> 28.6 us  [narrow(): return array.astype(jnp.bfloat16)]
    dynamic_slice x5 -> x0, local copies, waits for them, and re-layouts: 8.66 us -> none  [per_device(): lax.dynamic_slice_in_dim(left, first, size, 1)]
  transfers between devices with their start and end apart: 49 -> 50, of which waited for: 15 -> 20; matrix products, arithmetic and copies ran while one was open for 18% -> 10% of each run, Pallas kernels for 21% -> 28%
where the time goes in v14:
time: 734 us; the launch traced here: 727 us
  waiting for transfers between devices  268 us (37%)
  Pallas kernels  214 us (29%)
  blocking collectives  64 us (9%)
  other arithmetic  54.5 us (7%)
  starting transfers between devices  50 us (7%)
  local copies, waits for them, and re-layouts  49.5 us (7%)
  between operations  15.9 us (2%)
  matrix products  11.8 us (2%)
    ppermute x6, waiting for transfers between devices, chip_swap(): lax.ppermute(array, 'dp', [(at, at ^ 2 * bits) for at in range(count)])  97.3 us
    ppermute x21, waiting for transfers between devices, rank_swap(): return lax.ppermute(array, 'fsdp', [(at, at ^ bits) for at in range(count)])  63.8 us
    pallas_call x6, Pallas kernels, run_halves(): pl.pallas_call(body, grid_spec=pltpu.PrefetchScalarGridSpec(num_scalar_pr...  54.5 us
    all_gather x2, waiting for transfers between devices, gather_blocks(): all_rows = lax.all_gather(rows, ('fsdp', 'dp'), axis=0, tiled=True)  53.8 us
    pallas_call x1, Pallas kernels, run_attention(): pl.pallas_call(functools.partial(attention_kernel, frames), grid=(clips,)...  41.1 us
    convert_element_type x21, other arithmetic, narrow(): return array.astype(jnp.bfloat16)  28.6 us
    pallas_call x1, Pallas kernels, run_attention_back(): pl.pallas_call(functools.partial(attention_back_kernel, frames), grid=(cl...  26.2 us
    pallas_call x3, Pallas kernels, owned_step(): pl.pallas_call(functools.partial(products_kernel, dp_count // 2), in_spec...  25 us
  transfers between devices with their start and end apart: 50, of which 20 were waited for; matrix products, arithmetic and copies ran while one was open for 10% of the time, Pallas kernels for 28%

profile of v14, /device:TPU:0, one launch (start us, length us, event | category | flops | bytes accessed | tf_op | source)
XLA Modules:
  0.0 727.2 jit_solution(4991799729302292328)
XLA Ops:
  15.8 14.7 %all_gather.36 = bf16[256,128]{1,0:T(8,128)(2,1)S(1)} all-gather(bf16[32,128]{1,0:T(8,128)(2,1)S(1)} %fusion.52), channel_id=1, replica_groups=mesh['dp'=8,'fsdp'=4] {'dp'}, dimensions={0}, use_global_device_ids=true | all-gather | bytes 73728 | tf_op jit(solution)/shard_map/all_gather | solution.py:1062
  43.3 8.8 %all-to-all-done = f32[16,6,288]{2,1,0:T(8,128)S(1)} async-done(((f32[16,6,288]{2,1,0:T(8,128)}), f32[16,6,288]{2,1,0:T(8,128)S(1)}, u32[]{:S(2)}, u32[]{:S(2)}) %all-to-all-start) | async-done | bytes 110624 | tf_op jit(solution)/shard_map/all_to_all | solution.py:1080
  56.2 9.5 %all_gather.37 = f32[672,128]{1,0:T(8,128)S(1)} all-gather(f32[168,128]{1,0:T(8,128)S(1)} %pad_bitcast_fusion), channel_id=1, replica_groups=mesh['dp'=8,'fsdp'=4] {'fsdp'}, dimensions={0}, use_global_device_ids=true | all-gather | bytes 430080 | tf_op jit(solution)/shard_map/all_gather | solution.py:1087
  65.7 12.2 %collective-permute-done.4.refs_2_ = bf16[144,1152]{1,0:T(8,128)(2,1)S(1)} collective-permute-done((bf16[144,1152]{1,0:T(8,128)(2,1)S(1)}, bf16[144,1152]{1,0:T(8,128)(2,1)S(1)}, u32[]{:S(2)}, u32[]{:S(2)}) %collective-permute-start.4) | collective-permute-done | bytes 331808 | tf_op jit(solution)/shard_map/ppermute | solution.py:762
  85.8 53.8 %all-gather.20.cloned.1.call-done = bf16[1,4608,1152]{2,1,0:T(8,128)(2,1)} async-done(((bf16[1,144,1152]{2,1,0:T(8,128)(2,1)}), bf16[1,4608,1152]{2,1,0:T(8,128)(2,1)}) %all-gather.20.cloned.1.call-update) | async-done | bytes 10616848 | tf_op jit(solution)/shard_map/all_gather | solution.py:851
  146.8 41.1 %shard_map.206 = (bf16[512,1152]{1,0:T(8,128)(2,1)S(1)}, bf16[5,512,1152]{2,1,0:T(8,128)(2,1)}, bf16[512,1152]{1,0:T(8,128)(2,1)S(1)}, f32[512,1152]{1,0:T(8,128...) custom-call(s32[2]{0:T(128)S(1)} %copy-done.32, ...), custom_call_target="tpu_custom_call" | custom-call | flops 1024 | bytes 1024 | tf_op jit(solution)/shard_map/pallas_call | solution.py:216
  190.6 31.8 %collective-permute-done.9.refs_5_ = bf16[576,1152]{1,0:T(8,128)(2,1)} collective-permute-done((bf16[576,1152]{1,0:T(8,128)(2,1)}, bf16[576,1152]{1,0:T(8,128)(2,1)}, u32[]{:S(2)}, u32[]{:S(2)}) %collective-permute-start.9) | collective-permute-done | bytes 1327136 | tf_op jit(solution)/shard_map/ppermute | solution.py:772
  229.7 13.9 %shard_map.207 = (bf16[4608,1152]{1,0:T(8,128)(2,1)}, bf16[4,512,1152]{2,1,0:T(8,128)(2,1)}, bf16[4,512,1152]{2,1,0:T(8,128)(2,1)}) custom-call(s32[4]{0:T(128)S(1)} %get-tuple-element.272.order, s32[7]{0:T(128)S(1)} %stack.91.starts, bf16[512,1152]{1,0:T(8,128)(2,1)S(1)} %get-tuple-element.132.mlp_in.refs_0_, f32[4,1,1152]{2,1,0:T(1,128)S(1)} %copy.92.bias, ...), custom_call_target="tpu_custom_call" | custom-call | flops 1024 | bytes 1024 | tf_op jit(solution)/shard_map/pallas_call | solution.py:324
  243.6 8.8 %shard_map.208 = bf16[4,576,1152]{2,1,0:T(8,128)(2,1)} custom-call(s32[4]{0:T(128)S(1)} %get-tuple-element.273.order, s32[1]{0:T(128)} %bitcast.41.side, s32[16]{0:T(128)S(1)} %stack.112.table, bf16[4,512,1152]{2,1,0:T(8,128)(2,1)} %get-tuple-element.138.refs_0_.hidden, bf16[512,1152]{1,0:T(8,128)(2,1)S(1)} %copy-done.1), custom_call_target="tpu_custom_call" | custom-call | flops 1024 | bytes 1024 | tf_op jit(solution)/shard_map/pallas_call | solution.py:728
  262.3 21.6 %shard_map.209 = (bf16[4,512,1152]{2,1,0:T(8,128)(2,1)}, f32[4,1,1152]{2,1,0:T(1,128)S(1)}, bf16[512,1152]{1,0:T(8,128)(2,1)}, f32[2,1,1152]{2,1,0:T(1,128)S(1)}) custom-call(s32[4]{0:T(128)S(1)} %iota.6.order, s32[4]{0:T(128)S(1)} %copy-done.35, s32[2]{0:T(128)S(1)} %copy-done.33, bf16[4,512,1152]{2,1,0:T(8,128)(2,1)} %get-tuple-element.138.refs_0_.hidden, ...), custom_call_target="tpu_custom_call" | custom-call | flops 1024 | bytes 1024 | tf_op jit(solution)/shard_map/pallas_call | solution.py:404
  298.4 9.5 %shard_map.210 = (bf16[2,288,1152]{2,1,0:T(8,128)(2,1)S(1)}, bf16[2,288,1152]{2,1,0:T(8,128)(2,1)S(1)}, bf16[2,288,1152]{2,1,0:T(8,128)(2,1)}, bf16[2,288,1152]{2,1,0:T(8,128)(2,1)}) custom-call(s32[4]{0:T(128)S(1)} %copy-done.24, s32[1]{0:T(128)} %bitcast.55.side, s32[16]{0:T(128)S(1)} %stack.112.table, ...), custom_call_target="tpu_custom_call" | custom-call | flops 1024 | bytes 1024 | tf_op jit(solution)/shard_map/pallas_call | solution.py:728
  307.9 8.4 %shard_map.211 = bf16[4,576,1152]{2,1,0:T(8,128)(2,1)} custom-call(s32[4]{0:T(128)S(1)} %copy-done.24, s32[1]{0:T(128)} %bitcast.41.side, s32[16]{0:T(128)S(1)} %stack.112.table, bf16[512,1152]{1,0:T(8,128)(2,1)S(1)} %get-tuple-element.132.mlp_in.refs_0_, bf16[4,512,1152]{2,1,0:T(8,128)(2,1)} %get-tuple-element.155.refs_1_.d_pre), custom_call_target="tpu_custom_call" | custom-call | flops 1024 | bytes 1024 | tf_op jit(solution)/shard_map/pallas_call | solution.py:728
  318.8 15.7 %shard_map.212 = (f32[512,1152]{1,0:T(8,128)}, bf16[512,1152]{1,0:T(8,128)(2,1)S(1)}, f32[2,4,1152]{2,1,0:T(4,128)S(1)}) custom-call(s32[2]{0:T(128)S(1)} %copy-done.34, bf16[4,512,1152]{2,1,0:T(8,128)(2,1)} %get-tuple-element.155.refs_1_.d_pre, bf16[4,1152,1152]{2,1,0:T(8,128)(2,1)} %bitcast.262, f32[2,6,1152]{2,1,0:T(8,128)S(1)} %copy-done.20, ...), custom_call_target="tpu_custom_call" | custom-call | flops 1024 | bytes 1024 | tf_op jit(solution)/shard_map/pallas_call | solution.py:496
  334.5 14.2 %collective-permute-done.18 = bf16[2,288,1152]{2,1,0:T(8,128)(2,1)} collective-permute-done((bf16[2,288,1152]{2,1,0:T(8,128)(2,1)}, bf16[2,288,1152]{2,1,0:T(8,128)(2,1)}, u32[]{:S(2)}, u32[]{:S(2)}) %collective-permute-start.18) | collective-permute-done | bytes 1327136 | tf_op jit(solution)/shard_map/ppermute | solution.py:772
  353.3 8.9 %shard_map.213 = (bf16[2,288,1152]{2,1,0:T(8,128)(2,1)S(1)}, bf16[2,288,1152]{2,1,0:T(8,128)(2,1)S(1)}, bf16[2,288,1152]{2,1,0:T(8,128)(2,1)}, bf16[2,288,1152]{2,1,0:T(8,128)(2,1)}) custom-call(s32[4]{0:T(128)S(1)} %copy-done.24, s32[1]{0:T(128)} %bitcast.55.side, s32[16]{0:T(128)S(1)} %stack.112.table, ...), custom_call_target="tpu_custom_call" | custom-call | flops 1024 | bytes 1024 | tf_op jit(solution)/shard_map/pallas_call | solution.py:728
  370.4 26.2 %shard_map.214 = (bf16[4,512,1152]{2,1,0:T(8,128)(2,1)}, f32[2,3,1152]{2,1,0:T(4,128)S(1)}) custom-call(s32[2]{0:T(128)S(1)} %copy-done.34, bf16[512,1152]{1,0:T(8,128)(2,1)S(1)} %copy-done.22, bf16[5,512,1152]{2,1,0:T(8,128)(2,1)} %get-tuple-element.168.parts, bf16[4,1152,1152]{2,1,0:T(8,128)(2,1)} %bitcast.259), custom_call_target="tpu_custom_call" | custom-call | flops 1024 | bytes 1024 | tf_op jit(solution)/shard_map/pallas_call | solution.py:563
  396.5 13.8 %collective-permute-done.20 = bf16[2,144,1152]{2,1,0:T(8,128)(2,1)} collective-permute-done((bf16[2,144,1152]{2,1,0:T(8,128)(2,1)}, bf16[2,144,1152]{2,1,0:T(8,128)(2,1)}, u32[]{:S(2)}, u32[]{:S(2)}) %collective-permute-start.20) | collective-permute-done | bytes 663584 | tf_op jit(solution)/shard_map/ppermute | solution.py:772
  410.3 8.8 %shard_map.215 = bf16[4,576,1152]{2,1,0:T(8,128)(2,1)} custom-call(s32[4]{0:T(128)S(1)} %copy-done.24, s32[1]{0:T(128)} %bitcast.41.side, s32[16]{0:T(128)S(1)} %stack.112.table, bf16[512,1152]{1,0:T(8,128)(2,1)S(1)} %copy-done.4, bf16[512,1152]{1,0:T(8,128)(2,1)S(1)} %copy-done.6, bf16[4,512,1152]{2,1,0:T(8,128)(2,1)} %get-tuple-element.187.refs_2_.d_qkv), custom_call_target="tpu_custom_call" | custom-call | flops 1024 | bytes 1024 | tf_op jit(solution)/shard_map/pallas_call | solution.py:728
  431.6 29.7 %collective-permute-done.25 = bf16[2,144,1152]{2,1,0:T(8,128)(2,1)S(1)} collective-permute-done((bf16[2,144,1152]{2,1,0:T(8,128)(2,1)S(1)}, bf16[2,144,1152]{2,1,0:T(8,128)(2,1)S(1)}, u32[]{:S(2)}, u32[]{:S(2)}) %collective-permute-start.25) | collective-permute-done | bytes 663584 | tf_op jit(solution)/shard_map/ppermute | solution.py:767
  462.3 10.1 %shard_map.216 = (bf16[2,288,1152]{2,1,0:T(8,128)(2,1)S(1)}, bf16[2,288,1152]{2,1,0:T(8,128)(2,1)}, bf16[2,288,1152]{2,1,0:T(8,128)(2,1)}, bf16[2,288,1152]{2,1,0:T(8,128)(2,1)}) custom-call(s32[4]{0:T(128)S(1)} %copy-done.24, s32[1]{0:T(128)} %bitcast.55.side, s32[16]{0:T(128)S(1)} %stack.112.table, bf16[512,1152]{1,0:T(8,128)(2,1)S(1)} %copy-done.4, ...), custom_call_target="tpu_custom_call" | custom-call | flops 1024 | bytes 1024 | tf_op jit(solution)/shard_map/pallas_call | solution.py:728
  475.9 11.2 %shard_map.217 = (bf16[512,1152]{1,0:T(8,128)(2,1)}, f32[2,2,1152]{2,1,0:T(2,128)S(1)}) custom-call(bf16[4,512,1152]{2,1,0:T(8,128)(2,1)} %get-tuple-element.187.refs_2_.d_qkv, bf16[4,1152,1152]{2,1,0:T(8,128)(2,1)} %bitcast.260, f32[2,6,1152]{2,1,0:T(8,128)S(1)} %copy-done.20, bf16[512,1152]{1,0:T(8,128)(2,1)S(1)} %bitcast.257, f32[512,1152]{1,0:T(8,128)S(1)} %copy-done.7), custom_call_target="tpu_custom_call" | custom-call | flops 1024 | bytes 1024 | tf_op jit(solution)/shard_map/pallas_call | solution.py:623
  493.7 13.0 %all_to_all.44 = f32[4,1,7488]{2,1,0:T(1,128)S(1)} all-to-all(f32[4,1,7488]{2,1,0:T(1,128)S(1)} %copy.101), channel_id=1, replica_groups=mesh['dp'=8,'fsdp'=4] {'fsdp'}, dimensions={0} | all-to-all | bytes 239616 | tf_op jit(solution)/shard_map/all_to_all | solution.py:1207
  506.8 9.7 %collective-permute-done.31 = bf16[2,144,1152]{2,1,0:T(8,128)(2,1)} collective-permute-done((bf16[2,144,1152]{2,1,0:T(8,128)(2,1)S(1)}, bf16[2,144,1152]{2,1,0:T(8,128)(2,1)}, u32[]{:S(2)}, u32[]{:S(2)}) %collective-permute-start.31) | collective-permute-done | bytes 663584 | tf_op jit(solution)/shard_map/ppermute | solution.py:767
  525.9 16.9 %collective-permute-done.34 = bf16[1,144,1152]{2,1,0:T(8,128)(2,1)} collective-permute-done((bf16[1,144,1152]{2,1,0:T(8,128)(2,1)}, bf16[1,144,1152]{2,1,0:T(8,128)(2,1)}, u32[]{:S(2)}, u32[]{:S(2)}) %collective-permute-start.34) | collective-permute-done | bytes 331808 | tf_op jit(solution)/shard_map/ppermute | solution.py:767
  548.3 8.4 %shard_map.218 = bf16[4,3,144,288]{3,2,1,0:T(8,128)(2,1)} custom-call(s32[1]{0:T(128)} %bitcast.86.at, bf16[1152,1152]{1,0:T(8,128)(2,1)} %bitcast.289, bf16[144,1152]{1,0:T(8,128)(2,1)S(1)} %copy-done.12, bf16[1152,1152]{1,0:T(8,128)(2,1)} %bitcast.286), custom_call_target="tpu_custom_call" | custom-call | flops 1024 | bytes 1024 | tf_op jit(solution)/shard_map/pallas_call | solution.py:1001
  556.7 28.1 %collective-permute-done.35 = bf16[2,144,1152]{2,1,0:T(8,128)(2,1)S(1)} collective-permute-done((bf16[2,144,1152]{2,1,0:T(8,128)(2,1)S(1)}, bf16[2,144,1152]{2,1,0:T(8,128)(2,1)S(1)}, u32[]{:S(2)}, u32[]{:S(2)}) %collective-permute-start.35) | collective-permute-done | bytes 663584 | tf_op jit(solution)/shard_map/ppermute | solution.py:767
  591.4 12.8 %collective-permute-done.36 = bf16[1,144,1152]{2,1,0:T(8,128)(2,1)S(1)} collective-permute-done((bf16[1,144,1152]{2,1,0:T(8,128)(2,1)S(1)}, bf16[1,144,1152]{2,1,0:T(8,128)(2,1)S(1)}, u32[]{:S(2)}, u32[]{:S(2)}) %collective-permute-start.36) | collective-permute-done | bytes 331808 | tf_op jit(solution)/shard_map/ppermute | solution.py:767
  619.6 10.0 %all_gather.44 = f32[864,128]{1,0:T(8,128)S(1)} all-gather(f32[216,128]{1,0:T(8,128)S(1)} %reshape.311), channel_id=1, replica_groups=mesh['dp'=8,'fsdp'=4] {'fsdp'}, dimensions={0}, use_global_device_ids=true | all-gather | bytes 552960 | tf_op jit(solution)/shard_map/all_gather | solution.py:1231
  633.2 16.8 %all_gather.46 = f32[1728,128]{1,0:T(8,128)S(1)} all-gather(f32[216,128]{1,0:T(8,128)S(1)} %reshape.313), channel_id=1, replica_groups=mesh['dp'=8,'fsdp'=4] {'dp'}, dimensions={0}, use_global_device_ids=true | all-gather | bytes 995328 | tf_op jit(solution)/shard_map/all_gather | solution.py:1251
  652.2 8.3 %shard_map.220 = bf16[4,3,144,288]{3,2,1,0:T(8,128)(2,1)} custom-call(s32[1]{0:T(128)} %bitcast.86.at, bf16[1152,1152]{1,0:T(8,128)(2,1)} %bitcast.288, bf16[144,1152]{1,0:T(8,128)(2,1)S(1)} %copy-done.11, bf16[1152,1152]{1,0:T(8,128)(2,1)} %bitcast.285), custom_call_target="tpu_custom_call" | custom-call | flops 1024 | bytes 1024 | tf_op jit(solution)/shard_map/pallas_call | solution.py:1001
  668.6 8.3 %shard_map.219 = bf16[4,3,144,288]{3,2,1,0:T(8,128)(2,1)} custom-call(s32[1]{0:T(128)} %bitcast.86.at, bf16[1152,1152]{1,0:T(8,128)(2,1)} %bitcast.290, bf16[144,1152]{1,0:T(8,128)(2,1)S(1)} %copy-done.10, bf16[1152,1152]{1,0:T(8,128)(2,1)} %bitcast.287), custom_call_target="tpu_custom_call" | custom-call | flops 1024 | bytes 1024 | tf_op jit(solution)/shard_map/pallas_call | solution.py:1001
  691.6 12.5 %all-to-all-done.4 = bf16[4,3,144,288]{3,2,1,0:T(8,128)(2,1)} async-done(((bf16[4,3,144,288]{3,2,1,0:T(8,128)(2,1)}), bf16[4,3,144,288]{3,2,1,0:T(8,128)(2,1)}, u32[]{:S(2)}, u32[]{:S(2)}) %all-to-all-start.4) | async-done | bytes 995360 | tf_op jit(solution)/shard_map/all_to_all | solution.py:842
  (390 shorter events, 193.8 us)
Async XLA Ops:
  7.2 132.5 %all-gather.20.cloned.1.call-start = ((), (), s32[]{:S(2)}) async-start(), calls=%async_computation.9 | async-start | bytes 10948608 | tf_op jit(solution)/shard_map/all_gather | solution.py:851
  32.6 227.7 %all-gather.22.cloned.1.call-start = ((), (), s32[]{:S(2)}) async-start(), calls=%async_computation.10 | async-start | bytes 10948608 | tf_op jit(solution)/shard_map/all_gather | solution.py:851
  40.6 323.8 %all-gather.14.cloned.1.call-start = ((), (), s32[]{:S(2)}) async-start(), calls=%async_computation.6 | async-start | bytes 2985984 | tf_op jit(solution)/shard_map/all_gather | solution.py:900
  52.1 25.9 %collective-permute-start.4 = (bf16[144,1152]{1,0:T(8,128)(2,1)S(1)}, bf16[144,1152]{1,0:T(8,128)(2,1)S(1)}, u32[]{:S(2)}, u32[]{:S(2)}) collective-permute-start(bf16[144,1152]{1,0:T(8,128)(2,1)S(1)} %get-tuple-element.124.refs_0_), channel_id=1, source_target_pairs={{0,16},{4,20},{8,24},{12,28},{16,0},{20,4},{24,8},{28,12},{1,17},{... | collective-permute-start | bytes 995336 | tf_op jit(solution)/shard_map/ppermute | solution.py:762
  142.2 48.4 %collective-permute-start.7 = (bf16[576,1152]{1,0:T(8,128)(2,1)}, bf16[576,1152]{1,0:T(8,128)(2,1)S(1)}, u32[]{:S(2)}, u32[]{:S(2)}) collective-permute-start(bf16[576,1152]{1,0:T(8,128)(2,1)} %constant_dynamic-slice_fusion.3), channel_id=1, source_target_pairs={{0,1},{1,0},{2,3},{3,2},{4,5},{5,4},{6,7},{7,6},{8,9},{9,8},{10,11... | collective-permute-start | bytes 3981320 | tf_op jit(solution)/shard_map/ppermute | solution.py:772
  143.6 47.0 %collective-permute-start.8 = (bf16[576,1152]{1,0:T(8,128)(2,1)}, bf16[576,1152]{1,0:T(8,128)(2,1)}, u32[]{:S(2)}, u32[]{:S(2)}) collective-permute-start(bf16[576,1152]{1,0:T(8,128)(2,1)} %constant_dynamic-slice_fusion.3), channel_id=1, source_target_pairs={{0,2},{1,3},{2,0},{3,1},{4,6},{5,7},{6,4},{7,5},{8,10},{9,11},{10,... | collective-permute-start | bytes 3981320 | tf_op jit(solution)/shard_map/ppermute | solution.py:772
  144.2 78.2 %collective-permute-start.9 = (bf16[576,1152]{1,0:T(8,128)(2,1)}, bf16[576,1152]{1,0:T(8,128)(2,1)}, u32[]{:S(2)}, u32[]{:S(2)}) collective-permute-start(bf16[576,1152]{1,0:T(8,128)(2,1)} %constant_dynamic-slice_fusion.3), channel_id=1, source_target_pairs={{0,3},{1,2},{2,1},{3,0},{4,7},{5,6},{6,5},{7,4},{8,11},{9,10},{10,... | collective-permute-start | bytes 3981320 | tf_op jit(solution)/shard_map/ppermute | solution.py:772
  252.5 43.0 %collective-permute-start.16 = (bf16[4,576,1152]{2,1,0:T(8,128)(2,1)}, bf16[4,576,1152]{2,1,0:T(8,128)(2,1)}, u32[]{:S(2)}, u32[]{:S(2)}) collective-permute-start(bf16[4,576,1152]{2,1,0:T(8,128)(2,1)} %shard_map.208), channel_id=1, source_target_pairs={{0,4},{4,0},{8,12},{12,8},{16,20},{20,16},{24,28},{28,24},{1,5},{5... | collective-permute-start | bytes 15925256 | tf_op jit(solution)/shard_map/ppermute | solution.py:757
  254.1 29.9 %collective-permute-start.13 = (bf16[6,144,288]{2,1,0:T(8,128)(2,1)}, bf16[6,144,288]{2,1,0:T(8,128)(2,1)}, u32[]{:S(2)}, u32[]{:S(2)}) collective-permute-start(bf16[6,144,288]{2,1,0:T(8,128)(2,1)} %get-tuple-element.238), channel_id=1, source_target_pairs={{0,1},{1,0},{2,3},{3,2},{4,5},{5,4},{6,7},{7,6},{8,9},{9,8},{10,11... | collective-permute-start | bytes 1493000 | tf_op jit(solution)/shard_map/ppermute | solution.py:772
  254.6 32.4 %collective-permute-start.14 = (bf16[6,144,288]{2,1,0:T(8,128)(2,1)}, bf16[6,144,288]{2,1,0:T(8,128)(2,1)}, u32[]{:S(2)}, u32[]{:S(2)}) collective-permute-start(bf16[6,144,288]{2,1,0:T(8,128)(2,1)} %get-tuple-element.237), channel_id=1, source_target_pairs={{0,2},{1,3},{2,0},{3,1},{4,6},{5,7},{6,4},{7,5},{8,10},{9,11},{10,... | collective-permute-start | bytes 1493000 | tf_op jit(solution)/shard_map/ppermute | solution.py:772
  257.1 29.8 %collective-permute-start.15 = (bf16[6,144,288]{2,1,0:T(8,128)(2,1)}, bf16[6,144,288]{2,1,0:T(8,128)(2,1)}, u32[]{:S(2)}, u32[]{:S(2)}) collective-permute-start(bf16[6,144,288]{2,1,0:T(8,128)(2,1)} %get-tuple-element.236), channel_id=1, source_target_pairs={{0,3},{1,2},{2,1},{3,0},{4,7},{5,6},{6,5},{7,4},{8,11},{9,10},{10,... | collective-permute-start | bytes 1493000 | tf_op jit(solution)/shard_map/ppermute | solution.py:772
  298.3 98.2 %all-gather.16.cloned.1.call-start = ((), (), s32[]{:S(2)}) async-start(), calls=%async_computation.7 | async-start | bytes 2985984 | tf_op jit(solution)/shard_map/all_gather | solution.py:900
  316.3 33.5 %collective-permute-start.17 = (bf16[4,576,1152]{2,1,0:T(8,128)(2,1)}, bf16[4,576,1152]{2,1,0:T(8,128)(2,1)}, u32[]{:S(2)}, u32[]{:S(2)}) collective-permute-start(bf16[4,576,1152]{2,1,0:T(8,128)(2,1)} %shard_map.211), channel_id=1, source_target_pairs={{0,4},{4,0},{8,12},{12,8},{16,20},{20,16},{24,28},{28,24},{1,5},{5... | collective-permute-start | bytes 15925256 | tf_op jit(solution)/shard_map/ppermute | solution.py:757
  316.3 170.8 %all-gather.18.cloned.1.call-start = ((), (), s32[]{:S(2)}) async-start(), calls=%async_computation.8 | async-start | bytes 2985984 | tf_op jit(solution)/shard_map/all_gather | solution.py:900
  316.8 31.9 %collective-permute-start.18 = (bf16[2,288,1152]{2,1,0:T(8,128)(2,1)}, bf16[2,288,1152]{2,1,0:T(8,128)(2,1)}, u32[]{:S(2)}, u32[]{:S(2)}) collective-permute-start(bf16[2,288,1152]{2,1,0:T(8,128)(2,1)} %copy-done.36), channel_id=1, source_target_pairs={{0,1},{1,0},{2,3},{3,2},{4,5},{5,4},{6,7},{7,6},{8,9},{9,8},{10,11... | collective-permute-start | bytes 3981320 | tf_op jit(solution)/shard_map/ppermute | solution.py:772
  318.2 31.5 %collective-permute-start.19 = (bf16[2,288,1152]{2,1,0:T(8,128)(2,1)}, bf16[2,288,1152]{2,1,0:T(8,128)(2,1)}, u32[]{:S(2)}, u32[]{:S(2)}) collective-permute-start(bf16[2,288,1152]{2,1,0:T(8,128)(2,1)} %get-tuple-element.161), channel_id=1, source_target_pairs={{0,2},{1,3},{2,0},{3,1},{4,6},{5,7},{6,4},{7,5},{8,10},{9,11},{10,... | collective-permute-start | bytes 3981320 | tf_op jit(solution)/shard_map/ppermute | solution.py:772
  352.6 44.0 %collective-permute-start.21 = (bf16[2,144,1152]{2,1,0:T(8,128)(2,1)S(1)}, bf16[2,144,1152]{2,1,0:T(8,128)(2,1)}, u32[]{:S(2)}, u32[]{:S(2)}) collective-permute-start(bf16[2,144,1152]{2,1,0:T(8,128)(2,1)S(1)} %dynamic-slice_bitcast_fusion.7), channel_id=1, source_target_pairs={{0,1},{1,0},{2,3},{3,2},{4,5},{5,4},{6,7},{7,6},{8,9},{9,8},{10,11... | collective-permute-start | bytes 1990664 | tf_op jit(solution)/shard_map/ppermute | solution.py:772
  364.4 45.9 %collective-permute-start.22 = (bf16[2,288,1152]{2,1,0:T(8,128)(2,1)}, bf16[2,288,1152]{2,1,0:T(8,128)(2,1)}, u32[]{:S(2)}, u32[]{:S(2)}) collective-permute-start(bf16[2,288,1152]{2,1,0:T(8,128)(2,1)} %copy-done.37), channel_id=1, source_target_pairs={{0,1},{1,0},{2,3},{3,2},{4,5},{5,4},{6,7},{7,6},{8,9},{9,8},{10,11... | collective-permute-start | bytes 3981320 | tf_op jit(solution)/shard_map/ppermute | solution.py:772
  365.7 44.6 %collective-permute-start.23 = (bf16[2,288,1152]{2,1,0:T(8,128)(2,1)}, bf16[2,288,1152]{2,1,0:T(8,128)(2,1)}, u32[]{:S(2)}, u32[]{:S(2)}) collective-permute-start(bf16[2,288,1152]{2,1,0:T(8,128)(2,1)} %get-tuple-element.175), channel_id=1, source_target_pairs={{0,2},{1,3},{2,0},{3,1},{4,6},{5,7},{6,4},{7,5},{8,10},{9,11},{10,... | collective-permute-start | bytes 3981320 | tf_op jit(solution)/shard_map/ppermute | solution.py:772
  369.0 41.2 %collective-permute-start.20 = (bf16[2,144,1152]{2,1,0:T(8,128)(2,1)}, bf16[2,144,1152]{2,1,0:T(8,128)(2,1)}, u32[]{:S(2)}, u32[]{:S(2)}) collective-permute-start(bf16[2,144,1152]{2,1,0:T(8,128)(2,1)} %dynamic-slice_bitcast_fusion.8), channel_id=1, source_target_pairs={{0,2},{1,3},{2,0},{3,1},{4,6},{5,7},{6,4},{7,5},{8,10},{9,11},{10,... | collective-permute-start | bytes 1990664 | tf_op jit(solution)/shard_map/ppermute | solution.py:772
  419.1 42.2 %collective-permute-start.24 = (bf16[4,576,1152]{2,1,0:T(8,128)(2,1)}, bf16[4,576,1152]{2,1,0:T(8,128)(2,1)}, u32[]{:S(2)}, u32[]{:S(2)}) collective-permute-start(bf16[4,576,1152]{2,1,0:T(8,128)(2,1)} %shard_map.215), channel_id=1, source_target_pairs={{0,4},{4,0},{8,12},{12,8},{16,20},{20,16},{24,28},{28,24},{1,5},{5... | collective-permute-start | bytes 15925256 | tf_op jit(solution)/shard_map/ppermute | solution.py:757
  419.2 128.3 %all-gather.24.cloned.1.call-start = ((), (), s32[]{:S(2)}) async-start(), calls=%async_computation.11 | async-start | bytes 2985984 | tf_op jit(solution)/shard_map/all_gather | solution.py:954
  422.6 38.7 %collective-permute-start.25 = (bf16[2,144,1152]{2,1,0:T(8,128)(2,1)S(1)}, bf16[2,144,1152]{2,1,0:T(8,128)(2,1)S(1)}, u32[]{:S(2)}, u32[]{:S(2)}) collective-permute-start(bf16[2,144,1152]{2,1,0:T(8,128)(2,1)S(1)} %dynamic-slice_bitcast_fusion.6), channel_id=1, source_target_pairs={{0,8},{4,12},{8,0},{12,4},{16,24},{20,28},{24,16},{28,20},{1,9},{5... | collective-permute-start | bytes 1990664 | tf_op jit(solution)/shard_map/ppermute | solution.py:767
  426.5 60.7 %collective-permute-start.27 = (bf16[2,144,1152]{2,1,0:T(8,128)(2,1)}, bf16[2,144,1152]{2,1,0:T(8,128)(2,1)}, u32[]{:S(2)}, u32[]{:S(2)}) collective-permute-start(bf16[2,144,1152]{2,1,0:T(8,128)(2,1)} %dynamic-slice_bitcast_fusion.4), channel_id=1, source_target_pairs={{0,1},{1,0},{2,3},{3,2},{4,5},{5,4},{6,7},{7,6},{8,9},{9,8},{10,11... | collective-permute-start | bytes 1990664 | tf_op jit(solution)/shard_map/ppermute | solution.py:772
  430.2 56.9 %collective-permute-start.26 = (bf16[2,144,1152]{2,1,0:T(8,128)(2,1)}, bf16[2,144,1152]{2,1,0:T(8,128)(2,1)}, u32[]{:S(2)}, u32[]{:S(2)}) collective-permute-start(bf16[2,144,1152]{2,1,0:T(8,128)(2,1)} %dynamic-slice_bitcast_fusion.5), channel_id=1, source_target_pairs={{0,2},{1,3},{2,0},{3,1},{4,6},{5,7},{6,4},{7,5},{8,10},{9,11},{10,... | collective-permute-start | bytes 1990664 | tf_op jit(solution)/shard_map/ppermute | solution.py:772
  462.3 24.9 %collective-permute-start.28 = (bf16[1,144,1152]{2,1,0:T(8,128)(2,1)}, bf16[1,144,1152]{2,1,0:T(8,128)(2,1)}, u32[]{:S(2)}, u32[]{:S(2)}) collective-permute-start(bf16[1,144,1152]{2,1,0:T(8,128)(2,1)} %constant_dynamic-slice_fusion.2), channel_id=1, source_target_pairs={{0,16},{4,20},{8,24},{12,28},{16,0},{20,4},{24,8},{28,12},{1,17},{... | collective-permute-start | bytes 995336 | tf_op jit(solution)/shard_map/ppermute | solution.py:767
  473.4 43.0 %collective-permute-start.29 = (bf16[2,288,1152]{2,1,0:T(8,128)(2,1)}, bf16[2,288,1152]{2,1,0:T(8,128)(2,1)}, u32[]{:S(2)}, u32[]{:S(2)}) collective-permute-start(bf16[2,288,1152]{2,1,0:T(8,128)(2,1)} %get-tuple-element.202), channel_id=1, source_target_pairs={{0,1},{1,0},{2,3},{3,2},{4,5},{5,4},{6,7},{7,6},{8,9},{9,8},{10,11... | collective-permute-start | bytes 3981320 | tf_op jit(solution)/shard_map/ppermute | solution.py:772
  474.2 42.2 %collective-permute-start.30 = (bf16[2,288,1152]{2,1,0:T(8,128)(2,1)}, bf16[2,288,1152]{2,1,0:T(8,128)(2,1)}, u32[]{:S(2)}, u32[]{:S(2)}) collective-permute-start(bf16[2,288,1152]{2,1,0:T(8,128)(2,1)} %get-tuple-element.203), channel_id=1, source_target_pairs={{0,2},{1,3},{2,0},{3,1},{4,6},{5,7},{6,4},{7,5},{8,10},{9,11},{10,... | collective-permute-start | bytes 3981320 | tf_op jit(solution)/shard_map/ppermute | solution.py:772
  490.3 26.1 %collective-permute-start.31 = (bf16[2,144,1152]{2,1,0:T(8,128)(2,1)S(1)}, bf16[2,144,1152]{2,1,0:T(8,128)(2,1)}, u32[]{:S(2)}, u32[]{:S(2)}) collective-permute-start(bf16[2,144,1152]{2,1,0:T(8,128)(2,1)S(1)} %dynamic-slice_bitcast_fusion.3), channel_id=1, source_target_pairs={{0,8},{4,12},{8,0},{12,4},{16,24},{20,28},{24,16},{28,20},{1,9},{5... | collective-permute-start | bytes 1990664 | tf_op jit(solution)/shard_map/ppermute | solution.py:767
  493.5 158.7 %all-gather.28.cloned.1.call-start = ((), (), s32[]{:S(2)}) async-start(), calls=%async_computation.13 | async-start | bytes 2985984 | tf_op jit(solution)/shard_map/all_gather | solution.py:954
  547.4 37.5 %collective-permute-start.35 = (bf16[2,144,1152]{2,1,0:T(8,128)(2,1)S(1)}, bf16[2,144,1152]{2,1,0:T(8,128)(2,1)S(1)}, u32[]{:S(2)}, u32[]{:S(2)}) collective-permute-start(bf16[2,144,1152]{2,1,0:T(8,128)(2,1)S(1)} %dynamic-slice_bitcast_fusion), channel_id=1, source_target_pairs={{0,8},{4,12},{8,0},{12,4},{16,24},{20,28},{24,16},{28,20},{1,9},{5... | collective-permute-start | bytes 1990664 | tf_op jit(solution)/shard_map/ppermute | solution.py:767
  589.3 79.3 %all-gather.26.cloned.1.call-start = ((), (), s32[]{:S(2)}) async-start(), calls=%async_computation.12 | async-start | bytes 2985984 | tf_op jit(solution)/shard_map/all_gather | solution.py:954
  (90 other events, 955.8 us)
Sparse Core Ops, SparseCore 0:
  32.7 106.8 all-gather.19
  143.3 105.3 all-gather.21
  298.4 32.0 all-gather.13
  332.0 33.1 all-gather.15
  419.4 42.0 all-gather.17
  493.6 47.9 all-gather.23
  544.8 40.5 all-gather.27
  606.2 35.0 all-gather.25

commit v15 on v14

--- a/solution.py
+++ b/solution.py
@@ -1144,14 +1144,16 @@
     d_resid, d_proj, resid_sums = run_resid(
         frames, frame_counts, d_pre, one_w, mods, resid, grad_out, proj
     )
-    d_proj, one_parts, two_parts = tie(d_proj, one_parts, two_parts)
+    d_proj, one_parts = tie(d_proj, one_parts)
+    one_parts = one_steps.send(one_parts)
+    d_proj, one_parts, two_parts, right_wholes[2] = tie(
+        d_proj, one_parts, two_parts, right_wholes[2]
+    )
     two_parts = two_steps.send(two_parts)
     one_parts = one_steps.send(one_parts)
-    d_proj, one_parts, right_wholes[2] = tie(d_proj, one_parts, right_wholes[2])
-    one_parts = one_steps.send(one_parts)
     d_heads, head_sums = run_attention_back(frames, frame_counts, d_proj, parts, attn_w)
-    d_heads, two_parts, one_parts, right_wholes[1] = tie(
-        d_heads, two_parts, one_parts, right_wholes[1]
+    d_heads, two_parts, one_parts, right_wholes[1], right_wholes[0] = tie(
+        d_heads, two_parts, one_parts, right_wholes[1], right_wholes[0]
     )
     two_parts = two_steps.send(two_parts)
     one_parts = one_steps.send(one_parts)
@@ -1159,15 +1161,14 @@
     attn_parts = next(attn_steps)
     d_heads, attn_parts = tie(d_heads, attn_parts)
     attn_parts = attn_steps.send(attn_parts)
-    d_heads, attn_parts, two_parts = tie(d_heads, attn_parts, two_parts)
+    d_heads, attn_parts, two_parts, one_parts = tie(d_heads, attn_parts, two_parts, one_parts)
     two_parts = two_steps.send(two_parts)
+    one_parts = one_steps.send(one_parts)
     attn_parts = attn_steps.send(attn_parts)
     d_heads, attn_parts = tie(d_heads, attn_parts)
     attn_parts = attn_steps.send(attn_parts)
     input_grad, input_sums = run_input(d_heads, attn_w, mods, stream, d_resid)
-    input_sums, one_parts, two_parts, right_wholes[0] = tie(
-        input_sums, one_parts, two_parts, right_wholes[0]
-    )
+    input_sums, one_parts, two_parts = tie(input_sums, one_parts, two_parts)
     whole_two = two_steps.send(two_parts)
     one_parts = one_steps.send(one_parts)
 
@@ -1207,7 +1208,7 @@
     rank_sums = lax.all_to_all(to_ranks, "fsdp", 0, 0, tiled=True)
     rank_sums, attn_parts, one_parts = tie(rank_sums, attn_parts, one_parts)
     attn_parts = attn_steps.send(attn_parts)
-    one_parts = one_steps.send(one_parts)
+    whole_one = one_steps.send(one_parts)
     rank_sums = jnp.sum(rank_sums, axis=0)
     to_rows = jnp.concatenate(
         [
@@ -1216,15 +1217,16 @@
         ],
         axis=1,
     )
-    to_rows, attn_parts, one_parts = tie(to_rows, attn_parts, one_parts)
+    to_rows, attn_parts = tie(to_rows, attn_parts)
     attn_parts = attn_steps.send(attn_parts)
-    whole_one = one_steps.send(one_parts)
     products_two = owned_step(whole_two, left_rows[2], right_wholes[2], group)
     products_two, attn_parts = tie(products_two, attn_parts)
     attn_parts = attn_steps.send(attn_parts)
     back_two = shard_rows(products_two, group)
-    to_rows, back_two, attn_parts = tie(to_rows, back_two, attn_parts)
+    products_one = owned_step(whole_one, left_rows[1], right_wholes[1], group)
+    to_rows, back_two, products_one, attn_parts = tie(to_rows, back_two, products_one, attn_parts)
     whole_attn = attn_steps.send(attn_parts)
+    back_one = shard_rows(products_one, group)
     from_rows = lax.all_to_all(to_rows, "dp", 0, 0, tiled=True)
     bias_grad = jnp.sum(from_rows[:, mod_size:], axis=0)
     mod_grad_cols = from_rows[:, :mod_size].reshape(all_clips, mod_count, col_part)
@@ -1246,13 +1248,11 @@
     cond_side = jnp.einsum("cb,bje->jce", cond_gram, mod_grad_cols, precision=precise)
     ada_right = jnp.einsum("cjr,jce->jre", mod_grad_rows, cond_side, precision=precise)
 
-    products_one = owned_step(whole_one, left_rows[1], right_wholes[1], group)
-    back_one = shard_rows(products_one, group)
     right_parts = lax.all_gather(packed([right_parts], 8), "dp", axis=0, tiled=True)
     mod_right = jnp.sum(right_parts.reshape(dp_count, -1), axis=0)[: mod_grad_cols.size]
     mod_right = mod_right.reshape(all_clips, mod_count, col_part)
     ada_pre = jnp.einsum("jrc,cje->jre", left_cond, mod_right, precision=precise)
-    whole_attn, right_parts = tie(whole_attn, right_parts)
+    whole_attn, back_one = tie(whole_attn, back_one)
     back_attn = shard_rows(owned_step(whole_attn, left_rows[0], right_wholes[0], group), group)
 
     def joined(at, ada):

time: 734 us -> 710 us (0.967)
  waiting for transfers between devices: 268 us -> 211 us
  blocking collectives: 64 us -> 88.2 us
  starting transfers between devices: 50 us -> 58.2 us
    ppermute x6, waiting for transfers between devices: 97.3 us -> 31.1 us  [chip_swap(): lax.ppermute(array, 'dp', [(at, at ^ 2 * bits) for at in range(count)])]
    all_gather x3, waiting for transfers between devices: 0.01 us -> 14.2 us  [gather_own(): return lax.all_gather(rows, 'dp', axis=1, tiled=True)]
    all_to_all x1, blocking collectives: 13 us -> 26.7 us  [per_device(): rank_sums = lax.all_to_all(to_ranks, 'fsdp', 0, 0, tiled=True)]
    all_gather x1, blocking collectives: 9.96 us -> 21.3 us  [per_device(): lax.all_gather(packed([mod_grad_cols], 8), 'fsdp', axis=0, tiled=True)]
    unnamed x145 -> x151, local copies, waits for them, and re-layouts: 17.6 us -> 15.9 us
  transfers between devices with their start and end apart: 50 -> 50, of which waited for: 20 -> 22; matrix products, arithmetic and copies ran while one was open for 10% -> 10% of each run, Pallas kernels for 28% -> 28%
where the time goes in v15:
time: 710 us; the launch traced here: 704 us
  Pallas kernels  214 us (30%)
  waiting for transfers between devices  211 us (30%)
  blocking collectives  88.2 us (12%)
  starting transfers between devices  58.2 us (8%)
  other arithmetic  55.7 us (8%)
  local copies, waits for them, and re-layouts  48.9 us (7%)
  between operations  16 us (2%)
  matrix products  11.7 us (2%)
    ppermute x21, waiting for transfers between devices, rank_swap(): return lax.ppermute(array, 'fsdp', [(at, at ^ bits) for at in range(count)])  64.9 us
    pallas_call x6, Pallas kernels, run_halves(): pl.pallas_call(body, grid_spec=pltpu.PrefetchScalarGridSpec(num_scalar_pr...  54.9 us
    all_gather x2, waiting for transfers between devices, gather_blocks(): all_rows = lax.all_gather(rows, ('fsdp', 'dp'), axis=0, tiled=True)  53.8 us
    pallas_call x1, Pallas kernels, run_attention(): pl.pallas_call(functools.partial(attention_kernel, frames), grid=(clips,)...  41.1 us
    ppermute x6, waiting for transfers between devices, chip_swap(): lax.ppermute(array, 'dp', [(at, at ^ 2 * bits) for at in range(count)])  31.1 us
    convert_element_type x21, other arithmetic, narrow(): return array.astype(jnp.bfloat16)  29.8 us
    all_to_all x1, blocking collectives, per_device(): rank_sums = lax.all_to_all(to_ranks, 'fsdp', 0, 0, tiled=True)  26.7 us
    pallas_call x1, Pallas kernels, run_attention_back(): pl.pallas_call(functools.partial(attention_back_kernel, frames), grid=(cl...  26.2 us
  transfers between devices with their start and end apart: 50, of which 22 were waited for; matrix products, arithmetic and copies ran while one was open for 10% of the time, Pallas kernels for 28%

profile of v15, /device:TPU:0, one launch (start us, length us, event | category | flops | bytes accessed | tf_op | source)
XLA Modules:
  0.0 703.6 jit_solution(5551150787609155170)
XLA Ops:
  17.2 14.7 %all_gather.36 = bf16[256,128]{1,0:T(8,128)(2,1)S(1)} all-gather(bf16[32,128]{1,0:T(8,128)(2,1)S(1)} %fusion.49), channel_id=1, replica_groups=mesh['dp'=8,'fsdp'=4] {'dp'}, dimensions={0}, use_global_device_ids=true | all-gather | bytes 73728 | tf_op jit(solution)/shard_map/all_gather | solution.py:1062
  44.6 8.8 %all-to-all-done = f32[16,6,288]{2,1,0:T(8,128)S(1)} async-done(((f32[16,6,288]{2,1,0:T(8,128)}), f32[16,6,288]{2,1,0:T(8,128)S(1)}, u32[]{:S(2)}, u32[]{:S(2)}) %all-to-all-start) | async-done | bytes 110624 | tf_op jit(solution)/shard_map/all_to_all | solution.py:1080
  57.5 9.5 %all_gather.37 = f32[672,128]{1,0:T(8,128)S(1)} all-gather(f32[168,128]{1,0:T(8,128)S(1)} %pad_bitcast_fusion), channel_id=1, replica_groups=mesh['dp'=8,'fsdp'=4] {'fsdp'}, dimensions={0}, use_global_device_ids=true | all-gather | bytes 430080 | tf_op jit(solution)/shard_map/all_gather | solution.py:1087
  67.0 12.2 %collective-permute-done.4.refs_2_ = bf16[144,1152]{1,0:T(8,128)(2,1)S(1)} collective-permute-done((bf16[144,1152]{1,0:T(8,128)(2,1)S(1)}, bf16[144,1152]{1,0:T(8,128)(2,1)S(1)}, u32[]{:S(2)}, u32[]{:S(2)}) %collective-permute-start.4) | collective-permute-done | bytes 331808 | tf_op jit(solution)/shard_map/ppermute | solution.py:762
  87.2 53.8 %all-gather.20.cloned.1.call-done = bf16[1,4608,1152]{2,1,0:T(8,128)(2,1)} async-done(((bf16[1,144,1152]{2,1,0:T(8,128)(2,1)}), bf16[1,4608,1152]{2,1,0:T(8,128)(2,1)}) %all-gather.20.cloned.1.call-update) | async-done | bytes 10616848 | tf_op jit(solution)/shard_map/all_gather | solution.py:851
  148.1 41.1 %shard_map.206 = (bf16[512,1152]{1,0:T(8,128)(2,1)S(1)}, bf16[5,512,1152]{2,1,0:T(8,128)(2,1)}, bf16[512,1152]{1,0:T(8,128)(2,1)S(1)}, f32[512,1152]{1,0:T(8,128...) custom-call(s32[2]{0:T(128)S(1)} %copy-done.32, ...), custom_call_target="tpu_custom_call" | custom-call | flops 1024 | bytes 1024 | tf_op jit(solution)/shard_map/pallas_call | solution.py:216
  191.9 31.8 %collective-permute-done.9.refs_5_ = bf16[576,1152]{1,0:T(8,128)(2,1)} collective-permute-done((bf16[576,1152]{1,0:T(8,128)(2,1)}, bf16[576,1152]{1,0:T(8,128)(2,1)}, u32[]{:S(2)}, u32[]{:S(2)}) %collective-permute-start.9) | collective-permute-done | bytes 1327136 | tf_op jit(solution)/shard_map/ppermute | solution.py:772
  231.1 13.9 %shard_map.207 = (bf16[4608,1152]{1,0:T(8,128)(2,1)}, bf16[4,512,1152]{2,1,0:T(8,128)(2,1)}, bf16[4,512,1152]{2,1,0:T(8,128)(2,1)}) custom-call(s32[4]{0:T(128)S(1)} %get-tuple-element.276.order, s32[7]{0:T(128)S(1)} %stack.91.starts, bf16[512,1152]{1,0:T(8,128)(2,1)S(1)} %get-tuple-element.134.mlp_in.refs_0_, f32[4,1,1152]{2,1,0:T(1,128)S(1)} %copy.92.bias, ...), custom_call_target="tpu_custom_call" | custom-call | flops 1024 | bytes 1024 | tf_op jit(solution)/shard_map/pallas_call | solution.py:324
  245.0 8.8 %shard_map.208 = bf16[4,576,1152]{2,1,0:T(8,128)(2,1)} custom-call(s32[4]{0:T(128)S(1)} %get-tuple-element.277.order, s32[1]{0:T(128)} %bitcast.41.side, s32[16]{0:T(128)S(1)} %stack.112.table, bf16[4,512,1152]{2,1,0:T(8,128)(2,1)} %get-tuple-element.140.refs_0_.hidden, bf16[512,1152]{1,0:T(8,128)(2,1)S(1)} %copy-done.1), custom_call_target="tpu_custom_call" | custom-call | flops 1024 | bytes 1024 | tf_op jit(solution)/shard_map/pallas_call | solution.py:728
  263.7 21.6 %shard_map.209 = (bf16[4,512,1152]{2,1,0:T(8,128)(2,1)}, f32[4,1,1152]{2,1,0:T(1,128)S(1)}, bf16[512,1152]{1,0:T(8,128)(2,1)}, f32[2,1,1152]{2,1,0:T(1,128)S(1)}) custom-call(s32[4]{0:T(128)S(1)} %iota.6.order, s32[4]{0:T(128)S(1)} %copy-done.35, s32[2]{0:T(128)S(1)} %copy-done.33, bf16[4,512,1152]{2,1,0:T(8,128)(2,1)} %get-tuple-element.140.refs_0_.hidden, ...), custom_call_target="tpu_custom_call" | custom-call | flops 1024 | bytes 1024 | tf_op jit(solution)/shard_map/pallas_call | solution.py:404
  291.7 5.2 concatenate.46
  300.3 9.3 %shard_map.210 = (bf16[2,288,1152]{2,1,0:T(8,128)(2,1)S(1)}, bf16[2,288,1152]{2,1,0:T(8,128)(2,1)S(1)}, bf16[2,288,1152]{2,1,0:T(8,128)(2,1)}, bf16[2,288,1152]{2,1,0:T(8,128)(2,1)}) custom-call(s32[4]{0:T(128)S(1)} %copy-done.24, s32[1]{0:T(128)} %bitcast.55.side, s32[16]{0:T(128)S(1)} %stack.112.table, ...), custom_call_target="tpu_custom_call" | custom-call | flops 1024 | bytes 1024 | tf_op jit(solution)/shard_map/pallas_call | solution.py:728
  309.7 8.4 %shard_map.211 = bf16[4,576,1152]{2,1,0:T(8,128)(2,1)} custom-call(s32[4]{0:T(128)S(1)} %copy-done.24, s32[1]{0:T(128)} %bitcast.41.side, s32[16]{0:T(128)S(1)} %stack.112.table, bf16[512,1152]{1,0:T(8,128)(2,1)S(1)} %get-tuple-element.134.mlp_in.refs_0_, bf16[4,512,1152]{2,1,0:T(8,128)(2,1)} %get-tuple-element.157.refs_1_.d_pre), custom_call_target="tpu_custom_call" | custom-call | flops 1024 | bytes 1024 | tf_op jit(solution)/shard_map/pallas_call | solution.py:728
  320.8 15.6 %shard_map.212 = (f32[512,1152]{1,0:T(8,128)}, bf16[512,1152]{1,0:T(8,128)(2,1)S(1)}, f32[2,4,1152]{2,1,0:T(4,128)S(1)}) custom-call(s32[2]{0:T(128)S(1)} %copy-done.34, bf16[4,512,1152]{2,1,0:T(8,128)(2,1)} %get-tuple-element.157.refs_1_.d_pre, bf16[4,1152,1152]{2,1,0:T(8,128)(2,1)} %bitcast.258, f32[2,6,1152]{2,1,0:T(8,128)S(1)} %copy-done.20, ...), custom_call_target="tpu_custom_call" | custom-call | flops 1024 | bytes 1024 | tf_op jit(solution)/shard_map/pallas_call | solution.py:496
  337.5 9.5 %shard_map.213 = (bf16[2,288,1152]{2,1,0:T(8,128)(2,1)S(1)}, bf16[2,288,1152]{2,1,0:T(8,128)(2,1)}, bf16[2,288,1152]{2,1,0:T(8,128)(2,1)}, bf16[2,288,1152]{2,1,0:T(8,128)(2,1)}) custom-call(s32[4]{0:T(128)S(1)} %copy-done.24, s32[1]{0:T(128)} %bitcast.55.side, s32[16]{0:T(128)S(1)} %stack.112.table, ...), custom_call_target="tpu_custom_call" | custom-call | flops 1024 | bytes 1024 | tf_op jit(solution)/shard_map/pallas_call | solution.py:728
  360.8 26.2 %shard_map.214 = (bf16[4,512,1152]{2,1,0:T(8,128)(2,1)}, f32[2,3,1152]{2,1,0:T(4,128)S(1)}) custom-call(s32[2]{0:T(128)S(1)} %copy-done.34, bf16[512,1152]{1,0:T(8,128)(2,1)S(1)} %copy-done.22, bf16[5,512,1152]{2,1,0:T(8,128)(2,1)} %get-tuple-element.170.parts, bf16[4,1152,1152]{2,1,0:T(8,128)(2,1)} %bitcast.255), custom_call_target="tpu_custom_call" | custom-call | flops 1024 | bytes 1024 | tf_op jit(solution)/shard_map/pallas_call | solution.py:563
  387.0 14.2 %all-gather.18.cloned.1.call-done = bf16[1,1152,1152]{2,1,0:T(8,128)(2,1)} async-done(((bf16[1,144,1152]{2,1,0:T(8,128)(2,1)}), bf16[1,1152,1152]{2,1,0:T(8,128)(2,1)}) %all-gather.18.cloned.1.call-update) | async-done | bytes 2654224 | tf_op jit(solution)/shard_map/all_gather | solution.py:900
  401.2 9.0 %shard_map.215 = bf16[4,576,1152]{2,1,0:T(8,128)(2,1)} custom-call(s32[4]{0:T(128)S(1)} %copy-done.24, s32[1]{0:T(128)} %bitcast.41.side, s32[16]{0:T(128)S(1)} %stack.112.table, bf16[512,1152]{1,0:T(8,128)(2,1)S(1)} %copy-done.4, bf16[512,1152]{1,0:T(8,128)(2,1)S(1)} %copy-done.6, bf16[4,512,1152]{2,1,0:T(8,128)(2,1)} %get-tuple-element.193.refs_2_.d_qkv), custom_call_target="tpu_custom_call" | custom-call | flops 1024 | bytes 1024 | tf_op jit(solution)/shard_map/pallas_call | solution.py:728
  423.5 7.4 %collective-permute-done.27 = bf16[2,144,1152]{2,1,0:T(8,128)(2,1)} collective-permute-done((bf16[2,144,1152]{2,1,0:T(8,128)(2,1)}, bf16[2,144,1152]{2,1,0:T(8,128)(2,1)}, u32[]{:S(2)}, u32[]{:S(2)}) %collective-permute-start.27) | collective-permute-done | bytes 663584 | tf_op jit(solution)/shard_map/ppermute | solution.py:772
  447.9 9.9 %shard_map.216 = (bf16[2,288,1152]{2,1,0:T(8,128)(2,1)S(1)}, bf16[2,288,1152]{2,1,0:T(8,128)(2,1)}, bf16[2,288,1152]{2,1,0:T(8,128)(2,1)}, bf16[2,288,1152]{2,1,0:T(8,128)(2,1)}) custom-call(s32[4]{0:T(128)S(1)} %copy-done.24, s32[1]{0:T(128)} %bitcast.55.side, s32[16]{0:T(128)S(1)} %stack.112.table, bf16[512,1152]{1,0:T(8,128)(2,1)S(1)} %copy-done.4, ...), custom_call_target="tpu_custom_call" | custom-call | flops 1024 | bytes 1024 | tf_op jit(solution)/shard_map/pallas_call | solution.py:728
  458.9 11.2 %shard_map.217 = (bf16[512,1152]{1,0:T(8,128)(2,1)}, f32[2,2,1152]{2,1,0:T(2,128)S(1)}) custom-call(bf16[4,512,1152]{2,1,0:T(8,128)(2,1)} %get-tuple-element.193.refs_2_.d_qkv, bf16[4,1152,1152]{2,1,0:T(8,128)(2,1)} %bitcast.256, f32[2,6,1152]{2,1,0:T(8,128)S(1)} %copy-done.20, bf16[512,1152]{1,0:T(8,128)(2,1)S(1)} %bitcast.253, f32[512,1152]{1,0:T(8,128)S(1)} %copy-done.7), custom_call_target="tpu_custom_call" | custom-call | flops 1024 | bytes 1024 | tf_op jit(solution)/shard_map/pallas_call | solution.py:623
  477.9 26.7 %all_to_all.44 = f32[4,1,7488]{2,1,0:T(1,128)S(1)} all-to-all(f32[4,1,7488]{2,1,0:T(1,128)S(1)} %copy.101), channel_id=1, replica_groups=mesh['dp'=8,'fsdp'=4] {'fsdp'}, dimensions={0} | all-to-all | bytes 239616 | tf_op jit(solution)/shard_map/all_to_all | solution.py:1208
  518.1 10.4 %collective-permute-done.34 = bf16[2,144,1152]{2,1,0:T(8,128)(2,1)} collective-permute-done((bf16[2,144,1152]{2,1,0:T(8,128)(2,1)}, bf16[2,144,1152]{2,1,0:T(8,128)(2,1)}, u32[]{:S(2)}, u32[]{:S(2)}) %collective-permute-start.34) | collective-permute-done | bytes 663584 | tf_op jit(solution)/shard_map/ppermute | solution.py:772
  536.7 8.3 %shard_map.218 = bf16[4,3,144,288]{3,2,1,0:T(8,128)(2,1)} custom-call(s32[1]{0:T(128)} %bitcast.86.at, bf16[1152,1152]{1,0:T(8,128)(2,1)} %bitcast.284, bf16[144,1152]{1,0:T(8,128)(2,1)S(1)} %copy-done.12, bf16[1152,1152]{1,0:T(8,128)(2,1)} %bitcast.283), custom_call_target="tpu_custom_call" | custom-call | flops 1024 | bytes 1024 | tf_op jit(solution)/shard_map/pallas_call | solution.py:1001
  545.0 15.9 %collective-permute-done.35 = bf16[2,144,1152]{2,1,0:T(8,128)(2,1)S(1)} collective-permute-done((bf16[2,144,1152]{2,1,0:T(8,128)(2,1)S(1)}, bf16[2,144,1152]{2,1,0:T(8,128)(2,1)S(1)}, u32[]{:S(2)}, u32[]{:S(2)}) %collective-permute-start.35) | collective-permute-done | bytes 663584 | tf_op jit(solution)/shard_map/ppermute | solution.py:767
  570.8 8.4 %shard_map.219 = bf16[4,3,144,288]{3,2,1,0:T(8,128)(2,1)} custom-call(s32[1]{0:T(128)} %bitcast.86.at, bf16[1152,1152]{1,0:T(8,128)(2,1)} %bitcast.285, bf16[144,1152]{1,0:T(8,128)(2,1)S(1)} %copy-done.11, bf16[1152,1152]{1,0:T(8,128)(2,1)} %bitcast.282), custom_call_target="tpu_custom_call" | custom-call | flops 1024 | bytes 1024 | tf_op jit(solution)/shard_map/pallas_call | solution.py:1001
  579.2 6.3 collective-permute-done.36
  603.1 21.3 %all_gather.45 = f32[864,128]{1,0:T(8,128)S(1)} all-gather(f32[216,128]{1,0:T(8,128)S(1)} %reshape.307), channel_id=1, replica_groups=mesh['dp'=8,'fsdp'=4] {'fsdp'}, dimensions={0}, use_global_device_ids=true | all-gather | bytes 552960 | tf_op jit(solution)/shard_map/all_gather | solution.py:1233
  628.0 16.0 %all_gather.47 = f32[1728,128]{1,0:T(8,128)S(1)} all-gather(f32[216,128]{1,0:T(8,128)S(1)} %reshape.314), channel_id=1, replica_groups=mesh['dp'=8,'fsdp'=4] {'dp'}, dimensions={0}, use_global_device_ids=true | all-gather | bytes 995328 | tf_op jit(solution)/shard_map/all_gather | solution.py:1251
  650.0 8.3 %shard_map.220 = bf16[4,3,144,288]{3,2,1,0:T(8,128)(2,1)} custom-call(s32[1]{0:T(128)} %bitcast.86.at, bf16[1152,1152]{1,0:T(8,128)(2,1)} %bitcast.286, bf16[144,1152]{1,0:T(8,128)(2,1)S(1)} %copy-done.10, bf16[1152,1152]{1,0:T(8,128)(2,1)} %bitcast.281), custom_call_target="tpu_custom_call" | custom-call | flops 1024 | bytes 1024 | tf_op jit(solution)/shard_map/pallas_call | solution.py:1001
  667.5 13.0 %all-to-all-done.5 = bf16[4,3,144,288]{3,2,1,0:T(8,128)(2,1)} async-done(((bf16[4,3,144,288]{3,2,1,0:T(8,128)(2,1)}), bf16[4,3,144,288]{3,2,1,0:T(8,128)(2,1)}, u32[]{:S(2)}, u32[]{:S(2)}) %all-to-all-start.5) | async-done | bytes 995360 | tf_op jit(solution)/shard_map/all_to_all | solution.py:842
  683.0 7.2 %fusion.55 = (bf16[18,144,288]{2,1,0:T(8,128)(2,1)}, f32[18,144,288]{2,1,0:T(8,128)}, f32[18,144,288]{2,1,0:T(8,128)}) fusion(f32[18,144,288]{2,1,0:T(8,128)S(1)} %copy-done.37, f32[4,144,288]{2,1,0:T(8,128)} %get-tuple-element.256, f32[4,144,288]{2,1,0:T(8,128)} %get-tuple-element.253, f32[4,144,288]{2,1,0:T(8,128)S(1)} %get-tuple-element.250, ...), kind=kLoop, calls=%fused_computation.144 | loop fusion | flops 5971968 | bytes 16422912 | tf_op jit(solution)/shard_map/convert_element_type | solution.py:1266
  (396 shorter events, 203.7 us)
Async XLA Ops:
  7.2 133.8 %all-gather.20.cloned.1.call-start = ((), (), s32[]{:S(2)}) async-start(), calls=%async_computation.9 | async-start | bytes 10948608 | tf_op jit(solution)/shard_map/all_gather | solution.py:851
  33.9 227.8 %all-gather.22.cloned.1.call-start = ((), (), s32[]{:S(2)}) async-start(), calls=%async_computation.10 | async-start | bytes 10948608 | tf_op jit(solution)/shard_map/all_gather | solution.py:851
  41.9 310.0 %all-gather.14.cloned.1.call-start = ((), (), s32[]{:S(2)}) async-start(), calls=%async_computation.6 | async-start | bytes 2985984 | tf_op jit(solution)/shard_map/all_gather | solution.py:900
  53.4 25.9 %collective-permute-start.4 = (bf16[144,1152]{1,0:T(8,128)(2,1)S(1)}, bf16[144,1152]{1,0:T(8,128)(2,1)S(1)}, u32[]{:S(2)}, u32[]{:S(2)}) collective-permute-start(bf16[144,1152]{1,0:T(8,128)(2,1)S(1)} %get-tuple-element.126.refs_0_), channel_id=1, source_target_pairs={{0,16},{4,20},{8,24},{12,28},{16,0},{20,4},{24,8},{28,12},{1,17},{... | collective-permute-start | bytes 995336 | tf_op jit(solution)/shard_map/ppermute | solution.py:762
  55.4 23.9 %collective-permute-start.5 = (bf16[144,1152]{1,0:T(8,128)(2,1)S(1)}, bf16[144,1152]{1,0:T(8,128)(2,1)S(1)}, u32[]{:S(2)}, u32[]{:S(2)}) collective-permute-start(bf16[144,1152]{1,0:T(8,128)(2,1)S(1)} %get-tuple-element.126.refs_0_), channel_id=1, source_target_pairs={{0,24},{4,28},{8,0},{12,4},{16,8},{20,12},{24,16},{28,20},{1,25},{... | collective-permute-start | bytes 995336 | tf_op jit(solution)/shard_map/ppermute | solution.py:762
  143.5 48.4 %collective-permute-start.7 = (bf16[576,1152]{1,0:T(8,128)(2,1)}, bf16[576,1152]{1,0:T(8,128)(2,1)S(1)}, u32[]{:S(2)}, u32[]{:S(2)}) collective-permute-start(bf16[576,1152]{1,0:T(8,128)(2,1)} %constant_dynamic-slice_fusion.3), channel_id=1, source_target_pairs={{0,1},{1,0},{2,3},{3,2},{4,5},{5,4},{6,7},{7,6},{8,9},{9,8},{10,11... | collective-permute-start | bytes 3981320 | tf_op jit(solution)/shard_map/ppermute | solution.py:772
  144.9 47.0 %collective-permute-start.8 = (bf16[576,1152]{1,0:T(8,128)(2,1)}, bf16[576,1152]{1,0:T(8,128)(2,1)}, u32[]{:S(2)}, u32[]{:S(2)}) collective-permute-start(bf16[576,1152]{1,0:T(8,128)(2,1)} %constant_dynamic-slice_fusion.3), channel_id=1, source_target_pairs={{0,2},{1,3},{2,0},{3,1},{4,6},{5,7},{6,4},{7,5},{8,10},{9,11},{10,... | collective-permute-start | bytes 3981320 | tf_op jit(solution)/shard_map/ppermute | solution.py:772
  145.5 78.2 %collective-permute-start.9 = (bf16[576,1152]{1,0:T(8,128)(2,1)}, bf16[576,1152]{1,0:T(8,128)(2,1)}, u32[]{:S(2)}, u32[]{:S(2)}) collective-permute-start(bf16[576,1152]{1,0:T(8,128)(2,1)} %constant_dynamic-slice_fusion.3), channel_id=1, source_target_pairs={{0,3},{1,2},{2,1},{3,0},{4,7},{5,6},{6,5},{7,4},{8,11},{9,10},{10,... | collective-permute-start | bytes 3981320 | tf_op jit(solution)/shard_map/ppermute | solution.py:772
  253.8 43.1 %collective-permute-start.16 = (bf16[4,576,1152]{2,1,0:T(8,128)(2,1)}, bf16[4,576,1152]{2,1,0:T(8,128)(2,1)}, u32[]{:S(2)}, u32[]{:S(2)}) collective-permute-start(bf16[4,576,1152]{2,1,0:T(8,128)(2,1)} %shard_map.208), channel_id=1, source_target_pairs={{0,4},{4,0},{8,12},{12,8},{16,20},{20,16},{24,28},{28,24},{1,5},{5... | collective-permute-start | bytes 15925256 | tf_op jit(solution)/shard_map/ppermute | solution.py:757
  255.5 29.9 %collective-permute-start.13 = (bf16[6,144,288]{2,1,0:T(8,128)(2,1)}, bf16[6,144,288]{2,1,0:T(8,128)(2,1)}, u32[]{:S(2)}, u32[]{:S(2)}) collective-permute-start(bf16[6,144,288]{2,1,0:T(8,128)(2,1)} %get-tuple-element.242), channel_id=1, source_target_pairs={{0,1},{1,0},{2,3},{3,2},{4,5},{5,4},{6,7},{7,6},{8,9},{9,8},{10,11... | collective-permute-start | bytes 1493000 | tf_op jit(solution)/shard_map/ppermute | solution.py:772
  255.9 32.4 %collective-permute-start.14 = (bf16[6,144,288]{2,1,0:T(8,128)(2,1)}, bf16[6,144,288]{2,1,0:T(8,128)(2,1)}, u32[]{:S(2)}, u32[]{:S(2)}) collective-permute-start(bf16[6,144,288]{2,1,0:T(8,128)(2,1)} %get-tuple-element.241), channel_id=1, source_target_pairs={{0,2},{1,3},{2,0},{3,1},{4,6},{5,7},{6,4},{7,5},{8,10},{9,11},{10,... | collective-permute-start | bytes 1493000 | tf_op jit(solution)/shard_map/ppermute | solution.py:772
  258.5 29.8 %collective-permute-start.15 = (bf16[6,144,288]{2,1,0:T(8,128)(2,1)}, bf16[6,144,288]{2,1,0:T(8,128)(2,1)}, u32[]{:S(2)}, u32[]{:S(2)}) collective-permute-start(bf16[6,144,288]{2,1,0:T(8,128)(2,1)} %get-tuple-element.240), channel_id=1, source_target_pairs={{0,3},{1,2},{2,1},{3,0},{4,7},{5,6},{6,5},{7,4},{8,11},{9,10},{10,... | collective-permute-start | bytes 1493000 | tf_op jit(solution)/shard_map/ppermute | solution.py:772
  299.7 87.3 %all-gather.16.cloned.1.call-start = ((), (), s32[]{:S(2)}) async-start(), calls=%async_computation.7 | async-start | bytes 2985984 | tf_op jit(solution)/shard_map/all_gather | solution.py:900
  300.3 100.9 %all-gather.18.cloned.1.call-start = ((), (), s32[]{:S(2)}) async-start(), calls=%async_computation.8 | async-start | bytes 2985984 | tf_op jit(solution)/shard_map/all_gather | solution.py:900
  318.3 217.7 %all-gather.24.cloned.1.call-start = ((), (), s32[]{:S(2)}) async-start(), calls=%async_computation.11 | async-start | bytes 2985984 | tf_op jit(solution)/shard_map/all_gather | solution.py:954
  318.8 31.7 %collective-permute-start.18 = (bf16[2,288,1152]{2,1,0:T(8,128)(2,1)}, bf16[2,288,1152]{2,1,0:T(8,128)(2,1)}, u32[]{:S(2)}, u32[]{:S(2)}) collective-permute-start(bf16[2,288,1152]{2,1,0:T(8,128)(2,1)} %copy-done.36), channel_id=1, source_target_pairs={{0,1},{1,0},{2,3},{3,2},{4,5},{5,4},{6,7},{7,6},{8,9},{9,8},{10,11... | collective-permute-start | bytes 3981320 | tf_op jit(solution)/shard_map/ppermute | solution.py:772
  320.4 31.5 %collective-permute-start.19 = (bf16[2,288,1152]{2,1,0:T(8,128)(2,1)}, bf16[2,288,1152]{2,1,0:T(8,128)(2,1)}, u32[]{:S(2)}, u32[]{:S(2)}) collective-permute-start(bf16[2,288,1152]{2,1,0:T(8,128)(2,1)} %get-tuple-element.167), channel_id=1, source_target_pairs={{0,2},{1,3},{2,0},{3,1},{4,6},{5,7},{6,4},{7,5},{8,10},{9,11},{10,... | collective-permute-start | bytes 3981320 | tf_op jit(solution)/shard_map/ppermute | solution.py:772
  354.1 47.1 %collective-permute-start.21 = (bf16[2,144,1152]{2,1,0:T(8,128)(2,1)S(1)}, bf16[2,144,1152]{2,1,0:T(8,128)(2,1)}, u32[]{:S(2)}, u32[]{:S(2)}) collective-permute-start(bf16[2,144,1152]{2,1,0:T(8,128)(2,1)S(1)} %dynamic-slice_bitcast_fusion.7), channel_id=1, source_target_pairs={{0,1},{1,0},{2,3},{3,2},{4,5},{5,4},{6,7},{7,6},{8,9},{9,8},{10,11... | collective-permute-start | bytes 1990664 | tf_op jit(solution)/shard_map/ppermute | solution.py:772
  354.6 46.6 %collective-permute-start.22 = (bf16[2,288,1152]{2,1,0:T(8,128)(2,1)}, bf16[2,288,1152]{2,1,0:T(8,128)(2,1)}, u32[]{:S(2)}, u32[]{:S(2)}) collective-permute-start(bf16[2,288,1152]{2,1,0:T(8,128)(2,1)} %get-tuple-element.176), channel_id=1, source_target_pairs={{0,1},{1,0},{2,3},{3,2},{4,5},{5,4},{6,7},{7,6},{8,9},{9,8},{10,11... | collective-permute-start | bytes 3981320 | tf_op jit(solution)/shard_map/ppermute | solution.py:772
  356.2 45.0 %collective-permute-start.23 = (bf16[2,288,1152]{2,1,0:T(8,128)(2,1)}, bf16[2,288,1152]{2,1,0:T(8,128)(2,1)}, u32[]{:S(2)}, u32[]{:S(2)}) collective-permute-start(bf16[2,288,1152]{2,1,0:T(8,128)(2,1)} %get-tuple-element.177), channel_id=1, source_target_pairs={{0,2},{1,3},{2,0},{3,1},{4,6},{5,7},{6,4},{7,5},{8,10},{9,11},{10,... | collective-permute-start | bytes 3981320 | tf_op jit(solution)/shard_map/ppermute | solution.py:772
  359.3 41.9 %collective-permute-start.20 = (bf16[2,144,1152]{2,1,0:T(8,128)(2,1)}, bf16[2,144,1152]{2,1,0:T(8,128)(2,1)}, u32[]{:S(2)}, u32[]{:S(2)}) collective-permute-start(bf16[2,144,1152]{2,1,0:T(8,128)(2,1)} %dynamic-slice_bitcast_fusion.8), channel_id=1, source_target_pairs={{0,2},{1,3},{2,0},{3,1},{4,6},{5,7},{6,4},{7,5},{8,10},{9,11},{10,... | collective-permute-start | bytes 1990664 | tf_op jit(solution)/shard_map/ppermute | solution.py:772
  410.2 29.3 %collective-permute-start.24 = (bf16[4,576,1152]{2,1,0:T(8,128)(2,1)}, bf16[4,576,1152]{2,1,0:T(8,128)(2,1)}, u32[]{:S(2)}, u32[]{:S(2)}) collective-permute-start(bf16[4,576,1152]{2,1,0:T(8,128)(2,1)} %shard_map.215), channel_id=1, source_target_pairs={{0,4},{4,0},{8,12},{12,8},{16,20},{20,16},{24,28},{28,24},{1,5},{5... | collective-permute-start | bytes 15925256 | tf_op jit(solution)/shard_map/ppermute | solution.py:757
  443.3 26.8 %collective-permute-start.28 = (bf16[2,144,1152]{2,1,0:T(8,128)(2,1)}, bf16[2,144,1152]{2,1,0:T(8,128)(2,1)}, u32[]{:S(2)}, u32[]{:S(2)}) collective-permute-start(bf16[2,144,1152]{2,1,0:T(8,128)(2,1)} %dynamic-slice_bitcast_fusion.3), channel_id=1, source_target_pairs={{0,8},{4,12},{8,0},{12,4},{16,24},{20,28},{24,16},{28,20},{1,9},{5... | collective-permute-start | bytes 1990664 | tf_op jit(solution)/shard_map/ppermute | solution.py:767
  446.5 23.6 %collective-permute-start.29 = (bf16[1,144,1152]{2,1,0:T(8,128)(2,1)}, bf16[1,144,1152]{2,1,0:T(8,128)(2,1)S(1)}, u32[]{:S(2)}, u32[]{:S(2)}) collective-permute-start(bf16[1,144,1152]{2,1,0:T(8,128)(2,1)} %constant_dynamic-slice_fusion.2), channel_id=1, source_target_pairs={{0,16},{4,20},{8,24},{12,28},{16,0},{20,4},{24,8},{28,12},{1,17},{... | collective-permute-start | bytes 995336 | tf_op jit(solution)/shard_map/ppermute | solution.py:767
  470.9 99.8 %all-gather.26.cloned.1.call-start = ((), (), s32[]{:S(2)}) async-start(), calls=%async_computation.12 | async-start | bytes 2985984 | tf_op jit(solution)/shard_map/all_gather | solution.py:954
  471.2 37.4 %collective-permute-start.30 = (bf16[2,288,1152]{2,1,0:T(8,128)(2,1)}, bf16[2,288,1152]{2,1,0:T(8,128)(2,1)}, u32[]{:S(2)}, u32[]{:S(2)}) collective-permute-start(bf16[2,288,1152]{2,1,0:T(8,128)(2,1)} %get-tuple-element.206), channel_id=1, source_target_pairs={{0,1},{1,0},{2,3},{3,2},{4,5},{5,4},{6,7},{7,6},{8,9},{9,8},{10,11... | collective-permute-start | bytes 3981320 | tf_op jit(solution)/shard_map/ppermute | solution.py:772
  472.7 35.9 %collective-permute-start.31 = (bf16[2,288,1152]{2,1,0:T(8,128)(2,1)}, bf16[2,288,1152]{2,1,0:T(8,128)(2,1)}, u32[]{:S(2)}, u32[]{:S(2)}) collective-permute-start(bf16[2,288,1152]{2,1,0:T(8,128)(2,1)} %get-tuple-element.207), channel_id=1, source_target_pairs={{0,2},{1,3},{2,0},{3,1},{4,6},{5,7},{6,4},{7,5},{8,10},{9,11},{10,... | collective-permute-start | bytes 3981320 | tf_op jit(solution)/shard_map/ppermute | solution.py:772
  475.4 33.2 %collective-permute-start.32 = (bf16[1,144,1152]{2,1,0:T(8,128)(2,1)S(1)}, bf16[1,144,1152]{2,1,0:T(8,128)(2,1)S(1)}, u32[]{:S(2)}, u32[]{:S(2)}) collective-permute-start(bf16[1,144,1152]{2,1,0:T(8,128)(2,1)S(1)} %constant_dynamic-slice_fusion.1), channel_id=1, source_target_pairs={{0,16},{4,20},{8,24},{12,28},{16,0},{20,4},{24,8},{28,12},{1,17},{... | collective-permute-start | bytes 995336 | tf_op jit(solution)/shard_map/ppermute | solution.py:767
  535.8 25.2 %collective-permute-start.35 = (bf16[2,144,1152]{2,1,0:T(8,128)(2,1)S(1)}, bf16[2,144,1152]{2,1,0:T(8,128)(2,1)S(1)}, u32[]{:S(2)}, u32[]{:S(2)}) collective-permute-start(bf16[2,144,1152]{2,1,0:T(8,128)(2,1)S(1)} %dynamic-slice_bitcast_fusion), channel_id=1, source_target_pairs={{0,8},{4,12},{8,0},{12,4},{16,24},{20,28},{24,16},{28,20},{1,9},{5... | collective-permute-start | bytes 1990664 | tf_op jit(solution)/shard_map/ppermute | solution.py:767
  561.8 23.7 %all-to-all-start.2 = ((bf16[4,3,144,288]{3,2,1,0:T(8,128)(2,1)}), bf16[4,3,144,288]{3,2,1,0:T(8,128)(2,1)S(1)}, u32[]{:S(2)}, u32[]{:S(2)}) async-start(bf16[4,3,144,288]{3,2,1,0:T(8,128)(2,1)} %shard_map.218), calls=%async_computation.2 | async-start | bytes 2654208 | tf_op jit(solution)/shard_map/all_to_all | solution.py:842
  565.5 84.5 %all-gather.28.cloned.1.call-start = ((), (), s32[]{:S(2)}) async-start(), calls=%async_computation.13 | async-start | bytes 2985984 | tf_op jit(solution)/shard_map/all_gather | solution.py:954
  598.1 51.8 %all-to-all-start.4 = ((bf16[4,3,144,288]{3,2,1,0:T(8,128)(2,1)}), bf16[4,3,144,288]{3,2,1,0:T(8,128)(2,1)}, u32[]{:S(2)}, u32[]{:S(2)}) async-start(bf16[4,3,144,288]{3,2,1,0:T(8,128)(2,1)} %shard_map.219), calls=%async_computation.4 | async-start | bytes 2654208 | tf_op jit(solution)/shard_map/all_to_all | solution.py:842
  (93 other events, 844.9 us)
Sparse Core Ops, SparseCore 0:
  34.1 106.8 all-gather.19
  144.6 105.3 all-gather.21
  299.8 31.9 all-gather.13
  333.3 33.1 all-gather.15
  368.0 33.1 all-gather.17
  471.1 44.3 all-gather.23
  517.7 36.0 all-gather.25
  586.5 34.8 all-gather.27

commit v16 on v15

--- a/solution.py
+++ b/solution.py
@@ -959,7 +959,7 @@
 
 
 def products_kernel(chips, at, gathered, left_root, right_root, out, whole, semaphores):
-    chunk, width = left_root.shape
+    chunk, width = left_root.shape[1:]
     ranks = out.shape[0]
     copies = []
     for index in range(2 * chips):
@@ -979,8 +979,8 @@
     picked = lax.broadcasted_iota(jnp.int32, (width, chunk), 0) - first
     picked = picked == lax.broadcasted_iota(jnp.int32, (width, chunk), 1)
     own_columns = narrow(dot_nn(grad, narrow(picked.astype(jnp.float32))))
-    side_high, side_low = split_high(dot_nn(left_root[...], grad))
-    right = right_root[...]
+    side_high, side_low = split_high(dot_nn(left_root[0], grad))
+    right = right_root[0]
     precond = dot_nn(side_high, right) + dot_nn(side_low, right)
     outer = dot_nt(whole[pl.ds(pl.multiple_of(first, 16), chunk), :], grad)
     inner = dot_tn(own_columns, grad)
@@ -991,10 +991,10 @@
             out[rank, at_out] = low[:, span]
 
 
-def owned_step(whole, left_root, right_root, group):
+def owned_step(whole, left_roots, right_roots, index, group):
     ranks, dp_count = lax.axis_size("fsdp"), lax.axis_size("dp")
     shares = ranks // group
-    chunk, total = left_root.shape
+    chunk, total = left_roots.shape[1:]
     col_part = total // ranks
     first = lax.axis_index("dp") * (chunk * shares) + lax.axis_index("fsdp") % shares * chunk
     if shares == 1:
@@ -1003,10 +1003,11 @@
             in_specs=[
                 pl.BlockSpec(memory_space=pltpu.SMEM),
                 pl.BlockSpec(memory_space=pl.ANY),
-                pl.BlockSpec(memory_space=pltpu.VMEM),
-                pl.BlockSpec(memory_space=pltpu.VMEM),
+                pl.BlockSpec((1, chunk, total), lambda step: (index, 0, 0)),
+                pl.BlockSpec((1, total, total), lambda step: (index, 0, 0)),
             ],
-            out_specs=pl.BlockSpec(memory_space=pltpu.VMEM),
+            out_specs=pl.BlockSpec((ranks, 3, chunk, col_part), lambda step: (0, 0, 0, 0)),
+            grid=(1,),
             out_shape=jax.ShapeDtypeStruct((ranks, 3, chunk, col_part), jnp.bfloat16),
             scratch_shapes=[
                 pltpu.VMEM((total, total), jnp.bfloat16),
@@ -1014,7 +1015,8 @@
             ],
             compiler_params=pltpu.CompilerParams(vmem_limit_bytes=vmem_bytes),
             cost_estimate=little_cost,
-        )((first // 16)[None], whole, left_root, right_root)
+        )((first // 16)[None], whole, left_roots, right_roots)
+    left_root, right_root = left_roots[index], right_roots[index]
     grad_rows = lax.dynamic_slice_in_dim(whole, first, chunk, 0)
     own_columns = lax.dynamic_slice_in_dim(whole, first, chunk, 1)
     outer = fast_dot("rk,jk->rj", grad_rows, whole)
@@ -1135,8 +1137,7 @@
     two_parts = two_steps.send(two_parts)
     d_pre, two_parts = tie(d_pre, two_parts)
     two_parts = two_steps.send(two_parts)
-    left_rows, right_rows = jnp.split(root_rows, 2)
-    right_wholes = [gather_own(rows[None], group)[0] for rows in right_rows]
+    right_wholes = gather_own(root_rows[3:], group)
     one_steps = sum_blocks([mlp_in], [0] * group, d_pre, group)
     one_parts = next(one_steps)
     d_pre, one_parts = tie(d_pre, one_parts)
@@ -1146,14 +1147,12 @@
     )
     d_proj, one_parts = tie(d_proj, one_parts)
     one_parts = one_steps.send(one_parts)
-    d_proj, one_parts, two_parts, right_wholes[2] = tie(
-        d_proj, one_parts, two_parts, right_wholes[2]
-    )
+    d_proj, one_parts, two_parts = tie(d_proj, one_parts, two_parts)
     two_parts = two_steps.send(two_parts)
     one_parts = one_steps.send(one_parts)
     d_heads, head_sums = run_attention_back(frames, frame_counts, d_proj, parts, attn_w)
-    d_heads, two_parts, one_parts, right_wholes[1], right_wholes[0] = tie(
-        d_heads, two_parts, one_parts, right_wholes[1], right_wholes[0]
+    d_heads, two_parts, one_parts, right_wholes = tie(
+        d_heads, two_parts, one_parts, right_wholes
     )
     two_parts = two_steps.send(two_parts)
     one_parts = one_steps.send(one_parts)
@@ -1161,15 +1160,11 @@
     attn_parts = next(attn_steps)
     d_heads, attn_parts = tie(d_heads, attn_parts)
     attn_parts = attn_steps.send(attn_parts)
-    d_heads, attn_parts, two_parts, one_parts = tie(d_heads, attn_parts, two_parts, one_parts)
+    input_grad, input_sums = run_input(d_heads, attn_w, mods, stream, d_resid)
+    input_sums, attn_parts, two_parts, one_parts = tie(
+        input_sums, attn_parts, two_parts, one_parts
+    )
     two_parts = two_steps.send(two_parts)
-    one_parts = one_steps.send(one_parts)
-    attn_parts = attn_steps.send(attn_parts)
-    d_heads, attn_parts = tie(d_heads, attn_parts)
-    attn_parts = attn_steps.send(attn_parts)
-    input_grad, input_sums = run_input(d_heads, attn_w, mods, stream, d_resid)
-    input_sums, one_parts, two_parts = tie(input_sums, one_parts, two_parts)
-    whole_two = two_steps.send(two_parts)
     one_parts = one_steps.send(one_parts)
 
     d_mods = jnp.stack(
@@ -1206,9 +1201,8 @@
         axis=1,
     )
     rank_sums = lax.all_to_all(to_ranks, "fsdp", 0, 0, tiled=True)
-    rank_sums, attn_parts, one_parts = tie(rank_sums, attn_parts, one_parts)
+    rank_sums, attn_parts = tie(rank_sums, attn_parts)
     attn_parts = attn_steps.send(attn_parts)
-    whole_one = one_steps.send(one_parts)
     rank_sums = jnp.sum(rank_sums, axis=0)
     to_rows = jnp.concatenate(
         [
@@ -1219,18 +1213,28 @@
     )
     to_rows, attn_parts = tie(to_rows, attn_parts)
     attn_parts = attn_steps.send(attn_parts)
-    products_two = owned_step(whole_two, left_rows[2], right_wholes[2], group)
+    from_rows = lax.all_to_all(to_rows, "dp", 0, 0, tiled=True)
+    from_rows, two_parts, one_parts = tie(from_rows, two_parts, one_parts)
+    whole_two = two_steps.send(two_parts)
+    one_parts = one_steps.send(one_parts)
+    from_rows, attn_parts, one_parts = tie(from_rows, attn_parts, one_parts)
+    attn_parts = attn_steps.send(attn_parts)
+    whole_one = one_steps.send(one_parts)
+    bias_grad = jnp.sum(from_rows[:, mod_size:], axis=0)
+    mod_grad_cols = from_rows[:, :mod_size].reshape(all_clips, mod_count, col_part)
+    mod_grad = lax.all_gather(packed([mod_grad_cols], 8), "fsdp", axis=0, tiled=True)
+    mod_grad, attn_parts = tie(mod_grad, attn_parts)
+    attn_parts = attn_steps.send(attn_parts)
+    products_two = owned_step(whole_two, root_rows, right_wholes, 2, group)
     products_two, attn_parts = tie(products_two, attn_parts)
     attn_parts = attn_steps.send(attn_parts)
     back_two = shard_rows(products_two, group)
-    products_one = owned_step(whole_one, left_rows[1], right_wholes[1], group)
-    to_rows, back_two, products_one, attn_parts = tie(to_rows, back_two, products_one, attn_parts)
+    products_one = owned_step(whole_one, root_rows, right_wholes, 1, group)
+    mod_grad, back_two, products_one, attn_parts = tie(
+        mod_grad, back_two, products_one, attn_parts
+    )
     whole_attn = attn_steps.send(attn_parts)
     back_one = shard_rows(products_one, group)
-    from_rows = lax.all_to_all(to_rows, "dp", 0, 0, tiled=True)
-    bias_grad = jnp.sum(from_rows[:, mod_size:], axis=0)
-    mod_grad_cols = from_rows[:, :mod_size].reshape(all_clips, mod_count, col_part)
-    mod_grad = lax.all_gather(packed([mod_grad_cols], 8), "fsdp", axis=0, tiled=True)
     mod_grad = mod_grad.reshape(ranks, -1)[:, : mod_grad_cols.size]
     mod_grad = mod_grad.reshape(ranks, all_clips, mod_count, col_part).transpose(1, 2, 0, 3)
     mod_grad = mod_grad.reshape(all_clips, mod_count, width)
@@ -1253,7 +1257,7 @@
     mod_right = mod_right.reshape(all_clips, mod_count, col_part)
     ada_pre = jnp.einsum("jrc,cje->jre", left_cond, mod_right, precision=precise)
     whole_attn, back_one = tie(whole_attn, back_one)
-    back_attn = shard_rows(owned_step(whole_attn, left_rows[0], right_wholes[0], group), group)
+    back_attn = shard_rows(owned_step(whole_attn, root_rows, right_wholes, 0, group), group)
 
     def joined(at, ada):
         return jnp.concatenate([ada, wide(back_attn[at]), wide(back_one[at]), wide(back_two[at])])

time: 710 us -> 708 us (level)
  blocking collectives: 88.2 us -> 65.6 us
  waiting for transfers between devices: 211 us -> 224 us
  local copies, waits for them, and re-layouts: 48.9 us -> 57.1 us
    all_to_all x1 -> x0, blocking collectives: 26.7 us -> none  [per_device(): rank_sums = lax.all_to_all(to_ranks, 'fsdp', 0, 0, tiled=True)]
    ppermute x6, waiting for transfers between devices: 31.1 us -> 53.4 us  [chip_swap(): lax.ppermute(array, 'dp', [(at, at ^ 2 * bits) for at in range(count)])]
    all_gather x3 -> x1, waiting for transfers between devices: 14.2 us -> 0.01 us  [gather_own(): return lax.all_gather(rows, 'dp', axis=1, tiled=True)]
    all_to_all x3, waiting for transfers between devices: 13 us -> 22.1 us  [shard_rows(): moved = lax.all_to_all(split, 'fsdp', 0, 0, tiled=True)]
    unnamed x151 -> x135, local copies, waits for them, and re-layouts: 15.9 us -> 24.9 us
  transfers between devices with their start and end apart: 50 -> 49, of which waited for: 22 -> 21; matrix products, arithmetic and copies ran while one was open for 10% -> 10% of each run, Pallas kernels for 28% -> 28%
where the time goes in v16:
time: 708 us; the launch traced here: 701 us
  waiting for transfers between devices  224 us (32%)
  Pallas kernels  215 us (30%)
  blocking collectives  65.6 us (9%)
  starting transfers between devices  58.9 us (8%)
  local copies, waits for them, and re-layouts  57.1 us (8%)
  other arithmetic  52.4 us (7%)
  between operations  15.7 us (2%)
  matrix products  13.1 us (2%)
    ppermute x21, waiting for transfers between devices, rank_swap(): return lax.ppermute(array, 'fsdp', [(at, at ^ bits) for at in range(count)])  58.4 us
    pallas_call x6, Pallas kernels, run_halves(): pl.pallas_call(body, grid_spec=pltpu.PrefetchScalarGridSpec(num_scalar_pr...  54.3 us
    all_gather x2, waiting for transfers between devices, gather_blocks(): all_rows = lax.all_gather(rows, ('fsdp', 'dp'), axis=0, tiled=True)  53.8 us
    ppermute x6, waiting for transfers between devices, chip_swap(): lax.ppermute(array, 'dp', [(at, at ^ 2 * bits) for at in range(count)])  53.4 us
    pallas_call x1, Pallas kernels, run_attention(): pl.pallas_call(functools.partial(attention_kernel, frames), grid=(clips,)...  41.1 us
    pallas_call x1, Pallas kernels, run_attention_back(): pl.pallas_call(functools.partial(attention_back_kernel, frames), grid=(cl...  26.1 us
    convert_element_type x21, other arithmetic, narrow(): return array.astype(jnp.bfloat16)  25.4 us
    pallas_call x3, Pallas kernels, owned_step(): pl.pallas_call(functools.partial(products_kernel, dp_count // 2), in_spec...  25 us
  transfers between devices with their start and end apart: 49, of which 21 were waited for; matrix products, arithmetic and copies ran while one was open for 10% of the time, Pallas kernels for 28%

profile of v16, /device:TPU:0, one launch (start us, length us, event | category | flops | bytes accessed | tf_op | source)
XLA Modules:
  0.0 701.5 jit_solution(5602956174288885862)
XLA Ops:
  17.2 14.7 %all_gather.30 = bf16[256,128]{1,0:T(8,128)(2,1)S(1)} all-gather(bf16[32,128]{1,0:T(8,128)(2,1)S(1)} %fusion.49), channel_id=1, replica_groups=mesh['dp'=8,'fsdp'=4] {'dp'}, dimensions={0}, use_global_device_ids=true | all-gather | bytes 73728 | tf_op jit(solution)/shard_map/all_gather | solution.py:1064
  44.5 8.7 %all-to-all-done = f32[16,6,288]{2,1,0:T(8,128)S(1)} async-done(((f32[16,6,288]{2,1,0:T(8,128)}), f32[16,6,288]{2,1,0:T(8,128)S(1)}, u32[]{:S(2)}, u32[]{:S(2)}) %all-to-all-start) | async-done | bytes 110624 | tf_op jit(solution)/shard_map/all_to_all | solution.py:1082
  57.4 9.5 %all_gather.31 = f32[672,128]{1,0:T(8,128)S(1)} all-gather(f32[168,128]{1,0:T(8,128)S(1)} %pad_bitcast_fusion), channel_id=1, replica_groups=mesh['dp'=8,'fsdp'=4] {'fsdp'}, dimensions={0}, use_global_device_ids=true | all-gather | bytes 430080 | tf_op jit(solution)/shard_map/all_gather | solution.py:1089
  67.0 12.3 %collective-permute-done.4.refs_2_ = bf16[144,1152]{1,0:T(8,128)(2,1)S(1)} collective-permute-done((bf16[144,1152]{1,0:T(8,128)(2,1)S(1)}, bf16[144,1152]{1,0:T(8,128)(2,1)S(1)}, u32[]{:S(2)}, u32[]{:S(2)}) %collective-permute-start.4) | collective-permute-done | bytes 331808 | tf_op jit(solution)/shard_map/ppermute | solution.py:762
  87.2 53.8 %all-gather.14.cloned.1.call-done = bf16[1,4608,1152]{2,1,0:T(8,128)(2,1)} async-done(((bf16[1,144,1152]{2,1,0:T(8,128)(2,1)}), bf16[1,4608,1152]{2,1,0:T(8,128)(2,1)}) %all-gather.14.cloned.1.call-update) | async-done | bytes 10616848 | tf_op jit(solution)/shard_map/all_gather | solution.py:851
  148.1 41.1 %shard_map.206 = (bf16[512,1152]{1,0:T(8,128)(2,1)S(1)}, bf16[5,512,1152]{2,1,0:T(8,128)(2,1)}, bf16[512,1152]{1,0:T(8,128)(2,1)S(1)}, f32[512,1152]{1,0:T(8,128...) custom-call(s32[2]{0:T(128)S(1)} %copy-done.19, ...), custom_call_target="tpu_custom_call" | custom-call | flops 1024 | bytes 1024 | tf_op jit(solution)/shard_map/pallas_call | solution.py:216
  191.3 32.4 %collective-permute-done.9.refs_5_ = bf16[576,1152]{1,0:T(8,128)(2,1)} collective-permute-done((bf16[576,1152]{1,0:T(8,128)(2,1)}, bf16[576,1152]{1,0:T(8,128)(2,1)}, u32[]{:S(2)}, u32[]{:S(2)}) %collective-permute-start.9) | collective-permute-done | bytes 1327136 | tf_op jit(solution)/shard_map/ppermute | solution.py:772
  231.1 14.1 %shard_map.207 = (bf16[4608,1152]{1,0:T(8,128)(2,1)}, bf16[4,512,1152]{2,1,0:T(8,128)(2,1)}, bf16[4,512,1152]{2,1,0:T(8,128)(2,1)}) custom-call(s32[4]{0:T(128)S(1)} %get-tuple-element.270.order, s32[7]{0:T(128)S(1)} %stack.91.starts, bf16[512,1152]{1,0:T(8,128)(2,1)S(1)} %get-tuple-element.134.mlp_in.refs_0_, f32[4,1,1152]{2,1,0:T(1,128)S(1)} %copy.92.bias, ...), custom_call_target="tpu_custom_call" | custom-call | flops 1024 | bytes 1024 | tf_op jit(solution)/shard_map/pallas_call | solution.py:324
  245.1 8.8 %shard_map.208 = bf16[4,576,1152]{2,1,0:T(8,128)(2,1)} custom-call(s32[4]{0:T(128)S(1)} %get-tuple-element.271.order, s32[1]{0:T(128)} %bitcast.41.side, s32[16]{0:T(128)S(1)} %stack.112.table, bf16[4,512,1152]{2,1,0:T(8,128)(2,1)} %get-tuple-element.140.refs_0_.hidden, bf16[512,1152]{1,0:T(8,128)(2,1)S(1)} %copy-done.2), custom_call_target="tpu_custom_call" | custom-call | flops 1024 | bytes 1024 | tf_op jit(solution)/shard_map/pallas_call | solution.py:728
  260.2 21.6 %shard_map.209 = (bf16[4,512,1152]{2,1,0:T(8,128)(2,1)}, f32[4,1,1152]{2,1,0:T(1,128)S(1)}, bf16[512,1152]{1,0:T(8,128)(2,1)}, f32[2,1,1152]{2,1,0:T(1,128)S(1)}) custom-call(s32[4]{0:T(128)S(1)} %iota.6.order, s32[4]{0:T(128)S(1)} %iota_multiply_fusion.starts, s32[2]{0:T(128)S(1)} %copy-done.19, bf16[4,512,1152]{2,1,0:T(8,128)(2,1)} %get-tuple-element.140.refs_0_.hidden, ...), custom_call_target="tpu_custom_call" | custom-call | flops 1024 | bytes 1024 | tf_op jit(solution)/shard_map/pallas_call | solution.py:404
  281.8 6.5 collective-permute-done.14
  298.4 10.1 %shard_map.210 = (bf16[2,288,1152]{2,1,0:T(8,128)(2,1)S(1)}, bf16[2,288,1152]{2,1,0:T(8,128)(2,1)}, bf16[2,288,1152]{2,1,0:T(8,128)(2,1)}, bf16[2,288,1152]{2,1,0:T(8,128)(2,1)}) custom-call(s32[4]{0:T(128)S(1)} %get-tuple-element.271.order, s32[1]{0:T(128)} %bitcast.55.side, s32[16]{0:T(128)S(1)} %stack.112.table, ...), custom_call_target="tpu_custom_call" | custom-call | flops 1024 | bytes 1024 | tf_op jit(solution)/shard_map/pallas_call | solution.py:728
  308.5 8.0 %shard_map.211 = bf16[4,576,1152]{2,1,0:T(8,128)(2,1)} custom-call(s32[4]{0:T(128)S(1)} %get-tuple-element.271.order, s32[1]{0:T(128)} %bitcast.41.side, s32[16]{0:T(128)S(1)} %stack.112.table, bf16[512,1152]{1,0:T(8,128)(2,1)S(1)} %get-tuple-element.134.mlp_in.refs_0_, bf16[4,512,1152]{2,1,0:T(8,128)(2,1)} %get-tuple-element.157.refs_1_.d_pre), custom_call_target="tpu_custom_call" | custom-call | flops 1024 | bytes 1024 | tf_op jit(solution)/shard_map/pallas_call | solution.py:728
  319.7 16.2 %shard_map.212 = (f32[512,1152]{1,0:T(8,128)}, bf16[512,1152]{1,0:T(8,128)(2,1)S(1)}, f32[2,4,1152]{2,1,0:T(4,128)S(1)}) custom-call(s32[2]{0:T(128)S(1)} %copy-done.19, bf16[4,512,1152]{2,1,0:T(8,128)(2,1)} %get-tuple-element.157.refs_1_.d_pre, bf16[4,1152,1152]{2,1,0:T(8,128)(2,1)} %bitcast.249, f32[2,6,1152]{2,1,0:T(8,128)S(1)} %broadcast_add_fusion.mods, ...), custom_call_target="tpu_custom_call" | custom-call | flops 1024 | bytes 1024 | tf_op jit(solution)/shard_map/pallas_call | solution.py:496
  335.9 9.0 %shard_map.213 = (bf16[2,288,1152]{2,1,0:T(8,128)(2,1)S(1)}, bf16[2,288,1152]{2,1,0:T(8,128)(2,1)S(1)}, bf16[2,288,1152]{2,1,0:T(8,128)(2,1)}, bf16[2,288,1152]{2,1,0:T(8,128)(2,1)}) custom-call(s32[4]{0:T(128)S(1)} %get-tuple-element.271.order, s32[1]{0:T(128)} %bitcast.55.side, s32[16]{0:T(128)S(1)} %stack.112.table, ...), custom_call_target="tpu_custom_call" | custom-call | flops 1024 | bytes 1024 | tf_op jit(solution)/shard_map/pallas_call | solution.py:728
  357.2 26.1 %shard_map.214 = (bf16[4,512,1152]{2,1,0:T(8,128)(2,1)}, f32[2,3,1152]{2,1,0:T(4,128)S(1)}) custom-call(s32[2]{0:T(128)S(1)} %copy-done.19, bf16[512,1152]{1,0:T(8,128)(2,1)S(1)} %get-tuple-element.168.d_proj, bf16[5,512,1152]{2,1,0:T(8,128)(2,1)} %get-tuple-element.169.parts, bf16[4,1152,1152]{2,1,0:T(8,128)(2,1)} %bitcast.246), custom_call_target="tpu_custom_call" | custom-call | flops 1024 | bytes 1024 | tf_op jit(solution)/shard_map/pallas_call | solution.py:563
  383.3 14.3 %collective-permute-done.20 = bf16[2,144,1152]{2,1,0:T(8,128)(2,1)S(1)} collective-permute-done((bf16[2,144,1152]{2,1,0:T(8,128)(2,1)S(1)}, bf16[2,144,1152]{2,1,0:T(8,128)(2,1)S(1)}, u32[]{:S(2)}, u32[]{:S(2)}) %collective-permute-start.20) | collective-permute-done | bytes 663584 | tf_op jit(solution)/shard_map/ppermute | solution.py:772
  400.8 8.9 %shard_map.215 = bf16[4,576,1152]{2,1,0:T(8,128)(2,1)} custom-call(s32[4]{0:T(128)S(1)} %get-tuple-element.271.order, s32[1]{0:T(128)} %bitcast.41.side, s32[16]{0:T(128)S(1)} %stack.112.table, bf16[512,1152]{1,0:T(8,128)(2,1)S(1)} %copy-done.7, bf16[512,1152]{1,0:T(8,128)(2,1)S(1)} %copy-done.10, bf16[4,512,1152]{2,1,0:T(8,128)(2,1)} %get-tuple-element.181.refs_2_.d_qkv), custom_call_target="tpu_custom_call" | custom-call | flops 1024 | bytes 1024 | tf_op jit(solution)/shard_map/pallas_call | solution.py:728
  420.9 11.5 %shard_map.216 = (bf16[512,1152]{1,0:T(8,128)(2,1)}, f32[2,2,1152]{2,1,0:T(2,128)S(1)}) custom-call(bf16[4,512,1152]{2,1,0:T(8,128)(2,1)} %get-tuple-element.181.refs_2_.d_qkv, bf16[4,1152,1152]{2,1,0:T(8,128)(2,1)} %bitcast.247, f32[2,6,1152]{2,1,0:T(8,128)S(1)} %broadcast_add_fusion.mods, bf16[512,1152]{1,0:T(8,128)(2,1)S(1)} %bitcast.244, ...), custom_call_target="tpu_custom_call" | custom-call | flops 1024 | bytes 1024 | tf_op jit(solution)/shard_map/pallas_call | solution.py:623
  453.3 9.6 %shard_map.217 = (bf16[2,288,1152]{2,1,0:T(8,128)(2,1)S(1)}, bf16[2,288,1152]{2,1,0:T(8,128)(2,1)}, bf16[2,288,1152]{2,1,0:T(8,128)(2,1)}, bf16[2,288,1152]{2,1,0:T(8,128)(2,1)}) custom-call(s32[4]{0:T(128)S(1)} %get-tuple-element.271.order, s32[1]{0:T(128)} %bitcast.55.side, s32[16]{0:T(128)S(1)} %stack.112.table, bf16[512,1152]{1,0:T(8,128)(2,1)S(1)} %copy-done.8, ...), custom_call_target="tpu_custom_call" | custom-call | flops 1024 | bytes 1024 | tf_op jit(solution)/shard_map/pallas_call | solution.py:728
  468.8 6.7 all-to-all-done.2
  483.3 33.7 %collective-permute-done.32 = bf16[1,144,1152]{2,1,0:T(8,128)(2,1)S(1)} collective-permute-done((bf16[1,144,1152]{2,1,0:T(8,128)(2,1)S(1)}, bf16[1,144,1152]{2,1,0:T(8,128)(2,1)S(1)}, u32[]{:S(2)}, u32[]{:S(2)}) %collective-permute-start.32) | collective-permute-done | bytes 331808 | tf_op jit(solution)/shard_map/ppermute | solution.py:767
  526.2 19.5 %all_gather.35 = f32[864,128]{1,0:T(8,128)} all-gather(f32[216,128]{1,0:T(8,128)} %reshape.302), channel_id=1, replica_groups=mesh['dp'=8,'fsdp'=4] {'fsdp'}, dimensions={0}, use_global_device_ids=true | all-gather | bytes 552960 | tf_op jit(solution)/shard_map/all_gather | solution.py:1225
  549.2 8.3 %shard_map.218 = bf16[4,3,144,288]{3,2,1,0:T(8,128)(2,1)} custom-call(s32[1]{0:T(128)} %bitcast.83.at, bf16[1152,1152]{1,0:T(8,128)(2,1)} %bitcast.271, bf16[6,144,1152]{2,1,0:T(8,128)(2,1)S(1)} %concatenate.46.left_root, bf16[3,1152,1152]{2,1,0:T(8,128)(2,1)} %all-gather.12.cloned.1.call-done.right_root), custom_call_target="tpu_custom_call" | custom-call | flops 1024 | bytes 1024 | tf_op jit(solution)/shard_map/pallas_call | solution.py:1001
  557.6 10.4 %collective-permute-done.35 = bf16[2,144,1152]{2,1,0:T(8,128)(2,1)} collective-permute-done((bf16[2,144,1152]{2,1,0:T(8,128)(2,1)}, bf16[2,144,1152]{2,1,0:T(8,128)(2,1)}, u32[]{:S(2)}, u32[]{:S(2)}) %collective-permute-start.35) | collective-permute-done | bytes 663584 | tf_op jit(solution)/shard_map/ppermute | solution.py:767
  577.0 8.4 %shard_map.219 = bf16[4,3,144,288]{3,2,1,0:T(8,128)(2,1)} custom-call(s32[1]{0:T(128)} %bitcast.83.at, bf16[1152,1152]{1,0:T(8,128)(2,1)} %bitcast.272, bf16[6,144,1152]{2,1,0:T(8,128)(2,1)S(1)} %concatenate.46.left_root, bf16[3,1152,1152]{2,1,0:T(8,128)(2,1)} %all-gather.12.cloned.1.call-done.right_root), custom_call_target="tpu_custom_call" | custom-call | flops 1024 | bytes 1024 | tf_op jit(solution)/shard_map/pallas_call | solution.py:1001
  585.4 6.4 collective-permute-done.36
  602.6 21.9 %all_gather.39 = f32[1728,128]{1,0:T(8,128)} all-gather(f32[216,128]{1,0:T(8,128)S(1)} %reshape.314), channel_id=1, replica_groups=mesh['dp'=8,'fsdp'=4] {'dp'}, dimensions={0}, use_global_device_ids=true | all-gather | bytes 995328 | tf_op jit(solution)/shard_map/all_gather | solution.py:1255
  636.7 12.0 %all-to-all-done.4 = bf16[4,3,144,288]{3,2,1,0:T(8,128)(2,1)} async-done(((bf16[4,3,144,288]{3,2,1,0:T(8,128)(2,1)}), bf16[4,3,144,288]{3,2,1,0:T(8,128)(2,1)}, u32[]{:S(2)}, u32[]{:S(2)}) %all-to-all-start.4) | async-done | bytes 995360 | tf_op jit(solution)/shard_map/all_to_all | solution.py:842
  648.7 8.3 %shard_map.220 = bf16[4,3,144,288]{3,2,1,0:T(8,128)(2,1)} custom-call(s32[1]{0:T(128)} %bitcast.83.at, bf16[1152,1152]{1,0:T(8,128)(2,1)} %bitcast.273, bf16[6,144,1152]{2,1,0:T(8,128)(2,1)S(1)} %concatenate.46.left_root, bf16[3,1152,1152]{2,1,0:T(8,128)(2,1)} %all-gather.12.cloned.1.call-done.right_root), custom_call_target="tpu_custom_call" | custom-call | flops 1024 | bytes 1024 | tf_op jit(solution)/shard_map/pallas_call | solution.py:1001
  668.0 10.1 %all-to-all-done.5 = bf16[4,3,144,288]{3,2,1,0:T(8,128)(2,1)} async-done(((bf16[4,3,144,288]{3,2,1,0:T(8,128)(2,1)}), bf16[4,3,144,288]{3,2,1,0:T(8,128)(2,1)}, u32[]{:S(2)}, u32[]{:S(2)}) %all-to-all-start.5) | async-done | bytes 995360 | tf_op jit(solution)/shard_map/all_to_all | solution.py:842
  680.7 7.2 %fusion.55 = (bf16[18,144,288]{2,1,0:T(8,128)(2,1)}, f32[18,144,288]{2,1,0:T(8,128)}, f32[18,144,288]{2,1,0:T(8,128)}) fusion(f32[18,144,288]{2,1,0:T(8,128)S(1)} %copy-done.20, f32[4,144,288]{2,1,0:T(8,128)} %get-tuple-element.250, f32[4,144,288]{2,1,0:T(8,128)} %get-tuple-element.247, f32[4,144,288]{2,1,0:T(8,128)S(1)} %get-tuple-element.244, ...), kind=kLoop, calls=%fused_computation.141 | loop fusion | flops 5971968 | bytes 16422912 | tf_op jit(solution)/shard_map/convert_element_type | solution.py:1270
  (374 shorter events, 195.8 us)
Async XLA Ops:
  7.2 133.8 %all-gather.14.cloned.1.call-start = ((), (), s32[]{:S(2)}) async-start(), calls=%async_computation.7 | async-start | bytes 10948608 | tf_op jit(solution)/shard_map/all_gather | solution.py:851
  33.9 224.9 %all-gather.16.cloned.1.call-start = ((), (), s32[]{:S(2)}) async-start(), calls=%async_computation.8 | async-start | bytes 10948608 | tf_op jit(solution)/shard_map/all_gather | solution.py:851
  41.9 357.6 %all-gather.12.cloned.1.call-start = ((), (), s32[]{:S(2)}) async-start(), calls=%async_computation.6 | async-start | bytes 8957952 | tf_op jit(solution)/shard_map/all_gather | solution.py:900
  53.3 26.0 %collective-permute-start.4 = (bf16[144,1152]{1,0:T(8,128)(2,1)S(1)}, bf16[144,1152]{1,0:T(8,128)(2,1)S(1)}, u32[]{:S(2)}, u32[]{:S(2)}) collective-permute-start(bf16[144,1152]{1,0:T(8,128)(2,1)S(1)} %get-tuple-element.126.refs_0_), channel_id=1, source_target_pairs={{0,16},{4,20},{8,24},{12,28},{16,0},{20,4},{24,8},{28,12},{1,17},{... | collective-permute-start | bytes 995336 | tf_op jit(solution)/shard_map/ppermute | solution.py:762
  55.4 23.9 %collective-permute-start.5 = (bf16[144,1152]{1,0:T(8,128)(2,1)S(1)}, bf16[144,1152]{1,0:T(8,128)(2,1)S(1)}, u32[]{:S(2)}, u32[]{:S(2)}) collective-permute-start(bf16[144,1152]{1,0:T(8,128)(2,1)S(1)} %get-tuple-element.126.refs_0_), channel_id=1, source_target_pairs={{0,24},{4,28},{8,0},{12,4},{16,8},{20,12},{24,16},{28,20},{1,25},{... | collective-permute-start | bytes 995336 | tf_op jit(solution)/shard_map/ppermute | solution.py:762
  143.5 47.8 %collective-permute-start.7 = (bf16[576,1152]{1,0:T(8,128)(2,1)}, bf16[576,1152]{1,0:T(8,128)(2,1)S(1)}, u32[]{:S(2)}, u32[]{:S(2)}) collective-permute-start(bf16[576,1152]{1,0:T(8,128)(2,1)} %constant_dynamic-slice_fusion.3), channel_id=1, source_target_pairs={{0,1},{1,0},{2,3},{3,2},{4,5},{5,4},{6,7},{7,6},{8,9},{9,8},{10,11... | collective-permute-start | bytes 3981320 | tf_op jit(solution)/shard_map/ppermute | solution.py:772
  144.9 46.3 %collective-permute-start.8 = (bf16[576,1152]{1,0:T(8,128)(2,1)}, bf16[576,1152]{1,0:T(8,128)(2,1)}, u32[]{:S(2)}, u32[]{:S(2)}) collective-permute-start(bf16[576,1152]{1,0:T(8,128)(2,1)} %constant_dynamic-slice_fusion.3), channel_id=1, source_target_pairs={{0,2},{1,3},{2,0},{3,1},{4,6},{5,7},{6,4},{7,5},{8,10},{9,11},{10,... | collective-permute-start | bytes 3981320 | tf_op jit(solution)/shard_map/ppermute | solution.py:772
  145.5 78.2 %collective-permute-start.9 = (bf16[576,1152]{1,0:T(8,128)(2,1)}, bf16[576,1152]{1,0:T(8,128)(2,1)}, u32[]{:S(2)}, u32[]{:S(2)}) collective-permute-start(bf16[576,1152]{1,0:T(8,128)(2,1)} %constant_dynamic-slice_fusion.3), channel_id=1, source_target_pairs={{0,3},{1,2},{2,1},{3,0},{4,7},{5,6},{6,5},{7,4},{8,11},{9,10},{10,... | collective-permute-start | bytes 3981320 | tf_op jit(solution)/shard_map/ppermute | solution.py:772
  253.9 42.1 %collective-permute-start.16 = (bf16[4,576,1152]{2,1,0:T(8,128)(2,1)}, bf16[4,576,1152]{2,1,0:T(8,128)(2,1)}, u32[]{:S(2)}, u32[]{:S(2)}) collective-permute-start(bf16[4,576,1152]{2,1,0:T(8,128)(2,1)} %shard_map.208), channel_id=1, source_target_pairs={{0,4},{4,0},{8,12},{12,8},{16,20},{20,16},{24,28},{28,24},{1,5},{5... | collective-permute-start | bytes 15925256 | tf_op jit(solution)/shard_map/ppermute | solution.py:757
  255.3 26.5 %collective-permute-start.13 = (bf16[6,144,288]{2,1,0:T(8,128)(2,1)}, bf16[6,144,288]{2,1,0:T(8,128)(2,1)}, u32[]{:S(2)}, u32[]{:S(2)}) collective-permute-start(bf16[6,144,288]{2,1,0:T(8,128)(2,1)} %get-tuple-element.242), channel_id=1, source_target_pairs={{0,1},{1,0},{2,3},{3,2},{4,5},{5,4},{6,7},{7,6},{8,9},{9,8},{10,11... | collective-permute-start | bytes 1493000 | tf_op jit(solution)/shard_map/ppermute | solution.py:772
  255.8 32.5 %collective-permute-start.14 = (bf16[6,144,288]{2,1,0:T(8,128)(2,1)}, bf16[6,144,288]{2,1,0:T(8,128)(2,1)}, u32[]{:S(2)}, u32[]{:S(2)}) collective-permute-start(bf16[6,144,288]{2,1,0:T(8,128)(2,1)} %get-tuple-element.241), channel_id=1, source_target_pairs={{0,2},{1,3},{2,0},{3,1},{4,6},{5,7},{6,4},{7,5},{8,10},{9,11},{10,... | collective-permute-start | bytes 1493000 | tf_op jit(solution)/shard_map/ppermute | solution.py:772
  258.5 29.8 %collective-permute-start.15 = (bf16[6,144,288]{2,1,0:T(8,128)(2,1)}, bf16[6,144,288]{2,1,0:T(8,128)(2,1)}, u32[]{:S(2)}, u32[]{:S(2)}) collective-permute-start(bf16[6,144,288]{2,1,0:T(8,128)(2,1)} %get-tuple-element.240), channel_id=1, source_target_pairs={{0,3},{1,2},{2,1},{3,0},{4,7},{5,6},{6,5},{7,4},{8,11},{9,10},{10,... | collective-permute-start | bytes 1493000 | tf_op jit(solution)/shard_map/ppermute | solution.py:772
  316.5 31.9 %collective-permute-start.18 = (bf16[2,288,1152]{2,1,0:T(8,128)(2,1)}, bf16[2,288,1152]{2,1,0:T(8,128)(2,1)}, u32[]{:S(2)}, u32[]{:S(2)}) collective-permute-start(bf16[2,288,1152]{2,1,0:T(8,128)(2,1)} %get-tuple-element.166), channel_id=1, source_target_pairs={{0,1},{1,0},{2,3},{3,2},{4,5},{5,4},{6,7},{7,6},{8,9},{9,8},{10,11... | collective-permute-start | bytes 3981320 | tf_op jit(solution)/shard_map/ppermute | solution.py:772
  317.9 31.6 %collective-permute-start.19 = (bf16[2,288,1152]{2,1,0:T(8,128)(2,1)}, bf16[2,288,1152]{2,1,0:T(8,128)(2,1)}, u32[]{:S(2)}, u32[]{:S(2)}) collective-permute-start(bf16[2,288,1152]{2,1,0:T(8,128)(2,1)} %get-tuple-element.167), channel_id=1, source_target_pairs={{0,2},{1,3},{2,0},{3,1},{4,6},{5,7},{6,4},{7,5},{8,10},{9,11},{10,... | collective-permute-start | bytes 3981320 | tf_op jit(solution)/shard_map/ppermute | solution.py:772
  351.2 32.0 %collective-permute-start.21 = (bf16[2,144,1152]{2,1,0:T(8,128)(2,1)S(1)}, bf16[2,144,1152]{2,1,0:T(8,128)(2,1)S(1)}, u32[]{:S(2)}, u32[]{:S(2)}) collective-permute-start(bf16[2,144,1152]{2,1,0:T(8,128)(2,1)S(1)} %dynamic-slice_bitcast_fusion.7), channel_id=1, source_target_pairs={{0,1},{1,0},{2,3},{3,2},{4,5},{5,4},{6,7},{7,6},{8,9},{9,8},{10,11... | collective-permute-start | bytes 1990664 | tf_op jit(solution)/shard_map/ppermute | solution.py:772
  351.9 45.7 %collective-permute-start.22 = (bf16[2,288,1152]{2,1,0:T(8,128)(2,1)S(1)}, bf16[2,288,1152]{2,1,0:T(8,128)(2,1)S(1)}, u32[]{:S(2)}, u32[]{:S(2)}) collective-permute-start(bf16[2,288,1152]{2,1,0:T(8,128)(2,1)S(1)} %get-tuple-element.175), channel_id=1, source_target_pairs={{0,1},{1,0},{2,3},{3,2},{4,5},{5,4},{6,7},{7,6},{8,9},{9,8},{10,11... | collective-permute-start | bytes 3981320 | tf_op jit(solution)/shard_map/ppermute | solution.py:772
  353.3 46.2 %collective-permute-start.23 = (bf16[2,288,1152]{2,1,0:T(8,128)(2,1)}, bf16[2,288,1152]{2,1,0:T(8,128)(2,1)}, u32[]{:S(2)}, u32[]{:S(2)}) collective-permute-start(bf16[2,288,1152]{2,1,0:T(8,128)(2,1)} %get-tuple-element.176), channel_id=1, source_target_pairs={{0,2},{1,3},{2,0},{3,1},{4,6},{5,7},{6,4},{7,5},{8,10},{9,11},{10,... | collective-permute-start | bytes 3981320 | tf_op jit(solution)/shard_map/ppermute | solution.py:772
  355.7 41.9 %collective-permute-start.20 = (bf16[2,144,1152]{2,1,0:T(8,128)(2,1)S(1)}, bf16[2,144,1152]{2,1,0:T(8,128)(2,1)S(1)}, u32[]{:S(2)}, u32[]{:S(2)}) collective-permute-start(bf16[2,144,1152]{2,1,0:T(8,128)(2,1)S(1)} %dynamic-slice_bitcast_fusion.8), channel_id=1, source_target_pairs={{0,2},{1,3},{2,0},{3,1},{4,6},{5,7},{6,4},{7,5},{8,10},{9,11},{10,... | collective-permute-start | bytes 1990664 | tf_op jit(solution)/shard_map/ppermute | solution.py:772
  409.7 26.1 %collective-permute-start.24 = (bf16[4,576,1152]{2,1,0:T(8,128)(2,1)}, bf16[4,576,1152]{2,1,0:T(8,128)(2,1)}, u32[]{:S(2)}, u32[]{:S(2)}) collective-permute-start(bf16[4,576,1152]{2,1,0:T(8,128)(2,1)} %shard_map.215), channel_id=1, source_target_pairs={{0,4},{4,0},{8,12},{12,8},{16,20},{20,16},{24,28},{28,24},{1,5},{5... | collective-permute-start | bytes 15925256 | tf_op jit(solution)/shard_map/ppermute | solution.py:757
  439.5 37.5 %collective-permute-start.29 = (bf16[2,144,1152]{2,1,0:T(8,128)(2,1)}, bf16[2,144,1152]{2,1,0:T(8,128)(2,1)}, u32[]{:S(2)}, u32[]{:S(2)}) collective-permute-start(bf16[2,144,1152]{2,1,0:T(8,128)(2,1)} %dynamic-slice_bitcast_fusion.3), channel_id=1, source_target_pairs={{0,8},{4,12},{8,0},{12,4},{16,24},{20,28},{24,16},{28,20},{1,9},{5... | collective-permute-start | bytes 1990664 | tf_op jit(solution)/shard_map/ppermute | solution.py:767
  449.0 28.0 %collective-permute-start.28 = (bf16[1,144,1152]{2,1,0:T(8,128)(2,1)}, bf16[1,144,1152]{2,1,0:T(8,128)(2,1)}, u32[]{:S(2)}, u32[]{:S(2)}) collective-permute-start(bf16[1,144,1152]{2,1,0:T(8,128)(2,1)} %constant_dynamic-slice_fusion.2), channel_id=1, source_target_pairs={{0,16},{4,20},{8,24},{12,28},{16,0},{20,4},{24,8},{28,12},{1,17},{... | collective-permute-start | bytes 995336 | tf_op jit(solution)/shard_map/ppermute | solution.py:767
  468.7 80.5 %all-gather.18.cloned.1.call-start = ((), (), s32[]{:S(2)}) async-start(), calls=%async_computation.9 | async-start | bytes 2985984 | tf_op jit(solution)/shard_map/all_gather | solution.py:954
  479.0 98.0 %all-gather.20.cloned.1.call-start = ((), (), s32[]{:S(2)}) async-start(), calls=%async_computation.10 | async-start | bytes 2985984 | tf_op jit(solution)/shard_map/all_gather | solution.py:954
  479.0 37.9 %collective-permute-start.30 = (bf16[2,288,1152]{2,1,0:T(8,128)(2,1)}, bf16[2,288,1152]{2,1,0:T(8,128)(2,1)S(1)}, u32[]{:S(2)}, u32[]{:S(2)}) collective-permute-start(bf16[2,288,1152]{2,1,0:T(8,128)(2,1)} %get-tuple-element.208), channel_id=1, source_target_pairs={{0,1},{1,0},{2,3},{3,2},{4,5},{5,4},{6,7},{7,6},{8,9},{9,8},{10,11... | collective-permute-start | bytes 3981320 | tf_op jit(solution)/shard_map/ppermute | solution.py:772
  480.1 36.9 %collective-permute-start.31 = (bf16[2,288,1152]{2,1,0:T(8,128)(2,1)}, bf16[2,288,1152]{2,1,0:T(8,128)(2,1)S(1)}, u32[]{:S(2)}, u32[]{:S(2)}) collective-permute-start(bf16[2,288,1152]{2,1,0:T(8,128)(2,1)} %get-tuple-element.209), channel_id=1, source_target_pairs={{0,2},{1,3},{2,0},{3,1},{4,6},{5,7},{6,4},{7,5},{8,10},{9,11},{10,... | collective-permute-start | bytes 3981320 | tf_op jit(solution)/shard_map/ppermute | solution.py:772
  482.9 34.1 %collective-permute-start.32 = (bf16[1,144,1152]{2,1,0:T(8,128)(2,1)S(1)}, bf16[1,144,1152]{2,1,0:T(8,128)(2,1)S(1)}, u32[]{:S(2)}, u32[]{:S(2)}) collective-permute-start(bf16[1,144,1152]{2,1,0:T(8,128)(2,1)S(1)} %constant_dynamic-slice_fusion.1), channel_id=1, source_target_pairs={{0,16},{4,20},{8,24},{12,28},{16,0},{20,4},{24,8},{28,12},{1,17},{... | collective-permute-start | bytes 995336 | tf_op jit(solution)/shard_map/ppermute | solution.py:767
  520.3 25.3 %collective-permute-start.34 = (bf16[2,144,1152]{2,1,0:T(8,128)(2,1)}, bf16[2,144,1152]{2,1,0:T(8,128)(2,1)}, u32[]{:S(2)}, u32[]{:S(2)}) collective-permute-start(bf16[2,144,1152]{2,1,0:T(8,128)(2,1)} %dynamic-slice_bitcast_fusion.1), channel_id=1, source_target_pairs={{0,1},{1,0},{2,3},{3,2},{4,5},{5,4},{6,7},{7,6},{8,9},{9,8},{10,11... | collective-permute-start | bytes 1990664 | tf_op jit(solution)/shard_map/ppermute | solution.py:772
  524.3 21.3 %collective-permute-start.33 = (bf16[2,144,1152]{2,1,0:T(8,128)(2,1)S(1)}, bf16[2,144,1152]{2,1,0:T(8,128)(2,1)S(1)}, u32[]{:S(2)}, u32[]{:S(2)}) collective-permute-start(bf16[2,144,1152]{2,1,0:T(8,128)(2,1)S(1)} %dynamic-slice_bitcast_fusion.2), channel_id=1, source_target_pairs={{0,2},{1,3},{2,0},{3,1},{4,6},{5,7},{6,4},{7,5},{8,10},{9,11},{10,... | collective-permute-start | bytes 1990664 | tf_op jit(solution)/shard_map/ppermute | solution.py:772
  568.0 23.8 %all-to-all-start.3 = ((bf16[4,3,144,288]{3,2,1,0:T(8,128)(2,1)}), bf16[4,3,144,288]{3,2,1,0:T(8,128)(2,1)}, u32[]{:S(2)}, u32[]{:S(2)}) async-start(bf16[4,3,144,288]{3,2,1,0:T(8,128)(2,1)} %shard_map.218), calls=%async_computation.3 | async-start | bytes 2654208 | tf_op jit(solution)/shard_map/all_to_all | solution.py:842
  572.3 76.4 %all-gather.22.cloned.1.call-start = ((), (), s32[]{:S(2)}) async-start(), calls=%async_computation.11 | async-start | bytes 2985984 | tf_op jit(solution)/shard_map/all_gather | solution.py:954
  626.8 21.9 %all-to-all-start.4 = ((bf16[4,3,144,288]{3,2,1,0:T(8,128)(2,1)}), bf16[4,3,144,288]{3,2,1,0:T(8,128)(2,1)}, u32[]{:S(2)}, u32[]{:S(2)}) async-start(bf16[4,3,144,288]{3,2,1,0:T(8,128)(2,1)} %shard_map.219), calls=%async_computation.4 | async-start | bytes 2654208 | tf_op jit(solution)/shard_map/all_to_all | solution.py:842
  657.0 21.1 %all-to-all-start.5 = ((bf16[4,3,144,288]{3,2,1,0:T(8,128)(2,1)}), bf16[4,3,144,288]{3,2,1,0:T(8,128)(2,1)}, u32[]{:S(2)}, u32[]{:S(2)}) async-start(bf16[4,3,144,288]{3,2,1,0:T(8,128)(2,1)} %shard_map.220), calls=%async_computation.5 | async-start | bytes 2654208 | tf_op jit(solution)/shard_map/all_to_all | solution.py:842
  (83 other events, 642.6 us)
Sparse Core Ops, SparseCore 0:
  34.1 106.8 all-gather.13
  144.6 105.3 all-gather.15
  297.2 76.4 all-gather.11
  479.1 43.4 all-gather.17
  524.6 32.7 all-gather.19
  594.5 41.7 all-gather.21

commit v17 on v16

--- a/solution.py
+++ b/solution.py
@@ -866,7 +866,7 @@
     total = rows.shape[-1]
     if ranks != group:
         blocks = gather_blocks(rows, group).reshape(group * total, total)
-        for _ in range(3):
+        for _ in range(4):
             (blocks,) = yield (blocks,)
         cuts = [[(0, index * total, total)] for index in range(group)]
         yield [blocks], cuts, [index * (total // 16) for index in range(group)], range(group)
@@ -882,12 +882,19 @@
     ]
     (own,) = yield (place([line, core_swap(line)], cuts, starts, total),)
     share = lax.dynamic_slice_in_dim(own, core * half, half, 0)
-    mine = yield tuple(rank_swap(share, bits) for bits in range(1, ranks))
-    parts, cuts, starts = [own], [[(0, 0, total)]], [at * (total // 16)]
-    for bits in range(1, ranks):
-        parts += [mine[bits - 1], core_swap(mine[bits - 1])]
-        cuts.append([(2 * bits - 1, 0, half), (2 * bits, 0, half)])
+    low, high = yield (rank_swap(share, 1), rank_swap(share, 2))
+    quarter = half // 2
+    low_other, high_other = core_swap(low), core_swap(high)
+    last = yield (rank_swap(high[:quarter], 1), rank_swap(low[quarter:], 2))
+    parts = [own, low, low_other, high, high_other, *last, *[core_swap(part) for part in last]]
+    cuts = [[(0, 0, total)], [(1, 0, half), (2, 0, half)], [(3, 0, half), (4, 0, half)]]
+    cuts.append([(5 + index, 0, quarter) for index in range(4)])
+    starts = [at * (total // 16)]
+    for bits in (1, 2):
         starts += [((at ^ bits) * 2 + side) * (half // 16) for side in (core, 1 - core)]
+    for side in (core, 1 - core):
+        first = ((at ^ 3) * 2 + side) * (half // 16)
+        starts += [first, first + quarter // 16]
     yield parts, cuts, starts, [at ^ bits for bits in range(ranks)]
 
 
@@ -1090,7 +1097,8 @@
         packed([mod_cols, bias_rows, left_cond], 8), "fsdp", axis=0, tiled=True
     )
     second_parts, one_parts = tie(second_parts, one_parts)
-    one_parts, attn_w = tie(one_steps.send(one_parts), attn_w)
+    roots = jnp.stack([narrow(left_roots[mod_count:]), narrow(right_roots[mod_count:])])
+    one_parts, attn_w, roots = tie(one_steps.send(one_parts), attn_w, roots)
     one_parts = one_steps.send(one_parts)
     second_parts = second_parts.reshape(ranks, -1)
     mods = second_parts[:, :mod_size].reshape(ranks, clip_count, mod_count, col_part)
@@ -1109,12 +1117,12 @@
         frames, frame_counts, stream, grad_out, mods, bias_table, attn_w
     )
     mlp_in, one_parts = tie(mlp_in, one_parts)
+    one_parts = one_steps.send(one_parts)
     one_w, hidden, slope = run_hidden(mlp_in, one_steps.send(one_parts), bias_table[4:8, None])
     one_w = one_w.reshape(group, width, width)
 
     two_steps = sum_blocks([hidden], [0] * group, d_branch, group)
     two_parts = next(two_steps)
-    roots = jnp.stack([narrow(left_roots[mod_count:]), narrow(right_roots[mod_count:])])
     hidden, two_parts, roots = tie(hidden, two_parts, roots)
     two_parts = two_steps.send(two_parts)
     root_rows = own_rows(roots.reshape(-1, group, row_part, col_part), group)
@@ -1214,25 +1222,22 @@
     to_rows, attn_parts = tie(to_rows, attn_parts)
     attn_parts = attn_steps.send(attn_parts)
     from_rows = lax.all_to_all(to_rows, "dp", 0, 0, tiled=True)
-    from_rows, two_parts, one_parts = tie(from_rows, two_parts, one_parts)
+    from_rows, attn_parts, two_parts, one_parts = tie(from_rows, attn_parts, two_parts, one_parts)
+    attn_parts = attn_steps.send(attn_parts)
     whole_two = two_steps.send(two_parts)
     one_parts = one_steps.send(one_parts)
-    from_rows, attn_parts, one_parts = tie(from_rows, attn_parts, one_parts)
-    attn_parts = attn_steps.send(attn_parts)
-    whole_one = one_steps.send(one_parts)
     bias_grad = jnp.sum(from_rows[:, mod_size:], axis=0)
     mod_grad_cols = from_rows[:, :mod_size].reshape(all_clips, mod_count, col_part)
     mod_grad = lax.all_gather(packed([mod_grad_cols], 8), "fsdp", axis=0, tiled=True)
-    mod_grad, attn_parts = tie(mod_grad, attn_parts)
+    mod_grad, attn_parts, one_parts = tie(mod_grad, attn_parts, one_parts)
     attn_parts = attn_steps.send(attn_parts)
+    whole_one = one_steps.send(one_parts)
     products_two = owned_step(whole_two, root_rows, right_wholes, 2, group)
     products_two, attn_parts = tie(products_two, attn_parts)
     attn_parts = attn_steps.send(attn_parts)
     back_two = shard_rows(products_two, group)
     products_one = owned_step(whole_one, root_rows, right_wholes, 1, group)
-    mod_grad, back_two, products_one, attn_parts = tie(
-        mod_grad, back_two, products_one, attn_parts
-    )
+    mod_grad, back_two, attn_parts = tie(mod_grad, back_two, attn_parts)
     whole_attn = attn_steps.send(attn_parts)
     back_one = shard_rows(products_one, group)
     mod_grad = mod_grad.reshape(ranks, -1)[:, : mod_grad_cols.size]

time: 708 us -> 695 us (0.982)
  waiting for transfers between devices: 224 us -> 213 us
  other arithmetic: 52.4 us -> 59.7 us
    all_to_all x3, waiting for transfers between devices: 22.1 us -> 11.1 us  [shard_rows(): moved = lax.all_to_all(split, 'fsdp', 0, 0, tiled=True)]
    all_to_all x1, waiting for transfers between devices: 6.68 us -> 16.9 us  [per_device(): from_rows = lax.all_to_all(to_rows, 'dp', 0, 0, tiled=True)]
    ppermute x21 -> x22, waiting for transfers between devices: 58.4 us -> 49.7 us  [rank_swap(): return lax.ppermute(array, 'fsdp', [(at, at ^ bits) for at in range(count)])]
    unnamed x135 -> x131, local copies, waits for them, and re-layouts: 24.9 us -> 18.8 us
    ppermute x21 -> x22, starting transfers between devices: 23.5 us -> 22.8 us  [rank_swap(): return lax.ppermute(array, 'fsdp', [(at, at ^ bits) for at in range(count)])]
  transfers between devices with their start and end apart: 49 -> 51, of which waited for: 21 -> 20; matrix products, arithmetic and copies ran while one was open for 10% -> 11% of each run, Pallas kernels for 28% -> 27%
where the time goes in v17:
time: 695 us; the launch traced here: 689 us
  Pallas kernels  215 us (31%)
  waiting for transfers between devices  213 us (31%)
  blocking collectives  61.1 us (9%)
  other arithmetic  59.7 us (9%)
  starting transfers between devices  57.7 us (8%)
  local copies, waits for them, and re-layouts  54.6 us (8%)
  between operations  15.7 us (2%)
  matrix products  13.1 us (2%)
    ppermute x6, waiting for transfers between devices, chip_swap(): lax.ppermute(array, 'dp', [(at, at ^ 2 * bits) for at in range(count)])  56.8 us
    pallas_call x6, Pallas kernels, run_halves(): pl.pallas_call(body, grid_spec=pltpu.PrefetchScalarGridSpec(num_scalar_pr...  55 us
    all_gather x2, waiting for transfers between devices, gather_blocks(): all_rows = lax.all_gather(rows, ('fsdp', 'dp'), axis=0, tiled=True)  52.1 us
    ppermute x22, waiting for transfers between devices, rank_swap(): return lax.ppermute(array, 'fsdp', [(at, at ^ bits) for at in range(count)])  49.7 us
    pallas_call x1, Pallas kernels, run_attention(): pl.pallas_call(functools.partial(attention_kernel, frames), grid=(clips,)...  41.2 us
    convert_element_type x21, other arithmetic, narrow(): return array.astype(jnp.bfloat16)  29.6 us
    pallas_call x1, Pallas kernels, run_attention_back(): pl.pallas_call(functools.partial(attention_back_kernel, frames), grid=(cl...  26.1 us
    pallas_call x3, Pallas kernels, owned_step(): pl.pallas_call(functools.partial(products_kernel, dp_count // 2), in_spec...  25.1 us
  transfers between devices with their start and end apart: 51, of which 20 were waited for; matrix products, arithmetic and copies ran while one was open for 11% of the time, Pallas kernels for 27%

profile of v17, /device:TPU:0, one launch (start us, length us, event | category | flops | bytes accessed | tf_op | source)
XLA Modules:
  0.0 689.1 jit_solution(7748959100634343941)
XLA Ops:
  17.2 14.7 %all_gather.30 = bf16[256,128]{1,0:T(8,128)(2,1)S(1)} all-gather(bf16[32,128]{1,0:T(8,128)(2,1)S(1)} %fusion.49), channel_id=1, replica_groups=mesh['dp'=8,'fsdp'=4] {'dp'}, dimensions={0}, use_global_device_ids=true | all-gather | bytes 73728 | tf_op jit(solution)/shard_map/all_gather | solution.py:1071
  37.0 4.9 all-to-all-start
  44.5 8.7 %all-to-all-done = f32[16,6,288]{2,1,0:T(8,128)S(1)} async-done(((f32[16,6,288]{2,1,0:T(8,128)}), f32[16,6,288]{2,1,0:T(8,128)S(1)}, u32[]{:S(2)}, u32[]{:S(2)}) %all-to-all-start) | async-done | bytes 110624 | tf_op jit(solution)/shard_map/all_to_all | solution.py:1089
  57.4 9.8 %all_gather.31 = f32[672,128]{1,0:T(8,128)S(1)} all-gather(f32[168,128]{1,0:T(8,128)S(1)} %pad_bitcast_fusion), channel_id=1, replica_groups=mesh['dp'=8,'fsdp'=4] {'fsdp'}, dimensions={0}, use_global_device_ids=true | all-gather | bytes 430080 | tf_op jit(solution)/shard_map/all_gather | solution.py:1096
  67.2 12.1 %collective-permute-done.4.refs_2_ = bf16[144,1152]{1,0:T(8,128)(2,1)S(1)} collective-permute-done((bf16[144,1152]{1,0:T(8,128)(2,1)S(1)}, bf16[144,1152]{1,0:T(8,128)(2,1)S(1)}, u32[]{:S(2)}, u32[]{:S(2)}) %collective-permute-start.4) | collective-permute-done | bytes 331808 | tf_op jit(solution)/shard_map/ppermute | solution.py:762
  89.0 52.0 %all-gather.14.cloned.1.call-done = bf16[1,4608,1152]{2,1,0:T(8,128)(2,1)} async-done(((bf16[1,144,1152]{2,1,0:T(8,128)(2,1)}), bf16[1,4608,1152]{2,1,0:T(8,128)(2,1)}) %all-gather.14.cloned.1.call-update) | async-done | bytes 10616848 | tf_op jit(solution)/shard_map/all_gather | solution.py:851
  146.6 41.2 %shard_map.206 = (bf16[512,1152]{1,0:T(8,128)(2,1)S(1)}, bf16[5,512,1152]{2,1,0:T(8,128)(2,1)}, bf16[512,1152]{1,0:T(8,128)(2,1)S(1)}, f32[512,1152]{1,0:T(8,128...) custom-call(s32[2]{0:T(128)S(1)} %copy-done.19, ...), custom_call_target="tpu_custom_call" | custom-call | flops 1024 | bytes 1024 | tf_op jit(solution)/shard_map/pallas_call | solution.py:216
  192.1 20.0 %collective-permute-done.11.refs_5_ = bf16[288,1152]{1,0:T(8,128)(2,1)S(1)} collective-permute-done((bf16[288,1152]{1,0:T(8,128)(2,1)S(1)}, bf16[288,1152]{1,0:T(8,128)(2,1)S(1)}, u32[]{:S(2)}, u32[]{:S(2)}) %collective-permute-start.11) | collective-permute-done | bytes 663584 | tf_op jit(solution)/shard_map/ppermute | solution.py:772
  217.2 13.9 %shard_map.207 = (bf16[4608,1152]{1,0:T(8,128)(2,1)}, bf16[4,512,1152]{2,1,0:T(8,128)(2,1)}, bf16[4,512,1152]{2,1,0:T(8,128)(2,1)}) custom-call(s32[4]{0:T(128)S(1)} %get-tuple-element.266.order, s32[9]{0:T(128)S(1)} %stack.97.starts, bf16[512,1152]{1,0:T(8,128)(2,1)S(1)} %get-tuple-element.132.mlp_in.refs_0_, f32[4,1,1152]{2,1,0:T(1,128)S(1)} %copy.92.bias, ...), custom_call_target="tpu_custom_call" | custom-call | flops 1024 | bytes 1024 | tf_op jit(solution)/shard_map/pallas_call | solution.py:324
  231.1 9.0 %shard_map.208 = bf16[4,576,1152]{2,1,0:T(8,128)(2,1)} custom-call(s32[4]{0:T(128)S(1)} %get-tuple-element.267.order, s32[1]{0:T(128)} %bitcast.45.side, s32[16]{0:T(128)S(1)} %stack.121.table, bf16[4,512,1152]{2,1,0:T(8,128)(2,1)} %get-tuple-element.138.refs_0_.hidden, bf16[512,1152]{1,0:T(8,128)(2,1)S(1)} %copy-done.2), custom_call_target="tpu_custom_call" | custom-call | flops 1024 | bytes 1024 | tf_op jit(solution)/shard_map/pallas_call | solution.py:728
  246.4 21.6 %shard_map.209 = (bf16[4,512,1152]{2,1,0:T(8,128)(2,1)}, f32[4,1,1152]{2,1,0:T(1,128)S(1)}, bf16[512,1152]{1,0:T(8,128)(2,1)}, f32[2,1,1152]{2,1,0:T(1,128)S(1)}) custom-call(s32[4]{0:T(128)S(1)} %iota.6.order, s32[4]{0:T(128)S(1)} %iota_multiply_fusion.starts, s32[2]{0:T(128)S(1)} %copy-done.19, bf16[4,512,1152]{2,1,0:T(8,128)(2,1)} %get-tuple-element.138.refs_0_.hidden, ...), custom_call_target="tpu_custom_call" | custom-call | flops 1024 | bytes 1024 | tf_op jit(solution)/shard_map/pallas_call | solution.py:404
  268.1 5.6 collective-permute-done.16
  283.8 10.1 %shard_map.210 = (bf16[2,288,1152]{2,1,0:T(8,128)(2,1)S(1)}, bf16[2,288,1152]{2,1,0:T(8,128)(2,1)}, bf16[2,288,1152]{2,1,0:T(8,128)(2,1)}, bf16[2,288,1152]{2,1,0:T(8,128)(2,1)}) custom-call(s32[4]{0:T(128)S(1)} %get-tuple-element.267.order, s32[1]{0:T(128)} %bitcast.57.side, s32[16]{0:T(128)S(1)} %stack.121.table, ...), custom_call_target="tpu_custom_call" | custom-call | flops 1024 | bytes 1024 | tf_op jit(solution)/shard_map/pallas_call | solution.py:728
  293.9 8.5 %shard_map.211 = bf16[4,576,1152]{2,1,0:T(8,128)(2,1)} custom-call(s32[4]{0:T(128)S(1)} %get-tuple-element.267.order, s32[1]{0:T(128)} %bitcast.45.side, s32[16]{0:T(128)S(1)} %stack.121.table, bf16[512,1152]{1,0:T(8,128)(2,1)S(1)} %get-tuple-element.132.mlp_in.refs_0_, bf16[4,512,1152]{2,1,0:T(8,128)(2,1)} %get-tuple-element.155.refs_1_.d_pre), custom_call_target="tpu_custom_call" | custom-call | flops 1024 | bytes 1024 | tf_op jit(solution)/shard_map/pallas_call | solution.py:728
  305.5 15.7 %shard_map.212 = (f32[512,1152]{1,0:T(8,128)}, bf16[512,1152]{1,0:T(8,128)(2,1)S(1)}, f32[2,4,1152]{2,1,0:T(4,128)S(1)}) custom-call(s32[2]{0:T(128)S(1)} %copy-done.19, bf16[4,512,1152]{2,1,0:T(8,128)(2,1)} %get-tuple-element.155.refs_1_.d_pre, bf16[4,1152,1152]{2,1,0:T(8,128)(2,1)} %bitcast.251, f32[2,6,1152]{2,1,0:T(8,128)S(1)} %broadcast_add_fusion.mods, ...), custom_call_target="tpu_custom_call" | custom-call | flops 1024 | bytes 1024 | tf_op jit(solution)/shard_map/pallas_call | solution.py:496
  321.3 8.9 %shard_map.213 = (bf16[2,288,1152]{2,1,0:T(8,128)(2,1)S(1)}, bf16[2,288,1152]{2,1,0:T(8,128)(2,1)S(1)}, bf16[2,288,1152]{2,1,0:T(8,128)(2,1)}, bf16[2,288,1152]{2,1,0:T(8,128)(2,1)}) custom-call(s32[4]{0:T(128)S(1)} %get-tuple-element.267.order, s32[1]{0:T(128)} %bitcast.57.side, s32[16]{0:T(128)S(1)} %stack.121.table, ...), custom_call_target="tpu_custom_call" | custom-call | flops 1024 | bytes 1024 | tf_op jit(solution)/shard_map/pallas_call | solution.py:728
  343.0 26.1 %shard_map.214 = (bf16[4,512,1152]{2,1,0:T(8,128)(2,1)}, f32[2,3,1152]{2,1,0:T(4,128)S(1)}) custom-call(s32[2]{0:T(128)S(1)} %copy-done.19, bf16[512,1152]{1,0:T(8,128)(2,1)S(1)} %get-tuple-element.166.d_proj, bf16[5,512,1152]{2,1,0:T(8,128)(2,1)} %get-tuple-element.167.parts, bf16[4,1152,1152]{2,1,0:T(8,128)(2,1)} %bitcast.248), custom_call_target="tpu_custom_call" | custom-call | flops 1024 | bytes 1024 | tf_op jit(solution)/shard_map/pallas_call | solution.py:563
  369.2 14.3 %collective-permute-done.22 = bf16[2,144,1152]{2,1,0:T(8,128)(2,1)S(1)} collective-permute-done((bf16[2,144,1152]{2,1,0:T(8,128)(2,1)S(1)}, bf16[2,144,1152]{2,1,0:T(8,128)(2,1)S(1)}, u32[]{:S(2)}, u32[]{:S(2)}) %collective-permute-start.22) | collective-permute-done | bytes 663584 | tf_op jit(solution)/shard_map/ppermute | solution.py:772
  386.7 8.9 %shard_map.215 = bf16[4,576,1152]{2,1,0:T(8,128)(2,1)} custom-call(s32[4]{0:T(128)S(1)} %get-tuple-element.267.order, s32[1]{0:T(128)} %bitcast.45.side, s32[16]{0:T(128)S(1)} %stack.121.table, bf16[512,1152]{1,0:T(8,128)(2,1)S(1)} %copy-done.7, bf16[512,1152]{1,0:T(8,128)(2,1)S(1)} %copy-done.10, bf16[4,512,1152]{2,1,0:T(8,128)(2,1)} %get-tuple-element.179.refs_2_.d_qkv), custom_call_target="tpu_custom_call" | custom-call | flops 1024 | bytes 1024 | tf_op jit(solution)/shard_map/pallas_call | solution.py:728
  407.1 11.5 %shard_map.216 = (bf16[512,1152]{1,0:T(8,128)(2,1)}, f32[2,2,1152]{2,1,0:T(2,128)S(1)}) custom-call(bf16[4,512,1152]{2,1,0:T(8,128)(2,1)} %get-tuple-element.179.refs_2_.d_qkv, bf16[4,1152,1152]{2,1,0:T(8,128)(2,1)} %bitcast.249, f32[2,6,1152]{2,1,0:T(8,128)S(1)} %broadcast_add_fusion.mods, bf16[512,1152]{1,0:T(8,128)(2,1)S(1)} %bitcast.246, ...), custom_call_target="tpu_custom_call" | custom-call | flops 1024 | bytes 1024 | tf_op jit(solution)/shard_map/pallas_call | solution.py:623
  438.8 9.6 %shard_map.217 = (bf16[2,288,1152]{2,1,0:T(8,128)(2,1)S(1)}, bf16[2,288,1152]{2,1,0:T(8,128)(2,1)}, bf16[2,288,1152]{2,1,0:T(8,128)(2,1)}, bf16[2,288,1152]{2,1,0:T(8,128)(2,1)}) custom-call(s32[4]{0:T(128)S(1)} %get-tuple-element.267.order, s32[1]{0:T(128)} %bitcast.57.side, s32[16]{0:T(128)S(1)} %stack.121.table, bf16[512,1152]{1,0:T(8,128)(2,1)S(1)} %copy-done.8, ...), custom_call_target="tpu_custom_call" | custom-call | flops 1024 | bytes 1024 | tf_op jit(solution)/shard_map/pallas_call | solution.py:728
  461.5 16.9 %all-to-all-done.2 = f32[8,1,3960]{2,1,0:T(1,128)S(1)} async-done(((f32[8,1,3960]{2,1,0:T(1,128)}), f32[8,1,3960]{2,1,0:T(1,128)S(1)}, u32[]{:S(2)}, u32[]{:S(2)}) %all-to-all-start.2) | async-done | bytes 126752 | tf_op jit(solution)/shard_map/all_to_all | solution.py:1224
  494.5 16.2 %all_gather.35 = f32[864,128]{1,0:T(8,128)} all-gather(f32[216,128]{1,0:T(8,128)} %reshape.302), channel_id=1, replica_groups=mesh['dp'=8,'fsdp'=4] {'fsdp'}, dimensions={0}, use_global_device_ids=true | all-gather | bytes 552960 | tf_op jit(solution)/shard_map/all_gather | solution.py:1231
  510.7 15.4 %collective-permute-done.36 = bf16[1,144,1152]{2,1,0:T(8,128)(2,1)} collective-permute-done((bf16[1,144,1152]{2,1,0:T(8,128)(2,1)}, bf16[1,144,1152]{2,1,0:T(8,128)(2,1)}, u32[]{:S(2)}, u32[]{:S(2)}) %collective-permute-start.36) | collective-permute-done | bytes 331808 | tf_op jit(solution)/shard_map/ppermute | solution.py:767
  531.8 8.3 %shard_map.218 = bf16[4,3,144,288]{3,2,1,0:T(8,128)(2,1)} custom-call(s32[1]{0:T(128)} %bitcast.85.at, bf16[1152,1152]{1,0:T(8,128)(2,1)} %bitcast.274, bf16[6,144,1152]{2,1,0:T(8,128)(2,1)S(1)} %concatenate.46.left_root, bf16[3,1152,1152]{2,1,0:T(8,128)(2,1)} %all-gather.12.cloned.1.call-done.right_root), custom_call_target="tpu_custom_call" | custom-call | flops 1024 | bytes 1024 | tf_op jit(solution)/shard_map/pallas_call | solution.py:1008
  540.1 28.1 %collective-permute-done.37 = bf16[2,144,1152]{2,1,0:T(8,128)(2,1)} collective-permute-done((bf16[2,144,1152]{2,1,0:T(8,128)(2,1)}, bf16[2,144,1152]{2,1,0:T(8,128)(2,1)}, u32[]{:S(2)}, u32[]{:S(2)}) %collective-permute-start.37) | collective-permute-done | bytes 663584 | tf_op jit(solution)/shard_map/ppermute | solution.py:767
  574.9 10.2 %collective-permute-done.38 = bf16[1,144,1152]{2,1,0:T(8,128)(2,1)S(1)} collective-permute-done((bf16[1,144,1152]{2,1,0:T(8,128)(2,1)S(1)}, bf16[1,144,1152]{2,1,0:T(8,128)(2,1)S(1)}, u32[]{:S(2)}, u32[]{:S(2)}) %collective-permute-start.38) | collective-permute-done | bytes 331808 | tf_op jit(solution)/shard_map/ppermute | solution.py:767
  590.6 8.5 %shard_map.219 = bf16[4,3,144,288]{3,2,1,0:T(8,128)(2,1)} custom-call(s32[1]{0:T(128)} %bitcast.85.at, bf16[1152,1152]{1,0:T(8,128)(2,1)} %bitcast.273, bf16[6,144,1152]{2,1,0:T(8,128)(2,1)S(1)} %concatenate.46.left_root, bf16[3,1152,1152]{2,1,0:T(8,128)(2,1)} %all-gather.12.cloned.1.call-done.right_root), custom_call_target="tpu_custom_call" | custom-call | flops 1024 | bytes 1024 | tf_op jit(solution)/shard_map/pallas_call | solution.py:1008
  607.2 20.4 %all_gather.39 = f32[1728,128]{1,0:T(8,128)} all-gather(f32[216,128]{1,0:T(8,128)S(1)} %reshape.314), channel_id=1, replica_groups=mesh['dp'=8,'fsdp'=4] {'dp'}, dimensions={0}, use_global_device_ids=true | all-gather | bytes 995328 | tf_op jit(solution)/shard_map/all_gather | solution.py:1260
  635.4 8.3 %shard_map.220 = bf16[4,3,144,288]{3,2,1,0:T(8,128)(2,1)} custom-call(s32[1]{0:T(128)} %bitcast.85.at, bf16[1152,1152]{1,0:T(8,128)(2,1)} %bitcast.275, bf16[6,144,1152]{2,1,0:T(8,128)(2,1)S(1)} %concatenate.46.left_root, bf16[3,1152,1152]{2,1,0:T(8,128)(2,1)} %all-gather.12.cloned.1.call-done.right_root), custom_call_target="tpu_custom_call" | custom-call | flops 1024 | bytes 1024 | tf_op jit(solution)/shard_map/pallas_call | solution.py:1008
  654.7 11.0 %all-to-all-done.5 = bf16[4,3,144,288]{3,2,1,0:T(8,128)(2,1)} async-done(((bf16[4,3,144,288]{3,2,1,0:T(8,128)(2,1)}), bf16[4,3,144,288]{3,2,1,0:T(8,128)(2,1)}, u32[]{:S(2)}, u32[]{:S(2)}) %all-to-all-start.5) | async-done | bytes 995360 | tf_op jit(solution)/shard_map/all_to_all | solution.py:842
  668.3 7.2 %fusion.55 = (bf16[18,144,288]{2,1,0:T(8,128)(2,1)}, f32[18,144,288]{2,1,0:T(8,128)}, f32[18,144,288]{2,1,0:T(8,128)}) fusion(f32[18,144,288]{2,1,0:T(8,128)S(1)} %copy-done.20, f32[4,144,288]{2,1,0:T(8,128)} %get-tuple-element.246, f32[4,144,288]{2,1,0:T(8,128)} %get-tuple-element.243, f32[4,144,288]{2,1,0:T(8,128)S(1)} %get-tuple-element.240, ...), kind=kLoop, calls=%fused_computation.141 | loop fusion | flops 5971968 | bytes 16422912 | tf_op jit(solution)/shard_map/convert_element_type | solution.py:1275
  (376 shorter events, 195.5 us)
Async XLA Ops:
  7.2 133.8 %all-gather.14.cloned.1.call-start = ((), (), s32[]{:S(2)}) async-start(), calls=%async_computation.7 | async-start | bytes 10948608 | tf_op jit(solution)/shard_map/all_gather | solution.py:851
  33.9 211.2 %all-gather.16.cloned.1.call-start = ((), (), s32[]{:S(2)}) async-start(), calls=%async_computation.8 | async-start | bytes 10948608 | tf_op jit(solution)/shard_map/all_gather | solution.py:851
  41.9 343.5 %all-gather.12.cloned.1.call-start = ((), (), s32[]{:S(2)}) async-start(), calls=%async_computation.6 | async-start | bytes 8957952 | tf_op jit(solution)/shard_map/all_gather | solution.py:907
  53.3 26.0 %collective-permute-start.4 = (bf16[144,1152]{1,0:T(8,128)(2,1)S(1)}, bf16[144,1152]{1,0:T(8,128)(2,1)S(1)}, u32[]{:S(2)}, u32[]{:S(2)}) collective-permute-start(bf16[144,1152]{1,0:T(8,128)(2,1)S(1)} %get-tuple-element.124.refs_0_), channel_id=1, source_target_pairs={{0,16},{4,20},{8,24},{12,28},{16,0},{20,4},{24,8},{28,12},{1,17},{... | collective-permute-start | bytes 995336 | tf_op jit(solution)/shard_map/ppermute | solution.py:762
  55.4 23.9 %collective-permute-start.5 = (bf16[144,1152]{1,0:T(8,128)(2,1)S(1)}, bf16[144,1152]{1,0:T(8,128)(2,1)S(1)}, u32[]{:S(2)}, u32[]{:S(2)}) collective-permute-start(bf16[144,1152]{1,0:T(8,128)(2,1)S(1)} %get-tuple-element.124.refs_0_), channel_id=1, source_target_pairs={{0,24},{4,28},{8,0},{12,4},{16,8},{20,12},{24,16},{28,20},{1,25},{... | collective-permute-start | bytes 995336 | tf_op jit(solution)/shard_map/ppermute | solution.py:762
  143.5 44.4 %collective-permute-start.7 = (bf16[576,1152]{1,0:T(8,128)(2,1)}, bf16[576,1152]{1,0:T(8,128)(2,1)S(1)}, u32[]{:S(2)}, u32[]{:S(2)}) collective-permute-start(bf16[576,1152]{1,0:T(8,128)(2,1)} %constant_dynamic-slice_fusion.3), channel_id=1, source_target_pairs={{0,1},{1,0},{2,3},{3,2},{4,5},{5,4},{6,7},{7,6},{8,9},{9,8},{10,11... | collective-permute-start | bytes 3981320 | tf_op jit(solution)/shard_map/ppermute | solution.py:772
  144.9 43.0 %collective-permute-start.8 = (bf16[576,1152]{1,0:T(8,128)(2,1)}, bf16[576,1152]{1,0:T(8,128)(2,1)}, u32[]{:S(2)}, u32[]{:S(2)}) collective-permute-start(bf16[576,1152]{1,0:T(8,128)(2,1)} %constant_dynamic-slice_fusion.3), channel_id=1, source_target_pairs={{0,2},{1,3},{2,0},{3,1},{4,6},{5,7},{6,4},{7,5},{8,10},{9,11},{10,... | collective-permute-start | bytes 3981320 | tf_op jit(solution)/shard_map/ppermute | solution.py:772
  191.2 23.8 %collective-permute-start.12 = (bf16[288,1152]{1,0:T(8,128)(2,1)S(1)}, bf16[288,1152]{1,0:T(8,128)(2,1)S(1)}, u32[]{:S(2)}, u32[]{:S(2)}) collective-permute-start(bf16[288,1152]{1,0:T(8,128)(2,1)S(1)} %slice.142), channel_id=1, source_target_pairs={{0,2},{1,3},{2,0},{3,1},{4,6},{5,7},{6,4},{7,5},{8,10},{9,11},{10,... | collective-permute-start | bytes 1990664 | tf_op jit(solution)/shard_map/ppermute | solution.py:772
  191.6 25.6 %collective-permute-start.10 = (bf16[576,1152]{1,0:T(8,128)(2,1)}, bf16[576,1152]{1,0:T(8,128)(2,1)}, u32[]{:S(2)}, u32[]{:S(2)}) collective-permute-start(bf16[576,1152]{1,0:T(8,128)(2,1)} %collective-permute-done.8.refs_3_), channel_id=1, source_target_pairs={{0,4},{4,0},{8,12},{12,8},{16,20},{20,16},{24,28},{28,24},{1,5},{5... | collective-permute-start | bytes 3981320 | tf_op jit(solution)/shard_map/ppermute | solution.py:757
  191.6 25.6 %collective-permute-start.9 = (bf16[576,1152]{1,0:T(8,128)(2,1)}, bf16[576,1152]{1,0:T(8,128)(2,1)}, u32[]{:S(2)}, u32[]{:S(2)}) collective-permute-start(bf16[576,1152]{1,0:T(8,128)(2,1)} %copy-done.41), channel_id=1, source_target_pairs={{0,4},{4,0},{8,12},{12,8},{16,20},{20,16},{24,28},{28,24},{1,5},{5... | collective-permute-start | bytes 3981320 | tf_op jit(solution)/shard_map/ppermute | solution.py:757
  240.2 41.2 %collective-permute-start.18 = (bf16[4,576,1152]{2,1,0:T(8,128)(2,1)}, bf16[4,576,1152]{2,1,0:T(8,128)(2,1)}, u32[]{:S(2)}, u32[]{:S(2)}) collective-permute-start(bf16[4,576,1152]{2,1,0:T(8,128)(2,1)} %shard_map.208), channel_id=1, source_target_pairs={{0,4},{4,0},{8,12},{12,8},{16,20},{20,16},{24,28},{28,24},{1,5},{5... | collective-permute-start | bytes 15925256 | tf_op jit(solution)/shard_map/ppermute | solution.py:757
  241.6 26.5 %collective-permute-start.15 = (bf16[6,144,288]{2,1,0:T(8,128)(2,1)}, bf16[6,144,288]{2,1,0:T(8,128)(2,1)}, u32[]{:S(2)}, u32[]{:S(2)}) collective-permute-start(bf16[6,144,288]{2,1,0:T(8,128)(2,1)} %get-tuple-element.238), channel_id=1, source_target_pairs={{0,1},{1,0},{2,3},{3,2},{4,5},{5,4},{6,7},{7,6},{8,9},{9,8},{10,11... | collective-permute-start | bytes 1493000 | tf_op jit(solution)/shard_map/ppermute | solution.py:772
  242.1 31.6 %collective-permute-start.16 = (bf16[6,144,288]{2,1,0:T(8,128)(2,1)}, bf16[6,144,288]{2,1,0:T(8,128)(2,1)}, u32[]{:S(2)}, u32[]{:S(2)}) collective-permute-start(bf16[6,144,288]{2,1,0:T(8,128)(2,1)} %get-tuple-element.237), channel_id=1, source_target_pairs={{0,2},{1,3},{2,0},{3,1},{4,6},{5,7},{6,4},{7,5},{8,10},{9,11},{10,... | collective-permute-start | bytes 1493000 | tf_op jit(solution)/shard_map/ppermute | solution.py:772
  243.5 30.2 %collective-permute-start.17 = (bf16[6,144,288]{2,1,0:T(8,128)(2,1)}, bf16[6,144,288]{2,1,0:T(8,128)(2,1)}, u32[]{:S(2)}, u32[]{:S(2)}) collective-permute-start(bf16[6,144,288]{2,1,0:T(8,128)(2,1)} %get-tuple-element.236), channel_id=1, source_target_pairs={{0,3},{1,2},{2,1},{3,0},{4,7},{5,6},{6,5},{7,4},{8,11},{9,10},{10,... | collective-permute-start | bytes 1493000 | tf_op jit(solution)/shard_map/ppermute | solution.py:772
  302.3 31.9 %collective-permute-start.20 = (bf16[2,288,1152]{2,1,0:T(8,128)(2,1)}, bf16[2,288,1152]{2,1,0:T(8,128)(2,1)}, u32[]{:S(2)}, u32[]{:S(2)}) collective-permute-start(bf16[2,288,1152]{2,1,0:T(8,128)(2,1)} %get-tuple-element.164), channel_id=1, source_target_pairs={{0,1},{1,0},{2,3},{3,2},{4,5},{5,4},{6,7},{7,6},{8,9},{9,8},{10,11... | collective-permute-start | bytes 3981320 | tf_op jit(solution)/shard_map/ppermute | solution.py:772
  303.8 31.6 %collective-permute-start.21 = (bf16[2,288,1152]{2,1,0:T(8,128)(2,1)}, bf16[2,288,1152]{2,1,0:T(8,128)(2,1)}, u32[]{:S(2)}, u32[]{:S(2)}) collective-permute-start(bf16[2,288,1152]{2,1,0:T(8,128)(2,1)} %get-tuple-element.165), channel_id=1, source_target_pairs={{0,2},{1,3},{2,0},{3,1},{4,6},{5,7},{6,4},{7,5},{8,10},{9,11},{10,... | collective-permute-start | bytes 3981320 | tf_op jit(solution)/shard_map/ppermute | solution.py:772
  337.1 32.0 %collective-permute-start.23 = (bf16[2,144,1152]{2,1,0:T(8,128)(2,1)S(1)}, bf16[2,144,1152]{2,1,0:T(8,128)(2,1)S(1)}, u32[]{:S(2)}, u32[]{:S(2)}) collective-permute-start(bf16[2,144,1152]{2,1,0:T(8,128)(2,1)S(1)} %dynamic-slice_bitcast_fusion.7), channel_id=1, source_target_pairs={{0,1},{1,0},{2,3},{3,2},{4,5},{5,4},{6,7},{7,6},{8,9},{9,8},{10,11... | collective-permute-start | bytes 1990664 | tf_op jit(solution)/shard_map/ppermute | solution.py:772
  337.8 45.8 %collective-permute-start.24 = (bf16[2,288,1152]{2,1,0:T(8,128)(2,1)S(1)}, bf16[2,288,1152]{2,1,0:T(8,128)(2,1)S(1)}, u32[]{:S(2)}, u32[]{:S(2)}) collective-permute-start(bf16[2,288,1152]{2,1,0:T(8,128)(2,1)S(1)} %get-tuple-element.173), channel_id=1, source_target_pairs={{0,1},{1,0},{2,3},{3,2},{4,5},{5,4},{6,7},{7,6},{8,9},{9,8},{10,11... | collective-permute-start | bytes 3981320 | tf_op jit(solution)/shard_map/ppermute | solution.py:772
  339.2 46.2 %collective-permute-start.25 = (bf16[2,288,1152]{2,1,0:T(8,128)(2,1)}, bf16[2,288,1152]{2,1,0:T(8,128)(2,1)}, u32[]{:S(2)}, u32[]{:S(2)}) collective-permute-start(bf16[2,288,1152]{2,1,0:T(8,128)(2,1)} %get-tuple-element.174), channel_id=1, source_target_pairs={{0,2},{1,3},{2,0},{3,1},{4,6},{5,7},{6,4},{7,5},{8,10},{9,11},{10,... | collective-permute-start | bytes 3981320 | tf_op jit(solution)/shard_map/ppermute | solution.py:772
  341.4 42.1 %collective-permute-start.22 = (bf16[2,144,1152]{2,1,0:T(8,128)(2,1)S(1)}, bf16[2,144,1152]{2,1,0:T(8,128)(2,1)S(1)}, u32[]{:S(2)}, u32[]{:S(2)}) collective-permute-start(bf16[2,144,1152]{2,1,0:T(8,128)(2,1)S(1)} %dynamic-slice_bitcast_fusion.8), channel_id=1, source_target_pairs={{0,2},{1,3},{2,0},{3,1},{4,6},{5,7},{6,4},{7,5},{8,10},{9,11},{10,... | collective-permute-start | bytes 1990664 | tf_op jit(solution)/shard_map/ppermute | solution.py:772
  395.6 26.1 %collective-permute-start.26 = (bf16[4,576,1152]{2,1,0:T(8,128)(2,1)}, bf16[4,576,1152]{2,1,0:T(8,128)(2,1)}, u32[]{:S(2)}, u32[]{:S(2)}) collective-permute-start(bf16[4,576,1152]{2,1,0:T(8,128)(2,1)} %shard_map.215), channel_id=1, source_target_pairs={{0,4},{4,0},{8,12},{12,8},{16,20},{20,16},{24,28},{28,24},{1,5},{5... | collective-permute-start | bytes 15925256 | tf_op jit(solution)/shard_map/ppermute | solution.py:757
  449.6 30.5 %collective-permute-start.30 = (bf16[2,288,1152]{2,1,0:T(8,128)(2,1)}, bf16[2,288,1152]{2,1,0:T(8,128)(2,1)}, u32[]{:S(2)}, u32[]{:S(2)}) collective-permute-start(bf16[2,288,1152]{2,1,0:T(8,128)(2,1)} %get-tuple-element.202), channel_id=1, source_target_pairs={{0,1},{1,0},{2,3},{3,2},{4,5},{5,4},{6,7},{7,6},{8,9},{9,8},{10,11... | collective-permute-start | bytes 3981320 | tf_op jit(solution)/shard_map/ppermute | solution.py:772
  450.5 30.2 %collective-permute-start.31 = (bf16[2,288,1152]{2,1,0:T(8,128)(2,1)}, bf16[2,288,1152]{2,1,0:T(8,128)(2,1)}, u32[]{:S(2)}, u32[]{:S(2)}) collective-permute-start(bf16[2,288,1152]{2,1,0:T(8,128)(2,1)} %get-tuple-element.203), channel_id=1, source_target_pairs={{0,2},{1,3},{2,0},{3,1},{4,6},{5,7},{6,4},{7,5},{8,10},{9,11},{10,... | collective-permute-start | bytes 3981320 | tf_op jit(solution)/shard_map/ppermute | solution.py:772
  452.9 26.3 %collective-permute-start.33 = (bf16[2,144,1152]{2,1,0:T(8,128)(2,1)}, bf16[2,144,1152]{2,1,0:T(8,128)(2,1)}, u32[]{:S(2)}, u32[]{:S(2)}) collective-permute-start(bf16[2,144,1152]{2,1,0:T(8,128)(2,1)} %dynamic-slice_bitcast_fusion.3), channel_id=1, source_target_pairs={{0,8},{4,12},{8,0},{12,4},{16,24},{20,28},{24,16},{28,20},{1,9},{5... | collective-permute-start | bytes 1990664 | tf_op jit(solution)/shard_map/ppermute | solution.py:767
  461.5 70.4 %all-gather.18.cloned.1.call-start = ((), (), s32[]{:S(2)}) async-start(), calls=%async_computation.9 | async-start | bytes 2985984 | tf_op jit(solution)/shard_map/all_gather | solution.py:961
  482.5 108.1 %all-gather.22.cloned.1.call-start = ((), (), s32[]{:S(2)}) async-start(), calls=%async_computation.11 | async-start | bytes 2985984 | tf_op jit(solution)/shard_map/all_gather | solution.py:961
  485.5 40.6 %collective-permute-start.35 = (bf16[2,144,1152]{2,1,0:T(8,128)(2,1)}, bf16[2,144,1152]{2,1,0:T(8,128)(2,1)}, u32[]{:S(2)}, u32[]{:S(2)}) collective-permute-start(bf16[2,144,1152]{2,1,0:T(8,128)(2,1)} %dynamic-slice_bitcast_fusion.1), channel_id=1, source_target_pairs={{0,1},{1,0},{2,3},{3,2},{4,5},{5,4},{6,7},{7,6},{8,9},{9,8},{10,11... | collective-permute-start | bytes 1990664 | tf_op jit(solution)/shard_map/ppermute | solution.py:772
  489.3 36.9 %collective-permute-start.34 = (bf16[2,144,1152]{2,1,0:T(8,128)(2,1)}, bf16[2,144,1152]{2,1,0:T(8,128)(2,1)}, u32[]{:S(2)}, u32[]{:S(2)}) collective-permute-start(bf16[2,144,1152]{2,1,0:T(8,128)(2,1)} %dynamic-slice_bitcast_fusion.2), channel_id=1, source_target_pairs={{0,2},{1,3},{2,0},{3,1},{4,6},{5,7},{6,4},{7,5},{8,10},{9,11},{10,... | collective-permute-start | bytes 1990664 | tf_op jit(solution)/shard_map/ppermute | solution.py:772
  492.6 33.5 %collective-permute-start.36 = (bf16[1,144,1152]{2,1,0:T(8,128)(2,1)}, bf16[1,144,1152]{2,1,0:T(8,128)(2,1)}, u32[]{:S(2)}, u32[]{:S(2)}) collective-permute-start(bf16[1,144,1152]{2,1,0:T(8,128)(2,1)} %constant_dynamic-slice_fusion.1), channel_id=1, source_target_pairs={{0,16},{4,20},{8,24},{12,28},{16,0},{20,4},{24,8},{28,12},{1,17},{... | collective-permute-start | bytes 995336 | tf_op jit(solution)/shard_map/ppermute | solution.py:767
  531.8 36.5 %collective-permute-start.37 = (bf16[2,144,1152]{2,1,0:T(8,128)(2,1)}, bf16[2,144,1152]{2,1,0:T(8,128)(2,1)}, u32[]{:S(2)}, u32[]{:S(2)}) collective-permute-start(bf16[2,144,1152]{2,1,0:T(8,128)(2,1)} %dynamic-slice_bitcast_fusion), channel_id=1, source_target_pairs={{0,8},{4,12},{8,0},{12,4},{16,24},{20,28},{24,16},{28,20},{1,9},{5... | collective-permute-start | bytes 1990664 | tf_op jit(solution)/shard_map/ppermute | solution.py:767
  572.6 62.8 %all-gather.20.cloned.1.call-start = ((), (), s32[]{:S(2)}) async-start(), calls=%async_computation.10 | async-start | bytes 2985984 | tf_op jit(solution)/shard_map/all_gather | solution.py:961
  599.1 36.2 %all-to-all-start.4 = ((bf16[4,3,144,288]{3,2,1,0:T(8,128)(2,1)}), bf16[4,3,144,288]{3,2,1,0:T(8,128)(2,1)}, u32[]{:S(2)}, u32[]{:S(2)}) async-start(bf16[4,3,144,288]{3,2,1,0:T(8,128)(2,1)} %shard_map.219), calls=%async_computation.4 | async-start | bytes 2654208 | tf_op jit(solution)/shard_map/all_to_all | solution.py:842
  (83 other events, 643.9 us)
Sparse Core Ops, SparseCore 0:
  34.1 106.8 all-gather.13
  144.6 96.4 all-gather.15
  282.6 76.5 all-gather.11
  482.6 46.5 all-gather.17
  531.3 40.5 all-gather.21
  587.0 39.7 all-gather.19

commit v18 on v17

--- a/solution.py
+++ b/solution.py
@@ -1209,7 +1209,8 @@
         axis=1,
     )
     rank_sums = lax.all_to_all(to_ranks, "fsdp", 0, 0, tiled=True)
-    rank_sums, attn_parts = tie(rank_sums, attn_parts)
+    rank_sums, attn_parts, two_parts = tie(rank_sums, attn_parts, two_parts)
+    whole_two = two_steps.send(two_parts)
     attn_parts = attn_steps.send(attn_parts)
     rank_sums = jnp.sum(rank_sums, axis=0)
     to_rows = jnp.concatenate(
@@ -1219,19 +1220,18 @@
         ],
         axis=1,
     )
-    to_rows, attn_parts = tie(to_rows, attn_parts)
+    to_rows, attn_parts, one_parts = tie(to_rows, attn_parts, one_parts)
     attn_parts = attn_steps.send(attn_parts)
+    one_parts = one_steps.send(one_parts)
     from_rows = lax.all_to_all(to_rows, "dp", 0, 0, tiled=True)
-    from_rows, attn_parts, two_parts, one_parts = tie(from_rows, attn_parts, two_parts, one_parts)
+    from_rows, attn_parts, one_parts = tie(from_rows, attn_parts, one_parts)
     attn_parts = attn_steps.send(attn_parts)
-    whole_two = two_steps.send(two_parts)
-    one_parts = one_steps.send(one_parts)
+    whole_one = one_steps.send(one_parts)
     bias_grad = jnp.sum(from_rows[:, mod_size:], axis=0)
     mod_grad_cols = from_rows[:, :mod_size].reshape(all_clips, mod_count, col_part)
     mod_grad = lax.all_gather(packed([mod_grad_cols], 8), "fsdp", axis=0, tiled=True)
-    mod_grad, attn_parts, one_parts = tie(mod_grad, attn_parts, one_parts)
+    mod_grad, attn_parts = tie(mod_grad, attn_parts)
     attn_parts = attn_steps.send(attn_parts)
-    whole_one = one_steps.send(one_parts)
     products_two = owned_step(whole_two, root_rows, right_wholes, 2, group)
     products_two, attn_parts = tie(products_two, attn_parts)
     attn_parts = attn_steps.send(attn_parts)

time: 695 us -> 710 us (1.022)
  blocking collectives: 61.1 us -> 79.4 us
    all_to_all x1 -> x0, waiting for transfers between devices: 16.9 us -> none  [per_device(): from_rows = lax.all_to_all(to_rows, 'dp', 0, 0, tiled=True)]
    all_to_all x0 -> x1, blocking collectives: none -> 14.1 us  [per_device(): from_rows = lax.all_to_all(to_rows, 'dp', 0, 0, tiled=True)]
    all_to_all x3, waiting for transfers between devices: 11.1 us -> 22.8 us  [shard_rows(): moved = lax.all_to_all(split, 'fsdp', 0, 0, tiled=True)]
    ppermute x22, waiting for transfers between devices: 49.7 us -> 58.2 us  [rank_swap(): return lax.ppermute(array, 'fsdp', [(at, at ^ bits) for at in range(count)])]
    unnamed x131 -> x129, local copies, waits for them, and re-layouts: 18.8 us -> 18.3 us
  transfers between devices with their start and end apart: 51 -> 50, of which waited for: 20 -> 20; matrix products, arithmetic and copies ran while one was open for 11% -> 11% of each run, Pallas kernels for 27% -> 28%
where the time goes in v18:
time: 710 us; the launch traced here: 704 us
  waiting for transfers between devices  217 us (31%)
  Pallas kernels  215 us (30%)
  blocking collectives  79.4 us (11%)
  other arithmetic  57 us (8%)
  local copies, waits for them, and re-layouts  53.5 us (8%)
  starting transfers between devices  53.3 us (8%)
  between operations  15.8 us (2%)
  matrix products  13.1 us (2%)
    ppermute x22, waiting for transfers between devices, rank_swap(): return lax.ppermute(array, 'fsdp', [(at, at ^ bits) for at in range(count)])  58.2 us
    ppermute x6, waiting for transfers between devices, chip_swap(): lax.ppermute(array, 'dp', [(at, at ^ 2 * bits) for at in range(count)])  58.1 us
    pallas_call x6, Pallas kernels, run_halves(): pl.pallas_call(body, grid_spec=pltpu.PrefetchScalarGridSpec(num_scalar_pr...  55.1 us
    all_gather x2, waiting for transfers between devices, gather_blocks(): all_rows = lax.all_gather(rows, ('fsdp', 'dp'), axis=0, tiled=True)  52.1 us
    pallas_call x1, Pallas kernels, run_attention(): pl.pallas_call(functools.partial(attention_kernel, frames), grid=(clips,)...  41.2 us
    convert_element_type x21, other arithmetic, narrow(): return array.astype(jnp.bfloat16)  27.1 us
    pallas_call x1, Pallas kernels, run_attention_back(): pl.pallas_call(functools.partial(attention_back_kernel, frames), grid=(cl...  26.1 us
    pallas_call x3, Pallas kernels, owned_step(): pl.pallas_call(functools.partial(products_kernel, dp_count // 2), in_spec...  25 us
  transfers between devices with their start and end apart: 50, of which 20 were waited for; matrix products, arithmetic and copies ran while one was open for 11% of the time, Pallas kernels for 28%

profile of v18, /device:TPU:0, one launch (start us, length us, event | category | flops | bytes accessed | tf_op | source)
XLA Modules:
  0.0 704.1 jit_solution(11030462170137772883)
XLA Ops:
  17.2 14.7 %all_gather.30 = bf16[256,128]{1,0:T(8,128)(2,1)S(1)} all-gather(bf16[32,128]{1,0:T(8,128)(2,1)S(1)} %fusion.49), channel_id=1, replica_groups=mesh['dp'=8,'fsdp'=4] {'dp'}, dimensions={0}, use_global_device_ids=true | all-gather | bytes 73728 | tf_op jit(solution)/shard_map/all_gather | solution.py:1071
  44.5 8.7 %all-to-all-done = f32[16,6,288]{2,1,0:T(8,128)S(1)} async-done(((f32[16,6,288]{2,1,0:T(8,128)}), f32[16,6,288]{2,1,0:T(8,128)S(1)}, u32[]{:S(2)}, u32[]{:S(2)}) %all-to-all-start) | async-done | bytes 110624 | tf_op jit(solution)/shard_map/all_to_all | solution.py:1089
  57.4 9.8 %all_gather.31 = f32[672,128]{1,0:T(8,128)S(1)} all-gather(f32[168,128]{1,0:T(8,128)S(1)} %pad_bitcast_fusion), channel_id=1, replica_groups=mesh['dp'=8,'fsdp'=4] {'fsdp'}, dimensions={0}, use_global_device_ids=true | all-gather | bytes 430080 | tf_op jit(solution)/shard_map/all_gather | solution.py:1096
  67.2 12.1 %collective-permute-done.4.refs_2_ = bf16[144,1152]{1,0:T(8,128)(2,1)S(1)} collective-permute-done((bf16[144,1152]{1,0:T(8,128)(2,1)S(1)}, bf16[144,1152]{1,0:T(8,128)(2,1)S(1)}, u32[]{:S(2)}, u32[]{:S(2)}) %collective-permute-start.4) | collective-permute-done | bytes 331808 | tf_op jit(solution)/shard_map/ppermute | solution.py:762
  89.0 52.0 %all-gather.14.cloned.1.call-done = bf16[1,4608,1152]{2,1,0:T(8,128)(2,1)} async-done(((bf16[1,144,1152]{2,1,0:T(8,128)(2,1)}), bf16[1,4608,1152]{2,1,0:T(8,128)(2,1)}) %all-gather.14.cloned.1.call-update) | async-done | bytes 10616848 | tf_op jit(solution)/shard_map/all_gather | solution.py:851
  146.6 41.2 %shard_map.206 = (bf16[512,1152]{1,0:T(8,128)(2,1)S(1)}, bf16[5,512,1152]{2,1,0:T(8,128)(2,1)}, bf16[512,1152]{1,0:T(8,128)(2,1)S(1)}, f32[512,1152]{1,0:T(8,128...) custom-call(s32[2]{0:T(128)S(1)} %copy-done.17, ...), custom_call_target="tpu_custom_call" | custom-call | flops 1024 | bytes 1024 | tf_op jit(solution)/shard_map/pallas_call | solution.py:216
  192.1 20.0 %collective-permute-done.11.refs_5_ = bf16[288,1152]{1,0:T(8,128)(2,1)S(1)} collective-permute-done((bf16[288,1152]{1,0:T(8,128)(2,1)S(1)}, bf16[288,1152]{1,0:T(8,128)(2,1)S(1)}, u32[]{:S(2)}, u32[]{:S(2)}) %collective-permute-start.11) | collective-permute-done | bytes 663584 | tf_op jit(solution)/shard_map/ppermute | solution.py:772
  217.2 13.9 %shard_map.207 = (bf16[4608,1152]{1,0:T(8,128)(2,1)}, bf16[4,512,1152]{2,1,0:T(8,128)(2,1)}, bf16[4,512,1152]{2,1,0:T(8,128)(2,1)}) custom-call(s32[4]{0:T(128)S(1)} %get-tuple-element.266.order, s32[9]{0:T(128)S(1)} %stack.97.starts, bf16[512,1152]{1,0:T(8,128)(2,1)S(1)} %get-tuple-element.132.mlp_in.refs_0_, f32[4,1,1152]{2,1,0:T(1,128)S(1)} %copy.92.bias, ...), custom_call_target="tpu_custom_call" | custom-call | flops 1024 | bytes 1024 | tf_op jit(solution)/shard_map/pallas_call | solution.py:324
  231.1 9.0 %shard_map.208 = bf16[4,576,1152]{2,1,0:T(8,128)(2,1)} custom-call(s32[4]{0:T(128)S(1)} %get-tuple-element.267.order, s32[1]{0:T(128)} %bitcast.45.side, s32[16]{0:T(128)S(1)} %stack.121.table, bf16[4,512,1152]{2,1,0:T(8,128)(2,1)} %get-tuple-element.138.refs_0_.hidden, bf16[512,1152]{1,0:T(8,128)(2,1)S(1)} %copy-done.2), custom_call_target="tpu_custom_call" | custom-call | flops 1024 | bytes 1024 | tf_op jit(solution)/shard_map/pallas_call | solution.py:728
  246.4 21.6 %shard_map.209 = (bf16[4,512,1152]{2,1,0:T(8,128)(2,1)}, f32[4,1,1152]{2,1,0:T(1,128)S(1)}, bf16[512,1152]{1,0:T(8,128)(2,1)}, f32[2,1,1152]{2,1,0:T(1,128)S(1)}) custom-call(s32[4]{0:T(128)S(1)} %iota.6.order, s32[4]{0:T(128)S(1)} %iota_multiply_fusion.starts, s32[2]{0:T(128)S(1)} %copy-done.17, bf16[4,512,1152]{2,1,0:T(8,128)(2,1)} %get-tuple-element.138.refs_0_.hidden, ...), custom_call_target="tpu_custom_call" | custom-call | flops 1024 | bytes 1024 | tf_op jit(solution)/shard_map/pallas_call | solution.py:404
  283.8 10.1 %shard_map.210 = (bf16[2,288,1152]{2,1,0:T(8,128)(2,1)S(1)}, bf16[2,288,1152]{2,1,0:T(8,128)(2,1)}, bf16[2,288,1152]{2,1,0:T(8,128)(2,1)}, bf16[2,288,1152]{2,1,0:T(8,128)(2,1)}) custom-call(s32[4]{0:T(128)S(1)} %get-tuple-element.267.order, s32[1]{0:T(128)} %bitcast.57.side, s32[16]{0:T(128)S(1)} %stack.121.table, ...), custom_call_target="tpu_custom_call" | custom-call | flops 1024 | bytes 1024 | tf_op jit(solution)/shard_map/pallas_call | solution.py:728
  293.9 8.5 %shard_map.211 = bf16[4,576,1152]{2,1,0:T(8,128)(2,1)} custom-call(s32[4]{0:T(128)S(1)} %get-tuple-element.267.order, s32[1]{0:T(128)} %bitcast.45.side, s32[16]{0:T(128)S(1)} %stack.121.table, bf16[512,1152]{1,0:T(8,128)(2,1)S(1)} %get-tuple-element.132.mlp_in.refs_0_, bf16[4,512,1152]{2,1,0:T(8,128)(2,1)} %get-tuple-element.155.refs_1_.d_pre), custom_call_target="tpu_custom_call" | custom-call | flops 1024 | bytes 1024 | tf_op jit(solution)/shard_map/pallas_call | solution.py:728
  305.5 15.7 %shard_map.212 = (f32[512,1152]{1,0:T(8,128)}, bf16[512,1152]{1,0:T(8,128)(2,1)S(1)}, f32[2,4,1152]{2,1,0:T(4,128)S(1)}) custom-call(s32[2]{0:T(128)S(1)} %copy-done.17, bf16[4,512,1152]{2,1,0:T(8,128)(2,1)} %get-tuple-element.155.refs_1_.d_pre, bf16[4,1152,1152]{2,1,0:T(8,128)(2,1)} %bitcast.251, f32[2,6,1152]{2,1,0:T(8,128)S(1)} %broadcast_add_fusion.mods, ...), custom_call_target="tpu_custom_call" | custom-call | flops 1024 | bytes 1024 | tf_op jit(solution)/shard_map/pallas_call | solution.py:496
  321.2 8.9 %shard_map.213 = (bf16[2,288,1152]{2,1,0:T(8,128)(2,1)S(1)}, bf16[2,288,1152]{2,1,0:T(8,128)(2,1)S(1)}, bf16[2,288,1152]{2,1,0:T(8,128)(2,1)}, bf16[2,288,1152]{2,1,0:T(8,128)(2,1)}) custom-call(s32[4]{0:T(128)S(1)} %get-tuple-element.267.order, s32[1]{0:T(128)} %bitcast.57.side, s32[16]{0:T(128)S(1)} %stack.121.table, ...), custom_call_target="tpu_custom_call" | custom-call | flops 1024 | bytes 1024 | tf_op jit(solution)/shard_map/pallas_call | solution.py:728
  343.1 26.1 %shard_map.214 = (bf16[4,512,1152]{2,1,0:T(8,128)(2,1)}, f32[2,3,1152]{2,1,0:T(4,128)S(1)}) custom-call(s32[2]{0:T(128)S(1)} %copy-done.17, bf16[512,1152]{1,0:T(8,128)(2,1)S(1)} %get-tuple-element.166.d_proj, bf16[5,512,1152]{2,1,0:T(8,128)(2,1)} %get-tuple-element.167.parts, bf16[4,1152,1152]{2,1,0:T(8,128)(2,1)} %bitcast.248), custom_call_target="tpu_custom_call" | custom-call | flops 1024 | bytes 1024 | tf_op jit(solution)/shard_map/pallas_call | solution.py:563
  369.2 14.3 %collective-permute-done.22 = bf16[2,144,1152]{2,1,0:T(8,128)(2,1)S(1)} collective-permute-done((bf16[2,144,1152]{2,1,0:T(8,128)(2,1)S(1)}, bf16[2,144,1152]{2,1,0:T(8,128)(2,1)S(1)}, u32[]{:S(2)}, u32[]{:S(2)}) %collective-permute-start.22) | collective-permute-done | bytes 663584 | tf_op jit(solution)/shard_map/ppermute | solution.py:772
  386.7 8.9 %shard_map.215 = bf16[4,576,1152]{2,1,0:T(8,128)(2,1)} custom-call(s32[4]{0:T(128)S(1)} %get-tuple-element.267.order, s32[1]{0:T(128)} %bitcast.45.side, s32[16]{0:T(128)S(1)} %stack.121.table, bf16[512,1152]{1,0:T(8,128)(2,1)S(1)} %copy-done.7, bf16[512,1152]{1,0:T(8,128)(2,1)S(1)} %copy-done.10, bf16[4,512,1152]{2,1,0:T(8,128)(2,1)} %get-tuple-element.179.refs_2_.d_qkv), custom_call_target="tpu_custom_call" | custom-call | flops 1024 | bytes 1024 | tf_op jit(solution)/shard_map/pallas_call | solution.py:728
  407.1 11.5 %shard_map.216 = (bf16[512,1152]{1,0:T(8,128)(2,1)}, f32[2,2,1152]{2,1,0:T(2,128)S(1)}) custom-call(bf16[4,512,1152]{2,1,0:T(8,128)(2,1)} %get-tuple-element.179.refs_2_.d_qkv, bf16[4,1152,1152]{2,1,0:T(8,128)(2,1)} %bitcast.249, f32[2,6,1152]{2,1,0:T(8,128)S(1)} %broadcast_add_fusion.mods, bf16[512,1152]{1,0:T(8,128)(2,1)S(1)} %bitcast.246, ...), custom_call_target="tpu_custom_call" | custom-call | flops 1024 | bytes 1024 | tf_op jit(solution)/shard_map/pallas_call | solution.py:623
  448.0 9.7 %shard_map.217 = (bf16[2,288,1152]{2,1,0:T(8,128)(2,1)S(1)}, bf16[2,288,1152]{2,1,0:T(8,128)(2,1)}, bf16[2,288,1152]{2,1,0:T(8,128)(2,1)}, bf16[2,288,1152]{2,1,0:T(8,128)(2,1)}) custom-call(s32[4]{0:T(128)S(1)} %get-tuple-element.267.order, s32[1]{0:T(128)} %bitcast.57.side, s32[16]{0:T(128)S(1)} %stack.121.table, bf16[512,1152]{1,0:T(8,128)(2,1)S(1)} %copy-done.8, ...), custom_call_target="tpu_custom_call" | custom-call | flops 1024 | bytes 1024 | tf_op jit(solution)/shard_map/pallas_call | solution.py:728
  458.8 26.1 %collective-permute-done.31 = bf16[2,144,1152]{2,1,0:T(8,128)(2,1)} collective-permute-done((bf16[2,144,1152]{2,1,0:T(8,128)(2,1)}, bf16[2,144,1152]{2,1,0:T(8,128)(2,1)}, u32[]{:S(2)}, u32[]{:S(2)}) %collective-permute-start.31) | collective-permute-done | bytes 663584 | tf_op jit(solution)/shard_map/ppermute | solution.py:767
  488.4 14.1 %all_to_all.44 = f32[8,1,3960]{2,1,0:T(1,128)S(1)} all-to-all(f32[8,1,3960]{2,1,0:T(1,128)S(1)} %all_to_all.32), channel_id=1, replica_groups=mesh['dp'=8,'fsdp'=4] {'dp'}, dimensions={0} | all-to-all | bytes 253440 | tf_op jit(solution)/shard_map/all_to_all | solution.py:1226
  503.1 10.0 %collective-permute-done.32 = bf16[2,288,1152]{2,1,0:T(8,128)(2,1)S(1)} collective-permute-done((bf16[2,288,1152]{2,1,0:T(8,128)(2,1)}, bf16[2,288,1152]{2,1,0:T(8,128)(2,1)S(1)}, u32[]{:S(2)}, u32[]{:S(2)}) %collective-permute-start.32) | collective-permute-done | bytes 1327136 | tf_op jit(solution)/shard_map/ppermute | solution.py:772
  523.7 18.7 %all_gather.35 = f32[864,128]{1,0:T(8,128)} all-gather(f32[216,128]{1,0:T(8,128)} %reshape.302), channel_id=1, replica_groups=mesh['dp'=8,'fsdp'=4] {'fsdp'}, dimensions={0}, use_global_device_ids=true | all-gather | bytes 552960 | tf_op jit(solution)/shard_map/all_gather | solution.py:1232
  546.0 8.4 %shard_map.218 = bf16[4,3,144,288]{3,2,1,0:T(8,128)(2,1)} custom-call(s32[1]{0:T(128)} %bitcast.85.at, bf16[1152,1152]{1,0:T(8,128)(2,1)} %bitcast.273, bf16[6,144,1152]{2,1,0:T(8,128)(2,1)S(1)} %concatenate.46.left_root, bf16[3,1152,1152]{2,1,0:T(8,128)(2,1)} %all-gather.12.cloned.1.call-done.right_root), custom_call_target="tpu_custom_call" | custom-call | flops 1024 | bytes 1024 | tf_op jit(solution)/shard_map/pallas_call | solution.py:1008
  554.3 9.5 %collective-permute-done.37 = bf16[2,144,1152]{2,1,0:T(8,128)(2,1)} collective-permute-done((bf16[2,144,1152]{2,1,0:T(8,128)(2,1)}, bf16[2,144,1152]{2,1,0:T(8,128)(2,1)}, u32[]{:S(2)}, u32[]{:S(2)}) %collective-permute-start.37) | collective-permute-done | bytes 663584 | tf_op jit(solution)/shard_map/ppermute | solution.py:767
  572.8 13.6 %collective-permute-done.38 = bf16[1,144,1152]{2,1,0:T(8,128)(2,1)S(1)} collective-permute-done((bf16[1,144,1152]{2,1,0:T(8,128)(2,1)S(1)}, bf16[1,144,1152]{2,1,0:T(8,128)(2,1)S(1)}, u32[]{:S(2)}, u32[]{:S(2)}) %collective-permute-start.38) | collective-permute-done | bytes 331808 | tf_op jit(solution)/shard_map/ppermute | solution.py:767
  595.6 22.2 %all_gather.39 = f32[1728,128]{1,0:T(8,128)} all-gather(f32[216,128]{1,0:T(8,128)S(1)} %reshape.314), channel_id=1, replica_groups=mesh['dp'=8,'fsdp'=4] {'dp'}, dimensions={0}, use_global_device_ids=true | all-gather | bytes 995328 | tf_op jit(solution)/shard_map/all_gather | solution.py:1260
  620.8 8.3 %shard_map.219 = bf16[4,3,144,288]{3,2,1,0:T(8,128)(2,1)} custom-call(s32[1]{0:T(128)} %bitcast.85.at, bf16[1152,1152]{1,0:T(8,128)(2,1)} %bitcast.274, bf16[6,144,1152]{2,1,0:T(8,128)(2,1)S(1)} %concatenate.46.left_root, bf16[3,1152,1152]{2,1,0:T(8,128)(2,1)} %all-gather.12.cloned.1.call-done.right_root), custom_call_target="tpu_custom_call" | custom-call | flops 1024 | bytes 1024 | tf_op jit(solution)/shard_map/pallas_call | solution.py:1008
  638.4 12.7 %all-to-all-done.4 = bf16[4,3,144,288]{3,2,1,0:T(8,128)(2,1)} async-done(((bf16[4,3,144,288]{3,2,1,0:T(8,128)(2,1)}), bf16[4,3,144,288]{3,2,1,0:T(8,128)(2,1)}, u32[]{:S(2)}, u32[]{:S(2)}) %all-to-all-start.4) | async-done | bytes 995360 | tf_op jit(solution)/shard_map/all_to_all | solution.py:842
  651.1 8.3 %shard_map.220 = bf16[4,3,144,288]{3,2,1,0:T(8,128)(2,1)} custom-call(s32[1]{0:T(128)} %bitcast.85.at, bf16[1152,1152]{1,0:T(8,128)(2,1)} %bitcast.275, bf16[6,144,1152]{2,1,0:T(8,128)(2,1)S(1)} %concatenate.46.left_root, bf16[3,1152,1152]{2,1,0:T(8,128)(2,1)} %all-gather.12.cloned.1.call-done.right_root), custom_call_target="tpu_custom_call" | custom-call | flops 1024 | bytes 1024 | tf_op jit(solution)/shard_map/pallas_call | solution.py:1008
  670.6 10.1 %all-to-all-done.5 = bf16[4,3,144,288]{3,2,1,0:T(8,128)(2,1)} async-done(((bf16[4,3,144,288]{3,2,1,0:T(8,128)(2,1)}), bf16[4,3,144,288]{3,2,1,0:T(8,128)(2,1)}, u32[]{:S(2)}, u32[]{:S(2)}) %all-to-all-start.5) | async-done | bytes 995360 | tf_op jit(solution)/shard_map/all_to_all | solution.py:842
  683.3 7.2 %fusion.55 = (bf16[18,144,288]{2,1,0:T(8,128)(2,1)}, f32[18,144,288]{2,1,0:T(8,128)}, f32[18,144,288]{2,1,0:T(8,128)}) fusion(f32[18,144,288]{2,1,0:T(8,128)S(1)} %copy-done.18, f32[4,144,288]{2,1,0:T(8,128)} %get-tuple-element.246, f32[4,144,288]{2,1,0:T(8,128)} %get-tuple-element.243, f32[4,144,288]{2,1,0:T(8,128)S(1)} %get-tuple-element.240, ...), kind=kLoop, calls=%fused_computation.141 | loop fusion | flops 5971968 | bytes 16422912 | tf_op jit(solution)/shard_map/convert_element_type | solution.py:1275
  (373 shorter events, 202.4 us)
Async XLA Ops:
  7.2 133.8 %all-gather.14.cloned.1.call-start = ((), (), s32[]{:S(2)}) async-start(), calls=%async_computation.7 | async-start | bytes 10948608 | tf_op jit(solution)/shard_map/all_gather | solution.py:851
  33.9 211.2 %all-gather.16.cloned.1.call-start = ((), (), s32[]{:S(2)}) async-start(), calls=%async_computation.8 | async-start | bytes 10948608 | tf_op jit(solution)/shard_map/all_gather | solution.py:851
  41.9 343.5 %all-gather.12.cloned.1.call-start = ((), (), s32[]{:S(2)}) async-start(), calls=%async_computation.6 | async-start | bytes 8957952 | tf_op jit(solution)/shard_map/all_gather | solution.py:907
  53.3 26.0 %collective-permute-start.4 = (bf16[144,1152]{1,0:T(8,128)(2,1)S(1)}, bf16[144,1152]{1,0:T(8,128)(2,1)S(1)}, u32[]{:S(2)}, u32[]{:S(2)}) collective-permute-start(bf16[144,1152]{1,0:T(8,128)(2,1)S(1)} %get-tuple-element.124.refs_0_), channel_id=1, source_target_pairs={{0,16},{4,20},{8,24},{12,28},{16,0},{20,4},{24,8},{28,12},{1,17},{... | collective-permute-start | bytes 995336 | tf_op jit(solution)/shard_map/ppermute | solution.py:762
  55.4 23.9 %collective-permute-start.5 = (bf16[144,1152]{1,0:T(8,128)(2,1)S(1)}, bf16[144,1152]{1,0:T(8,128)(2,1)S(1)}, u32[]{:S(2)}, u32[]{:S(2)}) collective-permute-start(bf16[144,1152]{1,0:T(8,128)(2,1)S(1)} %get-tuple-element.124.refs_0_), channel_id=1, source_target_pairs={{0,24},{4,28},{8,0},{12,4},{16,8},{20,12},{24,16},{28,20},{1,25},{... | collective-permute-start | bytes 995336 | tf_op jit(solution)/shard_map/ppermute | solution.py:762
  143.5 44.4 %collective-permute-start.7 = (bf16[576,1152]{1,0:T(8,128)(2,1)}, bf16[576,1152]{1,0:T(8,128)(2,1)S(1)}, u32[]{:S(2)}, u32[]{:S(2)}) collective-permute-start(bf16[576,1152]{1,0:T(8,128)(2,1)} %constant_dynamic-slice_fusion.3), channel_id=1, source_target_pairs={{0,1},{1,0},{2,3},{3,2},{4,5},{5,4},{6,7},{7,6},{8,9},{9,8},{10,11... | collective-permute-start | bytes 3981320 | tf_op jit(solution)/shard_map/ppermute | solution.py:772
  144.9 43.0 %collective-permute-start.8 = (bf16[576,1152]{1,0:T(8,128)(2,1)}, bf16[576,1152]{1,0:T(8,128)(2,1)}, u32[]{:S(2)}, u32[]{:S(2)}) collective-permute-start(bf16[576,1152]{1,0:T(8,128)(2,1)} %constant_dynamic-slice_fusion.3), channel_id=1, source_target_pairs={{0,2},{1,3},{2,0},{3,1},{4,6},{5,7},{6,4},{7,5},{8,10},{9,11},{10,... | collective-permute-start | bytes 3981320 | tf_op jit(solution)/shard_map/ppermute | solution.py:772
  189.6 22.6 %collective-permute-start.11 = (bf16[288,1152]{1,0:T(8,128)(2,1)S(1)}, bf16[288,1152]{1,0:T(8,128)(2,1)S(1)}, u32[]{:S(2)}, u32[]{:S(2)}) collective-permute-start(bf16[288,1152]{1,0:T(8,128)(2,1)S(1)} %slice.141), channel_id=1, source_target_pairs={{0,1},{1,0},{2,3},{3,2},{4,5},{5,4},{6,7},{7,6},{8,9},{9,8},{10,11... | collective-permute-start | bytes 1990664 | tf_op jit(solution)/shard_map/ppermute | solution.py:772
  191.2 23.8 %collective-permute-start.12 = (bf16[288,1152]{1,0:T(8,128)(2,1)S(1)}, bf16[288,1152]{1,0:T(8,128)(2,1)S(1)}, u32[]{:S(2)}, u32[]{:S(2)}) collective-permute-start(bf16[288,1152]{1,0:T(8,128)(2,1)S(1)} %slice.142), channel_id=1, source_target_pairs={{0,2},{1,3},{2,0},{3,1},{4,6},{5,7},{6,4},{7,5},{8,10},{9,11},{10,... | collective-permute-start | bytes 1990664 | tf_op jit(solution)/shard_map/ppermute | solution.py:772
  191.6 25.6 %collective-permute-start.10 = (bf16[576,1152]{1,0:T(8,128)(2,1)}, bf16[576,1152]{1,0:T(8,128)(2,1)}, u32[]{:S(2)}, u32[]{:S(2)}) collective-permute-start(bf16[576,1152]{1,0:T(8,128)(2,1)} %collective-permute-done.8.refs_3_), channel_id=1, source_target_pairs={{0,4},{4,0},{8,12},{12,8},{16,20},{20,16},{24,28},{28,24},{1,5},{5... | collective-permute-start | bytes 3981320 | tf_op jit(solution)/shard_map/ppermute | solution.py:757
  191.6 25.6 %collective-permute-start.9 = (bf16[576,1152]{1,0:T(8,128)(2,1)}, bf16[576,1152]{1,0:T(8,128)(2,1)}, u32[]{:S(2)}, u32[]{:S(2)}) collective-permute-start(bf16[576,1152]{1,0:T(8,128)(2,1)} %copy-done.40), channel_id=1, source_target_pairs={{0,4},{4,0},{8,12},{12,8},{16,20},{20,16},{24,28},{28,24},{1,5},{5... | collective-permute-start | bytes 3981320 | tf_op jit(solution)/shard_map/ppermute | solution.py:757
  240.1 41.2 %collective-permute-start.18 = (bf16[4,576,1152]{2,1,0:T(8,128)(2,1)}, bf16[4,576,1152]{2,1,0:T(8,128)(2,1)}, u32[]{:S(2)}, u32[]{:S(2)}) collective-permute-start(bf16[4,576,1152]{2,1,0:T(8,128)(2,1)} %shard_map.208), channel_id=1, source_target_pairs={{0,4},{4,0},{8,12},{12,8},{16,20},{20,16},{24,28},{28,24},{1,5},{5... | collective-permute-start | bytes 15925256 | tf_op jit(solution)/shard_map/ppermute | solution.py:757
  241.6 26.5 %collective-permute-start.15 = (bf16[6,144,288]{2,1,0:T(8,128)(2,1)}, bf16[6,144,288]{2,1,0:T(8,128)(2,1)}, u32[]{:S(2)}, u32[]{:S(2)}) collective-permute-start(bf16[6,144,288]{2,1,0:T(8,128)(2,1)} %get-tuple-element.238), channel_id=1, source_target_pairs={{0,1},{1,0},{2,3},{3,2},{4,5},{5,4},{6,7},{7,6},{8,9},{9,8},{10,11... | collective-permute-start | bytes 1493000 | tf_op jit(solution)/shard_map/ppermute | solution.py:772
  242.2 31.6 %collective-permute-start.16 = (bf16[6,144,288]{2,1,0:T(8,128)(2,1)}, bf16[6,144,288]{2,1,0:T(8,128)(2,1)}, u32[]{:S(2)}, u32[]{:S(2)}) collective-permute-start(bf16[6,144,288]{2,1,0:T(8,128)(2,1)} %get-tuple-element.237), channel_id=1, source_target_pairs={{0,2},{1,3},{2,0},{3,1},{4,6},{5,7},{6,4},{7,5},{8,10},{9,11},{10,... | collective-permute-start | bytes 1493000 | tf_op jit(solution)/shard_map/ppermute | solution.py:772
  243.5 30.2 %collective-permute-start.17 = (bf16[6,144,288]{2,1,0:T(8,128)(2,1)}, bf16[6,144,288]{2,1,0:T(8,128)(2,1)}, u32[]{:S(2)}, u32[]{:S(2)}) collective-permute-start(bf16[6,144,288]{2,1,0:T(8,128)(2,1)} %get-tuple-element.236), channel_id=1, source_target_pairs={{0,3},{1,2},{2,1},{3,0},{4,7},{5,6},{6,5},{7,4},{8,11},{9,10},{10,... | collective-permute-start | bytes 1493000 | tf_op jit(solution)/shard_map/ppermute | solution.py:772
  302.4 31.9 %collective-permute-start.20 = (bf16[2,288,1152]{2,1,0:T(8,128)(2,1)}, bf16[2,288,1152]{2,1,0:T(8,128)(2,1)}, u32[]{:S(2)}, u32[]{:S(2)}) collective-permute-start(bf16[2,288,1152]{2,1,0:T(8,128)(2,1)} %get-tuple-element.164), channel_id=1, source_target_pairs={{0,1},{1,0},{2,3},{3,2},{4,5},{5,4},{6,7},{7,6},{8,9},{9,8},{10,11... | collective-permute-start | bytes 3981320 | tf_op jit(solution)/shard_map/ppermute | solution.py:772
  303.8 31.6 %collective-permute-start.21 = (bf16[2,288,1152]{2,1,0:T(8,128)(2,1)}, bf16[2,288,1152]{2,1,0:T(8,128)(2,1)}, u32[]{:S(2)}, u32[]{:S(2)}) collective-permute-start(bf16[2,288,1152]{2,1,0:T(8,128)(2,1)} %get-tuple-element.165), channel_id=1, source_target_pairs={{0,2},{1,3},{2,0},{3,1},{4,6},{5,7},{6,4},{7,5},{8,10},{9,11},{10,... | collective-permute-start | bytes 3981320 | tf_op jit(solution)/shard_map/ppermute | solution.py:772
  337.1 32.1 %collective-permute-start.23 = (bf16[2,144,1152]{2,1,0:T(8,128)(2,1)S(1)}, bf16[2,144,1152]{2,1,0:T(8,128)(2,1)S(1)}, u32[]{:S(2)}, u32[]{:S(2)}) collective-permute-start(bf16[2,144,1152]{2,1,0:T(8,128)(2,1)S(1)} %dynamic-slice_bitcast_fusion.7), channel_id=1, source_target_pairs={{0,1},{1,0},{2,3},{3,2},{4,5},{5,4},{6,7},{7,6},{8,9},{9,8},{10,11... | collective-permute-start | bytes 1990664 | tf_op jit(solution)/shard_map/ppermute | solution.py:772
  337.8 45.7 %collective-permute-start.24 = (bf16[2,288,1152]{2,1,0:T(8,128)(2,1)S(1)}, bf16[2,288,1152]{2,1,0:T(8,128)(2,1)S(1)}, u32[]{:S(2)}, u32[]{:S(2)}) collective-permute-start(bf16[2,288,1152]{2,1,0:T(8,128)(2,1)S(1)} %get-tuple-element.173), channel_id=1, source_target_pairs={{0,1},{1,0},{2,3},{3,2},{4,5},{5,4},{6,7},{7,6},{8,9},{9,8},{10,11... | collective-permute-start | bytes 3981320 | tf_op jit(solution)/shard_map/ppermute | solution.py:772
  339.2 46.2 %collective-permute-start.25 = (bf16[2,288,1152]{2,1,0:T(8,128)(2,1)}, bf16[2,288,1152]{2,1,0:T(8,128)(2,1)}, u32[]{:S(2)}, u32[]{:S(2)}) collective-permute-start(bf16[2,288,1152]{2,1,0:T(8,128)(2,1)} %get-tuple-element.174), channel_id=1, source_target_pairs={{0,2},{1,3},{2,0},{3,1},{4,6},{5,7},{6,4},{7,5},{8,10},{9,11},{10,... | collective-permute-start | bytes 3981320 | tf_op jit(solution)/shard_map/ppermute | solution.py:772
  341.4 42.2 %collective-permute-start.22 = (bf16[2,144,1152]{2,1,0:T(8,128)(2,1)S(1)}, bf16[2,144,1152]{2,1,0:T(8,128)(2,1)S(1)}, u32[]{:S(2)}, u32[]{:S(2)}) collective-permute-start(bf16[2,144,1152]{2,1,0:T(8,128)(2,1)S(1)} %dynamic-slice_bitcast_fusion.8), channel_id=1, source_target_pairs={{0,2},{1,3},{2,0},{3,1},{4,6},{5,7},{6,4},{7,5},{8,10},{9,11},{10,... | collective-permute-start | bytes 1990664 | tf_op jit(solution)/shard_map/ppermute | solution.py:772
  395.6 26.1 %collective-permute-start.26 = (bf16[4,576,1152]{2,1,0:T(8,128)(2,1)}, bf16[4,576,1152]{2,1,0:T(8,128)(2,1)}, u32[]{:S(2)}, u32[]{:S(2)}) collective-permute-start(bf16[4,576,1152]{2,1,0:T(8,128)(2,1)} %shard_map.215), channel_id=1, source_target_pairs={{0,4},{4,0},{8,12},{12,8},{16,20},{20,16},{24,28},{28,24},{1,5},{5... | collective-permute-start | bytes 15925256 | tf_op jit(solution)/shard_map/ppermute | solution.py:757
  431.9 114.1 %all-gather.18.cloned.1.call-start = ((), (), s32[]{:S(2)}) async-start(), calls=%async_computation.9 | async-start | bytes 2985984 | tf_op jit(solution)/shard_map/all_gather | solution.py:961
  444.3 176.5 %all-gather.22.cloned.1.call-start = ((), (), s32[]{:S(2)}) async-start(), calls=%async_computation.11 | async-start | bytes 2985984 | tf_op jit(solution)/shard_map/all_gather | solution.py:961
  447.2 37.7 %collective-permute-start.31 = (bf16[2,144,1152]{2,1,0:T(8,128)(2,1)}, bf16[2,144,1152]{2,1,0:T(8,128)(2,1)}, u32[]{:S(2)}, u32[]{:S(2)}) collective-permute-start(bf16[2,144,1152]{2,1,0:T(8,128)(2,1)} %dynamic-slice_bitcast_fusion.3), channel_id=1, source_target_pairs={{0,8},{4,12},{8,0},{12,4},{16,24},{20,28},{24,16},{28,20},{1,9},{5... | collective-permute-start | bytes 1990664 | tf_op jit(solution)/shard_map/ppermute | solution.py:767
  484.9 28.1 %collective-permute-start.32 = (bf16[2,288,1152]{2,1,0:T(8,128)(2,1)}, bf16[2,288,1152]{2,1,0:T(8,128)(2,1)S(1)}, u32[]{:S(2)}, u32[]{:S(2)}) collective-permute-start(bf16[2,288,1152]{2,1,0:T(8,128)(2,1)} %get-tuple-element.205), channel_id=1, source_target_pairs={{0,1},{1,0},{2,3},{3,2},{4,5},{5,4},{6,7},{7,6},{8,9},{9,8},{10,11... | collective-permute-start | bytes 3981320 | tf_op jit(solution)/shard_map/ppermute | solution.py:772
  485.2 27.9 %collective-permute-start.33 = (bf16[2,288,1152]{2,1,0:T(8,128)(2,1)}, bf16[2,288,1152]{2,1,0:T(8,128)(2,1)S(1)}, u32[]{:S(2)}, u32[]{:S(2)}) collective-permute-start(bf16[2,288,1152]{2,1,0:T(8,128)(2,1)} %get-tuple-element.206), channel_id=1, source_target_pairs={{0,2},{1,3},{2,0},{3,1},{4,6},{5,7},{6,4},{7,5},{8,10},{9,11},{10,... | collective-permute-start | bytes 3981320 | tf_op jit(solution)/shard_map/ppermute | solution.py:772
  516.4 26.0 %collective-permute-start.36 = (bf16[2,144,1152]{2,1,0:T(8,128)(2,1)}, bf16[2,144,1152]{2,1,0:T(8,128)(2,1)}, u32[]{:S(2)}, u32[]{:S(2)}) collective-permute-start(bf16[2,144,1152]{2,1,0:T(8,128)(2,1)} %dynamic-slice_bitcast_fusion.1), channel_id=1, source_target_pairs={{0,1},{1,0},{2,3},{3,2},{4,5},{5,4},{6,7},{7,6},{8,9},{9,8},{10,11... | collective-permute-start | bytes 1990664 | tf_op jit(solution)/shard_map/ppermute | solution.py:772
  563.8 22.6 %all-to-all-start.3 = ((bf16[4,3,144,288]{3,2,1,0:T(8,128)(2,1)}), bf16[4,3,144,288]{3,2,1,0:T(8,128)(2,1)}, u32[]{:S(2)}, u32[]{:S(2)}) async-start(bf16[4,3,144,288]{3,2,1,0:T(8,128)(2,1)} %shard_map.218), calls=%async_computation.3 | async-start | bytes 2654208 | tf_op jit(solution)/shard_map/all_to_all | solution.py:842
  568.1 83.0 %all-gather.20.cloned.1.call-start = ((), (), s32[]{:S(2)}) async-start(), calls=%async_computation.10 | async-start | bytes 2985984 | tf_op jit(solution)/shard_map/all_gather | solution.py:961
  629.2 21.9 %all-to-all-start.4 = ((bf16[4,3,144,288]{3,2,1,0:T(8,128)(2,1)}), bf16[4,3,144,288]{3,2,1,0:T(8,128)(2,1)}, u32[]{:S(2)}, u32[]{:S(2)}) async-start(bf16[4,3,144,288]{3,2,1,0:T(8,128)(2,1)} %shard_map.219), calls=%async_computation.4 | async-start | bytes 2654208 | tf_op jit(solution)/shard_map/all_to_all | solution.py:842
  659.4 21.3 %all-to-all-start.5 = ((bf16[4,3,144,288]{3,2,1,0:T(8,128)(2,1)}), bf16[4,3,144,288]{3,2,1,0:T(8,128)(2,1)}, u32[]{:S(2)}, u32[]{:S(2)}) async-start(bf16[4,3,144,288]{3,2,1,0:T(8,128)(2,1)} %shard_map.220), calls=%async_computation.5 | async-start | bytes 2654208 | tf_op jit(solution)/shard_map/all_to_all | solution.py:842
  (81 other events, 688.6 us)
Sparse Core Ops, SparseCore 0:
  34.1 106.8 all-gather.13
  144.6 96.4 all-gather.15
  282.6 76.5 all-gather.11
  444.5 40.8 all-gather.17
  520.7 33.1 all-gather.21
  588.4 41.9 all-gather.19

commit v19 on v17

--- a/solution.py
+++ b/solution.py
@@ -1209,7 +1209,8 @@
         axis=1,
     )
     rank_sums = lax.all_to_all(to_ranks, "fsdp", 0, 0, tiled=True)
-    rank_sums, attn_parts = tie(rank_sums, attn_parts)
+    rank_sums, attn_parts, two_parts = tie(rank_sums, attn_parts, two_parts)
+    whole_two = two_steps.send(two_parts)
     attn_parts = attn_steps.send(attn_parts)
     rank_sums = jnp.sum(rank_sums, axis=0)
     to_rows = jnp.concatenate(
@@ -1222,9 +1223,8 @@
     to_rows, attn_parts = tie(to_rows, attn_parts)
     attn_parts = attn_steps.send(attn_parts)
     from_rows = lax.all_to_all(to_rows, "dp", 0, 0, tiled=True)
-    from_rows, attn_parts, two_parts, one_parts = tie(from_rows, attn_parts, two_parts, one_parts)
+    from_rows, attn_parts, one_parts = tie(from_rows, attn_parts, one_parts)
     attn_parts = attn_steps.send(attn_parts)
-    whole_two = two_steps.send(two_parts)
     one_parts = one_steps.send(one_parts)
     bias_grad = jnp.sum(from_rows[:, mod_size:], axis=0)
     mod_grad_cols = from_rows[:, :mod_size].reshape(all_clips, mod_count, col_part)

time: 695 us -> 710 us (1.022)
  blocking collectives: 61.1 us -> 103 us
  waiting for transfers between devices: 213 us -> 197 us
    all_to_all x0 -> x1, blocking collectives: none -> 38.6 us  [per_device(): from_rows = lax.all_to_all(to_rows, 'dp', 0, 0, tiled=True)]
    all_to_all x1 -> x0, waiting for transfers between devices: 16.9 us -> none  [per_device(): from_rows = lax.all_to_all(to_rows, 'dp', 0, 0, tiled=True)]
    all_to_all x3, waiting for transfers between devices: 11.1 us -> 23.6 us  [shard_rows(): moved = lax.all_to_all(split, 'fsdp', 0, 0, tiled=True)]
    ppermute x6, waiting for transfers between devices: 56.8 us -> 46.5 us  [chip_swap(): lax.ppermute(array, 'dp', [(at, at ^ 2 * bits) for at in range(count)])]
    unnamed x131 -> x133, local copies, waits for them, and re-layouts: 18.8 us -> 17.8 us
  transfers between devices with their start and end apart: 51 -> 50, of which waited for: 20 -> 18; matrix products, arithmetic and copies ran while one was open for 11% -> 11% of each run, Pallas kernels for 27% -> 27%
where the time goes in v19:
time: 710 us; the launch traced here: 704 us
  Pallas kernels  215 us (30%)
  waiting for transfers between devices  197 us (28%)
  blocking collectives  103 us (15%)
  other arithmetic  55.9 us (8%)
  starting transfers between devices  53 us (7%)
  local copies, waits for them, and re-layouts  52 us (7%)
  between operations  15.9 us (2%)
  matrix products  13.1 us (2%)
    pallas_call x6, Pallas kernels, run_halves(): pl.pallas_call(body, grid_spec=pltpu.PrefetchScalarGridSpec(num_scalar_pr...  55 us
    all_gather x2, waiting for transfers between devices, gather_blocks(): all_rows = lax.all_gather(rows, ('fsdp', 'dp'), axis=0, tiled=True)  52.1 us
    ppermute x22, waiting for transfers between devices, rank_swap(): return lax.ppermute(array, 'fsdp', [(at, at ^ bits) for at in range(count)])  48.1 us
    ppermute x6, waiting for transfers between devices, chip_swap(): lax.ppermute(array, 'dp', [(at, at ^ 2 * bits) for at in range(count)])  46.5 us
    pallas_call x1, Pallas kernels, run_attention(): pl.pallas_call(functools.partial(attention_kernel, frames), grid=(clips,)...  41.2 us
    all_to_all x1, blocking collectives, per_device(): from_rows = lax.all_to_all(to_rows, 'dp', 0, 0, tiled=True)  38.6 us
    convert_element_type x21, other arithmetic, narrow(): return array.astype(jnp.bfloat16)  27.7 us
    pallas_call x1, Pallas kernels, run_attention_back(): pl.pallas_call(functools.partial(attention_back_kernel, frames), grid=(cl...  26.1 us
  transfers between devices with their start and end apart: 50, of which 18 were waited for; matrix products, arithmetic and copies ran while one was open for 11% of the time, Pallas kernels for 27%

profile of v19, /device:TPU:0, one launch (start us, length us, event | category | flops | bytes accessed | tf_op | source)
XLA Modules:
  0.0 704.2 jit_solution(17660673204933627748)
XLA Ops:
  17.2 14.7 %all_gather.30 = bf16[256,128]{1,0:T(8,128)(2,1)S(1)} all-gather(bf16[32,128]{1,0:T(8,128)(2,1)S(1)} %fusion.49), channel_id=1, replica_groups=mesh['dp'=8,'fsdp'=4] {'dp'}, dimensions={0}, use_global_device_ids=true | all-gather | bytes 73728 | tf_op jit(solution)/shard_map/all_gather | solution.py:1071
  44.5 8.7 %all-to-all-done = f32[16,6,288]{2,1,0:T(8,128)S(1)} async-done(((f32[16,6,288]{2,1,0:T(8,128)}), f32[16,6,288]{2,1,0:T(8,128)S(1)}, u32[]{:S(2)}, u32[]{:S(2)}) %all-to-all-start) | async-done | bytes 110624 | tf_op jit(solution)/shard_map/all_to_all | solution.py:1089
  57.4 9.8 %all_gather.31 = f32[672,128]{1,0:T(8,128)S(1)} all-gather(f32[168,128]{1,0:T(8,128)S(1)} %pad_bitcast_fusion), channel_id=1, replica_groups=mesh['dp'=8,'fsdp'=4] {'fsdp'}, dimensions={0}, use_global_device_ids=true | all-gather | bytes 430080 | tf_op jit(solution)/shard_map/all_gather | solution.py:1096
  67.2 12.1 %collective-permute-done.4.refs_2_ = bf16[144,1152]{1,0:T(8,128)(2,1)S(1)} collective-permute-done((bf16[144,1152]{1,0:T(8,128)(2,1)S(1)}, bf16[144,1152]{1,0:T(8,128)(2,1)S(1)}, u32[]{:S(2)}, u32[]{:S(2)}) %collective-permute-start.4) | collective-permute-done | bytes 331808 | tf_op jit(solution)/shard_map/ppermute | solution.py:762
  89.0 52.0 %all-gather.14.cloned.1.call-done = bf16[1,4608,1152]{2,1,0:T(8,128)(2,1)} async-done(((bf16[1,144,1152]{2,1,0:T(8,128)(2,1)}), bf16[1,4608,1152]{2,1,0:T(8,128)(2,1)}) %all-gather.14.cloned.1.call-update) | async-done | bytes 10616848 | tf_op jit(solution)/shard_map/all_gather | solution.py:851
  146.6 41.2 %shard_map.206 = (bf16[512,1152]{1,0:T(8,128)(2,1)S(1)}, bf16[5,512,1152]{2,1,0:T(8,128)(2,1)}, bf16[512,1152]{1,0:T(8,128)(2,1)S(1)}, f32[512,1152]{1,0:T(8,128...) custom-call(s32[2]{0:T(128)S(1)} %copy-done.19, ...), custom_call_target="tpu_custom_call" | custom-call | flops 1024 | bytes 1024 | tf_op jit(solution)/shard_map/pallas_call | solution.py:216
  192.1 20.0 %collective-permute-done.11.refs_5_ = bf16[288,1152]{1,0:T(8,128)(2,1)S(1)} collective-permute-done((bf16[288,1152]{1,0:T(8,128)(2,1)S(1)}, bf16[288,1152]{1,0:T(8,128)(2,1)S(1)}, u32[]{:S(2)}, u32[]{:S(2)}) %collective-permute-start.11) | collective-permute-done | bytes 663584 | tf_op jit(solution)/shard_map/ppermute | solution.py:772
  217.2 13.9 %shard_map.207 = (bf16[4608,1152]{1,0:T(8,128)(2,1)}, bf16[4,512,1152]{2,1,0:T(8,128)(2,1)}, bf16[4,512,1152]{2,1,0:T(8,128)(2,1)}) custom-call(s32[4]{0:T(128)S(1)} %get-tuple-element.266.order, s32[9]{0:T(128)S(1)} %stack.97.starts, bf16[512,1152]{1,0:T(8,128)(2,1)S(1)} %get-tuple-element.132.mlp_in.refs_0_, f32[4,1,1152]{2,1,0:T(1,128)S(1)} %copy.92.bias, ...), custom_call_target="tpu_custom_call" | custom-call | flops 1024 | bytes 1024 | tf_op jit(solution)/shard_map/pallas_call | solution.py:324
  231.1 9.0 %shard_map.208 = bf16[4,576,1152]{2,1,0:T(8,128)(2,1)} custom-call(s32[4]{0:T(128)S(1)} %get-tuple-element.267.order, s32[1]{0:T(128)} %bitcast.45.side, s32[16]{0:T(128)S(1)} %stack.121.table, bf16[4,512,1152]{2,1,0:T(8,128)(2,1)} %get-tuple-element.138.refs_0_.hidden, bf16[512,1152]{1,0:T(8,128)(2,1)S(1)} %copy-done.2), custom_call_target="tpu_custom_call" | custom-call | flops 1024 | bytes 1024 | tf_op jit(solution)/shard_map/pallas_call | solution.py:728
  246.4 21.6 %shard_map.209 = (bf16[4,512,1152]{2,1,0:T(8,128)(2,1)}, f32[4,1,1152]{2,1,0:T(1,128)S(1)}, bf16[512,1152]{1,0:T(8,128)(2,1)}, f32[2,1,1152]{2,1,0:T(1,128)S(1)}) custom-call(s32[4]{0:T(128)S(1)} %iota.6.order, s32[4]{0:T(128)S(1)} %iota_multiply_fusion.starts, s32[2]{0:T(128)S(1)} %copy-done.19, bf16[4,512,1152]{2,1,0:T(8,128)(2,1)} %get-tuple-element.138.refs_0_.hidden, ...), custom_call_target="tpu_custom_call" | custom-call | flops 1024 | bytes 1024 | tf_op jit(solution)/shard_map/pallas_call | solution.py:404
  268.1 5.6 collective-permute-done.16
  283.8 10.1 %shard_map.210 = (bf16[2,288,1152]{2,1,0:T(8,128)(2,1)S(1)}, bf16[2,288,1152]{2,1,0:T(8,128)(2,1)}, bf16[2,288,1152]{2,1,0:T(8,128)(2,1)}, bf16[2,288,1152]{2,1,0:T(8,128)(2,1)}) custom-call(s32[4]{0:T(128)S(1)} %get-tuple-element.267.order, s32[1]{0:T(128)} %bitcast.57.side, s32[16]{0:T(128)S(1)} %stack.121.table, ...), custom_call_target="tpu_custom_call" | custom-call | flops 1024 | bytes 1024 | tf_op jit(solution)/shard_map/pallas_call | solution.py:728
  293.9 8.5 %shard_map.211 = bf16[4,576,1152]{2,1,0:T(8,128)(2,1)} custom-call(s32[4]{0:T(128)S(1)} %get-tuple-element.267.order, s32[1]{0:T(128)} %bitcast.45.side, s32[16]{0:T(128)S(1)} %stack.121.table, bf16[512,1152]{1,0:T(8,128)(2,1)S(1)} %get-tuple-element.132.mlp_in.refs_0_, bf16[4,512,1152]{2,1,0:T(8,128)(2,1)} %get-tuple-element.155.refs_1_.d_pre), custom_call_target="tpu_custom_call" | custom-call | flops 1024 | bytes 1024 | tf_op jit(solution)/shard_map/pallas_call | solution.py:728
  305.5 15.7 %shard_map.212 = (f32[512,1152]{1,0:T(8,128)}, bf16[512,1152]{1,0:T(8,128)(2,1)S(1)}, f32[2,4,1152]{2,1,0:T(4,128)S(1)}) custom-call(s32[2]{0:T(128)S(1)} %copy-done.19, bf16[4,512,1152]{2,1,0:T(8,128)(2,1)} %get-tuple-element.155.refs_1_.d_pre, bf16[4,1152,1152]{2,1,0:T(8,128)(2,1)} %bitcast.251, f32[2,6,1152]{2,1,0:T(8,128)S(1)} %broadcast_add_fusion.mods, ...), custom_call_target="tpu_custom_call" | custom-call | flops 1024 | bytes 1024 | tf_op jit(solution)/shard_map/pallas_call | solution.py:496
  321.3 8.9 %shard_map.213 = (bf16[2,288,1152]{2,1,0:T(8,128)(2,1)S(1)}, bf16[2,288,1152]{2,1,0:T(8,128)(2,1)S(1)}, bf16[2,288,1152]{2,1,0:T(8,128)(2,1)}, bf16[2,288,1152]{2,1,0:T(8,128)(2,1)}) custom-call(s32[4]{0:T(128)S(1)} %get-tuple-element.267.order, s32[1]{0:T(128)} %bitcast.57.side, s32[16]{0:T(128)S(1)} %stack.121.table, ...), custom_call_target="tpu_custom_call" | custom-call | flops 1024 | bytes 1024 | tf_op jit(solution)/shard_map/pallas_call | solution.py:728
  343.1 26.1 %shard_map.214 = (bf16[4,512,1152]{2,1,0:T(8,128)(2,1)}, f32[2,3,1152]{2,1,0:T(4,128)S(1)}) custom-call(s32[2]{0:T(128)S(1)} %copy-done.19, bf16[512,1152]{1,0:T(8,128)(2,1)S(1)} %get-tuple-element.166.d_proj, bf16[5,512,1152]{2,1,0:T(8,128)(2,1)} %get-tuple-element.167.parts, bf16[4,1152,1152]{2,1,0:T(8,128)(2,1)} %bitcast.248), custom_call_target="tpu_custom_call" | custom-call | flops 1024 | bytes 1024 | tf_op jit(solution)/shard_map/pallas_call | solution.py:563
  369.2 14.3 %collective-permute-done.22 = bf16[2,144,1152]{2,1,0:T(8,128)(2,1)S(1)} collective-permute-done((bf16[2,144,1152]{2,1,0:T(8,128)(2,1)S(1)}, bf16[2,144,1152]{2,1,0:T(8,128)(2,1)S(1)}, u32[]{:S(2)}, u32[]{:S(2)}) %collective-permute-start.22) | collective-permute-done | bytes 663584 | tf_op jit(solution)/shard_map/ppermute | solution.py:772
  386.8 8.8 %shard_map.215 = bf16[4,576,1152]{2,1,0:T(8,128)(2,1)} custom-call(s32[4]{0:T(128)S(1)} %get-tuple-element.267.order, s32[1]{0:T(128)} %bitcast.45.side, s32[16]{0:T(128)S(1)} %stack.121.table, bf16[512,1152]{1,0:T(8,128)(2,1)S(1)} %copy-done.7, bf16[512,1152]{1,0:T(8,128)(2,1)S(1)} %copy-done.10, bf16[4,512,1152]{2,1,0:T(8,128)(2,1)} %get-tuple-element.179.refs_2_.d_qkv), custom_call_target="tpu_custom_call" | custom-call | flops 1024 | bytes 1024 | tf_op jit(solution)/shard_map/pallas_call | solution.py:728
  407.1 11.5 %shard_map.216 = (bf16[512,1152]{1,0:T(8,128)(2,1)}, f32[2,2,1152]{2,1,0:T(2,128)S(1)}) custom-call(bf16[4,512,1152]{2,1,0:T(8,128)(2,1)} %get-tuple-element.179.refs_2_.d_qkv, bf16[4,1152,1152]{2,1,0:T(8,128)(2,1)} %bitcast.249, f32[2,6,1152]{2,1,0:T(8,128)S(1)} %broadcast_add_fusion.mods, bf16[512,1152]{1,0:T(8,128)(2,1)S(1)} %bitcast.246, ...), custom_call_target="tpu_custom_call" | custom-call | flops 1024 | bytes 1024 | tf_op jit(solution)/shard_map/pallas_call | solution.py:623
  436.7 4.9 collective-permute-done.30
  443.0 9.6 %shard_map.217 = (bf16[2,288,1152]{2,1,0:T(8,128)(2,1)S(1)}, bf16[2,288,1152]{2,1,0:T(8,128)(2,1)}, bf16[2,288,1152]{2,1,0:T(8,128)(2,1)}, bf16[2,288,1152]{2,1,0:T(8,128)(2,1)}) custom-call(s32[4]{0:T(128)S(1)} %get-tuple-element.267.order, s32[1]{0:T(128)} %bitcast.57.side, s32[16]{0:T(128)S(1)} %stack.121.table, bf16[512,1152]{1,0:T(8,128)(2,1)S(1)} %copy-done.8, ...), custom_call_target="tpu_custom_call" | custom-call | flops 1024 | bytes 1024 | tf_op jit(solution)/shard_map/pallas_call | solution.py:728
  460.6 38.6 %all_to_all.44 = f32[8,1,3960]{2,1,0:T(1,128)S(1)} all-to-all(f32[8,1,3960]{2,1,0:T(1,128)S(1)} %all_to_all.32), channel_id=1, replica_groups=mesh['dp'=8,'fsdp'=4] {'dp'}, dimensions={0} | all-to-all | bytes 253440 | tf_op jit(solution)/shard_map/all_to_all | solution.py:1225
  508.6 19.3 %all_gather.35 = f32[864,128]{1,0:T(8,128)} all-gather(f32[216,128]{1,0:T(8,128)} %reshape.302), channel_id=1, replica_groups=mesh['dp'=8,'fsdp'=4] {'fsdp'}, dimensions={0}, use_global_device_ids=true | all-gather | bytes 552960 | tf_op jit(solution)/shard_map/all_gather | solution.py:1231
  533.6 8.4 %shard_map.218 = bf16[4,3,144,288]{3,2,1,0:T(8,128)(2,1)} custom-call(s32[1]{0:T(128)} %bitcast.85.at, bf16[1152,1152]{1,0:T(8,128)(2,1)} %bitcast.274, bf16[6,144,1152]{2,1,0:T(8,128)(2,1)S(1)} %concatenate.46.left_root, bf16[3,1152,1152]{2,1,0:T(8,128)(2,1)} %all-gather.12.cloned.1.call-done.right_root), custom_call_target="tpu_custom_call" | custom-call | flops 1024 | bytes 1024 | tf_op jit(solution)/shard_map/pallas_call | solution.py:1008
  542.0 28.0 %collective-permute-done.37 = bf16[2,144,1152]{2,1,0:T(8,128)(2,1)} collective-permute-done((bf16[2,144,1152]{2,1,0:T(8,128)(2,1)}, bf16[2,144,1152]{2,1,0:T(8,128)(2,1)}, u32[]{:S(2)}, u32[]{:S(2)}) %collective-permute-start.37) | collective-permute-done | bytes 663584 | tf_op jit(solution)/shard_map/ppermute | solution.py:767
  576.6 10.5 %collective-permute-done.38 = bf16[1,144,1152]{2,1,0:T(8,128)(2,1)S(1)} collective-permute-done((bf16[1,144,1152]{2,1,0:T(8,128)(2,1)S(1)}, bf16[1,144,1152]{2,1,0:T(8,128)(2,1)S(1)}, u32[]{:S(2)}, u32[]{:S(2)}) %collective-permute-start.38) | collective-permute-done | bytes 331808 | tf_op jit(solution)/shard_map/ppermute | solution.py:767
  596.4 20.7 %all_gather.39 = f32[1728,128]{1,0:T(8,128)} all-gather(f32[216,128]{1,0:T(8,128)S(1)} %reshape.314), channel_id=1, replica_groups=mesh['dp'=8,'fsdp'=4] {'dp'}, dimensions={0}, use_global_device_ids=true | all-gather | bytes 995328 | tf_op jit(solution)/shard_map/all_gather | solution.py:1260
  620.1 8.3 %shard_map.219 = bf16[4,3,144,288]{3,2,1,0:T(8,128)(2,1)} custom-call(s32[1]{0:T(128)} %bitcast.85.at, bf16[1152,1152]{1,0:T(8,128)(2,1)} %bitcast.273, bf16[6,144,1152]{2,1,0:T(8,128)(2,1)S(1)} %concatenate.46.left_root, bf16[3,1152,1152]{2,1,0:T(8,128)(2,1)} %all-gather.12.cloned.1.call-done.right_root), custom_call_target="tpu_custom_call" | custom-call | flops 1024 | bytes 1024 | tf_op jit(solution)/shard_map/pallas_call | solution.py:1008
  637.6 13.2 %all-to-all-done.4 = bf16[4,3,144,288]{3,2,1,0:T(8,128)(2,1)} async-done(((bf16[4,3,144,288]{3,2,1,0:T(8,128)(2,1)}), bf16[4,3,144,288]{3,2,1,0:T(8,128)(2,1)}, u32[]{:S(2)}, u32[]{:S(2)}) %all-to-all-start.4) | async-done | bytes 995360 | tf_op jit(solution)/shard_map/all_to_all | solution.py:842
  650.9 8.3 %shard_map.220 = bf16[4,3,144,288]{3,2,1,0:T(8,128)(2,1)} custom-call(s32[1]{0:T(128)} %bitcast.85.at, bf16[1152,1152]{1,0:T(8,128)(2,1)} %bitcast.275, bf16[6,144,1152]{2,1,0:T(8,128)(2,1)S(1)} %concatenate.46.left_root, bf16[3,1152,1152]{2,1,0:T(8,128)(2,1)} %all-gather.12.cloned.1.call-done.right_root), custom_call_target="tpu_custom_call" | custom-call | flops 1024 | bytes 1024 | tf_op jit(solution)/shard_map/pallas_call | solution.py:1008
  670.4 10.4 %all-to-all-done.5 = bf16[4,3,144,288]{3,2,1,0:T(8,128)(2,1)} async-done(((bf16[4,3,144,288]{3,2,1,0:T(8,128)(2,1)}), bf16[4,3,144,288]{3,2,1,0:T(8,128)(2,1)}, u32[]{:S(2)}, u32[]{:S(2)}) %all-to-all-start.5) | async-done | bytes 995360 | tf_op jit(solution)/shard_map/all_to_all | solution.py:842
  683.3 7.2 %fusion.55 = (bf16[18,144,288]{2,1,0:T(8,128)(2,1)}, f32[18,144,288]{2,1,0:T(8,128)}, f32[18,144,288]{2,1,0:T(8,128)}) fusion(f32[18,144,288]{2,1,0:T(8,128)S(1)} %copy-done.20, f32[4,144,288]{2,1,0:T(8,128)} %get-tuple-element.246, f32[4,144,288]{2,1,0:T(8,128)} %get-tuple-element.243, f32[4,144,288]{2,1,0:T(8,128)S(1)} %get-tuple-element.240, ...), kind=kLoop, calls=%fused_computation.141 | loop fusion | flops 5971968 | bytes 16422912 | tf_op jit(solution)/shard_map/convert_element_type | solution.py:1275
  (377 shorter events, 188.0 us)
Async XLA Ops:
  7.2 133.8 %all-gather.14.cloned.1.call-start = ((), (), s32[]{:S(2)}) async-start(), calls=%async_computation.7 | async-start | bytes 10948608 | tf_op jit(solution)/shard_map/all_gather | solution.py:851
  33.9 211.2 %all-gather.16.cloned.1.call-start = ((), (), s32[]{:S(2)}) async-start(), calls=%async_computation.8 | async-start | bytes 10948608 | tf_op jit(solution)/shard_map/all_gather | solution.py:851
  41.9 343.6 %all-gather.12.cloned.1.call-start = ((), (), s32[]{:S(2)}) async-start(), calls=%async_computation.6 | async-start | bytes 8957952 | tf_op jit(solution)/shard_map/all_gather | solution.py:907
  53.3 26.0 %collective-permute-start.4 = (bf16[144,1152]{1,0:T(8,128)(2,1)S(1)}, bf16[144,1152]{1,0:T(8,128)(2,1)S(1)}, u32[]{:S(2)}, u32[]{:S(2)}) collective-permute-start(bf16[144,1152]{1,0:T(8,128)(2,1)S(1)} %get-tuple-element.124.refs_0_), channel_id=1, source_target_pairs={{0,16},{4,20},{8,24},{12,28},{16,0},{20,4},{24,8},{28,12},{1,17},{... | collective-permute-start | bytes 995336 | tf_op jit(solution)/shard_map/ppermute | solution.py:762
  55.4 23.9 %collective-permute-start.5 = (bf16[144,1152]{1,0:T(8,128)(2,1)S(1)}, bf16[144,1152]{1,0:T(8,128)(2,1)S(1)}, u32[]{:S(2)}, u32[]{:S(2)}) collective-permute-start(bf16[144,1152]{1,0:T(8,128)(2,1)S(1)} %get-tuple-element.124.refs_0_), channel_id=1, source_target_pairs={{0,24},{4,28},{8,0},{12,4},{16,8},{20,12},{24,16},{28,20},{1,25},{... | collective-permute-start | bytes 995336 | tf_op jit(solution)/shard_map/ppermute | solution.py:762
  143.5 44.4 %collective-permute-start.7 = (bf16[576,1152]{1,0:T(8,128)(2,1)}, bf16[576,1152]{1,0:T(8,128)(2,1)S(1)}, u32[]{:S(2)}, u32[]{:S(2)}) collective-permute-start(bf16[576,1152]{1,0:T(8,128)(2,1)} %constant_dynamic-slice_fusion.3), channel_id=1, source_target_pairs={{0,1},{1,0},{2,3},{3,2},{4,5},{5,4},{6,7},{7,6},{8,9},{9,8},{10,11... | collective-permute-start | bytes 3981320 | tf_op jit(solution)/shard_map/ppermute | solution.py:772
  144.9 43.0 %collective-permute-start.8 = (bf16[576,1152]{1,0:T(8,128)(2,1)}, bf16[576,1152]{1,0:T(8,128)(2,1)}, u32[]{:S(2)}, u32[]{:S(2)}) collective-permute-start(bf16[576,1152]{1,0:T(8,128)(2,1)} %constant_dynamic-slice_fusion.3), channel_id=1, source_target_pairs={{0,2},{1,3},{2,0},{3,1},{4,6},{5,7},{6,4},{7,5},{8,10},{9,11},{10,... | collective-permute-start | bytes 3981320 | tf_op jit(solution)/shard_map/ppermute | solution.py:772
  189.6 22.6 %collective-permute-start.11 = (bf16[288,1152]{1,0:T(8,128)(2,1)S(1)}, bf16[288,1152]{1,0:T(8,128)(2,1)S(1)}, u32[]{:S(2)}, u32[]{:S(2)}) collective-permute-start(bf16[288,1152]{1,0:T(8,128)(2,1)S(1)} %slice.141), channel_id=1, source_target_pairs={{0,1},{1,0},{2,3},{3,2},{4,5},{5,4},{6,7},{7,6},{8,9},{9,8},{10,11... | collective-permute-start | bytes 1990664 | tf_op jit(solution)/shard_map/ppermute | solution.py:772
  191.2 23.8 %collective-permute-start.12 = (bf16[288,1152]{1,0:T(8,128)(2,1)S(1)}, bf16[288,1152]{1,0:T(8,128)(2,1)S(1)}, u32[]{:S(2)}, u32[]{:S(2)}) collective-permute-start(bf16[288,1152]{1,0:T(8,128)(2,1)S(1)} %slice.142), channel_id=1, source_target_pairs={{0,2},{1,3},{2,0},{3,1},{4,6},{5,7},{6,4},{7,5},{8,10},{9,11},{10,... | collective-permute-start | bytes 1990664 | tf_op jit(solution)/shard_map/ppermute | solution.py:772
  191.6 25.6 %collective-permute-start.10 = (bf16[576,1152]{1,0:T(8,128)(2,1)}, bf16[576,1152]{1,0:T(8,128)(2,1)}, u32[]{:S(2)}, u32[]{:S(2)}) collective-permute-start(bf16[576,1152]{1,0:T(8,128)(2,1)} %collective-permute-done.8.refs_3_), channel_id=1, source_target_pairs={{0,4},{4,0},{8,12},{12,8},{16,20},{20,16},{24,28},{28,24},{1,5},{5... | collective-permute-start | bytes 3981320 | tf_op jit(solution)/shard_map/ppermute | solution.py:757
  191.6 25.6 %collective-permute-start.9 = (bf16[576,1152]{1,0:T(8,128)(2,1)}, bf16[576,1152]{1,0:T(8,128)(2,1)}, u32[]{:S(2)}, u32[]{:S(2)}) collective-permute-start(bf16[576,1152]{1,0:T(8,128)(2,1)} %copy-done.39), channel_id=1, source_target_pairs={{0,4},{4,0},{8,12},{12,8},{16,20},{20,16},{24,28},{28,24},{1,5},{5... | collective-permute-start | bytes 3981320 | tf_op jit(solution)/shard_map/ppermute | solution.py:757
  240.2 41.2 %collective-permute-start.18 = (bf16[4,576,1152]{2,1,0:T(8,128)(2,1)}, bf16[4,576,1152]{2,1,0:T(8,128)(2,1)}, u32[]{:S(2)}, u32[]{:S(2)}) collective-permute-start(bf16[4,576,1152]{2,1,0:T(8,128)(2,1)} %shard_map.208), channel_id=1, source_target_pairs={{0,4},{4,0},{8,12},{12,8},{16,20},{20,16},{24,28},{28,24},{1,5},{5... | collective-permute-start | bytes 15925256 | tf_op jit(solution)/shard_map/ppermute | solution.py:757
  241.6 26.5 %collective-permute-start.15 = (bf16[6,144,288]{2,1,0:T(8,128)(2,1)}, bf16[6,144,288]{2,1,0:T(8,128)(2,1)}, u32[]{:S(2)}, u32[]{:S(2)}) collective-permute-start(bf16[6,144,288]{2,1,0:T(8,128)(2,1)} %get-tuple-element.238), channel_id=1, source_target_pairs={{0,1},{1,0},{2,3},{3,2},{4,5},{5,4},{6,7},{7,6},{8,9},{9,8},{10,11... | collective-permute-start | bytes 1493000 | tf_op jit(solution)/shard_map/ppermute | solution.py:772
  242.1 31.6 %collective-permute-start.16 = (bf16[6,144,288]{2,1,0:T(8,128)(2,1)}, bf16[6,144,288]{2,1,0:T(8,128)(2,1)}, u32[]{:S(2)}, u32[]{:S(2)}) collective-permute-start(bf16[6,144,288]{2,1,0:T(8,128)(2,1)} %get-tuple-element.237), channel_id=1, source_target_pairs={{0,2},{1,3},{2,0},{3,1},{4,6},{5,7},{6,4},{7,5},{8,10},{9,11},{10,... | collective-permute-start | bytes 1493000 | tf_op jit(solution)/shard_map/ppermute | solution.py:772
  243.5 30.2 %collective-permute-start.17 = (bf16[6,144,288]{2,1,0:T(8,128)(2,1)}, bf16[6,144,288]{2,1,0:T(8,128)(2,1)}, u32[]{:S(2)}, u32[]{:S(2)}) collective-permute-start(bf16[6,144,288]{2,1,0:T(8,128)(2,1)} %get-tuple-element.236), channel_id=1, source_target_pairs={{0,3},{1,2},{2,1},{3,0},{4,7},{5,6},{6,5},{7,4},{8,11},{9,10},{10,... | collective-permute-start | bytes 1493000 | tf_op jit(solution)/shard_map/ppermute | solution.py:772
  302.4 31.9 %collective-permute-start.20 = (bf16[2,288,1152]{2,1,0:T(8,128)(2,1)}, bf16[2,288,1152]{2,1,0:T(8,128)(2,1)}, u32[]{:S(2)}, u32[]{:S(2)}) collective-permute-start(bf16[2,288,1152]{2,1,0:T(8,128)(2,1)} %get-tuple-element.164), channel_id=1, source_target_pairs={{0,1},{1,0},{2,3},{3,2},{4,5},{5,4},{6,7},{7,6},{8,9},{9,8},{10,11... | collective-permute-start | bytes 3981320 | tf_op jit(solution)/shard_map/ppermute | solution.py:772
  303.8 31.6 %collective-permute-start.21 = (bf16[2,288,1152]{2,1,0:T(8,128)(2,1)}, bf16[2,288,1152]{2,1,0:T(8,128)(2,1)}, u32[]{:S(2)}, u32[]{:S(2)}) collective-permute-start(bf16[2,288,1152]{2,1,0:T(8,128)(2,1)} %get-tuple-element.165), channel_id=1, source_target_pairs={{0,2},{1,3},{2,0},{3,1},{4,6},{5,7},{6,4},{7,5},{8,10},{9,11},{10,... | collective-permute-start | bytes 3981320 | tf_op jit(solution)/shard_map/ppermute | solution.py:772
  337.1 32.1 %collective-permute-start.23 = (bf16[2,144,1152]{2,1,0:T(8,128)(2,1)S(1)}, bf16[2,144,1152]{2,1,0:T(8,128)(2,1)S(1)}, u32[]{:S(2)}, u32[]{:S(2)}) collective-permute-start(bf16[2,144,1152]{2,1,0:T(8,128)(2,1)S(1)} %dynamic-slice_bitcast_fusion.7), channel_id=1, source_target_pairs={{0,1},{1,0},{2,3},{3,2},{4,5},{5,4},{6,7},{7,6},{8,9},{9,8},{10,11... | collective-permute-start | bytes 1990664 | tf_op jit(solution)/shard_map/ppermute | solution.py:772
  337.8 45.8 %collective-permute-start.24 = (bf16[2,288,1152]{2,1,0:T(8,128)(2,1)S(1)}, bf16[2,288,1152]{2,1,0:T(8,128)(2,1)S(1)}, u32[]{:S(2)}, u32[]{:S(2)}) collective-permute-start(bf16[2,288,1152]{2,1,0:T(8,128)(2,1)S(1)} %get-tuple-element.173), channel_id=1, source_target_pairs={{0,1},{1,0},{2,3},{3,2},{4,5},{5,4},{6,7},{7,6},{8,9},{9,8},{10,11... | collective-permute-start | bytes 3981320 | tf_op jit(solution)/shard_map/ppermute | solution.py:772
  339.2 46.2 %collective-permute-start.25 = (bf16[2,288,1152]{2,1,0:T(8,128)(2,1)}, bf16[2,288,1152]{2,1,0:T(8,128)(2,1)}, u32[]{:S(2)}, u32[]{:S(2)}) collective-permute-start(bf16[2,288,1152]{2,1,0:T(8,128)(2,1)} %get-tuple-element.174), channel_id=1, source_target_pairs={{0,2},{1,3},{2,0},{3,1},{4,6},{5,7},{6,4},{7,5},{8,10},{9,11},{10,... | collective-permute-start | bytes 3981320 | tf_op jit(solution)/shard_map/ppermute | solution.py:772
  341.4 42.1 %collective-permute-start.22 = (bf16[2,144,1152]{2,1,0:T(8,128)(2,1)S(1)}, bf16[2,144,1152]{2,1,0:T(8,128)(2,1)S(1)}, u32[]{:S(2)}, u32[]{:S(2)}) collective-permute-start(bf16[2,144,1152]{2,1,0:T(8,128)(2,1)S(1)} %dynamic-slice_bitcast_fusion.8), channel_id=1, source_target_pairs={{0,2},{1,3},{2,0},{3,1},{4,6},{5,7},{6,4},{7,5},{8,10},{9,11},{10,... | collective-permute-start | bytes 1990664 | tf_op jit(solution)/shard_map/ppermute | solution.py:772
  395.6 26.1 %collective-permute-start.26 = (bf16[4,576,1152]{2,1,0:T(8,128)(2,1)}, bf16[4,576,1152]{2,1,0:T(8,128)(2,1)}, u32[]{:S(2)}, u32[]{:S(2)}) collective-permute-start(bf16[4,576,1152]{2,1,0:T(8,128)(2,1)} %shard_map.215), channel_id=1, source_target_pairs={{0,4},{4,0},{8,12},{12,8},{16,20},{20,16},{24,28},{28,24},{1,5},{5... | collective-permute-start | bytes 15925256 | tf_op jit(solution)/shard_map/ppermute | solution.py:757
  430.7 102.9 %all-gather.18.cloned.1.call-start = ((), (), s32[]{:S(2)}) async-start(), calls=%async_computation.9 | async-start | bytes 2985984 | tf_op jit(solution)/shard_map/all_gather | solution.py:961
  454.4 44.8 %collective-permute-start.31 = (bf16[2,288,1152]{2,1,0:T(8,128)(2,1)}, bf16[2,288,1152]{2,1,0:T(8,128)(2,1)}, u32[]{:S(2)}, u32[]{:S(2)}) collective-permute-start(bf16[2,288,1152]{2,1,0:T(8,128)(2,1)} %get-tuple-element.203), channel_id=1, source_target_pairs={{0,1},{1,0},{2,3},{3,2},{4,5},{5,4},{6,7},{7,6},{8,9},{9,8},{10,11... | collective-permute-start | bytes 3981320 | tf_op jit(solution)/shard_map/ppermute | solution.py:772
  454.7 44.5 %collective-permute-start.32 = (bf16[2,288,1152]{2,1,0:T(8,128)(2,1)}, bf16[2,288,1152]{2,1,0:T(8,128)(2,1)}, u32[]{:S(2)}, u32[]{:S(2)}) collective-permute-start(bf16[2,288,1152]{2,1,0:T(8,128)(2,1)} %get-tuple-element.204), channel_id=1, source_target_pairs={{0,2},{1,3},{2,0},{3,1},{4,6},{5,7},{6,4},{7,5},{8,10},{9,11},{10,... | collective-permute-start | bytes 3981320 | tf_op jit(solution)/shard_map/ppermute | solution.py:772
  458.2 161.9 %all-gather.22.cloned.1.call-start = ((), (), s32[]{:S(2)}) async-start(), calls=%async_computation.11 | async-start | bytes 2985984 | tf_op jit(solution)/shard_map/all_gather | solution.py:961
  459.8 39.4 %collective-permute-start.33 = (bf16[2,144,1152]{2,1,0:T(8,128)(2,1)S(1)}, bf16[2,144,1152]{2,1,0:T(8,128)(2,1)S(1)}, u32[]{:S(2)}, u32[]{:S(2)}) collective-permute-start(bf16[2,144,1152]{2,1,0:T(8,128)(2,1)S(1)} %dynamic-slice_bitcast_fusion.3), channel_id=1, source_target_pairs={{0,8},{4,12},{8,0},{12,4},{16,24},{20,28},{24,16},{28,20},{1,9},{5... | collective-permute-start | bytes 1990664 | tf_op jit(solution)/shard_map/ppermute | solution.py:767
  501.8 26.1 %collective-permute-start.35 = (bf16[2,144,1152]{2,1,0:T(8,128)(2,1)}, bf16[2,144,1152]{2,1,0:T(8,128)(2,1)}, u32[]{:S(2)}, u32[]{:S(2)}) collective-permute-start(bf16[2,144,1152]{2,1,0:T(8,128)(2,1)} %dynamic-slice_bitcast_fusion.1), channel_id=1, source_target_pairs={{0,1},{1,0},{2,3},{3,2},{4,5},{5,4},{6,7},{7,6},{8,9},{9,8},{10,11... | collective-permute-start | bytes 1990664 | tf_op jit(solution)/shard_map/ppermute | solution.py:772
  505.1 22.8 %collective-permute-start.34 = (bf16[2,144,1152]{2,1,0:T(8,128)(2,1)}, bf16[2,144,1152]{2,1,0:T(8,128)(2,1)}, u32[]{:S(2)}, u32[]{:S(2)}) collective-permute-start(bf16[2,144,1152]{2,1,0:T(8,128)(2,1)} %dynamic-slice_bitcast_fusion.2), channel_id=1, source_target_pairs={{0,2},{1,3},{2,0},{3,1},{4,6},{5,7},{6,4},{7,5},{8,10},{9,11},{10,... | collective-permute-start | bytes 1990664 | tf_op jit(solution)/shard_map/ppermute | solution.py:772
  533.6 36.4 %collective-permute-start.37 = (bf16[2,144,1152]{2,1,0:T(8,128)(2,1)}, bf16[2,144,1152]{2,1,0:T(8,128)(2,1)}, u32[]{:S(2)}, u32[]{:S(2)}) collective-permute-start(bf16[2,144,1152]{2,1,0:T(8,128)(2,1)} %dynamic-slice_bitcast_fusion), channel_id=1, source_target_pairs={{0,8},{4,12},{8,0},{12,4},{16,24},{20,28},{24,16},{28,20},{1,9},{5... | collective-permute-start | bytes 1990664 | tf_op jit(solution)/shard_map/ppermute | solution.py:767
  574.3 76.5 %all-gather.20.cloned.1.call-start = ((), (), s32[]{:S(2)}) async-start(), calls=%async_computation.10 | async-start | bytes 2985984 | tf_op jit(solution)/shard_map/all_gather | solution.py:961
  628.4 22.5 %all-to-all-start.4 = ((bf16[4,3,144,288]{3,2,1,0:T(8,128)(2,1)}), bf16[4,3,144,288]{3,2,1,0:T(8,128)(2,1)}, u32[]{:S(2)}, u32[]{:S(2)}) async-start(bf16[4,3,144,288]{3,2,1,0:T(8,128)(2,1)} %shard_map.219), calls=%async_computation.4 | async-start | bytes 2654208 | tf_op jit(solution)/shard_map/all_to_all | solution.py:842
  (83 other events, 667.9 us)
Sparse Core Ops, SparseCore 0:
  34.1 106.8 all-gather.13
  144.6 96.4 all-gather.15
  282.6 76.5 all-gather.11
  458.3 41.9 all-gather.17
  529.9 39.8 all-gather.21
  589.2 39.7 all-gather.19

commit v20 on v17

--- a/solution.py
+++ b/solution.py
@@ -1159,14 +1159,12 @@
     two_parts = two_steps.send(two_parts)
     one_parts = one_steps.send(one_parts)
     d_heads, head_sums = run_attention_back(frames, frame_counts, d_proj, parts, attn_w)
-    d_heads, two_parts, one_parts, right_wholes = tie(
-        d_heads, two_parts, one_parts, right_wholes
-    )
-    two_parts = two_steps.send(two_parts)
+    d_heads, one_parts, right_wholes = tie(d_heads, one_parts, right_wholes)
     one_parts = one_steps.send(one_parts)
     attn_steps = sum_blocks([attn_in, mixed], [0, 0, 0, 1], d_heads, group)
     attn_parts = next(attn_steps)
-    d_heads, attn_parts = tie(d_heads, attn_parts)
+    d_heads, attn_parts, two_parts = tie(d_heads, attn_parts, two_parts)
+    two_parts = two_steps.send(two_parts)
     attn_parts = attn_steps.send(attn_parts)
     input_grad, input_sums = run_input(d_heads, attn_w, mods, stream, d_resid)
     input_sums, attn_parts, two_parts, one_parts = tie(

time: 695 us -> 684 us (0.984)
  waiting for transfers between devices: 213 us -> 198 us
    ppermute x22, waiting for transfers between devices: 49.7 us -> 35.3 us  [rank_swap(): return lax.ppermute(array, 'fsdp', [(at, at ^ bits) for at in range(count)])]
    unnamed x131 -> x123, local copies, waits for them, and re-layouts: 18.8 us -> 17.4 us
  transfers between devices with their start and end apart: 51 -> 51, of which waited for: 20 -> 18; matrix products, arithmetic and copies ran while one was open for 11% -> 12% of each run, Pallas kernels for 27% -> 29%
where the time goes in v20:
time: 684 us; the launch traced here: 677 us
  Pallas kernels  215 us (31%)
  waiting for transfers between devices  198 us (29%)
  other arithmetic  61.8 us (9%)
  blocking collectives  60.6 us (9%)
  starting transfers between devices  57.8 us (8%)
  local copies, waits for them, and re-layouts  55 us (8%)
  between operations  15.8 us (2%)
  matrix products  13.1 us (2%)
    ppermute x6, waiting for transfers between devices, chip_swap(): lax.ppermute(array, 'dp', [(at, at ^ 2 * bits) for at in range(count)])  56.8 us
    pallas_call x6, Pallas kernels, run_halves(): pl.pallas_call(body, grid_spec=pltpu.PrefetchScalarGridSpec(num_scalar_pr...  55.1 us
    all_gather x2, waiting for transfers between devices, gather_blocks(): all_rows = lax.all_gather(rows, ('fsdp', 'dp'), axis=0, tiled=True)  52.1 us
    pallas_call x1, Pallas kernels, run_attention(): pl.pallas_call(functools.partial(attention_kernel, frames), grid=(clips,)...  41.2 us
    ppermute x22, waiting for transfers between devices, rank_swap(): return lax.ppermute(array, 'fsdp', [(at, at ^ bits) for at in range(count)])  35.3 us
    convert_element_type x21, other arithmetic, narrow(): return array.astype(jnp.bfloat16)  31.8 us
    pallas_call x1, Pallas kernels, run_attention_back(): pl.pallas_call(functools.partial(attention_back_kernel, frames), grid=(cl...  26.1 us
    pallas_call x3, Pallas kernels, owned_step(): pl.pallas_call(functools.partial(products_kernel, dp_count // 2), in_spec...  25.1 us
  transfers between devices with their start and end apart: 51, of which 18 were waited for; matrix products, arithmetic and copies ran while one was open for 12% of the time, Pallas kernels for 29%

profile of v20, /device:TPU:0, one launch (start us, length us, event | category | flops | bytes accessed | tf_op | source)
XLA Modules:
  0.0 676.9 jit_solution(13257094655440571723)
XLA Ops:
  17.2 14.7 %all_gather.30 = bf16[256,128]{1,0:T(8,128)(2,1)S(1)} all-gather(bf16[32,128]{1,0:T(8,128)(2,1)S(1)} %fusion.49), channel_id=1, replica_groups=mesh['dp'=8,'fsdp'=4] {'dp'}, dimensions={0}, use_global_device_ids=true | all-gather | bytes 73728 | tf_op jit(solution)/shard_map/all_gather | solution.py:1071
  37.0 4.9 all-to-all-start
  44.5 8.7 %all-to-all-done = f32[16,6,288]{2,1,0:T(8,128)S(1)} async-done(((f32[16,6,288]{2,1,0:T(8,128)}), f32[16,6,288]{2,1,0:T(8,128)S(1)}, u32[]{:S(2)}, u32[]{:S(2)}) %all-to-all-start) | async-done | bytes 110624 | tf_op jit(solution)/shard_map/all_to_all | solution.py:1089
  57.4 9.8 %all_gather.31 = f32[672,128]{1,0:T(8,128)S(1)} all-gather(f32[168,128]{1,0:T(8,128)S(1)} %pad_bitcast_fusion), channel_id=1, replica_groups=mesh['dp'=8,'fsdp'=4] {'fsdp'}, dimensions={0}, use_global_device_ids=true | all-gather | bytes 430080 | tf_op jit(solution)/shard_map/all_gather | solution.py:1096
  67.2 12.1 %collective-permute-done.4.refs_2_ = bf16[144,1152]{1,0:T(8,128)(2,1)S(1)} collective-permute-done((bf16[144,1152]{1,0:T(8,128)(2,1)S(1)}, bf16[144,1152]{1,0:T(8,128)(2,1)S(1)}, u32[]{:S(2)}, u32[]{:S(2)}) %collective-permute-start.4) | collective-permute-done | bytes 331808 | tf_op jit(solution)/shard_map/ppermute | solution.py:762
  89.0 52.0 %all-gather.14.cloned.1.call-done = bf16[1,4608,1152]{2,1,0:T(8,128)(2,1)} async-done(((bf16[1,144,1152]{2,1,0:T(8,128)(2,1)}), bf16[1,4608,1152]{2,1,0:T(8,128)(2,1)}) %all-gather.14.cloned.1.call-update) | async-done | bytes 10616848 | tf_op jit(solution)/shard_map/all_gather | solution.py:851
  146.6 41.2 %shard_map.206 = (bf16[512,1152]{1,0:T(8,128)(2,1)S(1)}, bf16[5,512,1152]{2,1,0:T(8,128)(2,1)}, bf16[512,1152]{1,0:T(8,128)(2,1)S(1)}, f32[512,1152]{1,0:T(8,128...) custom-call(s32[2]{0:T(128)S(1)} %copy-done.19, ...), custom_call_target="tpu_custom_call" | custom-call | flops 1024 | bytes 1024 | tf_op jit(solution)/shard_map/pallas_call | solution.py:216
  192.1 20.0 %collective-permute-done.11.refs_5_ = bf16[288,1152]{1,0:T(8,128)(2,1)S(1)} collective-permute-done((bf16[288,1152]{1,0:T(8,128)(2,1)S(1)}, bf16[288,1152]{1,0:T(8,128)(2,1)S(1)}, u32[]{:S(2)}, u32[]{:S(2)}) %collective-permute-start.11) | collective-permute-done | bytes 663584 | tf_op jit(solution)/shard_map/ppermute | solution.py:772
  217.2 13.9 %shard_map.207 = (bf16[4608,1152]{1,0:T(8,128)(2,1)}, bf16[4,512,1152]{2,1,0:T(8,128)(2,1)}, bf16[4,512,1152]{2,1,0:T(8,128)(2,1)}) custom-call(s32[4]{0:T(128)S(1)} %get-tuple-element.266.order, s32[9]{0:T(128)S(1)} %stack.97.starts, bf16[512,1152]{1,0:T(8,128)(2,1)S(1)} %get-tuple-element.132.mlp_in.refs_0_, f32[4,1,1152]{2,1,0:T(1,128)S(1)} %copy.92.bias, ...), custom_call_target="tpu_custom_call" | custom-call | flops 1024 | bytes 1024 | tf_op jit(solution)/shard_map/pallas_call | solution.py:324
  231.1 9.0 %shard_map.208 = bf16[4,576,1152]{2,1,0:T(8,128)(2,1)} custom-call(s32[4]{0:T(128)S(1)} %get-tuple-element.267.order, s32[1]{0:T(128)} %bitcast.45.side, s32[16]{0:T(128)S(1)} %stack.121.table, bf16[4,512,1152]{2,1,0:T(8,128)(2,1)} %get-tuple-element.138.refs_0_.hidden, bf16[512,1152]{1,0:T(8,128)(2,1)S(1)} %copy-done.2), custom_call_target="tpu_custom_call" | custom-call | flops 1024 | bytes 1024 | tf_op jit(solution)/shard_map/pallas_call | solution.py:728
  246.4 21.6 %shard_map.209 = (bf16[4,512,1152]{2,1,0:T(8,128)(2,1)}, f32[4,1,1152]{2,1,0:T(1,128)S(1)}, bf16[512,1152]{1,0:T(8,128)(2,1)}, f32[2,1,1152]{2,1,0:T(1,128)S(1)}) custom-call(s32[4]{0:T(128)S(1)} %iota.6.order, s32[4]{0:T(128)S(1)} %iota_multiply_fusion.starts, s32[2]{0:T(128)S(1)} %copy-done.19, bf16[4,512,1152]{2,1,0:T(8,128)(2,1)} %get-tuple-element.138.refs_0_.hidden, ...), custom_call_target="tpu_custom_call" | custom-call | flops 1024 | bytes 1024 | tf_op jit(solution)/shard_map/pallas_call | solution.py:404
  268.0 5.7 collective-permute-done.16
  283.8 10.1 %shard_map.210 = (bf16[2,288,1152]{2,1,0:T(8,128)(2,1)S(1)}, bf16[2,288,1152]{2,1,0:T(8,128)(2,1)}, bf16[2,288,1152]{2,1,0:T(8,128)(2,1)}, bf16[2,288,1152]{2,1,0:T(8,128)(2,1)}) custom-call(s32[4]{0:T(128)S(1)} %get-tuple-element.267.order, s32[1]{0:T(128)} %bitcast.57.side, s32[16]{0:T(128)S(1)} %stack.121.table, ...), custom_call_target="tpu_custom_call" | custom-call | flops 1024 | bytes 1024 | tf_op jit(solution)/shard_map/pallas_call | solution.py:728
  293.9 8.5 %shard_map.211 = bf16[4,576,1152]{2,1,0:T(8,128)(2,1)} custom-call(s32[4]{0:T(128)S(1)} %get-tuple-element.267.order, s32[1]{0:T(128)} %bitcast.45.side, s32[16]{0:T(128)S(1)} %stack.121.table, bf16[512,1152]{1,0:T(8,128)(2,1)S(1)} %get-tuple-element.132.mlp_in.refs_0_, bf16[4,512,1152]{2,1,0:T(8,128)(2,1)} %get-tuple-element.155.refs_1_.d_pre), custom_call_target="tpu_custom_call" | custom-call | flops 1024 | bytes 1024 | tf_op jit(solution)/shard_map/pallas_call | solution.py:728
  305.5 15.7 %shard_map.212 = (f32[512,1152]{1,0:T(8,128)}, bf16[512,1152]{1,0:T(8,128)(2,1)S(1)}, f32[2,4,1152]{2,1,0:T(4,128)S(1)}) custom-call(s32[2]{0:T(128)S(1)} %copy-done.19, bf16[4,512,1152]{2,1,0:T(8,128)(2,1)} %get-tuple-element.155.refs_1_.d_pre, bf16[4,1152,1152]{2,1,0:T(8,128)(2,1)} %bitcast.251, f32[2,6,1152]{2,1,0:T(8,128)S(1)} %broadcast_add_fusion.mods, ...), custom_call_target="tpu_custom_call" | custom-call | flops 1024 | bytes 1024 | tf_op jit(solution)/shard_map/pallas_call | solution.py:496
  321.2 8.9 %shard_map.213 = (bf16[2,288,1152]{2,1,0:T(8,128)(2,1)S(1)}, bf16[2,288,1152]{2,1,0:T(8,128)(2,1)S(1)}, bf16[2,288,1152]{2,1,0:T(8,128)(2,1)}, bf16[2,288,1152]{2,1,0:T(8,128)(2,1)}) custom-call(s32[4]{0:T(128)S(1)} %get-tuple-element.267.order, s32[1]{0:T(128)} %bitcast.57.side, s32[16]{0:T(128)S(1)} %stack.121.table, ...), custom_call_target="tpu_custom_call" | custom-call | flops 1024 | bytes 1024 | tf_op jit(solution)/shard_map/pallas_call | solution.py:728
  344.7 26.1 %shard_map.214 = (bf16[4,512,1152]{2,1,0:T(8,128)(2,1)}, f32[2,3,1152]{2,1,0:T(4,128)S(1)}) custom-call(s32[2]{0:T(128)S(1)} %copy-done.19, bf16[512,1152]{1,0:T(8,128)(2,1)S(1)} %get-tuple-element.166.d_proj, bf16[5,512,1152]{2,1,0:T(8,128)(2,1)} %get-tuple-element.167.parts, bf16[4,1152,1152]{2,1,0:T(8,128)(2,1)} %bitcast.248), custom_call_target="tpu_custom_call" | custom-call | flops 1024 | bytes 1024 | tf_op jit(solution)/shard_map/pallas_call | solution.py:563
  373.1 8.9 %shard_map.215 = bf16[4,576,1152]{2,1,0:T(8,128)(2,1)} custom-call(s32[4]{0:T(128)S(1)} %get-tuple-element.267.order, s32[1]{0:T(128)} %bitcast.45.side, s32[16]{0:T(128)S(1)} %stack.121.table, bf16[512,1152]{1,0:T(8,128)(2,1)S(1)} %copy-done.7, bf16[512,1152]{1,0:T(8,128)(2,1)S(1)} %copy-done.10, bf16[4,512,1152]{2,1,0:T(8,128)(2,1)} %get-tuple-element.179.refs_2_.d_qkv), custom_call_target="tpu_custom_call" | custom-call | flops 1024 | bytes 1024 | tf_op jit(solution)/shard_map/pallas_call | solution.py:728
  395.5 11.5 %shard_map.216 = (bf16[512,1152]{1,0:T(8,128)(2,1)}, f32[2,2,1152]{2,1,0:T(2,128)S(1)}) custom-call(bf16[4,512,1152]{2,1,0:T(8,128)(2,1)} %get-tuple-element.179.refs_2_.d_qkv, bf16[4,1152,1152]{2,1,0:T(8,128)(2,1)} %bitcast.249, f32[2,6,1152]{2,1,0:T(8,128)S(1)} %broadcast_add_fusion.mods, bf16[512,1152]{1,0:T(8,128)(2,1)S(1)} %bitcast.246, ...), custom_call_target="tpu_custom_call" | custom-call | flops 1024 | bytes 1024 | tf_op jit(solution)/shard_map/pallas_call | solution.py:623
  427.0 9.6 %shard_map.217 = (bf16[2,288,1152]{2,1,0:T(8,128)(2,1)S(1)}, bf16[2,288,1152]{2,1,0:T(8,128)(2,1)}, bf16[2,288,1152]{2,1,0:T(8,128)(2,1)}, bf16[2,288,1152]{2,1,0:T(8,128)(2,1)}) custom-call(s32[4]{0:T(128)S(1)} %get-tuple-element.267.order, s32[1]{0:T(128)} %bitcast.57.side, s32[16]{0:T(128)S(1)} %stack.121.table, bf16[512,1152]{1,0:T(8,128)(2,1)S(1)} %copy-done.8, ...), custom_call_target="tpu_custom_call" | custom-call | flops 1024 | bytes 1024 | tf_op jit(solution)/shard_map/pallas_call | solution.py:728
  449.8 16.9 %all-to-all-done.2 = f32[8,1,3960]{2,1,0:T(1,128)S(1)} async-done(((f32[8,1,3960]{2,1,0:T(1,128)}), f32[8,1,3960]{2,1,0:T(1,128)S(1)}, u32[]{:S(2)}, u32[]{:S(2)}) %all-to-all-start.2) | async-done | bytes 126752 | tf_op jit(solution)/shard_map/all_to_all | solution.py:1222
  482.7 15.8 %all_gather.35 = f32[864,128]{1,0:T(8,128)} all-gather(f32[216,128]{1,0:T(8,128)} %reshape.302), channel_id=1, replica_groups=mesh['dp'=8,'fsdp'=4] {'fsdp'}, dimensions={0}, use_global_device_ids=true | all-gather | bytes 552960 | tf_op jit(solution)/shard_map/all_gather | solution.py:1229
  498.5 15.9 %collective-permute-done.36 = bf16[1,144,1152]{2,1,0:T(8,128)(2,1)} collective-permute-done((bf16[1,144,1152]{2,1,0:T(8,128)(2,1)}, bf16[1,144,1152]{2,1,0:T(8,128)(2,1)}, u32[]{:S(2)}, u32[]{:S(2)}) %collective-permute-start.36) | collective-permute-done | bytes 331808 | tf_op jit(solution)/shard_map/ppermute | solution.py:767
  520.1 8.3 %shard_map.218 = bf16[4,3,144,288]{3,2,1,0:T(8,128)(2,1)} custom-call(s32[1]{0:T(128)} %bitcast.85.at, bf16[1152,1152]{1,0:T(8,128)(2,1)} %bitcast.274, bf16[6,144,1152]{2,1,0:T(8,128)(2,1)S(1)} %concatenate.46.left_root, bf16[3,1152,1152]{2,1,0:T(8,128)(2,1)} %all-gather.12.cloned.1.call-done.right_root), custom_call_target="tpu_custom_call" | custom-call | flops 1024 | bytes 1024 | tf_op jit(solution)/shard_map/pallas_call | solution.py:1008
  528.4 27.8 %collective-permute-done.37 = bf16[2,144,1152]{2,1,0:T(8,128)(2,1)} collective-permute-done((bf16[2,144,1152]{2,1,0:T(8,128)(2,1)}, bf16[2,144,1152]{2,1,0:T(8,128)(2,1)}, u32[]{:S(2)}, u32[]{:S(2)}) %collective-permute-start.37) | collective-permute-done | bytes 663584 | tf_op jit(solution)/shard_map/ppermute | solution.py:767
  562.8 10.2 %collective-permute-done.38 = bf16[1,144,1152]{2,1,0:T(8,128)(2,1)S(1)} collective-permute-done((bf16[1,144,1152]{2,1,0:T(8,128)(2,1)S(1)}, bf16[1,144,1152]{2,1,0:T(8,128)(2,1)S(1)}, u32[]{:S(2)}, u32[]{:S(2)}) %collective-permute-start.38) | collective-permute-done | bytes 331808 | tf_op jit(solution)/shard_map/ppermute | solution.py:767
  578.4 8.5 %shard_map.219 = bf16[4,3,144,288]{3,2,1,0:T(8,128)(2,1)} custom-call(s32[1]{0:T(128)} %bitcast.85.at, bf16[1152,1152]{1,0:T(8,128)(2,1)} %bitcast.273, bf16[6,144,1152]{2,1,0:T(8,128)(2,1)S(1)} %concatenate.46.left_root, bf16[3,1152,1152]{2,1,0:T(8,128)(2,1)} %all-gather.12.cloned.1.call-done.right_root), custom_call_target="tpu_custom_call" | custom-call | flops 1024 | bytes 1024 | tf_op jit(solution)/shard_map/pallas_call | solution.py:1008
  586.9 4.5 all-to-all-start.4
  595.0 20.4 %all_gather.39 = f32[1728,128]{1,0:T(8,128)} all-gather(f32[216,128]{1,0:T(8,128)S(1)} %reshape.314), channel_id=1, replica_groups=mesh['dp'=8,'fsdp'=4] {'dp'}, dimensions={0}, use_global_device_ids=true | all-gather | bytes 995328 | tf_op jit(solution)/shard_map/all_gather | solution.py:1258
  623.2 8.3 %shard_map.220 = bf16[4,3,144,288]{3,2,1,0:T(8,128)(2,1)} custom-call(s32[1]{0:T(128)} %bitcast.85.at, bf16[1152,1152]{1,0:T(8,128)(2,1)} %bitcast.275, bf16[6,144,1152]{2,1,0:T(8,128)(2,1)S(1)} %concatenate.46.left_root, bf16[3,1152,1152]{2,1,0:T(8,128)(2,1)} %all-gather.12.cloned.1.call-done.right_root), custom_call_target="tpu_custom_call" | custom-call | flops 1024 | bytes 1024 | tf_op jit(solution)/shard_map/pallas_call | solution.py:1008
  642.5 11.0 %all-to-all-done.5 = bf16[4,3,144,288]{3,2,1,0:T(8,128)(2,1)} async-done(((bf16[4,3,144,288]{3,2,1,0:T(8,128)(2,1)}), bf16[4,3,144,288]{3,2,1,0:T(8,128)(2,1)}, u32[]{:S(2)}, u32[]{:S(2)}) %all-to-all-start.5) | async-done | bytes 995360 | tf_op jit(solution)/shard_map/all_to_all | solution.py:842
  656.1 7.2 %fusion.55 = (bf16[18,144,288]{2,1,0:T(8,128)(2,1)}, f32[18,144,288]{2,1,0:T(8,128)}, f32[18,144,288]{2,1,0:T(8,128)}) fusion(f32[18,144,288]{2,1,0:T(8,128)S(1)} %copy-done.20, f32[4,144,288]{2,1,0:T(8,128)} %get-tuple-element.246, f32[4,144,288]{2,1,0:T(8,128)} %get-tuple-element.243, f32[4,144,288]{2,1,0:T(8,128)S(1)} %get-tuple-element.240, ...), kind=kLoop, calls=%fused_computation.141 | loop fusion | flops 5971968 | bytes 16422912 | tf_op jit(solution)/shard_map/convert_element_type | solution.py:1273
  (368 shorter events, 193.5 us)
Async XLA Ops:
  7.2 133.8 %all-gather.14.cloned.1.call-start = ((), (), s32[]{:S(2)}) async-start(), calls=%async_computation.7 | async-start | bytes 10948608 | tf_op jit(solution)/shard_map/all_gather | solution.py:851
  33.9 211.2 %all-gather.16.cloned.1.call-start = ((), (), s32[]{:S(2)}) async-start(), calls=%async_computation.8 | async-start | bytes 10948608 | tf_op jit(solution)/shard_map/all_gather | solution.py:851
  41.9 329.9 %all-gather.12.cloned.1.call-start = ((), (), s32[]{:S(2)}) async-start(), calls=%async_computation.6 | async-start | bytes 8957952 | tf_op jit(solution)/shard_map/all_gather | solution.py:907
  53.3 26.0 %collective-permute-start.4 = (bf16[144,1152]{1,0:T(8,128)(2,1)S(1)}, bf16[144,1152]{1,0:T(8,128)(2,1)S(1)}, u32[]{:S(2)}, u32[]{:S(2)}) collective-permute-start(bf16[144,1152]{1,0:T(8,128)(2,1)S(1)} %get-tuple-element.124.refs_0_), channel_id=1, source_target_pairs={{0,16},{4,20},{8,24},{12,28},{16,0},{20,4},{24,8},{28,12},{1,17},{... | collective-permute-start | bytes 995336 | tf_op jit(solution)/shard_map/ppermute | solution.py:762
  55.4 23.9 %collective-permute-start.5 = (bf16[144,1152]{1,0:T(8,128)(2,1)S(1)}, bf16[144,1152]{1,0:T(8,128)(2,1)S(1)}, u32[]{:S(2)}, u32[]{:S(2)}) collective-permute-start(bf16[144,1152]{1,0:T(8,128)(2,1)S(1)} %get-tuple-element.124.refs_0_), channel_id=1, source_target_pairs={{0,24},{4,28},{8,0},{12,4},{16,8},{20,12},{24,16},{28,20},{1,25},{... | collective-permute-start | bytes 995336 | tf_op jit(solution)/shard_map/ppermute | solution.py:762
  143.5 44.4 %collective-permute-start.7 = (bf16[576,1152]{1,0:T(8,128)(2,1)}, bf16[576,1152]{1,0:T(8,128)(2,1)S(1)}, u32[]{:S(2)}, u32[]{:S(2)}) collective-permute-start(bf16[576,1152]{1,0:T(8,128)(2,1)} %constant_dynamic-slice_fusion.3), channel_id=1, source_target_pairs={{0,1},{1,0},{2,3},{3,2},{4,5},{5,4},{6,7},{7,6},{8,9},{9,8},{10,11... | collective-permute-start | bytes 3981320 | tf_op jit(solution)/shard_map/ppermute | solution.py:772
  144.9 43.0 %collective-permute-start.8 = (bf16[576,1152]{1,0:T(8,128)(2,1)}, bf16[576,1152]{1,0:T(8,128)(2,1)}, u32[]{:S(2)}, u32[]{:S(2)}) collective-permute-start(bf16[576,1152]{1,0:T(8,128)(2,1)} %constant_dynamic-slice_fusion.3), channel_id=1, source_target_pairs={{0,2},{1,3},{2,0},{3,1},{4,6},{5,7},{6,4},{7,5},{8,10},{9,11},{10,... | collective-permute-start | bytes 3981320 | tf_op jit(solution)/shard_map/ppermute | solution.py:772
  191.2 23.8 %collective-permute-start.12 = (bf16[288,1152]{1,0:T(8,128)(2,1)S(1)}, bf16[288,1152]{1,0:T(8,128)(2,1)S(1)}, u32[]{:S(2)}, u32[]{:S(2)}) collective-permute-start(bf16[288,1152]{1,0:T(8,128)(2,1)S(1)} %slice.142), channel_id=1, source_target_pairs={{0,2},{1,3},{2,0},{3,1},{4,6},{5,7},{6,4},{7,5},{8,10},{9,11},{10,... | collective-permute-start | bytes 1990664 | tf_op jit(solution)/shard_map/ppermute | solution.py:772
  191.6 25.6 %collective-permute-start.10 = (bf16[576,1152]{1,0:T(8,128)(2,1)}, bf16[576,1152]{1,0:T(8,128)(2,1)}, u32[]{:S(2)}, u32[]{:S(2)}) collective-permute-start(bf16[576,1152]{1,0:T(8,128)(2,1)} %collective-permute-done.8.refs_3_), channel_id=1, source_target_pairs={{0,4},{4,0},{8,12},{12,8},{16,20},{20,16},{24,28},{28,24},{1,5},{5... | collective-permute-start | bytes 3981320 | tf_op jit(solution)/shard_map/ppermute | solution.py:757
  191.6 25.6 %collective-permute-start.9 = (bf16[576,1152]{1,0:T(8,128)(2,1)}, bf16[576,1152]{1,0:T(8,128)(2,1)}, u32[]{:S(2)}, u32[]{:S(2)}) collective-permute-start(bf16[576,1152]{1,0:T(8,128)(2,1)} %copy-done.41), channel_id=1, source_target_pairs={{0,4},{4,0},{8,12},{12,8},{16,20},{20,16},{24,28},{28,24},{1,5},{5... | collective-permute-start | bytes 3981320 | tf_op jit(solution)/shard_map/ppermute | solution.py:757
  240.1 41.2 %collective-permute-start.18 = (bf16[4,576,1152]{2,1,0:T(8,128)(2,1)}, bf16[4,576,1152]{2,1,0:T(8,128)(2,1)}, u32[]{:S(2)}, u32[]{:S(2)}) collective-permute-start(bf16[4,576,1152]{2,1,0:T(8,128)(2,1)} %shard_map.208), channel_id=1, source_target_pairs={{0,4},{4,0},{8,12},{12,8},{16,20},{20,16},{24,28},{28,24},{1,5},{5... | collective-permute-start | bytes 15925256 | tf_op jit(solution)/shard_map/ppermute | solution.py:757
  241.6 26.5 %collective-permute-start.15 = (bf16[6,144,288]{2,1,0:T(8,128)(2,1)}, bf16[6,144,288]{2,1,0:T(8,128)(2,1)}, u32[]{:S(2)}, u32[]{:S(2)}) collective-permute-start(bf16[6,144,288]{2,1,0:T(8,128)(2,1)} %get-tuple-element.238), channel_id=1, source_target_pairs={{0,1},{1,0},{2,3},{3,2},{4,5},{5,4},{6,7},{7,6},{8,9},{9,8},{10,11... | collective-permute-start | bytes 1493000 | tf_op jit(solution)/shard_map/ppermute | solution.py:772
  242.1 31.6 %collective-permute-start.16 = (bf16[6,144,288]{2,1,0:T(8,128)(2,1)}, bf16[6,144,288]{2,1,0:T(8,128)(2,1)}, u32[]{:S(2)}, u32[]{:S(2)}) collective-permute-start(bf16[6,144,288]{2,1,0:T(8,128)(2,1)} %get-tuple-element.237), channel_id=1, source_target_pairs={{0,2},{1,3},{2,0},{3,1},{4,6},{5,7},{6,4},{7,5},{8,10},{9,11},{10,... | collective-permute-start | bytes 1493000 | tf_op jit(solution)/shard_map/ppermute | solution.py:772
  243.5 30.2 %collective-permute-start.17 = (bf16[6,144,288]{2,1,0:T(8,128)(2,1)}, bf16[6,144,288]{2,1,0:T(8,128)(2,1)}, u32[]{:S(2)}, u32[]{:S(2)}) collective-permute-start(bf16[6,144,288]{2,1,0:T(8,128)(2,1)} %get-tuple-element.236), channel_id=1, source_target_pairs={{0,3},{1,2},{2,1},{3,0},{4,7},{5,6},{6,5},{7,4},{8,11},{9,10},{10,... | collective-permute-start | bytes 1493000 | tf_op jit(solution)/shard_map/ppermute | solution.py:772
  302.4 31.9 %collective-permute-start.20 = (bf16[2,288,1152]{2,1,0:T(8,128)(2,1)}, bf16[2,288,1152]{2,1,0:T(8,128)(2,1)}, u32[]{:S(2)}, u32[]{:S(2)}) collective-permute-start(bf16[2,288,1152]{2,1,0:T(8,128)(2,1)} %get-tuple-element.164), channel_id=1, source_target_pairs={{0,1},{1,0},{2,3},{3,2},{4,5},{5,4},{6,7},{7,6},{8,9},{9,8},{10,11... | collective-permute-start | bytes 3981320 | tf_op jit(solution)/shard_map/ppermute | solution.py:772
  303.8 31.6 %collective-permute-start.21 = (bf16[2,288,1152]{2,1,0:T(8,128)(2,1)}, bf16[2,288,1152]{2,1,0:T(8,128)(2,1)}, u32[]{:S(2)}, u32[]{:S(2)}) collective-permute-start(bf16[2,288,1152]{2,1,0:T(8,128)(2,1)} %get-tuple-element.165), channel_id=1, source_target_pairs={{0,2},{1,3},{2,0},{3,1},{4,6},{5,7},{6,4},{7,5},{8,10},{9,11},{10,... | collective-permute-start | bytes 3981320 | tf_op jit(solution)/shard_map/ppermute | solution.py:772
  335.4 35.4 %collective-permute-start.22 = (bf16[2,288,1152]{2,1,0:T(8,128)(2,1)S(1)}, bf16[2,288,1152]{2,1,0:T(8,128)(2,1)S(1)}, u32[]{:S(2)}, u32[]{:S(2)}) collective-permute-start(bf16[2,288,1152]{2,1,0:T(8,128)(2,1)S(1)} %get-tuple-element.169), channel_id=1, source_target_pairs={{0,1},{1,0},{2,3},{3,2},{4,5},{5,4},{6,7},{7,6},{8,9},{9,8},{10,11... | collective-permute-start | bytes 3981320 | tf_op jit(solution)/shard_map/ppermute | solution.py:772
  336.0 35.8 %collective-permute-start.23 = (bf16[2,288,1152]{2,1,0:T(8,128)(2,1)}, bf16[2,288,1152]{2,1,0:T(8,128)(2,1)}, u32[]{:S(2)}, u32[]{:S(2)}) collective-permute-start(bf16[2,288,1152]{2,1,0:T(8,128)(2,1)} %get-tuple-element.170), channel_id=1, source_target_pairs={{0,2},{1,3},{2,0},{3,1},{4,6},{5,7},{6,4},{7,5},{8,10},{9,11},{10,... | collective-permute-start | bytes 3981320 | tf_op jit(solution)/shard_map/ppermute | solution.py:772
  339.9 42.1 %collective-permute-start.25 = (bf16[2,144,1152]{2,1,0:T(8,128)(2,1)}, bf16[2,144,1152]{2,1,0:T(8,128)(2,1)}, u32[]{:S(2)}, u32[]{:S(2)}) collective-permute-start(bf16[2,144,1152]{2,1,0:T(8,128)(2,1)} %dynamic-slice_bitcast_fusion.7), channel_id=1, source_target_pairs={{0,1},{1,0},{2,3},{3,2},{4,5},{5,4},{6,7},{7,6},{8,9},{9,8},{10,11... | collective-permute-start | bytes 1990664 | tf_op jit(solution)/shard_map/ppermute | solution.py:772
  343.7 38.3 %collective-permute-start.24 = (bf16[2,144,1152]{2,1,0:T(8,128)(2,1)}, bf16[2,144,1152]{2,1,0:T(8,128)(2,1)}, u32[]{:S(2)}, u32[]{:S(2)}) collective-permute-start(bf16[2,144,1152]{2,1,0:T(8,128)(2,1)} %dynamic-slice_bitcast_fusion.8), channel_id=1, source_target_pairs={{0,2},{1,3},{2,0},{3,1},{4,6},{5,7},{6,4},{7,5},{8,10},{9,11},{10,... | collective-permute-start | bytes 1990664 | tf_op jit(solution)/shard_map/ppermute | solution.py:772
  382.0 28.0 %collective-permute-start.26 = (bf16[4,576,1152]{2,1,0:T(8,128)(2,1)}, bf16[4,576,1152]{2,1,0:T(8,128)(2,1)}, u32[]{:S(2)}, u32[]{:S(2)}) collective-permute-start(bf16[4,576,1152]{2,1,0:T(8,128)(2,1)} %shard_map.215), channel_id=1, source_target_pairs={{0,4},{4,0},{8,12},{12,8},{16,20},{20,16},{24,28},{28,24},{1,5},{5... | collective-permute-start | bytes 15925256 | tf_op jit(solution)/shard_map/ppermute | solution.py:757
  437.8 30.4 %collective-permute-start.30 = (bf16[2,288,1152]{2,1,0:T(8,128)(2,1)}, bf16[2,288,1152]{2,1,0:T(8,128)(2,1)}, u32[]{:S(2)}, u32[]{:S(2)}) collective-permute-start(bf16[2,288,1152]{2,1,0:T(8,128)(2,1)} %get-tuple-element.202), channel_id=1, source_target_pairs={{0,1},{1,0},{2,3},{3,2},{4,5},{5,4},{6,7},{7,6},{8,9},{9,8},{10,11... | collective-permute-start | bytes 3981320 | tf_op jit(solution)/shard_map/ppermute | solution.py:772
  438.8 30.1 %collective-permute-start.31 = (bf16[2,288,1152]{2,1,0:T(8,128)(2,1)}, bf16[2,288,1152]{2,1,0:T(8,128)(2,1)}, u32[]{:S(2)}, u32[]{:S(2)}) collective-permute-start(bf16[2,288,1152]{2,1,0:T(8,128)(2,1)} %get-tuple-element.203), channel_id=1, source_target_pairs={{0,2},{1,3},{2,0},{3,1},{4,6},{5,7},{6,4},{7,5},{8,10},{9,11},{10,... | collective-permute-start | bytes 3981320 | tf_op jit(solution)/shard_map/ppermute | solution.py:772
  441.1 26.3 %collective-permute-start.33 = (bf16[2,144,1152]{2,1,0:T(8,128)(2,1)}, bf16[2,144,1152]{2,1,0:T(8,128)(2,1)}, u32[]{:S(2)}, u32[]{:S(2)}) collective-permute-start(bf16[2,144,1152]{2,1,0:T(8,128)(2,1)} %dynamic-slice_bitcast_fusion.3), channel_id=1, source_target_pairs={{0,8},{4,12},{8,0},{12,4},{16,24},{20,28},{24,16},{28,20},{1,9},{5... | collective-permute-start | bytes 1990664 | tf_op jit(solution)/shard_map/ppermute | solution.py:767
  449.7 70.4 %all-gather.18.cloned.1.call-start = ((), (), s32[]{:S(2)}) async-start(), calls=%async_computation.9 | async-start | bytes 2985984 | tf_op jit(solution)/shard_map/all_gather | solution.py:961
  470.7 107.7 %all-gather.22.cloned.1.call-start = ((), (), s32[]{:S(2)}) async-start(), calls=%async_computation.11 | async-start | bytes 2985984 | tf_op jit(solution)/shard_map/all_gather | solution.py:961
  473.7 40.7 %collective-permute-start.35 = (bf16[2,144,1152]{2,1,0:T(8,128)(2,1)}, bf16[2,144,1152]{2,1,0:T(8,128)(2,1)}, u32[]{:S(2)}, u32[]{:S(2)}) collective-permute-start(bf16[2,144,1152]{2,1,0:T(8,128)(2,1)} %dynamic-slice_bitcast_fusion.1), channel_id=1, source_target_pairs={{0,1},{1,0},{2,3},{3,2},{4,5},{5,4},{6,7},{7,6},{8,9},{9,8},{10,11... | collective-permute-start | bytes 1990664 | tf_op jit(solution)/shard_map/ppermute | solution.py:772
  477.4 37.0 %collective-permute-start.34 = (bf16[2,144,1152]{2,1,0:T(8,128)(2,1)}, bf16[2,144,1152]{2,1,0:T(8,128)(2,1)}, u32[]{:S(2)}, u32[]{:S(2)}) collective-permute-start(bf16[2,144,1152]{2,1,0:T(8,128)(2,1)} %dynamic-slice_bitcast_fusion.2), channel_id=1, source_target_pairs={{0,2},{1,3},{2,0},{3,1},{4,6},{5,7},{6,4},{7,5},{8,10},{9,11},{10,... | collective-permute-start | bytes 1990664 | tf_op jit(solution)/shard_map/ppermute | solution.py:772
  480.8 33.6 %collective-permute-start.36 = (bf16[1,144,1152]{2,1,0:T(8,128)(2,1)}, bf16[1,144,1152]{2,1,0:T(8,128)(2,1)}, u32[]{:S(2)}, u32[]{:S(2)}) collective-permute-start(bf16[1,144,1152]{2,1,0:T(8,128)(2,1)} %constant_dynamic-slice_fusion.1), channel_id=1, source_target_pairs={{0,16},{4,20},{8,24},{12,28},{16,0},{20,4},{24,8},{28,12},{1,17},{... | collective-permute-start | bytes 995336 | tf_op jit(solution)/shard_map/ppermute | solution.py:767
  520.1 36.1 %collective-permute-start.37 = (bf16[2,144,1152]{2,1,0:T(8,128)(2,1)}, bf16[2,144,1152]{2,1,0:T(8,128)(2,1)}, u32[]{:S(2)}, u32[]{:S(2)}) collective-permute-start(bf16[2,144,1152]{2,1,0:T(8,128)(2,1)} %dynamic-slice_bitcast_fusion), channel_id=1, source_target_pairs={{0,8},{4,12},{8,0},{12,4},{16,24},{20,28},{24,16},{28,20},{1,9},{5... | collective-permute-start | bytes 1990664 | tf_op jit(solution)/shard_map/ppermute | solution.py:767
  560.5 62.8 %all-gather.20.cloned.1.call-start = ((), (), s32[]{:S(2)}) async-start(), calls=%async_computation.10 | async-start | bytes 2985984 | tf_op jit(solution)/shard_map/all_gather | solution.py:961
  586.9 36.3 %all-to-all-start.4 = ((bf16[4,3,144,288]{3,2,1,0:T(8,128)(2,1)}), bf16[4,3,144,288]{3,2,1,0:T(8,128)(2,1)}, u32[]{:S(2)}, u32[]{:S(2)}) async-start(bf16[4,3,144,288]{3,2,1,0:T(8,128)(2,1)} %shard_map.219), calls=%async_computation.4 | async-start | bytes 2654208 | tf_op jit(solution)/shard_map/all_to_all | solution.py:842
  (79 other events, 618.0 us)
Sparse Core Ops, SparseCore 0:
  34.1 106.8 all-gather.13
  144.6 96.4 all-gather.15
  282.6 76.5 all-gather.11
  470.8 46.6 all-gather.17
  519.5 40.2 all-gather.21
  574.9 39.7 all-gather.19
